TPU v7x, 32 devices: a whole 2x2x4 slice. The times are simulated.
32 devices in a mesh: role: 2 (over x), seq: 4 (over z), rep: 4 (over y, core).
Axes of the slice: x: 2, y: 2, z: 4, core: 2. Of those that a mesh axis runs over, the one named last changes fastest.
Arguments:
- hidden_in: bfloat16 [2, 1024, 2048], P('role', ('seq', 'rep')), may hold values from -6 to 6
- attn_gain: float32 [2048], replicated, may hold values from 0.25 to 1.75
- w_query: bfloat16 [2048, 2048], P(None, 'rep'), may hold values from -0.125 to 0.125
- w_keyval: bfloat16 [2, 2048, 256], replicated, may hold values from -0.125 to 0.125
- q_gain: float32 [128], replicated, may hold values from 1.2 to 14
- k_gain: float32 [128], replicated, may hold values from 1.2 to 14
- w_out: bfloat16 [2048, 2048], P('rep'), may hold values from -0.25 to 0.25
- moe_gain: float32 [2048], replicated, may hold values from 0.25 to 1.75
- expert_ids: int32 [2, 1024, 8], P('role', ('seq', 'rep')), may hold values from 0 to 31, all different within a row; in each aligned block of 64 rows (0 to 63, 64 to 127, ..., all dimensions but the last counted through in order) at most 28 rows name the same one
- gate_fixed: int32 [2, 1024, 8], P('role', ('seq', 'rep')), may hold values from 1 to 4095
- w_gateup: bfloat16 [32, 2048, 1536], P(('role', 'seq', 'rep')), may hold values from -0.125 to 0.125
- w_down: bfloat16 [32, 768, 2048], P(('role', 'seq', 'rep')), may hold values from -0.21875 to 0.21875
Outputs:
- layer_out: bfloat16 [2, 1024, 2048], P('role', ('seq', 'rep'))
Inputs may be any that keep to these rules, and one draw needn't show every extreme that they name: `expert_ids`: each row names 8 different experts; the 64 tokens of one device name no expert more than 28 times, and some device names some expert exactly 28 times.
All inputs are finite; a program needn't handle non-finite values.
Results may differ from a plain program's by a relative error of at most 0.015.
The roundings to bfloat16 on the way count: a program that leaves them out, or rounds other values in their place, can miss the bound.
Values may be sent and summed in bfloat16 or wider, within the bound.
No kernel may reach another device: no remote copies, remote signals or barrier semaphores. Data moves between devices by JAX's collectives and lax.ppermute only.
A program may use at most 128 MiB of HBM per device.

v0:
```python
import math

import jax
import jax.numpy as jnp
from jax import lax
from jax.sharding import PartitionSpec as P


def rms_rows(values_in, gain_vec):
    return (
        values_in
        * lax.rsqrt(jnp.mean(values_in * values_in, axis=-1, keepdims=True) + 1e-06)
        * gain_vec
    )


def per_device(
    hidden_in,
    attn_gain,
    w_query,
    w_keyval,
    q_gain,
    k_gain,
    w_out,
    moe_gain,
    expert_ids,
    gate_fixed,
    w_gateup,
    w_down,
):
    tokens = hidden_in[0]
    row_count, model_width = tokens.shape
    head_dim = q_gain.shape[0]
    local_heads = w_query.shape[1] // head_dim
    kv_heads = w_keyval.shape[2] // head_dim
    all_heads = local_heads * lax.axis_size("rep")
    group_size = all_heads // kv_heads
    kv_index = lax.axis_index("rep") * local_heads // group_size
    key_cols = lax.dynamic_slice_in_dim(w_keyval[0], kv_index * head_dim, head_dim, 1)
    value_cols = lax.dynamic_slice_in_dim(w_keyval[1], kv_index * head_dim, head_dim, 1)
    merged = jnp.concatenate([w_query, key_cols, value_cols], axis=1)
    normed = rms_rows(tokens.astype(jnp.float32), attn_gain).astype(jnp.bfloat16)
    projected = jnp.dot(
        lax.all_gather(normed, "rep", axis=0, tiled=True),
        merged,
        preferred_element_type=jnp.float32,
    )
    query_span = projected.shape[0]
    query_end = local_heads * head_dim
    query_part = projected[:, :query_end].reshape(query_span, local_heads, head_dim)
    queries = rms_rows(query_part, q_gain).astype(jnp.bfloat16)
    key_rows = rms_rows(projected[:, query_end : query_end + head_dim], k_gain).astype(jnp.bfloat16)
    value_rows = projected[:, query_end + head_dim :].astype(jnp.bfloat16)
    score_scale = head_dim ** (-0.5)
    initial = (
        jnp.full((query_span, local_heads), -1e30, jnp.float32),
        jnp.zeros((query_span, local_heads), jnp.float32),
        jnp.zeros((query_span, local_heads, head_dim), jnp.float32),
    )
    key_piece = lax.all_gather(key_rows, "seq", axis=0, tiled=True)
    value_piece = lax.all_gather(value_rows, "seq", axis=0, tiled=True)
    key_count = key_piece.shape[0]
    block_size = math.gcd(key_count, 1024)
    key_blocks = key_piece.reshape(key_count // block_size, block_size, head_dim)
    value_blocks = value_piece.reshape(key_count // block_size, block_size, head_dim)

    def one_block(state, blocks):
        run_max, run_sum, run_acc = state
        key_block, value_block = blocks
        scores = (
            jnp.einsum("qhd,kd->qhk", queries, key_block, preferred_element_type=jnp.float32)
            * score_scale
        )
        new_max = jnp.maximum(run_max, jnp.max(scores, axis=2))
        rescale = jnp.exp(run_max - new_max)
        weights = jnp.exp(scores - new_max[:, :, None])
        run_sum = run_sum * rescale + jnp.sum(weights, axis=2)
        run_acc = run_acc * rescale[:, :, None] + jnp.einsum(
            "qhk,kd->qhd",
            weights.astype(jnp.bfloat16),
            value_block,
            preferred_element_type=jnp.float32,
        )
        return ((new_max, run_sum, run_acc), None)

    final_state, _ = lax.scan(one_block, initial, (key_blocks, value_blocks))
    run_max, run_sum, run_acc = final_state
    context = (
        (run_acc / run_sum[:, :, None])
        .astype(jnp.bfloat16)
        .reshape(query_span, local_heads * head_dim)
    )
    attended = lax.psum_scatter(
        jnp.dot(context, w_out, preferred_element_type=jnp.float32).astype(jnp.bfloat16),
        "rep",
        scatter_dimension=0,
        tiled=True,
    ).astype(jnp.float32)
    mixed = tokens.astype(jnp.float32) + attended
    moe_in = rms_rows(mixed, moe_gain).astype(jnp.bfloat16)
    top_count = expert_ids.shape[2]
    expert_count = lax.axis_size(("role", "seq", "rep"))
    capacity = max(2, 7 * row_count * top_count // (4 * expert_count))
    pair_count = row_count * top_count
    expert_flat = expert_ids[0].reshape(pair_count)
    onehot = (expert_flat[:, None] == jnp.arange(expert_count, dtype=jnp.int32)[None, :]).astype(
        jnp.int32
    )
    ranking = jnp.sum((jnp.cumsum(onehot, axis=0) - onehot) * onehot, axis=1)
    slot_index = expert_flat * capacity + ranking
    owner_row = jnp.arange(pair_count, dtype=jnp.int32) // top_count
    outgoing = (
        jnp.zeros((expert_count * capacity, model_width), jnp.bfloat16)
        .at[slot_index]
        .set(moe_in[owner_row])
    )
    hidden_width = w_down.shape[1]
    arrived = lax.all_to_all(
        outgoing.reshape(expert_count, capacity, model_width),
        ("role", "seq", "rep"),
        split_axis=0,
        concat_axis=0,
        tiled=True,
    )
    flat_rows = arrived.reshape(-1, model_width)
    gate_up = jnp.dot(flat_rows, w_gateup[0], preferred_element_type=jnp.float32)
    expert_hidden = (jax.nn.silu(gate_up[:, :hidden_width]) * gate_up[:, hidden_width:]).astype(
        jnp.bfloat16
    )
    served = jnp.dot(expert_hidden, w_down[0], preferred_element_type=jnp.float32).astype(
        jnp.bfloat16
    )
    returned = lax.all_to_all(
        served.reshape(arrived.shape),
        ("role", "seq", "rep"),
        split_axis=0,
        concat_axis=0,
        tiled=True,
    )
    returned = returned.reshape(expert_count * capacity, model_width)
    fixed_gates = gate_fixed[0].astype(jnp.float32)
    gate_share = fixed_gates / jnp.sum(fixed_gates, axis=1, keepdims=True)
    picked = returned[slot_index].astype(jnp.float32).reshape(row_count, top_count, model_width)
    routed = jnp.sum(picked * gate_share[:, :, None], axis=1)
    return (mixed + routed).astype(jnp.bfloat16)[None]


def solution(mesh):
    placed = (
        P("role", ("seq", "rep"), None),
        P(),
        P(None, "rep"),
        P(),
        P(),
        P(),
        P("rep", None),
        P(),
        P("role", ("seq", "rep"), None),
        P("role", ("seq", "rep"), None),
        P(("role", "seq", "rep"), None, None),
        P(("role", "seq", "rep"), None, None),
    )
    return jax.shard_map(
        per_device,
        mesh=mesh,
        in_specs=placed,
        out_specs=P("role", ("seq", "rep"), None),
        check_vma=False,
    )
```

profile of v0, /device:TPU:0, one launch (start us, length us, event | category | flops | bytes accessed | tf_op | source)
XLA Modules:
  0.0 368.1 jit_solution(11794802918360570855)
XLA Ops:
  6.5 0.0 copy-start
  6.5 0.0 all-gather.2.cloned.1.call-start
  6.5 1.3 fusion.31
  7.8 1.8 fusion.33
  9.6 0.0 all-gather.2.cloned.1.call-update
  9.6 0.0 reduce-scatter.2.cloned.1.call-start
  9.7 0.7 broadcast_bitcast_fusion
  10.4 1.7 fusion.51
  12.0 1.1 dynamic-slice_bitcast_fusion
  13.1 16.1 %all-gather.2.cloned.1.call-done = bf16[256,2048]{1,0:T(8,128)(2,1)} async-done(((bf16[64,2048]{1,0:T(8,128)(2,1)}), bf16[256,2048]{1,0:T(8,128)(2,1)}) %all-gather.2.cloned.1.call-update) | async-done | bytes 1048592 | tf_op jit(solution)/shard_map/all_gather | solution.py:44
  29.2 0.0 copy-start.7
  29.2 3.2 fusion.5
  32.4 0.0 copy-start.2
  32.5 0.9 slice_multiply_fusion.1
  33.4 0.1 multiply_reduce_fusion.2
  33.5 0.0 copy-done.2
  33.5 2.0 mul.159
  35.6 1.4 reduce_sum.76
  37.0 0.0 copy-done.7
  37.0 1.0 multiply_convert_fusion.1
  38.0 13.9 %all_gather.10 = bf16[1024,128]{1,0:T(8,128)(2,1)S(1)} all-gather(bf16[256,128]{1,0:T(8,128)(2,1)S(1)} %multiply_convert_fusion.1), channel_id=1, replica_groups=mesh['role'=2,'seq'=4,'rep'=4] {'seq'}, dimensions={0}, use_global_device_ids=true | all-gather | bytes 327680 | tf_op jit(solution)/shard_map/all_gather | solution.py:60
  52.0 0.3 mul.160
  52.3 1.8 multiply_reduce_fusion
  54.2 0.9 fusion.3
  55.1 0.0 copy-start.3
  55.1 14.8 %all_gather.11 = bf16[1024,128]{1,0:T(8,128)(2,1)S(1)} all-gather(bf16[256,128]{1,0:T(8,128)(2,1)S(1)} %slice.63), channel_id=1, replica_groups=mesh['role'=2,'seq'=4,'rep'=4] {'seq'}, dimensions={0}, use_global_device_ids=true | all-gather | bytes 327680 | tf_op jit(solution)/shard_map/all_gather | solution.py:61
  69.9 1.0 fusion.28
  70.9 0.0 copy-start.4
  70.9 0.0 copy-start.1
  70.9 0.0 copy-start.6
  71.0 0.0 copy-done.3
  71.0 1.7 convolution_convert_fusion.1
  72.7 0.0 reduce-scatter.2.cloned.1.call-update
  72.7 0.0 copy-done.4
  72.7 0.1 copy.36
  72.8 0.1 eq.29
  72.9 0.1 eq.25
  73.0 1.2 reduce-window.6
  74.2 0.2 slice_reduce_fusion
  74.4 0.1 copy.35
  74.5 0.1 mul.177
  74.7 0.1 fusion.45
  74.8 23.0 %reduce-scatter.2.cloned.1.call-done = bf16[64,2048]{1,0:T(8,128)(2,1)} async-done(((bf16[256,2048]{1,0:T(8,128)(2,1)}), bf16[64,2048]{1,0:T(8,128)(2,1)}) %reduce-scatter.2.cloned.1.call-update) | async-done | bytes 262160 | tf_op jit(solution)/shard_map/reduce_scatter | solution.py:93
  97.8 0.0 copy-done.1
  97.8 1.1 multiply_reduce_fusion.1
  98.9 0.0 copy-done.6
  98.9 1.8 multiply_convert_fusion
  100.7 12.8 %scatter_custom_fusion = bf16[896,2048]{1,0:T(8,128)(2,1)} fusion(s32[512]{0:T(512)S(1)} %bitcast.83, bf16[64,2048]{1,0:T(8,128)(2,1)} %multiply_convert_fusion, s32[1024]{0:T(1024)S(1)} %pad_clamp_fusion.1, bf16[]{:T(256)} %constant.85.clone.1), kind=kCustom, calls=%fused_computation.23 | custom fusion | bytes 3670528 | tf_op jit(solution)/shard_map/scatter | solution.py:115
  113.5 5.8 %reshape.195 = bf16[32,28,2048]{2,1,0:T(8,128)(2,1)} reshape(bf16[896,2048]{1,0:T(8,128)(2,1)} %scatter_custom_fusion) | data formatting | bytes 7340032 | tf_op jit(solution)/shard_map/reshape | solution.py:119
  119.3 99.4 %all_to_all.10 = bf16[32,28,2048]{2,1,0:T(8,128)(2,1)} all-to-all(bf16[32,28,2048]{2,1,0:T(8,128)(2,1)} %reshape.195), channel_id=1, replica_groups=mesh['role'=2,'seq'=4,'rep'=4] {'role','seq','rep'}, dimensions={0} | all-to-all | bytes 7340032 | tf_op jit(solution)/shard_map/all_to_all | solution.py:118
  218.7 5.9 %reshape.196 = bf16[896,2048]{1,0:T(8,128)(2,1)} reshape(bf16[32,28,2048]{2,1,0:T(8,128)(2,1)} %all_to_all.10) | data formatting | bytes 7340032 | tf_op jit(solution)/shard_map/reshape | solution.py:125
  224.6 9.0 %fusion = f32[896,1536]{1,0:T(8,128)S(1)} fusion(bf16[896,2048]{1,0:T(8,128)(2,1)} %reshape.196, bf16[1,2048,1536]{2,1,0:T(8,128)(2,1)} %param.22), kind=kOutput, calls=%fused_computation.3 | convolution fusion | flops 5637144576 | bytes 15466496 | tf_op jit(solution)/shard_map/dot_general | solution.py:126
  233.6 0.0 copy-done
  233.6 4.6 %convolution_convert_fusion = bf16[896,2048]{1,0:T(8,128)(2,1)} fusion(bf16[1,768,2048]{2,1,0:T(8,128)(2,1)S(1)} %copy-done, f32[896,1536]{1,0:T(8,128)S(1)} %fusion), kind=kOutput, calls=%fused_computation.9 | convolution fusion | flops 2824536064 | bytes 12320768 | tf_op jit(solution)/shard_map/dot_general | solution.py:130
  238.2 5.8 %reshape.197 = bf16[32,28,2048]{2,1,0:T(8,128)(2,1)} reshape(bf16[896,2048]{1,0:T(8,128)(2,1)} %convolution_convert_fusion) | data formatting | bytes 7340032 | tf_op jit(solution)/shard_map/reshape | solution.py:134
  244.0 0.0 copy-start.5
  244.0 3.7 %all-to-all-start.1 = ((bf16[32,28,2048]{2,1,0:T(8,128)(2,1)}), bf16[32,28,2048]{2,1,0:T(8,128)(2,1)}, u32[]{:S(2)}, u32[]{:S(2)}) async-start(bf16[32,28,2048]{2,1,0:T(8,128)(2,1)} %reshape.197), calls=%async_computation.2 | async-start | bytes 8388608 | tf_op jit(solution)/shard_map/all_to_all | solution.py:133
  247.7 0.0 copy-done.5
  247.8 0.1 copy.39
  247.9 94.6 %all-to-all-done.1 = bf16[32,28,2048]{2,1,0:T(8,128)(2,1)} async-done(((bf16[32,28,2048]{2,1,0:T(8,128)(2,1)}), bf16[32,28,2048]{2,1,0:T(8,128)(2,1)}, u32[]{:S(2)}, u32[]{:S(2)}) %all-to-all-start.1) | async-done | bytes 3670048 | tf_op jit(solution)/shard_map/all_to_all | solution.py:133
  342.4 5.8 %reshape.198 = bf16[896,2048]{1,0:T(8,128)(2,1)} reshape(bf16[32,28,2048]{2,1,0:T(8,128)(2,1)} %all-to-all-done.1) | data formatting | bytes 7340032 | tf_op jit(solution)/shard_map/reshape | solution.py:140
  348.3 7.8 %gather_fusion = bf16[512,2048]{1,0:T(8,128)(2,1)} fusion(bf16[896,2048]{1,0:T(8,128)(2,1)} %reshape.198, s32[1024]{0:T(1024)S(1)} %pad_clamp_fusion), kind=kCustom, calls=%fused_computation.1 | custom fusion | bytes 4196352 | tf_op jit(solution)/shard_map/gather | solution.py:143
  356.1 3.4 fusion.2
  359.5 1.8 fusion.36
  (17 shorter events, 0.2 us)
Async XLA Ops:
  6.5 227.1 %copy-start = (bf16[1,768,2048]{2,1,0:T(8,128)(2,1)S(1)}, bf16[1,768,2048]{2,1,0:T(8,128)(2,1)}, u32[]{:S(2)}) copy-start(bf16[1,768,2048]{2,1,0:T(8,128)(2,1)} %param.23) | copy-start | bytes 9437188
  6.5 22.7 %all-gather.2.cloned.1.call-start = ((), (), s32[]{:S(2)}) async-start(), calls=%async_computation.3 | async-start | bytes 1310720 | tf_op jit(solution)/shard_map/all_gather | solution.py:44
  9.6 88.1 %reduce-scatter.2.cloned.1.call-start = ((), (), s32[]{:S(2)}) async-start(), calls=%async_computation.4 | async-start | bytes 1310720 | tf_op jit(solution)/shard_map/reduce_scatter | solution.py:93
  29.2 7.8 %copy-start.7 = (f32[128]{0:T(128)S(1)}, f32[128]{0:T(128)}, u32[]{:S(2)}) copy-start(f32[128]{0:T(128)} %param.17) | copy-start | bytes 1540
  32.4 1.1 copy-start.2
  55.1 15.9 %copy-start.3 = (bf16[512,2048]{1,0:T(8,128)(2,1)S(1)}, bf16[512,2048]{1,0:T(8,128)(2,1)}, u32[]{:S(2)}) copy-start(bf16[512,2048]{1,0:T(8,128)(2,1)} %param.18) | copy-start | bytes 6291460
  70.9 1.8 copy-start.4
  70.9 26.8 %copy-start.1 = (bf16[1,64,2048]{2,1,0:T(8,128)(2,1)S(1)}, bf16[1,64,2048]{2,1,0:T(8,128)(2,1)}, u32[]{:S(2)}) copy-start(bf16[1,64,2048]{2,1,0:T(8,128)(2,1)} %param.12) | copy-start | bytes 786436
  70.9 28.0 %copy-start.6 = (f32[2048]{0:T(1024)S(1)}, f32[2048]{0:T(1024)}, u32[]{:S(2)}) copy-start(f32[2048]{0:T(1024)} %param.19) | copy-start | bytes 24580
  244.0 3.7 %copy-start.5 = (s32[1,64,8]{1,2,0:T(8,128)S(1)}, s32[1,64,8]{1,2,0:T(8,128)}, u32[]{:S(2)}) copy-start(s32[1,64,8]{1,2,0:T(8,128)} %param.21) | copy-start | bytes 6148
  244.0 98.4 %all-to-all-start.1 = ((bf16[32,28,2048]{2,1,0:T(8,128)(2,1)}), bf16[32,28,2048]{2,1,0:T(8,128)(2,1)}, u32[]{:S(2)}, u32[]{:S(2)}) async-start(bf16[32,28,2048]{2,1,0:T(8,128)(2,1)} %reshape.197), calls=%async_computation.2 | async-start | bytes 8388608 | tf_op jit(solution)/shard_map/all_to_all | solution.py:133
Sparse Core Ops, SparseCore 0:
  9.7 19.4 all-gather.1
  72.8 24.8 reduce-scatter.1
where the time goes:
time: 369 us; the launch traced here: 368 us
  waiting for transfers between devices  134 us (36%)
  blocking collectives  128 us (35%)
  local copies, waits for them, and re-layouts  50.6 us (14%)
  matrix products  21.4 us (6%)
  other arithmetic  16.9 us (5%)
  between operations  13.7 us (4%)
  starting transfers between devices  3.74 us (1%)
    all_to_all x1, blocking collectives, per_device(): lax.all_to_all(outgoing.reshape(expert_count, capacity, model_width), ('r...  99.4 us
    all_to_all x1, waiting for transfers between devices, per_device(): lax.all_to_all(served.reshape(arrived.shape), ('role', 'seq', 'rep'), spl...  94.6 us
    reduce_scatter x1, waiting for transfers between devices, per_device(): lax.psum_scatter(jnp.dot(context, w_out, preferred_element_type=jnp.float...  23 us
    all_gather x1, waiting for transfers between devices, per_device(): lax.all_gather(normed, 'rep', axis=0, tiled=True)  16.1 us
    all_gather x1, blocking collectives, per_device(): value_piece = lax.all_gather(value_rows, 'seq', axis=0, tiled=True)  14.8 us
    all_gather x1, blocking collectives, per_device(): key_piece = lax.all_gather(key_rows, 'seq', axis=0, tiled=True)  13.9 us
    scatter x1, local copies, waits for them, and re-layouts, per_device(): outgoing = jnp.zeros((expert_count * capacity, model_width), jnp.bfloat16...  12.8 us
    dot_general x1, matrix products, per_device(): jnp.dot(flat_rows, w_gateup[0], preferred_element_type=jnp.float32)  9.04 us
  transfers between devices with their start and end apart: 3, of which 3 were waited for; matrix products, arithmetic and copies ran while one was open for 2% of the time, Pallas kernels for 0%

commit v1 on v0

v1 whole, which is shorter than its diff:
```python
import math

import jax
import jax.numpy as jnp
from jax import lax
from jax.sharding import PartitionSpec as P


EVERY = ("role", "seq", "rep")


def rms_rows(values_in, gain_vec):
    return (
        values_in
        * lax.rsqrt(jnp.mean(values_in * values_in, axis=-1, keepdims=True) + 1e-06)
        * gain_vec
    )


def per_device(
    hidden_in,
    attn_gain,
    w_query,
    w_keyval,
    q_gain,
    k_gain,
    w_out,
    moe_gain,
    expert_ids,
    gate_fixed,
    w_gateup,
    w_down,
):
    tokens = hidden_in[0]
    row_count, model_width = tokens.shape
    head_dim = q_gain.shape[0]
    local_heads = w_query.shape[1] // head_dim
    kv_heads = w_keyval.shape[2] // head_dim
    all_heads = local_heads * lax.axis_size("rep")
    group_size = all_heads // kv_heads
    kv_index = lax.axis_index("rep") * local_heads // group_size
    kv_width = kv_heads * head_dim
    top_count = expert_ids.shape[2]
    routes = lax.all_gather(
        jnp.concatenate([expert_ids[0], gate_fixed[0]], axis=1), EVERY, axis=0, tiled=True
    )
    normed = rms_rows(tokens.astype(jnp.float32), attn_gain).astype(jnp.bfloat16)
    gathered = lax.all_gather(normed, "rep", axis=0, tiled=True)
    own_keys = jnp.dot(normed, w_keyval[0], preferred_element_type=jnp.float32)
    own_values = jnp.dot(normed, w_keyval[1], preferred_element_type=jnp.float32)
    own_keys = rms_rows(own_keys.reshape(row_count, kv_heads, head_dim), k_gain)
    own_kv = jnp.concatenate([own_keys.reshape(row_count, kv_width), own_values], axis=1)
    all_kv = lax.all_gather(own_kv.astype(jnp.bfloat16), ("seq", "rep"), axis=0, tiled=True)
    key_piece = lax.dynamic_slice_in_dim(all_kv, kv_index * head_dim, head_dim, 1)
    value_piece = lax.dynamic_slice_in_dim(all_kv, kv_width + kv_index * head_dim, head_dim, 1)
    projected = jnp.dot(gathered, w_query, preferred_element_type=jnp.float32)
    query_span = projected.shape[0]
    query_part = projected.reshape(query_span, local_heads, head_dim)
    queries = rms_rows(query_part, q_gain).astype(jnp.bfloat16)
    score_scale = head_dim ** (-0.5)
    initial = (
        jnp.full((query_span, local_heads), -1e30, jnp.float32),
        jnp.zeros((query_span, local_heads), jnp.float32),
        jnp.zeros((query_span, local_heads, head_dim), jnp.float32),
    )
    key_count = key_piece.shape[0]
    block_size = math.gcd(key_count, 1024)
    key_blocks = key_piece.reshape(key_count // block_size, block_size, head_dim)
    value_blocks = value_piece.reshape(key_count // block_size, block_size, head_dim)

    def one_block(state, blocks):
        run_max, run_sum, run_acc = state
        key_block, value_block = blocks
        scores = (
            jnp.einsum("qhd,kd->qhk", queries, key_block, preferred_element_type=jnp.float32)
            * score_scale
        )
        new_max = jnp.maximum(run_max, jnp.max(scores, axis=2))
        rescale = jnp.exp(run_max - new_max)
        weights = jnp.exp(scores - new_max[:, :, None])
        run_sum = run_sum * rescale + jnp.sum(weights, axis=2)
        run_acc = run_acc * rescale[:, :, None] + jnp.einsum(
            "qhk,kd->qhd",
            weights.astype(jnp.bfloat16),
            value_block,
            preferred_element_type=jnp.float32,
        )
        return ((new_max, run_sum, run_acc), None)

    final_state, _ = lax.scan(one_block, initial, (key_blocks, value_blocks))
    run_max, run_sum, run_acc = final_state
    context = (
        (run_acc / run_sum[:, :, None])
        .astype(jnp.bfloat16)
        .reshape(query_span, local_heads * head_dim)
    )
    attended = lax.psum_scatter(
        jnp.dot(context, w_out, preferred_element_type=jnp.float32).astype(jnp.bfloat16),
        "rep",
        scatter_dimension=0,
        tiled=True,
    ).astype(jnp.float32)
    mixed = tokens.astype(jnp.float32) + attended
    moe_in = rms_rows(mixed, moe_gain).astype(jnp.bfloat16)
    everyone = moe_in
    for axis in reversed(EVERY) if lax.axis_size(EVERY) > 32 else (EVERY,):
        everyone = lax.all_gather(everyone, axis, axis=0, tiled=True)
    hidden_width = w_down.shape[1]
    my_expert = lax.axis_index(EVERY)
    gates = routes[:, top_count:].astype(jnp.float32)
    mine = jnp.sum(jnp.where(routes[:, :top_count] == my_expert, gates, 0.0), axis=1)
    share = mine / jnp.sum(gates, axis=1)
    span = math.gcd(everyone.shape[0], 2048)

    def one_span(packed):
        span_rows, span_share = packed
        gate_up = jnp.dot(span_rows, w_gateup[0], preferred_element_type=jnp.float32)
        expert_hidden = (
            jax.nn.silu(gate_up[:, :hidden_width]) * gate_up[:, hidden_width:]
        ).astype(jnp.bfloat16)
        served = jnp.dot(expert_hidden, w_down[0], preferred_element_type=jnp.float32)
        served = served.astype(jnp.bfloat16).astype(jnp.float32)
        return (served * span_share[:, None]).astype(jnp.bfloat16)

    weighted = lax.map(
        one_span, (everyone.reshape(-1, span, model_width), share.reshape(-1, span))
    ).reshape(-1, model_width)
    routed = lax.psum_scatter(weighted, EVERY, scatter_dimension=0, tiled=True).astype(jnp.float32)
    return (mixed + routed).astype(jnp.bfloat16)[None]


def solution(mesh):
    placed = (
        P("role", ("seq", "rep"), None),
        P(),
        P(None, "rep"),
        P(),
        P(),
        P(),
        P("rep", None),
        P(),
        P("role", ("seq", "rep"), None),
        P("role", ("seq", "rep"), None),
        P(("role", "seq", "rep"), None, None),
        P(("role", "seq", "rep"), None, None),
    )
    return jax.shard_map(
        per_device,
        mesh=mesh,
        in_specs=placed,
        out_specs=P("role", ("seq", "rep"), None),
        check_vma=False,
    )
```

time: 369 us -> 364 us (0.986)
  waiting for transfers between devices: 134 us -> 248 us
  blocking collectives: 128 us -> 42 us
  local copies, waits for them, and re-layouts: 50.6 us -> 8.83 us
  matrix products: 21.4 us -> 39 us
  other arithmetic: 16.9 us -> 12.5 us
    reduce_scatter x0 -> x1, waiting for transfers between devices: none -> 148 us  [per_device(): lax.psum_scatter(weighted, EVERY, scatter_dimension=0, tiled=True)]
    all_to_all x1 -> x0, blocking collectives: 99.4 us -> none  [per_device(): lax.all_to_all(outgoing.reshape(expert_count, capacity, model_width), ('r...]
    all_to_all x1 -> x0, waiting for transfers between devices: 94.6 us -> none  [per_device(): lax.all_to_all(served.reshape(arrived.shape), ('role', 'seq', 'rep'), spl...]
    all_gather x1 -> x3, waiting for transfers between devices: 16.1 us -> 76.1 us  [the longest x1 33.9 us: per_device(): everyone = lax.all_gather(everyone, axis, axis=0, tiled=True)]
    reshape x4 -> x0, local copies, waits for them, and re-layouts: 23.4 us -> none  [the longest x1 5.87 us: per_device(): flat_rows = arrived.reshape(-1, model_width)]
    dot_general x3 -> x5, matrix products: 16.8 us -> 33.4 us  [the longest x1 17.4 us: one_span(): jnp.dot(span_rows, w_gateup[0], preferred_element_type=jnp.float32)]
    all_gather x2 -> x1, blocking collectives: 28.7 us -> 42 us  [per_device(): lax.all_gather(jnp.concatenate([expert_ids[0], gate_fixed[0]], axis=1), E...]
    scatter x1 -> x0, local copies, waits for them, and re-layouts: 12.8 us -> none  [per_device(): outgoing = jnp.zeros((expert_count * capacity, model_width), jnp.bfloat16...]
  transfers between devices with their start and end apart: 3 -> 5, of which waited for: 3 -> 5; matrix products, arithmetic and copies ran while one was open for 2% -> 5% of each run, Pallas kernels for 0% -> 0%
where the time goes in v1:
time: 364 us
  waiting for transfers between devices  248 us (68%)
  blocking collectives  42 us (12%)
  matrix products  39 us (11%)
  between operations  13.4 us (4%)
  other arithmetic  12.5 us (3%)
  local copies, waits for them, and re-layouts  8.83 us (2%)
    reduce_scatter x1, waiting for transfers between devices, per_device(): lax.psum_scatter(weighted, EVERY, scatter_dimension=0, tiled=True)  148 us
    all_gather x1, blocking collectives, per_device(): lax.all_gather(jnp.concatenate([expert_ids[0], gate_fixed[0]], axis=1), E...  42 us
    all_gather x1, waiting for transfers between devices, per_device(): everyone = lax.all_gather(everyone, axis, axis=0, tiled=True)  33.9 us
    all_gather x1, waiting for transfers between devices, per_device(): lax.all_gather(own_kv.astype(jnp.bfloat16), ('seq', 'rep'), axis=0, tiled...  31.5 us
    reduce_scatter x1, waiting for transfers between devices, per_device(): lax.psum_scatter(jnp.dot(context, w_out, preferred_element_type=jnp.float...  23.9 us
    dot_general x1, matrix products, one_span(): jnp.dot(span_rows, w_gateup[0], preferred_element_type=jnp.float32)  17.4 us
    all_gather x1, waiting for transfers between devices, per_device(): gathered = lax.all_gather(normed, 'rep', axis=0, tiled=True)  10.7 us
    dot_general x1, matrix products, one_span(): jnp.dot(expert_hidden, w_down[0], preferred_element_type=jnp.float32)  9.06 us
  transfers between devices with their start and end apart: 5, of which 5 were waited for; matrix products, arithmetic and copies ran while one was open for 5% of the time, Pallas kernels for 0%

profile of v1, /device:TPU:0, one launch (start us, length us, event | category | flops | bytes accessed | tf_op | source)
XLA Modules:
  0.0 363.6 jit_solution(17966662618265370269)
XLA Ops:
  6.5 0.0 copy-start
  6.5 0.0 copy-start.1
  6.5 0.0 copy-start.3
  6.5 0.0 copy-start.7
  6.5 0.0 all-gather.5.cloned.1.call-start
  6.6 1.3 fusion.26
  7.9 0.0 copy-start.8
  7.9 1.8 fusion.28
  9.7 0.0 all-gather.5.cloned.1.call-update
  9.7 0.0 all-gather.7.cloned.1.call-start
  9.7 2.3 slice_bitcast_fusion
  12.1 2.3 copy.34
  14.3 0.0 copy-done.1
  14.3 0.0 copy-done.3
  14.4 1.8 multiply_reduce_fusion.2
  16.1 0.0 copy-done.7
  16.1 0.1 copy_bitcast_fusion
  16.2 1.6 convolution_convert_fusion.1
  17.8 0.6 pad_maximum_fusion
  18.4 0.0 all-gather.7.cloned.1.call-update
  18.4 0.0 reduce-scatter.3.cloned.1.call-start
  18.5 0.0 copy-done.8
  18.5 10.7 %all-gather.5.cloned.1.call-done = bf16[256,2048]{1,0:T(8,128)(2,1)} async-done(((bf16[64,2048]{1,0:T(8,128)(2,1)}), bf16[256,2048]{1,0:T(8,128)(2,1)}) %all-gather.5.cloned.1.call-update) | async-done | bytes 1048592 | tf_op jit(solution)/shard_map/all_gather | solution.py:48
  29.3 3.6 fusion.54
  32.9 2.0 mul.162
  34.9 2.0 reduce_sum.65
  36.9 0.9 add_rsqrt_fusion
  37.9 31.5 %all-gather.7.cloned.1.call-done = bf16[1024,512]{1,0:T(8,128)(2,1)} async-done(((bf16[64,512]{1,0:T(8,128)(2,1)}), bf16[1024,512]{1,0:T(8,128)(2,1)}) %all-gather.7.cloned.1.call-update) | async-done | bytes 1048592 | tf_op jit(solution)/shard_map/all_gather | solution.py:53
  69.4 0.3 mul.163
  69.7 1.9 multiply_reduce_fusion
  71.6 0.0 copy-start.2
  71.7 0.9 fusion.3
  72.6 0.0 copy-start.4
  72.6 2.0 fusion.18
  74.6 0.0 copy-start.5
  74.6 0.0 copy-start.6
  74.6 0.0 copy-done.2
  74.6 1.7 convolution_convert_fusion
  76.4 0.0 reduce-scatter.3.cloned.1.call-update
  76.4 0.0 all-gather.9.cloned.1.call-start
  76.4 23.9 %reduce-scatter.3.cloned.1.call-done = bf16[64,2048]{1,0:T(8,128)(2,1)} async-done(((bf16[256,2048]{1,0:T(8,128)(2,1)}), bf16[64,2048]{1,0:T(8,128)(2,1)}) %reduce-scatter.3.cloned.1.call-update) | async-done | bytes 262160 | tf_op jit(solution)/shard_map/reduce_scatter | solution.py:97
  100.3 1.1 multiply_reduce_fusion.1
  101.5 0.0 copy-done.4
  101.5 1.8 multiply_convert_fusion.1
  103.3 0.0 all-gather.9.cloned.1.call-update
  103.3 0.0 reduce-scatter.5.cloned.1.call-start
  103.4 0.0 copy-done.5
  103.4 0.0 copy-done.6
  103.4 42.0 %all-gather = s32[32,64,16]{1,2,0:T(8,128)S(1)} all-gather(s32[1,64,16]{1,2,0:T(8,128)S(1)} %add_bitcast_fusion), channel_id=1, replica_groups=mesh['role'=2,'seq'=4,'rep'=4] {'role','seq','rep'}, dimensions={0}, use_global_device_ids=true | all-gather | bytes 135168 | tf_op jit(solution)/shard_map/all_gather | solution.py:44
  145.4 0.8 copy.38
  146.1 1.1 reshape.111
  147.3 33.9 %all-gather.9.cloned.1.call-done = bf16[2048,2048]{1,0:T(8,128)(2,1)} async-done(((bf16[64,2048]{1,0:T(8,128)(2,1)}), bf16[2048,2048]{1,0:T(8,128)(2,1)}) %all-gather.9.cloned.1.call-update) | async-done | bytes 8388624 | tf_op jit(solution)/shard_map/all_gather | solution.py:107
  181.1 17.4 %fusion.1 = f32[2048,1536]{1,0:T(8,128)S(1)} fusion(bf16[2048,2048]{1,0:T(8,128)(2,1)} %all-gather.9.cloned.1.call-done, bf16[1,2048,1536]{2,1,0:T(8,128)(2,1)} %param.22), kind=kOutput, calls=%fused_computation.3 | convolution fusion | flops 12884901888 | bytes 27262976 | tf_op jit(solution)/shard_map/while/body/eval_jaxpr/dot_general | solution.py:117
  198.5 0.0 copy-done
  198.5 9.1 %multiply_convert_fusion = bf16[2048,2048]{1,0:T(8,128)(2,1)} fusion(f32[2048]{0:T(1024)S(1)} %div.54, f32[2048,1536]{1,0:T(8,128)S(1)} %fusion.1, bf16[1,768,2048]{2,1,0:T(8,128)(2,1)S(1)} %copy-done), kind=kOutput, calls=%fused_computation | convolution fusion | flops 6468665344 | bytes 24125440 | tf_op jit(solution)/shard_map/while/body/eval_jaxpr/dot_general | solution.py:121
  207.6 0.0 reduce-scatter.5.cloned.1.call-update
  207.6 147.7 %reduce-scatter.5.cloned.1.call-done = bf16[64,2048]{1,0:T(8,128)(2,1)} async-done(((bf16[2048,2048]{1,0:T(8,128)(2,1)}), bf16[64,2048]{1,0:T(8,128)(2,1)}) %reduce-scatter.5.cloned.1.call-update) | async-done | bytes 262160 | tf_op jit(solution)/shard_map/reduce_scatter | solution.py:128
  355.3 1.8 fusion.33
  (9 shorter events, 0.1 us)
Async XLA Ops:
  6.5 192.0 %copy-start = (bf16[1,768,2048]{2,1,0:T(8,128)(2,1)S(1)}, bf16[1,768,2048]{2,1,0:T(8,128)(2,1)}, u32[]{:S(2)}) copy-start(bf16[1,768,2048]{2,1,0:T(8,128)(2,1)} %param.23) | copy-start | bytes 9437188
  6.5 7.8 %copy-start.1 = (bf16[1,64,2048]{2,1,0:T(8,128)(2,1)S(1)}, bf16[1,64,2048]{2,1,0:T(8,128)(2,1)}, u32[]{:S(2)}) copy-start(bf16[1,64,2048]{2,1,0:T(8,128)(2,1)} %param.12) | copy-start | bytes 786436
  6.5 7.8 %copy-start.3 = (f32[2048]{0:T(1024)S(1)}, f32[2048]{0:T(1024)}, u32[]{:S(2)}) copy-start(f32[2048]{0:T(1024)} %param.13) | copy-start | bytes 24580
  6.5 9.6 %copy-start.7 = (f32[128]{0:T(128)S(1)}, f32[128]{0:T(128)}, u32[]{:S(2)}) copy-start(f32[128]{0:T(128)} %param.17) | copy-start | bytes 1540
  6.5 22.7 %all-gather.5.cloned.1.call-start = ((), (), s32[]{:S(2)}) async-start(), calls=%async_computation.2 | async-start | bytes 1310720 | tf_op jit(solution)/shard_map/all_gather | solution.py:48
  7.9 10.7 %copy-start.8 = (f32[128]{0:T(128)S(1)}, f32[128]{0:T(128)}, u32[]{:S(2)}) copy-start(f32[128]{0:T(128)} %param.16) | copy-start | bytes 1540
  9.7 59.7 %all-gather.7.cloned.1.call-start = ((), (), s32[]{:S(2)}) async-start(), calls=%async_computation.3 | async-start | bytes 1114112 | tf_op jit(solution)/shard_map/all_gather | solution.py:53
  18.4 81.9 %reduce-scatter.3.cloned.1.call-start = ((), (), s32[]{:S(2)}) async-start(), calls=%async_computation.4 | async-start | bytes 1310720 | tf_op jit(solution)/shard_map/reduce_scatter | solution.py:97
  71.6 3.0 copy-start.2
  72.6 28.9 %copy-start.4 = (f32[2048]{0:T(1024)S(1)}, f32[2048]{0:T(1024)}, u32[]{:S(2)}) copy-start(f32[2048]{0:T(1024)} %param.19) | copy-start | bytes 24580
  74.6 28.8 %copy-start.5 = (s32[1,64,8]{1,2,0:T(8,128)S(1)}, s32[1,64,8]{1,2,0:T(8,128)}, u32[]{:S(2)}) copy-start(s32[1,64,8]{1,2,0:T(8,128)} %param.21) | copy-start | bytes 6148
  74.6 28.8 %copy-start.6 = (s32[1,64,8]{1,2,0:T(8,128)S(1)}, s32[1,64,8]{1,2,0:T(8,128)}, u32[]{:S(2)}) copy-start(s32[1,64,8]{1,2,0:T(8,128)} %param.20) | copy-start | bytes 6148
  76.4 104.7 %all-gather.9.cloned.1.call-start = ((), (), s32[]{:S(2)}) async-start(), calls=%async_computation.5 | async-start | bytes 8650752 | tf_op jit(solution)/shard_map/all_gather | solution.py:107
  103.3 252.0 %reduce-scatter.5.cloned.1.call-start = ((), (), s32[]{:S(2)}) async-start(), calls=%async_computation.6 | async-start | bytes 8650752 | tf_op jit(solution)/shard_map/reduce_scatter | solution.py:128
Sparse Core Ops, SparseCore 0:
  9.8 19.4 all-gather.4
  31.4 37.9 all-gather.6
  76.5 23.7 reduce-scatter.2
  103.5 77.6 all-gather.8
  207.7 147.4 reduce-scatter.4

commit v2 on v1

v2 whole, which is shorter than its diff:
```python
import jax
import jax.numpy as jnp
from jax import lax
from jax.experimental import pallas as pl
from jax.experimental.pallas import tpu as pltpu
from jax.sharding import PartitionSpec as P

EVERY = ("role", "seq", "rep")
PAIR = 1
ACROSS = 2
TILE = 256


def rms_rows(values_in, gain_vec):
    return (
        values_in
        * lax.rsqrt(jnp.mean(values_in * values_in, axis=-1, keepdims=True) + 1e-06)
        * gain_vec
    )


def swap(block, axis, bits):
    size = lax.axis_size(axis)
    return lax.ppermute(block, axis, [(i, i ^ bits) for i in range(size)])


def along_seq(block):
    return [swap(block, "seq", bits) for bits in range(1, lax.axis_size("seq"))]


def spread_routes(own):
    near = jnp.concatenate([own] + along_seq(own), axis=0)
    by_rep = swap(near, "rep", ACROSS)
    both = jnp.stack([near, by_rep])
    return jnp.concatenate([both, swap(both, "role", 1)], axis=0)


def spread_rows(own):
    half = own.shape[1] // 2
    parts = [own, jnp.concatenate(along_seq(own), axis=0)]
    pieces = []
    for part in parts:
        by_rep = swap(part, "rep", ACROSS)
        by_role = swap(part, "role", 1)
        corner_low = swap(by_rep[:, :half], "role", 1)
        corner_high = swap(by_role[:, half:], "rep", ACROSS)
        pieces.append((part, by_rep, by_role, corner_low, corner_high))
    return pieces


def added(first, second):
    return (first.astype(jnp.float32) + second.astype(jnp.float32)).astype(jnp.bfloat16)


def collect_rows(parts, row_count):
    lows, highs = parts
    corner_low = swap(lows[3], "role", 1)
    corner_high = swap(highs[3], "rep", ACROSS)
    straight_low = swap(lows[2], "role", 1)
    straight_high = swap(highs[1], "rep", ACROSS)
    turned_low = swap(added(lows[1], corner_low), "rep", ACROSS)
    turned_high = swap(added(highs[2], corner_high), "role", 1)
    totals = []
    for base, first, second in (
        (lows[0], straight_low, turned_low),
        (highs[0], straight_high, turned_high),
    ):
        near = base.astype(jnp.float32) + first.astype(jnp.float32) + second.astype(jnp.float32)
        total = near[:row_count]
        rounded = near.astype(jnp.bfloat16)
        for bits in range(1, lax.axis_size("seq")):
            block = rounded[bits * row_count : (bits + 1) * row_count]
            total = total + swap(block, "seq", bits).astype(jnp.float32)
        totals.append(total)
    return jnp.concatenate(totals, axis=1)


def expert_kernel(
    row_count,
    pick_ref,
    place_ref,
    share_ref,
    own_gu_ref,
    far_gu_ref,
    own_dn_ref,
    far_dn_ref,
    *refs,
):
    piece_refs, out_refs = refs[:10], refs[10:18]
    x_buf, xs_buf, gu_buf, dn_buf, hid_buf, served_buf, y_buf, x_sem, w_sem, y_sem = refs[18:]
    groups, group_rows = place_ref.shape[1], place_ref.shape[2]
    slots = place_ref.shape[3]
    width = x_buf.shape[2]
    half = width // 2
    hidden = own_dn_ref.shape[0]
    tiles = hidden // TILE
    depth = x_buf.shape[0]

    def row_copies(group):
        copies = []
        for which in range(2):
            start = which * row_count
            rows = pl.ds(start, row_count if which == 0 else group_rows - row_count)
            base = piece_refs[5 * which : 5 * which + 5]
            slot = group % depth
            if group < 3:
                copies.append((base[group], x_buf.at[slot, rows]))
            else:
                copies.append((base[3], x_buf.at[slot, rows, pl.ds(0, half)]))
                copies.append((base[4], x_buf.at[slot, rows, pl.ds(half, half)]))
        return [
            pltpu.make_async_copy(src, dst, x_sem.at[group, number])
            for number, (src, dst) in enumerate(copies)
        ]

    weight_copies = []
    for expert, (gu_ref, dn_ref) in enumerate(((own_gu_ref, own_dn_ref), (far_gu_ref, far_dn_ref))):
        mine = []
        for tile in range(tiles):
            for side in range(2):
                mine.append(
                    pltpu.make_async_copy(
                        gu_ref.at[:, pl.ds(side * hidden + tile * TILE, TILE)],
                        gu_buf.at[expert, tile, side],
                        w_sem.at[expert, 2 * tile + side],
                    )
                )
        mine.append(pltpu.make_async_copy(dn_ref, dn_buf.at[expert], w_sem.at[expert, 2 * tiles]))
        weight_copies.append(mine)

    for group in range(min(depth, groups)):
        for copy in row_copies(group):
            copy.start()
    for mine in weight_copies:
        for copy in mine:
            copy.start()

    for group in range(groups):
        for copy in row_copies(group):
            copy.wait()
        chosen = jnp.dot(
            pick_ref[group], x_buf[group % depth], preferred_element_type=jnp.float32
        ).astype(jnp.bfloat16)
        xs_buf[0, pl.ds(group * slots, slots)] = chosen[:slots]
        xs_buf[1, pl.ds(group * slots, slots)] = chosen[slots:]
        if group + depth < groups:
            for copy in row_copies(group + depth):
                copy.start()

    for expert in range(2):
        for tile in range(tiles):
            weight_copies[expert][2 * tile].wait()
            weight_copies[expert][2 * tile + 1].wait()
            gate = jnp.dot(
                xs_buf[expert], gu_buf[expert, tile, 0], preferred_element_type=jnp.float32
            )
            up = jnp.dot(
                xs_buf[expert], gu_buf[expert, tile, 1], preferred_element_type=jnp.float32
            )
            value = gate / (1.0 + jnp.exp(-gate)) * up
            hid_buf[:, tile * TILE : (tile + 1) * TILE] = value.astype(jnp.bfloat16)
        weight_copies[expert][2 * tiles].wait()
        for column in range(0, width, 2 * TILE):
            served_buf[expert, :, column : column + 2 * TILE] = jnp.dot(
                hid_buf[...],
                dn_buf[expert, :, column : column + 2 * TILE],
                preferred_element_type=jnp.float32,
            ).astype(jnp.bfloat16)

    def out_copies(group):
        return [
            pltpu.make_async_copy(
                y_buf.at[group % depth, :, pl.ds(side * half, half)],
                out_refs[2 * group + side],
                y_sem.at[group, side],
            )
            for side in range(2)
        ]

    for number, group in enumerate(reversed(range(groups))):
        if number >= depth:
            for copy in out_copies(group + depth):
                copy.wait()
        for column in range(0, width, 2 * TILE):
            total = None
            for expert in range(2):
                placed = jnp.dot(
                    place_ref[expert, group],
                    served_buf[expert, pl.ds(group * slots, slots), column : column + 2 * TILE],
                    preferred_element_type=jnp.float32,
                )
                term = placed * share_ref[group, :, expert : expert + 1]
                total = term if total is None else total + term
            y_buf[group % depth, :, column : column + 2 * TILE] = total.astype(jnp.bfloat16)
        for copy in out_copies(group):
            copy.start()
    for group in range(min(depth, groups)):
        for copy in out_copies(group):
            copy.wait()


def run_experts(pieces, pick, place, share, own_gu, far_gu, own_dn, far_dn):
    row_count, width = pieces[0][0].shape
    groups, group_rows, slots = place.shape[1:]
    hidden = own_dn.shape[0]
    tiles = hidden // TILE
    depth = groups if groups * group_rows * width <= 1 << 22 else 2
    anywhere = pl.BlockSpec(memory_space=pl.ANY)
    inside = pl.BlockSpec(memory_space=pltpu.VMEM)
    outs = pl.pallas_call(
        lambda *refs: expert_kernel(row_count, *refs),
        out_shape=[jax.ShapeDtypeStruct((group_rows, width // 2), jnp.bfloat16)] * (2 * groups),
        in_specs=[inside] * 3 + [anywhere] * 14,
        out_specs=[anywhere] * (2 * groups),
        scratch_shapes=[
            pltpu.VMEM((depth, group_rows, width), jnp.bfloat16),
            pltpu.VMEM((2, groups * slots, width), jnp.bfloat16),
            pltpu.VMEM((2, tiles, 2, width, TILE), jnp.bfloat16),
            pltpu.VMEM((2, hidden, width), jnp.bfloat16),
            pltpu.VMEM((groups * slots, hidden), jnp.bfloat16),
            pltpu.VMEM((2, groups * slots, width), jnp.bfloat16),
            pltpu.VMEM((depth, group_rows, width), jnp.bfloat16),
            pltpu.SemaphoreType.DMA((groups, 4)),
            pltpu.SemaphoreType.DMA((2, 2 * tiles + 1)),
            pltpu.SemaphoreType.DMA((groups, 2)),
        ],
        compiler_params=pltpu.CompilerParams(vmem_limit_bytes=56 * 1024 * 1024),
        cost_estimate=pl.CostEstimate(
            flops=12 * groups * slots * width * hidden,
            bytes_accessed=12 * width * hidden + 8 * groups * group_rows * width // 2,
            transcendentals=2 * groups * slots * hidden,
        ),
        name="experts",
    )(pick, place, share, own_gu, far_gu, own_dn, far_dn, *pieces[0], *pieces[1])
    return outs[0::2], outs[1::2]


def per_device(
    hidden_in,
    attn_gain,
    w_query,
    w_keyval,
    q_gain,
    k_gain,
    w_out,
    moe_gain,
    expert_ids,
    gate_fixed,
    w_gateup,
    w_down,
):
    tokens = hidden_in[0].astype(jnp.float32)
    row_count, model_width = tokens.shape
    head_dim = q_gain.shape[0]
    local_heads = w_query.shape[1] // head_dim
    kv_heads = w_keyval.shape[2] // head_dim
    group_size = local_heads * lax.axis_size("rep") // kv_heads
    rep_index = lax.axis_index("rep")
    kv_width = kv_heads * head_dim
    top_count = expert_ids.shape[2]
    expert_count = lax.axis_size(EVERY)

    normed = rms_rows(tokens, attn_gain).astype(jnp.bfloat16)
    pair_rows = swap(normed, "rep", PAIR)
    across_rows = swap(normed, "rep", ACROSS)
    own_keys = jnp.dot(normed, w_keyval[0], preferred_element_type=jnp.float32)
    own_values = jnp.dot(normed, w_keyval[1], preferred_element_type=jnp.float32)
    own_keys = rms_rows(own_keys.reshape(row_count, kv_heads, head_dim), k_gain)
    own_keys = own_keys.reshape(row_count, kv_width).astype(jnp.bfloat16)
    own_kv = jnp.concatenate([own_keys, own_values.astype(jnp.bfloat16)], axis=1)
    line_kv = jnp.concatenate([own_kv] + along_seq(own_kv), axis=0)

    def head_kv(rep):
        index = rep * local_heads // group_size * head_dim
        return jnp.concatenate(
            [
                lax.dynamic_slice_in_dim(line_kv, index, head_dim, 1),
                lax.dynamic_slice_in_dim(line_kv, kv_width + index, head_dim, 1),
            ],
            axis=1,
        )

    far_kv = swap(head_kv(rep_index ^ ACROSS), "rep", ACROSS)
    half_kv = jnp.concatenate([head_kv(rep_index), far_kv], axis=0)
    all_kv = jnp.concatenate([half_kv, swap(half_kv, "rep", PAIR)], axis=0)
    key_rows, value_rows = all_kv[:, :head_dim], all_kv[:, head_dim:]

    corner_rows = swap(across_rows, "rep", PAIR)
    gathered = jnp.concatenate([normed, pair_rows, across_rows, corner_rows], axis=0)
    far_gu = swap(w_gateup[0], "rep", PAIR)
    far_dn = swap(w_down[0], "rep", PAIR)
    projected = jnp.dot(gathered, w_query, preferred_element_type=jnp.float32)
    query_span = projected.shape[0]
    query_part = projected.reshape(query_span, local_heads, head_dim)
    queries = rms_rows(query_part, q_gain).astype(jnp.bfloat16)
    scores = jnp.einsum("qhd,kd->hqk", queries, key_rows, preferred_element_type=jnp.float32)
    scores = scores * head_dim ** (-0.5)
    weights = jnp.exp(scores - jnp.max(scores, axis=2, keepdims=True))
    denom = jnp.sum(weights, axis=2)
    context = jnp.einsum(
        "hqk,kd->qhd", weights.astype(jnp.bfloat16), value_rows, preferred_element_type=jnp.float32
    )
    context = (context / denom.T[:, :, None]).astype(jnp.bfloat16)
    context = context.reshape(query_span, local_heads * head_dim)
    partial = jnp.dot(context, w_out, preferred_element_type=jnp.float32)
    partial = partial.reshape(4, row_count, model_width)
    back = swap(jnp.stack([partial[1], partial[3]]), "rep", PAIR)
    far_sum = (partial[2] + back[1]).astype(jnp.bfloat16)
    mixed = tokens + (partial[0] + back[0]) + swap(far_sum, "rep", ACROSS).astype(jnp.float32)
    moe_in = rms_rows(mixed, moe_gain).astype(jnp.bfloat16)

    routes = spread_routes(jnp.concatenate([expert_ids[0], gate_fixed[0]], axis=1))
    groups, group_rows = routes.shape[:2]
    capacity = max(2, 7 * row_count * top_count // (4 * expert_count))
    slots = -(-capacity * (group_rows // row_count) // 16) * 16
    gates = routes[:, :, top_count:].astype(jnp.float32)
    gate_sum = jnp.sum(gates, axis=2)
    earlier = jnp.tri(group_rows, k=-1, dtype=jnp.bfloat16)
    picks, shares = [], []
    for expert in (lax.axis_index(EVERY), lax.axis_index(EVERY) ^ PAIR):
        named = routes[:, :, :top_count] == expert
        hit = jnp.any(named, axis=2)
        shares.append(jnp.sum(jnp.where(named, gates, 0.0), axis=2) / gate_sum)
        rank = jnp.einsum(
            "ij,gj->gi", earlier, hit.astype(jnp.bfloat16), preferred_element_type=jnp.float32
        )
        rank = jnp.where(hit, rank.astype(jnp.int32), -1)
        picks.append((rank[:, None, :] == jnp.arange(slots)[None, :, None]).astype(jnp.bfloat16))
    pick = jnp.concatenate(picks, axis=1)
    place = jnp.stack([jnp.swapaxes(one, 1, 2) for one in picks])
    share = jnp.stack(shares, axis=2)

    parts = run_experts(
        spread_rows(moe_in), pick, place, share, w_gateup[0], far_gu, w_down[0], far_dn
    )
    routed = collect_rows(parts, row_count)
    return (mixed + routed).astype(jnp.bfloat16)[None]


def solution(mesh):
    placed = (
        P("role", ("seq", "rep"), None),
        P(),
        P(None, "rep"),
        P(),
        P(),
        P(),
        P("rep", None),
        P(),
        P("role", ("seq", "rep"), None),
        P("role", ("seq", "rep"), None),
        P(("role", "seq", "rep"), None, None),
        P(("role", "seq", "rep"), None, None),
    )
    return jax.shard_map(
        per_device,
        mesh=mesh,
        in_specs=placed,
        out_specs=P("role", ("seq", "rep"), None),
        check_vma=False,
    )
```

time: 364 us -> 189 us (0.52)
  waiting for transfers between devices: 248 us -> 80.5 us
  starting transfers between devices: 0.2 us -> 51.7 us
  blocking collectives: 42 us -> 0 us
  matrix products: 39 us -> 6.49 us
  Pallas kernels: 0 us -> 22.3 us
  between operations: 13.4 us -> 0.48 us
  local copies, waits for them, and re-layouts: 8.83 us -> 13.2 us
    reduce_scatter x2 -> x0, waiting for transfers between devices: 172 us -> none  [the longest x1 148 us: per_device(): lax.psum_scatter(weighted, EVERY, scatter_dimension=0, tiled=True)]
    ppermute x0 -> x40, waiting for transfers between devices: none -> 80.5 us  [swap(): return lax.ppermute(block, axis, [(i, i ^ bits) for i in range(size)])]
    all_gather x3 -> x0, waiting for transfers between devices: 76.1 us -> none  [the longest x1 33.9 us: per_device(): everyone = lax.all_gather(everyone, axis, axis=0, tiled=True)]
    ppermute x0 -> x40, starting transfers between devices: none -> 51.7 us  [swap(): return lax.ppermute(block, axis, [(i, i ^ bits) for i in range(size)])]
    all_gather x1 -> x0, blocking collectives: 42 us -> none  [per_device(): lax.all_gather(jnp.concatenate([expert_ids[0], gate_fixed[0]], axis=1), E...]
    dot_general x5, matrix products: 32 us -> 2.84 us  [the longest x1 0.92 us: per_device(): jnp.einsum('hqk,kd->qhd', weights.astype(jnp.bfloat16), value_rows, prefe...]
    pallas_call x0 -> x1, Pallas kernels: none -> 22.3 us  [run_experts(): pl.pallas_call(lambda *refs: expert_kernel(row_count, *refs), out_shape=[...]
    slice x0 -> x7, local copies, waits for them, and re-layouts: none -> 3.86 us  [the longest x2 1.94 us: spread_rows(): corner_high = swap(by_role[:, half:], 'rep', ACROSS)]
  transfers between devices with their start and end apart: 5 -> 40, of which waited for: 5 -> 17; matrix products, arithmetic and copies ran while one was open for 5% -> 13% of each run, Pallas kernels for 0% -> 0%
where the time goes in v2:
time: 189 us; the launch traced here: 188 us
  waiting for transfers between devices  80.5 us (43%)
  starting transfers between devices  51.7 us (27%)
  Pallas kernels  22.3 us (12%)
  other arithmetic  13.7 us (7%)
  local copies, waits for them, and re-layouts  13.2 us (7%)
  matrix products  6.49 us (3%)
    ppermute x40, waiting for transfers between devices, swap(): return lax.ppermute(block, axis, [(i, i ^ bits) for i in range(size)])  80.5 us
    ppermute x40, starting transfers between devices, swap(): return lax.ppermute(block, axis, [(i, i ^ bits) for i in range(size)])  51.7 us
    pallas_call x1, Pallas kernels, run_experts(): pl.pallas_call(lambda *refs: expert_kernel(row_count, *refs), out_shape=[...  22.3 us
    dot_general x2, local copies, waits for them, and re-layouts, per_device(): own_keys = jnp.dot(normed, w_keyval[0], preferred_element_type=jnp.float32)  3.8 us
  transfers between devices with their start and end apart: 40, of which 17 were waited for; matrix products, arithmetic and copies ran while one was open for 13% of the time, Pallas kernels for 0%

profile of v2, /device:TPU:0, one launch (start us, length us, event | category | flops | bytes accessed | tf_op | source)
XLA Modules:
  0.0 188.3 jit_solution(17931336208481038948)
XLA Ops:
  0.0 1.3 fusion.31
  1.3 2.3 %slice_bitcast_fusion = bf16[256,2048]{0,1:T(8,128)(2,1)} fusion(bf16[2,2048,256]{2,1,0:T(8,128)(2,1)} %param.15), kind=kLoop, calls=%fused_computation.31 | loop fusion | bytes 2097152 | tf_op jit(solution)/shard_map/dot_general | solution.py:266
  3.6 1.5 copy.37
  5.1 1.6 convolution_convert_fusion
  7.4 5.1 %collective-permute-start.2 = (bf16[64,512]{1,0:T(8,128)(2,1)S(1)}, bf16[64,512]{1,0:T(8,128)(2,1)S(1)}, u32[]{:S(2)}, u32[]{:S(2)}) collective-permute-start(bf16[64,512]{1,0:T(8,128)(2,1)S(1)} %pad_maximum_fusion.5), channel_id=1, source_target_pairs={{0,12},{4,8},{8,4},{12,0},{1,13},{5,9},{9,5},{13,1},{2,14},{6,10},... | collective-permute-start | bytes 196616 | tf_op jit(solution)/shard_map/ppermute | solution.py:24
  13.1 1.9 %collective-permute-done.2 = bf16[64,512]{1,0:T(8,128)(2,1)S(1)} collective-permute-done((bf16[64,512]{1,0:T(8,128)(2,1)S(1)}, bf16[64,512]{1,0:T(8,128)(2,1)S(1)}, u32[]{:S(2)}, u32[]{:S(2)}) %collective-permute-start.2) | collective-permute-done | bytes 65568 | tf_op jit(solution)/shard_map/ppermute | solution.py:24
  15.1 3.0 %collective-permute-done.1 = bf16[64,512]{1,0:T(8,128)(2,1)S(1)} collective-permute-done((bf16[64,512]{1,0:T(8,128)(2,1)S(1)}, bf16[64,512]{1,0:T(8,128)(2,1)S(1)}, u32[]{:S(2)}, u32[]{:S(2)}) %collective-permute-start.1) | collective-permute-done | bytes 65568 | tf_op jit(solution)/shard_map/ppermute | solution.py:24
  18.2 1.6 collective-permute-start.3
  20.5 4.0 %collective-permute-done.3 = bf16[256,256]{1,0:T(8,128)(2,1)S(1)} collective-permute-done((bf16[256,256]{1,0:T(8,128)(2,1)S(1)}, bf16[256,256]{1,0:T(8,128)(2,1)S(1)}, u32[]{:S(2)}, u32[]{:S(2)}) %collective-permute-start.3) | collective-permute-done | bytes 131104 | tf_op jit(solution)/shard_map/ppermute | solution.py:24
  25.1 3.8 %collective-permute-done.6 = bf16[64,2048]{1,0:T(8,128)(2,1)S(1)} collective-permute-done((bf16[64,2048]{1,0:T(8,128)(2,1)S(1)}, bf16[64,2048]{1,0:T(8,128)(2,1)S(1)}, u32[]{:S(2)}, u32[]{:S(2)}) %collective-permute-start.6) | collective-permute-done | bytes 262176 | tf_op jit(solution)/shard_map/ppermute | solution.py:24
  29.5 1.3 collective-permute-done.7
  30.8 1.6 fusion.18
  32.4 1.2 reshape.128
  34.3 0.7 bitcast_reduce_fusion
  35.7 0.9 fusion.13
  36.7 0.7 fusion.64
  37.5 1.2 pad_maximum_fusion
  39.2 1.8 collective-permute-start.12
  40.9 2.7 %collective-permute-start.10 = (s32[64,16]{0,1:T(8,128)S(1)}, s32[64,16]{0,1:T(8,128)S(1)}, u32[]{:S(2)}, u32[]{:S(2)}) collective-permute-start(s32[64,16]{0,1:T(8,128)S(1)} %pad_add_fusion.3), channel_id=1, source_target_pairs={{0,4},{4,0},{8,12},{12,8},{1,5},{5,1},{9,13},{13,9},{2,6},{6,2},{1... | collective-permute-start | bytes 12296 | tf_op jit(solution)/shard_map/ppermute | solution.py:24
  43.8 1.4 fusion.38
  45.2 1.8 collective-permute-start.9
  47.4 6.5 %collective-permute-done.13 = s32[256,16]{0,1:T(8,128)S(1)} collective-permute-done((s32[256,16]{0,1:T(8,128)S(1)}, s32[256,16]{0,1:T(8,128)S(1)}, u32[]{:S(2)}, u32[]{:S(2)}) %collective-permute-start.13) | collective-permute-done | bytes 16416 | tf_op jit(solution)/shard_map/ppermute | solution.py:24
  54.0 1.7 collective-permute-start.14
  55.7 1.4 multiply_reduce_fusion
  57.9 1.5 collective-permute-start.22
  59.5 2.4 %collective-permute-start.23 = (bf16[64,2048]{1,0:T(8,128)(2,1)S(1)}, bf16[64,2048]{1,0:T(8,128)(2,1)S(1)}, u32[]{:S(2)}, u32[]{:S(2)}) collective-permute-start(bf16[64,2048]{1,0:T(8,128)(2,1)S(1)} %multiply_convert_fusion.refs_7_), channel_id=1, source_target_pairs={{0,12},{4,8},{8,4},{12,0},{1,13},{5,9},{9,5},{13,1},{2,14},{6,10},... | collective-permute-start | bytes 786440 | tf_op jit(solution)/shard_map/ppermute | solution.py:24
  61.9 6.5 %collective-permute-done.21 = bf16[64,2048]{1,0:T(8,128)(2,1)S(1)} collective-permute-done((bf16[64,2048]{1,0:T(8,128)(2,1)S(1)}, bf16[64,2048]{1,0:T(8,128)(2,1)S(1)}, u32[]{:S(2)}, u32[]{:S(2)}) %collective-permute-start.21) | collective-permute-done | bytes 262176 | tf_op jit(solution)/shard_map/ppermute | solution.py:24
  68.5 0.7 constant_dynamic-update-slice_fusion.2
  69.2 10.1 %collective-permute-done.22 = bf16[64,2048]{1,0:T(8,128)(2,1)S(1)} collective-permute-done((bf16[64,2048]{1,0:T(8,128)(2,1)S(1)}, bf16[64,2048]{1,0:T(8,128)(2,1)S(1)}, u32[]{:S(2)}, u32[]{:S(2)}) %collective-permute-start.22) | collective-permute-done | bytes 262176 | tf_op jit(solution)/shard_map/ppermute | solution.py:24
  79.3 0.7 constant_dynamic-update-slice_fusion.1
  80.0 0.7 constant_dynamic-update-slice_fusion.refs_12_
  80.7 1.2 collective-permute-start.25
  82.0 1.5 collective-permute-start.24
  85.0 0.9 slice.118
  85.9 8.6 %collective-permute-done.25.refs_14_ = bf16[192,2048]{1,0:T(8,128)(2,1)} collective-permute-done((bf16[192,2048]{1,0:T(8,128)(2,1)}, bf16[192,2048]{1,0:T(8,128)(2,1)}, u32[]{:S(2)}, u32[]{:S(2)}) %collective-permute-start.25) | collective-permute-done | bytes 786464 | tf_op jit(solution)/shard_map/ppermute | solution.py:24
  94.5 1.5 collective-permute-start.20
  96.0 1.0 slice.120
  97.0 5.7 %collective-permute-done.24.refs_13_ = bf16[192,2048]{1,0:T(8,128)(2,1)} collective-permute-done((bf16[192,2048]{1,0:T(8,128)(2,1)}, bf16[192,2048]{1,0:T(8,128)(2,1)}, u32[]{:S(2)}, u32[]{:S(2)}) %collective-permute-start.24) | collective-permute-done | bytes 786464 | tf_op jit(solution)/shard_map/ppermute | solution.py:24
  102.7 1.5 collective-permute-start.27
  104.2 1.8 slice.119
  106.0 1.4 collective-permute-start.26
  107.4 0.9 add_convert_fusion.3.refs_0_
  108.3 0.8 collective-permute-start.19
  109.1 1.1 copy.44.refs_2_
  110.2 1.0 add_convert_fusion.2.refs_1_
  111.2 4.3 %collective-permute-done.19.refs_10_ = bf16[64,1024]{1,0:T(8,128)(2,1)S(1)} collective-permute-done((bf16[64,1024]{1,0:T(8,128)(2,1)S(1)}, bf16[64,1024]{1,0:T(8,128)(2,1)S(1)}, u32[]{:S(2)}, u32[]{:S(2)}) %collective-permute-start.19) | collective-permute-done | bytes 131104 | tf_op jit(solution)/shard_map/ppermute | solution.py:24
  116.1 22.3 %experts.1 = (bf16[256,1024]{1,0:T(8,128)(2,1)}, bf16[256,1024]{1,0:T(8,128)(2,1)}, bf16[256,1024]{1,0:T(8,128)(2,1)}, bf16[256,1024]{1,0:T(8,128)(2,1)}, bf16[2...) custom-call(bf16[4,224,256]{2,1,0:T(8,128)(2,1)} %add_convert_fusion.3.r, ...), custom_call_target="tpu_custom_call" | custom-call | flops 8455716864 | bytes 27262976 | tf_op jit(solution)/shard_map/experts/pallas_call | solution.py:210
  138.5 1.4 collective-permute-start.29
  139.8 1.5 collective-permute-start.35
  141.8 10.8 %collective-permute-done.29 = bf16[256,1024]{1,0:T(8,128)(2,1)S(1)} collective-permute-done((bf16[256,1024]{1,0:T(8,128)(2,1)}, bf16[256,1024]{1,0:T(8,128)(2,1)S(1)}, u32[]{:S(2)}, u32[]{:S(2)}) %collective-permute-start.29) | collective-permute-done | bytes 524320 | tf_op jit(solution)/shard_map/ppermute | solution.py:24
  152.7 1.2 add_convert_fusion.1
  153.9 1.3 collective-permute-start.30
  155.2 0.8 collective-permute-start.34
  156.0 1.2 add_convert_fusion
  157.3 1.8 collective-permute-start.36
  159.1 4.1 %collective-permute-done.30 = bf16[256,1024]{1,0:T(8,128)(2,1)S(1)} collective-permute-done((bf16[256,1024]{1,0:T(8,128)(2,1)S(1)}, bf16[256,1024]{1,0:T(8,128)(2,1)S(1)}, u32[]{:S(2)}, u32[]{:S(2)}) %collective-permute-start.30) | collective-permute-done | bytes 524320 | tf_op jit(solution)/shard_map/ppermute | solution.py:24
  163.5 7.7 %collective-permute-start.31 = (bf16[64,1024]{1,0:T(8,128)(2,1)S(1)}, bf16[64,1024]{1,0:T(8,128)(2,1)S(1)}, u32[]{:S(2)}, u32[]{:S(2)}) collective-permute-start(bf16[64,1024]{1,0:T(8,128)(2,1)S(1)} %get-tuple-element.34), channel_id=1, source_target_pairs={{0,4},{4,0},{8,12},{12,8},{1,5},{5,1},{9,13},{13,9},{2,6},{6,2},{1... | collective-permute-start | bytes 393224 | tf_op jit(solution)/shard_map/ppermute | solution.py:24
  171.2 1.5 collective-permute-start.33
  173.1 3.7 %collective-permute-start.37 = (bf16[64,1024]{1,0:T(8,128)(2,1)S(1)}, bf16[64,1024]{1,0:T(8,128)(2,1)S(1)}, u32[]{:S(2)}, u32[]{:S(2)}) collective-permute-start(bf16[64,1024]{1,0:T(8,128)(2,1)S(1)} %get-tuple-element.37), channel_id=1, source_target_pairs={{0,4},{4,0},{8,12},{12,8},{1,5},{5,1},{9,13},{13,9},{2,6},{6,2},{1... | collective-permute-start | bytes 393224 | tf_op jit(solution)/shard_map/ppermute | solution.py:24
  176.8 1.5 collective-permute-start.39
  178.4 3.5 %collective-permute-done.32 = bf16[64,1024]{1,0:T(8,128)(2,1)S(1)} collective-permute-done((bf16[64,1024]{1,0:T(8,128)(2,1)S(1)}, bf16[64,1024]{1,0:T(8,128)(2,1)S(1)}, u32[]{:S(2)}, u32[]{:S(2)}) %collective-permute-start.32) | collective-permute-done | bytes 131104 | tf_op jit(solution)/shard_map/ppermute | solution.py:24
  181.9 1.8 collective-permute-done.39
  183.7 3.8 %collective-permute-done.38 = bf16[64,1024]{1,0:T(8,128)(2,1)S(1)} collective-permute-done((bf16[64,1024]{1,0:T(8,128)(2,1)S(1)}, bf16[64,1024]{1,0:T(8,128)(2,1)S(1)}, u32[]{:S(2)}, u32[]{:S(2)}) %collective-permute-start.38) | collective-permute-done | bytes 131104 | tf_op jit(solution)/shard_map/ppermute | solution.py:24
  187.5 0.8 fusion.41
  (115 shorter events, 10.3 us)
Async XLA Ops:
  0.0 36.7 %copy-start = (bf16[512,2048]{1,0:T(8,128)(2,1)S(1)}, bf16[512,2048]{1,0:T(8,128)(2,1)}, u32[]{:S(2)}) copy-start(bf16[512,2048]{1,0:T(8,128)(2,1)} %param.18) | copy-start | bytes 6291460
  1.3 3.8 %copy-start.2 = (bf16[1,64,2048]{2,1,0:T(8,128)(2,1)S(1)}, bf16[1,64,2048]{2,1,0:T(8,128)(2,1)}, u32[]{:S(2)}) copy-start(bf16[1,64,2048]{2,1,0:T(8,128)(2,1)} %param.12) | copy-start | bytes 786436
  1.3 3.8 %copy-start.10 = (f32[2048]{0:T(1024)S(1)}, f32[2048]{0:T(1024)}, u32[]{:S(2)}) copy-start(f32[2048]{0:T(1024)} %param.13) | copy-start | bytes 24580
  3.6 3.6 %copy-start.12 = (f32[128]{0:T(128)S(1)}, f32[128]{0:T(128)}, u32[]{:S(2)}) copy-start(f32[128]{0:T(128)} %param.17) | copy-start | bytes 1540
  7.4 7.7 %collective-permute-start.2 = (bf16[64,512]{1,0:T(8,128)(2,1)S(1)}, bf16[64,512]{1,0:T(8,128)(2,1)S(1)}, u32[]{:S(2)}, u32[]{:S(2)}) collective-permute-start(bf16[64,512]{1,0:T(8,128)(2,1)S(1)} %pad_maximum_fusion.5), channel_id=1, source_target_pairs={{0,12},{4,8},{8,4},{12,0},{1,13},{5,9},{9,5},{13,1},{2,14},{6,10},... | collective-permute-start | bytes 196616 | tf_op jit(solution)/shard_map/ppermute | solution.py:24
  12.5 5.6 %collective-permute-start.1 = (bf16[64,512]{1,0:T(8,128)(2,1)S(1)}, bf16[64,512]{1,0:T(8,128)(2,1)S(1)}, u32[]{:S(2)}, u32[]{:S(2)}) collective-permute-start(bf16[64,512]{1,0:T(8,128)(2,1)S(1)} %pad_maximum_fusion.5), channel_id=1, source_target_pairs={{0,8},{4,12},{8,0},{12,4},{1,9},{5,13},{9,1},{13,5},{2,10},{6,14},... | collective-permute-start | bytes 196616 | tf_op jit(solution)/shard_map/ppermute | solution.py:24
  12.5 5.6 %collective-permute-start = (bf16[64,512]{1,0:T(8,128)(2,1)S(1)}, bf16[64,512]{1,0:T(8,128)(2,1)S(1)}, u32[]{:S(2)}, u32[]{:S(2)}) collective-permute-start(bf16[64,512]{1,0:T(8,128)(2,1)S(1)} %pad_maximum_fusion.5), channel_id=1, source_target_pairs={{0,4},{4,0},{8,12},{12,8},{1,5},{5,1},{9,13},{13,9},{2,6},{6,2},{1... | collective-permute-start | bytes 196616 | tf_op jit(solution)/shard_map/ppermute | solution.py:24
  13.1 17.7 %copy-start.14 = (bf16[2048,512]{1,0:T(8,128)(2,1)S(1)}, bf16[2048,512]{1,0:T(8,128)(2,1)}, u32[]{:S(2)}) copy-start(bf16[2048,512]{1,0:T(8,128)(2,1)} %param.14) | copy-start | bytes 6291460
  18.2 6.3 %collective-permute-start.3 = (bf16[256,256]{1,0:T(8,128)(2,1)S(1)}, bf16[256,256]{1,0:T(8,128)(2,1)S(1)}, u32[]{:S(2)}, u32[]{:S(2)}) collective-permute-start(bf16[256,256]{1,0:T(8,128)(2,1)S(1)} %pad_maximum_fusion.4), channel_id=1, source_target_pairs={{0,2},{1,3},{2,0},{3,1},{4,6},{5,7},{6,4},{7,5},{8,10},{9,11},{10,... | collective-permute-start | bytes 393224 | tf_op jit(solution)/shard_map/ppermute | solution.py:24
  19.9 9.0 %collective-permute-start.6 = (bf16[64,2048]{1,0:T(8,128)(2,1)S(1)}, bf16[64,2048]{1,0:T(8,128)(2,1)S(1)}, u32[]{:S(2)}, u32[]{:S(2)}) collective-permute-start(bf16[64,2048]{1,0:T(8,128)(2,1)S(1)} %fusion.33), channel_id=1, source_target_pairs={{0,2},{1,3},{2,0},{3,1},{4,6},{5,7},{6,4},{7,5},{8,10},{9,11},{10,... | collective-permute-start | bytes 786440 | tf_op jit(solution)/shard_map/ppermute | solution.py:24
  24.5 4.9 %collective-permute-start.4 = (bf16[512,256]{1,0:T(8,128)(2,1)S(1)}, bf16[512,256]{1,0:T(8,128)(2,1)S(1)}, u32[]{:S(2)}, u32[]{:S(2)}) collective-permute-start(bf16[512,256]{1,0:T(8,128)(2,1)S(1)} %pad_maximum_fusion.3), channel_id=1, source_target_pairs={{0,1},{1,0},{2,3},{3,2},{4,5},{5,4},{6,7},{7,6},{8,9},{9,8},{10,11... | collective-permute-start | bytes 786440 | tf_op jit(solution)/shard_map/ppermute | solution.py:24
  24.6 4.9 %collective-permute-start.5 = (bf16[64,2048]{1,0:T(8,128)(2,1)S(1)}, bf16[64,2048]{1,0:T(8,128)(2,1)S(1)}, u32[]{:S(2)}, u32[]{:S(2)}) collective-permute-start(bf16[64,2048]{1,0:T(8,128)(2,1)S(1)} %fusion.33), channel_id=1, source_target_pairs={{0,1},{1,0},{2,3},{3,2},{4,5},{5,4},{6,7},{7,6},{8,9},{9,8},{10,11... | collective-permute-start | bytes 786440 | tf_op jit(solution)/shard_map/ppermute | solution.py:24
  28.9 1.9 collective-permute-start.7
  28.9 86.6 %collective-permute-start.15 = (bf16[2048,1536]{1,0:T(8,128)(2,1)}, bf16[2048,1536]{1,0:T(8,128)(2,1)}, u32[]{:S(2)}, u32[]{:S(2)}) collective-permute-start(bf16[2048,1536]{1,0:T(8,128)(2,1)} %bitcast.117), channel_id=1, source_target_pairs={{0,1},{1,0},{2,3},{3,2},{4,5},{5,4},{6,7},{7,6},{8,9},{9,8},{10,11... | collective-permute-start | bytes 18874376 | tf_op jit(solution)/shard_map/ppermute | solution.py:24
  29.5 4.5 %copy-start.13 = (f32[128]{0:T(128)S(1)}, f32[128]{0:T(128)}, u32[]{:S(2)}) copy-start(f32[128]{0:T(128)} %param.16) | copy-start | bytes 1540
  37.4 1.6 copy-start.1
  37.4 1.8 copy-start.8
  37.4 1.8 copy-start.9
  39.1 18.1 %copy-start.11 = (f32[2048]{0:T(1024)S(1)}, f32[2048]{0:T(1024)}, u32[]{:S(2)}) copy-start(f32[2048]{0:T(1024)} %param.19) | copy-start | bytes 24580
  39.1 4.6 %collective-permute-start.8 = (f32[2,64,2048]{2,1,0:T(8,128)}, f32[2,64,2048]{2,1,0:T(8,128)S(1)}, u32[]{:S(2)}, u32[]{:S(2)}) collective-permute-start(f32[2,64,2048]{2,1,0:T(8,128)} %pad_maximum_fusion), channel_id=1, source_target_pairs={{0,1},{1,0},{2,3},{3,2},{4,5},{5,4},{6,7},{7,6},{8,9},{9,8},{10,11... | collective-permute-start | bytes 3145736 | tf_op jit(solution)/shard_map/ppermute | solution.py:24
  39.2 6.0 %collective-permute-start.12 = (s32[64,16]{0,1:T(8,128)S(1)}, s32[64,16]{0,1:T(8,128)S(1)}, u32[]{:S(2)}, u32[]{:S(2)}) collective-permute-start(s32[64,16]{0,1:T(8,128)S(1)} %pad_add_fusion.3), channel_id=1, source_target_pairs={{0,12},{4,8},{8,4},{12,0},{1,13},{5,9},{9,5},{13,1},{2,14},{6,10},... | collective-permute-start | bytes 12296 | tf_op jit(solution)/shard_map/ppermute | solution.py:24
  40.9 6.0 %collective-permute-start.11 = (s32[64,16]{0,1:T(8,128)S(1)}, s32[64,16]{0,1:T(8,128)S(1)}, u32[]{:S(2)}, u32[]{:S(2)}) collective-permute-start(s32[64,16]{0,1:T(8,128)S(1)} %pad_add_fusion.3), channel_id=1, source_target_pairs={{0,8},{4,12},{8,0},{12,4},{1,9},{5,13},{9,1},{13,5},{2,10},{6,14},... | collective-permute-start | bytes 12296 | tf_op jit(solution)/shard_map/ppermute | solution.py:24
  40.9 6.0 %collective-permute-start.10 = (s32[64,16]{0,1:T(8,128)S(1)}, s32[64,16]{0,1:T(8,128)S(1)}, u32[]{:S(2)}, u32[]{:S(2)}) collective-permute-start(s32[64,16]{0,1:T(8,128)S(1)} %pad_add_fusion.3), channel_id=1, source_target_pairs={{0,4},{4,0},{8,12},{12,8},{1,5},{5,1},{9,13},{13,9},{2,6},{6,2},{1... | collective-permute-start | bytes 12296 | tf_op jit(solution)/shard_map/ppermute | solution.py:24
  43.7 12.0 %copy-start.3 = (f32[2,64,2048]{2,1,0:T(8,128)}, f32[2,64,2048]{2,1,0:T(8,128)S(1)}, u32[]{:S(2)}) copy-start(f32[2,64,2048]{2,1,0:T(8,128)S(1)} %collective-permute-done.8) | copy-start | bytes 3145732
  43.7 71.8 %collective-permute-start.16 = (bf16[768,2048]{1,0:T(8,128)(2,1)}, bf16[768,2048]{1,0:T(8,128)(2,1)}, u32[]{:S(2)}, u32[]{:S(2)}) collective-permute-start(bf16[768,2048]{1,0:T(8,128)(2,1)} %bitcast.119), channel_id=1, source_target_pairs={{0,1},{1,0},{2,3},{3,2},{4,5},{5,4},{6,7},{7,6},{8,9},{9,8},{10,11... | collective-permute-start | bytes 9437192 | tf_op jit(solution)/shard_map/ppermute | solution.py:24
  45.2 10.5 %collective-permute-start.9 = (bf16[64,2048]{1,0:T(8,128)(2,1)S(1)}, bf16[64,2048]{1,0:T(8,128)(2,1)S(1)}, u32[]{:S(2)}, u32[]{:S(2)}) collective-permute-start(bf16[64,2048]{1,0:T(8,128)(2,1)S(1)} %fusion.38), channel_id=1, source_target_pairs={{0,2},{1,3},{2,0},{3,1},{4,6},{5,7},{6,4},{7,5},{8,10},{9,11},{10,... | collective-permute-start | bytes 786440 | tf_op jit(solution)/shard_map/ppermute | solution.py:24
  47.0 6.9 %collective-permute-start.13 = (s32[256,16]{0,1:T(8,128)S(1)}, s32[256,16]{0,1:T(8,128)S(1)}, u32[]{:S(2)}, u32[]{:S(2)}) collective-permute-start(s32[256,16]{0,1:T(8,128)S(1)} %pad_add_fusion.2), channel_id=1, source_target_pairs={{0,2},{1,3},{2,0},{3,1},{4,6},{5,7},{6,4},{7,5},{8,10},{9,11},{10,... | collective-permute-start | bytes 49160 | tf_op jit(solution)/shard_map/ppermute | solution.py:24
  54.0 3.9 %collective-permute-start.14 = (s32[2,256,16]{1,2,0:T(8,128)S(1)}, s32[2,256,16]{1,2,0:T(8,128)S(1)}, u32[]{:S(2)}, u32[]{:S(2)}) collective-permute-start(s32[2,256,16]{1,2,0:T(8,128)S(1)} %pad_add_fusion.1), channel_id=1, source_target_pairs={{0,16},{16,0},{1,17},{17,1},{2,18},{18,2},{3,19},{19,3},{4,20},{20... | collective-permute-start | bytes 98312 | tf_op jit(solution)/shard_map/ppermute | solution.py:24
  57.2 48.8 %copy-start.6 = (bf16[64,2048]{1,0:T(8,128)(2,1)}, bf16[64,2048]{1,0:T(8,128)(2,1)S(1)}, u32[]{:S(2)}) copy-start(bf16[64,2048]{1,0:T(8,128)(2,1)S(1)} %multiply_convert_fusion.refs_7_) | copy-start | bytes 786436
  57.3 11.2 %collective-permute-start.21 = (bf16[64,2048]{1,0:T(8,128)(2,1)S(1)}, bf16[64,2048]{1,0:T(8,128)(2,1)S(1)}, u32[]{:S(2)}, u32[]{:S(2)}) collective-permute-start(bf16[64,2048]{1,0:T(8,128)(2,1)S(1)} %multiply_convert_fusion.refs_7_), channel_id=1, source_target_pairs={{0,4},{4,0},{8,12},{12,8},{1,5},{5,1},{9,13},{13,9},{2,6},{6,2},{1... | collective-permute-start | bytes 786440 | tf_op jit(solution)/shard_map/ppermute | solution.py:24
  57.9 21.4 %collective-permute-start.22 = (bf16[64,2048]{1,0:T(8,128)(2,1)S(1)}, bf16[64,2048]{1,0:T(8,128)(2,1)S(1)}, u32[]{:S(2)}, u32[]{:S(2)}) collective-permute-start(bf16[64,2048]{1,0:T(8,128)(2,1)S(1)} %multiply_convert_fusion.refs_7_), channel_id=1, source_target_pairs={{0,8},{4,12},{8,0},{12,4},{1,9},{5,13},{9,1},{13,5},{2,10},{6,14},... | collective-permute-start | bytes 786440 | tf_op jit(solution)/shard_map/ppermute | solution.py:24
  59.5 20.5 %collective-permute-start.23 = (bf16[64,2048]{1,0:T(8,128)(2,1)S(1)}, bf16[64,2048]{1,0:T(8,128)(2,1)S(1)}, u32[]{:S(2)}, u32[]{:S(2)}) collective-permute-start(bf16[64,2048]{1,0:T(8,128)(2,1)S(1)} %multiply_convert_fusion.refs_7_), channel_id=1, source_target_pairs={{0,12},{4,8},{8,4},{12,0},{1,13},{5,9},{9,5},{13,1},{2,14},{6,10},... | collective-permute-start | bytes 786440 | tf_op jit(solution)/shard_map/ppermute | solution.py:24
  68.5 15.5 %collective-permute-start.18 = (bf16[64,2048]{1,0:T(8,128)(2,1)S(1)}, bf16[64,2048]{1,0:T(8,128)(2,1)}, u32[]{:S(2)}, u32[]{:S(2)}) collective-permute-start(bf16[64,2048]{1,0:T(8,128)(2,1)S(1)} %multiply_convert_fusion.refs_7_), channel_id=1, source_target_pairs={{0,16},{16,0},{1,17},{17,1},{2,18},{18,2},{3,19},{19,3},{4,20},{20... | collective-permute-start | bytes 786440 | tf_op jit(solution)/shard_map/ppermute | solution.py:24
  80.7 13.8 %collective-permute-start.25 = (bf16[192,2048]{1,0:T(8,128)(2,1)}, bf16[192,2048]{1,0:T(8,128)(2,1)}, u32[]{:S(2)}, u32[]{:S(2)}) collective-permute-start(bf16[192,2048]{1,0:T(8,128)(2,1)} %constant_dynamic-update-slice_fusion.refs_12_), channel_id=1, source_target_pairs={{0,16},{16,0},{1,17},{17,1},{2,18},{18,2},{3,19},{19,3},{4,20},{20... | collective-permute-start | bytes 2359304 | tf_op jit(solution)/shard_map/ppermute | solution.py:24
  82.0 20.8 %collective-permute-start.24 = (bf16[192,2048]{1,0:T(8,128)(2,1)}, bf16[192,2048]{1,0:T(8,128)(2,1)}, u32[]{:S(2)}, u32[]{:S(2)}) collective-permute-start(bf16[192,2048]{1,0:T(8,128)(2,1)} %constant_dynamic-update-slice_fusion.refs_12_), channel_id=1, source_target_pairs={{0,2},{1,3},{2,0},{3,1},{4,6},{5,7},{6,4},{7,5},{8,10},{9,11},{10,... | collective-permute-start | bytes 2359304 | tf_op jit(solution)/shard_map/ppermute | solution.py:24
  84.0 22.1 %collective-permute-start.17 = (bf16[64,2048]{1,0:T(8,128)(2,1)S(1)}, bf16[64,2048]{1,0:T(8,128)(2,1)S(1)}, u32[]{:S(2)}, u32[]{:S(2)}) collective-permute-start(bf16[64,2048]{1,0:T(8,128)(2,1)S(1)} %multiply_convert_fusion.refs_7_), channel_id=1, source_target_pairs={{0,2},{1,3},{2,0},{3,1},{4,6},{5,7},{6,4},{7,5},{8,10},{9,11},{10,... | collective-permute-start | bytes 786440 | tf_op jit(solution)/shard_map/ppermute | solution.py:24
  94.5 13.8 %collective-permute-start.20 = (bf16[64,1024]{1,0:T(8,128)(2,1)S(1)}, bf16[64,1024]{1,0:T(8,128)(2,1)S(1)}, u32[]{:S(2)}, u32[]{:S(2)}) collective-permute-start(bf16[64,1024]{1,0:T(8,128)(2,1)S(1)} %slice.118), channel_id=1, source_target_pairs={{0,2},{1,3},{2,0},{3,1},{4,6},{5,7},{6,4},{7,5},{8,10},{9,11},{10,... | collective-permute-start | bytes 393224 | tf_op jit(solution)/shard_map/ppermute | solution.py:24
  102.7 12.7 %collective-permute-start.27 = (bf16[192,1024]{1,0:T(8,128)(2,1)S(1)}, bf16[192,1024]{1,0:T(8,128)(2,1)}, u32[]{:S(2)}, u32[]{:S(2)}) collective-permute-start(bf16[192,1024]{1,0:T(8,128)(2,1)S(1)} %slice.120), channel_id=1, source_target_pairs={{0,2},{1,3},{2,0},{3,1},{4,6},{5,7},{6,4},{7,5},{8,10},{9,11},{10,... | collective-permute-start | bytes 1179656 | tf_op jit(solution)/shard_map/ppermute | solution.py:24
  106.0 3.1 %copy-start.7 = (bf16[64,2048]{1,0:T(8,128)(2,1)}, bf16[64,2048]{1,0:T(8,128)(2,1)S(1)}, u32[]{:S(2)}) copy-start(bf16[64,2048]{1,0:T(8,128)(2,1)S(1)} %collective-permute-done.17.refs_8_) | copy-start | bytes 786436
  106.0 9.5 %collective-permute-start.26 = (bf16[192,1024]{1,0:T(8,128)(2,1)}, bf16[192,1024]{1,0:T(8,128)(2,1)}, u32[]{:S(2)}, u32[]{:S(2)}) collective-permute-start(bf16[192,1024]{1,0:T(8,128)(2,1)} %slice.119), channel_id=1, source_target_pairs={{0,16},{16,0},{1,17},{17,1},{2,18},{18,2},{3,19},{19,3},{4,20},{20... | collective-permute-start | bytes 1179656 | tf_op jit(solution)/shard_map/ppermute | solution.py:24
  108.3 0.8 copy-start.15
  108.3 7.2 %collective-permute-start.19 = (bf16[64,1024]{1,0:T(8,128)(2,1)S(1)}, bf16[64,1024]{1,0:T(8,128)(2,1)S(1)}, u32[]{:S(2)}, u32[]{:S(2)}) collective-permute-start(bf16[64,1024]{1,0:T(8,128)(2,1)S(1)} %slice.117), channel_id=1, source_target_pairs={{0,16},{16,0},{1,17},{17,1},{2,18},{18,2},{3,19},{19,3},{4,20},{20... | collective-permute-start | bytes 393224 | tf_op jit(solution)/shard_map/ppermute | solution.py:24
  115.5 0.7 copy-start.16
  138.5 24.7 %copy-start.5 = (bf16[256,1024]{1,0:T(8,128)(2,1)S(1)}, bf16[256,1024]{1,0:T(8,128)(2,1)}, u32[]{:S(2)}) copy-start(bf16[256,1024]{1,0:T(8,128)(2,1)} %get-tuple-element.13) | copy-start | bytes 1572868
  138.5 14.2 %collective-permute-start.29 = (bf16[256,1024]{1,0:T(8,128)(2,1)}, bf16[256,1024]{1,0:T(8,128)(2,1)S(1)}, u32[]{:S(2)}, u32[]{:S(2)}) collective-permute-start(bf16[256,1024]{1,0:T(8,128)(2,1)} %get-tuple-element.16), channel_id=1, source_target_pairs={{0,16},{16,0},{1,17},{17,1},{2,18},{18,2},{3,19},{19,3},{4,20},{20... | collective-permute-start | bytes 1572872 | tf_op jit(solution)/shard_map/ppermute | solution.py:24
  139.8 16.2 %collective-permute-start.35 = (bf16[256,1024]{1,0:T(8,128)(2,1)}, bf16[256,1024]{1,0:T(8,128)(2,1)S(1)}, u32[]{:S(2)}, u32[]{:S(2)}) collective-permute-start(bf16[256,1024]{1,0:T(8,128)(2,1)} %get-tuple-element.20), channel_id=1, source_target_pairs={{0,2},{1,3},{2,0},{3,1},{4,6},{5,7},{6,4},{7,5},{8,10},{9,11},{10,... | collective-permute-start | bytes 1572872 | tf_op jit(solution)/shard_map/ppermute | solution.py:24
  141.3 17.8 %collective-permute-start.28 = (bf16[256,1024]{1,0:T(8,128)(2,1)}, bf16[256,1024]{1,0:T(8,128)(2,1)S(1)}, u32[]{:S(2)}, u32[]{:S(2)}) collective-permute-start(bf16[256,1024]{1,0:T(8,128)(2,1)} %get-tuple-element.14), channel_id=1, source_target_pairs={{0,16},{16,0},{1,17},{17,1},{2,18},{18,2},{3,19},{19,3},{4,20},{20... | collective-permute-start | bytes 1572872 | tf_op jit(solution)/shard_map/ppermute | solution.py:24
  153.9 9.2 %collective-permute-start.30 = (bf16[256,1024]{1,0:T(8,128)(2,1)S(1)}, bf16[256,1024]{1,0:T(8,128)(2,1)S(1)}, u32[]{:S(2)}, u32[]{:S(2)}) collective-permute-start(bf16[256,1024]{1,0:T(8,128)(2,1)S(1)} %add_convert_fusion.1), channel_id=1, source_target_pairs={{0,2},{1,3},{2,0},{3,1},{4,6},{5,7},{6,4},{7,5},{8,10},{9,11},{10,... | collective-permute-start | bytes 1572872 | tf_op jit(solution)/shard_map/ppermute | solution.py:24
  155.2 17.5 %collective-permute-start.34 = (bf16[256,1024]{1,0:T(8,128)(2,1)}, bf16[256,1024]{1,0:T(8,128)(2,1)S(1)}, u32[]{:S(2)}, u32[]{:S(2)}) collective-permute-start(bf16[256,1024]{1,0:T(8,128)(2,1)} %get-tuple-element.18), channel_id=1, source_target_pairs={{0,2},{1,3},{2,0},{3,1},{4,6},{5,7},{6,4},{7,5},{8,10},{9,11},{10,... | collective-permute-start | bytes 1572872 | tf_op jit(solution)/shard_map/ppermute | solution.py:24
  157.3 15.5 %copy-start.4 = (bf16[256,1024]{1,0:T(8,128)(2,1)S(1)}, bf16[256,1024]{1,0:T(8,128)(2,1)}, u32[]{:S(2)}) copy-start(bf16[256,1024]{1,0:T(8,128)(2,1)} %get-tuple-element.17) | copy-start | bytes 1572868
  157.3 15.5 %collective-permute-start.36 = (bf16[256,1024]{1,0:T(8,128)(2,1)S(1)}, bf16[256,1024]{1,0:T(8,128)(2,1)S(1)}, u32[]{:S(2)}, u32[]{:S(2)}) collective-permute-start(bf16[256,1024]{1,0:T(8,128)(2,1)S(1)} %add_convert_fusion), channel_id=1, source_target_pairs={{0,16},{16,0},{1,17},{17,1},{2,18},{18,2},{3,19},{19,3},{4,20},{20... | collective-permute-start | bytes 1572872 | tf_op jit(solution)/shard_map/ppermute | solution.py:24
  163.5 14.8 %collective-permute-start.31 = (bf16[64,1024]{1,0:T(8,128)(2,1)S(1)}, bf16[64,1024]{1,0:T(8,128)(2,1)S(1)}, u32[]{:S(2)}, u32[]{:S(2)}) collective-permute-start(bf16[64,1024]{1,0:T(8,128)(2,1)S(1)} %get-tuple-element.34), channel_id=1, source_target_pairs={{0,4},{4,0},{8,12},{12,8},{1,5},{5,1},{9,13},{13,9},{2,6},{6,2},{1... | collective-permute-start | bytes 393224 | tf_op jit(solution)/shard_map/ppermute | solution.py:24
  171.2 7.2 %collective-permute-start.33 = (bf16[64,1024]{1,0:T(8,128)(2,1)S(1)}, bf16[64,1024]{1,0:T(8,128)(2,1)S(1)}, u32[]{:S(2)}, u32[]{:S(2)}) collective-permute-start(bf16[64,1024]{1,0:T(8,128)(2,1)S(1)} %get-tuple-element.35), channel_id=1, source_target_pairs={{0,12},{4,8},{8,4},{12,0},{1,13},{5,9},{9,5},{13,1},{2,14},{6,10},... | collective-permute-start | bytes 393224 | tf_op jit(solution)/shard_map/ppermute | solution.py:24
  172.7 9.2 %collective-permute-start.32 = (bf16[64,1024]{1,0:T(8,128)(2,1)S(1)}, bf16[64,1024]{1,0:T(8,128)(2,1)S(1)}, u32[]{:S(2)}, u32[]{:S(2)}) collective-permute-start(bf16[64,1024]{1,0:T(8,128)(2,1)S(1)} %get-tuple-element.36), channel_id=1, source_target_pairs={{0,8},{4,12},{8,0},{12,4},{1,9},{5,13},{9,1},{13,5},{2,10},{6,14},... | collective-permute-start | bytes 393224 | tf_op jit(solution)/shard_map/ppermute | solution.py:24
  173.1 8.8 %collective-permute-start.37 = (bf16[64,1024]{1,0:T(8,128)(2,1)S(1)}, bf16[64,1024]{1,0:T(8,128)(2,1)S(1)}, u32[]{:S(2)}, u32[]{:S(2)}) collective-permute-start(bf16[64,1024]{1,0:T(8,128)(2,1)S(1)} %get-tuple-element.37), channel_id=1, source_target_pairs={{0,4},{4,0},{8,12},{12,8},{1,5},{5,1},{9,13},{13,9},{2,6},{6,2},{1... | collective-permute-start | bytes 393224 | tf_op jit(solution)/shard_map/ppermute | solution.py:24
  176.8 6.9 %collective-permute-start.39 = (bf16[64,1024]{1,0:T(8,128)(2,1)S(1)}, bf16[64,1024]{1,0:T(8,128)(2,1)S(1)}, u32[]{:S(2)}, u32[]{:S(2)}) collective-permute-start(bf16[64,1024]{1,0:T(8,128)(2,1)S(1)} %get-tuple-element.38), channel_id=1, source_target_pairs={{0,12},{4,8},{8,4},{12,0},{1,13},{5,9},{9,5},{13,1},{2,14},{6,10},... | collective-permute-start | bytes 393224 | tf_op jit(solution)/shard_map/ppermute | solution.py:24
  178.3 9.2 %collective-permute-start.38 = (bf16[64,1024]{1,0:T(8,128)(2,1)S(1)}, bf16[64,1024]{1,0:T(8,128)(2,1)S(1)}, u32[]{:S(2)}, u32[]{:S(2)}) collective-permute-start(bf16[64,1024]{1,0:T(8,128)(2,1)S(1)} %get-tuple-element.39), channel_id=1, source_target_pairs={{0,8},{4,12},{8,0},{12,4},{1,9},{5,13},{9,1},{13,5},{2,10},{6,14},... | collective-permute-start | bytes 393224 | tf_op jit(solution)/shard_map/ppermute | solution.py:24

commit v3 on v2

v3 whole, which is shorter than its diff:
```python
import jax
import jax.numpy as jnp
from jax import lax
from jax.experimental import pallas as pl
from jax.experimental.pallas import tpu as pltpu
from jax.sharding import PartitionSpec as P

EVERY = ("role", "seq", "rep")
PAIR = 1
ACROSS = 2
TILE = 256


def rms_rows(values_in, gain_vec):
    return (
        values_in
        * lax.rsqrt(jnp.mean(values_in * values_in, axis=-1, keepdims=True) + 1e-06)
        * gain_vec
    )


def swap(block, axis, bits):
    size = lax.axis_size(axis)
    return lax.ppermute(block, axis, [(i, i ^ bits) for i in range(size)])


def seq_bits():
    size = lax.axis_size("seq")
    return [1 << place for place in reversed(range(size.bit_length() - 1))]


def seq_blocks(own):
    blocks = [own]
    for bits in seq_bits():
        blocks = blocks + [swap(block, "seq", bits) for block in blocks]
    return blocks


def spread_routes(own):
    near = jnp.concatenate(seq_blocks(own), axis=0)
    both = jnp.stack([near, swap(near, "rep", ACROSS)])
    return jnp.concatenate([both, swap(both, "role", 1)], axis=0)


def ready(*arrays):
    return lax.optimization_barrier(arrays)


def spread_rows(own, early_work):
    half = own.shape[1] // 2

    def both_ways(part):
        return swap(part, "rep", ACROSS), swap(part, "role", 1)

    def corners(by_rep, by_role):
        return swap(by_rep[:, :half], "role", 1), swap(by_role[:, half:], "rep", ACROSS)

    first_bits, *bits_left = seq_bits()
    blocks = [own, swap(own, "seq", first_bits)]
    for bits in bits_left[:-1]:
        blocks = blocks + [swap(block, "seq", bits) for block in blocks]
    beyond = [swap(block, "seq", bits_left[-1]) for block in blocks[:-1]]
    outer = both_ways(own)
    middle = jnp.concatenate(blocks[1:] + beyond, axis=0)
    middle, by_rep, by_role = ready(middle, *outer)
    outer = by_rep, by_role
    last = swap(blocks[-1], "seq", bits_left[-1])
    rows = own.shape[0] + middle.shape[0] + last.shape[0]
    inner = both_ways(middle)
    outer_corner = corners(*outer)
    last, *outer_corner = ready(last, *outer_corner)
    final = both_ways(last)
    inner_corner = corners(*inner)
    early = early_work([(0, 0, own), (own.shape[0], 0, middle), (rows - last.shape[0], 0, last)])
    by_rep, by_role, *early = ready(*final, *early)
    final_corner = corners(by_rep, by_role)
    groups = [[], [], []]
    start = 0
    for part, beside, corner in (
        (own, outer, outer_corner),
        (middle, inner, inner_corner),
        (last, final, final_corner),
    ):
        groups[0].append((start, 0, beside[0]))
        groups[1].append((start, 0, beside[1]))
        groups[2].append((start, 0, corner[0]))
        groups[2].append((start, half, corner[1]))
        start += part.shape[0]
    return early, groups


def added(first, second):
    return (first.astype(jnp.float32) + second.astype(jnp.float32)).astype(jnp.bfloat16)


def collect_rows(near, by_rep, by_role, corner):
    straight_low = swap(by_role[0], "role", 1)
    straight_high = swap(by_rep[1], "rep", ACROSS)
    straight_low, straight_high, *corner = ready(straight_low, straight_high, *corner)
    corner_low, corner_high = ready(
        swap(corner[0], "role", 1), swap(corner[1], "rep", ACROSS)
    )
    cut = near[0].shape[0] // 2
    low_sum, high_sum = added(by_rep[0], corner_low), added(by_role[1], corner_high)

    def merged(rows, turned_low, turned_high):
        return jnp.concatenate(
            [
                base[rows].astype(jnp.float32)
                + first[rows].astype(jnp.float32)
                + second.astype(jnp.float32)
                for base, first, second in (
                    (near[0], straight_low, turned_low),
                    (near[1], straight_high, turned_high),
                )
            ],
            axis=1,
        )

    def turned(rows):
        return swap(low_sum[rows], "rep", ACROSS), swap(high_sum[rows], "role", 1)

    *far, low_sum, high_sum = ready(*turned(slice(cut, None)), low_sum, high_sum)
    leaving = merged(slice(cut, None), *far).astype(jnp.bfloat16)
    *beside, _ = ready(*turned(slice(0, cut)), leaving)
    total = merged(slice(0, cut), *beside)
    for bits in reversed(seq_bits()):
        total = total + swap(leaving, "seq", bits).astype(jnp.float32)
        if bits != seq_bits()[0]:
            cut = total.shape[0] // 2
            total, leaving = total[:cut], total[cut:].astype(jnp.bfloat16)
    return total


def expert_kernel(spots, *refs):
    pick_ref, place_ref, share_ref, own_gu_ref, far_gu_ref, own_dn_ref, far_dn_ref = refs[:7]
    groups, group_rows, slots = place_ref.shape[1:]
    piece_refs = refs[7 : 7 + len(spots)]
    out_refs = refs[7 + len(spots) : 7 + len(spots) + 2 * groups]
    x_buf, xs_buf, gu_buf, dn_buf, hid_buf, served_buf, y_buf, x_sem, w_sem, y_sem = refs[
        7 + len(spots) + 2 * groups :
    ]
    width = x_buf.shape[2]
    half = width // 2
    hidden = own_dn_ref.shape[0]
    tiles = hidden // TILE

    row_copies = []
    for number, ((group, row, column), piece) in enumerate(zip(spots, piece_refs)):
        rows, columns = piece.shape
        target = x_buf.at[group, pl.ds(row, rows), pl.ds(column, columns)]
        row_copies.append((group, pltpu.make_async_copy(piece, target, x_sem.at[number])))
    weight_copies = []
    for expert, (gu_ref, dn_ref) in enumerate(((own_gu_ref, own_dn_ref), (far_gu_ref, far_dn_ref))):
        mine = []
        for tile in range(tiles):
            for side in range(2):
                mine.append(
                    pltpu.make_async_copy(
                        gu_ref.at[:, pl.ds(side * hidden + tile * TILE, TILE)],
                        gu_buf.at[expert, tile, side],
                        w_sem.at[expert, 2 * tile + side],
                    )
                )
        mine.append(pltpu.make_async_copy(dn_ref, dn_buf.at[expert], w_sem.at[expert, 2 * tiles]))
        weight_copies.append(mine)
    for _, copy in row_copies:
        copy.start()
    for mine in weight_copies:
        for copy in mine:
            copy.start()

    for group in range(groups):
        for where, copy in row_copies:
            if where == group:
                copy.wait()
        chosen = jnp.dot(
            pick_ref[group], x_buf[group], preferred_element_type=jnp.float32
        ).astype(jnp.bfloat16)
        xs_buf[0, pl.ds(group * slots, slots)] = chosen[:slots]
        xs_buf[1, pl.ds(group * slots, slots)] = chosen[slots:]

    for expert in range(2):
        for tile in range(tiles):
            weight_copies[expert][2 * tile].wait()
            weight_copies[expert][2 * tile + 1].wait()
            gate = jnp.dot(
                xs_buf[expert], gu_buf[expert, tile, 0], preferred_element_type=jnp.float32
            )
            up = jnp.dot(
                xs_buf[expert], gu_buf[expert, tile, 1], preferred_element_type=jnp.float32
            )
            value = gate / (1.0 + jnp.exp(-gate)) * up
            hid_buf[:, tile * TILE : (tile + 1) * TILE] = value.astype(jnp.bfloat16)
        weight_copies[expert][2 * tiles].wait()
        for column in range(0, width, 2 * TILE):
            served_buf[expert, :, column : column + 2 * TILE] = jnp.dot(
                hid_buf[...],
                dn_buf[expert, :, column : column + 2 * TILE],
                preferred_element_type=jnp.float32,
            ).astype(jnp.bfloat16)

    out_copies = []
    for group in range(groups):
        for column in range(0, width, 2 * TILE):
            total = None
            for expert in range(2):
                placed = jnp.dot(
                    place_ref[expert, group],
                    served_buf[expert, pl.ds(group * slots, slots), column : column + 2 * TILE],
                    preferred_element_type=jnp.float32,
                )
                term = placed * share_ref[group, :, expert : expert + 1]
                total = term if total is None else total + term
            y_buf[group, :, column : column + 2 * TILE] = total.astype(jnp.bfloat16)
        for side in range(2):
            copy = pltpu.make_async_copy(
                y_buf.at[group, :, pl.ds(side * half, half)],
                out_refs[2 * group + side],
                y_sem.at[group, side],
            )
            copy.start()
            out_copies.append(copy)
    for copy in out_copies:
        copy.wait()


def run_experts(pieces, pick, place, share, weights):
    groups, group_rows, slots = place.shape[1:]
    hidden, width = weights[2].shape
    tiles = hidden // TILE
    spots = [
        (group, row, column) for group, held in enumerate(pieces) for row, column, _ in held
    ]
    arrays = [array for held in pieces for _, _, array in held]
    anywhere = pl.BlockSpec(memory_space=pl.ANY)
    inside = pl.BlockSpec(memory_space=pltpu.VMEM)
    outs = pl.pallas_call(
        lambda *refs: expert_kernel(spots, *refs),
        out_shape=[jax.ShapeDtypeStruct((group_rows, width // 2), jnp.bfloat16)] * (2 * groups),
        in_specs=[inside] * 3 + [anywhere] * (4 + len(arrays)),
        out_specs=[anywhere] * (2 * groups),
        scratch_shapes=[
            pltpu.VMEM((groups, group_rows, width), jnp.bfloat16),
            pltpu.VMEM((2, groups * slots, width), jnp.bfloat16),
            pltpu.VMEM((2, tiles, 2, width, TILE), jnp.bfloat16),
            pltpu.VMEM((2, hidden, width), jnp.bfloat16),
            pltpu.VMEM((groups * slots, hidden), jnp.bfloat16),
            pltpu.VMEM((2, groups * slots, width), jnp.bfloat16),
            pltpu.VMEM((groups, group_rows, width), jnp.bfloat16),
            pltpu.SemaphoreType.DMA((len(arrays),)),
            pltpu.SemaphoreType.DMA((2, 2 * tiles + 1)),
            pltpu.SemaphoreType.DMA((groups, 2)),
        ],
        compiler_params=pltpu.CompilerParams(vmem_limit_bytes=52 * 1024 * 1024),
        cost_estimate=pl.CostEstimate(
            flops=12 * groups * slots * width * hidden,
            bytes_accessed=12 * width * hidden + 4 * groups * group_rows * width,
            transcendentals=2 * groups * slots * hidden,
        ),
        name="experts",
    )(pick, place, share, *weights, *arrays)
    return [(outs[2 * group], outs[2 * group + 1]) for group in range(groups)]


def per_device(
    hidden_in,
    attn_gain,
    w_query,
    w_keyval,
    q_gain,
    k_gain,
    w_out,
    moe_gain,
    expert_ids,
    gate_fixed,
    w_gateup,
    w_down,
):
    tokens = hidden_in[0].astype(jnp.float32)
    row_count, model_width = tokens.shape
    head_dim = q_gain.shape[0]
    local_heads = w_query.shape[1] // head_dim
    kv_heads = w_keyval.shape[2] // head_dim
    group_size = local_heads * lax.axis_size("rep") // kv_heads
    rep_index = lax.axis_index("rep")
    kv_width = kv_heads * head_dim
    top_count = expert_ids.shape[2]
    expert_count = lax.axis_size(EVERY)

    normed = lax.optimization_barrier(rms_rows(tokens, attn_gain).astype(jnp.bfloat16))
    pair_rows = swap(normed, "rep", PAIR)
    across_rows = swap(normed, "rep", ACROSS)
    own_keys = jnp.dot(normed, w_keyval[0], preferred_element_type=jnp.float32)
    own_values = jnp.dot(normed, w_keyval[1], preferred_element_type=jnp.float32)
    own_keys = rms_rows(own_keys.reshape(row_count, kv_heads, head_dim), k_gain)
    own_keys = own_keys.reshape(row_count, kv_width).astype(jnp.bfloat16)
    own_kv = jnp.concatenate([own_keys, own_values.astype(jnp.bfloat16)], axis=1)
    line_kv = jnp.concatenate(seq_blocks(own_kv), axis=0)

    def head_kv(rep):
        index = rep * local_heads // group_size * head_dim
        return jnp.concatenate(
            [
                lax.dynamic_slice_in_dim(line_kv, index, head_dim, 1),
                lax.dynamic_slice_in_dim(line_kv, kv_width + index, head_dim, 1),
            ],
            axis=1,
        )

    far_kv = swap(head_kv(rep_index ^ ACROSS), "rep", ACROSS)
    half_kv = jnp.concatenate([head_kv(rep_index), far_kv], axis=0)
    all_kv = jnp.concatenate([half_kv, swap(half_kv, "rep", PAIR)], axis=0)
    key_rows, value_rows = all_kv[:, :head_dim], all_kv[:, head_dim:]

    routes = spread_routes(jnp.concatenate([expert_ids[0], gate_fixed[0]], axis=1))
    groups, group_rows = routes.shape[:2]
    capacity = max(2, 7 * row_count * top_count // (4 * expert_count))
    slots = -(-capacity * (group_rows // row_count) // 16) * 16
    gates = routes[:, :, top_count:].astype(jnp.float32)
    gate_sum = jnp.sum(gates, axis=2)
    earlier = jnp.tri(group_rows, k=-1, dtype=jnp.bfloat16)
    picks, shares = [], []
    for expert in (lax.axis_index(EVERY), lax.axis_index(EVERY) ^ PAIR):
        named = routes[:, :, :top_count] == expert
        hit = jnp.any(named, axis=2)
        shares.append(jnp.sum(jnp.where(named, gates, 0.0), axis=2) / gate_sum)
        rank = jnp.einsum(
            "ij,gj->gi", earlier, hit.astype(jnp.bfloat16), preferred_element_type=jnp.float32
        )
        rank = jnp.where(hit, rank.astype(jnp.int32), -1)
        picks.append((rank[:, None, :] == jnp.arange(slots)[None, :, None]).astype(jnp.bfloat16))
    pick = jnp.concatenate(picks, axis=1)
    place = jnp.stack([jnp.swapaxes(one, 1, 2) for one in picks])
    share = jnp.stack(shares, axis=2)

    corner_rows = swap(across_rows, "rep", PAIR)
    gathered = jnp.concatenate([normed, pair_rows, across_rows, corner_rows], axis=0)
    far_gu = swap(w_gateup[0], "rep", PAIR)
    far_dn = swap(w_down[0], "rep", PAIR)
    projected = jnp.dot(gathered, w_query, preferred_element_type=jnp.float32)
    query_span = projected.shape[0]
    query_part = projected.reshape(query_span, local_heads, head_dim)
    queries = rms_rows(query_part, q_gain).astype(jnp.bfloat16)
    scores = jnp.einsum("qhd,kd->hqk", queries, key_rows, preferred_element_type=jnp.float32)
    scores = scores * head_dim ** (-0.5)
    weights = jnp.exp(scores - jnp.max(scores, axis=2, keepdims=True))
    denom = jnp.sum(weights, axis=2)
    context = jnp.einsum(
        "hqk,kd->qhd", weights.astype(jnp.bfloat16), value_rows, preferred_element_type=jnp.float32
    )
    context = (context / denom.T[:, :, None]).astype(jnp.bfloat16)
    context = context.reshape(query_span, local_heads * head_dim)
    partial = jnp.dot(context, w_out, preferred_element_type=jnp.float32)
    partial = partial.reshape(4, row_count, model_width)
    back = swap(jnp.stack([partial[1], partial[3]]), "rep", PAIR)
    far_sum = (partial[2] + back[1]).astype(jnp.bfloat16)
    mixed = tokens + (partial[0] + back[0]) + swap(far_sum, "rep", ACROSS).astype(jnp.float32)
    mixed, far_gu, far_dn, pick, place, share = lax.optimization_barrier(
        (mixed, far_gu, far_dn, pick, place, share)
    )
    moe_in = rms_rows(mixed, moe_gain).astype(jnp.bfloat16)

    weights = (w_gateup[0], far_gu, w_down[0], far_dn)

    def serve(pieces, first, last):
        return run_experts(
            pieces, pick[first:last], place[:, first:last], share[first:last], weights
        )

    near, rows = spread_rows(moe_in, lambda pieces: serve([pieces], 0, 1)[0])
    by_rep, by_role = serve(rows[:2], 1, 3)
    rep_low, rep_high, role_low, role_high, *held = ready(
        *by_rep, *by_role, *(array for _, _, array in rows[2])
    )
    by_rep, by_role = (rep_low, rep_high), (role_low, role_high)
    pieces = [(row, column, array) for (row, column, _), array in zip(rows[2], held)]
    corner = serve([pieces], 3, 4)
    routed = collect_rows(near, by_rep, by_role, corner[0])
    routed = collect_rows(near, by_rep, by_role, corner[0])
    return (mixed + routed).astype(jnp.bfloat16)[None]


def solution(mesh):
    placed = (
        P("role", ("seq", "rep"), None),
        P(),
        P(None, "rep"),
        P(),
        P(),
        P(),
        P("rep", None),
        P(),
        P("role", ("seq", "rep"), None),
        P("role", ("seq", "rep"), None),
        P(("role", "seq", "rep"), None, None),
        P(("role", "seq", "rep"), None, None),
    )
    return jax.shard_map(
        per_device,
        mesh=mesh,
        in_specs=placed,
        out_specs=P("role", ("seq", "rep"), None),
        check_vma=False,
    )
```

time: 189 us -> 178 us (0.942)
  waiting for transfers between devices: 80.5 us -> 74.7 us
  Pallas kernels: 22.3 us -> 27.9 us
  local copies, waits for them, and re-layouts: 13.2 us -> 7.84 us
  starting transfers between devices: 51.7 us -> 46.7 us
  other arithmetic: 13.7 us -> 11.4 us
    ppermute x40 -> x42, waiting for transfers between devices: 80.5 us -> 74.7 us  [swap(): return lax.ppermute(block, axis, [(i, i ^ bits) for i in range(size)])]
    pallas_call x1 -> x3, Pallas kernels: 22.3 us -> 27.9 us  [run_experts(): pl.pallas_call(lambda *refs: expert_kernel(spots, *refs), out_shape=[jax....]
    ppermute x40 -> x42, starting transfers between devices: 51.7 us -> 46.7 us  [swap(): return lax.ppermute(block, axis, [(i, i ^ bits) for i in range(size)])]
    slice x6 -> x17, local copies, waits for them, and re-layouts: 3.79 us -> 1.37 us  [the longest x2 1.12 us: serve(): share[first:last]]
    unnamed x36 -> x30, local copies, waits for them, and re-layouts: 2.46 us -> 0.28 us
    convert_element_type x2, other arithmetic: 2.46 us -> 0.38 us  [added(): (first.astype(jnp.float32) + second.astype(jnp.float32)).astype(jnp.bfloa...]
  transfers between devices with their start and end apart: 40 -> 42, of which waited for: 17 -> 18; matrix products, arithmetic and copies ran while one was open for 13% -> 14% of each run, Pallas kernels for 0% -> 16%
where the time goes in v3:
time: 178 us; the launch traced here: 177 us
  waiting for transfers between devices  74.7 us (42%)
  starting transfers between devices  46.7 us (26%)
  Pallas kernels  27.9 us (16%)
  other arithmetic  11.4 us (6%)
  matrix products  8.16 us (5%)
  local copies, waits for them, and re-layouts  7.84 us (4%)
    ppermute x42, waiting for transfers between devices, swap(): return lax.ppermute(block, axis, [(i, i ^ bits) for i in range(size)])  74.7 us
    ppermute x42, starting transfers between devices, swap(): return lax.ppermute(block, axis, [(i, i ^ bits) for i in range(size)])  46.7 us
    pallas_call x3, Pallas kernels, run_experts(): pl.pallas_call(lambda *refs: expert_kernel(spots, *refs), out_shape=[jax....  27.9 us
    dot_general x2, local copies, waits for them, and re-layouts, per_device(): own_keys = jnp.dot(normed, w_keyval[0], preferred_element_type=jnp.float32)  3.78 us
  transfers between devices with their start and end apart: 42, of which 18 were waited for; matrix products, arithmetic and copies ran while one was open for 14% of the time, Pallas kernels for 16%

profile of v3, /device:TPU:0, one launch (start us, length us, event | category | flops | bytes accessed | tf_op | source)
XLA Modules:
  0.0 177.3 jit_solution(2932984540674976886)
XLA Ops:
  0.0 0.9 pad_add_fusion.3
  0.9 4.0 %collective-permute-start.12 = (s32[64,16]{0,1:T(8,128)S(1)}, s32[64,16]{0,1:T(8,128)S(1)}, u32[]{:S(2)}, u32[]{:S(2)}) collective-permute-start(s32[64,16]{0,1:T(8,128)S(1)} %pad_add_fusion.3), channel_id=1, source_target_pairs={{0,8},{4,12},{8,0},{12,4},{1,9},{5,13},{9,1},{13,5},{2,10},{6,14},... | collective-permute-start | bytes 12296 | tf_op jit(solution)/shard_map/ppermute | solution.py:24
  4.9 1.6 collective-permute-start.13
  6.5 1.1 fusion.28
  7.6 1.1 fusion.30
  8.7 2.3 %slice_bitcast_fusion = bf16[256,2048]{0,1:T(8,128)(2,1)} fusion(bf16[2,2048,256]{2,1,0:T(8,128)(2,1)} %param.15), kind=kLoop, calls=%fused_computation.30 | loop fusion | bytes 2097152 | tf_op jit(solution)/shard_map/dot_general | solution.py:294
  11.0 1.5 copy.39
  12.5 1.5 convolution_convert_fusion
  15.2 1.9 %collective-permute-start.1 = (bf16[64,512]{1,0:T(8,128)(2,1)S(1)}, bf16[64,512]{1,0:T(8,128)(2,1)S(1)}, u32[]{:S(2)}, u32[]{:S(2)}) collective-permute-start(bf16[64,512]{1,0:T(8,128)(2,1)S(1)} %pad_maximum_fusion.7), channel_id=1, source_target_pairs={{0,4},{4,0},{8,12},{12,8},{1,5},{5,1},{9,13},{13,9},{2,6},{6,2},{1... | collective-permute-start | bytes 196616 | tf_op jit(solution)/shard_map/ppermute | solution.py:24
  17.1 1.5 collective-permute-start.6
  18.7 1.3 collective-permute-start.15
  20.1 4.0 %collective-permute-done.15 = s32[256,16]{0,1:T(8,128)S(1)} collective-permute-done((s32[256,16]{0,1:T(8,128)S(1)}, s32[256,16]{0,1:T(8,128)S(1)}, u32[]{:S(2)}, u32[]{:S(2)}) %collective-permute-start.15) | collective-permute-done | bytes 16416 | tf_op jit(solution)/shard_map/ppermute | solution.py:24
  24.1 1.5 collective-permute-start.16
  25.6 2.4 %collective-permute-done.16 = s32[2,256,16]{1,2,0:T(8,128)S(1)} collective-permute-done((s32[2,256,16]{1,2,0:T(8,128)S(1)}, s32[2,256,16]{1,2,0:T(8,128)S(1)}, u32[]{:S(2)}, u32[]{:S(2)}) %collective-permute-start.16) | collective-permute-done | bytes 32800 | tf_op jit(solution)/shard_map/ppermute | solution.py:24
  28.8 3.8 %collective-permute-done.2 = bf16[64,512]{1,0:T(8,128)(2,1)S(1)} collective-permute-done((bf16[64,512]{1,0:T(8,128)(2,1)S(1)}, bf16[64,512]{1,0:T(8,128)(2,1)S(1)}, u32[]{:S(2)}, u32[]{:S(2)}) %collective-permute-start.2) | collective-permute-done | bytes 65568 | tf_op jit(solution)/shard_map/ppermute | solution.py:24
  32.7 1.6 collective-permute-start.3
  34.3 3.5 %collective-permute-done.3 = bf16[256,256]{1,0:T(8,128)(2,1)S(1)} collective-permute-done((bf16[256,256]{1,0:T(8,128)(2,1)S(1)}, bf16[256,256]{1,0:T(8,128)(2,1)S(1)}, u32[]{:S(2)}, u32[]{:S(2)}) %collective-permute-start.3) | collective-permute-done | bytes 131104 | tf_op jit(solution)/shard_map/ppermute | solution.py:24
  38.0 1.1 collective-permute-done.7
  39.1 3.3 %fusion.18 = f32[256,512]{1,0:T(8,128)} fusion(bf16[2048,512]{1,0:T(8,128)(2,1)} %param.14, bf16[64,2048]{1,0:T(8,128)(2,1)} %collective-permute-done.7, bf16[64,2048]{1,0:T(8,128)(2,1)S(1)} %collective-permute-done.6, bf16[64,2048]{1,0:T(8,128)(2,1)} %collective-permute-done.5, bf16[64,2048]{1,0:T(8,128)(2,1)S(1)} %fusion.30), kind=kOutput, calls=%fused_computation.16 | convolution fusion | flops 541065216 | bytes 3670016 | tf_op jit(solution)/shard_map/dot_general | solution.py:341
  42.3 1.2 reshape.101
  43.6 1.0 pad_maximum_fusion.1
  45.3 0.7 bitcast_reduce_fusion
  46.0 0.7 fusion.1
  46.7 0.9 fusion.13
  47.7 0.7 fusion.51
  49.8 1.5 collective-permute-done.8
  51.4 1.6 collective-permute-start.9
  52.9 0.9 add_convert_fusion.3
  53.8 0.9 add_convert_fusion.2
  54.7 5.0 %collective-permute-done.9 = bf16[64,2048]{1,0:T(8,128)(2,1)S(1)} collective-permute-done((bf16[64,2048]{1,0:T(8,128)(2,1)S(1)}, bf16[64,2048]{1,0:T(8,128)(2,1)S(1)}, u32[]{:S(2)}, u32[]{:S(2)}) %collective-permute-start.9) | collective-permute-done | bytes 262176 | tf_op jit(solution)/shard_map/ppermute | solution.py:24
  60.2 2.6 %collective-permute-start.17 = (bf16[64,2048]{1,0:T(8,128)(2,1)S(1)}, bf16[64,2048]{1,0:T(8,128)(2,1)}, u32[]{:S(2)}, u32[]{:S(2)}) collective-permute-start(bf16[64,2048]{1,0:T(8,128)(2,1)S(1)} %multiply_convert_fusion.refs_7_), channel_id=1, source_target_pairs={{0,8},{4,12},{8,0},{12,4},{1,9},{5,13},{9,1},{13,5},{2,10},{6,14},... | collective-permute-start | bytes 786440 | tf_op jit(solution)/shard_map/ppermute | solution.py:24
  63.3 1.5 collective-permute-start.20
  64.8 1.5 collective-permute-start.21
  66.3 1.1 copy.46
  67.3 1.1 fusion.48
  68.4 5.9 %collective-permute-done.17 = bf16[64,2048]{1,0:T(8,128)(2,1)} collective-permute-done((bf16[64,2048]{1,0:T(8,128)(2,1)S(1)}, bf16[64,2048]{1,0:T(8,128)(2,1)}, u32[]{:S(2)}, u32[]{:S(2)}) %collective-permute-start.17) | collective-permute-done | bytes 262176 | tf_op jit(solution)/shard_map/ppermute | solution.py:24
  74.4 1.3 collective-permute-done.19
  75.7 1.1 pad_maximum_fusion.2.refs_8_
  76.8 1.6 collective-permute-start.26
  78.4 1.5 collective-permute-start.27
  81.1 12.3 %collective-permute-done.22.refs_7_ = bf16[64,1024]{1,0:T(8,128)(2,1)S(1)} collective-permute-done((bf16[64,1024]{1,0:T(8,128)(2,1)S(1)}, bf16[64,1024]{1,0:T(8,128)(2,1)S(1)}, u32[]{:S(2)}, u32[]{:S(2)}) %collective-permute-start.22) | collective-permute-done | bytes 131104 | tf_op jit(solution)/shard_map/ppermute | solution.py:24
  93.9 1.5 collective-permute-start.25
  95.5 8.3 %experts.3 = (bf16[256,1024]{1,0:T(8,128)(2,1)S(1)}, bf16[256,1024]{1,0:T(8,128)(2,1)S(1)}) custom-call(bf16[1,224,256]{2,1,0:T(8,128)(2,1)S(1)} %get-tuple-element.109.refs_0_, bf16[2,1,256,112]{3,2,1,0:T(8,128)(2,1)S(1)} %get-tuple-element.107.refs_1_, f32[1,256,2]{2,1,0:T(8,128)S(1)} %get-tuple-element.105.refs_2_, bf16[2048,1536]{1,0:T(8,128)(2,1)} %bitcast.92, ...), custom_call_target="tpu_custom_call" | custom-call | flops 2113929216 | bytes 20971520 | tf_op jit(solution)/shard_map/experts/pallas_call | solution.py:238
  104.5 1.6 collective-permute-start.31
  106.1 1.6 collective-permute-start.28
  108.5 10.3 %experts.4 = (bf16[256,1024]{1,0:T(8,128)(2,1)}, bf16[256,1024]{1,0:T(8,128)(2,1)}, bf16[256,1024]{1,0:T(8,128)(2,1)}, bf16[256,1024]{1,0:T(8,128)(2,1)}) custom-call(bf16[2,224,256]{2,1,0:T(8,128)(2,1)S(1)} %slice.153.refs_0_, bf16[2,2,256,112]{3,2,1,0:T(8,128)(2,1)S(1)} %slice.154.refs_1_, f32[2,256,2]{2,1,0:T(8,128)S(1)} %slice.187.refs_2_, ...), custom_call_target="tpu_custom_call" | custom-call | flops 4227858432 | bytes 23068672 | tf_op jit(solution)/shard_map/experts/pallas_call | solution.py:238
  119.4 1.3 collective-permute-start.33
  120.7 9.2 %experts.5 = (bf16[256,1024]{1,0:T(8,128)(2,1)S(1)}, bf16[256,1024]{1,0:T(8,128)(2,1)}) custom-call(bf16[1,224,256]{2,1,0:T(8,128)(2,1)S(1)} %get-tuple-element.108.refs_0_, bf16[2,1,256,112]{3,2,1,0:T(8,128)(2,1)S(1)} %get-tuple-element.106.refs_1_, f32[1,256,2]{2,1,0:T(8,128)S(1)} %get-tuple-element.104.refs_2_, bf16[2048,1536]{1,0:T(8,128)(2,1)} %bitcast.94, ...), custom_call_target="tpu_custom_call" | custom-call | flops 2113929216 | bytes 20971520 | tf_op jit(solution)/shard_map/experts/pallas_call | solution.py:238
  130.0 1.5 collective-permute-start.34
  131.6 1.1 collective-permute-start.35
  132.6 9.2 %collective-permute-done.34 = bf16[256,1024]{1,0:T(8,128)(2,1)S(1)} collective-permute-done((bf16[256,1024]{1,0:T(8,128)(2,1)S(1)}, bf16[256,1024]{1,0:T(8,128)(2,1)S(1)}, u32[]{:S(2)}, u32[]{:S(2)}) %collective-permute-start.34) | collective-permute-done | bytes 524320 | tf_op jit(solution)/shard_map/ppermute | solution.py:24
  142.3 1.3 collective-permute-start.37
  143.9 1.1 collective-permute-start.36
  144.9 5.4 %collective-permute-done.37 = bf16[128,1024]{1,0:T(8,128)(2,1)S(1)} collective-permute-done((bf16[128,1024]{1,0:T(8,128)(2,1)S(1)}, bf16[128,1024]{1,0:T(8,128)(2,1)S(1)}, u32[]{:S(2)}, u32[]{:S(2)}) %collective-permute-start.37) | collective-permute-done | bytes 262176 | tf_op jit(solution)/shard_map/ppermute | solution.py:24
  150.3 1.6 collective-permute-done.36
  151.9 1.1 collective-permute-start.38
  153.1 1.1 collective-permute-start.39
  154.4 2.8 %collective-permute-start.40 = (bf16[128,2048]{1,0:T(8,128)(2,1)S(1)}, bf16[128,2048]{1,0:T(8,128)(2,1)S(1)}, u32[]{:S(2)}, u32[]{:S(2)}) collective-permute-start(bf16[128,2048]{1,0:T(8,128)(2,1)S(1)} %pad_maximum_fusion.3), channel_id=1, source_target_pairs={{0,4},{4,0},{8,12},{12,8},{1,5},{5,1},{9,13},{13,9},{2,6},{6,2},{1... | collective-permute-start | bytes 1572872 | tf_op jit(solution)/shard_map/ppermute | solution.py:24
  157.2 1.1 collective-permute-done.38
  158.4 1.1 collective-permute-done.39
  159.7 7.1 %collective-permute-done.40 = bf16[128,2048]{1,0:T(8,128)(2,1)S(1)} collective-permute-done((bf16[128,2048]{1,0:T(8,128)(2,1)S(1)}, bf16[128,2048]{1,0:T(8,128)(2,1)S(1)}, u32[]{:S(2)}, u32[]{:S(2)}) %collective-permute-start.40) | collective-permute-done | bytes 524320 | tf_op jit(solution)/shard_map/ppermute | solution.py:24
  167.0 1.6 collective-permute-start.41
  168.5 8.0 %collective-permute-done.41 = bf16[64,2048]{1,0:T(8,128)(2,1)S(1)} collective-permute-done((bf16[64,2048]{1,0:T(8,128)(2,1)S(1)}, bf16[64,2048]{1,0:T(8,128)(2,1)S(1)}, u32[]{:S(2)}, u32[]{:S(2)}) %collective-permute-start.41) | collective-permute-done | bytes 262176 | tf_op jit(solution)/shard_map/ppermute | solution.py:24
  176.5 0.8 fusion.37
  (129 shorter events, 10.5 us)
Async XLA Ops:
  0.0 47.7 %copy-start = (bf16[512,2048]{1,0:T(8,128)(2,1)S(1)}, bf16[512,2048]{1,0:T(8,128)(2,1)}, u32[]{:S(2)}) copy-start(bf16[512,2048]{1,0:T(8,128)(2,1)} %param.18) | copy-start | bytes 6291460
  0.9 13.8 %collective-permute-start.12 = (s32[64,16]{0,1:T(8,128)S(1)}, s32[64,16]{0,1:T(8,128)S(1)}, u32[]{:S(2)}, u32[]{:S(2)}) collective-permute-start(s32[64,16]{0,1:T(8,128)S(1)} %pad_add_fusion.3), channel_id=1, source_target_pairs={{0,8},{4,12},{8,0},{12,4},{1,9},{5,13},{9,1},{13,5},{2,10},{6,14},... | collective-permute-start | bytes 12296 | tf_op jit(solution)/shard_map/ppermute | solution.py:24
  4.9 13.7 %collective-permute-start.13 = (s32[64,16]{0,1:T(8,128)S(1)}, s32[64,16]{0,1:T(8,128)S(1)}, u32[]{:S(2)}, u32[]{:S(2)}) collective-permute-start(s32[64,16]{0,1:T(8,128)S(1)} %pad_add_fusion.3), channel_id=1, source_target_pairs={{0,4},{4,0},{8,12},{12,8},{1,5},{5,1},{9,13},{13,9},{2,6},{6,2},{1... | collective-permute-start | bytes 12296 | tf_op jit(solution)/shard_map/ppermute | solution.py:24
  10.9 3.6 %copy-start.13 = (f32[128]{0:T(128)S(1)}, f32[128]{0:T(128)}, u32[]{:S(2)}) copy-start(f32[128]{0:T(128)} %param.17) | copy-start | bytes 1540
  10.9 7.7 %copy-start.10 = (s32[1,64,8]{1,2,0:T(8,128)S(1)}, s32[1,64,8]{1,2,0:T(8,128)}, u32[]{:S(2)}) copy-start(s32[1,64,8]{1,2,0:T(8,128)} %param.21) | copy-start | bytes 6148
  11.0 7.7 %copy-start.11 = (s32[1,64,8]{1,2,0:T(8,128)S(1)}, s32[1,64,8]{1,2,0:T(8,128)}, u32[]{:S(2)}) copy-start(s32[1,64,8]{1,2,0:T(8,128)} %param.20) | copy-start | bytes 6148
  14.7 4.0 %collective-permute-start.14 = (s32[64,16]{0,1:T(8,128)S(1)}, s32[64,16]{0,1:T(8,128)S(1)}, u32[]{:S(2)}, u32[]{:S(2)}) collective-permute-start(s32[64,16]{0,1:T(8,128)S(1)} %collective-permute-done.12), channel_id=1, source_target_pairs={{0,4},{4,0},{8,12},{12,8},{1,5},{5,1},{9,13},{13,9},{2,6},{6,2},{1... | collective-permute-start | bytes 12296 | tf_op jit(solution)/shard_map/ppermute | solution.py:24
  15.2 12.9 %collective-permute-start = (bf16[64,512]{1,0:T(8,128)(2,1)S(1)}, bf16[64,512]{1,0:T(8,128)(2,1)S(1)}, u32[]{:S(2)}, u32[]{:S(2)}) collective-permute-start(bf16[64,512]{1,0:T(8,128)(2,1)S(1)} %pad_maximum_fusion.7), channel_id=1, source_target_pairs={{0,8},{4,12},{8,0},{12,4},{1,9},{5,13},{9,1},{13,5},{2,10},{6,14},... | collective-permute-start | bytes 196616 | tf_op jit(solution)/shard_map/ppermute | solution.py:24
  15.2 13.3 %collective-permute-start.1 = (bf16[64,512]{1,0:T(8,128)(2,1)S(1)}, bf16[64,512]{1,0:T(8,128)(2,1)S(1)}, u32[]{:S(2)}, u32[]{:S(2)}) collective-permute-start(bf16[64,512]{1,0:T(8,128)(2,1)S(1)} %pad_maximum_fusion.7), channel_id=1, source_target_pairs={{0,4},{4,0},{8,12},{12,8},{1,5},{5,1},{9,13},{13,9},{2,6},{6,2},{1... | collective-permute-start | bytes 196616 | tf_op jit(solution)/shard_map/ppermute | solution.py:24
  17.1 17.2 %collective-permute-start.6 = (bf16[64,2048]{1,0:T(8,128)(2,1)S(1)}, bf16[64,2048]{1,0:T(8,128)(2,1)S(1)}, u32[]{:S(2)}, u32[]{:S(2)}) collective-permute-start(bf16[64,2048]{1,0:T(8,128)(2,1)S(1)} %fusion.30), channel_id=1, source_target_pairs={{0,2},{1,3},{2,0},{3,1},{4,6},{5,7},{6,4},{7,5},{8,10},{9,11},{10,... | collective-permute-start | bytes 786440 | tf_op jit(solution)/shard_map/ppermute | solution.py:24
  18.6 19.3 %collective-permute-start.5 = (bf16[64,2048]{1,0:T(8,128)(2,1)S(1)}, bf16[64,2048]{1,0:T(8,128)(2,1)}, u32[]{:S(2)}, u32[]{:S(2)}) collective-permute-start(bf16[64,2048]{1,0:T(8,128)(2,1)S(1)} %fusion.30), channel_id=1, source_target_pairs={{0,1},{1,0},{2,3},{3,2},{4,5},{5,4},{6,7},{7,6},{8,9},{9,8},{10,11... | collective-permute-start | bytes 786440 | tf_op jit(solution)/shard_map/ppermute | solution.py:24
  18.7 5.4 %collective-permute-start.15 = (s32[256,16]{0,1:T(8,128)S(1)}, s32[256,16]{0,1:T(8,128)S(1)}, u32[]{:S(2)}, u32[]{:S(2)}) collective-permute-start(s32[256,16]{0,1:T(8,128)S(1)} %pad_add_fusion.2), channel_id=1, source_target_pairs={{0,2},{1,3},{2,0},{3,1},{4,6},{5,7},{6,4},{7,5},{8,10},{9,11},{10,... | collective-permute-start | bytes 49160 | tf_op jit(solution)/shard_map/ppermute | solution.py:24
  24.1 3.9 %collective-permute-start.16 = (s32[2,256,16]{1,2,0:T(8,128)S(1)}, s32[2,256,16]{1,2,0:T(8,128)S(1)}, u32[]{:S(2)}, u32[]{:S(2)}) collective-permute-start(s32[2,256,16]{1,2,0:T(8,128)S(1)} %pad_add_fusion.1), channel_id=1, source_target_pairs={{0,16},{16,0},{1,17},{17,1},{2,18},{18,2},{3,19},{19,3},{4,20},{20... | collective-permute-start | bytes 98312 | tf_op jit(solution)/shard_map/ppermute | solution.py:24
  28.0 31.9 %collective-permute-start.10 = (bf16[2048,1536]{1,0:T(8,128)(2,1)}, bf16[2048,1536]{1,0:T(8,128)(2,1)}, u32[]{:S(2)}, u32[]{:S(2)}) collective-permute-start(bf16[2048,1536]{1,0:T(8,128)(2,1)} %bitcast.91), channel_id=1, source_target_pairs={{0,1},{1,0},{2,3},{3,2},{4,5},{5,4},{6,7},{7,6},{8,9},{9,8},{10,11... | collective-permute-start | bytes 18874376 | tf_op jit(solution)/shard_map/ppermute | solution.py:24
  28.0 4.5 %collective-permute-start.2 = (bf16[64,512]{1,0:T(8,128)(2,1)S(1)}, bf16[64,512]{1,0:T(8,128)(2,1)S(1)}, u32[]{:S(2)}, u32[]{:S(2)}) collective-permute-start(bf16[64,512]{1,0:T(8,128)(2,1)S(1)} %collective-permute-done), channel_id=1, source_target_pairs={{0,4},{4,0},{8,12},{12,8},{1,5},{5,1},{9,13},{13,9},{2,6},{6,2},{1... | collective-permute-start | bytes 196616 | tf_op jit(solution)/shard_map/ppermute | solution.py:24
  28.5 31.4 %collective-permute-start.11 = (bf16[768,2048]{1,0:T(8,128)(2,1)}, bf16[768,2048]{1,0:T(8,128)(2,1)}, u32[]{:S(2)}, u32[]{:S(2)}) collective-permute-start(bf16[768,2048]{1,0:T(8,128)(2,1)} %bitcast.95), channel_id=1, source_target_pairs={{0,1},{1,0},{2,3},{3,2},{4,5},{5,4},{6,7},{7,6},{8,9},{9,8},{10,11... | collective-permute-start | bytes 9437192 | tf_op jit(solution)/shard_map/ppermute | solution.py:24
  32.7 5.2 %collective-permute-start.3 = (bf16[256,256]{1,0:T(8,128)(2,1)S(1)}, bf16[256,256]{1,0:T(8,128)(2,1)S(1)}, u32[]{:S(2)}, u32[]{:S(2)}) collective-permute-start(bf16[256,256]{1,0:T(8,128)(2,1)S(1)} %pad_maximum_fusion.6), channel_id=1, source_target_pairs={{0,2},{1,3},{2,0},{3,1},{4,6},{5,7},{6,4},{7,5},{8,10},{9,11},{10,... | collective-permute-start | bytes 393224 | tf_op jit(solution)/shard_map/ppermute | solution.py:24
  34.2 4.8 %collective-permute-start.7 = (bf16[64,2048]{1,0:T(8,128)(2,1)S(1)}, bf16[64,2048]{1,0:T(8,128)(2,1)}, u32[]{:S(2)}, u32[]{:S(2)}) collective-permute-start(bf16[64,2048]{1,0:T(8,128)(2,1)S(1)} %collective-permute-done.6), channel_id=1, source_target_pairs={{0,1},{1,0},{2,3},{3,2},{4,5},{5,4},{6,7},{7,6},{8,9},{9,8},{10,11... | collective-permute-start | bytes 786440 | tf_op jit(solution)/shard_map/ppermute | solution.py:24
  37.9 5.7 %collective-permute-start.4 = (bf16[512,256]{1,0:T(8,128)(2,1)S(1)}, bf16[512,256]{1,0:T(8,128)(2,1)}, u32[]{:S(2)}, u32[]{:S(2)}) collective-permute-start(bf16[512,256]{1,0:T(8,128)(2,1)S(1)} %pad_maximum_fusion.5), channel_id=1, source_target_pairs={{0,1},{1,0},{2,3},{3,2},{4,5},{5,4},{6,7},{7,6},{8,9},{9,8},{10,11... | collective-permute-start | bytes 786440 | tf_op jit(solution)/shard_map/ppermute | solution.py:24
  42.3 2.6 %copy-start.14 = (f32[128]{0:T(128)S(1)}, f32[128]{0:T(128)}, u32[]{:S(2)}) copy-start(f32[128]{0:T(128)} %param.16) | copy-start | bytes 1540
  48.5 11.2 %copy-start.1 = (bf16[1,64,2048]{2,1,0:T(8,128)(2,1)S(1)}, bf16[1,64,2048]{2,1,0:T(8,128)(2,1)}, u32[]{:S(2)}) copy-start(bf16[1,64,2048]{2,1,0:T(8,128)(2,1)} %param.12) | copy-start | bytes 786436
  48.6 2.7 %collective-permute-start.8 = (f32[2,64,2048]{2,1,0:T(8,128)S(1)}, f32[2,64,2048]{2,1,0:T(8,128)S(1)}, u32[]{:S(2)}, u32[]{:S(2)}) collective-permute-start(f32[2,64,2048]{2,1,0:T(8,128)S(1)} %pad_maximum_fusion), channel_id=1, source_target_pairs={{0,1},{1,0},{2,3},{3,2},{4,5},{5,4},{6,7},{7,6},{8,9},{9,8},{10,11... | collective-permute-start | bytes 3145736 | tf_op jit(solution)/shard_map/ppermute | solution.py:24
  51.3 8.7 %copy-start.12 = (f32[2048]{0:T(1024)S(1)}, f32[2048]{0:T(1024)}, u32[]{:S(2)}) copy-start(f32[2048]{0:T(1024)} %param.19) | copy-start | bytes 24580
  51.4 8.4 %collective-permute-start.9 = (bf16[64,2048]{1,0:T(8,128)(2,1)S(1)}, bf16[64,2048]{1,0:T(8,128)(2,1)S(1)}, u32[]{:S(2)}, u32[]{:S(2)}) collective-permute-start(bf16[64,2048]{1,0:T(8,128)(2,1)S(1)} %fusion.35), channel_id=1, source_target_pairs={{0,2},{1,3},{2,0},{3,1},{4,6},{5,7},{6,4},{7,5},{8,10},{9,11},{10,... | collective-permute-start | bytes 786440 | tf_op jit(solution)/shard_map/ppermute | solution.py:24
  60.2 14.2 %collective-permute-start.17 = (bf16[64,2048]{1,0:T(8,128)(2,1)S(1)}, bf16[64,2048]{1,0:T(8,128)(2,1)}, u32[]{:S(2)}, u32[]{:S(2)}) collective-permute-start(bf16[64,2048]{1,0:T(8,128)(2,1)S(1)} %multiply_convert_fusion.refs_7_), channel_id=1, source_target_pairs={{0,8},{4,12},{8,0},{12,4},{1,9},{5,13},{9,1},{13,5},{2,10},{6,14},... | collective-permute-start | bytes 786440 | tf_op jit(solution)/shard_map/ppermute | solution.py:24
  62.8 12.9 %collective-permute-start.19 = (bf16[64,2048]{1,0:T(8,128)(2,1)S(1)}, bf16[64,2048]{1,0:T(8,128)(2,1)}, u32[]{:S(2)}, u32[]{:S(2)}) collective-permute-start(bf16[64,2048]{1,0:T(8,128)(2,1)S(1)} %multiply_convert_fusion.refs_7_), channel_id=1, source_target_pairs={{0,4},{4,0},{8,12},{12,8},{1,5},{5,1},{9,13},{13,9},{2,6},{6,2},{1... | collective-permute-start | bytes 786440 | tf_op jit(solution)/shard_map/ppermute | solution.py:24
  63.3 13.5 %collective-permute-start.20 = (bf16[64,2048]{1,0:T(8,128)(2,1)S(1)}, bf16[64,2048]{1,0:T(8,128)(2,1)S(1)}, u32[]{:S(2)}, u32[]{:S(2)}) collective-permute-start(bf16[64,2048]{1,0:T(8,128)(2,1)S(1)} %multiply_convert_fusion.refs_7_), channel_id=1, source_target_pairs={{0,2},{1,3},{2,0},{3,1},{4,6},{5,7},{6,4},{7,5},{8,10},{9,11},{10,... | collective-permute-start | bytes 786440 | tf_op jit(solution)/shard_map/ppermute | solution.py:24
  64.8 12.0 %collective-permute-start.21 = (bf16[64,2048]{1,0:T(8,128)(2,1)S(1)}, bf16[64,2048]{1,0:T(8,128)(2,1)S(1)}, u32[]{:S(2)}, u32[]{:S(2)}) collective-permute-start(bf16[64,2048]{1,0:T(8,128)(2,1)S(1)} %multiply_convert_fusion.refs_7_), channel_id=1, source_target_pairs={{0,16},{16,0},{1,17},{17,1},{2,18},{18,2},{3,19},{19,3},{4,20},{20... | collective-permute-start | bytes 786440 | tf_op jit(solution)/shard_map/ppermute | solution.py:24
  67.3 13.7 %copy-start.3 = (bf16[2,4,256,112]{3,2,1,0:T(8,128)(2,1)S(1)}, bf16[2,4,256,112]{3,2,1,0:T(8,128)(2,1)}, u32[]{:S(2)}) copy-start(bf16[2,4,256,112]{3,2,1,0:T(8,128)(2,1)} %add_convert_fusion.2) | copy-start | bytes 1376260
  67.3 28.1 %copy-start.5 = (bf16[4,224,256]{2,1,0:T(8,128)(2,1)S(1)}, bf16[4,224,256]{2,1,0:T(8,128)(2,1)}, u32[]{:S(2)}) copy-start(bf16[4,224,256]{2,1,0:T(8,128)(2,1)} %add_convert_fusion.3) | copy-start | bytes 1376260
  67.3 28.1 %copy-start.4 = (f32[4,256,2]{2,1,0:T(8,128)S(1)}, f32[4,256,2]{2,1,0:T(8,128)}, u32[]{:S(2)}) copy-start(f32[4,256,2]{2,1,0:T(8,128)} %copy.46) | copy-start | bytes 24580
  74.4 19.0 %collective-permute-start.18 = (bf16[64,2048]{1,0:T(8,128)(2,1)}, bf16[64,2048]{1,0:T(8,128)(2,1)S(1)}, u32[]{:S(2)}, u32[]{:S(2)}) collective-permute-start(bf16[64,2048]{1,0:T(8,128)(2,1)} %collective-permute-done.17), channel_id=1, source_target_pairs={{0,4},{4,0},{8,12},{12,8},{1,5},{5,1},{9,13},{13,9},{2,6},{6,2},{1... | collective-permute-start | bytes 786440 | tf_op jit(solution)/shard_map/ppermute | solution.py:24
  76.7 18.7 %copy-start.2 = (bf16[128,2048]{1,0:T(8,128)(2,1)}, bf16[128,2048]{1,0:T(8,128)(2,1)S(1)}, u32[]{:S(2)}) copy-start(bf16[128,2048]{1,0:T(8,128)(2,1)S(1)} %pad_maximum_fusion.2.refs_8_) | copy-start | bytes 1572868
  76.8 29.3 %collective-permute-start.26 = (bf16[128,2048]{1,0:T(8,128)(2,1)S(1)}, bf16[128,2048]{1,0:T(8,128)(2,1)S(1)}, u32[]{:S(2)}, u32[]{:S(2)}) collective-permute-start(bf16[128,2048]{1,0:T(8,128)(2,1)S(1)} %pad_maximum_fusion.2.refs_8_), channel_id=1, source_target_pairs={{0,2},{1,3},{2,0},{3,1},{4,6},{5,7},{6,4},{7,5},{8,10},{9,11},{10,... | collective-permute-start | bytes 1572872 | tf_op jit(solution)/shard_map/ppermute | solution.py:24
  78.4 29.3 %collective-permute-start.27 = (bf16[128,2048]{1,0:T(8,128)(2,1)S(1)}, bf16[128,2048]{1,0:T(8,128)(2,1)S(1)}, u32[]{:S(2)}, u32[]{:S(2)}) collective-permute-start(bf16[128,2048]{1,0:T(8,128)(2,1)S(1)} %pad_maximum_fusion.2.refs_8_), channel_id=1, source_target_pairs={{0,16},{16,0},{1,17},{17,1},{2,18},{18,2},{3,19},{19,3},{4,20},{20... | collective-permute-start | bytes 1572872 | tf_op jit(solution)/shard_map/ppermute | solution.py:24
  79.9 13.5 %collective-permute-start.22 = (bf16[64,1024]{1,0:T(8,128)(2,1)S(1)}, bf16[64,1024]{1,0:T(8,128)(2,1)S(1)}, u32[]{:S(2)}, u32[]{:S(2)}) collective-permute-start(bf16[64,1024]{1,0:T(8,128)(2,1)S(1)} %slice.147), channel_id=1, source_target_pairs={{0,16},{16,0},{1,17},{17,1},{2,18},{18,2},{3,19},{19,3},{4,20},{20... | collective-permute-start | bytes 393224 | tf_op jit(solution)/shard_map/ppermute | solution.py:24
  80.5 12.9 %collective-permute-start.23 = (bf16[64,1024]{1,0:T(8,128)(2,1)S(1)}, bf16[64,1024]{1,0:T(8,128)(2,1)S(1)}, u32[]{:S(2)}, u32[]{:S(2)}) collective-permute-start(bf16[64,1024]{1,0:T(8,128)(2,1)S(1)} %slice.148), channel_id=1, source_target_pairs={{0,2},{1,3},{2,0},{3,1},{4,6},{5,7},{6,4},{7,5},{8,10},{9,11},{10,... | collective-permute-start | bytes 393224 | tf_op jit(solution)/shard_map/ppermute | solution.py:24
  93.4 10.5 %collective-permute-start.24 = (bf16[64,2048]{1,0:T(8,128)(2,1)S(1)}, bf16[64,2048]{1,0:T(8,128)(2,1)S(1)}, u32[]{:S(2)}, u32[]{:S(2)}) collective-permute-start(bf16[64,2048]{1,0:T(8,128)(2,1)S(1)} %collective-permute-done.18.refs_9_), channel_id=1, source_target_pairs={{0,2},{1,3},{2,0},{3,1},{4,6},{5,7},{6,4},{7,5},{8,10},{9,11},{10,... | collective-permute-start | bytes 786440 | tf_op jit(solution)/shard_map/ppermute | solution.py:24
  93.9 10.0 %collective-permute-start.25 = (bf16[64,2048]{1,0:T(8,128)(2,1)S(1)}, bf16[64,2048]{1,0:T(8,128)(2,1)S(1)}, u32[]{:S(2)}, u32[]{:S(2)}) collective-permute-start(bf16[64,2048]{1,0:T(8,128)(2,1)S(1)} %collective-permute-done.18.refs_9_), channel_id=1, source_target_pairs={{0,16},{16,0},{1,17},{17,1},{2,18},{18,2},{3,19},{19,3},{4,20},{20... | collective-permute-start | bytes 786440 | tf_op jit(solution)/shard_map/ppermute | solution.py:24
  103.9 14.9 %collective-permute-start.30 = (bf16[64,1024]{1,0:T(8,128)(2,1)S(1)}, bf16[64,1024]{1,0:T(8,128)(2,1)S(1)}, u32[]{:S(2)}, u32[]{:S(2)}) collective-permute-start(bf16[64,1024]{1,0:T(8,128)(2,1)S(1)} %slice.158), channel_id=1, source_target_pairs={{0,16},{16,0},{1,17},{17,1},{2,18},{18,2},{3,19},{19,3},{4,20},{20... | collective-permute-start | bytes 393224 | tf_op jit(solution)/shard_map/ppermute | solution.py:24
  104.5 14.3 %collective-permute-start.31 = (bf16[64,1024]{1,0:T(8,128)(2,1)S(1)}, bf16[64,1024]{1,0:T(8,128)(2,1)S(1)}, u32[]{:S(2)}, u32[]{:S(2)}) collective-permute-start(bf16[64,1024]{1,0:T(8,128)(2,1)S(1)} %slice.159), channel_id=1, source_target_pairs={{0,2},{1,3},{2,0},{3,1},{4,6},{5,7},{6,4},{7,5},{8,10},{9,11},{10,... | collective-permute-start | bytes 393224 | tf_op jit(solution)/shard_map/ppermute | solution.py:24
  106.1 2.2 %copy-start.6 = (bf16[128,2048]{1,0:T(8,128)(2,1)}, bf16[128,2048]{1,0:T(8,128)(2,1)S(1)}, u32[]{:S(2)}) copy-start(bf16[128,2048]{1,0:T(8,128)(2,1)S(1)} %collective-permute-done.26.refs_8_) | copy-start | bytes 1572868
  106.1 12.7 %collective-permute-start.28 = (bf16[128,1024]{1,0:T(8,128)(2,1)S(1)}, bf16[128,1024]{1,0:T(8,128)(2,1)S(1)}, u32[]{:S(2)}, u32[]{:S(2)}) collective-permute-start(bf16[128,1024]{1,0:T(8,128)(2,1)S(1)} %slice.188), channel_id=1, source_target_pairs={{0,16},{16,0},{1,17},{17,1},{2,18},{18,2},{3,19},{19,3},{4,20},{20... | collective-permute-start | bytes 786440 | tf_op jit(solution)/shard_map/ppermute | solution.py:24
  107.7 0.8 copy-start.7
  107.7 11.1 %collective-permute-start.29 = (bf16[128,1024]{1,0:T(8,128)(2,1)S(1)}, bf16[128,1024]{1,0:T(8,128)(2,1)S(1)}, u32[]{:S(2)}, u32[]{:S(2)}) collective-permute-start(bf16[128,1024]{1,0:T(8,128)(2,1)S(1)} %slice.189), channel_id=1, source_target_pairs={{0,2},{1,3},{2,0},{3,1},{4,6},{5,7},{6,4},{7,5},{8,10},{9,11},{10,... | collective-permute-start | bytes 786440 | tf_op jit(solution)/shard_map/ppermute | solution.py:24
  118.8 11.2 %collective-permute-start.32 = (bf16[256,1024]{1,0:T(8,128)(2,1)}, bf16[256,1024]{1,0:T(8,128)(2,1)S(1)}, u32[]{:S(2)}, u32[]{:S(2)}) collective-permute-start(bf16[256,1024]{1,0:T(8,128)(2,1)} %get-tuple-element.72), channel_id=1, source_target_pairs={{0,16},{16,0},{1,17},{17,1},{2,18},{18,2},{3,19},{19,3},{4,20},{20... | collective-permute-start | bytes 1572872 | tf_op jit(solution)/shard_map/ppermute | solution.py:24
  119.4 10.6 %collective-permute-start.33 = (bf16[256,1024]{1,0:T(8,128)(2,1)}, bf16[256,1024]{1,0:T(8,128)(2,1)S(1)}, u32[]{:S(2)}, u32[]{:S(2)}) collective-permute-start(bf16[256,1024]{1,0:T(8,128)(2,1)} %get-tuple-element.73), channel_id=1, source_target_pairs={{0,2},{1,3},{2,0},{3,1},{4,6},{5,7},{6,4},{7,5},{8,10},{9,11},{10,... | collective-permute-start | bytes 1572872 | tf_op jit(solution)/shard_map/ppermute | solution.py:24
  120.7 21.3 %copy-start.9 = (bf16[256,1024]{1,0:T(8,128)(2,1)S(1)}, bf16[256,1024]{1,0:T(8,128)(2,1)}, u32[]{:S(2)}) copy-start(bf16[256,1024]{1,0:T(8,128)(2,1)} %get-tuple-element.87) | copy-start | bytes 1572868
  130.0 13.6 %copy-start.8 = (bf16[256,1024]{1,0:T(8,128)(2,1)S(1)}, bf16[256,1024]{1,0:T(8,128)(2,1)}, u32[]{:S(2)}) copy-start(bf16[256,1024]{1,0:T(8,128)(2,1)} %get-tuple-element.83) | copy-start | bytes 1572868
  130.0 11.8 %collective-permute-start.34 = (bf16[256,1024]{1,0:T(8,128)(2,1)S(1)}, bf16[256,1024]{1,0:T(8,128)(2,1)S(1)}, u32[]{:S(2)}, u32[]{:S(2)}) collective-permute-start(bf16[256,1024]{1,0:T(8,128)(2,1)S(1)} %get-tuple-element.84), channel_id=1, source_target_pairs={{0,16},{16,0},{1,17},{17,1},{2,18},{18,2},{3,19},{19,3},{4,20},{20... | collective-permute-start | bytes 1572872 | tf_op jit(solution)/shard_map/ppermute | solution.py:24
  131.6 10.5 %collective-permute-start.35 = (bf16[256,1024]{1,0:T(8,128)(2,1)}, bf16[256,1024]{1,0:T(8,128)(2,1)S(1)}, u32[]{:S(2)}, u32[]{:S(2)}) collective-permute-start(bf16[256,1024]{1,0:T(8,128)(2,1)} %get-tuple-element.85), channel_id=1, source_target_pairs={{0,2},{1,3},{2,0},{3,1},{4,6},{5,7},{6,4},{7,5},{8,10},{9,11},{10,... | collective-permute-start | bytes 1572872 | tf_op jit(solution)/shard_map/ppermute | solution.py:24
  142.3 8.0 %collective-permute-start.37 = (bf16[128,1024]{1,0:T(8,128)(2,1)S(1)}, bf16[128,1024]{1,0:T(8,128)(2,1)S(1)}, u32[]{:S(2)}, u32[]{:S(2)}) collective-permute-start(bf16[128,1024]{1,0:T(8,128)(2,1)S(1)} %slice.192), channel_id=1, source_target_pairs={{0,16},{16,0},{1,17},{17,1},{2,18},{18,2},{3,19},{19,3},{4,20},{20... | collective-permute-start | bytes 786440 | tf_op jit(solution)/shard_map/ppermute | solution.py:24
  143.9 8.0 %collective-permute-start.36 = (bf16[128,1024]{1,0:T(8,128)(2,1)S(1)}, bf16[128,1024]{1,0:T(8,128)(2,1)S(1)}, u32[]{:S(2)}, u32[]{:S(2)}) collective-permute-start(bf16[128,1024]{1,0:T(8,128)(2,1)S(1)} %slice.191), channel_id=1, source_target_pairs={{0,2},{1,3},{2,0},{3,1},{4,6},{5,7},{6,4},{7,5},{8,10},{9,11},{10,... | collective-permute-start | bytes 786440 | tf_op jit(solution)/shard_map/ppermute | solution.py:24
  151.9 6.4 %collective-permute-start.38 = (bf16[128,1024]{1,0:T(8,128)(2,1)S(1)}, bf16[128,1024]{1,0:T(8,128)(2,1)S(1)}, u32[]{:S(2)}, u32[]{:S(2)}) collective-permute-start(bf16[128,1024]{1,0:T(8,128)(2,1)S(1)} %slice.166), channel_id=1, source_target_pairs={{0,2},{1,3},{2,0},{3,1},{4,6},{5,7},{6,4},{7,5},{8,10},{9,11},{10,... | collective-permute-start | bytes 786440 | tf_op jit(solution)/shard_map/ppermute | solution.py:24
  153.1 6.4 %collective-permute-start.39 = (bf16[128,1024]{1,0:T(8,128)(2,1)S(1)}, bf16[128,1024]{1,0:T(8,128)(2,1)S(1)}, u32[]{:S(2)}, u32[]{:S(2)}) collective-permute-start(bf16[128,1024]{1,0:T(8,128)(2,1)S(1)} %slice.167), channel_id=1, source_target_pairs={{0,16},{16,0},{1,17},{17,1},{2,18},{18,2},{3,19},{19,3},{4,20},{20... | collective-permute-start | bytes 786440 | tf_op jit(solution)/shard_map/ppermute | solution.py:24
  154.4 12.4 %collective-permute-start.40 = (bf16[128,2048]{1,0:T(8,128)(2,1)S(1)}, bf16[128,2048]{1,0:T(8,128)(2,1)S(1)}, u32[]{:S(2)}, u32[]{:S(2)}) collective-permute-start(bf16[128,2048]{1,0:T(8,128)(2,1)S(1)} %pad_maximum_fusion.3), channel_id=1, source_target_pairs={{0,4},{4,0},{8,12},{12,8},{1,5},{5,1},{9,13},{13,9},{2,6},{6,2},{1... | collective-permute-start | bytes 1572872 | tf_op jit(solution)/shard_map/ppermute | solution.py:24
  167.0 9.6 %collective-permute-start.41 = (bf16[64,2048]{1,0:T(8,128)(2,1)S(1)}, bf16[64,2048]{1,0:T(8,128)(2,1)S(1)}, u32[]{:S(2)}, u32[]{:S(2)}) collective-permute-start(bf16[64,2048]{1,0:T(8,128)(2,1)S(1)} %slice.243), channel_id=1, source_target_pairs={{0,8},{4,12},{8,0},{12,4},{1,9},{5,13},{9,1},{13,5},{2,10},{6,14},... | collective-permute-start | bytes 786440 | tf_op jit(solution)/shard_map/ppermute | solution.py:24

commit v4 on v3

--- a/solution.py
+++ b/solution.py
@@ -9,6 +9,7 @@
 PAIR = 1
 ACROSS = 2
 TILE = 256
+LANES = 128
 
 
 def rms_rows(values_in, gain_vec):
@@ -29,17 +30,11 @@
     return [1 << place for place in reversed(range(size.bit_length() - 1))]
 
 
-def seq_blocks(own):
-    blocks = [own]
+def seq_order():
+    order = [0]
     for bits in seq_bits():
-        blocks = blocks + [swap(block, "seq", bits) for block in blocks]
-    return blocks
-
-
-def spread_routes(own):
-    near = jnp.concatenate(seq_blocks(own), axis=0)
-    both = jnp.stack([near, swap(near, "rep", ACROSS)])
-    return jnp.concatenate([both, swap(both, "role", 1)], axis=0)
+        order = order + [place ^ bits for place in order]
+    return order
 
 
 def ready(*arrays):
@@ -62,13 +57,12 @@
     beyond = [swap(block, "seq", bits_left[-1]) for block in blocks[:-1]]
     outer = both_ways(own)
     middle = jnp.concatenate(blocks[1:] + beyond, axis=0)
-    middle, by_rep, by_role = ready(middle, *outer)
-    outer = by_rep, by_role
+    outer_low, outer_high = outer[0][:, :half], outer[1][:, half:]
+    middle, outer_low, outer_high = ready(middle, outer_low, outer_high)
+    outer_corner = swap(outer_low, "role", 1), swap(outer_high, "rep", ACROSS)
     last = swap(blocks[-1], "seq", bits_left[-1])
     rows = own.shape[0] + middle.shape[0] + last.shape[0]
     inner = both_ways(middle)
-    outer_corner = corners(*outer)
-    last, *outer_corner = ready(last, *outer_corner)
     final = both_ways(last)
     inner_corner = corners(*inner)
     early = early_work([(0, 0, own), (own.shape[0], 0, middle), (rows - last.shape[0], 0, last)])
@@ -130,6 +124,114 @@
             cut = total.shape[0] // 2
             total, leaving = total[:cut], total[cut:].astype(jnp.bfloat16)
     return total
+
+
+def prepare_kernel(tokens_ref, gain_ref, kv_ref, k_gain_ref, ids_ref, gates_ref, normed_ref, out_ref):
+    normed = rms_rows(tokens_ref[...].astype(jnp.float32), gain_ref[...]).astype(jnp.bfloat16)
+    normed_ref[...] = normed
+    kv_width, head_dim = kv_ref.shape[2], k_gain_ref.shape[1]
+    keys = jnp.dot(normed, kv_ref[0], preferred_element_type=jnp.float32)
+    for start in range(0, kv_width, head_dim):
+        head = rms_rows(keys[:, start : start + head_dim], k_gain_ref[...])
+        out_ref[:, start : start + head_dim] = head.astype(jnp.bfloat16)
+    values = jnp.dot(normed, kv_ref[1], preferred_element_type=jnp.float32)
+    out_ref[:, kv_width : 2 * kv_width] = values.astype(jnp.bfloat16)
+    ids, gates = ids_ref[...], gates_ref[...]
+    rest = jnp.zeros((ids.shape[0], LANES - 3 * ids.shape[1]), jnp.int32)
+    coded = jnp.concatenate([ids, gates // 64, gates % 64, rest], axis=1)
+    out_ref[:, 2 * kv_width :] = coded.astype(jnp.float32).astype(jnp.bfloat16)
+
+
+def prepare(tokens, attn_gain, w_keyval, k_gain, ids, gates):
+    rows, width = tokens.shape
+    return pl.pallas_call(
+        prepare_kernel,
+        out_shape=[
+            jax.ShapeDtypeStruct((rows, width), jnp.bfloat16),
+            jax.ShapeDtypeStruct((rows, 2 * w_keyval.shape[2] + LANES), jnp.bfloat16),
+        ],
+        compiler_params=pltpu.CompilerParams(vmem_limit_bytes=16 * 1024 * 1024),
+        cost_estimate=pl.CostEstimate(
+            flops=4 * rows * width * w_keyval.shape[2],
+            bytes_accessed=4 * width * w_keyval.shape[2] + 4 * rows * width,
+            transcendentals=rows,
+        ),
+        name="prepare",
+    )(tokens, attn_gain[None], w_keyval, k_gain[None], ids, gates)
+
+
+def queries_kernel(first_ref, second_ref, third_ref, fourth_ref, weight_ref, gain_ref, out_ref):
+    rows, head_dim = first_ref.shape[0], gain_ref.shape[1]
+    refs = (first_ref, second_ref, third_ref, fourth_ref)
+    held = jnp.concatenate([ref[...] for ref in refs], axis=0)
+    raw = jnp.dot(held, weight_ref[...], preferred_element_type=jnp.float32)
+    for start in range(0, weight_ref.shape[1], head_dim):
+        head = rms_rows(raw[:, start : start + head_dim], gain_ref[...])
+        out_ref[:, start : start + head_dim] = head.astype(jnp.bfloat16)
+
+
+def make_queries(blocks, w_query, q_gain):
+    rows, width = len(blocks) * blocks[0].shape[0], w_query.shape[1]
+    return pl.pallas_call(
+        queries_kernel,
+        out_shape=jax.ShapeDtypeStruct((rows, width), jnp.bfloat16),
+        compiler_params=pltpu.CompilerParams(vmem_limit_bytes=16 * 1024 * 1024),
+        cost_estimate=pl.CostEstimate(
+            flops=2 * rows * width * w_query.shape[0],
+            bytes_accessed=2 * width * w_query.shape[0],
+            transcendentals=rows,
+        ),
+        name="queries",
+    )(*blocks, w_query, q_gain[None])
+
+
+def attend_kernel(head_dim, query_ref, near_ref, far_ref, weight_ref, kept_ref, leaving_ref, held_ref):
+    keys = [ref[:, :head_dim] for ref in (near_ref, far_ref)]
+    values = [ref[:, head_dim:] for ref in (near_ref, far_ref)]
+    for start in range(0, query_ref.shape[1], head_dim):
+        query = query_ref[:, start : start + head_dim]
+        scores = [
+            lax.dot_general(
+                query, key, (((1,), (1,)), ((), ())), preferred_element_type=jnp.float32
+            )
+            * head_dim ** (-0.5)
+            for key in keys
+        ]
+        row_max = jnp.maximum(
+            jnp.max(scores[0], axis=1, keepdims=True), jnp.max(scores[1], axis=1, keepdims=True)
+        )
+        denom, total = 0.0, 0.0
+        for score, value in zip(scores, values):
+            weights = jnp.exp(score - row_max)
+            denom = denom + jnp.sum(weights, axis=1, keepdims=True)
+            total = total + jnp.dot(
+                weights.astype(jnp.bfloat16), value, preferred_element_type=jnp.float32
+            )
+        held_ref[:, start : start + head_dim] = (total / denom).astype(jnp.bfloat16)
+    cut = kept_ref.shape[0]
+    for column in range(0, weight_ref.shape[1], 2 * TILE):
+        columns = slice(column, column + 2 * TILE)
+        partial = jnp.dot(held_ref[...], weight_ref[:, columns], preferred_element_type=jnp.float32)
+        kept_ref[:, columns] = partial[:cut]
+        leaving_ref[:, columns] = partial[cut:]
+
+
+def attend(queries, near_kv, far_kv, w_out, head_dim):
+    rows, width = queries.shape
+    keys = 2 * near_kv.shape[0]
+    half = jax.ShapeDtypeStruct((rows // 2, w_out.shape[1]), jnp.float32)
+    return pl.pallas_call(
+        lambda *refs: attend_kernel(head_dim, *refs),
+        out_shape=[half, half],
+        scratch_shapes=[pltpu.VMEM((rows, width), jnp.bfloat16)],
+        compiler_params=pltpu.CompilerParams(vmem_limit_bytes=40 * 1024 * 1024),
+        cost_estimate=pl.CostEstimate(
+            flops=4 * rows * width * keys + 2 * rows * width * w_out.shape[1],
+            bytes_accessed=2 * width * w_out.shape[1] + 4 * rows * w_out.shape[1],
+            transcendentals=rows * keys * width // head_dim,
+        ),
+        name="attend",
+    )(queries, near_kv, far_kv, w_out)
 
 
 def expert_kernel(spots, *refs):
@@ -288,41 +390,55 @@
     top_count = expert_ids.shape[2]
     expert_count = lax.axis_size(EVERY)
 
-    normed = lax.optimization_barrier(rms_rows(tokens, attn_gain).astype(jnp.bfloat16))
+    normed, own_payload = prepare(
+        hidden_in[0], attn_gain, w_keyval, k_gain, expert_ids[0], gate_fixed[0]
+    )
+    across_rows = swap(normed, "rep", ACROSS)
     pair_rows = swap(normed, "rep", PAIR)
-    across_rows = swap(normed, "rep", ACROSS)
-    own_keys = jnp.dot(normed, w_keyval[0], preferred_element_type=jnp.float32)
-    own_values = jnp.dot(normed, w_keyval[1], preferred_element_type=jnp.float32)
-    own_keys = rms_rows(own_keys.reshape(row_count, kv_heads, head_dim), k_gain)
-    own_keys = own_keys.reshape(row_count, kv_width).astype(jnp.bfloat16)
-    own_kv = jnp.concatenate([own_keys, own_values.astype(jnp.bfloat16)], axis=1)
-    line_kv = jnp.concatenate(seq_blocks(own_kv), axis=0)
+    line = jnp.concatenate(
+        [own_payload] + [swap(own_payload, "seq", bits) for bits in seq_order()[1:]], axis=0
+    )
+    corner_rows = swap(across_rows, "rep", PAIR)
+    line_routes = line[:, 2 * kv_width :]
 
     def head_kv(rep):
         index = rep * local_heads // group_size * head_dim
-        return jnp.concatenate(
-            [
-                lax.dynamic_slice_in_dim(line_kv, index, head_dim, 1),
-                lax.dynamic_slice_in_dim(line_kv, kv_width + index, head_dim, 1),
-            ],
-            axis=1,
-        )
-
-    far_kv = swap(head_kv(rep_index ^ ACROSS), "rep", ACROSS)
-    half_kv = jnp.concatenate([head_kv(rep_index), far_kv], axis=0)
-    all_kv = jnp.concatenate([half_kv, swap(half_kv, "rep", PAIR)], axis=0)
-    key_rows, value_rows = all_kv[:, :head_dim], all_kv[:, head_dim:]
-
-    routes = spread_routes(jnp.concatenate([expert_ids[0], gate_fixed[0]], axis=1))
+        return [
+            lax.dynamic_slice_in_dim(line, index, head_dim, 1),
+            lax.dynamic_slice_in_dim(line, kv_width + index, head_dim, 1),
+        ]
+
+    sent = jnp.concatenate(head_kv(rep_index ^ ACROSS) + [line_routes], axis=1)
+    sent, across_rows, pair_rows = ready(sent, across_rows, pair_rows)
+    across = swap(sent, "rep", ACROSS)
+    half_kv = jnp.concatenate(
+        [jnp.concatenate(head_kv(rep_index), axis=1), across[:, : 2 * head_dim]], axis=0
+    )
+    pair_kv = swap(half_kv, "rep", PAIR)
+    both_routes = jnp.stack([line_routes, across[:, 2 * head_dim :]])
+    coded = jnp.concatenate([both_routes, swap(both_routes, "role", 1)], axis=0)
+    far_gu = swap(w_gateup[0], "rep", PAIR)
+    queries = make_queries([normed, across_rows, pair_rows, corner_rows], w_query, q_gain)
+    kept, leaving = attend(queries, half_kv, pair_kv, w_out, head_dim)
+    leaving, own_dn = ready(swap(leaving, "rep", PAIR), w_down[0])
+    halves = kept + leaving
+    far_dn = swap(own_dn, "rep", PAIR)
+    far_sum = halves[row_count:].astype(jnp.bfloat16)
+    attended = halves[:row_count] + swap(far_sum, "rep", ACROSS).astype(jnp.float32)
+    mixed = tokens + attended
+
+    coded = coded[:, :, : 3 * top_count].astype(jnp.int32)
+    routes = coded[:, :, :top_count]
+    gates = coded[:, :, top_count : 2 * top_count] * 64 + coded[:, :, 2 * top_count :]
+    gates = gates.astype(jnp.float32)
     groups, group_rows = routes.shape[:2]
     capacity = max(2, 7 * row_count * top_count // (4 * expert_count))
     slots = -(-capacity * (group_rows // row_count) // 16) * 16
-    gates = routes[:, :, top_count:].astype(jnp.float32)
     gate_sum = jnp.sum(gates, axis=2)
     earlier = jnp.tri(group_rows, k=-1, dtype=jnp.bfloat16)
     picks, shares = [], []
     for expert in (lax.axis_index(EVERY), lax.axis_index(EVERY) ^ PAIR):
-        named = routes[:, :, :top_count] == expert
+        named = routes == expert
         hit = jnp.any(named, axis=2)
         shares.append(jnp.sum(jnp.where(named, gates, 0.0), axis=2) / gate_sum)
         rank = jnp.einsum(
@@ -333,29 +449,6 @@
     pick = jnp.concatenate(picks, axis=1)
     place = jnp.stack([jnp.swapaxes(one, 1, 2) for one in picks])
     share = jnp.stack(shares, axis=2)
-
-    corner_rows = swap(across_rows, "rep", PAIR)
-    gathered = jnp.concatenate([normed, pair_rows, across_rows, corner_rows], axis=0)
-    far_gu = swap(w_gateup[0], "rep", PAIR)
-    far_dn = swap(w_down[0], "rep", PAIR)
-    projected = jnp.dot(gathered, w_query, preferred_element_type=jnp.float32)
-    query_span = projected.shape[0]
-    query_part = projected.reshape(query_span, local_heads, head_dim)
-    queries = rms_rows(query_part, q_gain).astype(jnp.bfloat16)
-    scores = jnp.einsum("qhd,kd->hqk", queries, key_rows, preferred_element_type=jnp.float32)
-    scores = scores * head_dim ** (-0.5)
-    weights = jnp.exp(scores - jnp.max(scores, axis=2, keepdims=True))
-    denom = jnp.sum(weights, axis=2)
-    context = jnp.einsum(
-        "hqk,kd->qhd", weights.astype(jnp.bfloat16), value_rows, preferred_element_type=jnp.float32
-    )
-    context = (context / denom.T[:, :, None]).astype(jnp.bfloat16)
-    context = context.reshape(query_span, local_heads * head_dim)
-    partial = jnp.dot(context, w_out, preferred_element_type=jnp.float32)
-    partial = partial.reshape(4, row_count, model_width)
-    back = swap(jnp.stack([partial[1], partial[3]]), "rep", PAIR)
-    far_sum = (partial[2] + back[1]).astype(jnp.bfloat16)
-    mixed = tokens + (partial[0] + back[0]) + swap(far_sum, "rep", ACROSS).astype(jnp.float32)
     mixed, far_gu, far_dn, pick, place, share = lax.optimization_barrier(
         (mixed, far_gu, far_dn, pick, place, share)
     )

time: 178 us -> 161 us (0.904)
  matrix products: 8.16 us -> 0.5 us
  other arithmetic: 11.4 us -> 5.36 us
  starting transfers between devices: 46.7 us -> 41.4 us
  Pallas kernels: 27.9 us -> 32 us
    dot_general x6 -> x0, matrix products: 7.67 us -> none  [the longest x1 3.26 us: per_device(): projected = jnp.dot(gathered, w_query, preferred_element_type=jnp.float32)]
    ppermute x42 -> x38, starting transfers between devices: 46.7 us -> 41.4 us  [swap(): return lax.ppermute(block, axis, [(i, i ^ bits) for i in range(size)])]
    unnamed x30 -> x33, local copies, waits for them, and re-layouts: 0.28 us -> 5.51 us
    pallas_call x0 -> x3, Pallas kernels: none -> 4.26 us  [the longest x1 2.72 us: attend(): pl.pallas_call(lambda *refs: attend_kernel(head_dim, *refs), out_shape=[h...]
    dot_general x2 -> x0, local copies, waits for them, and re-layouts: 3.78 us -> none  [per_device(): own_keys = jnp.dot(normed, w_keyval[0], preferred_element_type=jnp.float32)]
    concatenate x8 -> x2, other arithmetic: 2 us -> 0.05 us  [the longest x1 0.03 us: per_device(): sent = jnp.concatenate(head_kv(rep_index ^ ACROSS) + [line_routes], axis=1)]
    ppermute x42 -> x38, waiting for transfers between devices: 74.7 us -> 74.7 us  [swap(): return lax.ppermute(block, axis, [(i, i ^ bits) for i in range(size)])]
  transfers between devices with their start and end apart: 42 -> 38, of which waited for: 18 -> 23; matrix products, arithmetic and copies ran while one was open for 14% -> 4% of each run, Pallas kernels for 16% -> 20%
where the time goes in v4:
time: 161 us
  waiting for transfers between devices  74.7 us (46%)
  starting transfers between devices  41.4 us (26%)
  Pallas kernels  32 us (20%)
  local copies, waits for them, and re-layouts  6.14 us (4%)
  other arithmetic  5.36 us (3%)
    ppermute x38, waiting for transfers between devices, swap(): return lax.ppermute(block, axis, [(i, i ^ bits) for i in range(size)])  74.7 us
    ppermute x38, starting transfers between devices, swap(): return lax.ppermute(block, axis, [(i, i ^ bits) for i in range(size)])  41.4 us
    pallas_call x3, Pallas kernels, run_experts(): pl.pallas_call(lambda *refs: expert_kernel(spots, *refs), out_shape=[jax....  27.8 us
    unnamed x33, local copies, waits for them, and re-layouts  5.51 us
  transfers between devices with their start and end apart: 38, of which 23 were waited for; matrix products, arithmetic and copies ran while one was open for 4% of the time, Pallas kernels for 20%

profile of v4, /device:TPU:0, one launch (start us, length us, event | category | flops | bytes accessed | tf_op | source)
XLA Modules:
  0.0 160.6 jit_solution(9433408813688081160)
XLA Ops:
  0.5 0.8 copy.23
  1.2 0.8 copy.24
  2.0 1.6 copy-done
  3.6 0.9 copy-done.2
  4.5 0.7 copy-done.4
  5.2 0.7 copy-done.6
  5.9 0.7 prepare.1
  6.6 3.7 %collective-permute-start = (bf16[64,640]{1,0:T(8,128)(2,1)S(1)}, bf16[64,640]{1,0:T(8,128)(2,1)S(1)}, u32[]{:S(2)}, u32[]{:S(2)}) collective-permute-start(bf16[64,640]{1,0:T(8,128)(2,1)S(1)} %get-tuple-element.58), channel_id=1, source_target_pairs={{0,8},{4,12},{8,0},{12,4},{1,9},{5,13},{9,1},{13,5},{2,10},{6,14},... | collective-permute-start | bytes 245768 | tf_op jit(solution)/shard_map/ppermute | solution.py:25
  10.2 1.6 collective-permute-start.1
  11.8 1.7 %collective-permute-start.3 = (bf16[64,2048]{1,0:T(8,128)(2,1)S(1)}, bf16[64,2048]{1,0:T(8,128)(2,1)S(1)}, u32[]{:S(2)}, u32[]{:S(2)}) collective-permute-start(bf16[64,2048]{1,0:T(8,128)(2,1)S(1)} %get-tuple-element.57.first_ref), channel_id=1, source_target_pairs={{0,2},{1,3},{2,0},{3,1},{4,6},{5,7},{6,4},{7,5},{8,10},{9,11},{10,... | collective-permute-start | bytes 786440 | tf_op jit(solution)/shard_map/ppermute | solution.py:25
  13.6 1.7 %collective-permute-done = bf16[64,640]{1,0:T(8,128)(2,1)S(1)} collective-permute-done((bf16[64,640]{1,0:T(8,128)(2,1)S(1)}, bf16[64,640]{1,0:T(8,128)(2,1)S(1)}, u32[]{:S(2)}, u32[]{:S(2)}) %collective-permute-start) | collective-permute-done | bytes 81952 | tf_op jit(solution)/shard_map/ppermute | solution.py:25
  15.4 2.7 %collective-permute-done.2 = bf16[64,640]{1,0:T(8,128)(2,1)S(1)} collective-permute-done((bf16[64,640]{1,0:T(8,128)(2,1)S(1)}, bf16[64,640]{1,0:T(8,128)(2,1)S(1)}, u32[]{:S(2)}, u32[]{:S(2)}) %collective-permute-start.2) | collective-permute-done | bytes 81952 | tf_op jit(solution)/shard_map/ppermute | solution.py:25
  18.2 1.7 %collective-permute-done.3.second_ref = bf16[64,2048]{1,0:T(8,128)(2,1)S(1)} collective-permute-done((bf16[64,2048]{1,0:T(8,128)(2,1)S(1)}, bf16[64,2048]{1,0:T(8,128)(2,1)S(1)}, u32[]{:S(2)}, u32[]{:S(2)}) %collective-permute-start.3) | collective-permute-done | bytes 262176 | tf_op jit(solution)/shard_map/ppermute | solution.py:25
  20.0 1.5 collective-permute-start.6
  21.5 4.4 %collective-permute-done.6 = bf16[256,384]{1,0:T(8,128)(2,1)S(1)} collective-permute-done((bf16[256,384]{1,0:T(8,128)(2,1)S(1)}, bf16[256,384]{1,0:T(8,128)(2,1)S(1)}, u32[]{:S(2)}, u32[]{:S(2)}) %collective-permute-start.6) | collective-permute-done | bytes 196640 | tf_op jit(solution)/shard_map/ppermute | solution.py:25
  26.0 0.9 queries.1.refs_0_
  26.9 0.6 collective-permute-done.7.refs_2_
  27.5 2.7 %attend.1 = (f32[128,2048]{1,0:T(8,128)S(1)}, f32[128,2048]{1,0:T(8,128)S(1)}) custom-call(bf16[256,512]{1,0:T(8,128)(2,1)S(1)} %queries.1.refs_0_, bf16[512,256]{1,0:T(8,128)(2,1)S(1)} %pad_maximum_fusion.4.refs_1_, bf16[512,256]{1,0:T(8,128)(2,1)S(1)} %collective-permute-done.7.refs_2_, bf16[512,2048]{1,0:T(8,128)(2,1)S(1)} %copy-done.7), custom_call_target="tpu_custom_call" | custom-call | flops 1073741824 | bytes 4194304 | tf_op jit(solution)/shard_map/attend/pallas_call | solution.py:223
  30.4 2.5 %collective-permute-done.8 = f32[128,2048]{1,0:T(8,128)S(1)} collective-permute-done((f32[128,2048]{1,0:T(8,128)S(1)}, f32[128,2048]{1,0:T(8,128)S(1)}, u32[]{:S(2)}, u32[]{:S(2)}) %collective-permute-start.8) | collective-permute-done | bytes 1048608 | tf_op jit(solution)/shard_map/ppermute | solution.py:25
  33.1 1.4 collective-permute-start.12
  34.5 4.5 %collective-permute-done.12 = bf16[2,256,128]{2,1,0:T(8,128)(2,1)S(1)} collective-permute-done((bf16[2,256,128]{2,1,0:T(8,128)(2,1)S(1)}, bf16[2,256,128]{2,1,0:T(8,128)(2,1)S(1)}, u32[]{:S(2)}, u32[]{:S(2)}) %collective-permute-start.12) | collective-permute-done | bytes 131104 | tf_op jit(solution)/shard_map/ppermute | solution.py:25
  39.0 0.8 select_reduce_fusion.1
  41.5 1.4 collective-permute-start.9
  43.1 6.2 %collective-permute-done.9 = bf16[64,2048]{1,0:T(8,128)(2,1)S(1)} collective-permute-done((bf16[64,2048]{1,0:T(8,128)(2,1)S(1)}, bf16[64,2048]{1,0:T(8,128)(2,1)S(1)}, u32[]{:S(2)}, u32[]{:S(2)}) %collective-permute-start.9) | collective-permute-done | bytes 262176 | tf_op jit(solution)/shard_map/ppermute | solution.py:25
  49.7 2.6 %collective-permute-start.13 = (bf16[64,2048]{1,0:T(8,128)(2,1)S(1)}, bf16[64,2048]{1,0:T(8,128)(2,1)}, u32[]{:S(2)}, u32[]{:S(2)}) collective-permute-start(bf16[64,2048]{1,0:T(8,128)(2,1)S(1)} %multiply_convert_fusion.refs_7_), channel_id=1, source_target_pairs={{0,8},{4,12},{8,0},{12,4},{1,9},{5,13},{9,1},{13,5},{2,10},{6,14},... | collective-permute-start | bytes 786440 | tf_op jit(solution)/shard_map/ppermute | solution.py:25
  52.3 1.4 collective-permute-start.17
  53.7 1.5 collective-permute-start.18
  55.2 1.5 collective-permute-start.19
  56.9 6.4 %collective-permute-done.13 = bf16[64,2048]{1,0:T(8,128)(2,1)} collective-permute-done((bf16[64,2048]{1,0:T(8,128)(2,1)S(1)}, bf16[64,2048]{1,0:T(8,128)(2,1)}, u32[]{:S(2)}, u32[]{:S(2)}) %collective-permute-start.13) | collective-permute-done | bytes 262176 | tf_op jit(solution)/shard_map/ppermute | solution.py:25
  63.8 1.1 pad_maximum_fusion.refs_8_
  64.9 1.5 collective-permute-start.20
  66.4 1.5 collective-permute-start.21
  67.9 3.1 %collective-permute-done.14.refs_9_ = bf16[64,2048]{1,0:T(8,128)(2,1)S(1)} collective-permute-done((bf16[64,2048]{1,0:T(8,128)(2,1)}, bf16[64,2048]{1,0:T(8,128)(2,1)S(1)}, u32[]{:S(2)}, u32[]{:S(2)}) %collective-permute-start.14) | collective-permute-done | bytes 262176 | tf_op jit(solution)/shard_map/ppermute | solution.py:25
  71.0 1.2 collective-permute-start.15
  72.2 1.5 collective-permute-start.16
  73.8 0.6 collective-permute-start.22
  74.4 8.3 %experts.3 = (bf16[256,1024]{1,0:T(8,128)(2,1)S(1)}, bf16[256,1024]{1,0:T(8,128)(2,1)S(1)}) custom-call(bf16[1,224,256]{2,1,0:T(8,128)(2,1)S(1)} %get-tuple-element.119.refs_0_, bf16[2,1,256,112]{3,2,1,0:T(8,128)(2,1)S(1)} %get-tuple-element.117.refs_1_, f32[1,256,2]{2,1,0:T(8,128)S(1)} %get-tuple-element.115.refs_2_, bf16[2048,1536]{1,0:T(8,128)(2,1)} %bitcast.28, ...), custom_call_target="tpu_custom_call" | custom-call | flops 2113929216 | bytes 20971520 | tf_op jit(solution)/shard_map/experts/pallas_call | solution.py:340
  82.7 1.3 collective-permute-done.15.refs_9_
  84.0 1.5 collective-permute-start.23
  85.5 1.1 collective-permute-done.16.refs_12_
  86.6 1.6 collective-permute-start.26
  88.2 0.6 collective-permute-start.27
  88.8 0.6 collective-permute-start.24
  89.5 1.6 collective-permute-start.25
  91.1 10.3 %experts.4 = (bf16[256,1024]{1,0:T(8,128)(2,1)}, bf16[256,1024]{1,0:T(8,128)(2,1)}, bf16[256,1024]{1,0:T(8,128)(2,1)}, bf16[256,1024]{1,0:T(8,128)(2,1)}) custom-call(bf16[2,224,256]{2,1,0:T(8,128)(2,1)S(1)} %slice.131.refs_0_, bf16[2,2,256,112]{3,2,1,0:T(8,128)(2,1)S(1)} %slice.132.refs_1_, f32[2,256,2]{2,1,0:T(8,128)S(1)} %slice.165.refs_2_, ...), custom_call_target="tpu_custom_call" | custom-call | flops 4227858432 | bytes 23068672 | tf_op jit(solution)/shard_map/experts/pallas_call | solution.py:340
  101.4 1.6 collective-permute-start.28
  103.5 9.2 %experts.5 = (bf16[256,1024]{1,0:T(8,128)(2,1)S(1)}, bf16[256,1024]{1,0:T(8,128)(2,1)}) custom-call(bf16[1,224,256]{2,1,0:T(8,128)(2,1)S(1)} %get-tuple-element.118.refs_0_, bf16[2,1,256,112]{3,2,1,0:T(8,128)(2,1)S(1)} %get-tuple-element.116.refs_1_, f32[1,256,2]{2,1,0:T(8,128)S(1)} %get-tuple-element.114.refs_2_, bf16[2048,1536]{1,0:T(8,128)(2,1)} %bitcast.30, ...), custom_call_target="tpu_custom_call" | custom-call | flops 2113929216 | bytes 20971520 | tf_op jit(solution)/shard_map/experts/pallas_call | solution.py:340
  112.7 1.3 collective-permute-done.29
  113.9 0.5 collective-permute-start.30
  114.4 0.7 collective-permute-start.31
  115.2 9.1 %collective-permute-done.30 = bf16[256,1024]{1,0:T(8,128)(2,1)S(1)} collective-permute-done((bf16[256,1024]{1,0:T(8,128)(2,1)S(1)}, bf16[256,1024]{1,0:T(8,128)(2,1)S(1)}, u32[]{:S(2)}, u32[]{:S(2)}) %collective-permute-start.30) | collective-permute-done | bytes 524320 | tf_op jit(solution)/shard_map/ppermute | solution.py:25
  124.3 1.4 collective-permute-done.31
  125.9 1.1 collective-permute-start.33
  127.7 6.8 %collective-permute-done.33 = bf16[128,1024]{1,0:T(8,128)(2,1)S(1)} collective-permute-done((bf16[128,1024]{1,0:T(8,128)(2,1)S(1)}, bf16[128,1024]{1,0:T(8,128)(2,1)S(1)}, u32[]{:S(2)}, u32[]{:S(2)}) %collective-permute-start.33) | collective-permute-done | bytes 262176 | tf_op jit(solution)/shard_map/ppermute | solution.py:25
  134.4 0.7 collective-permute-done.32
  135.2 1.0 collective-permute-start.34
  136.2 1.0 collective-permute-start.35
  137.5 1.8 %collective-permute-start.36 = (bf16[128,2048]{1,0:T(8,128)(2,1)S(1)}, bf16[128,2048]{1,0:T(8,128)(2,1)S(1)}, u32[]{:S(2)}, u32[]{:S(2)}) collective-permute-start(bf16[128,2048]{1,0:T(8,128)(2,1)S(1)} %pad_maximum_fusion.1), channel_id=1, source_target_pairs={{0,4},{4,0},{8,12},{12,8},{1,5},{5,1},{9,13},{13,9},{2,6},{6,2},{1... | collective-permute-start | bytes 1572872 | tf_op jit(solution)/shard_map/ppermute | solution.py:25
  139.3 2.3 %collective-permute-done.34 = bf16[128,1024]{1,0:T(8,128)(2,1)S(1)} collective-permute-done((bf16[128,1024]{1,0:T(8,128)(2,1)S(1)}, bf16[128,1024]{1,0:T(8,128)(2,1)S(1)}, u32[]{:S(2)}, u32[]{:S(2)}) %collective-permute-start.34) | collective-permute-done | bytes 262176 | tf_op jit(solution)/shard_map/ppermute | solution.py:25
  141.6 1.0 collective-permute-done.35
  142.8 6.7 %collective-permute-done.36 = bf16[128,2048]{1,0:T(8,128)(2,1)S(1)} collective-permute-done((bf16[128,2048]{1,0:T(8,128)(2,1)S(1)}, bf16[128,2048]{1,0:T(8,128)(2,1)S(1)}, u32[]{:S(2)}, u32[]{:S(2)}) %collective-permute-start.36) | collective-permute-done | bytes 524320 | tf_op jit(solution)/shard_map/ppermute | solution.py:25
  149.7 1.2 collective-permute-start.37
  150.9 9.0 %collective-permute-done.37 = bf16[64,2048]{1,0:T(8,128)(2,1)S(1)} collective-permute-done((bf16[64,2048]{1,0:T(8,128)(2,1)S(1)}, bf16[64,2048]{1,0:T(8,128)(2,1)S(1)}, u32[]{:S(2)}, u32[]{:S(2)}) %collective-permute-start.37) | collective-permute-done | bytes 262176 | tf_op jit(solution)/shard_map/ppermute | solution.py:25
  159.9 0.8 fusion.6
  (105 shorter events, 6.3 us)
Async XLA Ops:
  0.0 26.0 %copy-start.5 = (f32[128]{0:T(128)S(1)}, f32[128]{0:T(128)}, u32[]{:S(2)}) copy-start(f32[128]{0:T(128)} %param.16) | copy-start | bytes 1540
  0.0 49.4 %collective-permute-start.10 = (bf16[2048,1536]{1,0:T(8,128)(2,1)}, bf16[2048,1536]{1,0:T(8,128)(2,1)}, u32[]{:S(2)}, u32[]{:S(2)}) collective-permute-start(bf16[2048,1536]{1,0:T(8,128)(2,1)} %bitcast.27), channel_id=1, source_target_pairs={{0,1},{1,0},{2,3},{3,2},{4,5},{5,4},{6,7},{7,6},{8,9},{9,8},{10,11... | collective-permute-start | bytes 18874376 | tf_op jit(solution)/shard_map/ppermute | solution.py:25
  2.0 1.6 copy-start
  3.6 0.9 copy-start.2
  4.5 0.7 copy-start.4
  5.2 0.7 copy-start.6
  5.9 20.1 %copy-start.1 = (bf16[2048,512]{1,0:T(8,128)(2,1)S(1)}, bf16[2048,512]{1,0:T(8,128)(2,1)}, u32[]{:S(2)}) copy-start(bf16[2048,512]{1,0:T(8,128)(2,1)} %weight_ref.1) | copy-start | bytes 6291460
  6.6 8.7 %collective-permute-start = (bf16[64,640]{1,0:T(8,128)(2,1)S(1)}, bf16[64,640]{1,0:T(8,128)(2,1)S(1)}, u32[]{:S(2)}, u32[]{:S(2)}) collective-permute-start(bf16[64,640]{1,0:T(8,128)(2,1)S(1)} %get-tuple-element.58), channel_id=1, source_target_pairs={{0,8},{4,12},{8,0},{12,4},{1,9},{5,13},{9,1},{13,5},{2,10},{6,14},... | collective-permute-start | bytes 245768 | tf_op jit(solution)/shard_map/ppermute | solution.py:25
  10.2 5.2 %collective-permute-start.1 = (bf16[64,640]{1,0:T(8,128)(2,1)S(1)}, bf16[64,640]{1,0:T(8,128)(2,1)S(1)}, u32[]{:S(2)}, u32[]{:S(2)}) collective-permute-start(bf16[64,640]{1,0:T(8,128)(2,1)S(1)} %get-tuple-element.58), channel_id=1, source_target_pairs={{0,4},{4,0},{8,12},{12,8},{1,5},{5,1},{9,13},{13,9},{2,6},{6,2},{1... | collective-permute-start | bytes 245768 | tf_op jit(solution)/shard_map/ppermute | solution.py:25
  11.8 6.3 %collective-permute-start.2 = (bf16[64,640]{1,0:T(8,128)(2,1)S(1)}, bf16[64,640]{1,0:T(8,128)(2,1)S(1)}, u32[]{:S(2)}, u32[]{:S(2)}) collective-permute-start(bf16[64,640]{1,0:T(8,128)(2,1)S(1)} %get-tuple-element.58), channel_id=1, source_target_pairs={{0,12},{4,8},{8,4},{12,0},{1,13},{5,9},{9,5},{13,1},{2,14},{6,10},... | collective-permute-start | bytes 245768 | tf_op jit(solution)/shard_map/ppermute | solution.py:25
  11.8 8.1 %collective-permute-start.3 = (bf16[64,2048]{1,0:T(8,128)(2,1)S(1)}, bf16[64,2048]{1,0:T(8,128)(2,1)S(1)}, u32[]{:S(2)}, u32[]{:S(2)}) collective-permute-start(bf16[64,2048]{1,0:T(8,128)(2,1)S(1)} %get-tuple-element.57.first_ref), channel_id=1, source_target_pairs={{0,2},{1,3},{2,0},{3,1},{4,6},{5,7},{6,4},{7,5},{8,10},{9,11},{10,... | collective-permute-start | bytes 786440 | tf_op jit(solution)/shard_map/ppermute | solution.py:25
  13.6 13.9 %copy-start.7 = (bf16[512,2048]{1,0:T(8,128)(2,1)S(1)}, bf16[512,2048]{1,0:T(8,128)(2,1)}, u32[]{:S(2)}) copy-start(bf16[512,2048]{1,0:T(8,128)(2,1)} %refs_3_.1) | copy-start | bytes 6291460
  15.3 4.7 %collective-permute-start.4 = (bf16[64,2048]{1,0:T(8,128)(2,1)S(1)}, bf16[64,2048]{1,0:T(8,128)(2,1)S(1)}, u32[]{:S(2)}, u32[]{:S(2)}) collective-permute-start(bf16[64,2048]{1,0:T(8,128)(2,1)S(1)} %get-tuple-element.57.first_ref), channel_id=1, source_target_pairs={{0,1},{1,0},{2,3},{3,2},{4,5},{5,4},{6,7},{7,6},{8,9},{9,8},{10,11... | collective-permute-start | bytes 786440 | tf_op jit(solution)/shard_map/ppermute | solution.py:25
  20.0 5.9 %collective-permute-start.6 = (bf16[256,384]{1,0:T(8,128)(2,1)S(1)}, bf16[256,384]{1,0:T(8,128)(2,1)S(1)}, u32[]{:S(2)}, u32[]{:S(2)}) collective-permute-start(bf16[256,384]{1,0:T(8,128)(2,1)S(1)} %pad_maximum_fusion.5), channel_id=1, source_target_pairs={{0,2},{1,3},{2,0},{3,1},{4,6},{5,7},{6,4},{7,5},{8,10},{9,11},{10,... | collective-permute-start | bytes 589832 | tf_op jit(solution)/shard_map/ppermute | solution.py:25
  21.5 4.5 %collective-permute-start.5 = (bf16[64,2048]{1,0:T(8,128)(2,1)S(1)}, bf16[64,2048]{1,0:T(8,128)(2,1)S(1)}, u32[]{:S(2)}, u32[]{:S(2)}) collective-permute-start(bf16[64,2048]{1,0:T(8,128)(2,1)S(1)} %collective-permute-done.3.second_ref), channel_id=1, source_target_pairs={{0,1},{1,0},{2,3},{3,2},{4,5},{5,4},{6,7},{7,6},{8,9},{9,8},{10,11... | collective-permute-start | bytes 786440 | tf_op jit(solution)/shard_map/ppermute | solution.py:25
  25.9 1.6 collective-permute-start.7
  30.2 2.7 %collective-permute-start.8 = (f32[128,2048]{1,0:T(8,128)S(1)}, f32[128,2048]{1,0:T(8,128)S(1)}, u32[]{:S(2)}, u32[]{:S(2)}) collective-permute-start(f32[128,2048]{1,0:T(8,128)S(1)} %get-tuple-element.63), channel_id=1, source_target_pairs={{0,1},{1,0},{2,3},{3,2},{4,5},{5,4},{6,7},{7,6},{8,9},{9,8},{10,11... | collective-permute-start | bytes 3145736 | tf_op jit(solution)/shard_map/ppermute | solution.py:25
  33.0 16.4 %collective-permute-start.11 = (bf16[768,2048]{1,0:T(8,128)(2,1)}, bf16[768,2048]{1,0:T(8,128)(2,1)}, u32[]{:S(2)}, u32[]{:S(2)}) collective-permute-start(bf16[768,2048]{1,0:T(8,128)(2,1)} %bitcast.6.refs_5_), channel_id=1, source_target_pairs={{0,1},{1,0},{2,3},{3,2},{4,5},{5,4},{6,7},{7,6},{8,9},{9,8},{10,11... | collective-permute-start | bytes 9437192 | tf_op jit(solution)/shard_map/ppermute | solution.py:25
  33.1 5.8 %collective-permute-start.12 = (bf16[2,256,128]{2,1,0:T(8,128)(2,1)S(1)}, bf16[2,256,128]{2,1,0:T(8,128)(2,1)S(1)}, u32[]{:S(2)}, u32[]{:S(2)}) collective-permute-start(bf16[2,256,128]{2,1,0:T(8,128)(2,1)S(1)} %pad_maximum_fusion.6), channel_id=1, source_target_pairs={{0,16},{16,0},{1,17},{17,1},{2,18},{18,2},{3,19},{19,3},{4,20},{20... | collective-permute-start | bytes 393224 | tf_op jit(solution)/shard_map/ppermute | solution.py:25
  39.8 9.5 %copy-start.3 = (bf16[1,64,2048]{2,1,0:T(8,128)(2,1)S(1)}, bf16[1,64,2048]{2,1,0:T(8,128)(2,1)}, u32[]{:S(2)}) copy-start(bf16[1,64,2048]{2,1,0:T(8,128)(2,1)} %param.12) | copy-start | bytes 786436
  41.3 8.3 %copy-start.13 = (f32[2048]{0:T(1024)S(1)}, f32[2048]{0:T(1024)}, u32[]{:S(2)}) copy-start(f32[2048]{0:T(1024)} %param.19) | copy-start | bytes 24580
  41.5 7.8 %collective-permute-start.9 = (bf16[64,2048]{1,0:T(8,128)(2,1)S(1)}, bf16[64,2048]{1,0:T(8,128)(2,1)S(1)}, u32[]{:S(2)}, u32[]{:S(2)}) collective-permute-start(bf16[64,2048]{1,0:T(8,128)(2,1)S(1)} %slice.216), channel_id=1, source_target_pairs={{0,2},{1,3},{2,0},{3,1},{4,6},{5,7},{6,4},{7,5},{8,10},{9,11},{10,... | collective-permute-start | bytes 786440 | tf_op jit(solution)/shard_map/ppermute | solution.py:25
  49.7 13.7 %collective-permute-start.13 = (bf16[64,2048]{1,0:T(8,128)(2,1)S(1)}, bf16[64,2048]{1,0:T(8,128)(2,1)}, u32[]{:S(2)}, u32[]{:S(2)}) collective-permute-start(bf16[64,2048]{1,0:T(8,128)(2,1)S(1)} %multiply_convert_fusion.refs_7_), channel_id=1, source_target_pairs={{0,8},{4,12},{8,0},{12,4},{1,9},{5,13},{9,1},{13,5},{2,10},{6,14},... | collective-permute-start | bytes 786440 | tf_op jit(solution)/shard_map/ppermute | solution.py:25
  52.3 11.5 %collective-permute-start.17 = (bf16[64,2048]{1,0:T(8,128)(2,1)S(1)}, bf16[64,2048]{1,0:T(8,128)(2,1)}, u32[]{:S(2)}, u32[]{:S(2)}) collective-permute-start(bf16[64,2048]{1,0:T(8,128)(2,1)S(1)} %multiply_convert_fusion.refs_7_), channel_id=1, source_target_pairs={{0,4},{4,0},{8,12},{12,8},{1,5},{5,1},{9,13},{13,9},{2,6},{6,2},{1... | collective-permute-start | bytes 786440 | tf_op jit(solution)/shard_map/ppermute | solution.py:25
  53.7 11.2 %collective-permute-start.18 = (bf16[64,2048]{1,0:T(8,128)(2,1)S(1)}, bf16[64,2048]{1,0:T(8,128)(2,1)S(1)}, u32[]{:S(2)}, u32[]{:S(2)}) collective-permute-start(bf16[64,2048]{1,0:T(8,128)(2,1)S(1)} %multiply_convert_fusion.refs_7_), channel_id=1, source_target_pairs={{0,2},{1,3},{2,0},{3,1},{4,6},{5,7},{6,4},{7,5},{8,10},{9,11},{10,... | collective-permute-start | bytes 786440 | tf_op jit(solution)/shard_map/ppermute | solution.py:25
  55.2 9.7 %collective-permute-start.19 = (bf16[64,2048]{1,0:T(8,128)(2,1)S(1)}, bf16[64,2048]{1,0:T(8,128)(2,1)S(1)}, u32[]{:S(2)}, u32[]{:S(2)}) collective-permute-start(bf16[64,2048]{1,0:T(8,128)(2,1)S(1)} %multiply_convert_fusion.refs_7_), channel_id=1, source_target_pairs={{0,16},{16,0},{1,17},{17,1},{2,18},{18,2},{3,19},{19,3},{4,20},{20... | collective-permute-start | bytes 786440 | tf_op jit(solution)/shard_map/ppermute | solution.py:25
  63.3 7.6 %collective-permute-start.14 = (bf16[64,2048]{1,0:T(8,128)(2,1)}, bf16[64,2048]{1,0:T(8,128)(2,1)S(1)}, u32[]{:S(2)}, u32[]{:S(2)}) collective-permute-start(bf16[64,2048]{1,0:T(8,128)(2,1)} %collective-permute-done.13), channel_id=1, source_target_pairs={{0,4},{4,0},{8,12},{12,8},{1,5},{5,1},{9,13},{13,9},{2,6},{6,2},{1... | collective-permute-start | bytes 786440 | tf_op jit(solution)/shard_map/ppermute | solution.py:25
  64.8 9.6 %copy-start.8 = (bf16[128,2048]{1,0:T(8,128)(2,1)}, bf16[128,2048]{1,0:T(8,128)(2,1)S(1)}, u32[]{:S(2)}) copy-start(bf16[128,2048]{1,0:T(8,128)(2,1)S(1)} %pad_maximum_fusion.refs_8_) | copy-start | bytes 1572868
  64.9 23.3 %collective-permute-start.20 = (bf16[128,2048]{1,0:T(8,128)(2,1)S(1)}, bf16[128,2048]{1,0:T(8,128)(2,1)S(1)}, u32[]{:S(2)}, u32[]{:S(2)}) collective-permute-start(bf16[128,2048]{1,0:T(8,128)(2,1)S(1)} %pad_maximum_fusion.refs_8_), channel_id=1, source_target_pairs={{0,2},{1,3},{2,0},{3,1},{4,6},{5,7},{6,4},{7,5},{8,10},{9,11},{10,... | collective-permute-start | bytes 1572872 | tf_op jit(solution)/shard_map/ppermute | solution.py:25
  66.4 22.4 %collective-permute-start.21 = (bf16[128,2048]{1,0:T(8,128)(2,1)S(1)}, bf16[128,2048]{1,0:T(8,128)(2,1)S(1)}, u32[]{:S(2)}, u32[]{:S(2)}) collective-permute-start(bf16[128,2048]{1,0:T(8,128)(2,1)S(1)} %pad_maximum_fusion.refs_8_), channel_id=1, source_target_pairs={{0,16},{16,0},{1,17},{17,1},{2,18},{18,2},{3,19},{19,3},{4,20},{20... | collective-permute-start | bytes 1572872 | tf_op jit(solution)/shard_map/ppermute | solution.py:25
  71.0 13.0 %collective-permute-start.15 = (bf16[64,2048]{1,0:T(8,128)(2,1)S(1)}, bf16[64,2048]{1,0:T(8,128)(2,1)S(1)}, u32[]{:S(2)}, u32[]{:S(2)}) collective-permute-start(bf16[64,2048]{1,0:T(8,128)(2,1)S(1)} %collective-permute-done.14.refs_9_), channel_id=1, source_target_pairs={{0,2},{1,3},{2,0},{3,1},{4,6},{5,7},{6,4},{7,5},{8,10},{9,11},{10,... | collective-permute-start | bytes 786440 | tf_op jit(solution)/shard_map/ppermute | solution.py:25
  72.2 14.4 %collective-permute-start.16 = (bf16[64,2048]{1,0:T(8,128)(2,1)S(1)}, bf16[64,2048]{1,0:T(8,128)(2,1)S(1)}, u32[]{:S(2)}, u32[]{:S(2)}) collective-permute-start(bf16[64,2048]{1,0:T(8,128)(2,1)S(1)} %collective-permute-done.14.refs_9_), channel_id=1, source_target_pairs={{0,16},{16,0},{1,17},{17,1},{2,18},{18,2},{3,19},{19,3},{4,20},{20... | collective-permute-start | bytes 786440 | tf_op jit(solution)/shard_map/ppermute | solution.py:25
  73.8 15.7 %collective-permute-start.22 = (bf16[64,1024]{1,0:T(8,128)(2,1)S(1)}, bf16[64,1024]{1,0:T(8,128)(2,1)S(1)}, u32[]{:S(2)}, u32[]{:S(2)}) collective-permute-start(bf16[64,1024]{1,0:T(8,128)(2,1)S(1)} %slice.163), channel_id=1, source_target_pairs={{0,16},{16,0},{1,17},{17,1},{2,18},{18,2},{3,19},{19,3},{4,20},{20... | collective-permute-start | bytes 393224 | tf_op jit(solution)/shard_map/ppermute | solution.py:25
  84.0 17.4 %collective-permute-start.23 = (bf16[64,1024]{1,0:T(8,128)(2,1)S(1)}, bf16[64,1024]{1,0:T(8,128)(2,1)S(1)}, u32[]{:S(2)}, u32[]{:S(2)}) collective-permute-start(bf16[64,1024]{1,0:T(8,128)(2,1)S(1)} %slice.164), channel_id=1, source_target_pairs={{0,2},{1,3},{2,0},{3,1},{4,6},{5,7},{6,4},{7,5},{8,10},{9,11},{10,... | collective-permute-start | bytes 393224 | tf_op jit(solution)/shard_map/ppermute | solution.py:25
  86.6 14.7 %collective-permute-start.26 = (bf16[64,1024]{1,0:T(8,128)(2,1)S(1)}, bf16[64,1024]{1,0:T(8,128)(2,1)S(1)}, u32[]{:S(2)}, u32[]{:S(2)}) collective-permute-start(bf16[64,1024]{1,0:T(8,128)(2,1)S(1)} %slice.136), channel_id=1, source_target_pairs={{0,16},{16,0},{1,17},{17,1},{2,18},{18,2},{3,19},{19,3},{4,20},{20... | collective-permute-start | bytes 393224 | tf_op jit(solution)/shard_map/ppermute | solution.py:25
  88.2 2.8 %copy-start.9 = (bf16[128,2048]{1,0:T(8,128)(2,1)}, bf16[128,2048]{1,0:T(8,128)(2,1)S(1)}, u32[]{:S(2)}) copy-start(bf16[128,2048]{1,0:T(8,128)(2,1)S(1)} %collective-permute-done.20.refs_8_) | copy-start | bytes 1572868
  88.2 13.1 %collective-permute-start.27 = (bf16[64,1024]{1,0:T(8,128)(2,1)S(1)}, bf16[64,1024]{1,0:T(8,128)(2,1)S(1)}, u32[]{:S(2)}, u32[]{:S(2)}) collective-permute-start(bf16[64,1024]{1,0:T(8,128)(2,1)S(1)} %slice.137), channel_id=1, source_target_pairs={{0,2},{1,3},{2,0},{3,1},{4,6},{5,7},{6,4},{7,5},{8,10},{9,11},{10,... | collective-permute-start | bytes 393224 | tf_op jit(solution)/shard_map/ppermute | solution.py:25
  88.8 2.2 %copy-start.10 = (bf16[128,2048]{1,0:T(8,128)(2,1)}, bf16[128,2048]{1,0:T(8,128)(2,1)S(1)}, u32[]{:S(2)}) copy-start(bf16[128,2048]{1,0:T(8,128)(2,1)S(1)} %collective-permute-done.21.refs_11_) | copy-start | bytes 1572868
  88.8 12.6 %collective-permute-start.24 = (bf16[128,1024]{1,0:T(8,128)(2,1)S(1)}, bf16[128,1024]{1,0:T(8,128)(2,1)S(1)}, u32[]{:S(2)}, u32[]{:S(2)}) collective-permute-start(bf16[128,1024]{1,0:T(8,128)(2,1)S(1)} %slice.166), channel_id=1, source_target_pairs={{0,16},{16,0},{1,17},{17,1},{2,18},{18,2},{3,19},{19,3},{4,20},{20... | collective-permute-start | bytes 786440 | tf_op jit(solution)/shard_map/ppermute | solution.py:25
  89.5 11.9 %collective-permute-start.25 = (bf16[128,1024]{1,0:T(8,128)(2,1)S(1)}, bf16[128,1024]{1,0:T(8,128)(2,1)S(1)}, u32[]{:S(2)}, u32[]{:S(2)}) collective-permute-start(bf16[128,1024]{1,0:T(8,128)(2,1)S(1)} %slice.167), channel_id=1, source_target_pairs={{0,2},{1,3},{2,0},{3,1},{4,6},{5,7},{6,4},{7,5},{8,10},{9,11},{10,... | collective-permute-start | bytes 786440 | tf_op jit(solution)/shard_map/ppermute | solution.py:25
  101.4 11.3 %collective-permute-start.28 = (bf16[256,1024]{1,0:T(8,128)(2,1)}, bf16[256,1024]{1,0:T(8,128)(2,1)S(1)}, u32[]{:S(2)}, u32[]{:S(2)}) collective-permute-start(bf16[256,1024]{1,0:T(8,128)(2,1)} %get-tuple-element.84), channel_id=1, source_target_pairs={{0,16},{16,0},{1,17},{17,1},{2,18},{18,2},{3,19},{19,3},{4,20},{20... | collective-permute-start | bytes 1572872 | tf_op jit(solution)/shard_map/ppermute | solution.py:25
  103.0 11.0 %collective-permute-start.29 = (bf16[256,1024]{1,0:T(8,128)(2,1)}, bf16[256,1024]{1,0:T(8,128)(2,1)S(1)}, u32[]{:S(2)}, u32[]{:S(2)}) collective-permute-start(bf16[256,1024]{1,0:T(8,128)(2,1)} %get-tuple-element.85), channel_id=1, source_target_pairs={{0,2},{1,3},{2,0},{3,1},{4,6},{5,7},{6,4},{7,5},{8,10},{9,11},{10,... | collective-permute-start | bytes 1572872 | tf_op jit(solution)/shard_map/ppermute | solution.py:25
  103.5 22.2 %copy-start.12 = (bf16[256,1024]{1,0:T(8,128)(2,1)S(1)}, bf16[256,1024]{1,0:T(8,128)(2,1)}, u32[]{:S(2)}) copy-start(bf16[256,1024]{1,0:T(8,128)(2,1)} %get-tuple-element.99) | copy-start | bytes 1572868
  103.5 23.5 %copy-start.11 = (bf16[256,1024]{1,0:T(8,128)(2,1)S(1)}, bf16[256,1024]{1,0:T(8,128)(2,1)}, u32[]{:S(2)}) copy-start(bf16[256,1024]{1,0:T(8,128)(2,1)} %get-tuple-element.95) | copy-start | bytes 1572868
  113.9 10.3 %collective-permute-start.30 = (bf16[256,1024]{1,0:T(8,128)(2,1)S(1)}, bf16[256,1024]{1,0:T(8,128)(2,1)S(1)}, u32[]{:S(2)}, u32[]{:S(2)}) collective-permute-start(bf16[256,1024]{1,0:T(8,128)(2,1)S(1)} %get-tuple-element.96), channel_id=1, source_target_pairs={{0,16},{16,0},{1,17},{17,1},{2,18},{18,2},{3,19},{19,3},{4,20},{20... | collective-permute-start | bytes 1572872 | tf_op jit(solution)/shard_map/ppermute | solution.py:25
  114.4 11.2 %collective-permute-start.31 = (bf16[256,1024]{1,0:T(8,128)(2,1)}, bf16[256,1024]{1,0:T(8,128)(2,1)S(1)}, u32[]{:S(2)}, u32[]{:S(2)}) collective-permute-start(bf16[256,1024]{1,0:T(8,128)(2,1)} %get-tuple-element.97), channel_id=1, source_target_pairs={{0,2},{1,3},{2,0},{3,1},{4,6},{5,7},{6,4},{7,5},{8,10},{9,11},{10,... | collective-permute-start | bytes 1572872 | tf_op jit(solution)/shard_map/ppermute | solution.py:25
  125.9 8.5 %collective-permute-start.33 = (bf16[128,1024]{1,0:T(8,128)(2,1)S(1)}, bf16[128,1024]{1,0:T(8,128)(2,1)S(1)}, u32[]{:S(2)}, u32[]{:S(2)}) collective-permute-start(bf16[128,1024]{1,0:T(8,128)(2,1)S(1)} %slice.170), channel_id=1, source_target_pairs={{0,16},{16,0},{1,17},{17,1},{2,18},{18,2},{3,19},{19,3},{4,20},{20... | collective-permute-start | bytes 786440 | tf_op jit(solution)/shard_map/ppermute | solution.py:25
  127.2 7.9 %collective-permute-start.32 = (bf16[128,1024]{1,0:T(8,128)(2,1)S(1)}, bf16[128,1024]{1,0:T(8,128)(2,1)S(1)}, u32[]{:S(2)}, u32[]{:S(2)}) collective-permute-start(bf16[128,1024]{1,0:T(8,128)(2,1)S(1)} %slice.169), channel_id=1, source_target_pairs={{0,2},{1,3},{2,0},{3,1},{4,6},{5,7},{6,4},{7,5},{8,10},{9,11},{10,... | collective-permute-start | bytes 786440 | tf_op jit(solution)/shard_map/ppermute | solution.py:25
  135.2 6.4 %collective-permute-start.34 = (bf16[128,1024]{1,0:T(8,128)(2,1)S(1)}, bf16[128,1024]{1,0:T(8,128)(2,1)S(1)}, u32[]{:S(2)}, u32[]{:S(2)}) collective-permute-start(bf16[128,1024]{1,0:T(8,128)(2,1)S(1)} %slice.144), channel_id=1, source_target_pairs={{0,2},{1,3},{2,0},{3,1},{4,6},{5,7},{6,4},{7,5},{8,10},{9,11},{10,... | collective-permute-start | bytes 786440 | tf_op jit(solution)/shard_map/ppermute | solution.py:25
  136.2 6.4 %collective-permute-start.35 = (bf16[128,1024]{1,0:T(8,128)(2,1)S(1)}, bf16[128,1024]{1,0:T(8,128)(2,1)S(1)}, u32[]{:S(2)}, u32[]{:S(2)}) collective-permute-start(bf16[128,1024]{1,0:T(8,128)(2,1)S(1)} %slice.145), channel_id=1, source_target_pairs={{0,16},{16,0},{1,17},{17,1},{2,18},{18,2},{3,19},{19,3},{4,20},{20... | collective-permute-start | bytes 786440 | tf_op jit(solution)/shard_map/ppermute | solution.py:25
  137.5 12.1 %collective-permute-start.36 = (bf16[128,2048]{1,0:T(8,128)(2,1)S(1)}, bf16[128,2048]{1,0:T(8,128)(2,1)S(1)}, u32[]{:S(2)}, u32[]{:S(2)}) collective-permute-start(bf16[128,2048]{1,0:T(8,128)(2,1)S(1)} %pad_maximum_fusion.1), channel_id=1, source_target_pairs={{0,4},{4,0},{8,12},{12,8},{1,5},{5,1},{9,13},{13,9},{2,6},{6,2},{1... | collective-permute-start | bytes 1572872 | tf_op jit(solution)/shard_map/ppermute | solution.py:25
  149.7 10.1 %collective-permute-start.37 = (bf16[64,2048]{1,0:T(8,128)(2,1)S(1)}, bf16[64,2048]{1,0:T(8,128)(2,1)S(1)}, u32[]{:S(2)}, u32[]{:S(2)}) collective-permute-start(bf16[64,2048]{1,0:T(8,128)(2,1)S(1)} %slice.215), channel_id=1, source_target_pairs={{0,8},{4,12},{8,0},{12,4},{1,9},{5,13},{9,1},{13,5},{2,10},{6,14},... | collective-permute-start | bytes 786440 | tf_op jit(solution)/shard_map/ppermute | solution.py:25

commit v5 on v4

--- a/solution.py
+++ b/solution.py
@@ -126,7 +126,19 @@
     return total
 
 
-def prepare_kernel(tokens_ref, gain_ref, kv_ref, k_gain_ref, ids_ref, gates_ref, normed_ref, out_ref):
+def prepare_kernel(*refs):
+    tokens_in, gain_in, kv_in, k_gain_in, ids_in, gates_in, normed_ref, out_ref = refs[:8]
+    held, sem = refs[8:14], refs[14]
+    sources = (tokens_in, gain_in, kv_in, k_gain_in, ids_in, gates_in)
+    copies = [
+        pltpu.make_async_copy(src, dst, sem.at[number])
+        for number, (src, dst) in enumerate(zip(sources, held))
+    ]
+    for copy in copies:
+        copy.start()
+    for copy in copies:
+        copy.wait()
+    tokens_ref, gain_ref, kv_ref, k_gain_ref, ids_ref, gates_ref = held
     normed = rms_rows(tokens_ref[...].astype(jnp.float32), gain_ref[...]).astype(jnp.bfloat16)
     normed_ref[...] = normed
     kv_width, head_dim = kv_ref.shape[2], k_gain_ref.shape[1]
@@ -136,20 +148,33 @@
         out_ref[:, start : start + head_dim] = head.astype(jnp.bfloat16)
     values = jnp.dot(normed, kv_ref[1], preferred_element_type=jnp.float32)
     out_ref[:, kv_width : 2 * kv_width] = values.astype(jnp.bfloat16)
-    ids, gates = ids_ref[...], gates_ref[...]
-    rest = jnp.zeros((ids.shape[0], LANES - 3 * ids.shape[1]), jnp.int32)
-    coded = jnp.concatenate([ids, gates // 64, gates % 64, rest], axis=1)
-    out_ref[:, 2 * kv_width :] = coded.astype(jnp.float32).astype(jnp.bfloat16)
+    coded = jnp.concatenate([ids_ref[...], gates_ref[...] // 64, gates_ref[...] % 64], axis=0)
+    count = coded.shape[0]
+    spread = lax.broadcasted_iota(jnp.int32, (count, LANES), 0)
+    spread = spread == lax.broadcasted_iota(jnp.int32, (count, LANES), 1)
+    out_ref[:, 2 * kv_width :] = lax.dot_general(
+        coded.astype(jnp.float32).astype(jnp.bfloat16),
+        spread.astype(jnp.float32).astype(jnp.bfloat16),
+        (((0,), (0,)), ((), ())),
+        preferred_element_type=jnp.float32,
+    ).astype(jnp.bfloat16)
 
 
 def prepare(tokens, attn_gain, w_keyval, k_gain, ids, gates):
     rows, width = tokens.shape
+    operands = [
+        pltpu.with_memory_space_constraint(one, pltpu.HBM)
+        for one in (tokens, attn_gain[None], w_keyval, k_gain[None], ids.T, gates.T)
+    ]
     return pl.pallas_call(
         prepare_kernel,
         out_shape=[
             jax.ShapeDtypeStruct((rows, width), jnp.bfloat16),
             jax.ShapeDtypeStruct((rows, 2 * w_keyval.shape[2] + LANES), jnp.bfloat16),
         ],
+        in_specs=[pl.BlockSpec(memory_space=pltpu.HBM)] * len(operands),
+        scratch_shapes=[pltpu.VMEM(one.shape, one.dtype) for one in operands]
+        + [pltpu.SemaphoreType.DMA((len(operands),))],
         compiler_params=pltpu.CompilerParams(vmem_limit_bytes=16 * 1024 * 1024),
         cost_estimate=pl.CostEstimate(
             flops=4 * rows * width * w_keyval.shape[2],
@@ -157,7 +182,7 @@
             transcendentals=rows,
         ),
         name="prepare",
-    )(tokens, attn_gain[None], w_keyval, k_gain[None], ids, gates)
+    )(*operands)
 
 
 def queries_kernel(first_ref, second_ref, third_ref, fourth_ref, weight_ref, gain_ref, out_ref):
@@ -239,70 +264,44 @@
     groups, group_rows, slots = place_ref.shape[1:]
     piece_refs = refs[7 : 7 + len(spots)]
     out_refs = refs[7 + len(spots) : 7 + len(spots) + 2 * groups]
-    x_buf, xs_buf, gu_buf, dn_buf, hid_buf, served_buf, y_buf, x_sem, w_sem, y_sem = refs[
-        7 + len(spots) + 2 * groups :
-    ]
-    width = x_buf.shape[2]
+    xs_buf, hid_buf, served_buf = refs[7 + len(spots) + 2 * groups :]
+    hidden, width = own_dn_ref.shape
     half = width // 2
-    hidden = own_dn_ref.shape[0]
-    tiles = hidden // TILE
-
-    row_copies = []
-    for number, ((group, row, column), piece) in enumerate(zip(spots, piece_refs)):
-        rows, columns = piece.shape
-        target = x_buf.at[group, pl.ds(row, rows), pl.ds(column, columns)]
-        row_copies.append((group, pltpu.make_async_copy(piece, target, x_sem.at[number])))
-    weight_copies = []
+
+    for group in range(groups):
+        for column in range(0, width, half):
+            held = [
+                (row, piece[:, column - start : column - start + half])
+                for (where, row, start), piece in zip(spots, piece_refs)
+                if where == group and start <= column < start + piece.shape[1]
+            ]
+            held = jnp.concatenate([block for _, block in sorted(held, key=lambda e: e[0])], axis=0)
+            chosen = jnp.dot(pick_ref[group], held, preferred_element_type=jnp.float32)
+            chosen = chosen.astype(jnp.bfloat16)
+            for expert in range(2):
+                xs_buf[expert, pl.ds(group * slots, slots), column : column + half] = chosen[
+                    expert * slots : (expert + 1) * slots
+                ]
+
     for expert, (gu_ref, dn_ref) in enumerate(((own_gu_ref, own_dn_ref), (far_gu_ref, far_dn_ref))):
-        mine = []
-        for tile in range(tiles):
-            for side in range(2):
-                mine.append(
-                    pltpu.make_async_copy(
-                        gu_ref.at[:, pl.ds(side * hidden + tile * TILE, TILE)],
-                        gu_buf.at[expert, tile, side],
-                        w_sem.at[expert, 2 * tile + side],
-                    )
+        for column in range(0, hidden, TILE):
+            gate, up = (
+                jnp.dot(
+                    xs_buf[expert],
+                    gu_ref[:, start : start + TILE],
+                    preferred_element_type=jnp.float32,
                 )
-        mine.append(pltpu.make_async_copy(dn_ref, dn_buf.at[expert], w_sem.at[expert, 2 * tiles]))
-        weight_copies.append(mine)
-    for _, copy in row_copies:
-        copy.start()
-    for mine in weight_copies:
-        for copy in mine:
-            copy.start()
-
-    for group in range(groups):
-        for where, copy in row_copies:
-            if where == group:
-                copy.wait()
-        chosen = jnp.dot(
-            pick_ref[group], x_buf[group], preferred_element_type=jnp.float32
-        ).astype(jnp.bfloat16)
-        xs_buf[0, pl.ds(group * slots, slots)] = chosen[:slots]
-        xs_buf[1, pl.ds(group * slots, slots)] = chosen[slots:]
-
-    for expert in range(2):
-        for tile in range(tiles):
-            weight_copies[expert][2 * tile].wait()
-            weight_copies[expert][2 * tile + 1].wait()
-            gate = jnp.dot(
-                xs_buf[expert], gu_buf[expert, tile, 0], preferred_element_type=jnp.float32
-            )
-            up = jnp.dot(
-                xs_buf[expert], gu_buf[expert, tile, 1], preferred_element_type=jnp.float32
+                for start in (column, hidden + column)
             )
             value = gate / (1.0 + jnp.exp(-gate)) * up
-            hid_buf[:, tile * TILE : (tile + 1) * TILE] = value.astype(jnp.bfloat16)
-        weight_copies[expert][2 * tiles].wait()
+            hid_buf[:, column : column + TILE] = value.astype(jnp.bfloat16)
         for column in range(0, width, 2 * TILE):
             served_buf[expert, :, column : column + 2 * TILE] = jnp.dot(
                 hid_buf[...],
-                dn_buf[expert, :, column : column + 2 * TILE],
+                dn_ref[:, column : column + 2 * TILE],
                 preferred_element_type=jnp.float32,
             ).astype(jnp.bfloat16)
 
-    out_copies = []
     for group in range(groups):
         for column in range(0, width, 2 * TILE):
             total = None
@@ -314,47 +313,28 @@
                 )
                 term = placed * share_ref[group, :, expert : expert + 1]
                 total = term if total is None else total + term
-            y_buf[group, :, column : column + 2 * TILE] = total.astype(jnp.bfloat16)
-        for side in range(2):
-            copy = pltpu.make_async_copy(
-                y_buf.at[group, :, pl.ds(side * half, half)],
-                out_refs[2 * group + side],
-                y_sem.at[group, side],
-            )
-            copy.start()
-            out_copies.append(copy)
-    for copy in out_copies:
-        copy.wait()
+            start = column % half
+            out_ref = out_refs[2 * group + column // half]
+            out_ref[:, start : start + 2 * TILE] = total.astype(jnp.bfloat16)
 
 
 def run_experts(pieces, pick, place, share, weights):
     groups, group_rows, slots = place.shape[1:]
     hidden, width = weights[2].shape
-    tiles = hidden // TILE
     spots = [
         (group, row, column) for group, held in enumerate(pieces) for row, column, _ in held
     ]
     arrays = [array for held in pieces for _, _, array in held]
-    anywhere = pl.BlockSpec(memory_space=pl.ANY)
-    inside = pl.BlockSpec(memory_space=pltpu.VMEM)
     outs = pl.pallas_call(
         lambda *refs: expert_kernel(spots, *refs),
         out_shape=[jax.ShapeDtypeStruct((group_rows, width // 2), jnp.bfloat16)] * (2 * groups),
-        in_specs=[inside] * 3 + [anywhere] * (4 + len(arrays)),
-        out_specs=[anywhere] * (2 * groups),
+        in_specs=[pl.BlockSpec(memory_space=pltpu.VMEM)] * (7 + len(arrays)),
         scratch_shapes=[
-            pltpu.VMEM((groups, group_rows, width), jnp.bfloat16),
             pltpu.VMEM((2, groups * slots, width), jnp.bfloat16),
-            pltpu.VMEM((2, tiles, 2, width, TILE), jnp.bfloat16),
-            pltpu.VMEM((2, hidden, width), jnp.bfloat16),
             pltpu.VMEM((groups * slots, hidden), jnp.bfloat16),
             pltpu.VMEM((2, groups * slots, width), jnp.bfloat16),
-            pltpu.VMEM((groups, group_rows, width), jnp.bfloat16),
-            pltpu.SemaphoreType.DMA((len(arrays),)),
-            pltpu.SemaphoreType.DMA((2, 2 * tiles + 1)),
-            pltpu.SemaphoreType.DMA((groups, 2)),
         ],
-        compiler_params=pltpu.CompilerParams(vmem_limit_bytes=52 * 1024 * 1024),
+        compiler_params=pltpu.CompilerParams(vmem_limit_bytes=28 * 1024 * 1024),
         cost_estimate=pl.CostEstimate(
             flops=12 * groups * slots * width * hidden,
             bytes_accessed=12 * width * hidden + 4 * groups * group_rows * width,
@@ -420,12 +400,16 @@
     far_gu = swap(w_gateup[0], "rep", PAIR)
     queries = make_queries([normed, across_rows, pair_rows, corner_rows], w_query, q_gain)
     kept, leaving = attend(queries, half_kv, pair_kv, w_out, head_dim)
+    kept, leaving, coded = ready(kept, leaving, coded)
     leaving, own_dn = ready(swap(leaving, "rep", PAIR), w_down[0])
     halves = kept + leaving
     far_dn = swap(own_dn, "rep", PAIR)
     far_sum = halves[row_count:].astype(jnp.bfloat16)
     attended = halves[:row_count] + swap(far_sum, "rep", ACROSS).astype(jnp.float32)
     mixed = tokens + attended
+
+    mixed, far_gu, far_dn, coded = ready(mixed, far_gu, far_dn, coded)
+    moe_in = rms_rows(mixed, moe_gain).astype(jnp.bfloat16)
 
     coded = coded[:, :, : 3 * top_count].astype(jnp.int32)
     routes = coded[:, :, :top_count]
@@ -449,12 +433,11 @@
     pick = jnp.concatenate(picks, axis=1)
     place = jnp.stack([jnp.swapaxes(one, 1, 2) for one in picks])
     share = jnp.stack(shares, axis=2)
-    mixed, far_gu, far_dn, pick, place, share = lax.optimization_barrier(
-        (mixed, far_gu, far_dn, pick, place, share)
-    )
-    moe_in = rms_rows(mixed, moe_gain).astype(jnp.bfloat16)
-
-    weights = (w_gateup[0], far_gu, w_down[0], far_dn)
+
+    weights = [
+        pltpu.with_memory_space_constraint(one, pltpu.VMEM)
+        for one in (w_gateup[0], far_gu, w_down[0], far_dn)
+    ]
 
     def serve(pieces, first, last):
         return run_experts(

time: 161 us -> 188 us (1.17)
  local copies, waits for them, and re-layouts: 6.14 us -> 29.3 us
  other arithmetic: 5.36 us -> 17.9 us
  waiting for transfers between devices: 74.7 us -> 65 us
    unnamed x33 -> x86, local copies, waits for them, and re-layouts: 5.51 us -> 22.3 us
    ppermute x38, waiting for transfers between devices: 74.7 us -> 65 us  [swap(): return lax.ppermute(block, axis, [(i, i ^ bits) for i in range(size)])]
    slice x2, local copies, waits for them, and re-layouts: 0.02 us -> 3.13 us  [spread_rows(): outer_low, outer_high = (outer[0][:, :half], outer[1][:, half:])]
    slice x0 -> x2, other arithmetic: none -> 2.99 us  [the longest x1 1.53 us: serve(): place[:, first:last]]
    add x1, other arithmetic: 0.08 us -> 2.05 us  [per_device(): mixed = tokens + attended]
    another operation x2, other arithmetic: 0.24 us -> 2.14 us
    add x2, other arithmetic: 0.21 us -> 2.11 us  [merged(): base[rows].astype(jnp.float32) + first[rows].astype(jnp.float32)]
  transfers between devices with their start and end apart: 38 -> 38, of which waited for: 23 -> 17; matrix products, arithmetic and copies ran while one was open for 4% -> 11% of each run, Pallas kernels for 20% -> 17%
where the time goes in v5:
time: 188 us; the launch traced here: 187 us
  waiting for transfers between devices  65 us (35%)
  starting transfers between devices  41.3 us (22%)
  Pallas kernels  32.1 us (17%)
  local copies, waits for them, and re-layouts  29.3 us (16%)
  other arithmetic  17.9 us (10%)
    ppermute x38, waiting for transfers between devices, swap(): return lax.ppermute(block, axis, [(i, i ^ bits) for i in range(size)])  65 us
    ppermute x38, starting transfers between devices, swap(): return lax.ppermute(block, axis, [(i, i ^ bits) for i in range(size)])  41.3 us
    pallas_call x3, Pallas kernels, run_experts(): pl.pallas_call(lambda *refs: expert_kernel(spots, *refs), out_shape=[jax....  26.1 us
    unnamed x86, local copies, waits for them, and re-layouts  22.3 us
  transfers between devices with their start and end apart: 38, of which 17 were waited for; matrix products, arithmetic and copies ran while one was open for 11% of the time, Pallas kernels for 17%

profile of v5, /device:TPU:0, one launch (start us, length us, event | category | flops | bytes accessed | tf_op | source)
XLA Modules:
  0.0 186.6 jit_solution(3538146675381156891)
XLA Ops:
  0.5 2.4 %prepare.1 = (bf16[64,2048]{1,0:T(8,128)(2,1)S(1)}, bf16[64,640]{1,0:T(8,128)(2,1)S(1)}) custom-call(bf16[64,2048]{1,0:T(8,128)(2,1)} %bitcast.34, f32[1,2048]{1,0:T(1,128)} %bitcast.35, bf16[2,2048,256]{2,1,0:T(8,128)(2,1)} %refs_2_.1, f32[1,128]{1,0:T(1,128)} %bitcast.38, s32[8,64]{1,0:T(8,128)} %bitcast.36, s32[8,64]{1,0:T(8,128)} %bitcast.37), custom_call_target="tpu_custom_call" | custom-call | flops 134217728 | bytes 2621440 | tf_op jit(solution)/shard_map/prepare/pallas_call | solution.py:169
  2.9 3.7 %collective-permute-start = (bf16[64,640]{1,0:T(8,128)(2,1)S(1)}, bf16[64,640]{1,0:T(8,128)(2,1)S(1)}, u32[]{:S(2)}, u32[]{:S(2)}) collective-permute-start(bf16[64,640]{1,0:T(8,128)(2,1)S(1)} %get-tuple-element.59), channel_id=1, source_target_pairs={{0,8},{4,12},{8,0},{12,4},{1,9},{5,13},{9,1},{13,5},{2,10},{6,14},... | collective-permute-start | bytes 245768 | tf_op jit(solution)/shard_map/ppermute | solution.py:25
  6.6 1.6 collective-permute-start.1
  8.1 1.7 collective-permute-start.3
  9.9 1.7 collective-permute-done
  11.7 2.7 %collective-permute-done.2 = bf16[64,640]{1,0:T(8,128)(2,1)S(1)} collective-permute-done((bf16[64,640]{1,0:T(8,128)(2,1)S(1)}, bf16[64,640]{1,0:T(8,128)(2,1)S(1)}, u32[]{:S(2)}, u32[]{:S(2)}) %collective-permute-start.2) | collective-permute-done | bytes 81952 | tf_op jit(solution)/shard_map/ppermute | solution.py:25
  14.6 1.7 collective-permute-done.3.second_ref
  16.3 1.5 collective-permute-start.6
  17.8 4.4 %collective-permute-done.6 = bf16[256,384]{1,0:T(8,128)(2,1)S(1)} collective-permute-done((bf16[256,384]{1,0:T(8,128)(2,1)S(1)}, bf16[256,384]{1,0:T(8,128)(2,1)S(1)}, u32[]{:S(2)}, u32[]{:S(2)}) %collective-permute-start.6) | collective-permute-done | bytes 196640 | tf_op jit(solution)/shard_map/ppermute | solution.py:25
  22.3 1.3 collective-permute-start.8
  23.7 0.9 copy-done.21
  25.5 2.8 %collective-permute-done.8 = bf16[2,256,128]{2,1,0:T(8,128)(2,1)S(1)} collective-permute-done((bf16[2,256,128]{2,1,0:T(8,128)(2,1)S(1)}, bf16[2,256,128]{2,1,0:T(8,128)(2,1)S(1)}, u32[]{:S(2)}, u32[]{:S(2)}) %collective-permute-start.8) | collective-permute-done | bytes 131104 | tf_op jit(solution)/shard_map/ppermute | solution.py:25
  28.3 1.6 copy-done.31
  29.9 2.7 %attend.1 = (f32[128,2048]{1,0:T(8,128)S(1)}, f32[128,2048]{1,0:T(8,128)S(1)}) custom-call(bf16[256,512]{1,0:T(8,128)(2,1)S(1)} %queries.1.refs_0_, bf16[512,256]{1,0:T(8,128)(2,1)S(1)} %pad_maximum_fusion.2.refs_1_, bf16[512,256]{1,0:T(8,128)(2,1)S(1)} %collective-permute-done.7.refs_2_, bf16[512,2048]{1,0:T(8,128)(2,1)S(1)} %copy-done.31), custom_call_target="tpu_custom_call" | custom-call | flops 1073741824 | bytes 4194304 | tf_op jit(solution)/shard_map/attend/pallas_call | solution.py:248
  32.7 2.6 %collective-permute-done.9 = f32[128,2048]{1,0:T(8,128)S(1)} collective-permute-done((f32[128,2048]{1,0:T(8,128)S(1)}, f32[128,2048]{1,0:T(8,128)S(1)}, u32[]{:S(2)}, u32[]{:S(2)}) %collective-permute-start.9) | collective-permute-done | bytes 1048608 | tf_op jit(solution)/shard_map/ppermute | solution.py:25
  35.7 1.0 copy-done.33
  37.4 1.3 collective-permute-start.10
  38.7 7.6 %collective-permute-done.10 = bf16[64,2048]{1,0:T(8,128)(2,1)} collective-permute-done((bf16[64,2048]{1,0:T(8,128)(2,1)}, bf16[64,2048]{1,0:T(8,128)(2,1)}, u32[]{:S(2)}, u32[]{:S(2)}) %collective-permute-start.10) | collective-permute-done | bytes 262176 | tf_op jit(solution)/shard_map/ppermute | solution.py:25
  46.3 2.1 %fusion.5 = f32[64,2048]{1,0:T(8,128)} fusion(f32[128,2048]{1,0:T(8,128)} %copy-done.33, bf16[64,2048]{1,0:T(8,128)(2,1)} %collective-permute-done.10, bf16[1,64,2048]{2,1,0:T(8,128)(2,1)} %param.12), kind=kLoop, calls=%fused_computation.18 | loop fusion | flops 524288 | bytes 1572864 | tf_op jit(solution)/shard_map/add | solution.py:409
  50.7 1.3 multiply_reduce_fusion
  52.0 1.9 multiply_convert_fusion.refs_7_
  53.8 1.3 collective-permute-start.18
  55.9 3.3 %collective-permute-start.13 = (bf16[64,2048]{1,0:T(8,128)(2,1)}, bf16[64,2048]{1,0:T(8,128)(2,1)}, u32[]{:S(2)}, u32[]{:S(2)}) collective-permute-start(bf16[64,2048]{1,0:T(8,128)(2,1)} %multiply_convert_fusion.refs_7_), channel_id=1, source_target_pairs={{0,8},{4,12},{8,0},{12,4},{1,9},{5,13},{9,1},{13,5},{2,10},{6,14},... | collective-permute-start | bytes 786440 | tf_op jit(solution)/shard_map/ppermute | solution.py:25
  59.2 1.5 collective-permute-start.19
  62.7 4.3 %collective-permute-done.13 = bf16[64,2048]{1,0:T(8,128)(2,1)} collective-permute-done((bf16[64,2048]{1,0:T(8,128)(2,1)}, bf16[64,2048]{1,0:T(8,128)(2,1)}, u32[]{:S(2)}, u32[]{:S(2)}) %collective-permute-start.13) | collective-permute-done | bytes 262176 | tf_op jit(solution)/shard_map/ppermute | solution.py:25
  66.9 4.4 %collective-permute-start.14 = (bf16[64,2048]{1,0:T(8,128)(2,1)}, bf16[64,2048]{1,0:T(8,128)(2,1)}, u32[]{:S(2)}, u32[]{:S(2)}) collective-permute-start(bf16[64,2048]{1,0:T(8,128)(2,1)} %collective-permute-done.13), channel_id=1, source_target_pairs={{0,4},{4,0},{8,12},{12,8},{1,5},{5,1},{9,13},{13,9},{2,6},{6,2},{1... | collective-permute-start | bytes 786440 | tf_op jit(solution)/shard_map/ppermute | solution.py:25
  71.3 1.9 %pad_maximum_fusion.refs_8_ = bf16[128,2048]{1,0:T(8,128)(2,1)} fusion(bf16[64,2048]{1,0:T(8,128)(2,1)} %collective-permute-done.17, bf16[64,2048]{1,0:T(8,128)(2,1)} %collective-permute-done.13), kind=kLoop, calls=%fused_computation.19 | loop fusion | flops 1048576 | bytes 1048576 | tf_op jit(solution)/shard_map/concatenate | solution.py:59
  73.2 1.6 slice.162
  74.7 1.6 slice.163
  76.8 1.5 collective-permute-start.21
  78.5 1.5 add_convert_fusion.6
  80.0 1.5 collective-permute-start.15
  82.0 1.5 add_convert_fusion.8
  83.5 1.5 collective-permute-start.22
  85.0 2.8 %copy-done = bf16[1,2048,1536]{2,1,0:T(8,128)(2,1)S(1)} copy-done((bf16[1,2048,1536]{2,1,0:T(8,128)(2,1)S(1)}, bf16[1,2048,1536]{2,1,0:T(8,128)(2,1)}, u32[]{:S(2)}) %copy-start) | copy-done | bytes 6291480
  87.8 7.7 %experts.3 = (bf16[256,1024]{1,0:T(8,128)(2,1)S(1)}, bf16[256,1024]{1,0:T(8,128)(2,1)S(1)}) custom-call(bf16[1,224,256]{2,1,0:T(8,128)(2,1)S(1)} %get-tuple-element.125.refs_0_, bf16[2,1,256,112]{3,2,1,0:T(8,128)(2,1)S(1)} %get-tuple-element.123.refs_1_, f32[1,256,2]{2,1,0:T(8,128)S(1)} %copy.20.refs_2_, bf16[2048,1536]{1,0:T(8,128)(2,1)S(1)} %bitcast.26, ...), custom_call_target="tpu_custom_call" | custom-call | flops 2113929216 | bytes 20971520 | tf_op jit(solution)/shard_map/experts/pallas_call | solution.py:328
  96.1 1.1 slice.168
  97.9 1.0 slice.169
  98.8 1.6 collective-permute-start.25
  100.4 1.6 collective-permute-start.26
  103.2 10.9 %experts.4 = (bf16[256,1024]{1,0:T(8,128)(2,1)S(1)}, bf16[256,1024]{1,0:T(8,128)(2,1)}, bf16[256,1024]{1,0:T(8,128)(2,1)}, bf16[256,1024]{1,0:T(8,128)(2,1)S(1)}) custom-call(bf16[2,224,256]{2,1,0:T(8,128)(2,1)S(1)} %copy-done.5, bf16[2,2,256,112]{3,2,1,0:T(8,128)(2,1)S(1)} %slice.165.refs_1_, f32[2,256,2]{2,1,0:T(8,128)S(1)} %copy-done.4, ...), custom_call_target="tpu_custom_call" | custom-call | flops 4227858432 | bytes 23068672 | tf_op jit(solution)/shard_map/experts/pallas_call | solution.py:328
  119.6 1.5 collective-permute-start.29
  121.3 2.8 %copy-done.1 = bf16[1,2048,1536]{2,1,0:T(8,128)(2,1)S(1)} copy-done((bf16[1,2048,1536]{2,1,0:T(8,128)(2,1)S(1)}, bf16[1,2048,1536]{2,1,0:T(8,128)(2,1)}, u32[]{:S(2)}) %copy-start.1) | copy-done | bytes 6291480
  124.1 0.9 copy-done.15
  125.0 0.9 copy-done.17
  125.9 0.9 copy-done.19
  126.9 0.9 copy-done.23
  127.8 0.9 copy-done.25
  128.7 0.9 copy-done.27
  129.6 0.9 copy-done.29
  130.5 7.5 %experts.5 = (bf16[256,1024]{1,0:T(8,128)(2,1)S(1)}, bf16[256,1024]{1,0:T(8,128)(2,1)S(1)}) custom-call(bf16[1,224,256]{2,1,0:T(8,128)(2,1)S(1)} %copy-done.15, bf16[2,1,256,112]{3,2,1,0:T(8,128)(2,1)S(1)} %copy-done.6, f32[1,256,2]{2,1,0:T(8,128)S(1)} %copy.22.refs_2_, bf16[2048,1536]{1,0:T(8,128)(2,1)S(1)} %bitcast.28, ...), custom_call_target="tpu_custom_call" | custom-call | flops 2113929216 | bytes 20971520 | tf_op jit(solution)/shard_map/experts/pallas_call | solution.py:328
  138.1 1.5 collective-permute-start.30
  140.1 8.8 %collective-permute-done.30 = bf16[256,1024]{1,0:T(8,128)(2,1)S(1)} collective-permute-done((bf16[256,1024]{1,0:T(8,128)(2,1)S(1)}, bf16[256,1024]{1,0:T(8,128)(2,1)S(1)}, u32[]{:S(2)}, u32[]{:S(2)}) %collective-permute-start.30) | collective-permute-done | bytes 524320 | tf_op jit(solution)/shard_map/ppermute | solution.py:25
  148.9 2.7 %collective-permute-done.31 = bf16[256,1024]{1,0:T(8,128)(2,1)S(1)} collective-permute-done((bf16[256,1024]{1,0:T(8,128)(2,1)S(1)}, bf16[256,1024]{1,0:T(8,128)(2,1)S(1)}, u32[]{:S(2)}, u32[]{:S(2)}) %collective-permute-start.31) | collective-permute-done | bytes 524320 | tf_op jit(solution)/shard_map/ppermute | solution.py:25
  153.2 6.1 %collective-permute-done.32 = bf16[128,1024]{1,0:T(8,128)(2,1)S(1)} collective-permute-done((bf16[128,1024]{1,0:T(8,128)(2,1)S(1)}, bf16[128,1024]{1,0:T(8,128)(2,1)S(1)}, u32[]{:S(2)}, u32[]{:S(2)}) %collective-permute-start.32) | collective-permute-done | bytes 262176 | tf_op jit(solution)/shard_map/ppermute | solution.py:25
  159.7 1.5 collective-permute-start.34
  162.0 1.1 add_convert_fusion.4
  163.1 1.1 add_convert_fusion.5
  164.3 1.9 collective-permute-done.34
  166.2 1.6 collective-permute-done.35
  167.7 1.1 convert_add_fusion
  168.8 1.1 convert_add_fusion.1
  169.9 6.3 %collective-permute-done.36 = bf16[128,2048]{1,0:T(8,128)(2,1)S(1)} collective-permute-done((bf16[128,2048]{1,0:T(8,128)(2,1)S(1)}, bf16[128,2048]{1,0:T(8,128)(2,1)S(1)}, u32[]{:S(2)}, u32[]{:S(2)}) %collective-permute-start.36) | collective-permute-done | bytes 524320 | tf_op jit(solution)/shard_map/ppermute | solution.py:25
  176.4 9.4 %collective-permute-done.37 = bf16[64,2048]{1,0:T(8,128)(2,1)S(1)} collective-permute-done((bf16[64,2048]{1,0:T(8,128)(2,1)S(1)}, bf16[64,2048]{1,0:T(8,128)(2,1)S(1)}, u32[]{:S(2)}, u32[]{:S(2)}) %collective-permute-start.37) | collective-permute-done | bytes 262176 | tf_op jit(solution)/shard_map/ppermute | solution.py:25
  (157 shorter events, 21.4 us)
Async XLA Ops:
  0.0 23.7 %copy-start.30 = (f32[128]{0:T(128)S(1)}, f32[128]{0:T(128)}, u32[]{:S(2)}) copy-start(f32[128]{0:T(128)} %param.16) | copy-start | bytes 1540
  0.0 48.3 %collective-permute-start.11 = (bf16[2048,1536]{1,0:T(8,128)(2,1)}, bf16[2048,1536]{1,0:T(8,128)(2,1)}, u32[]{:S(2)}, u32[]{:S(2)}) collective-permute-start(bf16[2048,1536]{1,0:T(8,128)(2,1)} %bitcast.25), channel_id=1, source_target_pairs={{0,1},{1,0},{2,3},{3,2},{4,5},{5,4},{6,7},{7,6},{8,9},{9,8},{10,11... | collective-permute-start | bytes 18874376 | tf_op jit(solution)/shard_map/ppermute | solution.py:25
  2.9 8.7 %collective-permute-start = (bf16[64,640]{1,0:T(8,128)(2,1)S(1)}, bf16[64,640]{1,0:T(8,128)(2,1)S(1)}, u32[]{:S(2)}, u32[]{:S(2)}) collective-permute-start(bf16[64,640]{1,0:T(8,128)(2,1)S(1)} %get-tuple-element.59), channel_id=1, source_target_pairs={{0,8},{4,12},{8,0},{12,4},{1,9},{5,13},{9,1},{13,5},{2,10},{6,14},... | collective-permute-start | bytes 245768 | tf_op jit(solution)/shard_map/ppermute | solution.py:25
  6.6 5.2 %collective-permute-start.1 = (bf16[64,640]{1,0:T(8,128)(2,1)S(1)}, bf16[64,640]{1,0:T(8,128)(2,1)S(1)}, u32[]{:S(2)}, u32[]{:S(2)}) collective-permute-start(bf16[64,640]{1,0:T(8,128)(2,1)S(1)} %get-tuple-element.59), channel_id=1, source_target_pairs={{0,4},{4,0},{8,12},{12,8},{1,5},{5,1},{9,13},{13,9},{2,6},{6,2},{1... | collective-permute-start | bytes 245768 | tf_op jit(solution)/shard_map/ppermute | solution.py:25
  8.1 6.3 %collective-permute-start.2 = (bf16[64,640]{1,0:T(8,128)(2,1)S(1)}, bf16[64,640]{1,0:T(8,128)(2,1)S(1)}, u32[]{:S(2)}, u32[]{:S(2)}) collective-permute-start(bf16[64,640]{1,0:T(8,128)(2,1)S(1)} %get-tuple-element.59), channel_id=1, source_target_pairs={{0,12},{4,8},{8,4},{12,0},{1,13},{5,9},{9,5},{13,1},{2,14},{6,10},... | collective-permute-start | bytes 245768 | tf_op jit(solution)/shard_map/ppermute | solution.py:25
  8.1 8.1 %collective-permute-start.3 = (bf16[64,2048]{1,0:T(8,128)(2,1)S(1)}, bf16[64,2048]{1,0:T(8,128)(2,1)S(1)}, u32[]{:S(2)}, u32[]{:S(2)}) collective-permute-start(bf16[64,2048]{1,0:T(8,128)(2,1)S(1)} %get-tuple-element.58.first_ref), channel_id=1, source_target_pairs={{0,2},{1,3},{2,0},{3,1},{4,6},{5,7},{6,4},{7,5},{8,10},{9,11},{10,... | collective-permute-start | bytes 786440 | tf_op jit(solution)/shard_map/ppermute | solution.py:25
  9.9 13.8 %copy-start.3 = (bf16[2048,512]{1,0:T(8,128)(2,1)S(1)}, bf16[2048,512]{1,0:T(8,128)(2,1)}, u32[]{:S(2)}) copy-start(bf16[2048,512]{1,0:T(8,128)(2,1)} %weight_ref.1) | copy-start | bytes 6291460
  11.6 4.7 %collective-permute-start.4 = (bf16[64,2048]{1,0:T(8,128)(2,1)S(1)}, bf16[64,2048]{1,0:T(8,128)(2,1)S(1)}, u32[]{:S(2)}, u32[]{:S(2)}) collective-permute-start(bf16[64,2048]{1,0:T(8,128)(2,1)S(1)} %get-tuple-element.58.first_ref), channel_id=1, source_target_pairs={{0,1},{1,0},{2,3},{3,2},{4,5},{5,4},{6,7},{7,6},{8,9},{9,8},{10,11... | collective-permute-start | bytes 786440 | tf_op jit(solution)/shard_map/ppermute | solution.py:25
  16.3 7.4 %copy-start.20 = (bf16[64,2048]{1,0:T(8,128)(2,1)}, bf16[64,2048]{1,0:T(8,128)(2,1)S(1)}, u32[]{:S(2)}) copy-start(bf16[64,2048]{1,0:T(8,128)(2,1)S(1)} %collective-permute-done.3.second_ref) | copy-start | bytes 786436
  16.3 5.9 %collective-permute-start.6 = (bf16[256,384]{1,0:T(8,128)(2,1)S(1)}, bf16[256,384]{1,0:T(8,128)(2,1)S(1)}, u32[]{:S(2)}, u32[]{:S(2)}) collective-permute-start(bf16[256,384]{1,0:T(8,128)(2,1)S(1)} %pad_maximum_fusion.4), channel_id=1, source_target_pairs={{0,2},{1,3},{2,0},{3,1},{4,6},{5,7},{6,4},{7,5},{8,10},{9,11},{10,... | collective-permute-start | bytes 589832 | tf_op jit(solution)/shard_map/ppermute | solution.py:25
  17.8 5.9 %collective-permute-start.5 = (bf16[64,2048]{1,0:T(8,128)(2,1)S(1)}, bf16[64,2048]{1,0:T(8,128)(2,1)S(1)}, u32[]{:S(2)}, u32[]{:S(2)}) collective-permute-start(bf16[64,2048]{1,0:T(8,128)(2,1)S(1)} %collective-permute-done.3.second_ref), channel_id=1, source_target_pairs={{0,1},{1,0},{2,3},{3,2},{4,5},{5,4},{6,7},{7,6},{8,9},{9,8},{10,11... | collective-permute-start | bytes 786440 | tf_op jit(solution)/shard_map/ppermute | solution.py:25
  22.2 6.1 %collective-permute-start.7 = (bf16[512,256]{1,0:T(8,128)(2,1)S(1)}, bf16[512,256]{1,0:T(8,128)(2,1)S(1)}, u32[]{:S(2)}, u32[]{:S(2)}) collective-permute-start(bf16[512,256]{1,0:T(8,128)(2,1)S(1)} %pad_maximum_fusion.2.refs_1_), channel_id=1, source_target_pairs={{0,1},{1,0},{2,3},{3,2},{4,5},{5,4},{6,7},{7,6},{8,9},{9,8},{10,11... | collective-permute-start | bytes 786440 | tf_op jit(solution)/shard_map/ppermute | solution.py:25
  22.3 5.9 %collective-permute-start.8 = (bf16[2,256,128]{2,1,0:T(8,128)(2,1)S(1)}, bf16[2,256,128]{2,1,0:T(8,128)(2,1)S(1)}, u32[]{:S(2)}, u32[]{:S(2)}) collective-permute-start(bf16[2,256,128]{2,1,0:T(8,128)(2,1)S(1)} %pad_maximum_fusion.5), channel_id=1, source_target_pairs={{0,16},{16,0},{1,17},{17,1},{2,18},{18,2},{3,19},{19,3},{4,20},{20... | collective-permute-start | bytes 393224 | tf_op jit(solution)/shard_map/ppermute | solution.py:25
  23.7 1.0 copy-start.21
  24.7 10.7 %copy-start.2 = (bf16[1,768,2048]{2,1,0:T(8,128)(2,1)S(1)}, bf16[1,768,2048]{2,1,0:T(8,128)(2,1)}, u32[]{:S(2)}) copy-start(bf16[1,768,2048]{2,1,0:T(8,128)(2,1)} %param.23) | copy-start | bytes 9437188
  28.3 1.6 copy-start.31
  32.7 2.7 %collective-permute-start.9 = (f32[128,2048]{1,0:T(8,128)S(1)}, f32[128,2048]{1,0:T(8,128)S(1)}, u32[]{:S(2)}, u32[]{:S(2)}) collective-permute-start(f32[128,2048]{1,0:T(8,128)S(1)} %get-tuple-element.66), channel_id=1, source_target_pairs={{0,1},{1,0},{2,3},{3,2},{4,5},{5,4},{6,7},{7,6},{8,9},{9,8},{10,11... | collective-permute-start | bytes 3145736 | tf_op jit(solution)/shard_map/ppermute | solution.py:25
  35.4 12.9 %collective-permute-start.12 = (bf16[768,2048]{1,0:T(8,128)(2,1)S(1)}, bf16[768,2048]{1,0:T(8,128)(2,1)}, u32[]{:S(2)}, u32[]{:S(2)}) collective-permute-start(bf16[768,2048]{1,0:T(8,128)(2,1)S(1)} %bitcast.29), channel_id=1, source_target_pairs={{0,1},{1,0},{2,3},{3,2},{4,5},{5,4},{6,7},{7,6},{8,9},{9,8},{10,11... | collective-permute-start | bytes 9437192 | tf_op jit(solution)/shard_map/ppermute | solution.py:25
  35.7 1.0 copy-start.33
  36.6 15.3 %copy-start.39 = (f32[2048]{0:T(1024)S(1)}, f32[2048]{0:T(1024)}, u32[]{:S(2)}) copy-start(f32[2048]{0:T(1024)} %param.19) | copy-start | bytes 24580
  37.4 8.9 %collective-permute-start.10 = (bf16[64,2048]{1,0:T(8,128)(2,1)}, bf16[64,2048]{1,0:T(8,128)(2,1)}, u32[]{:S(2)}, u32[]{:S(2)}) collective-permute-start(bf16[64,2048]{1,0:T(8,128)(2,1)} %slice.224), channel_id=1, source_target_pairs={{0,2},{1,3},{2,0},{3,1},{4,6},{5,7},{6,4},{7,5},{8,10},{9,11},{10,... | collective-permute-start | bytes 786440 | tf_op jit(solution)/shard_map/ppermute | solution.py:25
  50.3 10.6 %copy-start.36 = (pred[4,112,256]{2,1,0:T(8,128)(4,1)}, pred[4,112,256]{2,1,0:T(8,128)(4,1)S(1)}, u32[]{:S(2)}) copy-start(pred[4,112,256]{2,1,0:T(8,128)(4,1)S(1)} %get-tuple-element.130) | copy-start | bytes 344068
  50.3 10.6 %copy-start.37 = (pred[4,112,256]{2,1,0:T(8,128)(4,1)}, pred[4,112,256]{2,1,0:T(8,128)(4,1)S(1)}, u32[]{:S(2)}) copy-start(pred[4,112,256]{2,1,0:T(8,128)(4,1)S(1)} %get-tuple-element.131) | copy-start | bytes 344068
  50.7 10.4 %copy-start.34 = (pred[1,4,256,112]{3,2,1,0:T(8,128)(4,1)}, pred[1,4,256,112]{3,2,1,0:T(8,128)(4,1)S(1)}, u32[]{:S(2)}) copy-start(pred[1,4,256,112]{3,2,1,0:T(8,128)(4,1)S(1)} %get-tuple-element.132) | copy-start | bytes 344068
  50.7 11.1 %copy-start.35 = (pred[1,4,256,112]{3,2,1,0:T(8,128)(4,1)}, pred[1,4,256,112]{3,2,1,0:T(8,128)(4,1)S(1)}, u32[]{:S(2)}) copy-start(pred[1,4,256,112]{3,2,1,0:T(8,128)(4,1)S(1)} %get-tuple-element.133) | copy-start | bytes 344068
  53.8 19.3 %collective-permute-start.18 = (bf16[64,2048]{1,0:T(8,128)(2,1)}, bf16[64,2048]{1,0:T(8,128)(2,1)}, u32[]{:S(2)}, u32[]{:S(2)}) collective-permute-start(bf16[64,2048]{1,0:T(8,128)(2,1)} %multiply_convert_fusion.refs_7_), channel_id=1, source_target_pairs={{0,2},{1,3},{2,0},{3,1},{4,6},{5,7},{6,4},{7,5},{8,10},{9,11},{10,... | collective-permute-start | bytes 786440 | tf_op jit(solution)/shard_map/ppermute | solution.py:25
  55.1 16.1 %collective-permute-start.17 = (bf16[64,2048]{1,0:T(8,128)(2,1)}, bf16[64,2048]{1,0:T(8,128)(2,1)}, u32[]{:S(2)}, u32[]{:S(2)}) collective-permute-start(bf16[64,2048]{1,0:T(8,128)(2,1)} %multiply_convert_fusion.refs_7_), channel_id=1, source_target_pairs={{0,4},{4,0},{8,12},{12,8},{1,5},{5,1},{9,13},{13,9},{2,6},{6,2},{1... | collective-permute-start | bytes 786440 | tf_op jit(solution)/shard_map/ppermute | solution.py:25
  55.9 11.0 %collective-permute-start.13 = (bf16[64,2048]{1,0:T(8,128)(2,1)}, bf16[64,2048]{1,0:T(8,128)(2,1)}, u32[]{:S(2)}, u32[]{:S(2)}) collective-permute-start(bf16[64,2048]{1,0:T(8,128)(2,1)} %multiply_convert_fusion.refs_7_), channel_id=1, source_target_pairs={{0,8},{4,12},{8,0},{12,4},{1,9},{5,13},{9,1},{13,5},{2,10},{6,14},... | collective-permute-start | bytes 786440 | tf_op jit(solution)/shard_map/ppermute | solution.py:25
  59.2 15.5 %collective-permute-start.19 = (bf16[64,2048]{1,0:T(8,128)(2,1)}, bf16[64,2048]{1,0:T(8,128)(2,1)}, u32[]{:S(2)}, u32[]{:S(2)}) collective-permute-start(bf16[64,2048]{1,0:T(8,128)(2,1)} %multiply_convert_fusion.refs_7_), channel_id=1, source_target_pairs={{0,16},{16,0},{1,17},{17,1},{2,18},{18,2},{3,19},{19,3},{4,20},{20... | collective-permute-start | bytes 786440 | tf_op jit(solution)/shard_map/ppermute | solution.py:25
  66.9 13.1 %collective-permute-start.14 = (bf16[64,2048]{1,0:T(8,128)(2,1)}, bf16[64,2048]{1,0:T(8,128)(2,1)}, u32[]{:S(2)}, u32[]{:S(2)}) collective-permute-start(bf16[64,2048]{1,0:T(8,128)(2,1)} %collective-permute-done.13), channel_id=1, source_target_pairs={{0,4},{4,0},{8,12},{12,8},{1,5},{5,1},{9,13},{13,9},{2,6},{6,2},{1... | collective-permute-start | bytes 786440 | tf_op jit(solution)/shard_map/ppermute | solution.py:25
  76.3 19.2 %collective-permute-start.20 = (bf16[128,2048]{1,0:T(8,128)(2,1)}, bf16[128,2048]{1,0:T(8,128)(2,1)}, u32[]{:S(2)}, u32[]{:S(2)}) collective-permute-start(bf16[128,2048]{1,0:T(8,128)(2,1)} %pad_maximum_fusion.refs_8_), channel_id=1, source_target_pairs={{0,2},{1,3},{2,0},{3,1},{4,6},{5,7},{6,4},{7,5},{8,10},{9,11},{10,... | collective-permute-start | bytes 1572872 | tf_op jit(solution)/shard_map/ppermute | solution.py:25
  76.8 20.5 %collective-permute-start.21 = (bf16[128,2048]{1,0:T(8,128)(2,1)}, bf16[128,2048]{1,0:T(8,128)(2,1)}, u32[]{:S(2)}, u32[]{:S(2)}) collective-permute-start(bf16[128,2048]{1,0:T(8,128)(2,1)} %pad_maximum_fusion.refs_8_), channel_id=1, source_target_pairs={{0,16},{16,0},{1,17},{17,1},{2,18},{18,2},{3,19},{19,3},{4,20},{20... | collective-permute-start | bytes 1572872 | tf_op jit(solution)/shard_map/ppermute | solution.py:25
  80.0 18.9 %collective-permute-start.15 = (bf16[64,2048]{1,0:T(8,128)(2,1)}, bf16[64,2048]{1,0:T(8,128)(2,1)S(1)}, u32[]{:S(2)}, u32[]{:S(2)}) collective-permute-start(bf16[64,2048]{1,0:T(8,128)(2,1)} %collective-permute-done.14.refs_9_), channel_id=1, source_target_pairs={{0,2},{1,3},{2,0},{3,1},{4,6},{5,7},{6,4},{7,5},{8,10},{9,11},{10,... | collective-permute-start | bytes 786440 | tf_op jit(solution)/shard_map/ppermute | solution.py:25
  81.5 18.9 %collective-permute-start.16 = (bf16[64,2048]{1,0:T(8,128)(2,1)}, bf16[64,2048]{1,0:T(8,128)(2,1)S(1)}, u32[]{:S(2)}, u32[]{:S(2)}) collective-permute-start(bf16[64,2048]{1,0:T(8,128)(2,1)} %collective-permute-done.14.refs_9_), channel_id=1, source_target_pairs={{0,16},{16,0},{1,17},{17,1},{2,18},{18,2},{3,19},{19,3},{4,20},{20... | collective-permute-start | bytes 786440 | tf_op jit(solution)/shard_map/ppermute | solution.py:25
  83.5 18.5 %collective-permute-start.22 = (bf16[64,1024]{1,0:T(8,128)(2,1)}, bf16[64,1024]{1,0:T(8,128)(2,1)S(1)}, u32[]{:S(2)}, u32[]{:S(2)}) collective-permute-start(bf16[64,1024]{1,0:T(8,128)(2,1)} %slice.162), channel_id=1, source_target_pairs={{0,16},{16,0},{1,17},{17,1},{2,18},{18,2},{3,19},{19,3},{4,20},{20... | collective-permute-start | bytes 393224 | tf_op jit(solution)/shard_map/ppermute | solution.py:25
  85.0 2.8 %copy-start = (bf16[1,2048,1536]{2,1,0:T(8,128)(2,1)S(1)}, bf16[1,2048,1536]{2,1,0:T(8,128)(2,1)}, u32[]{:S(2)}) copy-start(bf16[1,2048,1536]{2,1,0:T(8,128)(2,1)} %param.22) | copy-start | bytes 18874372
  87.8 7.7 %copy-start.38 = (bf16[64,1024]{1,0:T(8,128)(2,1)S(1)}, bf16[64,1024]{1,0:T(8,128)(2,1)}, u32[]{:S(2)}) copy-start(bf16[64,1024]{1,0:T(8,128)(2,1)} %slice.163) | copy-start | bytes 393220
  87.8 15.5 %copy-start.4 = (f32[2,256,2]{2,1,0:T(8,128)S(1)}, f32[2,256,2]{2,1,0:T(8,128)}, u32[]{:S(2)}) copy-start(f32[2,256,2]{2,1,0:T(8,128)} %copy.21.refs_2_) | copy-start | bytes 12292
  87.8 15.5 %copy-start.5 = (bf16[2,224,256]{2,1,0:T(8,128)(2,1)S(1)}, bf16[2,224,256]{2,1,0:T(8,128)(2,1)}, u32[]{:S(2)}) copy-start(bf16[2,224,256]{2,1,0:T(8,128)(2,1)} %slice.164.refs_0_) | copy-start | bytes 688132
  95.5 6.5 %copy-start.11 = (bf16[256,1024]{1,0:T(8,128)(2,1)}, bf16[256,1024]{1,0:T(8,128)(2,1)S(1)}, u32[]{:S(2)}) copy-start(bf16[256,1024]{1,0:T(8,128)(2,1)S(1)} %get-tuple-element.77) | copy-start | bytes 1572868
  95.5 18.6 %copy-start.13 = (bf16[256,1024]{1,0:T(8,128)(2,1)}, bf16[256,1024]{1,0:T(8,128)(2,1)S(1)}, u32[]{:S(2)}) copy-start(bf16[256,1024]{1,0:T(8,128)(2,1)S(1)} %get-tuple-element.106) | copy-start | bytes 1572868
  95.5 20.2 %collective-permute-start.23 = (bf16[64,1024]{1,0:T(8,128)(2,1)S(1)}, bf16[64,1024]{1,0:T(8,128)(2,1)S(1)}, u32[]{:S(2)}, u32[]{:S(2)}) collective-permute-start(bf16[64,1024]{1,0:T(8,128)(2,1)S(1)} %copy-done.38), channel_id=1, source_target_pairs={{0,2},{1,3},{2,0},{3,1},{4,6},{5,7},{6,4},{7,5},{8,10},{9,11},{10,... | collective-permute-start | bytes 393224 | tf_op jit(solution)/shard_map/ppermute | solution.py:25
  97.3 20.4 %collective-permute-start.24 = (bf16[128,1024]{1,0:T(8,128)(2,1)S(1)}, bf16[128,1024]{1,0:T(8,128)(2,1)S(1)}, u32[]{:S(2)}, u32[]{:S(2)}) collective-permute-start(bf16[128,1024]{1,0:T(8,128)(2,1)S(1)} %slice.168), channel_id=1, source_target_pairs={{0,16},{16,0},{1,17},{17,1},{2,18},{18,2},{3,19},{19,3},{4,20},{20... | collective-permute-start | bytes 786440 | tf_op jit(solution)/shard_map/ppermute | solution.py:25
  98.8 19.5 %collective-permute-start.25 = (bf16[128,1024]{1,0:T(8,128)(2,1)S(1)}, bf16[128,1024]{1,0:T(8,128)(2,1)S(1)}, u32[]{:S(2)}, u32[]{:S(2)}) collective-permute-start(bf16[128,1024]{1,0:T(8,128)(2,1)S(1)} %slice.169), channel_id=1, source_target_pairs={{0,2},{1,3},{2,0},{3,1},{4,6},{5,7},{6,4},{7,5},{8,10},{9,11},{10,... | collective-permute-start | bytes 786440 | tf_op jit(solution)/shard_map/ppermute | solution.py:25
  100.4 15.9 %collective-permute-start.26 = (bf16[64,1024]{1,0:T(8,128)(2,1)S(1)}, bf16[64,1024]{1,0:T(8,128)(2,1)S(1)}, u32[]{:S(2)}, u32[]{:S(2)}) collective-permute-start(bf16[64,1024]{1,0:T(8,128)(2,1)S(1)} %slice.136), channel_id=1, source_target_pairs={{0,16},{16,0},{1,17},{17,1},{2,18},{18,2},{3,19},{19,3},{4,20},{20... | collective-permute-start | bytes 393224 | tf_op jit(solution)/shard_map/ppermute | solution.py:25
  102.0 19.3 %copy-start.6 = (bf16[2,1,256,112]{3,2,1,0:T(8,128)(2,1)S(1)}, bf16[2,1,256,112]{3,2,1,0:T(8,128)(2,1)}, u32[]{:S(2)}) copy-start(bf16[2,1,256,112]{3,2,1,0:T(8,128)(2,1)} %get-tuple-element.122.refs_1_) | copy-start | bytes 344068
  102.7 14.4 %collective-permute-start.27 = (bf16[64,1024]{1,0:T(8,128)(2,1)S(1)}, bf16[64,1024]{1,0:T(8,128)(2,1)S(1)}, u32[]{:S(2)}, u32[]{:S(2)}) collective-permute-start(bf16[64,1024]{1,0:T(8,128)(2,1)S(1)} %slice.137), channel_id=1, source_target_pairs={{0,2},{1,3},{2,0},{3,1},{4,6},{5,7},{6,4},{7,5},{8,10},{9,11},{10,... | collective-permute-start | bytes 393224 | tf_op jit(solution)/shard_map/ppermute | solution.py:25
  119.1 18.9 %collective-permute-start.28 = (bf16[256,1024]{1,0:T(8,128)(2,1)}, bf16[256,1024]{1,0:T(8,128)(2,1)}, u32[]{:S(2)}, u32[]{:S(2)}) collective-permute-start(bf16[256,1024]{1,0:T(8,128)(2,1)} %get-tuple-element.86), channel_id=1, source_target_pairs={{0,16},{16,0},{1,17},{17,1},{2,18},{18,2},{3,19},{19,3},{4,20},{20... | collective-permute-start | bytes 1572872 | tf_op jit(solution)/shard_map/ppermute | solution.py:25
  119.6 18.4 %collective-permute-start.29 = (bf16[256,1024]{1,0:T(8,128)(2,1)}, bf16[256,1024]{1,0:T(8,128)(2,1)}, u32[]{:S(2)}, u32[]{:S(2)}) collective-permute-start(bf16[256,1024]{1,0:T(8,128)(2,1)} %get-tuple-element.87), channel_id=1, source_target_pairs={{0,2},{1,3},{2,0},{3,1},{4,6},{5,7},{6,4},{7,5},{8,10},{9,11},{10,... | collective-permute-start | bytes 1572872 | tf_op jit(solution)/shard_map/ppermute | solution.py:25
  121.3 2.8 %copy-start.1 = (bf16[1,2048,1536]{2,1,0:T(8,128)(2,1)S(1)}, bf16[1,2048,1536]{2,1,0:T(8,128)(2,1)}, u32[]{:S(2)}) copy-start(bf16[1,2048,1536]{2,1,0:T(8,128)(2,1)} %param.22) | copy-start | bytes 18874372
  125.0 0.9 copy-start.17
  130.5 21.1 %copy-start.10 = (bf16[256,1024]{1,0:T(8,128)(2,1)S(1)}, bf16[256,1024]{1,0:T(8,128)(2,1)}, u32[]{:S(2)}) copy-start(bf16[256,1024]{1,0:T(8,128)(2,1)} %copy-done.9) | copy-start | bytes 1572868
  130.5 21.9 %copy-start.8 = (bf16[256,1024]{1,0:T(8,128)(2,1)S(1)}, bf16[256,1024]{1,0:T(8,128)(2,1)}, u32[]{:S(2)}) copy-start(bf16[256,1024]{1,0:T(8,128)(2,1)} %copy-done.7) | copy-start | bytes 1572868
  138.0 24.0 %copy-start.14 = (bf16[256,1024]{1,0:T(8,128)(2,1)S(1)}, bf16[256,1024]{1,0:T(8,128)(2,1)}, u32[]{:S(2)}) copy-start(bf16[256,1024]{1,0:T(8,128)(2,1)} %copy-done.13) | copy-start | bytes 1572868
  138.0 25.1 %copy-start.12 = (bf16[256,1024]{1,0:T(8,128)(2,1)S(1)}, bf16[256,1024]{1,0:T(8,128)(2,1)}, u32[]{:S(2)}) copy-start(bf16[256,1024]{1,0:T(8,128)(2,1)} %copy-done.11) | copy-start | bytes 1572868
  138.1 10.9 %collective-permute-start.30 = (bf16[256,1024]{1,0:T(8,128)(2,1)S(1)}, bf16[256,1024]{1,0:T(8,128)(2,1)S(1)}, u32[]{:S(2)}, u32[]{:S(2)}) collective-permute-start(bf16[256,1024]{1,0:T(8,128)(2,1)S(1)} %get-tuple-element.98), channel_id=1, source_target_pairs={{0,16},{16,0},{1,17},{17,1},{2,18},{18,2},{3,19},{19,3},{4,20},{20... | collective-permute-start | bytes 1572872 | tf_op jit(solution)/shard_map/ppermute | solution.py:25
  139.6 12.0 %collective-permute-start.31 = (bf16[256,1024]{1,0:T(8,128)(2,1)S(1)}, bf16[256,1024]{1,0:T(8,128)(2,1)S(1)}, u32[]{:S(2)}, u32[]{:S(2)}) collective-permute-start(bf16[256,1024]{1,0:T(8,128)(2,1)S(1)} %get-tuple-element.99), channel_id=1, source_target_pairs={{0,2},{1,3},{2,0},{3,1},{4,6},{5,7},{6,4},{7,5},{8,10},{9,11},{10,... | collective-permute-start | bytes 1572872 | tf_op jit(solution)/shard_map/ppermute | solution.py:25
  151.8 7.5 %collective-permute-start.32 = (bf16[128,1024]{1,0:T(8,128)(2,1)S(1)}, bf16[128,1024]{1,0:T(8,128)(2,1)S(1)}, u32[]{:S(2)}, u32[]{:S(2)}) collective-permute-start(bf16[128,1024]{1,0:T(8,128)(2,1)S(1)} %slice.170), channel_id=1, source_target_pairs={{0,2},{1,3},{2,0},{3,1},{4,6},{5,7},{6,4},{7,5},{8,10},{9,11},{10,... | collective-permute-start | bytes 786440 | tf_op jit(solution)/shard_map/ppermute | solution.py:25
  152.6 7.1 %collective-permute-start.33 = (bf16[128,1024]{1,0:T(8,128)(2,1)S(1)}, bf16[128,1024]{1,0:T(8,128)(2,1)S(1)}, u32[]{:S(2)}, u32[]{:S(2)}) collective-permute-start(bf16[128,1024]{1,0:T(8,128)(2,1)S(1)} %slice.171), channel_id=1, source_target_pairs={{0,16},{16,0},{1,17},{17,1},{2,18},{18,2},{3,19},{19,3},{4,20},{20... | collective-permute-start | bytes 786440 | tf_op jit(solution)/shard_map/ppermute | solution.py:25
  159.7 6.4 %collective-permute-start.34 = (bf16[128,1024]{1,0:T(8,128)(2,1)S(1)}, bf16[128,1024]{1,0:T(8,128)(2,1)S(1)}, u32[]{:S(2)}, u32[]{:S(2)}) collective-permute-start(bf16[128,1024]{1,0:T(8,128)(2,1)S(1)} %slice.144), channel_id=1, source_target_pairs={{0,2},{1,3},{2,0},{3,1},{4,6},{5,7},{6,4},{7,5},{8,10},{9,11},{10,... | collective-permute-start | bytes 786440 | tf_op jit(solution)/shard_map/ppermute | solution.py:25
  161.3 6.4 %collective-permute-start.35 = (bf16[128,1024]{1,0:T(8,128)(2,1)S(1)}, bf16[128,1024]{1,0:T(8,128)(2,1)S(1)}, u32[]{:S(2)}, u32[]{:S(2)}) collective-permute-start(bf16[128,1024]{1,0:T(8,128)(2,1)S(1)} %slice.145), channel_id=1, source_target_pairs={{0,16},{16,0},{1,17},{17,1},{2,18},{18,2},{3,19},{19,3},{4,20},{20... | collective-permute-start | bytes 786440 | tf_op jit(solution)/shard_map/ppermute | solution.py:25
  164.2 21.6 %copy-start.32 = (f32[64,2048]{1,0:T(8,128)S(1)}, f32[64,2048]{1,0:T(8,128)}, u32[]{:S(2)}) copy-start(f32[64,2048]{1,0:T(8,128)} %fusion.5) | copy-start | bytes 1572868
  164.2 12.0 %collective-permute-start.36 = (bf16[128,2048]{1,0:T(8,128)(2,1)S(1)}, bf16[128,2048]{1,0:T(8,128)(2,1)S(1)}, u32[]{:S(2)}, u32[]{:S(2)}) collective-permute-start(bf16[128,2048]{1,0:T(8,128)(2,1)S(1)} %pad_maximum_fusion.1), channel_id=1, source_target_pairs={{0,4},{4,0},{8,12},{12,8},{1,5},{5,1},{9,13},{13,9},{2,6},{6,2},{1... | collective-permute-start | bytes 1572872 | tf_op jit(solution)/shard_map/ppermute | solution.py:25
  176.4 9.5 %collective-permute-start.37 = (bf16[64,2048]{1,0:T(8,128)(2,1)S(1)}, bf16[64,2048]{1,0:T(8,128)(2,1)S(1)}, u32[]{:S(2)}, u32[]{:S(2)}) collective-permute-start(bf16[64,2048]{1,0:T(8,128)(2,1)S(1)} %slice.223), channel_id=1, source_target_pairs={{0,8},{4,12},{8,0},{12,4},{1,9},{5,13},{9,1},{13,5},{2,10},{6,14},... | collective-permute-start | bytes 786440 | tf_op jit(solution)/shard_map/ppermute | solution.py:25
  (14 other events, 11.1 us)

commit v6 on v4

--- a/solution.py
+++ b/solution.py
@@ -41,7 +41,7 @@
     return lax.optimization_barrier(arrays)
 
 
-def spread_rows(own, early_work):
+def spread_rows(own, coded):
     half = own.shape[1] // 2
 
     def both_ways(part):
@@ -54,45 +54,44 @@
     blocks = [own, swap(own, "seq", first_bits)]
     for bits in bits_left[:-1]:
         blocks = blocks + [swap(block, "seq", bits) for block in blocks]
-    beyond = [swap(block, "seq", bits_left[-1]) for block in blocks[:-1]]
+    beyond = [swap(block, "seq", bits_left[-1]) for block in blocks]
     outer = both_ways(own)
-    middle = jnp.concatenate(blocks[1:] + beyond, axis=0)
-    outer_low, outer_high = outer[0][:, :half], outer[1][:, half:]
-    middle, outer_low, outer_high = ready(middle, outer_low, outer_high)
+    outer_low, outer_high, first = ready(outer[0][:, :half], outer[1][:, half:], blocks[1])
+    middle = jnp.concatenate([first] + blocks[2:] + beyond[:-1], axis=0)
     outer_corner = swap(outer_low, "role", 1), swap(outer_high, "rep", ACROSS)
-    last = swap(blocks[-1], "seq", bits_left[-1])
-    rows = own.shape[0] + middle.shape[0] + last.shape[0]
+    last, coded = ready(beyond[-1], coded)
     inner = both_ways(middle)
     final = both_ways(last)
     inner_corner = corners(*inner)
-    early = early_work([(0, 0, own), (own.shape[0], 0, middle), (rows - last.shape[0], 0, last)])
-    by_rep, by_role, *early = ready(*final, *early)
+    by_rep, by_role, *outer_corner = ready(*final, *outer_corner)
     final_corner = corners(by_rep, by_role)
-    groups = [[], [], []]
+    groups = [[], [], [], []]
     start = 0
     for part, beside, corner in (
         (own, outer, outer_corner),
         (middle, inner, inner_corner),
         (last, final, final_corner),
     ):
-        groups[0].append((start, 0, beside[0]))
-        groups[1].append((start, 0, beside[1]))
-        groups[2].append((start, 0, corner[0]))
-        groups[2].append((start, half, corner[1]))
+        groups[0].append((start, 0, part))
+        groups[1].append((start, 0, beside[0]))
+        groups[2].append((start, 0, beside[1]))
+        groups[3].append((start, 0, corner[0]))
+        groups[3].append((start, half, corner[1]))
         start += part.shape[0]
-    return early, groups
+    return groups, coded
 
 
 def added(first, second):
     return (first.astype(jnp.float32) + second.astype(jnp.float32)).astype(jnp.bfloat16)
 
 
-def collect_rows(near, by_rep, by_role, corner):
+def collect_rows(make_near, by_rep, by_role, corner):
     straight_low = swap(by_role[0], "role", 1)
     straight_high = swap(by_rep[1], "rep", ACROSS)
     straight_low, straight_high, *corner = ready(straight_low, straight_high, *corner)
-    corner_low, corner_high = ready(
-        swap(corner[0], "role", 1), swap(corner[1], "rep", ACROSS)
+    near = make_near(corner[0])
+    corner_low, corner_high, *near = ready(
+        swap(corner[0], "role", 1), swap(corner[1], "rep", ACROSS), *near
     )
     cut = near[0].shape[0] // 2
     low_sum, high_sum = added(by_rep[0], corner_low), added(by_role[1], corner_high)
@@ -126,7 +125,19 @@
     return total
 
 
-def prepare_kernel(tokens_ref, gain_ref, kv_ref, k_gain_ref, ids_ref, gates_ref, normed_ref, out_ref):
+def prepare_kernel(*refs):
+    tokens_in, gain_in, kv_in, k_gain_in, ids_in, gates_in, normed_ref, out_ref = refs[:8]
+    held, sem = refs[8:14], refs[14]
+    sources = (tokens_in, gain_in, kv_in, k_gain_in, ids_in, gates_in)
+    copies = [
+        pltpu.make_async_copy(src, dst, sem.at[number])
+        for number, (src, dst) in enumerate(zip(sources, held))
+    ]
+    for copy in copies:
+        copy.start()
+    for copy in copies:
+        copy.wait()
+    tokens_ref, gain_ref, kv_ref, k_gain_ref, ids_ref, gates_ref = held
     normed = rms_rows(tokens_ref[...].astype(jnp.float32), gain_ref[...]).astype(jnp.bfloat16)
     normed_ref[...] = normed
     kv_width, head_dim = kv_ref.shape[2], k_gain_ref.shape[1]
@@ -136,28 +147,41 @@
         out_ref[:, start : start + head_dim] = head.astype(jnp.bfloat16)
     values = jnp.dot(normed, kv_ref[1], preferred_element_type=jnp.float32)
     out_ref[:, kv_width : 2 * kv_width] = values.astype(jnp.bfloat16)
-    ids, gates = ids_ref[...], gates_ref[...]
-    rest = jnp.zeros((ids.shape[0], LANES - 3 * ids.shape[1]), jnp.int32)
-    coded = jnp.concatenate([ids, gates // 64, gates % 64, rest], axis=1)
-    out_ref[:, 2 * kv_width :] = coded.astype(jnp.float32).astype(jnp.bfloat16)
+    coded = jnp.concatenate([ids_ref[...], gates_ref[...] // 64, gates_ref[...] % 64], axis=0)
+    count = coded.shape[0]
+    spread = lax.broadcasted_iota(jnp.int32, (count, LANES), 0)
+    spread = spread == lax.broadcasted_iota(jnp.int32, (count, LANES), 1)
+    out_ref[:, 2 * kv_width :] = lax.dot_general(
+        coded.astype(jnp.float32).astype(jnp.bfloat16),
+        spread.astype(jnp.float32).astype(jnp.bfloat16),
+        (((0,), (0,)), ((), ())),
+        preferred_element_type=jnp.float32,
+    ).astype(jnp.bfloat16)
 
 
 def prepare(tokens, attn_gain, w_keyval, k_gain, ids, gates):
     rows, width = tokens.shape
+    operands = [
+        pltpu.with_memory_space_constraint(one, pltpu.HBM)
+        for one in (tokens, attn_gain[None], w_keyval, k_gain[None], ids.T, gates.T)
+    ]
     return pl.pallas_call(
         prepare_kernel,
         out_shape=[
             jax.ShapeDtypeStruct((rows, width), jnp.bfloat16),
             jax.ShapeDtypeStruct((rows, 2 * w_keyval.shape[2] + LANES), jnp.bfloat16),
         ],
-        compiler_params=pltpu.CompilerParams(vmem_limit_bytes=16 * 1024 * 1024),
+        in_specs=[pl.BlockSpec(memory_space=pltpu.HBM)] * len(operands),
+        scratch_shapes=[pltpu.VMEM(one.shape, one.dtype) for one in operands]
+        + [pltpu.SemaphoreType.DMA((len(operands),))],
+        compiler_params=pltpu.CompilerParams(vmem_limit_bytes=8 * 1024 * 1024),
         cost_estimate=pl.CostEstimate(
             flops=4 * rows * width * w_keyval.shape[2],
             bytes_accessed=4 * width * w_keyval.shape[2] + 4 * rows * width,
             transcendentals=rows,
         ),
         name="prepare",
-    )(tokens, attn_gain[None], w_keyval, k_gain[None], ids, gates)
+    )(*operands)
 
 
 def queries_kernel(first_ref, second_ref, third_ref, fourth_ref, weight_ref, gain_ref, out_ref):
@@ -175,7 +199,7 @@
     return pl.pallas_call(
         queries_kernel,
         out_shape=jax.ShapeDtypeStruct((rows, width), jnp.bfloat16),
-        compiler_params=pltpu.CompilerParams(vmem_limit_bytes=16 * 1024 * 1024),
+        compiler_params=pltpu.CompilerParams(vmem_limit_bytes=8 * 1024 * 1024),
         cost_estimate=pl.CostEstimate(
             flops=2 * rows * width * w_query.shape[0],
             bytes_accessed=2 * width * w_query.shape[0],
@@ -224,7 +248,7 @@
         lambda *refs: attend_kernel(head_dim, *refs),
         out_shape=[half, half],
         scratch_shapes=[pltpu.VMEM((rows, width), jnp.bfloat16)],
-        compiler_params=pltpu.CompilerParams(vmem_limit_bytes=40 * 1024 * 1024),
+        compiler_params=pltpu.CompilerParams(vmem_limit_bytes=12 * 1024 * 1024),
         cost_estimate=pl.CostEstimate(
             flops=4 * rows * width * keys + 2 * rows * width * w_out.shape[1],
             bytes_accessed=2 * width * w_out.shape[1] + 4 * rows * w_out.shape[1],
@@ -420,6 +444,7 @@
     far_gu = swap(w_gateup[0], "rep", PAIR)
     queries = make_queries([normed, across_rows, pair_rows, corner_rows], w_query, q_gain)
     kept, leaving = attend(queries, half_kv, pair_kv, w_out, head_dim)
+    kept, leaving, coded = ready(kept, leaving, coded)
     leaving, own_dn = ready(swap(leaving, "rep", PAIR), w_down[0])
     halves = kept + leaving
     far_dn = swap(own_dn, "rep", PAIR)
@@ -427,6 +452,10 @@
     attended = halves[:row_count] + swap(far_sum, "rep", ACROSS).astype(jnp.float32)
     mixed = tokens + attended
 
+    mixed, far_gu, far_dn, coded = ready(mixed, far_gu, far_dn, coded)
+    moe_in = rms_rows(mixed, moe_gain).astype(jnp.bfloat16)
+
+    rows, coded = spread_rows(moe_in, coded)
     coded = coded[:, :, : 3 * top_count].astype(jnp.int32)
     routes = coded[:, :, :top_count]
     gates = coded[:, :, top_count : 2 * top_count] * 64 + coded[:, :, 2 * top_count :]
@@ -449,10 +478,6 @@
     pick = jnp.concatenate(picks, axis=1)
     place = jnp.stack([jnp.swapaxes(one, 1, 2) for one in picks])
     share = jnp.stack(shares, axis=2)
-    mixed, far_gu, far_dn, pick, place, share = lax.optimization_barrier(
-        (mixed, far_gu, far_dn, pick, place, share)
-    )
-    moe_in = rms_rows(mixed, moe_gain).astype(jnp.bfloat16)
 
     weights = (w_gateup[0], far_gu, w_down[0], far_dn)
 
@@ -461,16 +486,23 @@
             pieces, pick[first:last], place[:, first:last], share[first:last], weights
         )
 
-    near, rows = spread_rows(moe_in, lambda pieces: serve([pieces], 0, 1)[0])
-    by_rep, by_role = serve(rows[:2], 1, 3)
-    rep_low, rep_high, role_low, role_high, *held = ready(
-        *by_rep, *by_role, *(array for _, _, array in rows[2])
-    )
-    by_rep, by_role = (rep_low, rep_high), (role_low, role_high)
-    pieces = [(row, column, array) for (row, column, _), array in zip(rows[2], held)]
-    corner = serve([pieces], 3, 4)
-    routed = collect_rows(near, by_rep, by_role, corner[0])
-    routed = collect_rows(near, by_rep, by_role, corner[0])
+    def with_all(pieces, *others):
+        held = ready(*others, *(array for _, _, array in pieces))
+        pieces = [
+            (row, column, array)
+            for (row, column, _), array in zip(pieces, held[len(others) :])
+        ]
+        return pieces, held[: len(others)]
+
+    by_rep, by_role = serve(rows[1:3], 1, 3)
+    pieces, (*by_rep, role_low, role_high) = with_all(rows[3], *by_rep, *by_role)
+    (corner,) = serve([pieces], 3, 4)
+    routed = collect_rows(
+        lambda after: serve([with_all(rows[0], after)[0]], 0, 1)[0],
+        by_rep,
+        (role_low, role_high),
+        corner,
+    )
     return (mixed + routed).astype(jnp.bfloat16)[None]
 
 

time: 161 us -> 165 us (1.025)
  other arithmetic: 5.36 us -> 9.03 us
  Pallas kernels: 32 us -> 34.1 us
    unnamed x33 -> x41, local copies, waits for them, and re-layouts: 5.51 us -> 2.85 us
    pallas_call x1, Pallas kernels: 0.68 us -> 2.6 us  [prepare(): pl.pallas_call(prepare_kernel, out_shape=[jax.ShapeDtypeStruct((rows, wid...]
    slice x0 -> x2, other arithmetic: none -> 1.67 us  [the longest x1 0.85 us: serve(): place[:, first:last]]
  transfers between devices with their start and end apart: 38 -> 38, of which waited for: 23 -> 20; matrix products, arithmetic and copies ran while one was open for 4% -> 6% of each run, Pallas kernels for 20% -> 21%
where the time goes in v6:
time: 165 us
  waiting for transfers between devices  75.5 us (46%)
  starting transfers between devices  40.3 us (24%)
  Pallas kernels  34.1 us (21%)
  other arithmetic  9.03 us (5%)
  local copies, waits for them, and re-layouts  4.86 us (3%)
    ppermute x38, waiting for transfers between devices, swap(): return lax.ppermute(block, axis, [(i, i ^ bits) for i in range(size)])  75.5 us
    ppermute x38, starting transfers between devices, swap(): return lax.ppermute(block, axis, [(i, i ^ bits) for i in range(size)])  40.3 us
    pallas_call x3, Pallas kernels, run_experts(): pl.pallas_call(lambda *refs: expert_kernel(spots, *refs), out_shape=[jax....  27.8 us
  transfers between devices with their start and end apart: 38, of which 20 were waited for; matrix products, arithmetic and copies ran while one was open for 6% of the time, Pallas kernels for 21%

profile of v6, /device:TPU:0, one launch (start us, length us, event | category | flops | bytes accessed | tf_op | source)
XLA Modules:
  0.0 164.9 jit_solution(11997836988510772340)
XLA Ops:
  0.5 2.6 %prepare.1 = (bf16[64,2048]{1,0:T(8,128)(2,1)S(1)}, bf16[64,640]{1,0:T(8,128)(2,1)S(1)}) custom-call(bf16[64,2048]{1,0:T(8,128)(2,1)} %bitcast.34, f32[1,2048]{1,0:T(1,128)} %bitcast.35, bf16[2,2048,256]{2,1,0:T(8,128)(2,1)} %refs_2_.1, f32[1,128]{1,0:T(1,128)} %bitcast.38, s32[8,64]{1,0:T(8,128)} %bitcast.36, s32[8,64]{1,0:T(8,128)} %bitcast.37), custom_call_target="tpu_custom_call" | custom-call | flops 134217728 | bytes 2621440 | tf_op jit(solution)/shard_map/prepare/pallas_call | solution.py:168
  3.1 3.6 %collective-permute-start = (bf16[64,640]{1,0:T(8,128)(2,1)S(1)}, bf16[64,640]{1,0:T(8,128)(2,1)S(1)}, u32[]{:S(2)}, u32[]{:S(2)}) collective-permute-start(bf16[64,640]{1,0:T(8,128)(2,1)S(1)} %get-tuple-element.66), channel_id=1, source_target_pairs={{0,8},{4,12},{8,0},{12,4},{1,9},{5,13},{9,1},{13,5},{2,10},{6,14},... | collective-permute-start | bytes 245768 | tf_op jit(solution)/shard_map/ppermute | solution.py:25
  6.7 1.6 collective-permute-start.1
  8.3 1.7 %collective-permute-start.3 = (bf16[64,2048]{1,0:T(8,128)(2,1)S(1)}, bf16[64,2048]{1,0:T(8,128)(2,1)S(1)}, u32[]{:S(2)}, u32[]{:S(2)}) collective-permute-start(bf16[64,2048]{1,0:T(8,128)(2,1)S(1)} %get-tuple-element.65.first_ref), channel_id=1, source_target_pairs={{0,2},{1,3},{2,0},{3,1},{4,6},{5,7},{6,4},{7,5},{8,10},{9,11},{10,... | collective-permute-start | bytes 786440 | tf_op jit(solution)/shard_map/ppermute | solution.py:25
  10.0 1.7 %collective-permute-done = bf16[64,640]{1,0:T(8,128)(2,1)S(1)} collective-permute-done((bf16[64,640]{1,0:T(8,128)(2,1)S(1)}, bf16[64,640]{1,0:T(8,128)(2,1)S(1)}, u32[]{:S(2)}, u32[]{:S(2)}) %collective-permute-start) | collective-permute-done | bytes 81952 | tf_op jit(solution)/shard_map/ppermute | solution.py:25
  11.8 2.8 %collective-permute-done.2 = bf16[64,640]{1,0:T(8,128)(2,1)S(1)} collective-permute-done((bf16[64,640]{1,0:T(8,128)(2,1)S(1)}, bf16[64,640]{1,0:T(8,128)(2,1)S(1)}, u32[]{:S(2)}, u32[]{:S(2)}) %collective-permute-start.2) | collective-permute-done | bytes 81952 | tf_op jit(solution)/shard_map/ppermute | solution.py:25
  14.7 1.6 collective-permute-done.3.second_ref
  16.3 1.5 collective-permute-start.6
  17.8 4.2 %collective-permute-done.6 = bf16[256,384]{1,0:T(8,128)(2,1)S(1)} collective-permute-done((bf16[256,384]{1,0:T(8,128)(2,1)S(1)}, bf16[256,384]{1,0:T(8,128)(2,1)S(1)}, u32[]{:S(2)}, u32[]{:S(2)}) %collective-permute-start.6) | collective-permute-done | bytes 196640 | tf_op jit(solution)/shard_map/ppermute | solution.py:25
  22.2 1.5 collective-permute-start.8
  23.7 0.9 queries.1.refs_0_
  24.6 3.5 %collective-permute-done.8 = bf16[2,256,128]{2,1,0:T(8,128)(2,1)S(1)} collective-permute-done((bf16[2,256,128]{2,1,0:T(8,128)(2,1)S(1)}, bf16[2,256,128]{2,1,0:T(8,128)(2,1)S(1)}, u32[]{:S(2)}, u32[]{:S(2)}) %collective-permute-start.8) | collective-permute-done | bytes 131104 | tf_op jit(solution)/shard_map/ppermute | solution.py:25
  28.2 2.8 %attend.1 = (f32[128,2048]{1,0:T(8,128)S(1)}, f32[128,2048]{1,0:T(8,128)S(1)}) custom-call(bf16[256,512]{1,0:T(8,128)(2,1)S(1)} %queries.1.refs_0_, bf16[512,256]{1,0:T(8,128)(2,1)S(1)} %pad_maximum_fusion.1.refs_1_, bf16[512,256]{1,0:T(8,128)(2,1)S(1)} %collective-permute-done.7.refs_2_, bf16[512,2048]{1,0:T(8,128)(2,1)S(1)} %copy-done.2), custom_call_target="tpu_custom_call" | custom-call | flops 1073741824 | bytes 4194304 | tf_op jit(solution)/shard_map/attend/pallas_call | solution.py:247
  31.1 2.6 %collective-permute-done.9 = f32[128,2048]{1,0:T(8,128)S(1)} collective-permute-done((f32[128,2048]{1,0:T(8,128)S(1)}, f32[128,2048]{1,0:T(8,128)S(1)}, u32[]{:S(2)}, u32[]{:S(2)}) %collective-permute-start.9) | collective-permute-done | bytes 1048608 | tf_op jit(solution)/shard_map/ppermute | solution.py:25
  34.0 1.5 collective-permute-start.10
  35.6 7.1 %collective-permute-done.10 = bf16[64,2048]{1,0:T(8,128)(2,1)S(1)} collective-permute-done((bf16[64,2048]{1,0:T(8,128)(2,1)S(1)}, bf16[64,2048]{1,0:T(8,128)(2,1)S(1)}, u32[]{:S(2)}, u32[]{:S(2)}) %collective-permute-start.10) | collective-permute-done | bytes 262176 | tf_op jit(solution)/shard_map/ppermute | solution.py:25
  43.1 1.5 collective-permute-start.15
  44.6 1.5 collective-permute-start.16
  46.1 2.7 %collective-permute-start.13 = (bf16[64,2048]{1,0:T(8,128)(2,1)S(1)}, bf16[64,2048]{1,0:T(8,128)(2,1)S(1)}, u32[]{:S(2)}, u32[]{:S(2)}) collective-permute-start(bf16[64,2048]{1,0:T(8,128)(2,1)S(1)} %multiply_convert_fusion.refs_7_), channel_id=1, source_target_pairs={{0,8},{4,12},{8,0},{12,4},{1,9},{5,13},{9,1},{13,5},{2,10},{6,14},... | collective-permute-start | bytes 786440 | tf_op jit(solution)/shard_map/ppermute | solution.py:25
  48.8 1.4 collective-permute-start.17
  50.2 0.7 collective-permute-done.15.refs_7_
  50.9 1.2 collective-permute-done.16.refs_10_
  52.1 7.9 %collective-permute-done.13 = bf16[64,2048]{1,0:T(8,128)(2,1)S(1)} collective-permute-done((bf16[64,2048]{1,0:T(8,128)(2,1)S(1)}, bf16[64,2048]{1,0:T(8,128)(2,1)S(1)}, u32[]{:S(2)}, u32[]{:S(2)}) %collective-permute-start.13) | collective-permute-done | bytes 262176 | tf_op jit(solution)/shard_map/ppermute | solution.py:25
  60.6 0.7 constant_dynamic-update-slice_fusion.5
  61.3 0.7 constant_dynamic-update-slice_fusion.4.refs_8_
  62.5 1.4 collective-permute-start.20
  63.9 0.6 collective-permute-start.22
  64.5 2.7 %collective-permute-done.14.refs_9_ = bf16[64,2048]{1,0:T(8,128)(2,1)S(1)} collective-permute-done((bf16[64,2048]{1,0:T(8,128)(2,1)S(1)}, bf16[64,2048]{1,0:T(8,128)(2,1)S(1)}, u32[]{:S(2)}, u32[]{:S(2)}) %collective-permute-start.14) | collective-permute-done | bytes 262176 | tf_op jit(solution)/shard_map/ppermute | solution.py:25
  67.3 0.8 select_reduce_fusion
  69.6 0.6 collective-permute-start.19
  70.2 1.4 collective-permute-start.21
  71.8 8.6 %collective-permute-done.22.refs_7_ = bf16[64,1024]{1,0:T(8,128)(2,1)S(1)} collective-permute-done((bf16[64,1024]{1,0:T(8,128)(2,1)S(1)}, bf16[64,1024]{1,0:T(8,128)(2,1)S(1)}, u32[]{:S(2)}, u32[]{:S(2)}) %collective-permute-start.22) | collective-permute-done | bytes 131104 | tf_op jit(solution)/shard_map/ppermute | solution.py:25
  80.4 1.5 collective-permute-start.23
  82.2 3.1 %collective-permute-done.23.refs_8_ = bf16[64,1024]{1,0:T(8,128)(2,1)S(1)} collective-permute-done((bf16[64,1024]{1,0:T(8,128)(2,1)S(1)}, bf16[64,1024]{1,0:T(8,128)(2,1)S(1)}, u32[]{:S(2)}, u32[]{:S(2)}) %collective-permute-start.23) | collective-permute-done | bytes 131104 | tf_op jit(solution)/shard_map/ppermute | solution.py:25
  85.4 0.8 copy-done.7
  86.2 1.5 collective-permute-start.24
  87.7 1.0 slice.169
  88.7 0.7 collective-permute-start.25
  89.4 1.6 collective-permute-start.26
  90.9 0.6 collective-permute-start.27
  91.5 10.3 %experts.3 = (bf16[256,1024]{1,0:T(8,128)(2,1)}, bf16[256,1024]{1,0:T(8,128)(2,1)}, bf16[256,1024]{1,0:T(8,128)(2,1)}, bf16[256,1024]{1,0:T(8,128)(2,1)}) custom-call(bf16[2,224,256]{2,1,0:T(8,128)(2,1)S(1)} %slice.160.refs_0_, bf16[2,2,256,112]{3,2,1,0:T(8,128)(2,1)S(1)} %slice.161.refs_1_, f32[2,256,2]{2,1,0:T(8,128)S(1)} %copy.20.refs_2_, ...), custom_call_target="tpu_custom_call" | custom-call | flops 4227858432 | bytes 23068672 | tf_op jit(solution)/shard_map/experts/pallas_call | solution.py:364
  101.9 1.5 collective-permute-start.28
  103.4 0.6 collective-permute-start.29
  104.2 0.8 add_convert_fusion.8
  105.0 0.8 add_convert_fusion.6
  105.8 9.0 %experts.4 = (bf16[256,1024]{1,0:T(8,128)(2,1)S(1)}, bf16[256,1024]{1,0:T(8,128)(2,1)}) custom-call(bf16[1,224,256]{2,1,0:T(8,128)(2,1)S(1)} %get-tuple-element.139.refs_0_, bf16[2,1,256,112]{3,2,1,0:T(8,128)(2,1)S(1)} %get-tuple-element.137.refs_1_, f32[1,256,2]{2,1,0:T(8,128)S(1)} %copy.21.refs_2_, bf16[2048,1536]{1,0:T(8,128)(2,1)} %bitcast.28, ...), custom_call_target="tpu_custom_call" | custom-call | flops 2113929216 | bytes 20971520 | tf_op jit(solution)/shard_map/experts/pallas_call | solution.py:364
  114.9 0.8 copy-done.14
  115.7 1.5 collective-permute-start.30
  117.9 8.5 %experts.5 = (bf16[256,1024]{1,0:T(8,128)(2,1)S(1)}, bf16[256,1024]{1,0:T(8,128)(2,1)S(1)}) custom-call(bf16[1,224,256]{2,1,0:T(8,128)(2,1)S(1)} %get-tuple-element.138.refs_0_, bf16[2,1,256,112]{3,2,1,0:T(8,128)(2,1)S(1)} %get-tuple-element.136.refs_1_, f32[1,256,2]{2,1,0:T(8,128)S(1)} %copy.22.refs_2_, bf16[2048,1536]{1,0:T(8,128)(2,1)} %bitcast.29, ...), custom_call_target="tpu_custom_call" | custom-call | flops 2113929216 | bytes 20971520 | tf_op jit(solution)/shard_map/experts/pallas_call | solution.py:364
  126.4 1.4 collective-permute-done.31
  127.8 1.3 add_convert_fusion.1
  129.5 1.8 %collective-permute-start.33 = (bf16[128,1024]{1,0:T(8,128)(2,1)S(1)}, bf16[128,1024]{1,0:T(8,128)(2,1)S(1)}, u32[]{:S(2)}, u32[]{:S(2)}) collective-permute-start(bf16[128,1024]{1,0:T(8,128)(2,1)S(1)} %slice.173), channel_id=1, source_target_pairs={{0,16},{16,0},{1,17},{17,1},{2,18},{18,2},{3,19},{19,3},{4,20},{20... | collective-permute-start | bytes 786440 | tf_op jit(solution)/shard_map/ppermute | solution.py:25
  131.3 6.8 %collective-permute-done.32 = bf16[128,1024]{1,0:T(8,128)(2,1)S(1)} collective-permute-done((bf16[128,1024]{1,0:T(8,128)(2,1)S(1)}, bf16[128,1024]{1,0:T(8,128)(2,1)S(1)}, u32[]{:S(2)}, u32[]{:S(2)}) %collective-permute-start.32) | collective-permute-done | bytes 262176 | tf_op jit(solution)/shard_map/ppermute | solution.py:25
  138.4 1.6 collective-permute-start.34
  140.0 0.6 collective-permute-start.35
  140.6 1.1 add_convert_fusion.4
  141.9 0.9 collective-permute-start.36
  142.8 2.0 %collective-permute-done.34 = bf16[128,1024]{1,0:T(8,128)(2,1)S(1)} collective-permute-done((bf16[128,1024]{1,0:T(8,128)(2,1)S(1)}, bf16[128,1024]{1,0:T(8,128)(2,1)S(1)}, u32[]{:S(2)}, u32[]{:S(2)}) %collective-permute-start.34) | collective-permute-done | bytes 262176 | tf_op jit(solution)/shard_map/ppermute | solution.py:25
  144.9 1.6 collective-permute-done.35
  146.5 1.1 convert_add_fusion
  147.6 6.2 %collective-permute-done.36 = bf16[128,2048]{1,0:T(8,128)(2,1)S(1)} collective-permute-done((bf16[128,2048]{1,0:T(8,128)(2,1)S(1)}, bf16[128,2048]{1,0:T(8,128)(2,1)S(1)}, u32[]{:S(2)}, u32[]{:S(2)}) %collective-permute-start.36) | collective-permute-done | bytes 524320 | tf_op jit(solution)/shard_map/ppermute | solution.py:25
  154.0 0.8 collective-permute-start.37
  154.8 9.4 %collective-permute-done.37 = bf16[64,2048]{1,0:T(8,128)(2,1)S(1)} collective-permute-done((bf16[64,2048]{1,0:T(8,128)(2,1)S(1)}, bf16[64,2048]{1,0:T(8,128)(2,1)S(1)}, u32[]{:S(2)}, u32[]{:S(2)}) %collective-permute-start.37) | collective-permute-done | bytes 262176 | tf_op jit(solution)/shard_map/ppermute | solution.py:25
  164.1 0.8 fusion.6
  (112 shorter events, 6.6 us)
Async XLA Ops:
  0.0 23.7 %copy-start = (bf16[2048,512]{1,0:T(8,128)(2,1)S(1)}, bf16[2048,512]{1,0:T(8,128)(2,1)}, u32[]{:S(2)}) copy-start(bf16[2048,512]{1,0:T(8,128)(2,1)} %weight_ref.1) | copy-start | bytes 6291460
  0.0 23.7 %copy-start.1 = (f32[128]{0:T(128)S(1)}, f32[128]{0:T(128)}, u32[]{:S(2)}) copy-start(f32[128]{0:T(128)} %param.16) | copy-start | bytes 1540
  0.0 42.8 %collective-permute-start.11 = (bf16[2048,1536]{1,0:T(8,128)(2,1)}, bf16[2048,1536]{1,0:T(8,128)(2,1)}, u32[]{:S(2)}, u32[]{:S(2)}) collective-permute-start(bf16[2048,1536]{1,0:T(8,128)(2,1)} %bitcast.26), channel_id=1, source_target_pairs={{0,1},{1,0},{2,3},{3,2},{4,5},{5,4},{6,7},{7,6},{8,9},{9,8},{10,11... | collective-permute-start | bytes 18874376 | tf_op jit(solution)/shard_map/ppermute | solution.py:25
  3.1 8.7 %collective-permute-start = (bf16[64,640]{1,0:T(8,128)(2,1)S(1)}, bf16[64,640]{1,0:T(8,128)(2,1)S(1)}, u32[]{:S(2)}, u32[]{:S(2)}) collective-permute-start(bf16[64,640]{1,0:T(8,128)(2,1)S(1)} %get-tuple-element.66), channel_id=1, source_target_pairs={{0,8},{4,12},{8,0},{12,4},{1,9},{5,13},{9,1},{13,5},{2,10},{6,14},... | collective-permute-start | bytes 245768 | tf_op jit(solution)/shard_map/ppermute | solution.py:25
  6.7 5.1 %collective-permute-start.1 = (bf16[64,640]{1,0:T(8,128)(2,1)S(1)}, bf16[64,640]{1,0:T(8,128)(2,1)S(1)}, u32[]{:S(2)}, u32[]{:S(2)}) collective-permute-start(bf16[64,640]{1,0:T(8,128)(2,1)S(1)} %get-tuple-element.66), channel_id=1, source_target_pairs={{0,4},{4,0},{8,12},{12,8},{1,5},{5,1},{9,13},{13,9},{2,6},{6,2},{1... | collective-permute-start | bytes 245768 | tf_op jit(solution)/shard_map/ppermute | solution.py:25
  8.3 6.3 %collective-permute-start.2 = (bf16[64,640]{1,0:T(8,128)(2,1)S(1)}, bf16[64,640]{1,0:T(8,128)(2,1)S(1)}, u32[]{:S(2)}, u32[]{:S(2)}) collective-permute-start(bf16[64,640]{1,0:T(8,128)(2,1)S(1)} %get-tuple-element.66), channel_id=1, source_target_pairs={{0,12},{4,8},{8,4},{12,0},{1,13},{5,9},{9,5},{13,1},{2,14},{6,10},... | collective-permute-start | bytes 245768 | tf_op jit(solution)/shard_map/ppermute | solution.py:25
  8.3 8.0 %collective-permute-start.3 = (bf16[64,2048]{1,0:T(8,128)(2,1)S(1)}, bf16[64,2048]{1,0:T(8,128)(2,1)S(1)}, u32[]{:S(2)}, u32[]{:S(2)}) collective-permute-start(bf16[64,2048]{1,0:T(8,128)(2,1)S(1)} %get-tuple-element.65.first_ref), channel_id=1, source_target_pairs={{0,2},{1,3},{2,0},{3,1},{4,6},{5,7},{6,4},{7,5},{8,10},{9,11},{10,... | collective-permute-start | bytes 786440 | tf_op jit(solution)/shard_map/ppermute | solution.py:25
  11.7 4.6 %collective-permute-start.4 = (bf16[64,2048]{1,0:T(8,128)(2,1)S(1)}, bf16[64,2048]{1,0:T(8,128)(2,1)S(1)}, u32[]{:S(2)}, u32[]{:S(2)}) collective-permute-start(bf16[64,2048]{1,0:T(8,128)(2,1)S(1)} %get-tuple-element.65.first_ref), channel_id=1, source_target_pairs={{0,1},{1,0},{2,3},{3,2},{4,5},{5,4},{6,7},{7,6},{8,9},{9,8},{10,11... | collective-permute-start | bytes 786440 | tf_op jit(solution)/shard_map/ppermute | solution.py:25
  14.6 13.6 %copy-start.2 = (bf16[512,2048]{1,0:T(8,128)(2,1)S(1)}, bf16[512,2048]{1,0:T(8,128)(2,1)}, u32[]{:S(2)}) copy-start(bf16[512,2048]{1,0:T(8,128)(2,1)} %refs_3_.1) | copy-start | bytes 6291460
  16.3 5.7 %collective-permute-start.6 = (bf16[256,384]{1,0:T(8,128)(2,1)S(1)}, bf16[256,384]{1,0:T(8,128)(2,1)S(1)}, u32[]{:S(2)}, u32[]{:S(2)}) collective-permute-start(bf16[256,384]{1,0:T(8,128)(2,1)S(1)} %pad_maximum_fusion.3), channel_id=1, source_target_pairs={{0,2},{1,3},{2,0},{3,1},{4,6},{5,7},{6,4},{7,5},{8,10},{9,11},{10,... | collective-permute-start | bytes 589832 | tf_op jit(solution)/shard_map/ppermute | solution.py:25
  17.8 5.9 %collective-permute-start.5 = (bf16[64,2048]{1,0:T(8,128)(2,1)S(1)}, bf16[64,2048]{1,0:T(8,128)(2,1)S(1)}, u32[]{:S(2)}, u32[]{:S(2)}) collective-permute-start(bf16[64,2048]{1,0:T(8,128)(2,1)S(1)} %collective-permute-done.3.second_ref), channel_id=1, source_target_pairs={{0,1},{1,0},{2,3},{3,2},{4,5},{5,4},{6,7},{7,6},{8,9},{9,8},{10,11... | collective-permute-start | bytes 786440 | tf_op jit(solution)/shard_map/ppermute | solution.py:25
  22.1 6.1 %collective-permute-start.7 = (bf16[512,256]{1,0:T(8,128)(2,1)S(1)}, bf16[512,256]{1,0:T(8,128)(2,1)S(1)}, u32[]{:S(2)}, u32[]{:S(2)}) collective-permute-start(bf16[512,256]{1,0:T(8,128)(2,1)S(1)} %pad_maximum_fusion.1.refs_1_), channel_id=1, source_target_pairs={{0,1},{1,0},{2,3},{3,2},{4,5},{5,4},{6,7},{7,6},{8,9},{9,8},{10,11... | collective-permute-start | bytes 786440 | tf_op jit(solution)/shard_map/ppermute | solution.py:25
  22.2 5.9 %collective-permute-start.8 = (bf16[2,256,128]{2,1,0:T(8,128)(2,1)S(1)}, bf16[2,256,128]{2,1,0:T(8,128)(2,1)S(1)}, u32[]{:S(2)}, u32[]{:S(2)}) collective-permute-start(bf16[2,256,128]{2,1,0:T(8,128)(2,1)S(1)} %pad_maximum_fusion.4), channel_id=1, source_target_pairs={{0,16},{16,0},{1,17},{17,1},{2,18},{18,2},{3,19},{19,3},{4,20},{20... | collective-permute-start | bytes 393224 | tf_op jit(solution)/shard_map/ppermute | solution.py:25
  23.7 10.0 %copy-start.3 = (bf16[1,768,2048]{2,1,0:T(8,128)(2,1)S(1)}, bf16[1,768,2048]{2,1,0:T(8,128)(2,1)}, u32[]{:S(2)}) copy-start(bf16[1,768,2048]{2,1,0:T(8,128)(2,1)} %param.23) | copy-start | bytes 9437188
  28.2 14.5 %copy-start.9 = (bf16[1,64,2048]{2,1,0:T(8,128)(2,1)S(1)}, bf16[1,64,2048]{2,1,0:T(8,128)(2,1)}, u32[]{:S(2)}) copy-start(bf16[1,64,2048]{2,1,0:T(8,128)(2,1)} %param.12) | copy-start | bytes 786436
  31.0 12.0 %copy-start.16 = (f32[2048]{0:T(1024)S(1)}, f32[2048]{0:T(1024)}, u32[]{:S(2)}) copy-start(f32[2048]{0:T(1024)} %param.19) | copy-start | bytes 24580
  31.0 2.7 %collective-permute-start.9 = (f32[128,2048]{1,0:T(8,128)S(1)}, f32[128,2048]{1,0:T(8,128)S(1)}, u32[]{:S(2)}, u32[]{:S(2)}) collective-permute-start(f32[128,2048]{1,0:T(8,128)S(1)} %get-tuple-element.73), channel_id=1, source_target_pairs={{0,1},{1,0},{2,3},{3,2},{4,5},{5,4},{6,7},{7,6},{8,9},{9,8},{10,11... | collective-permute-start | bytes 3145736 | tf_op jit(solution)/shard_map/ppermute | solution.py:25
  33.7 9.1 %collective-permute-start.12 = (bf16[768,2048]{1,0:T(8,128)(2,1)S(1)}, bf16[768,2048]{1,0:T(8,128)(2,1)S(1)}, u32[]{:S(2)}, u32[]{:S(2)}) collective-permute-start(bf16[768,2048]{1,0:T(8,128)(2,1)S(1)} %bitcast.33), channel_id=1, source_target_pairs={{0,1},{1,0},{2,3},{3,2},{4,5},{5,4},{6,7},{7,6},{8,9},{9,8},{10,11... | collective-permute-start | bytes 9437192 | tf_op jit(solution)/shard_map/ppermute | solution.py:25
  34.0 8.7 %collective-permute-start.10 = (bf16[64,2048]{1,0:T(8,128)(2,1)S(1)}, bf16[64,2048]{1,0:T(8,128)(2,1)S(1)}, u32[]{:S(2)}, u32[]{:S(2)}) collective-permute-start(bf16[64,2048]{1,0:T(8,128)(2,1)S(1)} %slice.232), channel_id=1, source_target_pairs={{0,2},{1,3},{2,0},{3,1},{4,6},{5,7},{6,4},{7,5},{8,10},{9,11},{10,... | collective-permute-start | bytes 786440 | tf_op jit(solution)/shard_map/ppermute | solution.py:25
  42.8 6.0 %copy-start.5 = (f32[64,2048]{1,0:T(8,128)}, f32[64,2048]{1,0:T(8,128)S(1)}, u32[]{:S(2)}) copy-start(f32[64,2048]{1,0:T(8,128)S(1)} %fusion.5) | copy-start | bytes 1572868
  42.8 3.3 %copy-start.4 = (bf16[768,2048]{1,0:T(8,128)(2,1)}, bf16[768,2048]{1,0:T(8,128)(2,1)S(1)}, u32[]{:S(2)}) copy-start(bf16[768,2048]{1,0:T(8,128)(2,1)S(1)} %collective-permute-done.12.refs_6_) | copy-start | bytes 9437188
  43.1 7.8 %collective-permute-start.15 = (bf16[64,2048]{1,0:T(8,128)(2,1)S(1)}, bf16[64,2048]{1,0:T(8,128)(2,1)S(1)}, u32[]{:S(2)}, u32[]{:S(2)}) collective-permute-start(bf16[64,2048]{1,0:T(8,128)(2,1)S(1)} %multiply_convert_fusion.refs_7_), channel_id=1, source_target_pairs={{0,2},{1,3},{2,0},{3,1},{4,6},{5,7},{6,4},{7,5},{8,10},{9,11},{10,... | collective-permute-start | bytes 786440 | tf_op jit(solution)/shard_map/ppermute | solution.py:25
  44.6 7.5 %collective-permute-start.16 = (bf16[64,2048]{1,0:T(8,128)(2,1)S(1)}, bf16[64,2048]{1,0:T(8,128)(2,1)S(1)}, u32[]{:S(2)}, u32[]{:S(2)}) collective-permute-start(bf16[64,2048]{1,0:T(8,128)(2,1)S(1)} %multiply_convert_fusion.refs_7_), channel_id=1, source_target_pairs={{0,16},{16,0},{1,17},{17,1},{2,18},{18,2},{3,19},{19,3},{4,20},{20... | collective-permute-start | bytes 786440 | tf_op jit(solution)/shard_map/ppermute | solution.py:25
  46.1 13.9 %collective-permute-start.13 = (bf16[64,2048]{1,0:T(8,128)(2,1)S(1)}, bf16[64,2048]{1,0:T(8,128)(2,1)S(1)}, u32[]{:S(2)}, u32[]{:S(2)}) collective-permute-start(bf16[64,2048]{1,0:T(8,128)(2,1)S(1)} %multiply_convert_fusion.refs_7_), channel_id=1, source_target_pairs={{0,8},{4,12},{8,0},{12,4},{1,9},{5,13},{9,1},{13,5},{2,10},{6,14},... | collective-permute-start | bytes 786440 | tf_op jit(solution)/shard_map/ppermute | solution.py:25
  48.8 12.5 %collective-permute-start.17 = (bf16[64,2048]{1,0:T(8,128)(2,1)S(1)}, bf16[64,2048]{1,0:T(8,128)(2,1)S(1)}, u32[]{:S(2)}, u32[]{:S(2)}) collective-permute-start(bf16[64,2048]{1,0:T(8,128)(2,1)S(1)} %multiply_convert_fusion.refs_7_), channel_id=1, source_target_pairs={{0,4},{4,0},{8,12},{12,8},{1,5},{5,1},{9,13},{13,9},{2,6},{6,2},{1... | collective-permute-start | bytes 786440 | tf_op jit(solution)/shard_map/ppermute | solution.py:25
  60.0 7.2 %collective-permute-start.14 = (bf16[64,2048]{1,0:T(8,128)(2,1)S(1)}, bf16[64,2048]{1,0:T(8,128)(2,1)S(1)}, u32[]{:S(2)}, u32[]{:S(2)}) collective-permute-start(bf16[64,2048]{1,0:T(8,128)(2,1)S(1)} %collective-permute-done.13), channel_id=1, source_target_pairs={{0,4},{4,0},{8,12},{12,8},{1,5},{5,1},{9,13},{13,9},{2,6},{6,2},{1... | collective-permute-start | bytes 786440 | tf_op jit(solution)/shard_map/ppermute | solution.py:25
  62.0 23.4 %collective-permute-start.18 = (bf16[128,2048]{1,0:T(8,128)(2,1)}, bf16[128,2048]{1,0:T(8,128)(2,1)S(1)}, u32[]{:S(2)}, u32[]{:S(2)}) collective-permute-start(bf16[128,2048]{1,0:T(8,128)(2,1)} %constant_dynamic-update-slice_fusion.4.refs_8_), channel_id=1, source_target_pairs={{0,2},{1,3},{2,0},{3,1},{4,6},{5,7},{6,4},{7,5},{8,10},{9,11},{10,... | collective-permute-start | bytes 1572872 | tf_op jit(solution)/shard_map/ppermute | solution.py:25
  62.5 25.2 %collective-permute-start.20 = (bf16[128,2048]{1,0:T(8,128)(2,1)}, bf16[128,2048]{1,0:T(8,128)(2,1)}, u32[]{:S(2)}, u32[]{:S(2)}) collective-permute-start(bf16[128,2048]{1,0:T(8,128)(2,1)} %constant_dynamic-update-slice_fusion.4.refs_8_), channel_id=1, source_target_pairs={{0,16},{16,0},{1,17},{17,1},{2,18},{18,2},{3,19},{19,3},{4,20},{20... | collective-permute-start | bytes 1572872 | tf_op jit(solution)/shard_map/ppermute | solution.py:25
  63.9 16.5 %collective-permute-start.22 = (bf16[64,1024]{1,0:T(8,128)(2,1)S(1)}, bf16[64,1024]{1,0:T(8,128)(2,1)S(1)}, u32[]{:S(2)}, u32[]{:S(2)}) collective-permute-start(bf16[64,1024]{1,0:T(8,128)(2,1)S(1)} %slice.166), channel_id=1, source_target_pairs={{0,16},{16,0},{1,17},{17,1},{2,18},{18,2},{3,19},{19,3},{4,20},{20... | collective-permute-start | bytes 393224 | tf_op jit(solution)/shard_map/ppermute | solution.py:25
  69.2 12.8 %copy-start.10 = (pred[4,112,256]{2,1,0:T(8,128)(4,1)}, pred[4,112,256]{2,1,0:T(8,128)(4,1)S(1)}, u32[]{:S(2)}) copy-start(pred[4,112,256]{2,1,0:T(8,128)(4,1)S(1)} %get-tuple-element.144) | copy-start | bytes 344068
  69.2 12.8 %copy-start.11 = (pred[4,112,256]{2,1,0:T(8,128)(4,1)}, pred[4,112,256]{2,1,0:T(8,128)(4,1)S(1)}, u32[]{:S(2)}) copy-start(pred[4,112,256]{2,1,0:T(8,128)(4,1)S(1)} %get-tuple-element.145) | copy-start | bytes 344068
  69.6 2.2 %copy-start.8 = (pred[1,4,256,112]{3,2,1,0:T(8,128)(4,1)}, pred[1,4,256,112]{3,2,1,0:T(8,128)(4,1)S(1)}, u32[]{:S(2)}) copy-start(pred[1,4,256,112]{3,2,1,0:T(8,128)(4,1)S(1)} %get-tuple-element.147) | copy-start | bytes 344068
  69.6 15.8 %collective-permute-start.19 = (bf16[64,2048]{1,0:T(8,128)(2,1)S(1)}, bf16[64,2048]{1,0:T(8,128)(2,1)S(1)}, u32[]{:S(2)}, u32[]{:S(2)}) collective-permute-start(bf16[64,2048]{1,0:T(8,128)(2,1)S(1)} %collective-permute-done.14.refs_9_), channel_id=1, source_target_pairs={{0,2},{1,3},{2,0},{3,1},{4,6},{5,7},{6,4},{7,5},{8,10},{9,11},{10,... | collective-permute-start | bytes 786440 | tf_op jit(solution)/shard_map/ppermute | solution.py:25
  70.2 15.2 %collective-permute-start.21 = (bf16[64,2048]{1,0:T(8,128)(2,1)S(1)}, bf16[64,2048]{1,0:T(8,128)(2,1)S(1)}, u32[]{:S(2)}, u32[]{:S(2)}) collective-permute-start(bf16[64,2048]{1,0:T(8,128)(2,1)S(1)} %collective-permute-done.14.refs_9_), channel_id=1, source_target_pairs={{0,16},{16,0},{1,17},{17,1},{2,18},{18,2},{3,19},{19,3},{4,20},{20... | collective-permute-start | bytes 786440 | tf_op jit(solution)/shard_map/ppermute | solution.py:25
  80.4 5.0 %collective-permute-start.23 = (bf16[64,1024]{1,0:T(8,128)(2,1)S(1)}, bf16[64,1024]{1,0:T(8,128)(2,1)S(1)}, u32[]{:S(2)}, u32[]{:S(2)}) collective-permute-start(bf16[64,1024]{1,0:T(8,128)(2,1)S(1)} %slice.167), channel_id=1, source_target_pairs={{0,2},{1,3},{2,0},{3,1},{4,6},{5,7},{6,4},{7,5},{8,10},{9,11},{10,... | collective-permute-start | bytes 393224 | tf_op jit(solution)/shard_map/ppermute | solution.py:25
  85.4 0.8 copy-start.7
  86.2 15.7 %collective-permute-start.24 = (bf16[128,1024]{1,0:T(8,128)(2,1)S(1)}, bf16[128,1024]{1,0:T(8,128)(2,1)S(1)}, u32[]{:S(2)}, u32[]{:S(2)}) collective-permute-start(bf16[128,1024]{1,0:T(8,128)(2,1)S(1)} %slice.168), channel_id=1, source_target_pairs={{0,16},{16,0},{1,17},{17,1},{2,18},{18,2},{3,19},{19,3},{4,20},{20... | collective-permute-start | bytes 786440 | tf_op jit(solution)/shard_map/ppermute | solution.py:25
  88.7 13.2 %collective-permute-start.25 = (bf16[128,1024]{1,0:T(8,128)(2,1)S(1)}, bf16[128,1024]{1,0:T(8,128)(2,1)S(1)}, u32[]{:S(2)}, u32[]{:S(2)}) collective-permute-start(bf16[128,1024]{1,0:T(8,128)(2,1)S(1)} %slice.169), channel_id=1, source_target_pairs={{0,2},{1,3},{2,0},{3,1},{4,6},{5,7},{6,4},{7,5},{8,10},{9,11},{10,... | collective-permute-start | bytes 786440 | tf_op jit(solution)/shard_map/ppermute | solution.py:25
  89.4 12.5 %collective-permute-start.26 = (bf16[64,1024]{1,0:T(8,128)(2,1)S(1)}, bf16[64,1024]{1,0:T(8,128)(2,1)S(1)}, u32[]{:S(2)}, u32[]{:S(2)}) collective-permute-start(bf16[64,1024]{1,0:T(8,128)(2,1)S(1)} %slice.132), channel_id=1, source_target_pairs={{0,16},{16,0},{1,17},{17,1},{2,18},{18,2},{3,19},{19,3},{4,20},{20... | collective-permute-start | bytes 393224 | tf_op jit(solution)/shard_map/ppermute | solution.py:25
  90.9 10.9 %collective-permute-start.27 = (bf16[64,1024]{1,0:T(8,128)(2,1)S(1)}, bf16[64,1024]{1,0:T(8,128)(2,1)S(1)}, u32[]{:S(2)}, u32[]{:S(2)}) collective-permute-start(bf16[64,1024]{1,0:T(8,128)(2,1)S(1)} %slice.133), channel_id=1, source_target_pairs={{0,2},{1,3},{2,0},{3,1},{4,6},{5,7},{6,4},{7,5},{8,10},{9,11},{10,... | collective-permute-start | bytes 393224 | tf_op jit(solution)/shard_map/ppermute | solution.py:25
  101.9 13.0 %collective-permute-start.28 = (bf16[256,1024]{1,0:T(8,128)(2,1)}, bf16[256,1024]{1,0:T(8,128)(2,1)S(1)}, u32[]{:S(2)}, u32[]{:S(2)}) collective-permute-start(bf16[256,1024]{1,0:T(8,128)(2,1)} %get-tuple-element.94), channel_id=1, source_target_pairs={{0,16},{16,0},{1,17},{17,1},{2,18},{18,2},{3,19},{19,3},{4,20},{20... | collective-permute-start | bytes 1572872 | tf_op jit(solution)/shard_map/ppermute | solution.py:25
  103.4 11.5 %collective-permute-start.29 = (bf16[256,1024]{1,0:T(8,128)(2,1)}, bf16[256,1024]{1,0:T(8,128)(2,1)}, u32[]{:S(2)}, u32[]{:S(2)}) collective-permute-start(bf16[256,1024]{1,0:T(8,128)(2,1)} %get-tuple-element.95), channel_id=1, source_target_pairs={{0,2},{1,3},{2,0},{3,1},{4,6},{5,7},{6,4},{7,5},{8,10},{9,11},{10,... | collective-permute-start | bytes 1572872 | tf_op jit(solution)/shard_map/ppermute | solution.py:25
  114.9 0.8 copy-start.14
  115.7 10.7 %collective-permute-start.30 = (bf16[256,1024]{1,0:T(8,128)(2,1)S(1)}, bf16[256,1024]{1,0:T(8,128)(2,1)}, u32[]{:S(2)}, u32[]{:S(2)}) collective-permute-start(bf16[256,1024]{1,0:T(8,128)(2,1)S(1)} %get-tuple-element.104), channel_id=1, source_target_pairs={{0,16},{16,0},{1,17},{17,1},{2,18},{18,2},{3,19},{19,3},{4,20},{20... | collective-permute-start | bytes 1572872 | tf_op jit(solution)/shard_map/ppermute | solution.py:25
  117.2 10.6 %collective-permute-start.31 = (bf16[256,1024]{1,0:T(8,128)(2,1)}, bf16[256,1024]{1,0:T(8,128)(2,1)S(1)}, u32[]{:S(2)}, u32[]{:S(2)}) collective-permute-start(bf16[256,1024]{1,0:T(8,128)(2,1)} %get-tuple-element.105), channel_id=1, source_target_pairs={{0,2},{1,3},{2,0},{3,1},{4,6},{5,7},{6,4},{7,5},{8,10},{9,11},{10,... | collective-permute-start | bytes 1572872 | tf_op jit(solution)/shard_map/ppermute | solution.py:25
  117.8 9.9 %copy-start.13 = (bf16[256,1024]{1,0:T(8,128)(2,1)S(1)}, bf16[256,1024]{1,0:T(8,128)(2,1)}, u32[]{:S(2)}) copy-start(bf16[256,1024]{1,0:T(8,128)(2,1)} %get-tuple-element.113) | copy-start | bytes 1572868
  117.8 11.5 %copy-start.12 = (bf16[256,1024]{1,0:T(8,128)(2,1)S(1)}, bf16[256,1024]{1,0:T(8,128)(2,1)}, u32[]{:S(2)}) copy-start(bf16[256,1024]{1,0:T(8,128)(2,1)} %get-tuple-element.115) | copy-start | bytes 1572868
  127.8 13.9 %copy-start.15 = (bf16[256,1024]{1,0:T(8,128)(2,1)S(1)}, bf16[256,1024]{1,0:T(8,128)(2,1)}, u32[]{:S(2)}) copy-start(bf16[256,1024]{1,0:T(8,128)(2,1)} %copy-done.14) | copy-start | bytes 1572868
  129.1 9.0 %collective-permute-start.32 = (bf16[128,1024]{1,0:T(8,128)(2,1)S(1)}, bf16[128,1024]{1,0:T(8,128)(2,1)S(1)}, u32[]{:S(2)}, u32[]{:S(2)}) collective-permute-start(bf16[128,1024]{1,0:T(8,128)(2,1)S(1)} %slice.172), channel_id=1, source_target_pairs={{0,2},{1,3},{2,0},{3,1},{4,6},{5,7},{6,4},{7,5},{8,10},{9,11},{10,... | collective-permute-start | bytes 786440 | tf_op jit(solution)/shard_map/ppermute | solution.py:25
  129.5 8.9 %collective-permute-start.33 = (bf16[128,1024]{1,0:T(8,128)(2,1)S(1)}, bf16[128,1024]{1,0:T(8,128)(2,1)S(1)}, u32[]{:S(2)}, u32[]{:S(2)}) collective-permute-start(bf16[128,1024]{1,0:T(8,128)(2,1)S(1)} %slice.173), channel_id=1, source_target_pairs={{0,16},{16,0},{1,17},{17,1},{2,18},{18,2},{3,19},{19,3},{4,20},{20... | collective-permute-start | bytes 786440 | tf_op jit(solution)/shard_map/ppermute | solution.py:25
  138.4 6.4 %collective-permute-start.34 = (bf16[128,1024]{1,0:T(8,128)(2,1)S(1)}, bf16[128,1024]{1,0:T(8,128)(2,1)S(1)}, u32[]{:S(2)}, u32[]{:S(2)}) collective-permute-start(bf16[128,1024]{1,0:T(8,128)(2,1)S(1)} %slice.144), channel_id=1, source_target_pairs={{0,2},{1,3},{2,0},{3,1},{4,6},{5,7},{6,4},{7,5},{8,10},{9,11},{10,... | collective-permute-start | bytes 786440 | tf_op jit(solution)/shard_map/ppermute | solution.py:25
  140.0 6.4 %collective-permute-start.35 = (bf16[128,1024]{1,0:T(8,128)(2,1)S(1)}, bf16[128,1024]{1,0:T(8,128)(2,1)S(1)}, u32[]{:S(2)}, u32[]{:S(2)}) collective-permute-start(bf16[128,1024]{1,0:T(8,128)(2,1)S(1)} %slice.145), channel_id=1, source_target_pairs={{0,16},{16,0},{1,17},{17,1},{2,18},{18,2},{3,19},{19,3},{4,20},{20... | collective-permute-start | bytes 786440 | tf_op jit(solution)/shard_map/ppermute | solution.py:25
  141.9 22.2 %copy-start.6 = (f32[64,2048]{1,0:T(8,128)S(1)}, f32[64,2048]{1,0:T(8,128)}, u32[]{:S(2)}) copy-start(f32[64,2048]{1,0:T(8,128)} %copy-done.5) | copy-start | bytes 1572868
  141.9 11.9 %collective-permute-start.36 = (bf16[128,2048]{1,0:T(8,128)(2,1)S(1)}, bf16[128,2048]{1,0:T(8,128)(2,1)S(1)}, u32[]{:S(2)}, u32[]{:S(2)}) collective-permute-start(bf16[128,2048]{1,0:T(8,128)(2,1)S(1)} %pad_maximum_fusion), channel_id=1, source_target_pairs={{0,4},{4,0},{8,12},{12,8},{1,5},{5,1},{9,13},{13,9},{2,6},{6,2},{1... | collective-permute-start | bytes 1572872 | tf_op jit(solution)/shard_map/ppermute | solution.py:25
  154.0 10.1 %collective-permute-start.37 = (bf16[64,2048]{1,0:T(8,128)(2,1)S(1)}, bf16[64,2048]{1,0:T(8,128)(2,1)S(1)}, u32[]{:S(2)}, u32[]{:S(2)}) collective-permute-start(bf16[64,2048]{1,0:T(8,128)(2,1)S(1)} %slice.231), channel_id=1, source_target_pairs={{0,8},{4,12},{8,0},{12,4},{1,9},{5,13},{9,1},{13,5},{2,10},{6,14},... | collective-permute-start | bytes 786440 | tf_op jit(solution)/shard_map/ppermute | solution.py:25

commit v7 on v6

--- a/solution.py
+++ b/solution.py
@@ -56,15 +56,13 @@
         blocks = blocks + [swap(block, "seq", bits) for block in blocks]
     beyond = [swap(block, "seq", bits_left[-1]) for block in blocks]
     outer = both_ways(own)
-    outer_low, outer_high, first = ready(outer[0][:, :half], outer[1][:, half:], blocks[1])
-    middle = jnp.concatenate([first] + blocks[2:] + beyond[:-1], axis=0)
-    outer_corner = swap(outer_low, "role", 1), swap(outer_high, "rep", ACROSS)
+    middle = jnp.concatenate(blocks[1:] + beyond[:-1], axis=0)
+    middle, *outer_corner = ready(middle, *corners(*outer))
     last, coded = ready(beyond[-1], coded)
     inner = both_ways(middle)
     final = both_ways(last)
     inner_corner = corners(*inner)
-    by_rep, by_role, *outer_corner = ready(*final, *outer_corner)
-    final_corner = corners(by_rep, by_role)
+    final_corner = corners(*final)
     groups = [[], [], [], []]
     start = 0
     for part, beside, corner in (
@@ -72,11 +70,11 @@
         (middle, inner, inner_corner),
         (last, final, final_corner),
     ):
-        groups[0].append((start, 0, part))
-        groups[1].append((start, 0, beside[0]))
-        groups[2].append((start, 0, beside[1]))
-        groups[3].append((start, 0, corner[0]))
-        groups[3].append((start, half, corner[1]))
+        groups[0].append((start, 0, beside[0]))
+        groups[1].append((start, 0, beside[1]))
+        groups[2].append((start, 0, corner[0]))
+        groups[2].append((start, half, corner[1]))
+        groups[3].append((start, 0, part))
         start += part.shape[0]
     return groups, coded
 
@@ -85,16 +83,14 @@
     return (first.astype(jnp.float32) + second.astype(jnp.float32)).astype(jnp.bfloat16)
 
 
-def collect_rows(make_near, by_rep, by_role, corner):
+def collect_rows(near, by_rep, by_role, corner):
     straight_low = swap(by_role[0], "role", 1)
     straight_high = swap(by_rep[1], "rep", ACROSS)
-    straight_low, straight_high, *corner = ready(straight_low, straight_high, *corner)
-    near = make_near(corner[0])
-    corner_low, corner_high, *near = ready(
-        swap(corner[0], "role", 1), swap(corner[1], "rep", ACROSS), *near
-    )
-    cut = near[0].shape[0] // 2
-    low_sum, high_sum = added(by_rep[0], corner_low), added(by_role[1], corner_high)
+    straight_low, straight_high, near_low, near_high, *corner = ready(
+        straight_low, straight_high, *near, *corner[0], *corner[1]
+    )
+    cut = near_low.shape[0] // 2
+    halves = slice(0, cut), slice(cut, None)
 
     def merged(rows, turned_low, turned_high):
         return jnp.concatenate(
@@ -103,20 +99,30 @@
                 + first[rows].astype(jnp.float32)
                 + second.astype(jnp.float32)
                 for base, first, second in (
-                    (near[0], straight_low, turned_low),
-                    (near[1], straight_high, turned_high),
+                    (near_low, straight_low, turned_low),
+                    (near_high, straight_high, turned_high),
                 )
             ],
             axis=1,
         )
 
-    def turned(rows):
-        return swap(low_sum[rows], "rep", ACROSS), swap(high_sum[rows], "role", 1)
-
-    *far, low_sum, high_sum = ready(*turned(slice(cut, None)), low_sum, high_sum)
-    leaving = merged(slice(cut, None), *far).astype(jnp.bfloat16)
-    *beside, _ = ready(*turned(slice(0, cut)), leaving)
-    total = merged(slice(0, cut), *beside)
+    def corners(number):
+        low, high = corner[2 * number : 2 * number + 2]
+        return swap(low, "role", 1), swap(high, "rep", ACROSS)
+
+    def turned(number, corner_low, corner_high):
+        rows = halves[number]
+        return (
+            swap(added(by_rep[0][rows], corner_low), "rep", ACROSS),
+            swap(added(by_role[1][rows], corner_high), "role", 1),
+        )
+
+    far_corner, beside_corner = corners(1), corners(0)
+    far = turned(1, *far_corner)
+    *far, corner_low, corner_high = ready(*far, *beside_corner)
+    leaving = merged(halves[1], *far).astype(jnp.bfloat16)
+    *beside, _ = ready(*turned(0, corner_low, corner_high), leaving)
+    total = merged(halves[0], *beside)
     for bits in reversed(seq_bits()):
         total = total + swap(leaving, "seq", bits).astype(jnp.float32)
         if bits != seq_bits()[0]:
@@ -258,13 +264,14 @@
     )(queries, near_kv, far_kv, w_out)
 
 
-def expert_kernel(spots, *refs):
+def expert_kernel(first, spots, cuts, *refs):
     pick_ref, place_ref, share_ref, own_gu_ref, far_gu_ref, own_dn_ref, far_dn_ref = refs[:7]
-    groups, group_rows, slots = place_ref.shape[1:]
+    group_rows, slots = place_ref.shape[2:]
+    groups = len(cuts)
     piece_refs = refs[7 : 7 + len(spots)]
-    out_refs = refs[7 + len(spots) : 7 + len(spots) + 2 * groups]
+    out_refs = refs[7 + len(spots) : 7 + len(spots) + 2 * sum(cuts)]
     x_buf, xs_buf, gu_buf, dn_buf, hid_buf, served_buf, y_buf, x_sem, w_sem, y_sem = refs[
-        7 + len(spots) + 2 * groups :
+        7 + len(spots) + len(out_refs) :
     ]
     width = x_buf.shape[2]
     half = width // 2
@@ -301,7 +308,7 @@
             if where == group:
                 copy.wait()
         chosen = jnp.dot(
-            pick_ref[group], x_buf[group], preferred_element_type=jnp.float32
+            pick_ref[first + group], x_buf[group], preferred_element_type=jnp.float32
         ).astype(jnp.bfloat16)
         xs_buf[0, pl.ds(group * slots, slots)] = chosen[:slots]
         xs_buf[1, pl.ds(group * slots, slots)] = chosen[slots:]
@@ -332,18 +339,21 @@
             total = None
             for expert in range(2):
                 placed = jnp.dot(
-                    place_ref[expert, group],
+                    place_ref[expert, first + group],
                     served_buf[expert, pl.ds(group * slots, slots), column : column + 2 * TILE],
                     preferred_element_type=jnp.float32,
                 )
-                term = placed * share_ref[group, :, expert : expert + 1]
+                term = placed * share_ref[first + group, :, expert : expert + 1]
                 total = term if total is None else total + term
             y_buf[group, :, column : column + 2 * TILE] = total.astype(jnp.bfloat16)
-        for side in range(2):
+        cut = group_rows // cuts[group]
+        for number in range(2 * cuts[group]):
+            row, side = divmod(number, 2)
+            done = len(out_copies)
             copy = pltpu.make_async_copy(
-                y_buf.at[group, :, pl.ds(side * half, half)],
-                out_refs[2 * group + side],
-                y_sem.at[group, side],
+                y_buf.at[group, pl.ds(row * cut, cut), pl.ds(side * half, half)],
+                out_refs[done],
+                y_sem.at[done],
             )
             copy.start()
             out_copies.append(copy)
@@ -351,8 +361,9 @@
         copy.wait()
 
 
-def run_experts(pieces, pick, place, share, weights):
-    groups, group_rows, slots = place.shape[1:]
+def run_experts(first, pieces, cuts, pick, place, share, weights):
+    group_rows, slots = place.shape[2:]
+    groups = len(pieces)
     hidden, width = weights[2].shape
     tiles = hidden // TILE
     spots = [
@@ -362,10 +373,14 @@
     anywhere = pl.BlockSpec(memory_space=pl.ANY)
     inside = pl.BlockSpec(memory_space=pltpu.VMEM)
     outs = pl.pallas_call(
-        lambda *refs: expert_kernel(spots, *refs),
-        out_shape=[jax.ShapeDtypeStruct((group_rows, width // 2), jnp.bfloat16)] * (2 * groups),
+        lambda *refs: expert_kernel(first, spots, cuts, *refs),
+        out_shape=[
+            jax.ShapeDtypeStruct((group_rows // cut, width // 2), jnp.bfloat16)
+            for cut in cuts
+            for _ in range(2 * cut)
+        ],
         in_specs=[inside] * 3 + [anywhere] * (4 + len(arrays)),
-        out_specs=[anywhere] * (2 * groups),
+        out_specs=[anywhere] * (2 * sum(cuts)),
         scratch_shapes=[
             pltpu.VMEM((groups, group_rows, width), jnp.bfloat16),
             pltpu.VMEM((2, groups * slots, width), jnp.bfloat16),
@@ -376,9 +391,9 @@
             pltpu.VMEM((groups, group_rows, width), jnp.bfloat16),
             pltpu.SemaphoreType.DMA((len(arrays),)),
             pltpu.SemaphoreType.DMA((2, 2 * tiles + 1)),
-            pltpu.SemaphoreType.DMA((groups, 2)),
+            pltpu.SemaphoreType.DMA((2 * sum(cuts),)),
         ],
-        compiler_params=pltpu.CompilerParams(vmem_limit_bytes=52 * 1024 * 1024),
+        compiler_params=pltpu.CompilerParams(vmem_limit_bytes=(28 + 6 * group_rows // 256) * 1024 * 1024),
         cost_estimate=pl.CostEstimate(
             flops=12 * groups * slots * width * hidden,
             bytes_accessed=12 * width * hidden + 4 * groups * group_rows * width,
@@ -386,7 +401,7 @@
         ),
         name="experts",
     )(pick, place, share, *weights, *arrays)
-    return [(outs[2 * group], outs[2 * group + 1]) for group in range(groups)]
+    return list(zip(outs[0::2], outs[1::2]))
 
 
 def per_device(
@@ -440,16 +455,17 @@
     )
     pair_kv = swap(half_kv, "rep", PAIR)
     both_routes = jnp.stack([line_routes, across[:, 2 * head_dim :]])
-    coded = jnp.concatenate([both_routes, swap(both_routes, "role", 1)], axis=0)
+    far_routes = swap(both_routes, "role", 1)
+    coded = jnp.concatenate([both_routes[1:], far_routes[:1], far_routes[1:], both_routes[:1]])
     far_gu = swap(w_gateup[0], "rep", PAIR)
     queries = make_queries([normed, across_rows, pair_rows, corner_rows], w_query, q_gain)
     kept, leaving = attend(queries, half_kv, pair_kv, w_out, head_dim)
-    kept, leaving, coded = ready(kept, leaving, coded)
     leaving, own_dn = ready(swap(leaving, "rep", PAIR), w_down[0])
     halves = kept + leaving
     far_dn = swap(own_dn, "rep", PAIR)
     far_sum = halves[row_count:].astype(jnp.bfloat16)
-    attended = halves[:row_count] + swap(far_sum, "rep", ACROSS).astype(jnp.float32)
+    across_sum, coded = ready(swap(far_sum, "rep", ACROSS), coded)
+    attended = halves[:row_count] + across_sum.astype(jnp.float32)
     mixed = tokens + attended
 
     mixed, far_gu, far_dn, coded = ready(mixed, far_gu, far_dn, coded)
@@ -481,28 +497,15 @@
 
     weights = (w_gateup[0], far_gu, w_down[0], far_dn)
 
-    def serve(pieces, first, last):
-        return run_experts(
-            pieces, pick[first:last], place[:, first:last], share[first:last], weights
-        )
-
-    def with_all(pieces, *others):
-        held = ready(*others, *(array for _, _, array in pieces))
-        pieces = [
-            (row, column, array)
-            for (row, column, _), array in zip(pieces, held[len(others) :])
-        ]
-        return pieces, held[: len(others)]
-
-    by_rep, by_role = serve(rows[1:3], 1, 3)
-    pieces, (*by_rep, role_low, role_high) = with_all(rows[3], *by_rep, *by_role)
-    (corner,) = serve([pieces], 3, 4)
-    routed = collect_rows(
-        lambda after: serve([with_all(rows[0], after)[0]], 0, 1)[0],
-        by_rep,
-        (role_low, role_high),
-        corner,
-    )
+    tables = (pick, place, share, weights)
+    by_rep, by_role = run_experts(0, rows[:2], (1, 1), *tables)
+    rep_low, rep_high, role_low, role_high, *held = ready(
+        *by_rep, *by_role, *(array for _, _, array in rows[2])
+    )
+    by_rep, by_role = (rep_low, rep_high), (role_low, role_high)
+    pieces = [(row, column, array) for (row, column, _), array in zip(rows[2], held)]
+    *corner, near = run_experts(2, [pieces, rows[3]], (2, 1), *tables)
+    routed = collect_rows(near, by_rep, by_role, corner)
     return (mixed + routed).astype(jnp.bfloat16)[None]
 
 

time: 165 us -> 171 us (1.036)
  local copies, waits for them, and re-layouts: 4.86 us -> 16.5 us
  Pallas kernels: 34.1 us -> 25 us
  waiting for transfers between devices: 75.5 us -> 68.5 us
  other arithmetic: 9.03 us -> 14.6 us
  starting transfers between devices: 40.3 us -> 43.5 us
    pallas_call x3 -> x2, Pallas kernels: 27.8 us -> 19 us  [run_experts(): pl.pallas_call(lambda *refs: expert_kernel(first, spots, cuts, *refs), ou...]
    ppermute x38 -> x40, waiting for transfers between devices: 75.5 us -> 68.5 us  [swap(): return lax.ppermute(block, axis, [(i, i ^ bits) for i in range(size)])]
    unnamed x41 -> x35, local copies, waits for them, and re-layouts: 2.85 us -> 9.73 us
    ppermute x38 -> x40, starting transfers between devices: 40.3 us -> 43.5 us  [swap(): return lax.ppermute(block, axis, [(i, i ^ bits) for i in range(size)])]
    slice x2 -> x3, local copies, waits for them, and re-layouts: 0.03 us -> 2.8 us  [corners(): by_rep[:, :half]]
    concatenate x1 -> x2, other arithmetic: 0.03 us -> 2.61 us  [the longest x1 1.87 us: spread_rows(): middle = jnp.concatenate(blocks[1:] + beyond[:-1], axis=0)]
    reduce_or x2, other arithmetic: 0.43 us -> 2.81 us  [per_device(): hit = jnp.any(named, axis=2)]
    slice x2 -> x3, local copies, waits for them, and re-layouts: 0.98 us -> 2.79 us  [corners(): by_role[:, half:]]
  transfers between devices with their start and end apart: 38 -> 40, of which waited for: 20 -> 20; matrix products, arithmetic and copies ran while one was open for 6% -> 13% of each run, Pallas kernels for 21% -> 15%
where the time goes in v7:
time: 171 us; the launch traced here: 170 us
  waiting for transfers between devices  68.5 us (40%)
  starting transfers between devices  43.5 us (25%)
  Pallas kernels  25 us (15%)
  local copies, waits for them, and re-layouts  16.5 us (10%)
  other arithmetic  14.6 us (9%)
  matrix products  1.87 us (1%)
    ppermute x40, waiting for transfers between devices, swap(): return lax.ppermute(block, axis, [(i, i ^ bits) for i in range(size)])  68.5 us
    ppermute x40, starting transfers between devices, swap(): return lax.ppermute(block, axis, [(i, i ^ bits) for i in range(size)])  43.5 us
    pallas_call x2, Pallas kernels, run_experts(): pl.pallas_call(lambda *refs: expert_kernel(first, spots, cuts, *refs), ou...  19 us
    unnamed x35, local copies, waits for them, and re-layouts  9.73 us
  transfers between devices with their start and end apart: 40, of which 20 were waited for; matrix products, arithmetic and copies ran while one was open for 13% of the time, Pallas kernels for 15%

profile of v7, /device:TPU:0, one launch (start us, length us, event | category | flops | bytes accessed | tf_op | source)
XLA Modules:
  0.0 170.4 jit_solution(3358783101256145637)
XLA Ops:
  0.5 2.4 %prepare.1 = (bf16[64,2048]{1,0:T(8,128)(2,1)S(1)}, bf16[64,640]{1,0:T(8,128)(2,1)S(1)}) custom-call(bf16[64,2048]{1,0:T(8,128)(2,1)} %bitcast.32, f32[1,2048]{1,0:T(1,128)} %bitcast.33, bf16[2,2048,256]{2,1,0:T(8,128)(2,1)} %refs_2_.1, f32[1,128]{1,0:T(1,128)} %bitcast.36, s32[8,64]{1,0:T(8,128)} %bitcast.34, s32[8,64]{1,0:T(8,128)} %bitcast.35), custom_call_target="tpu_custom_call" | custom-call | flops 134217728 | bytes 2621440 | tf_op jit(solution)/shard_map/prepare/pallas_call | solution.py:174
  2.9 4.7 %collective-permute-start.2 = (bf16[64,640]{1,0:T(8,128)(2,1)S(1)}, bf16[64,640]{1,0:T(8,128)(2,1)S(1)}, u32[]{:S(2)}, u32[]{:S(2)}) collective-permute-start(bf16[64,640]{1,0:T(8,128)(2,1)S(1)} %get-tuple-element.60), channel_id=1, source_target_pairs={{0,12},{4,8},{8,4},{12,0},{1,13},{5,9},{9,5},{13,1},{2,14},{6,10},... | collective-permute-start | bytes 245768 | tf_op jit(solution)/shard_map/ppermute | solution.py:25
  8.2 6.9 %collective-permute-done = bf16[64,640]{1,0:T(8,128)(2,1)S(1)} collective-permute-done((bf16[64,640]{1,0:T(8,128)(2,1)S(1)}, bf16[64,640]{1,0:T(8,128)(2,1)S(1)}, u32[]{:S(2)}, u32[]{:S(2)}) %collective-permute-start) | collective-permute-done | bytes 81952 | tf_op jit(solution)/shard_map/ppermute | solution.py:25
  15.1 1.5 collective-permute-start.3
  16.8 6.2 %collective-permute-done.3.second_ref = bf16[64,2048]{1,0:T(8,128)(2,1)S(1)} collective-permute-done((bf16[64,2048]{1,0:T(8,128)(2,1)S(1)}, bf16[64,2048]{1,0:T(8,128)(2,1)S(1)}, u32[]{:S(2)}, u32[]{:S(2)}) %collective-permute-start.3) | collective-permute-done | bytes 262176 | tf_op jit(solution)/shard_map/ppermute | solution.py:25
  23.0 1.5 collective-permute-start.6
  24.5 4.1 %collective-permute-done.6 = bf16[256,384]{1,0:T(8,128)(2,1)S(1)} collective-permute-done((bf16[256,384]{1,0:T(8,128)(2,1)S(1)}, bf16[256,384]{1,0:T(8,128)(2,1)S(1)}, u32[]{:S(2)}, u32[]{:S(2)}) %collective-permute-start.6) | collective-permute-done | bytes 196640 | tf_op jit(solution)/shard_map/ppermute | solution.py:25
  28.9 0.9 copy-done.7
  30.7 1.6 copy-done.11
  32.3 2.7 %attend.1 = (f32[128,2048]{1,0:T(8,128)S(1)}, f32[128,2048]{1,0:T(8,128)S(1)}) custom-call(bf16[256,512]{1,0:T(8,128)(2,1)S(1)} %queries.1.refs_0_, bf16[512,256]{1,0:T(8,128)(2,1)S(1)} %pad_maximum_fusion.2.refs_1_, bf16[512,256]{1,0:T(8,128)(2,1)S(1)} %collective-permute-done.7.refs_2_, bf16[512,2048]{1,0:T(8,128)(2,1)S(1)} %copy-done.11), custom_call_target="tpu_custom_call" | custom-call | flops 1073741824 | bytes 4194304 | tf_op jit(solution)/shard_map/attend/pallas_call | solution.py:253
  35.6 2.3 %collective-permute-done.8 = f32[128,2048]{1,0:T(8,128)S(1)} collective-permute-done((f32[128,2048]{1,0:T(8,128)S(1)}, f32[128,2048]{1,0:T(8,128)S(1)}, u32[]{:S(2)}, u32[]{:S(2)}) %collective-permute-start.8) | collective-permute-done | bytes 1048608 | tf_op jit(solution)/shard_map/ppermute | solution.py:25
  38.5 1.6 collective-permute-start.9
  40.1 1.5 collective-permute-start.10
  41.6 3.8 %collective-permute-done.10 = bf16[2,256,128]{2,1,0:T(8,128)(2,1)S(1)} collective-permute-done((bf16[2,256,128]{2,1,0:T(8,128)(2,1)S(1)}, bf16[2,256,128]{2,1,0:T(8,128)(2,1)S(1)}, u32[]{:S(2)}, u32[]{:S(2)}) %collective-permute-start.10) | collective-permute-done | bytes 131104 | tf_op jit(solution)/shard_map/ppermute | solution.py:25
  47.0 1.7 %copy-done.2 = bf16[768,2048]{1,0:T(8,128)(2,1)} copy-done((bf16[768,2048]{1,0:T(8,128)(2,1)}, bf16[768,2048]{1,0:T(8,128)(2,1)S(1)}, u32[]{:S(2)}) %copy-start.2) | copy-done | bytes 3145752
  49.0 1.8 %collective-permute-start.13 = (bf16[64,2048]{1,0:T(8,128)(2,1)S(1)}, bf16[64,2048]{1,0:T(8,128)(2,1)}, u32[]{:S(2)}, u32[]{:S(2)}) collective-permute-start(bf16[64,2048]{1,0:T(8,128)(2,1)S(1)} %multiply_convert_fusion.refs_13_), channel_id=1, source_target_pairs={{0,8},{4,12},{8,0},{12,4},{1,9},{5,13},{9,1},{13,5},{2,10},{6,14},... | collective-permute-start | bytes 786440 | tf_op jit(solution)/shard_map/ppermute | solution.py:25
  50.8 1.5 collective-permute-start.18
  52.3 1.5 collective-permute-start.15
  54.5 8.0 %collective-permute-done.13 = bf16[64,2048]{1,0:T(8,128)(2,1)} collective-permute-done((bf16[64,2048]{1,0:T(8,128)(2,1)S(1)}, bf16[64,2048]{1,0:T(8,128)(2,1)}, u32[]{:S(2)}, u32[]{:S(2)}) %collective-permute-start.13) | collective-permute-done | bytes 262176 | tf_op jit(solution)/shard_map/ppermute | solution.py:25
  63.0 0.9 slice.130
  64.0 1.6 collective-permute-start.19
  65.5 0.9 slice.129
  66.5 1.6 collective-permute-start.17
  68.0 1.9 %pad_maximum_fusion.refs_14_ = bf16[128,2048]{1,0:T(8,128)(2,1)} fusion(bf16[64,2048]{1,0:T(8,128)(2,1)} %collective-permute-done.16, bf16[64,2048]{1,0:T(8,128)(2,1)} %collective-permute-done.13), kind=kLoop, calls=%fused_computation.17 | loop fusion | flops 1048576 | bytes 1048576 | tf_op jit(solution)/shard_map/concatenate | solution.py:59
  69.9 1.7 collective-permute-done.17.refs_7_
  72.2 1.5 collective-permute-start.22
  74.3 1.0 slice_convert_fusion.2
  75.3 1.3 select_reduce_fusion.1
  76.6 1.1 reduce_or.18
  77.7 1.7 reduce_or.19
  79.4 1.0 fusion
  80.4 0.9 fusion.1
  82.1 1.0 iota_compare_fusion
  83.7 1.5 collective-permute-start.21
  85.2 1.0 copy.17.refs_2_
  86.3 1.1 add_convert_fusion.1.refs_0_
  87.4 1.1 add_convert_fusion.refs_1_
  88.5 2.4 %collective-permute-done.23.refs_12_ = bf16[64,2048]{1,0:T(8,128)(2,1)} collective-permute-done((bf16[64,2048]{1,0:T(8,128)(2,1)}, bf16[64,2048]{1,0:T(8,128)(2,1)}, u32[]{:S(2)}, u32[]{:S(2)}) %collective-permute-start.23) | collective-permute-done | bytes 262176 | tf_op jit(solution)/shard_map/ppermute | solution.py:25
  90.9 0.9 slice.134
  92.5 0.9 slice.133
  93.4 1.4 collective-permute-start.26
  94.9 1.0 slice.132
  95.8 1.6 collective-permute-start.25
  97.4 1.0 slice.131
  99.0 2.8 %copy-done = bf16[1,2048,1536]{2,1,0:T(8,128)(2,1)S(1)} copy-done((bf16[1,2048,1536]{2,1,0:T(8,128)(2,1)S(1)}, bf16[1,2048,1536]{2,1,0:T(8,128)(2,1)}, u32[]{:S(2)}) %copy-start) | copy-done | bytes 6291480
  101.8 1.9 %copy-done.3 = bf16[768,2048]{1,0:T(8,128)(2,1)S(1)} copy-done((bf16[768,2048]{1,0:T(8,128)(2,1)S(1)}, bf16[768,2048]{1,0:T(8,128)(2,1)}, u32[]{:S(2)}) %copy-start.3) | copy-done | bytes 3145752
  103.7 9.5 %experts.2 = (bf16[256,1024]{1,0:T(8,128)(2,1)S(1)}, bf16[256,1024]{1,0:T(8,128)(2,1)S(1)}, bf16[256,1024]{1,0:T(8,128)(2,1)S(1)}, bf16[256,1024]{1,0:T(8,128)(2,1)S(1)}) custom-call(bf16[4,224,256]{2,1,0:T(8,128)(2,1)S(1)} %add_convert_fusion.1.refs_0_, bf16[2,4,256,112]{3,2,1,0:T(8,128)(2,1)S(1)} %add_convert_fusion.refs_1_, f32[4,256,2]{2,1,0:T(8,128)S(1)} %copy-done.4, ...), custom_call_target="tpu_custom_call" | custom-call | flops 4227858432 | bytes 23068672 | tf_op jit(solution)/shard_map/experts/pallas_call | solution.py:375
  113.2 1.6 collective-permute-start.28
  115.3 9.5 %experts.3 = (bf16[128,1024]{1,0:T(8,128)(2,1)S(1)}, bf16[128,1024]{1,0:T(8,128)(2,1)S(1)}, bf16[128,1024]{1,0:T(8,128)(2,1)S(1)}, bf16[128,1024]{1,0:T(8,128)(2...) custom-call(bf16[4,224,256]{2,1,0:T(8,128)(2,1)S(1)} %add_convert_fusion.1.refs_0_, ...), custom_call_target="tpu_custom_call" | custom-call | flops 4227858432 | bytes 23068672 | tf_op jit(solution)/shard_map/experts/pallas_call | solution.py:375
  124.8 1.8 %collective-permute-done.29 = bf16[256,1024]{1,0:T(8,128)(2,1)S(1)} collective-permute-done((bf16[256,1024]{1,0:T(8,128)(2,1)S(1)}, bf16[256,1024]{1,0:T(8,128)(2,1)S(1)}, u32[]{:S(2)}, u32[]{:S(2)}) %collective-permute-start.29) | collective-permute-done | bytes 524320 | tf_op jit(solution)/shard_map/ppermute | solution.py:25
  126.9 1.7 collective-permute-start.34
  128.6 2.0 %collective-permute-start.35 = (bf16[128,1024]{1,0:T(8,128)(2,1)S(1)}, bf16[128,1024]{1,0:T(8,128)(2,1)S(1)}, u32[]{:S(2)}, u32[]{:S(2)}) collective-permute-start(bf16[128,1024]{1,0:T(8,128)(2,1)S(1)} %get-tuple-element.104), channel_id=1, source_target_pairs={{0,2},{1,3},{2,0},{3,1},{4,6},{5,7},{6,4},{7,5},{8,10},{9,11},{10,... | collective-permute-start | bytes 786440 | tf_op jit(solution)/shard_map/ppermute | solution.py:25
  130.6 4.4 %collective-permute-done.30 = bf16[128,1024]{1,0:T(8,128)(2,1)S(1)} collective-permute-done((bf16[128,1024]{1,0:T(8,128)(2,1)S(1)}, bf16[128,1024]{1,0:T(8,128)(2,1)S(1)}, u32[]{:S(2)}, u32[]{:S(2)}) %collective-permute-start.30) | collective-permute-done | bytes 262176 | tf_op jit(solution)/shard_map/ppermute | solution.py:25
  136.2 1.2 collective-permute-start.33
  137.4 1.2 collective-permute-done.34
  138.6 1.0 collective-permute-done.35
  139.6 4.8 %collective-permute-done.31 = bf16[128,1024]{1,0:T(8,128)(2,1)S(1)} collective-permute-done((bf16[128,1024]{1,0:T(8,128)(2,1)S(1)}, bf16[128,1024]{1,0:T(8,128)(2,1)S(1)}, u32[]{:S(2)}, u32[]{:S(2)}) %collective-permute-start.31) | collective-permute-done | bytes 262176 | tf_op jit(solution)/shard_map/ppermute | solution.py:25
  144.6 0.9 collective-permute-start.36
  145.5 1.7 collective-permute-start.37
  148.2 2.8 %collective-permute-done.36 = bf16[128,1024]{1,0:T(8,128)(2,1)S(1)} collective-permute-done((bf16[128,1024]{1,0:T(8,128)(2,1)S(1)}, bf16[128,1024]{1,0:T(8,128)(2,1)S(1)}, u32[]{:S(2)}, u32[]{:S(2)}) %collective-permute-start.36) | collective-permute-done | bytes 262176 | tf_op jit(solution)/shard_map/ppermute | solution.py:25
  151.0 0.9 collective-permute-done.37
  152.1 7.4 %collective-permute-done.38 = bf16[128,2048]{1,0:T(8,128)(2,1)S(1)} collective-permute-done((bf16[128,2048]{1,0:T(8,128)(2,1)S(1)}, bf16[128,2048]{1,0:T(8,128)(2,1)S(1)}, u32[]{:S(2)}, u32[]{:S(2)}) %collective-permute-start.38) | collective-permute-done | bytes 524320 | tf_op jit(solution)/shard_map/ppermute | solution.py:25
  159.7 2.3 %collective-permute-start.39 = (bf16[64,2048]{1,0:T(8,128)(2,1)S(1)}, bf16[64,2048]{1,0:T(8,128)(2,1)S(1)}, u32[]{:S(2)}, u32[]{:S(2)}) collective-permute-start(bf16[64,2048]{1,0:T(8,128)(2,1)S(1)} %slice.184), channel_id=1, source_target_pairs={{0,8},{4,12},{8,0},{12,4},{1,9},{5,13},{9,1},{13,5},{2,10},{6,14},... | collective-permute-start | bytes 786440 | tf_op jit(solution)/shard_map/ppermute | solution.py:25
  162.0 7.6 %collective-permute-done.39 = bf16[64,2048]{1,0:T(8,128)(2,1)S(1)} collective-permute-done((bf16[64,2048]{1,0:T(8,128)(2,1)S(1)}, bf16[64,2048]{1,0:T(8,128)(2,1)S(1)}, u32[]{:S(2)}, u32[]{:S(2)}) %collective-permute-start.39) | collective-permute-done | bytes 262176 | tf_op jit(solution)/shard_map/ppermute | solution.py:25
  (103 shorter events, 14.6 us)
Async XLA Ops:
  0.0 28.8 %copy-start.10 = (f32[128]{0:T(128)S(1)}, f32[128]{0:T(128)}, u32[]{:S(2)}) copy-start(f32[128]{0:T(128)} %param.16) | copy-start | bytes 1540
  0.0 48.7 %collective-permute-start.11 = (bf16[2048,1536]{1,0:T(8,128)(2,1)}, bf16[2048,1536]{1,0:T(8,128)(2,1)}, u32[]{:S(2)}, u32[]{:S(2)}) collective-permute-start(bf16[2048,1536]{1,0:T(8,128)(2,1)} %bitcast.25), channel_id=1, source_target_pairs={{0,1},{1,0},{2,3},{3,2},{4,5},{5,4},{6,7},{7,6},{8,9},{9,8},{10,11... | collective-permute-start | bytes 18874376 | tf_op jit(solution)/shard_map/ppermute | solution.py:25
  2.9 13.8 %collective-permute-start.2 = (bf16[64,640]{1,0:T(8,128)(2,1)S(1)}, bf16[64,640]{1,0:T(8,128)(2,1)S(1)}, u32[]{:S(2)}, u32[]{:S(2)}) collective-permute-start(bf16[64,640]{1,0:T(8,128)(2,1)S(1)} %get-tuple-element.60), channel_id=1, source_target_pairs={{0,12},{4,8},{8,4},{12,0},{1,13},{5,9},{9,5},{13,1},{2,14},{6,10},... | collective-permute-start | bytes 245768 | tf_op jit(solution)/shard_map/ppermute | solution.py:25
  7.6 9.1 %collective-permute-start.1 = (bf16[64,640]{1,0:T(8,128)(2,1)S(1)}, bf16[64,640]{1,0:T(8,128)(2,1)S(1)}, u32[]{:S(2)}, u32[]{:S(2)}) collective-permute-start(bf16[64,640]{1,0:T(8,128)(2,1)S(1)} %get-tuple-element.60), channel_id=1, source_target_pairs={{0,4},{4,0},{8,12},{12,8},{1,5},{5,1},{9,13},{13,9},{2,6},{6,2},{1... | collective-permute-start | bytes 245768 | tf_op jit(solution)/shard_map/ppermute | solution.py:25
  7.6 7.5 %collective-permute-start = (bf16[64,640]{1,0:T(8,128)(2,1)S(1)}, bf16[64,640]{1,0:T(8,128)(2,1)S(1)}, u32[]{:S(2)}, u32[]{:S(2)}) collective-permute-start(bf16[64,640]{1,0:T(8,128)(2,1)S(1)} %get-tuple-element.60), channel_id=1, source_target_pairs={{0,8},{4,12},{8,0},{12,4},{1,9},{5,13},{9,1},{13,5},{2,10},{6,14},... | collective-permute-start | bytes 245768 | tf_op jit(solution)/shard_map/ppermute | solution.py:25
  8.2 8.6 %collective-permute-start.4 = (bf16[64,2048]{1,0:T(8,128)(2,1)S(1)}, bf16[64,2048]{1,0:T(8,128)(2,1)S(1)}, u32[]{:S(2)}, u32[]{:S(2)}) collective-permute-start(bf16[64,2048]{1,0:T(8,128)(2,1)S(1)} %get-tuple-element.59.first_ref), channel_id=1, source_target_pairs={{0,1},{1,0},{2,3},{3,2},{4,5},{5,4},{6,7},{7,6},{8,9},{9,8},{10,11... | collective-permute-start | bytes 786440 | tf_op jit(solution)/shard_map/ppermute | solution.py:25
  8.2 20.6 %copy-start.5 = (bf16[2048,512]{1,0:T(8,128)(2,1)S(1)}, bf16[2048,512]{1,0:T(8,128)(2,1)}, u32[]{:S(2)}) copy-start(bf16[2048,512]{1,0:T(8,128)(2,1)} %weight_ref.1) | copy-start | bytes 6291460
  15.1 7.9 %collective-permute-start.3 = (bf16[64,2048]{1,0:T(8,128)(2,1)S(1)}, bf16[64,2048]{1,0:T(8,128)(2,1)S(1)}, u32[]{:S(2)}, u32[]{:S(2)}) collective-permute-start(bf16[64,2048]{1,0:T(8,128)(2,1)S(1)} %get-tuple-element.59.first_ref), channel_id=1, source_target_pairs={{0,2},{1,3},{2,0},{3,1},{4,6},{5,7},{6,4},{7,5},{8,10},{9,11},{10,... | collective-permute-start | bytes 786440 | tf_op jit(solution)/shard_map/ppermute | solution.py:25
  16.8 12.0 %copy-start.6 = (bf16[64,2048]{1,0:T(8,128)(2,1)}, bf16[64,2048]{1,0:T(8,128)(2,1)S(1)}, u32[]{:S(2)}) copy-start(bf16[64,2048]{1,0:T(8,128)(2,1)S(1)} %collective-permute-done.4.third_ref) | copy-start | bytes 786436
  23.0 5.7 %collective-permute-start.6 = (bf16[256,384]{1,0:T(8,128)(2,1)S(1)}, bf16[256,384]{1,0:T(8,128)(2,1)S(1)}, u32[]{:S(2)}, u32[]{:S(2)}) collective-permute-start(bf16[256,384]{1,0:T(8,128)(2,1)S(1)} %pad_maximum_fusion.4), channel_id=1, source_target_pairs={{0,2},{1,3},{2,0},{3,1},{4,6},{5,7},{6,4},{7,5},{8,10},{9,11},{10,... | collective-permute-start | bytes 589832 | tf_op jit(solution)/shard_map/ppermute | solution.py:25
  24.5 4.3 %collective-permute-start.5 = (bf16[64,2048]{1,0:T(8,128)(2,1)S(1)}, bf16[64,2048]{1,0:T(8,128)(2,1)S(1)}, u32[]{:S(2)}, u32[]{:S(2)}) collective-permute-start(bf16[64,2048]{1,0:T(8,128)(2,1)S(1)} %collective-permute-done.3.second_ref), channel_id=1, source_target_pairs={{0,1},{1,0},{2,3},{3,2},{4,5},{5,4},{6,7},{7,6},{8,9},{9,8},{10,11... | collective-permute-start | bytes 786440 | tf_op jit(solution)/shard_map/ppermute | solution.py:25
  28.7 1.9 %collective-permute-start.7 = (bf16[512,256]{1,0:T(8,128)(2,1)S(1)}, bf16[512,256]{1,0:T(8,128)(2,1)S(1)}, u32[]{:S(2)}, u32[]{:S(2)}) collective-permute-start(bf16[512,256]{1,0:T(8,128)(2,1)S(1)} %pad_maximum_fusion.2.refs_1_), channel_id=1, source_target_pairs={{0,1},{1,0},{2,3},{3,2},{4,5},{5,4},{6,7},{7,6},{8,9},{9,8},{10,11... | collective-permute-start | bytes 786440 | tf_op jit(solution)/shard_map/ppermute | solution.py:25
  28.8 1.0 copy-start.7
  29.8 8.1 %copy-start.1 = (bf16[1,768,2048]{2,1,0:T(8,128)(2,1)S(1)}, bf16[1,768,2048]{2,1,0:T(8,128)(2,1)}, u32[]{:S(2)}) copy-start(bf16[1,768,2048]{2,1,0:T(8,128)(2,1)} %param.23) | copy-start | bytes 9437188
  30.7 1.7 copy-start.11
  35.1 11.8 %copy-start.14 = (bf16[1,64,2048]{2,1,0:T(8,128)(2,1)S(1)}, bf16[1,64,2048]{2,1,0:T(8,128)(2,1)}, u32[]{:S(2)}) copy-start(bf16[1,64,2048]{2,1,0:T(8,128)(2,1)} %param.12) | copy-start | bytes 786436
  35.1 2.8 %collective-permute-start.8 = (f32[128,2048]{1,0:T(8,128)S(1)}, f32[128,2048]{1,0:T(8,128)S(1)}, u32[]{:S(2)}, u32[]{:S(2)}) collective-permute-start(f32[128,2048]{1,0:T(8,128)S(1)} %get-tuple-element.65), channel_id=1, source_target_pairs={{0,1},{1,0},{2,3},{3,2},{4,5},{5,4},{6,7},{7,6},{8,9},{9,8},{10,11... | collective-permute-start | bytes 3145736 | tf_op jit(solution)/shard_map/ppermute | solution.py:25
  37.9 9.1 %collective-permute-start.12 = (bf16[768,2048]{1,0:T(8,128)(2,1)S(1)}, bf16[768,2048]{1,0:T(8,128)(2,1)S(1)}, u32[]{:S(2)}, u32[]{:S(2)}) collective-permute-start(bf16[768,2048]{1,0:T(8,128)(2,1)S(1)} %bitcast.28), channel_id=1, source_target_pairs={{0,1},{1,0},{2,3},{3,2},{4,5},{5,4},{6,7},{7,6},{8,9},{9,8},{10,11... | collective-permute-start | bytes 9437192 | tf_op jit(solution)/shard_map/ppermute | solution.py:25
  38.3 10.6 %copy-start.15 = (f32[2048]{0:T(1024)S(1)}, f32[2048]{0:T(1024)}, u32[]{:S(2)}) copy-start(f32[2048]{0:T(1024)} %param.19) | copy-start | bytes 24580
  38.5 8.4 %collective-permute-start.9 = (bf16[64,2048]{1,0:T(8,128)(2,1)S(1)}, bf16[64,2048]{1,0:T(8,128)(2,1)S(1)}, u32[]{:S(2)}, u32[]{:S(2)}) collective-permute-start(bf16[64,2048]{1,0:T(8,128)(2,1)S(1)} %slice.185), channel_id=1, source_target_pairs={{0,2},{1,3},{2,0},{3,1},{4,6},{5,7},{6,4},{7,5},{8,10},{9,11},{10,... | collective-permute-start | bytes 786440 | tf_op jit(solution)/shard_map/ppermute | solution.py:25
  40.1 5.3 %collective-permute-start.10 = (bf16[2,256,128]{2,1,0:T(8,128)(2,1)S(1)}, bf16[2,256,128]{2,1,0:T(8,128)(2,1)S(1)}, u32[]{:S(2)}, u32[]{:S(2)}) collective-permute-start(bf16[2,256,128]{2,1,0:T(8,128)(2,1)S(1)} %pad_maximum_fusion.5), channel_id=1, source_target_pairs={{0,16},{16,0},{1,17},{17,1},{2,18},{18,2},{3,19},{19,3},{4,20},{20... | collective-permute-start | bytes 393224 | tf_op jit(solution)/shard_map/ppermute | solution.py:25
  47.0 15.5 %copy-start.12 = (f32[64,2048]{1,0:T(8,128)}, f32[64,2048]{1,0:T(8,128)S(1)}, u32[]{:S(2)}) copy-start(f32[64,2048]{1,0:T(8,128)S(1)} %fusion.5) | copy-start | bytes 1572868
  47.0 1.7 %copy-start.2 = (bf16[768,2048]{1,0:T(8,128)(2,1)}, bf16[768,2048]{1,0:T(8,128)(2,1)S(1)}, u32[]{:S(2)}) copy-start(bf16[768,2048]{1,0:T(8,128)(2,1)S(1)} %collective-permute-done.12.refs_6_) | copy-start | bytes 9437188
  49.0 13.5 %collective-permute-start.13 = (bf16[64,2048]{1,0:T(8,128)(2,1)S(1)}, bf16[64,2048]{1,0:T(8,128)(2,1)}, u32[]{:S(2)}, u32[]{:S(2)}) collective-permute-start(bf16[64,2048]{1,0:T(8,128)(2,1)S(1)} %multiply_convert_fusion.refs_13_), channel_id=1, source_target_pairs={{0,8},{4,12},{8,0},{12,4},{1,9},{5,13},{9,1},{13,5},{2,10},{6,14},... | collective-permute-start | bytes 786440 | tf_op jit(solution)/shard_map/ppermute | solution.py:25
  50.8 12.2 %collective-permute-start.18 = (bf16[64,2048]{1,0:T(8,128)(2,1)S(1)}, bf16[64,2048]{1,0:T(8,128)(2,1)}, u32[]{:S(2)}, u32[]{:S(2)}) collective-permute-start(bf16[64,2048]{1,0:T(8,128)(2,1)S(1)} %multiply_convert_fusion.refs_13_), channel_id=1, source_target_pairs={{0,16},{16,0},{1,17},{17,1},{2,18},{18,2},{3,19},{19,3},{4,20},{20... | collective-permute-start | bytes 786440 | tf_op jit(solution)/shard_map/ppermute | solution.py:25
  52.3 13.2 %collective-permute-start.15 = (bf16[64,2048]{1,0:T(8,128)(2,1)S(1)}, bf16[64,2048]{1,0:T(8,128)(2,1)}, u32[]{:S(2)}, u32[]{:S(2)}) collective-permute-start(bf16[64,2048]{1,0:T(8,128)(2,1)S(1)} %multiply_convert_fusion.refs_13_), channel_id=1, source_target_pairs={{0,2},{1,3},{2,0},{3,1},{4,6},{5,7},{6,4},{7,5},{8,10},{9,11},{10,... | collective-permute-start | bytes 786440 | tf_op jit(solution)/shard_map/ppermute | solution.py:25
  53.8 14.2 %collective-permute-start.16 = (bf16[64,2048]{1,0:T(8,128)(2,1)S(1)}, bf16[64,2048]{1,0:T(8,128)(2,1)}, u32[]{:S(2)}, u32[]{:S(2)}) collective-permute-start(bf16[64,2048]{1,0:T(8,128)(2,1)S(1)} %multiply_convert_fusion.refs_13_), channel_id=1, source_target_pairs={{0,4},{4,0},{8,12},{12,8},{1,5},{5,1},{9,13},{13,9},{2,6},{6,2},{1... | collective-permute-start | bytes 786440 | tf_op jit(solution)/shard_map/ppermute | solution.py:25
  62.5 11.8 %collective-permute-start.14 = (bf16[64,2048]{1,0:T(8,128)(2,1)}, bf16[64,2048]{1,0:T(8,128)(2,1)}, u32[]{:S(2)}, u32[]{:S(2)}) collective-permute-start(bf16[64,2048]{1,0:T(8,128)(2,1)} %collective-permute-done.13), channel_id=1, source_target_pairs={{0,4},{4,0},{8,12},{12,8},{1,5},{5,1},{9,13},{13,9},{2,6},{6,2},{1... | collective-permute-start | bytes 786440 | tf_op jit(solution)/shard_map/ppermute | solution.py:25
  64.0 5.9 %collective-permute-start.19 = (bf16[64,1024]{1,0:T(8,128)(2,1)S(1)}, bf16[64,1024]{1,0:T(8,128)(2,1)S(1)}, u32[]{:S(2)}, u32[]{:S(2)}) collective-permute-start(bf16[64,1024]{1,0:T(8,128)(2,1)S(1)} %slice.130), channel_id=1, source_target_pairs={{0,2},{1,3},{2,0},{3,1},{4,6},{5,7},{6,4},{7,5},{8,10},{9,11},{10,... | collective-permute-start | bytes 393224 | tf_op jit(solution)/shard_map/ppermute | solution.py:25
  66.5 5.1 %collective-permute-start.17 = (bf16[64,1024]{1,0:T(8,128)(2,1)S(1)}, bf16[64,1024]{1,0:T(8,128)(2,1)S(1)}, u32[]{:S(2)}, u32[]{:S(2)}) collective-permute-start(bf16[64,1024]{1,0:T(8,128)(2,1)S(1)} %slice.129), channel_id=1, source_target_pairs={{0,16},{16,0},{1,17},{17,1},{2,18},{18,2},{3,19},{19,3},{4,20},{20... | collective-permute-start | bytes 393224 | tf_op jit(solution)/shard_map/ppermute | solution.py:25
  71.6 0.6 copy-start.8
  72.2 22.6 %collective-permute-start.22 = (bf16[128,2048]{1,0:T(8,128)(2,1)}, bf16[128,2048]{1,0:T(8,128)(2,1)}, u32[]{:S(2)}, u32[]{:S(2)}) collective-permute-start(bf16[128,2048]{1,0:T(8,128)(2,1)} %pad_maximum_fusion.refs_14_), channel_id=1, source_target_pairs={{0,16},{16,0},{1,17},{17,1},{2,18},{18,2},{3,19},{19,3},{4,20},{20... | collective-permute-start | bytes 1572872 | tf_op jit(solution)/shard_map/ppermute | solution.py:25
  73.7 23.7 %collective-permute-start.20 = (bf16[128,2048]{1,0:T(8,128)(2,1)}, bf16[128,2048]{1,0:T(8,128)(2,1)}, u32[]{:S(2)}, u32[]{:S(2)}) collective-permute-start(bf16[128,2048]{1,0:T(8,128)(2,1)} %pad_maximum_fusion.refs_14_), channel_id=1, source_target_pairs={{0,2},{1,3},{2,0},{3,1},{4,6},{5,7},{6,4},{7,5},{8,10},{9,11},{10,... | collective-permute-start | bytes 1572872 | tf_op jit(solution)/shard_map/ppermute | solution.py:25
  83.2 7.7 %collective-permute-start.23 = (bf16[64,2048]{1,0:T(8,128)(2,1)}, bf16[64,2048]{1,0:T(8,128)(2,1)}, u32[]{:S(2)}, u32[]{:S(2)}) collective-permute-start(bf16[64,2048]{1,0:T(8,128)(2,1)} %collective-permute-done.14.refs_15_), channel_id=1, source_target_pairs={{0,16},{16,0},{1,17},{17,1},{2,18},{18,2},{3,19},{19,3},{4,20},{20... | collective-permute-start | bytes 786440 | tf_op jit(solution)/shard_map/ppermute | solution.py:25
  83.7 8.8 %collective-permute-start.21 = (bf16[64,2048]{1,0:T(8,128)(2,1)}, bf16[64,2048]{1,0:T(8,128)(2,1)}, u32[]{:S(2)}, u32[]{:S(2)}) collective-permute-start(bf16[64,2048]{1,0:T(8,128)(2,1)} %collective-permute-done.14.refs_15_), channel_id=1, source_target_pairs={{0,2},{1,3},{2,0},{3,1},{4,6},{5,7},{6,4},{7,5},{8,10},{9,11},{10,... | collective-permute-start | bytes 786440 | tf_op jit(solution)/shard_map/ppermute | solution.py:25
  86.3 12.7 %copy-start.4 = (f32[4,256,2]{2,1,0:T(8,128)S(1)}, f32[4,256,2]{2,1,0:T(8,128)}, u32[]{:S(2)}) copy-start(f32[4,256,2]{2,1,0:T(8,128)} %copy.17.refs_2_) | copy-start | bytes 24580
  91.8 21.4 %collective-permute-start.27 = (bf16[64,1024]{1,0:T(8,128)(2,1)S(1)}, bf16[64,1024]{1,0:T(8,128)(2,1)S(1)}, u32[]{:S(2)}, u32[]{:S(2)}) collective-permute-start(bf16[64,1024]{1,0:T(8,128)(2,1)S(1)} %slice.134), channel_id=1, source_target_pairs={{0,2},{1,3},{2,0},{3,1},{4,6},{5,7},{6,4},{7,5},{8,10},{9,11},{10,... | collective-permute-start | bytes 393224 | tf_op jit(solution)/shard_map/ppermute | solution.py:25
  93.4 19.7 %collective-permute-start.26 = (bf16[64,1024]{1,0:T(8,128)(2,1)S(1)}, bf16[64,1024]{1,0:T(8,128)(2,1)S(1)}, u32[]{:S(2)}, u32[]{:S(2)}) collective-permute-start(bf16[64,1024]{1,0:T(8,128)(2,1)S(1)} %slice.133), channel_id=1, source_target_pairs={{0,16},{16,0},{1,17},{17,1},{2,18},{18,2},{3,19},{19,3},{4,20},{20... | collective-permute-start | bytes 393224 | tf_op jit(solution)/shard_map/ppermute | solution.py:25
  95.8 17.3 %collective-permute-start.25 = (bf16[128,1024]{1,0:T(8,128)(2,1)S(1)}, bf16[128,1024]{1,0:T(8,128)(2,1)S(1)}, u32[]{:S(2)}, u32[]{:S(2)}) collective-permute-start(bf16[128,1024]{1,0:T(8,128)(2,1)S(1)} %slice.132), channel_id=1, source_target_pairs={{0,2},{1,3},{2,0},{3,1},{4,6},{5,7},{6,4},{7,5},{8,10},{9,11},{10,... | collective-permute-start | bytes 786440 | tf_op jit(solution)/shard_map/ppermute | solution.py:25
  98.4 14.8 %collective-permute-start.24 = (bf16[128,1024]{1,0:T(8,128)(2,1)S(1)}, bf16[128,1024]{1,0:T(8,128)(2,1)S(1)}, u32[]{:S(2)}, u32[]{:S(2)}) collective-permute-start(bf16[128,1024]{1,0:T(8,128)(2,1)S(1)} %slice.131), channel_id=1, source_target_pairs={{0,16},{16,0},{1,17},{17,1},{2,18},{18,2},{3,19},{19,3},{4,20},{20... | collective-permute-start | bytes 786440 | tf_op jit(solution)/shard_map/ppermute | solution.py:25
  99.0 2.8 %copy-start = (bf16[1,2048,1536]{2,1,0:T(8,128)(2,1)S(1)}, bf16[1,2048,1536]{2,1,0:T(8,128)(2,1)}, u32[]{:S(2)}) copy-start(bf16[1,2048,1536]{2,1,0:T(8,128)(2,1)} %param.22) | copy-start | bytes 18874372
  101.8 1.9 %copy-start.3 = (bf16[768,2048]{1,0:T(8,128)(2,1)S(1)}, bf16[768,2048]{1,0:T(8,128)(2,1)}, u32[]{:S(2)}) copy-start(bf16[768,2048]{1,0:T(8,128)(2,1)} %copy-done.2) | copy-start | bytes 9437188
  103.7 11.6 %copy-start.9 = (bf16[64,1024]{1,0:T(8,128)(2,1)S(1)}, bf16[64,1024]{1,0:T(8,128)(2,1)}, u32[]{:S(2)}) copy-start(bf16[64,1024]{1,0:T(8,128)(2,1)} %copy-done.8) | copy-start | bytes 393220
  113.2 11.6 %collective-permute-start.28 = (bf16[256,1024]{1,0:T(8,128)(2,1)S(1)}, bf16[256,1024]{1,0:T(8,128)(2,1)S(1)}, u32[]{:S(2)}, u32[]{:S(2)}) collective-permute-start(bf16[256,1024]{1,0:T(8,128)(2,1)S(1)} %get-tuple-element.83), channel_id=1, source_target_pairs={{0,16},{16,0},{1,17},{17,1},{2,18},{18,2},{3,19},{19,3},{4,20},{20... | collective-permute-start | bytes 1572872 | tf_op jit(solution)/shard_map/ppermute | solution.py:25
  114.8 11.8 %collective-permute-start.29 = (bf16[256,1024]{1,0:T(8,128)(2,1)S(1)}, bf16[256,1024]{1,0:T(8,128)(2,1)S(1)}, u32[]{:S(2)}, u32[]{:S(2)}) collective-permute-start(bf16[256,1024]{1,0:T(8,128)(2,1)S(1)} %get-tuple-element.84), channel_id=1, source_target_pairs={{0,2},{1,3},{2,0},{3,1},{4,6},{5,7},{6,4},{7,5},{8,10},{9,11},{10,... | collective-permute-start | bytes 1572872 | tf_op jit(solution)/shard_map/ppermute | solution.py:25
  126.6 8.5 %collective-permute-start.30 = (bf16[128,1024]{1,0:T(8,128)(2,1)S(1)}, bf16[128,1024]{1,0:T(8,128)(2,1)S(1)}, u32[]{:S(2)}, u32[]{:S(2)}) collective-permute-start(bf16[128,1024]{1,0:T(8,128)(2,1)S(1)} %get-tuple-element.100), channel_id=1, source_target_pairs={{0,16},{16,0},{1,17},{17,1},{2,18},{18,2},{3,19},{19,3},{4,20},{20... | collective-permute-start | bytes 786440 | tf_op jit(solution)/shard_map/ppermute | solution.py:25
  126.9 9.2 %collective-permute-start.32 = (bf16[128,1024]{1,0:T(8,128)(2,1)S(1)}, bf16[128,1024]{1,0:T(8,128)(2,1)S(1)}, u32[]{:S(2)}, u32[]{:S(2)}) collective-permute-start(bf16[128,1024]{1,0:T(8,128)(2,1)S(1)} %get-tuple-element.102), channel_id=1, source_target_pairs={{0,2},{1,3},{2,0},{3,1},{4,6},{5,7},{6,4},{7,5},{8,10},{9,11},{10,... | collective-permute-start | bytes 786440 | tf_op jit(solution)/shard_map/ppermute | solution.py:25
  126.9 11.6 %collective-permute-start.34 = (bf16[128,1024]{1,0:T(8,128)(2,1)S(1)}, bf16[128,1024]{1,0:T(8,128)(2,1)S(1)}, u32[]{:S(2)}, u32[]{:S(2)}) collective-permute-start(bf16[128,1024]{1,0:T(8,128)(2,1)S(1)} %get-tuple-element.103), channel_id=1, source_target_pairs={{0,16},{16,0},{1,17},{17,1},{2,18},{18,2},{3,19},{19,3},{4,20},{20... | collective-permute-start | bytes 786440 | tf_op jit(solution)/shard_map/ppermute | solution.py:25
  128.6 11.0 %collective-permute-start.35 = (bf16[128,1024]{1,0:T(8,128)(2,1)S(1)}, bf16[128,1024]{1,0:T(8,128)(2,1)S(1)}, u32[]{:S(2)}, u32[]{:S(2)}) collective-permute-start(bf16[128,1024]{1,0:T(8,128)(2,1)S(1)} %get-tuple-element.104), channel_id=1, source_target_pairs={{0,2},{1,3},{2,0},{3,1},{4,6},{5,7},{6,4},{7,5},{8,10},{9,11},{10,... | collective-permute-start | bytes 786440 | tf_op jit(solution)/shard_map/ppermute | solution.py:25
  135.1 9.2 %collective-permute-start.31 = (bf16[128,1024]{1,0:T(8,128)(2,1)S(1)}, bf16[128,1024]{1,0:T(8,128)(2,1)S(1)}, u32[]{:S(2)}, u32[]{:S(2)}) collective-permute-start(bf16[128,1024]{1,0:T(8,128)(2,1)S(1)} %add_convert_fusion.7), channel_id=1, source_target_pairs={{0,2},{1,3},{2,0},{3,1},{4,6},{5,7},{6,4},{7,5},{8,10},{9,11},{10,... | collective-permute-start | bytes 786440 | tf_op jit(solution)/shard_map/ppermute | solution.py:25
  136.2 8.2 %collective-permute-start.33 = (bf16[128,1024]{1,0:T(8,128)(2,1)S(1)}, bf16[128,1024]{1,0:T(8,128)(2,1)S(1)}, u32[]{:S(2)}, u32[]{:S(2)}) collective-permute-start(bf16[128,1024]{1,0:T(8,128)(2,1)S(1)} %add_convert_fusion.6), channel_id=1, source_target_pairs={{0,16},{16,0},{1,17},{17,1},{2,18},{18,2},{3,19},{19,3},{4,20},{20... | collective-permute-start | bytes 786440 | tf_op jit(solution)/shard_map/ppermute | solution.py:25
  144.6 6.4 %collective-permute-start.36 = (bf16[128,1024]{1,0:T(8,128)(2,1)S(1)}, bf16[128,1024]{1,0:T(8,128)(2,1)S(1)}, u32[]{:S(2)}, u32[]{:S(2)}) collective-permute-start(bf16[128,1024]{1,0:T(8,128)(2,1)S(1)} %add_convert_fusion.5), channel_id=1, source_target_pairs={{0,2},{1,3},{2,0},{3,1},{4,6},{5,7},{6,4},{7,5},{8,10},{9,11},{10,... | collective-permute-start | bytes 786440 | tf_op jit(solution)/shard_map/ppermute | solution.py:25
  145.5 6.4 %collective-permute-start.37 = (bf16[128,1024]{1,0:T(8,128)(2,1)S(1)}, bf16[128,1024]{1,0:T(8,128)(2,1)S(1)}, u32[]{:S(2)}, u32[]{:S(2)}) collective-permute-start(bf16[128,1024]{1,0:T(8,128)(2,1)S(1)} %add_convert_fusion.4), channel_id=1, source_target_pairs={{0,16},{16,0},{1,17},{17,1},{2,18},{18,2},{3,19},{19,3},{4,20},{20... | collective-permute-start | bytes 786440 | tf_op jit(solution)/shard_map/ppermute | solution.py:25
  147.5 22.2 %copy-start.13 = (f32[64,2048]{1,0:T(8,128)S(1)}, f32[64,2048]{1,0:T(8,128)}, u32[]{:S(2)}) copy-start(f32[64,2048]{1,0:T(8,128)} %copy-done.12) | copy-start | bytes 1572868
  147.5 12.1 %collective-permute-start.38 = (bf16[128,2048]{1,0:T(8,128)(2,1)S(1)}, bf16[128,2048]{1,0:T(8,128)(2,1)S(1)}, u32[]{:S(2)}, u32[]{:S(2)}) collective-permute-start(bf16[128,2048]{1,0:T(8,128)(2,1)S(1)} %pad_maximum_fusion.1), channel_id=1, source_target_pairs={{0,4},{4,0},{8,12},{12,8},{1,5},{5,1},{9,13},{13,9},{2,6},{6,2},{1... | collective-permute-start | bytes 1572872 | tf_op jit(solution)/shard_map/ppermute | solution.py:25
  159.7 10.0 %collective-permute-start.39 = (bf16[64,2048]{1,0:T(8,128)(2,1)S(1)}, bf16[64,2048]{1,0:T(8,128)(2,1)S(1)}, u32[]{:S(2)}, u32[]{:S(2)}) collective-permute-start(bf16[64,2048]{1,0:T(8,128)(2,1)S(1)} %slice.184), channel_id=1, source_target_pairs={{0,8},{4,12},{8,0},{12,4},{1,9},{5,13},{9,1},{13,5},{2,10},{6,14},... | collective-permute-start | bytes 786440 | tf_op jit(solution)/shard_map/ppermute | solution.py:25

commit v8 on v7

--- a/solution.py
+++ b/solution.py
@@ -264,6 +264,76 @@
     )(queries, near_kv, far_kv, w_out)
 
 
+def tables_kernel(top_count, expert_ref, coded_ref, pick_ref, place_ref, share_ref):
+    groups, rows, lanes = coded_ref.shape
+    slots = place_ref.shape[3]
+    lane = lax.broadcasted_iota(jnp.int32, (rows, lanes), 1)
+    source = lax.broadcasted_iota(jnp.int32, (lanes, lanes), 0)
+    target = lax.broadcasted_iota(jnp.int32, (lanes, lanes), 1)
+    joined = jnp.where(source == target + top_count, 64.0, 0.0)
+    joined = joined + jnp.where(source == target + 2 * top_count, 1.0, 0.0)
+    joined = jnp.where(target < top_count, joined, 0.0).astype(jnp.bfloat16)
+    first = lax.broadcasted_iota(jnp.int32, (rows, rows), 0)
+    second = lax.broadcasted_iota(jnp.int32, (rows, rows), 1)
+    later = jnp.where(first < second, 1.0, 0.0).astype(jnp.bfloat16)
+    earlier = jnp.where(second < first, 1.0, 0.0).astype(jnp.bfloat16)
+    ones = jnp.ones((8, lanes), jnp.bfloat16)
+    slot_row = lax.broadcasted_iota(jnp.int32, (slots, rows), 0).astype(jnp.float32)
+    slot_lane = lax.broadcasted_iota(jnp.int32, (rows, slots), 1).astype(jnp.float32)
+    for group in range(groups):
+        coded = coded_ref[group]
+        gates = jnp.dot(coded, joined, preferred_element_type=jnp.float32)
+        gate_sum = jnp.sum(gates, axis=1, keepdims=True)
+        named = coded.astype(jnp.float32).astype(jnp.int32)
+        for number in range(2):
+            expert = expert_ref[0] ^ (number * PAIR)
+            hits = jnp.where((named == expert) & (lane < top_count), 1.0, 0.0)
+            share_ref[group, :, number : number + 1] = (
+                jnp.sum(hits * gates, axis=1, keepdims=True) / gate_sum
+            )
+            hit = jnp.sum(hits, axis=1, keepdims=True)
+            held = jnp.broadcast_to(hit, (rows, lanes)).astype(jnp.bfloat16)
+            rank = jnp.dot(earlier, held, preferred_element_type=jnp.float32)[:, :1]
+            rank = jnp.where(hit > 0.0, rank, -1.0)
+            place_ref[number, group] = jnp.where(rank == slot_lane, 1.0, 0.0).astype(jnp.bfloat16)
+            hit_row = lax.dot_general(
+                ones,
+                hits.astype(jnp.bfloat16),
+                (((1,), (1,)), ((), ())),
+                preferred_element_type=jnp.float32,
+            )
+            rank_row = jnp.dot(
+                hit_row.astype(jnp.bfloat16), later, preferred_element_type=jnp.float32
+            )
+            rank_row = jnp.where(hit_row > 0.0, rank_row, -1.0)[:1]
+            pick_ref[group, number * slots : (number + 1) * slots] = jnp.where(
+                rank_row == slot_row, 1.0, 0.0
+            ).astype(jnp.bfloat16)
+
+
+def make_tables(coded, expert, slots, top_count):
+    groups, rows, lanes = coded.shape
+    return pl.pallas_call(
+        lambda *refs: tables_kernel(top_count, *refs),
+        out_shape=[
+            jax.ShapeDtypeStruct((groups, 2 * slots, rows), jnp.bfloat16),
+            jax.ShapeDtypeStruct((2, groups, rows, slots), jnp.bfloat16),
+            jax.ShapeDtypeStruct((groups, rows, 2), jnp.float32),
+        ],
+        in_specs=[
+            pl.BlockSpec(memory_space=pltpu.SMEM),
+            pl.BlockSpec(memory_space=pltpu.VMEM),
+        ],
+        compiler_params=pltpu.CompilerParams(vmem_limit_bytes=24 * 1024 * 1024),
+        cost_estimate=pl.CostEstimate(
+            flops=4 * groups * rows * rows * lanes,
+            bytes_accessed=8 * groups * rows * slots,
+            transcendentals=0,
+        ),
+        name="tables",
+    )(expert.astype(jnp.int32)[None], coded)
+
+
 def expert_kernel(first, spots, cuts, *refs):
     pick_ref, place_ref, share_ref, own_gu_ref, far_gu_ref, own_dn_ref, far_dn_ref = refs[:7]
     group_rows, slots = place_ref.shape[2:]
@@ -371,6 +441,7 @@
     ]
     arrays = [array for held in pieces for _, _, array in held]
     anywhere = pl.BlockSpec(memory_space=pl.ANY)
+    stored = pl.BlockSpec(memory_space=pltpu.HBM)
     inside = pl.BlockSpec(memory_space=pltpu.VMEM)
     outs = pl.pallas_call(
         lambda *refs: expert_kernel(first, spots, cuts, *refs),
@@ -379,7 +450,7 @@
             for cut in cuts
             for _ in range(2 * cut)
         ],
-        in_specs=[inside] * 3 + [anywhere] * (4 + len(arrays)),
+        in_specs=[inside] * 3 + [stored] * 4 + [anywhere] * len(arrays),
         out_specs=[anywhere] * (2 * sum(cuts)),
         scratch_shapes=[
             pltpu.VMEM((groups, group_rows, width), jnp.bfloat16),
@@ -472,30 +543,13 @@
     moe_in = rms_rows(mixed, moe_gain).astype(jnp.bfloat16)
 
     rows, coded = spread_rows(moe_in, coded)
-    coded = coded[:, :, : 3 * top_count].astype(jnp.int32)
-    routes = coded[:, :, :top_count]
-    gates = coded[:, :, top_count : 2 * top_count] * 64 + coded[:, :, 2 * top_count :]
-    gates = gates.astype(jnp.float32)
-    groups, group_rows = routes.shape[:2]
     capacity = max(2, 7 * row_count * top_count // (4 * expert_count))
-    slots = -(-capacity * (group_rows // row_count) // 16) * 16
-    gate_sum = jnp.sum(gates, axis=2)
-    earlier = jnp.tri(group_rows, k=-1, dtype=jnp.bfloat16)
-    picks, shares = [], []
-    for expert in (lax.axis_index(EVERY), lax.axis_index(EVERY) ^ PAIR):
-        named = routes == expert
-        hit = jnp.any(named, axis=2)
-        shares.append(jnp.sum(jnp.where(named, gates, 0.0), axis=2) / gate_sum)
-        rank = jnp.einsum(
-            "ij,gj->gi", earlier, hit.astype(jnp.bfloat16), preferred_element_type=jnp.float32
-        )
-        rank = jnp.where(hit, rank.astype(jnp.int32), -1)
-        picks.append((rank[:, None, :] == jnp.arange(slots)[None, :, None]).astype(jnp.bfloat16))
-    pick = jnp.concatenate(picks, axis=1)
-    place = jnp.stack([jnp.swapaxes(one, 1, 2) for one in picks])
-    share = jnp.stack(shares, axis=2)
-
-    weights = (w_gateup[0], far_gu, w_down[0], far_dn)
+    slots = -(-capacity * (coded.shape[1] // row_count) // 16) * 16
+    pick, place, share = make_tables(coded, lax.axis_index(EVERY), slots, top_count)
+    weights = [
+        pltpu.with_memory_space_constraint(one, pltpu.HBM)
+        for one in (w_gateup[0], far_gu, w_down[0], far_dn)
+    ]
 
     tables = (pick, place, share, weights)
     by_rep, by_role = run_experts(0, rows[:2], (1, 1), *tables)

time: 171 us -> 152 us (0.89)
  local copies, waits for them, and re-layouts: 16.5 us -> 1.6 us
  other arithmetic: 14.6 us -> 2.27 us
  waiting for transfers between devices: 68.5 us -> 78.8 us
  Pallas kernels: 25 us -> 27 us
  matrix products: 1.87 us -> 0 us
    ppermute x40, waiting for transfers between devices: 68.5 us -> 78.8 us  [swap(): return lax.ppermute(block, axis, [(i, i ^ bits) for i in range(size)])]
    unnamed x35 -> x25, local copies, waits for them, and re-layouts: 9.73 us -> 1.37 us
    reduce_or x2 -> x0, other arithmetic: 2.81 us -> none  [per_device(): hit = jnp.any(named, axis=2)]
    slice x3, local copies, waits for them, and re-layouts: 2.8 us -> 0.04 us  [corners(): by_rep[:, :half]]
    slice x3, local copies, waits for them, and re-layouts: 2.79 us -> 0.04 us  [corners(): by_role[:, half:]]
    eq x2 -> x0, other arithmetic: 1.88 us -> none  [per_device(): rank[:, None, :] == jnp.arange(slots)[None, :, None]]
    dot_general x2 -> x0, matrix products: 1.87 us -> none  [per_device(): jnp.einsum('ij,gj->gi', earlier, hit.astype(jnp.bfloat16), preferred_elem...]
    concatenate x1, other arithmetic: 1.87 us -> 0.04 us  [spread_rows(): middle = jnp.concatenate(blocks[1:] + beyond[:-1], axis=0)]
  transfers between devices with their start and end apart: 40 -> 40, of which waited for: 20 -> 21; matrix products, arithmetic and copies ran while one was open for 13% -> 1% of each run, Pallas kernels for 15% -> 18%
where the time goes in v8:
time: 152 us
  waiting for transfers between devices  78.8 us (52%)
  starting transfers between devices  41.9 us (28%)
  Pallas kernels  27 us (18%)
  other arithmetic  2.27 us (1%)
  local copies, waits for them, and re-layouts  1.6 us (1%)
    ppermute x40, waiting for transfers between devices, swap(): return lax.ppermute(block, axis, [(i, i ^ bits) for i in range(size)])  78.8 us
    ppermute x40, starting transfers between devices, swap(): return lax.ppermute(block, axis, [(i, i ^ bits) for i in range(size)])  41.9 us
    pallas_call x2, Pallas kernels, run_experts(): pl.pallas_call(lambda *refs: expert_kernel(first, spots, cuts, *refs), ou...  19.2 us
  transfers between devices with their start and end apart: 40, of which 21 were waited for; matrix products, arithmetic and copies ran while one was open for 1% of the time, Pallas kernels for 18%

profile of v8, /device:TPU:0, one launch (start us, length us, event | category | flops | bytes accessed | tf_op | source)
XLA Modules:
  0.0 152.0 jit_solution(5215514257306247274)
XLA Ops:
  0.0 0.5 collective-permute-start.11
  0.5 2.6 %prepare.1 = (bf16[64,2048]{1,0:T(8,128)(2,1)S(1)}, bf16[64,640]{1,0:T(8,128)(2,1)S(1)}) custom-call(bf16[64,2048]{1,0:T(8,128)(2,1)} %bitcast.27, f32[1,2048]{1,0:T(1,128)} %bitcast.28, bf16[2,2048,256]{2,1,0:T(8,128)(2,1)} %refs_2_.1, f32[1,128]{1,0:T(1,128)} %bitcast.31, s32[8,64]{1,0:T(8,128)} %bitcast.29, s32[8,64]{1,0:T(8,128)} %bitcast.30), custom_call_target="tpu_custom_call" | custom-call | flops 134217728 | bytes 2621440 | tf_op jit(solution)/shard_map/prepare/pallas_call | solution.py:174
  3.1 4.7 %collective-permute-start.2 = (bf16[64,640]{1,0:T(8,128)(2,1)S(1)}, bf16[64,640]{1,0:T(8,128)(2,1)S(1)}, u32[]{:S(2)}, u32[]{:S(2)}) collective-permute-start(bf16[64,640]{1,0:T(8,128)(2,1)S(1)} %get-tuple-element.63), channel_id=1, source_target_pairs={{0,12},{4,8},{8,4},{12,0},{1,13},{5,9},{9,5},{13,1},{2,14},{6,10},... | collective-permute-start | bytes 245768 | tf_op jit(solution)/shard_map/ppermute | solution.py:25
  7.7 0.6 collective-permute-start
  8.4 6.7 %collective-permute-done = bf16[64,640]{1,0:T(8,128)(2,1)S(1)} collective-permute-done((bf16[64,640]{1,0:T(8,128)(2,1)S(1)}, bf16[64,640]{1,0:T(8,128)(2,1)S(1)}, u32[]{:S(2)}, u32[]{:S(2)}) %collective-permute-start) | collective-permute-done | bytes 81952 | tf_op jit(solution)/shard_map/ppermute | solution.py:25
  15.1 1.5 collective-permute-start.3
  16.8 5.1 %collective-permute-done.3.second_ref = bf16[64,2048]{1,0:T(8,128)(2,1)S(1)} collective-permute-done((bf16[64,2048]{1,0:T(8,128)(2,1)S(1)}, bf16[64,2048]{1,0:T(8,128)(2,1)S(1)}, u32[]{:S(2)}, u32[]{:S(2)}) %collective-permute-start.3) | collective-permute-done | bytes 262176 | tf_op jit(solution)/shard_map/ppermute | solution.py:25
  22.0 1.5 collective-permute-start.6
  23.5 4.1 %collective-permute-done.6 = bf16[256,384]{1,0:T(8,128)(2,1)S(1)} collective-permute-done((bf16[256,384]{1,0:T(8,128)(2,1)S(1)}, bf16[256,384]{1,0:T(8,128)(2,1)S(1)}, u32[]{:S(2)}, u32[]{:S(2)}) %collective-permute-start.6) | collective-permute-done | bytes 196640 | tf_op jit(solution)/shard_map/ppermute | solution.py:25
  27.8 0.9 queries.1.refs_0_
  28.7 0.6 collective-permute-done.7.refs_2_
  29.3 2.7 %attend.1 = (f32[128,2048]{1,0:T(8,128)S(1)}, f32[128,2048]{1,0:T(8,128)S(1)}) custom-call(bf16[256,512]{1,0:T(8,128)(2,1)S(1)} %queries.1.refs_0_, bf16[512,256]{1,0:T(8,128)(2,1)S(1)} %pad_maximum_fusion.2.refs_1_, bf16[512,256]{1,0:T(8,128)(2,1)S(1)} %collective-permute-done.7.refs_2_, bf16[512,2048]{1,0:T(8,128)(2,1)S(1)} %copy-done.4), custom_call_target="tpu_custom_call" | custom-call | flops 1073741824 | bytes 4194304 | tf_op jit(solution)/shard_map/attend/pallas_call | solution.py:253
  32.0 0.2 collective-permute-start.8
  32.2 2.5 %collective-permute-done.8 = f32[128,2048]{1,0:T(8,128)S(1)} collective-permute-done((f32[128,2048]{1,0:T(8,128)S(1)}, f32[128,2048]{1,0:T(8,128)S(1)}, u32[]{:S(2)}, u32[]{:S(2)}) %collective-permute-start.8) | collective-permute-done | bytes 1048608 | tf_op jit(solution)/shard_map/ppermute | solution.py:25
  35.1 1.6 %collective-permute-start.9 = (bf16[64,2048]{1,0:T(8,128)(2,1)S(1)}, bf16[64,2048]{1,0:T(8,128)(2,1)S(1)}, u32[]{:S(2)}, u32[]{:S(2)}) collective-permute-start(bf16[64,2048]{1,0:T(8,128)(2,1)S(1)} %slice.145), channel_id=1, source_target_pairs={{0,2},{1,3},{2,0},{3,1},{4,6},{5,7},{6,4},{7,5},{8,10},{9,11},{10,... | collective-permute-start | bytes 786440 | tf_op jit(solution)/shard_map/ppermute | solution.py:25
  36.7 1.6 %collective-permute-start.10 = (bf16[2,256,128]{2,1,0:T(8,128)(2,1)S(1)}, bf16[2,256,128]{2,1,0:T(8,128)(2,1)S(1)}, u32[]{:S(2)}, u32[]{:S(2)}) collective-permute-start(bf16[2,256,128]{2,1,0:T(8,128)(2,1)S(1)} %pad_maximum_fusion.5), channel_id=1, source_target_pairs={{0,16},{16,0},{1,17},{17,1},{2,18},{18,2},{3,19},{19,3},{4,20},{20... | collective-permute-start | bytes 393224 | tf_op jit(solution)/shard_map/ppermute | solution.py:25
  38.2 4.0 %collective-permute-done.10 = bf16[2,256,128]{2,1,0:T(8,128)(2,1)S(1)} collective-permute-done((bf16[2,256,128]{2,1,0:T(8,128)(2,1)S(1)}, bf16[2,256,128]{2,1,0:T(8,128)(2,1)S(1)}, u32[]{:S(2)}, u32[]{:S(2)}) %collective-permute-start.10) | collective-permute-done | bytes 131104 | tf_op jit(solution)/shard_map/ppermute | solution.py:25
  42.2 1.5 collective-permute-done.9
  43.8 0.1 multiply_reduce_fusion
  44.0 0.6 copy-done.7
  44.7 1.6 %collective-permute-start.18 = (bf16[64,2048]{1,0:T(8,128)(2,1)S(1)}, bf16[64,2048]{1,0:T(8,128)(2,1)S(1)}, u32[]{:S(2)}, u32[]{:S(2)}) collective-permute-start(bf16[64,2048]{1,0:T(8,128)(2,1)S(1)} %multiply_convert_fusion.refs_13_), channel_id=1, source_target_pairs={{0,16},{16,0},{1,17},{17,1},{2,18},{18,2},{3,19},{19,3},{4,20},{20... | collective-permute-start | bytes 786440 | tf_op jit(solution)/shard_map/ppermute | solution.py:25
  46.3 1.5 %collective-permute-start.15 = (bf16[64,2048]{1,0:T(8,128)(2,1)S(1)}, bf16[64,2048]{1,0:T(8,128)(2,1)S(1)}, u32[]{:S(2)}, u32[]{:S(2)}) collective-permute-start(bf16[64,2048]{1,0:T(8,128)(2,1)S(1)} %multiply_convert_fusion.refs_13_), channel_id=1, source_target_pairs={{0,2},{1,3},{2,0},{3,1},{4,6},{5,7},{6,4},{7,5},{8,10},{9,11},{10,... | collective-permute-start | bytes 786440 | tf_op jit(solution)/shard_map/ppermute | solution.py:25
  47.8 2.6 %collective-permute-start.13 = (bf16[64,2048]{1,0:T(8,128)(2,1)S(1)}, bf16[64,2048]{1,0:T(8,128)(2,1)S(1)}, u32[]{:S(2)}, u32[]{:S(2)}) collective-permute-start(bf16[64,2048]{1,0:T(8,128)(2,1)S(1)} %multiply_convert_fusion.refs_13_), channel_id=1, source_target_pairs={{0,8},{4,12},{8,0},{12,4},{1,9},{5,13},{9,1},{13,5},{2,10},{6,14},... | collective-permute-start | bytes 786440 | tf_op jit(solution)/shard_map/ppermute | solution.py:25
  50.4 0.9 collective-permute-start.16
  51.3 1.2 collective-permute-done.18.refs_10_
  52.6 1.6 %collective-permute-start.19 = (bf16[64,1024]{1,0:T(8,128)(2,1)S(1)}, bf16[64,1024]{1,0:T(8,128)(2,1)S(1)}, u32[]{:S(2)}, u32[]{:S(2)}) collective-permute-start(bf16[64,1024]{1,0:T(8,128)(2,1)S(1)} %slice.111), channel_id=1, source_target_pairs={{0,2},{1,3},{2,0},{3,1},{4,6},{5,7},{6,4},{7,5},{8,10},{9,11},{10,... | collective-permute-start | bytes 393224 | tf_op jit(solution)/shard_map/ppermute | solution.py:25
  54.2 1.6 %collective-permute-start.17 = (bf16[64,1024]{1,0:T(8,128)(2,1)S(1)}, bf16[64,1024]{1,0:T(8,128)(2,1)S(1)}, u32[]{:S(2)}, u32[]{:S(2)}) collective-permute-start(bf16[64,1024]{1,0:T(8,128)(2,1)S(1)} %slice.110), channel_id=1, source_target_pairs={{0,16},{16,0},{1,17},{17,1},{2,18},{18,2},{3,19},{19,3},{4,20},{20... | collective-permute-start | bytes 393224 | tf_op jit(solution)/shard_map/ppermute | solution.py:25
  55.7 5.9 %collective-permute-done.13 = bf16[64,2048]{1,0:T(8,128)(2,1)S(1)} collective-permute-done((bf16[64,2048]{1,0:T(8,128)(2,1)S(1)}, bf16[64,2048]{1,0:T(8,128)(2,1)S(1)}, u32[]{:S(2)}, u32[]{:S(2)}) %collective-permute-start.13) | collective-permute-done | bytes 262176 | tf_op jit(solution)/shard_map/ppermute | solution.py:25
  61.7 0.9 collective-permute-done.16
  62.7 0.6 copy-done.1
  63.3 0.5 collective-permute-start.22
  63.8 0.5 collective-permute-start.20
  64.3 5.1 %collective-permute-done.14.refs_15_ = bf16[64,2048]{1,0:T(8,128)(2,1)S(1)} collective-permute-done((bf16[64,2048]{1,0:T(8,128)(2,1)S(1)}, bf16[64,2048]{1,0:T(8,128)(2,1)S(1)}, u32[]{:S(2)}, u32[]{:S(2)}) %collective-permute-start.14) | collective-permute-done | bytes 262176 | tf_op jit(solution)/shard_map/ppermute | solution.py:25
  69.4 0.5 collective-permute-start.23
  70.0 0.5 collective-permute-start.21
  70.5 1.6 %tables.1 = (bf16[4,224,256]{2,1,0:T(8,128)(2,1)S(1)}, bf16[2,4,256,112]{3,2,1,0:T(8,128)(2,1)S(1)}, f32[4,256,2]{2,1,0:T(8,128)S(1)}) custom-call(s32[1]{0:T(128)} %bitcast.12.refs_0_, bf16[4,256,128]{2,1,0:T(8,128)(2,1)S(1)} %pad_maximum_fusion.3.refs_1_), custom_call_target="tpu_custom_call" | custom-call | flops 134217728 | bytes 917504 | tf_op jit(solution)/shard_map/tables/pallas_call | solution.py:316
  72.1 9.3 %collective-permute-done.23.refs_12_ = bf16[64,2048]{1,0:T(8,128)(2,1)S(1)} collective-permute-done((bf16[64,2048]{1,0:T(8,128)(2,1)S(1)}, bf16[64,2048]{1,0:T(8,128)(2,1)S(1)}, u32[]{:S(2)}, u32[]{:S(2)}) %collective-permute-start.23) | collective-permute-done | bytes 262176 | tf_op jit(solution)/shard_map/ppermute | solution.py:25
  81.4 0.6 collective-permute-start.27
  82.0 2.0 %collective-permute-start.26 = (bf16[64,1024]{1,0:T(8,128)(2,1)S(1)}, bf16[64,1024]{1,0:T(8,128)(2,1)S(1)}, u32[]{:S(2)}, u32[]{:S(2)}) collective-permute-start(bf16[64,1024]{1,0:T(8,128)(2,1)S(1)} %slice.114), channel_id=1, source_target_pairs={{0,16},{16,0},{1,17},{17,1},{2,18},{18,2},{3,19},{19,3},{4,20},{20... | collective-permute-start | bytes 393224 | tf_op jit(solution)/shard_map/ppermute | solution.py:25
  84.0 0.5 collective-permute-start.25
  84.5 1.3 collective-permute-start.24
  85.8 9.5 %experts.2 = (bf16[256,1024]{1,0:T(8,128)(2,1)S(1)}, bf16[256,1024]{1,0:T(8,128)(2,1)S(1)}, bf16[256,1024]{1,0:T(8,128)(2,1)S(1)}, bf16[256,1024]{1,0:T(8,128)(2,1)S(1)}) custom-call(bf16[4,224,256]{2,1,0:T(8,128)(2,1)S(1)} %get-tuple-element.76.refs_0_, bf16[2,4,256,112]{3,2,1,0:T(8,128)(2,1)S(1)} %get-tuple-element.77.refs_1_, ...), custom_call_target="tpu_custom_call" | custom-call | flops 4227858432 | bytes 23068672 | tf_op jit(solution)/shard_map/experts/pallas_call | solution.py:446
  95.3 0.9 collective-permute-start.28
  96.2 1.6 %collective-permute-start.29 = (bf16[256,1024]{1,0:T(8,128)(2,1)S(1)}, bf16[256,1024]{1,0:T(8,128)(2,1)S(1)}, u32[]{:S(2)}, u32[]{:S(2)}) collective-permute-start(bf16[256,1024]{1,0:T(8,128)(2,1)S(1)} %get-tuple-element.90), channel_id=1, source_target_pairs={{0,2},{1,3},{2,0},{3,1},{4,6},{5,7},{6,4},{7,5},{8,10},{9,11},{10,... | collective-permute-start | bytes 1572872 | tf_op jit(solution)/shard_map/ppermute | solution.py:25
  97.8 9.8 %experts.3 = (bf16[128,1024]{1,0:T(8,128)(2,1)S(1)}, bf16[128,1024]{1,0:T(8,128)(2,1)S(1)}, bf16[128,1024]{1,0:T(8,128)(2,1)S(1)}, bf16[128,1024]{1,0:T(8,128)(2...) custom-call(bf16[4,224,256]{2,1,0:T(8,128)(2,1)S(1)} %get-tuple-element.76.refs_0_, ...), custom_call_target="tpu_custom_call" | custom-call | flops 4227858432 | bytes 23068672 | tf_op jit(solution)/shard_map/experts/pallas_call | solution.py:446
  107.6 0.3 collective-permute-start.30
  107.9 1.4 collective-permute-start.32
  109.3 0.8 collective-permute-start.34
  110.2 1.6 %collective-permute-start.35 = (bf16[128,1024]{1,0:T(8,128)(2,1)S(1)}, bf16[128,1024]{1,0:T(8,128)(2,1)S(1)}, u32[]{:S(2)}, u32[]{:S(2)}) collective-permute-start(bf16[128,1024]{1,0:T(8,128)(2,1)S(1)} %get-tuple-element.110), channel_id=1, source_target_pairs={{0,2},{1,3},{2,0},{3,1},{4,6},{5,7},{6,4},{7,5},{8,10},{9,11},{10,... | collective-permute-start | bytes 786440 | tf_op jit(solution)/shard_map/ppermute | solution.py:25
  111.7 5.1 %collective-permute-done.30 = bf16[128,1024]{1,0:T(8,128)(2,1)S(1)} collective-permute-done((bf16[128,1024]{1,0:T(8,128)(2,1)S(1)}, bf16[128,1024]{1,0:T(8,128)(2,1)S(1)}, u32[]{:S(2)}, u32[]{:S(2)}) %collective-permute-start.30) | collective-permute-done | bytes 262176 | tf_op jit(solution)/shard_map/ppermute | solution.py:25
  117.2 1.8 %collective-permute-start.33 = (bf16[128,1024]{1,0:T(8,128)(2,1)S(1)}, bf16[128,1024]{1,0:T(8,128)(2,1)S(1)}, u32[]{:S(2)}, u32[]{:S(2)}) collective-permute-start(bf16[128,1024]{1,0:T(8,128)(2,1)S(1)} %add_convert_fusion.4), channel_id=1, source_target_pairs={{0,16},{16,0},{1,17},{17,1},{2,18},{18,2},{3,19},{19,3},{4,20},{20... | collective-permute-start | bytes 786440 | tf_op jit(solution)/shard_map/ppermute | solution.py:25
  119.0 0.9 collective-permute-done.34
  119.9 0.3 collective-permute-done.35
  120.2 6.0 %collective-permute-done.31 = bf16[128,1024]{1,0:T(8,128)(2,1)S(1)} collective-permute-done((bf16[128,1024]{1,0:T(8,128)(2,1)S(1)}, bf16[128,1024]{1,0:T(8,128)(2,1)S(1)}, u32[]{:S(2)}, u32[]{:S(2)}) %collective-permute-start.31) | collective-permute-done | bytes 262176 | tf_op jit(solution)/shard_map/ppermute | solution.py:25
  126.3 1.8 %collective-permute-start.36 = (bf16[128,1024]{1,0:T(8,128)(2,1)S(1)}, bf16[128,1024]{1,0:T(8,128)(2,1)S(1)}, u32[]{:S(2)}, u32[]{:S(2)}) collective-permute-start(bf16[128,1024]{1,0:T(8,128)(2,1)S(1)} %add_convert_fusion.3), channel_id=1, source_target_pairs={{0,2},{1,3},{2,0},{3,1},{4,6},{5,7},{6,4},{7,5},{8,10},{9,11},{10,... | collective-permute-start | bytes 786440 | tf_op jit(solution)/shard_map/ppermute | solution.py:25
  128.1 0.5 collective-permute-start.37
  128.9 0.8 collective-permute-start.38
  129.7 3.0 %collective-permute-done.36 = bf16[128,1024]{1,0:T(8,128)(2,1)S(1)} collective-permute-done((bf16[128,1024]{1,0:T(8,128)(2,1)S(1)}, bf16[128,1024]{1,0:T(8,128)(2,1)S(1)}, u32[]{:S(2)}, u32[]{:S(2)}) %collective-permute-start.36) | collective-permute-done | bytes 262176 | tf_op jit(solution)/shard_map/ppermute | solution.py:25
  132.7 1.8 %collective-permute-done.37 = bf16[128,1024]{1,0:T(8,128)(2,1)S(1)} collective-permute-done((bf16[128,1024]{1,0:T(8,128)(2,1)S(1)}, bf16[128,1024]{1,0:T(8,128)(2,1)S(1)}, u32[]{:S(2)}, u32[]{:S(2)}) %collective-permute-start.37) | collective-permute-done | bytes 262176 | tf_op jit(solution)/shard_map/ppermute | solution.py:25
  134.5 0.3 convert_add_fusion
  134.8 6.2 %collective-permute-done.38 = bf16[128,2048]{1,0:T(8,128)(2,1)S(1)} collective-permute-done((bf16[128,2048]{1,0:T(8,128)(2,1)S(1)}, bf16[128,2048]{1,0:T(8,128)(2,1)S(1)}, u32[]{:S(2)}, u32[]{:S(2)}) %collective-permute-start.38) | collective-permute-done | bytes 524320 | tf_op jit(solution)/shard_map/ppermute | solution.py:25
  141.1 1.9 %collective-permute-start.39 = (bf16[64,2048]{1,0:T(8,128)(2,1)S(1)}, bf16[64,2048]{1,0:T(8,128)(2,1)S(1)}, u32[]{:S(2)}, u32[]{:S(2)}) collective-permute-start(bf16[64,2048]{1,0:T(8,128)(2,1)S(1)} %slice.144), channel_id=1, source_target_pairs={{0,8},{4,12},{8,0},{12,4},{1,9},{5,13},{9,1},{13,5},{2,10},{6,14},... | collective-permute-start | bytes 786440 | tf_op jit(solution)/shard_map/ppermute | solution.py:25
  143.0 8.2 %collective-permute-done.39 = bf16[64,2048]{1,0:T(8,128)(2,1)S(1)} collective-permute-done((bf16[64,2048]{1,0:T(8,128)(2,1)S(1)}, bf16[64,2048]{1,0:T(8,128)(2,1)S(1)}, u32[]{:S(2)}, u32[]{:S(2)}) %collective-permute-start.39) | collective-permute-done | bytes 262176 | tf_op jit(solution)/shard_map/ppermute | solution.py:25
  151.2 0.8 fusion.3
  (79 shorter events, 1.9 us)
Async XLA Ops:
  0.0 27.8 %copy-start.3 = (f32[128]{0:T(128)S(1)}, f32[128]{0:T(128)}, u32[]{:S(2)}) copy-start(f32[128]{0:T(128)} %param.16) | copy-start | bytes 1540
  0.0 27.8 %copy-start = (bf16[2048,512]{1,0:T(8,128)(2,1)S(1)}, bf16[2048,512]{1,0:T(8,128)(2,1)}, u32[]{:S(2)}) copy-start(bf16[2048,512]{1,0:T(8,128)(2,1)} %weight_ref.1) | copy-start | bytes 6291460
  0.0 43.8 %collective-permute-start.11 = (bf16[2048,1536]{1,0:T(8,128)(2,1)}, bf16[2048,1536]{1,0:T(8,128)(2,1)}, u32[]{:S(2)}, u32[]{:S(2)}) collective-permute-start(bf16[2048,1536]{1,0:T(8,128)(2,1)} %bitcast.21), channel_id=1, source_target_pairs={{0,1},{1,0},{2,3},{3,2},{4,5},{5,4},{6,7},{7,6},{8,9},{9,8},{10,11... | collective-permute-start | bytes 18874376 | tf_op jit(solution)/shard_map/ppermute | solution.py:25
  3.1 13.6 %collective-permute-start.2 = (bf16[64,640]{1,0:T(8,128)(2,1)S(1)}, bf16[64,640]{1,0:T(8,128)(2,1)S(1)}, u32[]{:S(2)}, u32[]{:S(2)}) collective-permute-start(bf16[64,640]{1,0:T(8,128)(2,1)S(1)} %get-tuple-element.63), channel_id=1, source_target_pairs={{0,12},{4,8},{8,4},{12,0},{1,13},{5,9},{9,5},{13,1},{2,14},{6,10},... | collective-permute-start | bytes 245768 | tf_op jit(solution)/shard_map/ppermute | solution.py:25
  7.7 8.9 %collective-permute-start.1 = (bf16[64,640]{1,0:T(8,128)(2,1)S(1)}, bf16[64,640]{1,0:T(8,128)(2,1)S(1)}, u32[]{:S(2)}, u32[]{:S(2)}) collective-permute-start(bf16[64,640]{1,0:T(8,128)(2,1)S(1)} %get-tuple-element.63), channel_id=1, source_target_pairs={{0,4},{4,0},{8,12},{12,8},{1,5},{5,1},{9,13},{13,9},{2,6},{6,2},{1... | collective-permute-start | bytes 245768 | tf_op jit(solution)/shard_map/ppermute | solution.py:25
  7.7 7.4 %collective-permute-start = (bf16[64,640]{1,0:T(8,128)(2,1)S(1)}, bf16[64,640]{1,0:T(8,128)(2,1)S(1)}, u32[]{:S(2)}, u32[]{:S(2)}) collective-permute-start(bf16[64,640]{1,0:T(8,128)(2,1)S(1)} %get-tuple-element.63), channel_id=1, source_target_pairs={{0,8},{4,12},{8,0},{12,4},{1,9},{5,13},{9,1},{13,5},{2,10},{6,14},... | collective-permute-start | bytes 245768 | tf_op jit(solution)/shard_map/ppermute | solution.py:25
  8.4 8.4 %collective-permute-start.4 = (bf16[64,2048]{1,0:T(8,128)(2,1)S(1)}, bf16[64,2048]{1,0:T(8,128)(2,1)S(1)}, u32[]{:S(2)}, u32[]{:S(2)}) collective-permute-start(bf16[64,2048]{1,0:T(8,128)(2,1)S(1)} %get-tuple-element.62.first_ref), channel_id=1, source_target_pairs={{0,1},{1,0},{2,3},{3,2},{4,5},{5,4},{6,7},{7,6},{8,9},{9,8},{10,11... | collective-permute-start | bytes 786440 | tf_op jit(solution)/shard_map/ppermute | solution.py:25
  8.4 20.9 %copy-start.4 = (bf16[512,2048]{1,0:T(8,128)(2,1)S(1)}, bf16[512,2048]{1,0:T(8,128)(2,1)}, u32[]{:S(2)}) copy-start(bf16[512,2048]{1,0:T(8,128)(2,1)} %refs_3_.1) | copy-start | bytes 6291460
  15.1 6.9 %collective-permute-start.3 = (bf16[64,2048]{1,0:T(8,128)(2,1)S(1)}, bf16[64,2048]{1,0:T(8,128)(2,1)S(1)}, u32[]{:S(2)}, u32[]{:S(2)}) collective-permute-start(bf16[64,2048]{1,0:T(8,128)(2,1)S(1)} %get-tuple-element.62.first_ref), channel_id=1, source_target_pairs={{0,2},{1,3},{2,0},{3,1},{4,6},{5,7},{6,4},{7,5},{8,10},{9,11},{10,... | collective-permute-start | bytes 786440 | tf_op jit(solution)/shard_map/ppermute | solution.py:25
  22.0 5.7 %collective-permute-start.6 = (bf16[256,384]{1,0:T(8,128)(2,1)S(1)}, bf16[256,384]{1,0:T(8,128)(2,1)S(1)}, u32[]{:S(2)}, u32[]{:S(2)}) collective-permute-start(bf16[256,384]{1,0:T(8,128)(2,1)S(1)} %pad_maximum_fusion.4), channel_id=1, source_target_pairs={{0,2},{1,3},{2,0},{3,1},{4,6},{5,7},{6,4},{7,5},{8,10},{9,11},{10,... | collective-permute-start | bytes 589832 | tf_op jit(solution)/shard_map/ppermute | solution.py:25
  23.5 4.3 %collective-permute-start.5 = (bf16[64,2048]{1,0:T(8,128)(2,1)S(1)}, bf16[64,2048]{1,0:T(8,128)(2,1)S(1)}, u32[]{:S(2)}, u32[]{:S(2)}) collective-permute-start(bf16[64,2048]{1,0:T(8,128)(2,1)S(1)} %collective-permute-done.3.second_ref), channel_id=1, source_target_pairs={{0,1},{1,0},{2,3},{3,2},{4,5},{5,4},{6,7},{7,6},{8,9},{9,8},{10,11... | collective-permute-start | bytes 786440 | tf_op jit(solution)/shard_map/ppermute | solution.py:25
  27.7 1.6 %collective-permute-start.7 = (bf16[512,256]{1,0:T(8,128)(2,1)S(1)}, bf16[512,256]{1,0:T(8,128)(2,1)S(1)}, u32[]{:S(2)}, u32[]{:S(2)}) collective-permute-start(bf16[512,256]{1,0:T(8,128)(2,1)S(1)} %pad_maximum_fusion.2.refs_1_), channel_id=1, source_target_pairs={{0,1},{1,0},{2,3},{3,2},{4,5},{5,4},{6,7},{7,6},{8,9},{9,8},{10,11... | collective-permute-start | bytes 786440 | tf_op jit(solution)/shard_map/ppermute | solution.py:25
  27.8 7.0 %copy-start.5 = (bf16[1,768,2048]{2,1,0:T(8,128)(2,1)S(1)}, bf16[1,768,2048]{2,1,0:T(8,128)(2,1)}, u32[]{:S(2)}) copy-start(bf16[1,768,2048]{2,1,0:T(8,128)(2,1)} %param.23) | copy-start | bytes 9437188
  32.0 11.7 %copy-start.9 = (bf16[1,64,2048]{2,1,0:T(8,128)(2,1)S(1)}, bf16[1,64,2048]{2,1,0:T(8,128)(2,1)}, u32[]{:S(2)}) copy-start(bf16[1,64,2048]{2,1,0:T(8,128)(2,1)} %param.12) | copy-start | bytes 786436
  32.0 2.7 %collective-permute-start.8 = (f32[128,2048]{1,0:T(8,128)S(1)}, f32[128,2048]{1,0:T(8,128)S(1)}, u32[]{:S(2)}, u32[]{:S(2)}) collective-permute-start(f32[128,2048]{1,0:T(8,128)S(1)} %get-tuple-element.68), channel_id=1, source_target_pairs={{0,1},{1,0},{2,3},{3,2},{4,5},{5,4},{6,7},{7,6},{8,9},{9,8},{10,11... | collective-permute-start | bytes 3145736 | tf_op jit(solution)/shard_map/ppermute | solution.py:25
  34.7 9.0 %collective-permute-start.12 = (bf16[768,2048]{1,0:T(8,128)(2,1)S(1)}, bf16[768,2048]{1,0:T(8,128)(2,1)S(1)}, u32[]{:S(2)}, u32[]{:S(2)}) collective-permute-start(bf16[768,2048]{1,0:T(8,128)(2,1)S(1)} %bitcast.26), channel_id=1, source_target_pairs={{0,1},{1,0},{2,3},{3,2},{4,5},{5,4},{6,7},{7,6},{8,9},{9,8},{10,11... | collective-permute-start | bytes 9437192 | tf_op jit(solution)/shard_map/ppermute | solution.py:25
  34.9 9.7 %copy-start.10 = (f32[2048]{0:T(1024)S(1)}, f32[2048]{0:T(1024)}, u32[]{:S(2)}) copy-start(f32[2048]{0:T(1024)} %param.19) | copy-start | bytes 24580
  35.1 8.6 %collective-permute-start.9 = (bf16[64,2048]{1,0:T(8,128)(2,1)S(1)}, bf16[64,2048]{1,0:T(8,128)(2,1)S(1)}, u32[]{:S(2)}, u32[]{:S(2)}) collective-permute-start(bf16[64,2048]{1,0:T(8,128)(2,1)S(1)} %slice.145), channel_id=1, source_target_pairs={{0,2},{1,3},{2,0},{3,1},{4,6},{5,7},{6,4},{7,5},{8,10},{9,11},{10,... | collective-permute-start | bytes 786440 | tf_op jit(solution)/shard_map/ppermute | solution.py:25
  36.7 5.5 %collective-permute-start.10 = (bf16[2,256,128]{2,1,0:T(8,128)(2,1)S(1)}, bf16[2,256,128]{2,1,0:T(8,128)(2,1)S(1)}, u32[]{:S(2)}, u32[]{:S(2)}) collective-permute-start(bf16[2,256,128]{2,1,0:T(8,128)(2,1)S(1)} %pad_maximum_fusion.5), channel_id=1, source_target_pairs={{0,16},{16,0},{1,17},{17,1},{2,18},{18,2},{3,19},{19,3},{4,20},{20... | collective-permute-start | bytes 393224 | tf_op jit(solution)/shard_map/ppermute | solution.py:25
  43.8 0.8 copy-start.7
  43.8 25.6 %copy-start.6 = (bf16[768,2048]{1,0:T(8,128)(2,1)}, bf16[768,2048]{1,0:T(8,128)(2,1)S(1)}, u32[]{:S(2)}) copy-start(bf16[768,2048]{1,0:T(8,128)(2,1)S(1)} %collective-permute-done.12.refs_6_) | copy-start | bytes 9437188
  44.7 7.8 %collective-permute-start.18 = (bf16[64,2048]{1,0:T(8,128)(2,1)S(1)}, bf16[64,2048]{1,0:T(8,128)(2,1)S(1)}, u32[]{:S(2)}, u32[]{:S(2)}) collective-permute-start(bf16[64,2048]{1,0:T(8,128)(2,1)S(1)} %multiply_convert_fusion.refs_13_), channel_id=1, source_target_pairs={{0,16},{16,0},{1,17},{17,1},{2,18},{18,2},{3,19},{19,3},{4,20},{20... | collective-permute-start | bytes 786440 | tf_op jit(solution)/shard_map/ppermute | solution.py:25
  46.3 7.9 %collective-permute-start.15 = (bf16[64,2048]{1,0:T(8,128)(2,1)S(1)}, bf16[64,2048]{1,0:T(8,128)(2,1)S(1)}, u32[]{:S(2)}, u32[]{:S(2)}) collective-permute-start(bf16[64,2048]{1,0:T(8,128)(2,1)S(1)} %multiply_convert_fusion.refs_13_), channel_id=1, source_target_pairs={{0,2},{1,3},{2,0},{3,1},{4,6},{5,7},{6,4},{7,5},{8,10},{9,11},{10,... | collective-permute-start | bytes 786440 | tf_op jit(solution)/shard_map/ppermute | solution.py:25
  47.8 13.8 %collective-permute-start.13 = (bf16[64,2048]{1,0:T(8,128)(2,1)S(1)}, bf16[64,2048]{1,0:T(8,128)(2,1)S(1)}, u32[]{:S(2)}, u32[]{:S(2)}) collective-permute-start(bf16[64,2048]{1,0:T(8,128)(2,1)S(1)} %multiply_convert_fusion.refs_13_), channel_id=1, source_target_pairs={{0,8},{4,12},{8,0},{12,4},{1,9},{5,13},{9,1},{13,5},{2,10},{6,14},... | collective-permute-start | bytes 786440 | tf_op jit(solution)/shard_map/ppermute | solution.py:25
  50.4 12.1 %collective-permute-start.16 = (bf16[64,2048]{1,0:T(8,128)(2,1)S(1)}, bf16[64,2048]{1,0:T(8,128)(2,1)S(1)}, u32[]{:S(2)}, u32[]{:S(2)}) collective-permute-start(bf16[64,2048]{1,0:T(8,128)(2,1)S(1)} %multiply_convert_fusion.refs_13_), channel_id=1, source_target_pairs={{0,4},{4,0},{8,12},{12,8},{1,5},{5,1},{9,13},{13,9},{2,6},{6,2},{1... | collective-permute-start | bytes 786440 | tf_op jit(solution)/shard_map/ppermute | solution.py:25
  52.6 10.0 %collective-permute-start.19 = (bf16[64,1024]{1,0:T(8,128)(2,1)S(1)}, bf16[64,1024]{1,0:T(8,128)(2,1)S(1)}, u32[]{:S(2)}, u32[]{:S(2)}) collective-permute-start(bf16[64,1024]{1,0:T(8,128)(2,1)S(1)} %slice.111), channel_id=1, source_target_pairs={{0,2},{1,3},{2,0},{3,1},{4,6},{5,7},{6,4},{7,5},{8,10},{9,11},{10,... | collective-permute-start | bytes 393224 | tf_op jit(solution)/shard_map/ppermute | solution.py:25
  54.2 8.5 %collective-permute-start.17 = (bf16[64,1024]{1,0:T(8,128)(2,1)S(1)}, bf16[64,1024]{1,0:T(8,128)(2,1)S(1)}, u32[]{:S(2)}, u32[]{:S(2)}) collective-permute-start(bf16[64,1024]{1,0:T(8,128)(2,1)S(1)} %slice.110), channel_id=1, source_target_pairs={{0,16},{16,0},{1,17},{17,1},{2,18},{18,2},{3,19},{19,3},{4,20},{20... | collective-permute-start | bytes 393224 | tf_op jit(solution)/shard_map/ppermute | solution.py:25
  61.6 7.8 %collective-permute-start.14 = (bf16[64,2048]{1,0:T(8,128)(2,1)S(1)}, bf16[64,2048]{1,0:T(8,128)(2,1)S(1)}, u32[]{:S(2)}, u32[]{:S(2)}) collective-permute-start(bf16[64,2048]{1,0:T(8,128)(2,1)S(1)} %collective-permute-done.13), channel_id=1, source_target_pairs={{0,4},{4,0},{8,12},{12,8},{1,5},{5,1},{9,13},{13,9},{2,6},{6,2},{1... | collective-permute-start | bytes 786440 | tf_op jit(solution)/shard_map/ppermute | solution.py:25
  62.6 0.7 copy-start.1
  63.3 20.7 %collective-permute-start.22 = (bf16[128,2048]{1,0:T(8,128)(2,1)S(1)}, bf16[128,2048]{1,0:T(8,128)(2,1)S(1)}, u32[]{:S(2)}, u32[]{:S(2)}) collective-permute-start(bf16[128,2048]{1,0:T(8,128)(2,1)S(1)} %pad_maximum_fusion.refs_14_), channel_id=1, source_target_pairs={{0,16},{16,0},{1,17},{17,1},{2,18},{18,2},{3,19},{19,3},{4,20},{20... | collective-permute-start | bytes 1572872 | tf_op jit(solution)/shard_map/ppermute | solution.py:25
  63.8 20.7 %collective-permute-start.20 = (bf16[128,2048]{1,0:T(8,128)(2,1)S(1)}, bf16[128,2048]{1,0:T(8,128)(2,1)S(1)}, u32[]{:S(2)}, u32[]{:S(2)}) collective-permute-start(bf16[128,2048]{1,0:T(8,128)(2,1)S(1)} %pad_maximum_fusion.refs_14_), channel_id=1, source_target_pairs={{0,2},{1,3},{2,0},{3,1},{4,6},{5,7},{6,4},{7,5},{8,10},{9,11},{10,... | collective-permute-start | bytes 1572872 | tf_op jit(solution)/shard_map/ppermute | solution.py:25
  69.4 12.0 %collective-permute-start.23 = (bf16[64,2048]{1,0:T(8,128)(2,1)S(1)}, bf16[64,2048]{1,0:T(8,128)(2,1)S(1)}, u32[]{:S(2)}, u32[]{:S(2)}) collective-permute-start(bf16[64,2048]{1,0:T(8,128)(2,1)S(1)} %collective-permute-done.14.refs_15_), channel_id=1, source_target_pairs={{0,16},{16,0},{1,17},{17,1},{2,18},{18,2},{3,19},{19,3},{4,20},{20... | collective-permute-start | bytes 786440 | tf_op jit(solution)/shard_map/ppermute | solution.py:25
  70.0 12.0 %collective-permute-start.21 = (bf16[64,2048]{1,0:T(8,128)(2,1)S(1)}, bf16[64,2048]{1,0:T(8,128)(2,1)S(1)}, u32[]{:S(2)}, u32[]{:S(2)}) collective-permute-start(bf16[64,2048]{1,0:T(8,128)(2,1)S(1)} %collective-permute-done.14.refs_15_), channel_id=1, source_target_pairs={{0,2},{1,3},{2,0},{3,1},{4,6},{5,7},{6,4},{7,5},{8,10},{9,11},{10,... | collective-permute-start | bytes 786440 | tf_op jit(solution)/shard_map/ppermute | solution.py:25
  81.4 13.9 %collective-permute-start.27 = (bf16[64,1024]{1,0:T(8,128)(2,1)S(1)}, bf16[64,1024]{1,0:T(8,128)(2,1)S(1)}, u32[]{:S(2)}, u32[]{:S(2)}) collective-permute-start(bf16[64,1024]{1,0:T(8,128)(2,1)S(1)} %slice.115), channel_id=1, source_target_pairs={{0,2},{1,3},{2,0},{3,1},{4,6},{5,7},{6,4},{7,5},{8,10},{9,11},{10,... | collective-permute-start | bytes 393224 | tf_op jit(solution)/shard_map/ppermute | solution.py:25
  82.0 13.3 %collective-permute-start.26 = (bf16[64,1024]{1,0:T(8,128)(2,1)S(1)}, bf16[64,1024]{1,0:T(8,128)(2,1)S(1)}, u32[]{:S(2)}, u32[]{:S(2)}) collective-permute-start(bf16[64,1024]{1,0:T(8,128)(2,1)S(1)} %slice.114), channel_id=1, source_target_pairs={{0,16},{16,0},{1,17},{17,1},{2,18},{18,2},{3,19},{19,3},{4,20},{20... | collective-permute-start | bytes 393224 | tf_op jit(solution)/shard_map/ppermute | solution.py:25
  84.0 11.3 %collective-permute-start.25 = (bf16[128,1024]{1,0:T(8,128)(2,1)S(1)}, bf16[128,1024]{1,0:T(8,128)(2,1)S(1)}, u32[]{:S(2)}, u32[]{:S(2)}) collective-permute-start(bf16[128,1024]{1,0:T(8,128)(2,1)S(1)} %slice.113), channel_id=1, source_target_pairs={{0,2},{1,3},{2,0},{3,1},{4,6},{5,7},{6,4},{7,5},{8,10},{9,11},{10,... | collective-permute-start | bytes 786440 | tf_op jit(solution)/shard_map/ppermute | solution.py:25
  84.5 10.8 %collective-permute-start.24 = (bf16[128,1024]{1,0:T(8,128)(2,1)S(1)}, bf16[128,1024]{1,0:T(8,128)(2,1)S(1)}, u32[]{:S(2)}, u32[]{:S(2)}) collective-permute-start(bf16[128,1024]{1,0:T(8,128)(2,1)S(1)} %slice.112), channel_id=1, source_target_pairs={{0,16},{16,0},{1,17},{17,1},{2,18},{18,2},{3,19},{19,3},{4,20},{20... | collective-permute-start | bytes 786440 | tf_op jit(solution)/shard_map/ppermute | solution.py:25
  85.8 12.0 %copy-start.2 = (bf16[64,1024]{1,0:T(8,128)(2,1)S(1)}, bf16[64,1024]{1,0:T(8,128)(2,1)}, u32[]{:S(2)}) copy-start(bf16[64,1024]{1,0:T(8,128)(2,1)} %copy-done.1) | copy-start | bytes 393220
  95.3 12.3 %collective-permute-start.28 = (bf16[256,1024]{1,0:T(8,128)(2,1)S(1)}, bf16[256,1024]{1,0:T(8,128)(2,1)S(1)}, u32[]{:S(2)}, u32[]{:S(2)}) collective-permute-start(bf16[256,1024]{1,0:T(8,128)(2,1)S(1)} %get-tuple-element.89), channel_id=1, source_target_pairs={{0,16},{16,0},{1,17},{17,1},{2,18},{18,2},{3,19},{19,3},{4,20},{20... | collective-permute-start | bytes 1572872 | tf_op jit(solution)/shard_map/ppermute | solution.py:25
  96.2 11.4 %collective-permute-start.29 = (bf16[256,1024]{1,0:T(8,128)(2,1)S(1)}, bf16[256,1024]{1,0:T(8,128)(2,1)S(1)}, u32[]{:S(2)}, u32[]{:S(2)}) collective-permute-start(bf16[256,1024]{1,0:T(8,128)(2,1)S(1)} %get-tuple-element.90), channel_id=1, source_target_pairs={{0,2},{1,3},{2,0},{3,1},{4,6},{5,7},{6,4},{7,5},{8,10},{9,11},{10,... | collective-permute-start | bytes 1572872 | tf_op jit(solution)/shard_map/ppermute | solution.py:25
  107.6 9.2 %collective-permute-start.30 = (bf16[128,1024]{1,0:T(8,128)(2,1)S(1)}, bf16[128,1024]{1,0:T(8,128)(2,1)S(1)}, u32[]{:S(2)}, u32[]{:S(2)}) collective-permute-start(bf16[128,1024]{1,0:T(8,128)(2,1)S(1)} %get-tuple-element.106), channel_id=1, source_target_pairs={{0,16},{16,0},{1,17},{17,1},{2,18},{18,2},{3,19},{19,3},{4,20},{20... | collective-permute-start | bytes 786440 | tf_op jit(solution)/shard_map/ppermute | solution.py:25
  107.9 9.2 %collective-permute-start.32 = (bf16[128,1024]{1,0:T(8,128)(2,1)S(1)}, bf16[128,1024]{1,0:T(8,128)(2,1)S(1)}, u32[]{:S(2)}, u32[]{:S(2)}) collective-permute-start(bf16[128,1024]{1,0:T(8,128)(2,1)S(1)} %get-tuple-element.108), channel_id=1, source_target_pairs={{0,2},{1,3},{2,0},{3,1},{4,6},{5,7},{6,4},{7,5},{8,10},{9,11},{10,... | collective-permute-start | bytes 786440 | tf_op jit(solution)/shard_map/ppermute | solution.py:25
  109.3 10.6 %collective-permute-start.34 = (bf16[128,1024]{1,0:T(8,128)(2,1)S(1)}, bf16[128,1024]{1,0:T(8,128)(2,1)S(1)}, u32[]{:S(2)}, u32[]{:S(2)}) collective-permute-start(bf16[128,1024]{1,0:T(8,128)(2,1)S(1)} %get-tuple-element.109), channel_id=1, source_target_pairs={{0,16},{16,0},{1,17},{17,1},{2,18},{18,2},{3,19},{19,3},{4,20},{20... | collective-permute-start | bytes 786440 | tf_op jit(solution)/shard_map/ppermute | solution.py:25
  110.2 10.0 %collective-permute-start.35 = (bf16[128,1024]{1,0:T(8,128)(2,1)S(1)}, bf16[128,1024]{1,0:T(8,128)(2,1)S(1)}, u32[]{:S(2)}, u32[]{:S(2)}) collective-permute-start(bf16[128,1024]{1,0:T(8,128)(2,1)S(1)} %get-tuple-element.110), channel_id=1, source_target_pairs={{0,2},{1,3},{2,0},{3,1},{4,6},{5,7},{6,4},{7,5},{8,10},{9,11},{10,... | collective-permute-start | bytes 786440 | tf_op jit(solution)/shard_map/ppermute | solution.py:25
  116.9 9.2 %collective-permute-start.31 = (bf16[128,1024]{1,0:T(8,128)(2,1)S(1)}, bf16[128,1024]{1,0:T(8,128)(2,1)S(1)}, u32[]{:S(2)}, u32[]{:S(2)}) collective-permute-start(bf16[128,1024]{1,0:T(8,128)(2,1)S(1)} %add_convert_fusion.5), channel_id=1, source_target_pairs={{0,2},{1,3},{2,0},{3,1},{4,6},{5,7},{6,4},{7,5},{8,10},{9,11},{10,... | collective-permute-start | bytes 786440 | tf_op jit(solution)/shard_map/ppermute | solution.py:25
  117.2 9.0 %collective-permute-start.33 = (bf16[128,1024]{1,0:T(8,128)(2,1)S(1)}, bf16[128,1024]{1,0:T(8,128)(2,1)S(1)}, u32[]{:S(2)}, u32[]{:S(2)}) collective-permute-start(bf16[128,1024]{1,0:T(8,128)(2,1)S(1)} %add_convert_fusion.4), channel_id=1, source_target_pairs={{0,16},{16,0},{1,17},{17,1},{2,18},{18,2},{3,19},{19,3},{4,20},{20... | collective-permute-start | bytes 786440 | tf_op jit(solution)/shard_map/ppermute | solution.py:25
  126.3 6.4 %collective-permute-start.36 = (bf16[128,1024]{1,0:T(8,128)(2,1)S(1)}, bf16[128,1024]{1,0:T(8,128)(2,1)S(1)}, u32[]{:S(2)}, u32[]{:S(2)}) collective-permute-start(bf16[128,1024]{1,0:T(8,128)(2,1)S(1)} %add_convert_fusion.3), channel_id=1, source_target_pairs={{0,2},{1,3},{2,0},{3,1},{4,6},{5,7},{6,4},{7,5},{8,10},{9,11},{10,... | collective-permute-start | bytes 786440 | tf_op jit(solution)/shard_map/ppermute | solution.py:25
  128.1 6.4 %collective-permute-start.37 = (bf16[128,1024]{1,0:T(8,128)(2,1)S(1)}, bf16[128,1024]{1,0:T(8,128)(2,1)S(1)}, u32[]{:S(2)}, u32[]{:S(2)}) collective-permute-start(bf16[128,1024]{1,0:T(8,128)(2,1)S(1)} %add_convert_fusion.2), channel_id=1, source_target_pairs={{0,16},{16,0},{1,17},{17,1},{2,18},{18,2},{3,19},{19,3},{4,20},{20... | collective-permute-start | bytes 786440 | tf_op jit(solution)/shard_map/ppermute | solution.py:25
  128.9 22.4 %copy-start.8 = (f32[64,2048]{1,0:T(8,128)S(1)}, f32[64,2048]{1,0:T(8,128)}, u32[]{:S(2)}) copy-start(f32[64,2048]{1,0:T(8,128)} %copy-done.7) | copy-start | bytes 1572868
  128.9 12.1 %collective-permute-start.38 = (bf16[128,2048]{1,0:T(8,128)(2,1)S(1)}, bf16[128,2048]{1,0:T(8,128)(2,1)S(1)}, u32[]{:S(2)}, u32[]{:S(2)}) collective-permute-start(bf16[128,2048]{1,0:T(8,128)(2,1)S(1)} %pad_maximum_fusion.1), channel_id=1, source_target_pairs={{0,4},{4,0},{8,12},{12,8},{1,5},{5,1},{9,13},{13,9},{2,6},{6,2},{1... | collective-permute-start | bytes 1572872 | tf_op jit(solution)/shard_map/ppermute | solution.py:25
  141.1 10.1 %collective-permute-start.39 = (bf16[64,2048]{1,0:T(8,128)(2,1)S(1)}, bf16[64,2048]{1,0:T(8,128)(2,1)S(1)}, u32[]{:S(2)}, u32[]{:S(2)}) collective-permute-start(bf16[64,2048]{1,0:T(8,128)(2,1)S(1)} %slice.144), channel_id=1, source_target_pairs={{0,8},{4,12},{8,0},{12,4},{1,9},{5,13},{9,1},{13,5},{2,10},{6,14},... | collective-permute-start | bytes 786440 | tf_op jit(solution)/shard_map/ppermute | solution.py:25

commit v9 on v8

--- a/solution.py
+++ b/solution.py
@@ -41,7 +41,7 @@
     return lax.optimization_barrier(arrays)
 
 
-def spread_rows(own, coded):
+def spread_rows(own, coded, weight):
     half = own.shape[1] // 2
 
     def both_ways(part):
@@ -55,13 +55,14 @@
     for bits in bits_left[:-1]:
         blocks = blocks + [swap(block, "seq", bits) for block in blocks]
     beyond = [swap(block, "seq", bits_left[-1]) for block in blocks]
-    outer = both_ways(own)
     middle = jnp.concatenate(blocks[1:] + beyond[:-1], axis=0)
-    middle, *outer_corner = ready(middle, *corners(*outer))
+    middle, weight, *outer = ready(middle, weight, *both_ways(own))
+    outer_corner = corners(*outer)
     last, coded = ready(beyond[-1], coded)
     inner = both_ways(middle)
     final = both_ways(last)
-    inner_corner = corners(*inner)
+    by_rep, by_role, *outer_corner = ready(*inner, *outer_corner)
+    inner_corner = corners(by_rep, by_role)
     final_corner = corners(*final)
     groups = [[], [], [], []]
     start = 0
@@ -76,7 +77,7 @@
         groups[2].append((start, half, corner[1]))
         groups[3].append((start, 0, part))
         start += part.shape[0]
-    return groups, coded
+    return groups, coded, weight
 
 
 def added(first, second):
@@ -110,25 +111,26 @@
         low, high = corner[2 * number : 2 * number + 2]
         return swap(low, "role", 1), swap(high, "rep", ACROSS)
 
-    def turned(number, corner_low, corner_high):
+    def sums(number, corner_low, corner_high):
         rows = halves[number]
-        return (
-            swap(added(by_rep[0][rows], corner_low), "rep", ACROSS),
-            swap(added(by_role[1][rows], corner_high), "role", 1),
-        )
+        return added(by_rep[0][rows], corner_low), added(by_role[1][rows], corner_high)
+
+    def turned(low, high):
+        return swap(low, "rep", ACROSS), swap(high, "role", 1)
 
     far_corner, beside_corner = corners(1), corners(0)
-    far = turned(1, *far_corner)
-    *far, corner_low, corner_high = ready(*far, *beside_corner)
+    *far, corner_low, corner_high = ready(*turned(*sums(1, *far_corner)), *beside_corner)
     leaving = merged(halves[1], *far).astype(jnp.bfloat16)
-    *beside, _ = ready(*turned(0, corner_low, corner_high), leaving)
+    *near_sums, leaving = ready(*sums(0, corner_low, corner_high), leaving)
+    beside = turned(*near_sums)
     total = merged(halves[0], *beside)
-    for bits in reversed(seq_bits()):
-        total = total + swap(leaving, "seq", bits).astype(jnp.float32)
-        if bits != seq_bits()[0]:
-            cut = total.shape[0] // 2
-            total, leaving = total[:cut], total[cut:].astype(jnp.bfloat16)
-    return total
+    *later_bits, last_bits = reversed(seq_bits())
+    for bits in later_bits:
+        cut = total.shape[0] // 2
+        far, near = ready(swap(leaving[cut:], "seq", bits), leaving[:cut])
+        leaving = (total[cut:] + far.astype(jnp.float32)).astype(jnp.bfloat16)
+        total = total[:cut] + swap(near, "seq", bits).astype(jnp.float32)
+    return total + swap(leaving, "seq", last_bits).astype(jnp.float32)
 
 
 def prepare_kernel(*refs):
@@ -528,21 +530,20 @@
     both_routes = jnp.stack([line_routes, across[:, 2 * head_dim :]])
     far_routes = swap(both_routes, "role", 1)
     coded = jnp.concatenate([both_routes[1:], far_routes[:1], far_routes[1:], both_routes[:1]])
-    far_gu = swap(w_gateup[0], "rep", PAIR)
     queries = make_queries([normed, across_rows, pair_rows, corner_rows], w_query, q_gain)
     kept, leaving = attend(queries, half_kv, pair_kv, w_out, head_dim)
-    leaving, own_dn = ready(swap(leaving, "rep", PAIR), w_down[0])
+    leaving, own_dn, own_gu = ready(swap(leaving, "rep", PAIR), w_down[0], w_gateup[0])
     halves = kept + leaving
-    far_dn = swap(own_dn, "rep", PAIR)
+    far_dn, far_gu = swap(own_dn, "rep", PAIR), swap(own_gu, "rep", PAIR)
     far_sum = halves[row_count:].astype(jnp.bfloat16)
     across_sum, coded = ready(swap(far_sum, "rep", ACROSS), coded)
     attended = halves[:row_count] + across_sum.astype(jnp.float32)
     mixed = tokens + attended
 
-    mixed, far_gu, far_dn, coded = ready(mixed, far_gu, far_dn, coded)
+    mixed, far_dn, coded = ready(mixed, far_dn, coded)
     moe_in = rms_rows(mixed, moe_gain).astype(jnp.bfloat16)
 
-    rows, coded = spread_rows(moe_in, coded)
+    rows, coded, far_gu = spread_rows(moe_in, coded, far_gu)
     capacity = max(2, 7 * row_count * top_count // (4 * expert_count))
     slots = -(-capacity * (coded.shape[1] // row_count) // 16) * 16
     pick, place, share = make_tables(coded, lax.axis_index(EVERY), slots, top_count)

time: 152 us -> 150 us (0.987)
  waiting for transfers between devices: 78.8 us -> 66.4 us
  starting transfers between devices: 41.9 us -> 52.6 us
    ppermute x40 -> x41, waiting for transfers between devices: 78.8 us -> 66.4 us  [swap(): return lax.ppermute(block, axis, [(i, i ^ bits) for i in range(size)])]
    ppermute x40 -> x41, starting transfers between devices: 41.9 us -> 52.6 us  [swap(): return lax.ppermute(block, axis, [(i, i ^ bits) for i in range(size)])]
  transfers between devices with their start and end apart: 40 -> 41, of which waited for: 21 -> 23; matrix products, arithmetic and copies ran while one was open for 1% -> 2% of each run, Pallas kernels for 18% -> 14%
where the time goes in v9:
time: 150 us
  waiting for transfers between devices  66.4 us (44%)
  starting transfers between devices  52.6 us (35%)
  Pallas kernels  27 us (18%)
  other arithmetic  2.3 us (2%)
  local copies, waits for them, and re-layouts  1.64 us (1%)
    ppermute x41, waiting for transfers between devices, swap(): return lax.ppermute(block, axis, [(i, i ^ bits) for i in range(size)])  66.4 us
    ppermute x41, starting transfers between devices, swap(): return lax.ppermute(block, axis, [(i, i ^ bits) for i in range(size)])  52.6 us
    pallas_call x2, Pallas kernels, run_experts(): pl.pallas_call(lambda *refs: expert_kernel(first, spots, cuts, *refs), ou...  19.2 us
  transfers between devices with their start and end apart: 41, of which 23 were waited for; matrix products, arithmetic and copies ran while one was open for 2% of the time, Pallas kernels for 14%

profile of v9, /device:TPU:0, one launch (start us, length us, event | category | flops | bytes accessed | tf_op | source)
XLA Modules:
  0.0 150.3 jit_solution(15161519210589607095)
XLA Ops:
  0.0 2.6 %prepare.1 = (bf16[64,2048]{1,0:T(8,128)(2,1)S(1)}, bf16[64,640]{1,0:T(8,128)(2,1)S(1)}) custom-call(bf16[64,2048]{1,0:T(8,128)(2,1)} %bitcast.27, f32[1,2048]{1,0:T(1,128)} %bitcast.28, bf16[2,2048,256]{2,1,0:T(8,128)(2,1)} %refs_2_.1, f32[1,128]{1,0:T(1,128)} %bitcast.31, s32[8,64]{1,0:T(8,128)} %bitcast.29, s32[8,64]{1,0:T(8,128)} %bitcast.30), custom_call_target="tpu_custom_call" | custom-call | flops 134217728 | bytes 2621440 | tf_op jit(solution)/shard_map/prepare/pallas_call | solution.py:176
  2.6 5.1 %collective-permute-start.2 = (bf16[64,640]{1,0:T(8,128)(2,1)S(1)}, bf16[64,640]{1,0:T(8,128)(2,1)S(1)}, u32[]{:S(2)}, u32[]{:S(2)}) collective-permute-start(bf16[64,640]{1,0:T(8,128)(2,1)S(1)} %get-tuple-element.71), channel_id=1, source_target_pairs={{0,12},{4,8},{8,4},{12,0},{1,13},{5,9},{9,5},{13,1},{2,14},{6,10},... | collective-permute-start | bytes 245768 | tf_op jit(solution)/shard_map/ppermute | solution.py:25
  7.7 0.6 collective-permute-start
  8.3 1.7 %collective-permute-start.3 = (bf16[64,2048]{1,0:T(8,128)(2,1)S(1)}, bf16[64,2048]{1,0:T(8,128)(2,1)S(1)}, u32[]{:S(2)}, u32[]{:S(2)}) collective-permute-start(bf16[64,2048]{1,0:T(8,128)(2,1)S(1)} %get-tuple-element.70.first_ref), channel_id=1, source_target_pairs={{0,2},{1,3},{2,0},{3,1},{4,6},{5,7},{6,4},{7,5},{8,10},{9,11},{10,... | collective-permute-start | bytes 786440 | tf_op jit(solution)/shard_map/ppermute | solution.py:25
  10.0 3.7 %collective-permute-done = bf16[64,640]{1,0:T(8,128)(2,1)S(1)} collective-permute-done((bf16[64,640]{1,0:T(8,128)(2,1)S(1)}, bf16[64,640]{1,0:T(8,128)(2,1)S(1)}, u32[]{:S(2)}, u32[]{:S(2)}) %collective-permute-start) | collective-permute-done | bytes 81952 | tf_op jit(solution)/shard_map/ppermute | solution.py:25
  14.1 3.0 %collective-permute-done.3.second_ref = bf16[64,2048]{1,0:T(8,128)(2,1)S(1)} collective-permute-done((bf16[64,2048]{1,0:T(8,128)(2,1)S(1)}, bf16[64,2048]{1,0:T(8,128)(2,1)S(1)}, u32[]{:S(2)}, u32[]{:S(2)}) %collective-permute-start.3) | collective-permute-done | bytes 262176 | tf_op jit(solution)/shard_map/ppermute | solution.py:25
  17.1 1.7 %collective-permute-start.6 = (bf16[256,384]{1,0:T(8,128)(2,1)S(1)}, bf16[256,384]{1,0:T(8,128)(2,1)S(1)}, u32[]{:S(2)}, u32[]{:S(2)}) collective-permute-start(bf16[256,384]{1,0:T(8,128)(2,1)S(1)} %pad_maximum_fusion.5), channel_id=1, source_target_pairs={{0,2},{1,3},{2,0},{3,1},{4,6},{5,7},{6,4},{7,5},{8,10},{9,11},{10,... | collective-permute-start | bytes 589832 | tf_op jit(solution)/shard_map/ppermute | solution.py:25
  18.7 4.9 %collective-permute-done.6 = bf16[256,384]{1,0:T(8,128)(2,1)S(1)} collective-permute-done((bf16[256,384]{1,0:T(8,128)(2,1)S(1)}, bf16[256,384]{1,0:T(8,128)(2,1)S(1)}, u32[]{:S(2)}, u32[]{:S(2)}) %collective-permute-start.6) | collective-permute-done | bytes 196640 | tf_op jit(solution)/shard_map/ppermute | solution.py:25
  23.8 0.9 queries.1.refs_0_
  24.6 0.6 collective-permute-done.7.refs_2_
  25.2 2.7 %attend.1 = (f32[128,2048]{1,0:T(8,128)S(1)}, f32[128,2048]{1,0:T(8,128)S(1)}) custom-call(bf16[256,512]{1,0:T(8,128)(2,1)S(1)} %queries.1.refs_0_, bf16[512,256]{1,0:T(8,128)(2,1)S(1)} %pad_maximum_fusion.3.refs_1_, bf16[512,256]{1,0:T(8,128)(2,1)S(1)} %collective-permute-done.7.refs_2_, bf16[512,2048]{1,0:T(8,128)(2,1)S(1)} %copy-done.2), custom_call_target="tpu_custom_call" | custom-call | flops 1073741824 | bytes 4194304 | tf_op jit(solution)/shard_map/attend/pallas_call | solution.py:255
  28.2 2.5 %collective-permute-done.8 = f32[128,2048]{1,0:T(8,128)S(1)} collective-permute-done((f32[128,2048]{1,0:T(8,128)S(1)}, f32[128,2048]{1,0:T(8,128)S(1)}, u32[]{:S(2)}, u32[]{:S(2)}) %collective-permute-start.8) | collective-permute-done | bytes 1048608 | tf_op jit(solution)/shard_map/ppermute | solution.py:25
  30.8 0.4 collective-permute-start.11
  31.4 1.7 %collective-permute-start.9 = (bf16[64,2048]{1,0:T(8,128)(2,1)S(1)}, bf16[64,2048]{1,0:T(8,128)(2,1)S(1)}, u32[]{:S(2)}, u32[]{:S(2)}) collective-permute-start(bf16[64,2048]{1,0:T(8,128)(2,1)S(1)} %slice.157), channel_id=1, source_target_pairs={{0,2},{1,3},{2,0},{3,1},{4,6},{5,7},{6,4},{7,5},{8,10},{9,11},{10,... | collective-permute-start | bytes 786440 | tf_op jit(solution)/shard_map/ppermute | solution.py:25
  33.1 1.6 %collective-permute-start.10 = (bf16[2,256,128]{2,1,0:T(8,128)(2,1)S(1)}, bf16[2,256,128]{2,1,0:T(8,128)(2,1)S(1)}, u32[]{:S(2)}, u32[]{:S(2)}) collective-permute-start(bf16[2,256,128]{2,1,0:T(8,128)(2,1)S(1)} %pad_maximum_fusion.6), channel_id=1, source_target_pairs={{0,16},{16,0},{1,17},{17,1},{2,18},{18,2},{3,19},{19,3},{4,20},{20... | collective-permute-start | bytes 393224 | tf_op jit(solution)/shard_map/ppermute | solution.py:25
  34.7 3.8 %collective-permute-done.10 = bf16[2,256,128]{2,1,0:T(8,128)(2,1)S(1)} collective-permute-done((bf16[2,256,128]{2,1,0:T(8,128)(2,1)S(1)}, bf16[2,256,128]{2,1,0:T(8,128)(2,1)S(1)}, u32[]{:S(2)}, u32[]{:S(2)}) %collective-permute-start.10) | collective-permute-done | bytes 131104 | tf_op jit(solution)/shard_map/ppermute | solution.py:25
  38.5 1.3 collective-permute-done.9
  39.9 4.7 %collective-permute-done.11.refs_6_ = bf16[768,2048]{1,0:T(8,128)(2,1)S(1)} collective-permute-done((bf16[768,2048]{1,0:T(8,128)(2,1)}, bf16[768,2048]{1,0:T(8,128)(2,1)S(1)}, u32[]{:S(2)}, u32[]{:S(2)}) %collective-permute-start.11) | collective-permute-done | bytes 3145760 | tf_op jit(solution)/shard_map/ppermute | solution.py:25
  44.8 2.4 %collective-permute-start.12 = (bf16[64,2048]{1,0:T(8,128)(2,1)S(1)}, bf16[64,2048]{1,0:T(8,128)(2,1)S(1)}, u32[]{:S(2)}, u32[]{:S(2)}) collective-permute-start(bf16[64,2048]{1,0:T(8,128)(2,1)S(1)} %multiply_convert_fusion.refs_13_), channel_id=1, source_target_pairs={{0,8},{4,12},{8,0},{12,4},{1,9},{5,13},{9,1},{13,5},{2,10},{6,14},... | collective-permute-start | bytes 786440 | tf_op jit(solution)/shard_map/ppermute | solution.py:25
  47.2 2.0 %collective-permute-start.14 = (bf16[64,2048]{1,0:T(8,128)(2,1)S(1)}, bf16[64,2048]{1,0:T(8,128)(2,1)S(1)}, u32[]{:S(2)}, u32[]{:S(2)}) collective-permute-start(bf16[64,2048]{1,0:T(8,128)(2,1)S(1)} %multiply_convert_fusion.refs_13_), channel_id=1, source_target_pairs={{0,4},{4,0},{8,12},{12,8},{1,5},{5,1},{9,13},{13,9},{2,6},{6,2},{1... | collective-permute-start | bytes 786440 | tf_op jit(solution)/shard_map/ppermute | solution.py:25
  49.2 1.5 %collective-permute-start.17 = (bf16[64,2048]{1,0:T(8,128)(2,1)S(1)}, bf16[64,2048]{1,0:T(8,128)(2,1)S(1)}, u32[]{:S(2)}, u32[]{:S(2)}) collective-permute-start(bf16[64,2048]{1,0:T(8,128)(2,1)S(1)} %multiply_convert_fusion.refs_13_), channel_id=1, source_target_pairs={{0,16},{16,0},{1,17},{17,1},{2,18},{18,2},{3,19},{19,3},{4,20},{20... | collective-permute-start | bytes 786440 | tf_op jit(solution)/shard_map/ppermute | solution.py:25
  50.7 1.5 %collective-permute-start.16 = (bf16[64,2048]{1,0:T(8,128)(2,1)S(1)}, bf16[64,2048]{1,0:T(8,128)(2,1)S(1)}, u32[]{:S(2)}, u32[]{:S(2)}) collective-permute-start(bf16[64,2048]{1,0:T(8,128)(2,1)S(1)} %multiply_convert_fusion.refs_13_), channel_id=1, source_target_pairs={{0,2},{1,3},{2,0},{3,1},{4,6},{5,7},{6,4},{7,5},{8,10},{9,11},{10,... | collective-permute-start | bytes 786440 | tf_op jit(solution)/shard_map/ppermute | solution.py:25
  52.3 7.8 %collective-permute-done.12 = bf16[64,2048]{1,0:T(8,128)(2,1)S(1)} collective-permute-done((bf16[64,2048]{1,0:T(8,128)(2,1)S(1)}, bf16[64,2048]{1,0:T(8,128)(2,1)S(1)}, u32[]{:S(2)}, u32[]{:S(2)}) %collective-permute-start.12) | collective-permute-done | bytes 262176 | tf_op jit(solution)/shard_map/ppermute | solution.py:25
  60.1 0.3 collective-permute-start.13
  60.5 1.6 %collective-permute-start.20 = (bf16[128,2048]{1,0:T(8,128)(2,1)S(1)}, bf16[128,2048]{1,0:T(8,128)(2,1)S(1)}, u32[]{:S(2)}, u32[]{:S(2)}) collective-permute-start(bf16[128,2048]{1,0:T(8,128)(2,1)S(1)} %pad_maximum_fusion.1.refs_14_), channel_id=1, source_target_pairs={{0,16},{16,0},{1,17},{17,1},{2,18},{18,2},{3,19},{19,3},{4,20},{20... | collective-permute-start | bytes 1572872 | tf_op jit(solution)/shard_map/ppermute | solution.py:25
  62.1 1.5 %collective-permute-start.18 = (bf16[128,2048]{1,0:T(8,128)(2,1)S(1)}, bf16[128,2048]{1,0:T(8,128)(2,1)S(1)}, u32[]{:S(2)}, u32[]{:S(2)}) collective-permute-start(bf16[128,2048]{1,0:T(8,128)(2,1)S(1)} %pad_maximum_fusion.1.refs_14_), channel_id=1, source_target_pairs={{0,2},{1,3},{2,0},{3,1},{4,6},{5,7},{6,4},{7,5},{8,10},{9,11},{10,... | collective-permute-start | bytes 1572872 | tf_op jit(solution)/shard_map/ppermute | solution.py:25
  63.6 4.2 %collective-permute-done.13.refs_15_ = bf16[64,2048]{1,0:T(8,128)(2,1)S(1)} collective-permute-done((bf16[64,2048]{1,0:T(8,128)(2,1)S(1)}, bf16[64,2048]{1,0:T(8,128)(2,1)S(1)}, u32[]{:S(2)}, u32[]{:S(2)}) %collective-permute-start.13) | collective-permute-done | bytes 262176 | tf_op jit(solution)/shard_map/ppermute | solution.py:25
  67.8 1.6 %collective-permute-start.21 = (bf16[64,2048]{1,0:T(8,128)(2,1)S(1)}, bf16[64,2048]{1,0:T(8,128)(2,1)S(1)}, u32[]{:S(2)}, u32[]{:S(2)}) collective-permute-start(bf16[64,2048]{1,0:T(8,128)(2,1)S(1)} %collective-permute-done.13.refs_15_), channel_id=1, source_target_pairs={{0,16},{16,0},{1,17},{17,1},{2,18},{18,2},{3,19},{19,3},{4,20},{20... | collective-permute-start | bytes 786440 | tf_op jit(solution)/shard_map/ppermute | solution.py:25
  69.5 1.5 %collective-permute-start.19 = (bf16[64,2048]{1,0:T(8,128)(2,1)S(1)}, bf16[64,2048]{1,0:T(8,128)(2,1)S(1)}, u32[]{:S(2)}, u32[]{:S(2)}) collective-permute-start(bf16[64,2048]{1,0:T(8,128)(2,1)S(1)} %collective-permute-done.13.refs_15_), channel_id=1, source_target_pairs={{0,2},{1,3},{2,0},{3,1},{4,6},{5,7},{6,4},{7,5},{8,10},{9,11},{10,... | collective-permute-start | bytes 786440 | tf_op jit(solution)/shard_map/ppermute | solution.py:25
  71.0 0.7 slice.90
  71.7 0.7 slice.91
  72.3 0.5 collective-permute-start.23
  72.8 6.9 %collective-permute-done.21.refs_12_ = bf16[64,2048]{1,0:T(8,128)(2,1)S(1)} collective-permute-done((bf16[64,2048]{1,0:T(8,128)(2,1)S(1)}, bf16[64,2048]{1,0:T(8,128)(2,1)S(1)}, u32[]{:S(2)}, u32[]{:S(2)}) %collective-permute-start.21) | collective-permute-done | bytes 262176 | tf_op jit(solution)/shard_map/ppermute | solution.py:25
  79.8 1.5 collective-permute-start.22
  81.3 1.6 %tables.1 = (bf16[4,224,256]{2,1,0:T(8,128)(2,1)S(1)}, bf16[2,4,256,112]{3,2,1,0:T(8,128)(2,1)S(1)}, f32[4,256,2]{2,1,0:T(8,128)S(1)}) custom-call(s32[1]{0:T(128)} %bitcast.12.refs_0_, bf16[4,256,128]{2,1,0:T(8,128)(2,1)S(1)} %pad_maximum_fusion.4.refs_1_), custom_call_target="tpu_custom_call" | custom-call | flops 134217728 | bytes 917504 | tf_op jit(solution)/shard_map/tables/pallas_call | solution.py:318
  82.9 1.6 %collective-permute-start.27 = (bf16[64,1024]{1,0:T(8,128)(2,1)S(1)}, bf16[64,1024]{1,0:T(8,128)(2,1)S(1)}, u32[]{:S(2)}, u32[]{:S(2)}) collective-permute-start(bf16[64,1024]{1,0:T(8,128)(2,1)S(1)} %slice.118), channel_id=1, source_target_pairs={{0,2},{1,3},{2,0},{3,1},{4,6},{5,7},{6,4},{7,5},{8,10},{9,11},{10,... | collective-permute-start | bytes 393224 | tf_op jit(solution)/shard_map/ppermute | solution.py:25
  84.5 0.6 collective-permute-start.26
  85.2 1.6 %collective-permute-start.25 = (bf16[128,1024]{1,0:T(8,128)(2,1)S(1)}, bf16[128,1024]{1,0:T(8,128)(2,1)S(1)}, u32[]{:S(2)}, u32[]{:S(2)}) collective-permute-start(bf16[128,1024]{1,0:T(8,128)(2,1)S(1)} %slice.93), channel_id=1, source_target_pairs={{0,2},{1,3},{2,0},{3,1},{4,6},{5,7},{6,4},{7,5},{8,10},{9,11},{10,... | collective-permute-start | bytes 786440 | tf_op jit(solution)/shard_map/ppermute | solution.py:25
  86.8 2.5 %collective-permute-start.24 = (bf16[128,1024]{1,0:T(8,128)(2,1)S(1)}, bf16[128,1024]{1,0:T(8,128)(2,1)S(1)}, u32[]{:S(2)}, u32[]{:S(2)}) collective-permute-start(bf16[128,1024]{1,0:T(8,128)(2,1)S(1)} %slice.92), channel_id=1, source_target_pairs={{0,16},{16,0},{1,17},{17,1},{2,18},{18,2},{3,19},{19,3},{4,20},{20... | collective-permute-start | bytes 786440 | tf_op jit(solution)/shard_map/ppermute | solution.py:25
  89.3 9.5 %experts.2 = (bf16[256,1024]{1,0:T(8,128)(2,1)S(1)}, bf16[256,1024]{1,0:T(8,128)(2,1)S(1)}, bf16[256,1024]{1,0:T(8,128)(2,1)S(1)}, bf16[256,1024]{1,0:T(8,128)(2,1)S(1)}) custom-call(bf16[4,224,256]{2,1,0:T(8,128)(2,1)S(1)} %get-tuple-element.84.refs_0_, bf16[2,4,256,112]{3,2,1,0:T(8,128)(2,1)S(1)} %get-tuple-element.85.refs_1_, ...), custom_call_target="tpu_custom_call" | custom-call | flops 4227858432 | bytes 23068672 | tf_op jit(solution)/shard_map/experts/pallas_call | solution.py:448
  99.2 9.8 %experts.3 = (bf16[128,1024]{1,0:T(8,128)(2,1)S(1)}, bf16[128,1024]{1,0:T(8,128)(2,1)S(1)}, bf16[128,1024]{1,0:T(8,128)(2,1)S(1)}, bf16[128,1024]{1,0:T(8,128)(2...) custom-call(bf16[4,224,256]{2,1,0:T(8,128)(2,1)S(1)} %get-tuple-element.84.refs_0_, ...), custom_call_target="tpu_custom_call" | custom-call | flops 4227858432 | bytes 23068672 | tf_op jit(solution)/shard_map/experts/pallas_call | solution.py:448
  108.9 0.7 collective-permute-done.28
  109.6 1.7 %collective-permute-start.30 = (bf16[128,1024]{1,0:T(8,128)(2,1)S(1)}, bf16[128,1024]{1,0:T(8,128)(2,1)S(1)}, u32[]{:S(2)}, u32[]{:S(2)}) collective-permute-start(bf16[128,1024]{1,0:T(8,128)(2,1)S(1)} %get-tuple-element.119), channel_id=1, source_target_pairs={{0,16},{16,0},{1,17},{17,1},{2,18},{18,2},{3,19},{19,3},{4,20},{20... | collective-permute-start | bytes 786440 | tf_op jit(solution)/shard_map/ppermute | solution.py:25
  111.3 1.5 collective-permute-start.32
  112.9 0.8 collective-permute-start.35
  113.6 5.2 %collective-permute-done.30 = bf16[128,1024]{1,0:T(8,128)(2,1)S(1)} collective-permute-done((bf16[128,1024]{1,0:T(8,128)(2,1)S(1)}, bf16[128,1024]{1,0:T(8,128)(2,1)S(1)}, u32[]{:S(2)}, u32[]{:S(2)}) %collective-permute-start.30) | collective-permute-done | bytes 262176 | tf_op jit(solution)/shard_map/ppermute | solution.py:25
  118.9 1.1 collective-permute-start.31
  120.0 0.6 collective-permute-done.32
  120.7 1.6 %collective-permute-start.33 = (bf16[128,1024]{1,0:T(8,128)(2,1)S(1)}, bf16[128,1024]{1,0:T(8,128)(2,1)S(1)}, u32[]{:S(2)}, u32[]{:S(2)}) collective-permute-start(bf16[128,1024]{1,0:T(8,128)(2,1)S(1)} %add_convert_fusion.4), channel_id=1, source_target_pairs={{0,16},{16,0},{1,17},{17,1},{2,18},{18,2},{3,19},{19,3},{4,20},{20... | collective-permute-start | bytes 786440 | tf_op jit(solution)/shard_map/ppermute | solution.py:25
  122.2 0.7 collective-permute-done.34
  123.0 0.5 collective-permute-done.35
  123.5 3.9 %collective-permute-done.31 = bf16[128,1024]{1,0:T(8,128)(2,1)S(1)} collective-permute-done((bf16[128,1024]{1,0:T(8,128)(2,1)S(1)}, bf16[128,1024]{1,0:T(8,128)(2,1)S(1)}, u32[]{:S(2)}, u32[]{:S(2)}) %collective-permute-start.31) | collective-permute-done | bytes 262176 | tf_op jit(solution)/shard_map/ppermute | solution.py:25
  127.4 1.4 collective-permute-done.33
  129.0 0.3 add_convert_fusion
  129.4 0.8 collective-permute-start.38
  130.1 0.7 collective-permute-start.36
  130.9 1.8 %collective-permute-start.37 = (bf16[128,1024]{1,0:T(8,128)(2,1)S(1)}, bf16[128,1024]{1,0:T(8,128)(2,1)S(1)}, u32[]{:S(2)}, u32[]{:S(2)}) collective-permute-start(bf16[128,1024]{1,0:T(8,128)(2,1)S(1)} %get-tuple-element.131), channel_id=1, source_target_pairs={{0,16},{16,0},{1,17},{17,1},{2,18},{18,2},{3,19},{19,3},{4,20},{20... | collective-permute-start | bytes 786440 | tf_op jit(solution)/shard_map/ppermute | solution.py:25
  132.6 4.2 %collective-permute-done.38 = bf16[64,2048]{1,0:T(8,128)(2,1)S(1)} collective-permute-done((bf16[64,2048]{1,0:T(8,128)(2,1)S(1)}, bf16[64,2048]{1,0:T(8,128)(2,1)S(1)}, u32[]{:S(2)}, u32[]{:S(2)}) %collective-permute-start.38) | collective-permute-done | bytes 262176 | tf_op jit(solution)/shard_map/ppermute | solution.py:25
  136.9 0.3 collective-permute-done.37
  137.4 4.5 %collective-permute-start.40 = (bf16[64,2048]{1,0:T(8,128)(2,1)S(1)}, bf16[64,2048]{1,0:T(8,128)(2,1)S(1)}, u32[]{:S(2)}, u32[]{:S(2)}) collective-permute-start(bf16[64,2048]{1,0:T(8,128)(2,1)S(1)} %fusion.6), channel_id=1, source_target_pairs={{0,8},{4,12},{8,0},{12,4},{1,9},{5,13},{9,1},{13,5},{2,10},{6,14},... | collective-permute-start | bytes 786440 | tf_op jit(solution)/shard_map/ppermute | solution.py:25
  141.9 2.4 %collective-permute-start.39 = (bf16[64,2048]{1,0:T(8,128)(2,1)S(1)}, bf16[64,2048]{1,0:T(8,128)(2,1)S(1)}, u32[]{:S(2)}, u32[]{:S(2)}) collective-permute-start(bf16[64,2048]{1,0:T(8,128)(2,1)S(1)} %get-tuple-element.133), channel_id=1, source_target_pairs={{0,4},{4,0},{8,12},{12,8},{1,5},{5,1},{9,13},{13,9},{2,6},{6,2},{1... | collective-permute-start | bytes 786440 | tf_op jit(solution)/shard_map/ppermute | solution.py:25
  144.3 4.9 %collective-permute-done.40 = bf16[64,2048]{1,0:T(8,128)(2,1)S(1)} collective-permute-done((bf16[64,2048]{1,0:T(8,128)(2,1)S(1)}, bf16[64,2048]{1,0:T(8,128)(2,1)S(1)}, u32[]{:S(2)}, u32[]{:S(2)}) %collective-permute-start.40) | collective-permute-done | bytes 262176 | tf_op jit(solution)/shard_map/ppermute | solution.py:25
  149.2 0.4 collective-permute-done.39
  149.5 0.8 fusion.8
  (78 shorter events, 2.6 us)
Async XLA Ops:
  0.0 23.7 %copy-start.1 = (f32[128]{0:T(128)S(1)}, f32[128]{0:T(128)}, u32[]{:S(2)}) copy-start(f32[128]{0:T(128)} %param.16) | copy-start | bytes 1540
  0.0 23.7 %copy-start = (bf16[2048,512]{1,0:T(8,128)(2,1)S(1)}, bf16[2048,512]{1,0:T(8,128)(2,1)}, u32[]{:S(2)}) copy-start(bf16[2048,512]{1,0:T(8,128)(2,1)} %weight_ref.1) | copy-start | bytes 6291460
  2.6 11.4 %collective-permute-start.2 = (bf16[64,640]{1,0:T(8,128)(2,1)S(1)}, bf16[64,640]{1,0:T(8,128)(2,1)S(1)}, u32[]{:S(2)}, u32[]{:S(2)}) collective-permute-start(bf16[64,640]{1,0:T(8,128)(2,1)S(1)} %get-tuple-element.71), channel_id=1, source_target_pairs={{0,12},{4,8},{8,4},{12,0},{1,13},{5,9},{9,5},{13,1},{2,14},{6,10},... | collective-permute-start | bytes 245768 | tf_op jit(solution)/shard_map/ppermute | solution.py:25
  7.7 6.2 %collective-permute-start.1 = (bf16[64,640]{1,0:T(8,128)(2,1)S(1)}, bf16[64,640]{1,0:T(8,128)(2,1)S(1)}, u32[]{:S(2)}, u32[]{:S(2)}) collective-permute-start(bf16[64,640]{1,0:T(8,128)(2,1)S(1)} %get-tuple-element.71), channel_id=1, source_target_pairs={{0,4},{4,0},{8,12},{12,8},{1,5},{5,1},{9,13},{13,9},{2,6},{6,2},{1... | collective-permute-start | bytes 245768 | tf_op jit(solution)/shard_map/ppermute | solution.py:25
  7.7 6.0 %collective-permute-start = (bf16[64,640]{1,0:T(8,128)(2,1)S(1)}, bf16[64,640]{1,0:T(8,128)(2,1)S(1)}, u32[]{:S(2)}, u32[]{:S(2)}) collective-permute-start(bf16[64,640]{1,0:T(8,128)(2,1)S(1)} %get-tuple-element.71), channel_id=1, source_target_pairs={{0,8},{4,12},{8,0},{12,4},{1,9},{5,13},{9,1},{13,5},{2,10},{6,14},... | collective-permute-start | bytes 245768 | tf_op jit(solution)/shard_map/ppermute | solution.py:25
  8.3 5.7 %collective-permute-start.4 = (bf16[64,2048]{1,0:T(8,128)(2,1)S(1)}, bf16[64,2048]{1,0:T(8,128)(2,1)S(1)}, u32[]{:S(2)}, u32[]{:S(2)}) collective-permute-start(bf16[64,2048]{1,0:T(8,128)(2,1)S(1)} %get-tuple-element.70.first_ref), channel_id=1, source_target_pairs={{0,1},{1,0},{2,3},{3,2},{4,5},{5,4},{6,7},{7,6},{8,9},{9,8},{10,11... | collective-permute-start | bytes 786440 | tf_op jit(solution)/shard_map/ppermute | solution.py:25
  8.3 8.7 %collective-permute-start.3 = (bf16[64,2048]{1,0:T(8,128)(2,1)S(1)}, bf16[64,2048]{1,0:T(8,128)(2,1)S(1)}, u32[]{:S(2)}, u32[]{:S(2)}) collective-permute-start(bf16[64,2048]{1,0:T(8,128)(2,1)S(1)} %get-tuple-element.70.first_ref), channel_id=1, source_target_pairs={{0,2},{1,3},{2,0},{3,1},{4,6},{5,7},{6,4},{7,5},{8,10},{9,11},{10,... | collective-permute-start | bytes 786440 | tf_op jit(solution)/shard_map/ppermute | solution.py:25
  10.0 15.2 %copy-start.2 = (bf16[512,2048]{1,0:T(8,128)(2,1)S(1)}, bf16[512,2048]{1,0:T(8,128)(2,1)}, u32[]{:S(2)}) copy-start(bf16[512,2048]{1,0:T(8,128)(2,1)} %refs_3_.1) | copy-start | bytes 6291460
  17.1 6.5 %collective-permute-start.6 = (bf16[256,384]{1,0:T(8,128)(2,1)S(1)}, bf16[256,384]{1,0:T(8,128)(2,1)S(1)}, u32[]{:S(2)}, u32[]{:S(2)}) collective-permute-start(bf16[256,384]{1,0:T(8,128)(2,1)S(1)} %pad_maximum_fusion.5), channel_id=1, source_target_pairs={{0,2},{1,3},{2,0},{3,1},{4,6},{5,7},{6,4},{7,5},{8,10},{9,11},{10,... | collective-permute-start | bytes 589832 | tf_op jit(solution)/shard_map/ppermute | solution.py:25
  18.7 5.0 %collective-permute-start.5 = (bf16[64,2048]{1,0:T(8,128)(2,1)S(1)}, bf16[64,2048]{1,0:T(8,128)(2,1)S(1)}, u32[]{:S(2)}, u32[]{:S(2)}) collective-permute-start(bf16[64,2048]{1,0:T(8,128)(2,1)S(1)} %collective-permute-done.3.second_ref), channel_id=1, source_target_pairs={{0,1},{1,0},{2,3},{3,2},{4,5},{5,4},{6,7},{7,6},{8,9},{9,8},{10,11... | collective-permute-start | bytes 786440 | tf_op jit(solution)/shard_map/ppermute | solution.py:25
  23.6 1.6 %collective-permute-start.7 = (bf16[512,256]{1,0:T(8,128)(2,1)S(1)}, bf16[512,256]{1,0:T(8,128)(2,1)S(1)}, u32[]{:S(2)}, u32[]{:S(2)}) collective-permute-start(bf16[512,256]{1,0:T(8,128)(2,1)S(1)} %pad_maximum_fusion.3.refs_1_), channel_id=1, source_target_pairs={{0,1},{1,0},{2,3},{3,2},{4,5},{5,4},{6,7},{7,6},{8,9},{9,8},{10,11... | collective-permute-start | bytes 786440 | tf_op jit(solution)/shard_map/ppermute | solution.py:25
  23.7 7.0 %copy-start.3 = (bf16[1,2048,1536]{2,1,0:T(8,128)(2,1)S(1)}, bf16[1,2048,1536]{2,1,0:T(8,128)(2,1)}, u32[]{:S(2)}) copy-start(bf16[1,2048,1536]{2,1,0:T(8,128)(2,1)} %param.22) | copy-start | bytes 18874372
  28.0 11.8 %copy-start.8 = (bf16[1,64,2048]{2,1,0:T(8,128)(2,1)S(1)}, bf16[1,64,2048]{2,1,0:T(8,128)(2,1)}, u32[]{:S(2)}) copy-start(bf16[1,64,2048]{2,1,0:T(8,128)(2,1)} %param.12) | copy-start | bytes 786436
  28.0 2.7 %collective-permute-start.8 = (f32[128,2048]{1,0:T(8,128)S(1)}, f32[128,2048]{1,0:T(8,128)S(1)}, u32[]{:S(2)}, u32[]{:S(2)}) collective-permute-start(f32[128,2048]{1,0:T(8,128)S(1)} %get-tuple-element.76), channel_id=1, source_target_pairs={{0,1},{1,0},{2,3},{3,2},{4,5},{5,4},{6,7},{7,6},{8,9},{9,8},{10,11... | collective-permute-start | bytes 3145736 | tf_op jit(solution)/shard_map/ppermute | solution.py:25
  30.7 29.8 %collective-permute-start.15 = (bf16[2048,1536]{1,0:T(8,128)(2,1)S(1)}, bf16[2048,1536]{1,0:T(8,128)(2,1)S(1)}, u32[]{:S(2)}, u32[]{:S(2)}) collective-permute-start(bf16[2048,1536]{1,0:T(8,128)(2,1)S(1)} %bitcast.23), channel_id=1, source_target_pairs={{0,1},{1,0},{2,3},{3,2},{4,5},{5,4},{6,7},{7,6},{8,9},{9,8},{10,11... | collective-permute-start | bytes 18874376 | tf_op jit(solution)/shard_map/ppermute | solution.py:25
  30.8 13.7 %collective-permute-start.11 = (bf16[768,2048]{1,0:T(8,128)(2,1)}, bf16[768,2048]{1,0:T(8,128)(2,1)S(1)}, u32[]{:S(2)}, u32[]{:S(2)}) collective-permute-start(bf16[768,2048]{1,0:T(8,128)(2,1)} %bitcast.24), channel_id=1, source_target_pairs={{0,1},{1,0},{2,3},{3,2},{4,5},{5,4},{6,7},{7,6},{8,9},{9,8},{10,11... | collective-permute-start | bytes 9437192 | tf_op jit(solution)/shard_map/ppermute | solution.py:25
  31.2 13.5 %copy-start.9 = (f32[2048]{0:T(1024)S(1)}, f32[2048]{0:T(1024)}, u32[]{:S(2)}) copy-start(f32[2048]{0:T(1024)} %param.19) | copy-start | bytes 24580
  31.4 8.4 %collective-permute-start.9 = (bf16[64,2048]{1,0:T(8,128)(2,1)S(1)}, bf16[64,2048]{1,0:T(8,128)(2,1)S(1)}, u32[]{:S(2)}, u32[]{:S(2)}) collective-permute-start(bf16[64,2048]{1,0:T(8,128)(2,1)S(1)} %slice.157), channel_id=1, source_target_pairs={{0,2},{1,3},{2,0},{3,1},{4,6},{5,7},{6,4},{7,5},{8,10},{9,11},{10,... | collective-permute-start | bytes 786440 | tf_op jit(solution)/shard_map/ppermute | solution.py:25
  33.1 5.3 %collective-permute-start.10 = (bf16[2,256,128]{2,1,0:T(8,128)(2,1)S(1)}, bf16[2,256,128]{2,1,0:T(8,128)(2,1)S(1)}, u32[]{:S(2)}, u32[]{:S(2)}) collective-permute-start(bf16[2,256,128]{2,1,0:T(8,128)(2,1)S(1)} %pad_maximum_fusion.6), channel_id=1, source_target_pairs={{0,16},{16,0},{1,17},{17,1},{2,18},{18,2},{3,19},{19,3},{4,20},{20... | collective-permute-start | bytes 393224 | tf_op jit(solution)/shard_map/ppermute | solution.py:25
  39.9 7.3 %copy-start.6 = (f32[64,2048]{1,0:T(8,128)}, f32[64,2048]{1,0:T(8,128)S(1)}, u32[]{:S(2)}) copy-start(f32[64,2048]{1,0:T(8,128)S(1)} %fusion.7) | copy-start | bytes 1572868
  44.6 35.2 %copy-start.5 = (bf16[768,2048]{1,0:T(8,128)(2,1)}, bf16[768,2048]{1,0:T(8,128)(2,1)S(1)}, u32[]{:S(2)}) copy-start(bf16[768,2048]{1,0:T(8,128)(2,1)S(1)} %collective-permute-done.11.refs_6_) | copy-start | bytes 9437188
  44.8 15.3 %collective-permute-start.12 = (bf16[64,2048]{1,0:T(8,128)(2,1)S(1)}, bf16[64,2048]{1,0:T(8,128)(2,1)S(1)}, u32[]{:S(2)}, u32[]{:S(2)}) collective-permute-start(bf16[64,2048]{1,0:T(8,128)(2,1)S(1)} %multiply_convert_fusion.refs_13_), channel_id=1, source_target_pairs={{0,8},{4,12},{8,0},{12,4},{1,9},{5,13},{9,1},{13,5},{2,10},{6,14},... | collective-permute-start | bytes 786440 | tf_op jit(solution)/shard_map/ppermute | solution.py:25
  47.2 13.2 %collective-permute-start.14 = (bf16[64,2048]{1,0:T(8,128)(2,1)S(1)}, bf16[64,2048]{1,0:T(8,128)(2,1)S(1)}, u32[]{:S(2)}, u32[]{:S(2)}) collective-permute-start(bf16[64,2048]{1,0:T(8,128)(2,1)S(1)} %multiply_convert_fusion.refs_13_), channel_id=1, source_target_pairs={{0,4},{4,0},{8,12},{12,8},{1,5},{5,1},{9,13},{13,9},{2,6},{6,2},{1... | collective-permute-start | bytes 786440 | tf_op jit(solution)/shard_map/ppermute | solution.py:25
  49.2 11.2 %collective-permute-start.17 = (bf16[64,2048]{1,0:T(8,128)(2,1)S(1)}, bf16[64,2048]{1,0:T(8,128)(2,1)S(1)}, u32[]{:S(2)}, u32[]{:S(2)}) collective-permute-start(bf16[64,2048]{1,0:T(8,128)(2,1)S(1)} %multiply_convert_fusion.refs_13_), channel_id=1, source_target_pairs={{0,16},{16,0},{1,17},{17,1},{2,18},{18,2},{3,19},{19,3},{4,20},{20... | collective-permute-start | bytes 786440 | tf_op jit(solution)/shard_map/ppermute | solution.py:25
  50.7 9.7 %collective-permute-start.16 = (bf16[64,2048]{1,0:T(8,128)(2,1)S(1)}, bf16[64,2048]{1,0:T(8,128)(2,1)S(1)}, u32[]{:S(2)}, u32[]{:S(2)}) collective-permute-start(bf16[64,2048]{1,0:T(8,128)(2,1)S(1)} %multiply_convert_fusion.refs_13_), channel_id=1, source_target_pairs={{0,2},{1,3},{2,0},{3,1},{4,6},{5,7},{6,4},{7,5},{8,10},{9,11},{10,... | collective-permute-start | bytes 786440 | tf_op jit(solution)/shard_map/ppermute | solution.py:25
  60.1 7.7 %collective-permute-start.13 = (bf16[64,2048]{1,0:T(8,128)(2,1)S(1)}, bf16[64,2048]{1,0:T(8,128)(2,1)S(1)}, u32[]{:S(2)}, u32[]{:S(2)}) collective-permute-start(bf16[64,2048]{1,0:T(8,128)(2,1)S(1)} %collective-permute-done.12), channel_id=1, source_target_pairs={{0,4},{4,0},{8,12},{12,8},{1,5},{5,1},{9,13},{13,9},{2,6},{6,2},{1... | collective-permute-start | bytes 786440 | tf_op jit(solution)/shard_map/ppermute | solution.py:25
  60.5 19.3 %copy-start.4 = (bf16[2048,1536]{1,0:T(8,128)(2,1)}, bf16[2048,1536]{1,0:T(8,128)(2,1)S(1)}, u32[]{:S(2)}) copy-start(bf16[2048,1536]{1,0:T(8,128)(2,1)S(1)} %collective-permute-done.15.refs_4_) | copy-start | bytes 18874372
  60.5 24.6 %collective-permute-start.20 = (bf16[128,2048]{1,0:T(8,128)(2,1)S(1)}, bf16[128,2048]{1,0:T(8,128)(2,1)S(1)}, u32[]{:S(2)}, u32[]{:S(2)}) collective-permute-start(bf16[128,2048]{1,0:T(8,128)(2,1)S(1)} %pad_maximum_fusion.1.refs_14_), channel_id=1, source_target_pairs={{0,16},{16,0},{1,17},{17,1},{2,18},{18,2},{3,19},{19,3},{4,20},{20... | collective-permute-start | bytes 1572872 | tf_op jit(solution)/shard_map/ppermute | solution.py:25
  62.1 23.0 %collective-permute-start.18 = (bf16[128,2048]{1,0:T(8,128)(2,1)S(1)}, bf16[128,2048]{1,0:T(8,128)(2,1)S(1)}, u32[]{:S(2)}, u32[]{:S(2)}) collective-permute-start(bf16[128,2048]{1,0:T(8,128)(2,1)S(1)} %pad_maximum_fusion.1.refs_14_), channel_id=1, source_target_pairs={{0,2},{1,3},{2,0},{3,1},{4,6},{5,7},{6,4},{7,5},{8,10},{9,11},{10,... | collective-permute-start | bytes 1572872 | tf_op jit(solution)/shard_map/ppermute | solution.py:25
  67.8 12.0 %collective-permute-start.21 = (bf16[64,2048]{1,0:T(8,128)(2,1)S(1)}, bf16[64,2048]{1,0:T(8,128)(2,1)S(1)}, u32[]{:S(2)}, u32[]{:S(2)}) collective-permute-start(bf16[64,2048]{1,0:T(8,128)(2,1)S(1)} %collective-permute-done.13.refs_15_), channel_id=1, source_target_pairs={{0,16},{16,0},{1,17},{17,1},{2,18},{18,2},{3,19},{19,3},{4,20},{20... | collective-permute-start | bytes 786440 | tf_op jit(solution)/shard_map/ppermute | solution.py:25
  69.5 13.4 %collective-permute-start.19 = (bf16[64,2048]{1,0:T(8,128)(2,1)S(1)}, bf16[64,2048]{1,0:T(8,128)(2,1)S(1)}, u32[]{:S(2)}, u32[]{:S(2)}) collective-permute-start(bf16[64,2048]{1,0:T(8,128)(2,1)S(1)} %collective-permute-done.13.refs_15_), channel_id=1, source_target_pairs={{0,2},{1,3},{2,0},{3,1},{4,6},{5,7},{6,4},{7,5},{8,10},{9,11},{10,... | collective-permute-start | bytes 786440 | tf_op jit(solution)/shard_map/ppermute | solution.py:25
  72.3 12.2 %collective-permute-start.23 = (bf16[64,1024]{1,0:T(8,128)(2,1)}, bf16[64,1024]{1,0:T(8,128)(2,1)S(1)}, u32[]{:S(2)}, u32[]{:S(2)}) collective-permute-start(bf16[64,1024]{1,0:T(8,128)(2,1)} %slice.91), channel_id=1, source_target_pairs={{0,2},{1,3},{2,0},{3,1},{4,6},{5,7},{6,4},{7,5},{8,10},{9,11},{10,... | collective-permute-start | bytes 393224 | tf_op jit(solution)/shard_map/ppermute | solution.py:25
  79.8 5.3 %collective-permute-start.22 = (bf16[64,1024]{1,0:T(8,128)(2,1)}, bf16[64,1024]{1,0:T(8,128)(2,1)}, u32[]{:S(2)}, u32[]{:S(2)}) collective-permute-start(bf16[64,1024]{1,0:T(8,128)(2,1)} %slice.90), channel_id=1, source_target_pairs={{0,16},{16,0},{1,17},{17,1},{2,18},{18,2},{3,19},{19,3},{4,20},{20... | collective-permute-start | bytes 393224 | tf_op jit(solution)/shard_map/ppermute | solution.py:25
  82.9 15.9 %collective-permute-start.27 = (bf16[64,1024]{1,0:T(8,128)(2,1)S(1)}, bf16[64,1024]{1,0:T(8,128)(2,1)S(1)}, u32[]{:S(2)}, u32[]{:S(2)}) collective-permute-start(bf16[64,1024]{1,0:T(8,128)(2,1)S(1)} %slice.118), channel_id=1, source_target_pairs={{0,2},{1,3},{2,0},{3,1},{4,6},{5,7},{6,4},{7,5},{8,10},{9,11},{10,... | collective-permute-start | bytes 393224 | tf_op jit(solution)/shard_map/ppermute | solution.py:25
  84.5 14.3 %collective-permute-start.26 = (bf16[64,1024]{1,0:T(8,128)(2,1)S(1)}, bf16[64,1024]{1,0:T(8,128)(2,1)S(1)}, u32[]{:S(2)}, u32[]{:S(2)}) collective-permute-start(bf16[64,1024]{1,0:T(8,128)(2,1)S(1)} %slice.117), channel_id=1, source_target_pairs={{0,16},{16,0},{1,17},{17,1},{2,18},{18,2},{3,19},{19,3},{4,20},{20... | collective-permute-start | bytes 393224 | tf_op jit(solution)/shard_map/ppermute | solution.py:25
  85.2 13.6 %collective-permute-start.25 = (bf16[128,1024]{1,0:T(8,128)(2,1)S(1)}, bf16[128,1024]{1,0:T(8,128)(2,1)S(1)}, u32[]{:S(2)}, u32[]{:S(2)}) collective-permute-start(bf16[128,1024]{1,0:T(8,128)(2,1)S(1)} %slice.93), channel_id=1, source_target_pairs={{0,2},{1,3},{2,0},{3,1},{4,6},{5,7},{6,4},{7,5},{8,10},{9,11},{10,... | collective-permute-start | bytes 786440 | tf_op jit(solution)/shard_map/ppermute | solution.py:25
  86.8 12.0 %collective-permute-start.24 = (bf16[128,1024]{1,0:T(8,128)(2,1)S(1)}, bf16[128,1024]{1,0:T(8,128)(2,1)S(1)}, u32[]{:S(2)}, u32[]{:S(2)}) collective-permute-start(bf16[128,1024]{1,0:T(8,128)(2,1)S(1)} %slice.92), channel_id=1, source_target_pairs={{0,16},{16,0},{1,17},{17,1},{2,18},{18,2},{3,19},{19,3},{4,20},{20... | collective-permute-start | bytes 786440 | tf_op jit(solution)/shard_map/ppermute | solution.py:25
  98.8 10.8 %collective-permute-start.28 = (bf16[256,1024]{1,0:T(8,128)(2,1)S(1)}, bf16[256,1024]{1,0:T(8,128)(2,1)S(1)}, u32[]{:S(2)}, u32[]{:S(2)}) collective-permute-start(bf16[256,1024]{1,0:T(8,128)(2,1)S(1)} %get-tuple-element.102), channel_id=1, source_target_pairs={{0,16},{16,0},{1,17},{17,1},{2,18},{18,2},{3,19},{19,3},{4,20},{20... | collective-permute-start | bytes 1572872 | tf_op jit(solution)/shard_map/ppermute | solution.py:25
  98.9 10.7 %collective-permute-start.29 = (bf16[256,1024]{1,0:T(8,128)(2,1)S(1)}, bf16[256,1024]{1,0:T(8,128)(2,1)S(1)}, u32[]{:S(2)}, u32[]{:S(2)}) collective-permute-start(bf16[256,1024]{1,0:T(8,128)(2,1)S(1)} %get-tuple-element.103), channel_id=1, source_target_pairs={{0,2},{1,3},{2,0},{3,1},{4,6},{5,7},{6,4},{7,5},{8,10},{9,11},{10,... | collective-permute-start | bytes 1572872 | tf_op jit(solution)/shard_map/ppermute | solution.py:25
  109.6 9.2 %collective-permute-start.30 = (bf16[128,1024]{1,0:T(8,128)(2,1)S(1)}, bf16[128,1024]{1,0:T(8,128)(2,1)S(1)}, u32[]{:S(2)}, u32[]{:S(2)}) collective-permute-start(bf16[128,1024]{1,0:T(8,128)(2,1)S(1)} %get-tuple-element.119), channel_id=1, source_target_pairs={{0,16},{16,0},{1,17},{17,1},{2,18},{18,2},{3,19},{19,3},{4,20},{20... | collective-permute-start | bytes 786440 | tf_op jit(solution)/shard_map/ppermute | solution.py:25
  111.3 9.3 %collective-permute-start.32 = (bf16[128,1024]{1,0:T(8,128)(2,1)S(1)}, bf16[128,1024]{1,0:T(8,128)(2,1)S(1)}, u32[]{:S(2)}, u32[]{:S(2)}) collective-permute-start(bf16[128,1024]{1,0:T(8,128)(2,1)S(1)} %get-tuple-element.121), channel_id=1, source_target_pairs={{0,2},{1,3},{2,0},{3,1},{4,6},{5,7},{6,4},{7,5},{8,10},{9,11},{10,... | collective-permute-start | bytes 786440 | tf_op jit(solution)/shard_map/ppermute | solution.py:25
  112.8 10.2 %collective-permute-start.34 = (bf16[128,1024]{1,0:T(8,128)(2,1)S(1)}, bf16[128,1024]{1,0:T(8,128)(2,1)S(1)}, u32[]{:S(2)}, u32[]{:S(2)}) collective-permute-start(bf16[128,1024]{1,0:T(8,128)(2,1)S(1)} %get-tuple-element.122), channel_id=1, source_target_pairs={{0,16},{16,0},{1,17},{17,1},{2,18},{18,2},{3,19},{19,3},{4,20},{20... | collective-permute-start | bytes 786440 | tf_op jit(solution)/shard_map/ppermute | solution.py:25
  112.9 10.6 %collective-permute-start.35 = (bf16[128,1024]{1,0:T(8,128)(2,1)S(1)}, bf16[128,1024]{1,0:T(8,128)(2,1)S(1)}, u32[]{:S(2)}, u32[]{:S(2)}) collective-permute-start(bf16[128,1024]{1,0:T(8,128)(2,1)S(1)} %get-tuple-element.123), channel_id=1, source_target_pairs={{0,2},{1,3},{2,0},{3,1},{4,6},{5,7},{6,4},{7,5},{8,10},{9,11},{10,... | collective-permute-start | bytes 786440 | tf_op jit(solution)/shard_map/ppermute | solution.py:25
  118.9 8.5 %collective-permute-start.31 = (bf16[128,1024]{1,0:T(8,128)(2,1)S(1)}, bf16[128,1024]{1,0:T(8,128)(2,1)S(1)}, u32[]{:S(2)}, u32[]{:S(2)}) collective-permute-start(bf16[128,1024]{1,0:T(8,128)(2,1)S(1)} %add_convert_fusion.5), channel_id=1, source_target_pairs={{0,2},{1,3},{2,0},{3,1},{4,6},{5,7},{6,4},{7,5},{8,10},{9,11},{10,... | collective-permute-start | bytes 786440 | tf_op jit(solution)/shard_map/ppermute | solution.py:25
  120.7 8.1 %collective-permute-start.33 = (bf16[128,1024]{1,0:T(8,128)(2,1)S(1)}, bf16[128,1024]{1,0:T(8,128)(2,1)S(1)}, u32[]{:S(2)}, u32[]{:S(2)}) collective-permute-start(bf16[128,1024]{1,0:T(8,128)(2,1)S(1)} %add_convert_fusion.4), channel_id=1, source_target_pairs={{0,16},{16,0},{1,17},{17,1},{2,18},{18,2},{3,19},{19,3},{4,20},{20... | collective-permute-start | bytes 786440 | tf_op jit(solution)/shard_map/ppermute | solution.py:25
  129.3 20.2 %copy-start.7 = (f32[64,2048]{1,0:T(8,128)S(1)}, f32[64,2048]{1,0:T(8,128)}, u32[]{:S(2)}) copy-start(f32[64,2048]{1,0:T(8,128)} %copy-done.6) | copy-start | bytes 1572868
  129.4 7.4 %collective-permute-start.38 = (bf16[64,2048]{1,0:T(8,128)(2,1)S(1)}, bf16[64,2048]{1,0:T(8,128)(2,1)S(1)}, u32[]{:S(2)}, u32[]{:S(2)}) collective-permute-start(bf16[64,2048]{1,0:T(8,128)(2,1)S(1)} %get-tuple-element.136), channel_id=1, source_target_pairs={{0,4},{4,0},{8,12},{12,8},{1,5},{5,1},{9,13},{13,9},{2,6},{6,2},{1... | collective-permute-start | bytes 786440 | tf_op jit(solution)/shard_map/ppermute | solution.py:25
  130.1 6.6 %collective-permute-start.36 = (bf16[128,1024]{1,0:T(8,128)(2,1)S(1)}, bf16[128,1024]{1,0:T(8,128)(2,1)S(1)}, u32[]{:S(2)}, u32[]{:S(2)}) collective-permute-start(bf16[128,1024]{1,0:T(8,128)(2,1)S(1)} %get-tuple-element.130), channel_id=1, source_target_pairs={{0,2},{1,3},{2,0},{3,1},{4,6},{5,7},{6,4},{7,5},{8,10},{9,11},{10,... | collective-permute-start | bytes 786440 | tf_op jit(solution)/shard_map/ppermute | solution.py:25
  130.9 6.4 %collective-permute-start.37 = (bf16[128,1024]{1,0:T(8,128)(2,1)S(1)}, bf16[128,1024]{1,0:T(8,128)(2,1)S(1)}, u32[]{:S(2)}, u32[]{:S(2)}) collective-permute-start(bf16[128,1024]{1,0:T(8,128)(2,1)S(1)} %get-tuple-element.131), channel_id=1, source_target_pairs={{0,16},{16,0},{1,17},{17,1},{2,18},{18,2},{3,19},{19,3},{4,20},{20... | collective-permute-start | bytes 786440 | tf_op jit(solution)/shard_map/ppermute | solution.py:25
  137.4 11.8 %collective-permute-start.40 = (bf16[64,2048]{1,0:T(8,128)(2,1)S(1)}, bf16[64,2048]{1,0:T(8,128)(2,1)S(1)}, u32[]{:S(2)}, u32[]{:S(2)}) collective-permute-start(bf16[64,2048]{1,0:T(8,128)(2,1)S(1)} %fusion.6), channel_id=1, source_target_pairs={{0,8},{4,12},{8,0},{12,4},{1,9},{5,13},{9,1},{13,5},{2,10},{6,14},... | collective-permute-start | bytes 786440 | tf_op jit(solution)/shard_map/ppermute | solution.py:25
  141.9 7.6 %collective-permute-start.39 = (bf16[64,2048]{1,0:T(8,128)(2,1)S(1)}, bf16[64,2048]{1,0:T(8,128)(2,1)S(1)}, u32[]{:S(2)}, u32[]{:S(2)}) collective-permute-start(bf16[64,2048]{1,0:T(8,128)(2,1)S(1)} %get-tuple-element.133), channel_id=1, source_target_pairs={{0,4},{4,0},{8,12},{12,8},{1,5},{5,1},{9,13},{13,9},{2,6},{6,2},{1... | collective-permute-start | bytes 786440 | tf_op jit(solution)/shard_map/ppermute | solution.py:25

commit v10 on v9

--- a/solution.py
+++ b/solution.py
@@ -41,14 +41,37 @@
     return lax.optimization_barrier(arrays)
 
 
-def spread_rows(own, coded, weight):
-    half = own.shape[1] // 2
+def pack_kernel(*refs):
+    low_ref, high_ref = refs[-2:]
+    count = len(refs) // 2 - 1
+    half = low_ref.shape[1]
+    start = 0
+    for rep_ref, role_ref in zip(refs[:count], refs[count:-2]):
+        rows = pl.ds(start, rep_ref.shape[0])
+        low_ref[rows] = rep_ref[:, :half]
+        high_ref[rows] = role_ref[:, half:]
+        start += rep_ref.shape[0]
+
+
+def pack_corners(by_rep, by_role):
+    rows, width = sum(part.shape[0] for part in by_rep), by_rep[0].shape[1]
+    half = jax.ShapeDtypeStruct((rows, width // 2), jnp.bfloat16)
+    return pl.pallas_call(
+        pack_kernel,
+        out_shape=[half, half],
+        compiler_params=pltpu.CompilerParams(vmem_limit_bytes=(4 + rows // 64) * 1024 * 1024),
+        cost_estimate=pl.CostEstimate(
+            flops=0, bytes_accessed=4 * rows * width, transcendentals=0
+        ),
+        name="pack_corners",
+    )(*by_rep, *by_role)
+
+
+def spread_rows(own, weight, coded, tables_of):
+    rows, half = own.shape[0], own.shape[1] // 2
 
     def both_ways(part):
         return swap(part, "rep", ACROSS), swap(part, "role", 1)
-
-    def corners(by_rep, by_role):
-        return swap(by_rep[:, :half], "role", 1), swap(by_role[:, half:], "rep", ACROSS)
 
     first_bits, *bits_left = seq_bits()
     blocks = [own, swap(own, "seq", first_bits)]
@@ -56,28 +79,18 @@
         blocks = blocks + [swap(block, "seq", bits) for block in blocks]
     beyond = [swap(block, "seq", bits_left[-1]) for block in blocks]
     middle = jnp.concatenate(blocks[1:] + beyond[:-1], axis=0)
-    middle, weight, *outer = ready(middle, weight, *both_ways(own))
-    outer_corner = corners(*outer)
-    last, coded = ready(beyond[-1], coded)
-    inner = both_ways(middle)
-    final = both_ways(last)
-    by_rep, by_role, *outer_corner = ready(*inner, *outer_corner)
-    inner_corner = corners(by_rep, by_role)
-    final_corner = corners(*final)
-    groups = [[], [], [], []]
-    start = 0
-    for part, beside, corner in (
-        (own, outer, outer_corner),
-        (middle, inner, inner_corner),
-        (last, final, final_corner),
-    ):
-        groups[0].append((start, 0, beside[0]))
-        groups[1].append((start, 0, beside[1]))
-        groups[2].append((start, 0, corner[0]))
-        groups[2].append((start, half, corner[1]))
-        groups[3].append((start, 0, part))
-        start += part.shape[0]
-    return groups, coded, weight
+    middle, weight, coded, *outer = ready(middle, weight, coded, *both_ways(own))
+    last, *tables = ready(beyond[-1], *tables_of(coded))
+    by_rep, by_role = zip(outer, both_ways(middle), both_ways(last))
+    low, high = pack_corners(by_rep, by_role)
+    corner_low, corner_high = swap(low, "role", 1), swap(high, "rep", ACROSS)
+    starts = (0, rows, rows + middle.shape[0])
+    groups = [
+        [(start, 0, part) for start, part in zip(starts, parts)]
+        for parts in (by_rep, by_role, (own, middle, last))
+    ]
+    groups.insert(2, [(0, 0, corner_low), (0, half, corner_high)])
+    return groups, weight, tables
 
 
 def added(first, second):
@@ -532,27 +545,33 @@
     coded = jnp.concatenate([both_routes[1:], far_routes[:1], far_routes[1:], both_routes[:1]])
     queries = make_queries([normed, across_rows, pair_rows, corner_rows], w_query, q_gain)
     kept, leaving = attend(queries, half_kv, pair_kv, w_out, head_dim)
-    leaving, own_dn, own_gu = ready(swap(leaving, "rep", PAIR), w_down[0], w_gateup[0])
+    leaving, own_dn = ready(swap(leaving, "rep", PAIR), w_down[0])
     halves = kept + leaving
-    far_dn, far_gu = swap(own_dn, "rep", PAIR), swap(own_gu, "rep", PAIR)
+    far_dn = swap(own_dn, "rep", PAIR)
     far_sum = halves[row_count:].astype(jnp.bfloat16)
-    across_sum, coded = ready(swap(far_sum, "rep", ACROSS), coded)
+    across_sum, coded, far_dn, own_gu = ready(
+        swap(far_sum, "rep", ACROSS), coded, far_dn, w_gateup[0]
+    )
+    far_gu = swap(own_gu, "rep", PAIR)
     attended = halves[:row_count] + across_sum.astype(jnp.float32)
     mixed = tokens + attended
 
-    mixed, far_dn, coded = ready(mixed, far_dn, coded)
     moe_in = rms_rows(mixed, moe_gain).astype(jnp.bfloat16)
 
-    rows, coded, far_gu = spread_rows(moe_in, coded, far_gu)
     capacity = max(2, 7 * row_count * top_count // (4 * expert_count))
     slots = -(-capacity * (coded.shape[1] // row_count) // 16) * 16
-    pick, place, share = make_tables(coded, lax.axis_index(EVERY), slots, top_count)
+    rows, far_gu, tables = spread_rows(
+        moe_in,
+        far_gu,
+        coded,
+        lambda codes: make_tables(codes, lax.axis_index(EVERY), slots, top_count),
+    )
     weights = [
         pltpu.with_memory_space_constraint(one, pltpu.HBM)
         for one in (w_gateup[0], far_gu, w_down[0], far_dn)
     ]
 
-    tables = (pick, place, share, weights)
+    tables = (*tables, weights)
     by_rep, by_role = run_experts(0, rows[:2], (1, 1), *tables)
     rep_low, rep_high, role_low, role_high, *held = ready(
         *by_rep, *by_role, *(array for _, _, array in rows[2])

time: 150 us -> 146 us (0.973)
  starting transfers between devices: 52.6 us -> 45.2 us
  local copies, waits for them, and re-layouts: 1.64 us -> 4.63 us
    ppermute x41 -> x37, starting transfers between devices: 52.6 us -> 45.2 us  [swap(): return lax.ppermute(block, axis, [(i, i ^ bits) for i in range(size)])]
    unnamed x23 -> x27, local copies, waits for them, and re-layouts: 0.08 us -> 4.46 us
    ppermute x41 -> x37, waiting for transfers between devices: 66.4 us -> 65.7 us  [swap(): return lax.ppermute(block, axis, [(i, i ^ bits) for i in range(size)])]
  transfers between devices with their start and end apart: 41 -> 37, of which waited for: 23 -> 22; matrix products, arithmetic and copies ran while one was open for 2% -> 1% of each run, Pallas kernels for 14% -> 15%
where the time goes in v10:
time: 146 us
  waiting for transfers between devices  65.7 us (45%)
  starting transfers between devices  45.2 us (31%)
  Pallas kernels  27 us (18%)
  local copies, waits for them, and re-layouts  4.63 us (3%)
  other arithmetic  3.34 us (2%)
    ppermute x37, waiting for transfers between devices, swap(): return lax.ppermute(block, axis, [(i, i ^ bits) for i in range(size)])  65.7 us
    ppermute x37, starting transfers between devices, swap(): return lax.ppermute(block, axis, [(i, i ^ bits) for i in range(size)])  45.2 us
    pallas_call x2, Pallas kernels, run_experts(): pl.pallas_call(lambda *refs: expert_kernel(first, spots, cuts, *refs), ou...  19.2 us
    unnamed x27, local copies, waits for them, and re-layouts  4.46 us
  transfers between devices with their start and end apart: 37, of which 22 were waited for; matrix products, arithmetic and copies ran while one was open for 1% of the time, Pallas kernels for 15%

profile of v10, /device:TPU:0, one launch (start us, length us, event | category | flops | bytes accessed | tf_op | source)
XLA Modules:
  0.0 146.3 jit_solution(15407813991841858971)
XLA Ops:
  0.0 2.6 %prepare.1 = (bf16[64,2048]{1,0:T(8,128)(2,1)S(1)}, bf16[64,640]{1,0:T(8,128)(2,1)S(1)}) custom-call(bf16[64,2048]{1,0:T(8,128)(2,1)} %bitcast.35, f32[1,2048]{1,0:T(1,128)} %bitcast.36, bf16[2,2048,256]{2,1,0:T(8,128)(2,1)} %refs_2_.1, f32[1,128]{1,0:T(1,128)} %bitcast.39, s32[8,64]{1,0:T(8,128)} %bitcast.37, s32[8,64]{1,0:T(8,128)} %bitcast.38), custom_call_target="tpu_custom_call" | custom-call | flops 134217728 | bytes 2621440 | tf_op jit(solution)/shard_map/prepare/pallas_call | solution.py:189
  2.6 5.1 %collective-permute-start.2 = (bf16[64,640]{1,0:T(8,128)(2,1)S(1)}, bf16[64,640]{1,0:T(8,128)(2,1)S(1)}, u32[]{:S(2)}, u32[]{:S(2)}) collective-permute-start(bf16[64,640]{1,0:T(8,128)(2,1)S(1)} %get-tuple-element.66), channel_id=1, source_target_pairs={{0,12},{4,8},{8,4},{12,0},{1,13},{5,9},{9,5},{13,1},{2,14},{6,10},... | collective-permute-start | bytes 245768 | tf_op jit(solution)/shard_map/ppermute | solution.py:25
  7.7 0.6 collective-permute-start
  8.3 1.7 %collective-permute-start.3 = (bf16[64,2048]{1,0:T(8,128)(2,1)S(1)}, bf16[64,2048]{1,0:T(8,128)(2,1)S(1)}, u32[]{:S(2)}, u32[]{:S(2)}) collective-permute-start(bf16[64,2048]{1,0:T(8,128)(2,1)S(1)} %get-tuple-element.65.first_ref), channel_id=1, source_target_pairs={{0,2},{1,3},{2,0},{3,1},{4,6},{5,7},{6,4},{7,5},{8,10},{9,11},{10,... | collective-permute-start | bytes 786440 | tf_op jit(solution)/shard_map/ppermute | solution.py:25
  10.0 3.7 %collective-permute-done = bf16[64,640]{1,0:T(8,128)(2,1)S(1)} collective-permute-done((bf16[64,640]{1,0:T(8,128)(2,1)S(1)}, bf16[64,640]{1,0:T(8,128)(2,1)S(1)}, u32[]{:S(2)}, u32[]{:S(2)}) %collective-permute-start) | collective-permute-done | bytes 81952 | tf_op jit(solution)/shard_map/ppermute | solution.py:25
  14.1 3.0 %collective-permute-done.3.second_ref = bf16[64,2048]{1,0:T(8,128)(2,1)S(1)} collective-permute-done((bf16[64,2048]{1,0:T(8,128)(2,1)S(1)}, bf16[64,2048]{1,0:T(8,128)(2,1)S(1)}, u32[]{:S(2)}, u32[]{:S(2)}) %collective-permute-start.3) | collective-permute-done | bytes 262176 | tf_op jit(solution)/shard_map/ppermute | solution.py:25
  17.1 1.7 %collective-permute-start.6 = (bf16[256,384]{1,0:T(8,128)(2,1)S(1)}, bf16[256,384]{1,0:T(8,128)(2,1)S(1)}, u32[]{:S(2)}, u32[]{:S(2)}) collective-permute-start(bf16[256,384]{1,0:T(8,128)(2,1)S(1)} %pad_maximum_fusion.5), channel_id=1, source_target_pairs={{0,2},{1,3},{2,0},{3,1},{4,6},{5,7},{6,4},{7,5},{8,10},{9,11},{10,... | collective-permute-start | bytes 589832 | tf_op jit(solution)/shard_map/ppermute | solution.py:25
  18.7 4.9 %collective-permute-done.6 = bf16[256,384]{1,0:T(8,128)(2,1)S(1)} collective-permute-done((bf16[256,384]{1,0:T(8,128)(2,1)S(1)}, bf16[256,384]{1,0:T(8,128)(2,1)S(1)}, u32[]{:S(2)}, u32[]{:S(2)}) %collective-permute-start.6) | collective-permute-done | bytes 196640 | tf_op jit(solution)/shard_map/ppermute | solution.py:25
  23.8 0.9 queries.1.refs_0_
  24.7 0.6 collective-permute-done.7.refs_2_
  25.2 2.7 %attend.1 = (f32[128,2048]{1,0:T(8,128)S(1)}, f32[128,2048]{1,0:T(8,128)S(1)}) custom-call(bf16[256,512]{1,0:T(8,128)(2,1)S(1)} %queries.1.refs_0_, bf16[512,256]{1,0:T(8,128)(2,1)S(1)} %pad_maximum_fusion.3.refs_1_, bf16[512,256]{1,0:T(8,128)(2,1)S(1)} %collective-permute-done.7.refs_2_, bf16[512,2048]{1,0:T(8,128)(2,1)S(1)} %copy-done.2), custom_call_target="tpu_custom_call" | custom-call | flops 1073741824 | bytes 4194304 | tf_op jit(solution)/shard_map/attend/pallas_call | solution.py:268
  28.0 0.2 collective-permute-start.8
  28.2 2.5 %collective-permute-done.8 = f32[128,2048]{1,0:T(8,128)S(1)} collective-permute-done((f32[128,2048]{1,0:T(8,128)S(1)}, f32[128,2048]{1,0:T(8,128)S(1)}, u32[]{:S(2)}, u32[]{:S(2)}) %collective-permute-start.8) | collective-permute-done | bytes 1048608 | tf_op jit(solution)/shard_map/ppermute | solution.py:25
  31.0 1.7 %collective-permute-start.9 = (bf16[64,2048]{1,0:T(8,128)(2,1)S(1)}, bf16[64,2048]{1,0:T(8,128)(2,1)S(1)}, u32[]{:S(2)}, u32[]{:S(2)}) collective-permute-start(bf16[64,2048]{1,0:T(8,128)(2,1)S(1)} %slice.137), channel_id=1, source_target_pairs={{0,2},{1,3},{2,0},{3,1},{4,6},{5,7},{6,4},{7,5},{8,10},{9,11},{10,... | collective-permute-start | bytes 786440 | tf_op jit(solution)/shard_map/ppermute | solution.py:25
  32.8 1.6 %collective-permute-start.10 = (bf16[2,256,128]{2,1,0:T(8,128)(2,1)S(1)}, bf16[2,256,128]{2,1,0:T(8,128)(2,1)S(1)}, u32[]{:S(2)}, u32[]{:S(2)}) collective-permute-start(bf16[2,256,128]{2,1,0:T(8,128)(2,1)S(1)} %pad_maximum_fusion.6), channel_id=1, source_target_pairs={{0,16},{16,0},{1,17},{17,1},{2,18},{18,2},{3,19},{19,3},{4,20},{20... | collective-permute-start | bytes 393224 | tf_op jit(solution)/shard_map/ppermute | solution.py:25
  34.4 4.0 %collective-permute-done.10 = bf16[2,256,128]{2,1,0:T(8,128)(2,1)S(1)} collective-permute-done((bf16[2,256,128]{2,1,0:T(8,128)(2,1)S(1)}, bf16[2,256,128]{2,1,0:T(8,128)(2,1)S(1)}, u32[]{:S(2)}, u32[]{:S(2)}) %collective-permute-start.10) | collective-permute-done | bytes 131104 | tf_op jit(solution)/shard_map/ppermute | solution.py:25
  38.4 1.3 collective-permute-done.9
  39.7 1.7 %copy-done.5 = bf16[768,2048]{1,0:T(8,128)(2,1)} copy-done((bf16[768,2048]{1,0:T(8,128)(2,1)}, bf16[768,2048]{1,0:T(8,128)(2,1)S(1)}, u32[]{:S(2)}) %copy-start.5) | copy-done | bytes 3145752
  41.4 0.2 multiply_reduce_fusion
  41.8 2.4 %collective-permute-start.12 = (bf16[64,2048]{1,0:T(8,128)(2,1)S(1)}, bf16[64,2048]{1,0:T(8,128)(2,1)}, u32[]{:S(2)}, u32[]{:S(2)}) collective-permute-start(bf16[64,2048]{1,0:T(8,128)(2,1)S(1)} %multiply_convert_fusion.refs_9_), channel_id=1, source_target_pairs={{0,8},{4,12},{8,0},{12,4},{1,9},{5,13},{9,1},{13,5},{2,10},{6,14},... | collective-permute-start | bytes 786440 | tf_op jit(solution)/shard_map/ppermute | solution.py:25
  44.1 2.0 %collective-permute-start.14 = (bf16[64,2048]{1,0:T(8,128)(2,1)S(1)}, bf16[64,2048]{1,0:T(8,128)(2,1)S(1)}, u32[]{:S(2)}, u32[]{:S(2)}) collective-permute-start(bf16[64,2048]{1,0:T(8,128)(2,1)S(1)} %multiply_convert_fusion.refs_9_), channel_id=1, source_target_pairs={{0,4},{4,0},{8,12},{12,8},{1,5},{5,1},{9,13},{13,9},{2,6},{6,2},{1... | collective-permute-start | bytes 786440 | tf_op jit(solution)/shard_map/ppermute | solution.py:25
  46.1 1.5 %collective-permute-start.17 = (bf16[64,2048]{1,0:T(8,128)(2,1)S(1)}, bf16[64,2048]{1,0:T(8,128)(2,1)S(1)}, u32[]{:S(2)}, u32[]{:S(2)}) collective-permute-start(bf16[64,2048]{1,0:T(8,128)(2,1)S(1)} %multiply_convert_fusion.refs_9_), channel_id=1, source_target_pairs={{0,16},{16,0},{1,17},{17,1},{2,18},{18,2},{3,19},{19,3},{4,20},{20... | collective-permute-start | bytes 786440 | tf_op jit(solution)/shard_map/ppermute | solution.py:25
  47.6 1.5 %collective-permute-start.16 = (bf16[64,2048]{1,0:T(8,128)(2,1)S(1)}, bf16[64,2048]{1,0:T(8,128)(2,1)S(1)}, u32[]{:S(2)}, u32[]{:S(2)}) collective-permute-start(bf16[64,2048]{1,0:T(8,128)(2,1)S(1)} %multiply_convert_fusion.refs_9_), channel_id=1, source_target_pairs={{0,2},{1,3},{2,0},{3,1},{4,6},{5,7},{6,4},{7,5},{8,10},{9,11},{10,... | collective-permute-start | bytes 786440 | tf_op jit(solution)/shard_map/ppermute | solution.py:25
  49.2 8.1 %collective-permute-done.12 = bf16[64,2048]{1,0:T(8,128)(2,1)} collective-permute-done((bf16[64,2048]{1,0:T(8,128)(2,1)S(1)}, bf16[64,2048]{1,0:T(8,128)(2,1)}, u32[]{:S(2)}, u32[]{:S(2)}) %collective-permute-start.12) | collective-permute-done | bytes 262176 | tf_op jit(solution)/shard_map/ppermute | solution.py:25
  57.5 1.0 pad_maximum_fusion.1.refs_10_
  58.5 2.7 %copy-done.3 = bf16[2048,1536]{1,0:T(8,128)(2,1)} copy-done((bf16[2048,1536]{1,0:T(8,128)(2,1)}, bf16[2048,1536]{1,0:T(8,128)(2,1)S(1)}, u32[]{:S(2)}) %copy-start.3) | copy-done | bytes 6291480
  61.2 1.5 %collective-permute-start.20 = (bf16[128,2048]{1,0:T(8,128)(2,1)S(1)}, bf16[128,2048]{1,0:T(8,128)(2,1)S(1)}, u32[]{:S(2)}, u32[]{:S(2)}) collective-permute-start(bf16[128,2048]{1,0:T(8,128)(2,1)S(1)} %pad_maximum_fusion.1.refs_10_), channel_id=1, source_target_pairs={{0,16},{16,0},{1,17},{17,1},{2,18},{18,2},{3,19},{19,3},{4,20},{20... | collective-permute-start | bytes 1572872 | tf_op jit(solution)/shard_map/ppermute | solution.py:25
  62.7 1.5 %collective-permute-start.18 = (bf16[128,2048]{1,0:T(8,128)(2,1)S(1)}, bf16[128,2048]{1,0:T(8,128)(2,1)S(1)}, u32[]{:S(2)}, u32[]{:S(2)}) collective-permute-start(bf16[128,2048]{1,0:T(8,128)(2,1)S(1)} %pad_maximum_fusion.1.refs_10_), channel_id=1, source_target_pairs={{0,2},{1,3},{2,0},{3,1},{4,6},{5,7},{6,4},{7,5},{8,10},{9,11},{10,... | collective-permute-start | bytes 1572872 | tf_op jit(solution)/shard_map/ppermute | solution.py:25
  64.2 1.6 %tables.1 = (bf16[4,224,256]{2,1,0:T(8,128)(2,1)S(1)}, bf16[2,4,256,112]{3,2,1,0:T(8,128)(2,1)S(1)}, f32[4,256,2]{2,1,0:T(8,128)S(1)}) custom-call(s32[1]{0:T(128)} %bitcast.12.refs_0_, bf16[4,256,128]{2,1,0:T(8,128)(2,1)S(1)} %pad_maximum_fusion.4.refs_1_), custom_call_target="tpu_custom_call" | custom-call | flops 134217728 | bytes 917504 | tf_op jit(solution)/shard_map/tables/pallas_call | solution.py:331
  65.8 1.2 collective-permute-start.21
  67.0 1.5 %collective-permute-start.19 = (bf16[64,2048]{1,0:T(8,128)(2,1)S(1)}, bf16[64,2048]{1,0:T(8,128)(2,1)S(1)}, u32[]{:S(2)}, u32[]{:S(2)}) collective-permute-start(bf16[64,2048]{1,0:T(8,128)(2,1)S(1)} %collective-permute-done.13.refs_11_), channel_id=1, source_target_pairs={{0,2},{1,3},{2,0},{3,1},{4,6},{5,7},{6,4},{7,5},{8,10},{9,11},{10,... | collective-permute-start | bytes 786440 | tf_op jit(solution)/shard_map/ppermute | solution.py:25
  68.5 11.9 %collective-permute-done.21.refs_12_.refs_5_ = bf16[64,2048]{1,0:T(8,128)(2,1)S(1)} collective-permute-done((bf16[64,2048]{1,0:T(8,128)(2,1)S(1)}, bf16[64,2048]{1,0:T(8,128)(2,1)S(1)}, u32[]{:S(2)}, u32[]{:S(2)}) %collective-permute-start.21) | collective-permute-done | bytes 262176 | tf_op jit(solution)/shard_map/ppermute | solution.py:25
  80.4 1.2 collective-permute-done.19.refs_9_.refs_2_
  81.7 0.6 collective-permute-start.22
  82.3 1.5 %collective-permute-start.23 = (bf16[256,1024]{1,0:T(8,128)(2,1)S(1)}, bf16[256,1024]{1,0:T(8,128)(2,1)S(1)}, u32[]{:S(2)}, u32[]{:S(2)}) collective-permute-start(bf16[256,1024]{1,0:T(8,128)(2,1)S(1)} %get-tuple-element.95), channel_id=1, source_target_pairs={{0,2},{1,3},{2,0},{3,1},{4,6},{5,7},{6,4},{7,5},{8,10},{9,11},{10,... | collective-permute-start | bytes 1572872 | tf_op jit(solution)/shard_map/ppermute | solution.py:25
  83.8 9.5 %experts.2 = (bf16[256,1024]{1,0:T(8,128)(2,1)S(1)}, bf16[256,1024]{1,0:T(8,128)(2,1)S(1)}, bf16[256,1024]{1,0:T(8,128)(2,1)S(1)}, bf16[256,1024]{1,0:T(8,128)(2,1)S(1)}) custom-call(bf16[4,224,256]{2,1,0:T(8,128)(2,1)S(1)} %get-tuple-element.81.refs_0_, bf16[2,4,256,112]{3,2,1,0:T(8,128)(2,1)S(1)} %get-tuple-element.82.refs_1_, ...), custom_call_target="tpu_custom_call" | custom-call | flops 4227858432 | bytes 23068672 | tf_op jit(solution)/shard_map/experts/pallas_call | solution.py:461
  93.3 0.9 collective-permute-done.22.refs_7_
  94.2 0.3 collective-permute-done.23.refs_8_
  94.5 1.4 collective-permute-start.24
  95.9 1.5 %collective-permute-start.25 = (bf16[256,1024]{1,0:T(8,128)(2,1)S(1)}, bf16[256,1024]{1,0:T(8,128)(2,1)S(1)}, u32[]{:S(2)}, u32[]{:S(2)}) collective-permute-start(bf16[256,1024]{1,0:T(8,128)(2,1)S(1)} %get-tuple-element.97), channel_id=1, source_target_pairs={{0,2},{1,3},{2,0},{3,1},{4,6},{5,7},{6,4},{7,5},{8,10},{9,11},{10,... | collective-permute-start | bytes 1572872 | tf_op jit(solution)/shard_map/ppermute | solution.py:25
  97.4 9.7 %experts.3 = (bf16[128,1024]{1,0:T(8,128)(2,1)S(1)}, bf16[128,1024]{1,0:T(8,128)(2,1)S(1)}, bf16[128,1024]{1,0:T(8,128)(2,1)S(1)}, bf16[128,1024]{1,0:T(8,128)(2...) custom-call(bf16[4,224,256]{2,1,0:T(8,128)(2,1)S(1)} %get-tuple-element.81.refs_0_, ...), custom_call_target="tpu_custom_call" | custom-call | flops 4227858432 | bytes 23068672 | tf_op jit(solution)/shard_map/experts/pallas_call | solution.py:461
  107.2 0.7 collective-permute-start.26
  107.8 1.5 %collective-permute-start.28 = (bf16[128,1024]{1,0:T(8,128)(2,1)S(1)}, bf16[128,1024]{1,0:T(8,128)(2,1)S(1)}, u32[]{:S(2)}, u32[]{:S(2)}) collective-permute-start(bf16[128,1024]{1,0:T(8,128)(2,1)S(1)} %get-tuple-element.111), channel_id=1, source_target_pairs={{0,2},{1,3},{2,0},{3,1},{4,6},{5,7},{6,4},{7,5},{8,10},{9,11},{10,... | collective-permute-start | bytes 786440 | tf_op jit(solution)/shard_map/ppermute | solution.py:25
  109.3 1.7 %collective-permute-start.30 = (bf16[128,1024]{1,0:T(8,128)(2,1)S(1)}, bf16[128,1024]{1,0:T(8,128)(2,1)S(1)}, u32[]{:S(2)}, u32[]{:S(2)}) collective-permute-start(bf16[128,1024]{1,0:T(8,128)(2,1)S(1)} %get-tuple-element.112), channel_id=1, source_target_pairs={{0,16},{16,0},{1,17},{17,1},{2,18},{18,2},{3,19},{19,3},{4,20},{20... | collective-permute-start | bytes 786440 | tf_op jit(solution)/shard_map/ppermute | solution.py:25
  111.1 0.2 collective-permute-start.31
  111.3 5.2 %collective-permute-done.26 = bf16[128,1024]{1,0:T(8,128)(2,1)S(1)} collective-permute-done((bf16[128,1024]{1,0:T(8,128)(2,1)S(1)}, bf16[128,1024]{1,0:T(8,128)(2,1)S(1)}, u32[]{:S(2)}, u32[]{:S(2)}) %collective-permute-start.26) | collective-permute-done | bytes 262176 | tf_op jit(solution)/shard_map/ppermute | solution.py:25
  116.5 1.1 collective-permute-start.27
  117.7 1.1 collective-permute-start.29
  118.9 1.8 %collective-permute-done.30 = bf16[128,1024]{1,0:T(8,128)(2,1)S(1)} collective-permute-done((bf16[128,1024]{1,0:T(8,128)(2,1)S(1)}, bf16[128,1024]{1,0:T(8,128)(2,1)S(1)}, u32[]{:S(2)}, u32[]{:S(2)}) %collective-permute-start.30) | collective-permute-done | bytes 262176 | tf_op jit(solution)/shard_map/ppermute | solution.py:25
  120.7 0.4 collective-permute-done.31
  121.1 3.8 %collective-permute-done.27 = bf16[128,1024]{1,0:T(8,128)(2,1)S(1)} collective-permute-done((bf16[128,1024]{1,0:T(8,128)(2,1)S(1)}, bf16[128,1024]{1,0:T(8,128)(2,1)S(1)}, u32[]{:S(2)}, u32[]{:S(2)}) %collective-permute-start.27) | collective-permute-done | bytes 262176 | tf_op jit(solution)/shard_map/ppermute | solution.py:25
  124.8 0.2 add_convert_fusion.2
  125.0 0.3 add_convert_fusion
  125.4 0.3 collective-permute-start.34
  125.7 1.4 collective-permute-start.32
  127.1 1.2 collective-permute-start.33
  128.3 3.5 %collective-permute-done.34 = bf16[64,2048]{1,0:T(8,128)(2,1)S(1)} collective-permute-done((bf16[64,2048]{1,0:T(8,128)(2,1)S(1)}, bf16[64,2048]{1,0:T(8,128)(2,1)S(1)}, u32[]{:S(2)}, u32[]{:S(2)}) %collective-permute-start.34) | collective-permute-done | bytes 262176 | tf_op jit(solution)/shard_map/ppermute | solution.py:25
  131.8 0.2 collective-permute-done.32
  132.2 1.3 collective-permute-done.33
  133.6 3.7 %collective-permute-start.36 = (bf16[64,2048]{1,0:T(8,128)(2,1)S(1)}, bf16[64,2048]{1,0:T(8,128)(2,1)S(1)}, u32[]{:S(2)}, u32[]{:S(2)}) collective-permute-start(bf16[64,2048]{1,0:T(8,128)(2,1)S(1)} %fusion.6), channel_id=1, source_target_pairs={{0,8},{4,12},{8,0},{12,4},{1,9},{5,13},{9,1},{13,5},{2,10},{6,14},... | collective-permute-start | bytes 786440 | tf_op jit(solution)/shard_map/ppermute | solution.py:25
  137.3 1.2 collective-permute-start.35
  138.4 6.1 %collective-permute-done.36 = bf16[64,2048]{1,0:T(8,128)(2,1)S(1)} collective-permute-done((bf16[64,2048]{1,0:T(8,128)(2,1)S(1)}, bf16[64,2048]{1,0:T(8,128)(2,1)S(1)}, u32[]{:S(2)}, u32[]{:S(2)}) %collective-permute-start.36) | collective-permute-done | bytes 262176 | tf_op jit(solution)/shard_map/ppermute | solution.py:25
  144.5 0.9 collective-permute-done.35
  145.4 0.9 fusion.8
  (69 shorter events, 1.7 us)
Async XLA Ops:
  0.0 23.7 %copy-start.1 = (f32[128]{0:T(128)S(1)}, f32[128]{0:T(128)}, u32[]{:S(2)}) copy-start(f32[128]{0:T(128)} %param.16) | copy-start | bytes 1540
  0.0 23.7 %copy-start = (bf16[2048,512]{1,0:T(8,128)(2,1)S(1)}, bf16[2048,512]{1,0:T(8,128)(2,1)}, u32[]{:S(2)}) copy-start(bf16[2048,512]{1,0:T(8,128)(2,1)} %weight_ref.1) | copy-start | bytes 6291460
  2.6 11.4 %collective-permute-start.2 = (bf16[64,640]{1,0:T(8,128)(2,1)S(1)}, bf16[64,640]{1,0:T(8,128)(2,1)S(1)}, u32[]{:S(2)}, u32[]{:S(2)}) collective-permute-start(bf16[64,640]{1,0:T(8,128)(2,1)S(1)} %get-tuple-element.66), channel_id=1, source_target_pairs={{0,12},{4,8},{8,4},{12,0},{1,13},{5,9},{9,5},{13,1},{2,14},{6,10},... | collective-permute-start | bytes 245768 | tf_op jit(solution)/shard_map/ppermute | solution.py:25
  7.7 6.2 %collective-permute-start.1 = (bf16[64,640]{1,0:T(8,128)(2,1)S(1)}, bf16[64,640]{1,0:T(8,128)(2,1)S(1)}, u32[]{:S(2)}, u32[]{:S(2)}) collective-permute-start(bf16[64,640]{1,0:T(8,128)(2,1)S(1)} %get-tuple-element.66), channel_id=1, source_target_pairs={{0,4},{4,0},{8,12},{12,8},{1,5},{5,1},{9,13},{13,9},{2,6},{6,2},{1... | collective-permute-start | bytes 245768 | tf_op jit(solution)/shard_map/ppermute | solution.py:25
  7.7 6.0 %collective-permute-start = (bf16[64,640]{1,0:T(8,128)(2,1)S(1)}, bf16[64,640]{1,0:T(8,128)(2,1)S(1)}, u32[]{:S(2)}, u32[]{:S(2)}) collective-permute-start(bf16[64,640]{1,0:T(8,128)(2,1)S(1)} %get-tuple-element.66), channel_id=1, source_target_pairs={{0,8},{4,12},{8,0},{12,4},{1,9},{5,13},{9,1},{13,5},{2,10},{6,14},... | collective-permute-start | bytes 245768 | tf_op jit(solution)/shard_map/ppermute | solution.py:25
  8.3 5.7 %collective-permute-start.4 = (bf16[64,2048]{1,0:T(8,128)(2,1)S(1)}, bf16[64,2048]{1,0:T(8,128)(2,1)S(1)}, u32[]{:S(2)}, u32[]{:S(2)}) collective-permute-start(bf16[64,2048]{1,0:T(8,128)(2,1)S(1)} %get-tuple-element.65.first_ref), channel_id=1, source_target_pairs={{0,1},{1,0},{2,3},{3,2},{4,5},{5,4},{6,7},{7,6},{8,9},{9,8},{10,11... | collective-permute-start | bytes 786440 | tf_op jit(solution)/shard_map/ppermute | solution.py:25
  8.3 8.7 %collective-permute-start.3 = (bf16[64,2048]{1,0:T(8,128)(2,1)S(1)}, bf16[64,2048]{1,0:T(8,128)(2,1)S(1)}, u32[]{:S(2)}, u32[]{:S(2)}) collective-permute-start(bf16[64,2048]{1,0:T(8,128)(2,1)S(1)} %get-tuple-element.65.first_ref), channel_id=1, source_target_pairs={{0,2},{1,3},{2,0},{3,1},{4,6},{5,7},{6,4},{7,5},{8,10},{9,11},{10,... | collective-permute-start | bytes 786440 | tf_op jit(solution)/shard_map/ppermute | solution.py:25
  10.0 15.2 %copy-start.2 = (bf16[512,2048]{1,0:T(8,128)(2,1)S(1)}, bf16[512,2048]{1,0:T(8,128)(2,1)}, u32[]{:S(2)}) copy-start(bf16[512,2048]{1,0:T(8,128)(2,1)} %refs_3_.1) | copy-start | bytes 6291460
  17.1 6.5 %collective-permute-start.6 = (bf16[256,384]{1,0:T(8,128)(2,1)S(1)}, bf16[256,384]{1,0:T(8,128)(2,1)S(1)}, u32[]{:S(2)}, u32[]{:S(2)}) collective-permute-start(bf16[256,384]{1,0:T(8,128)(2,1)S(1)} %pad_maximum_fusion.5), channel_id=1, source_target_pairs={{0,2},{1,3},{2,0},{3,1},{4,6},{5,7},{6,4},{7,5},{8,10},{9,11},{10,... | collective-permute-start | bytes 589832 | tf_op jit(solution)/shard_map/ppermute | solution.py:25
  18.7 5.0 %collective-permute-start.5 = (bf16[64,2048]{1,0:T(8,128)(2,1)S(1)}, bf16[64,2048]{1,0:T(8,128)(2,1)S(1)}, u32[]{:S(2)}, u32[]{:S(2)}) collective-permute-start(bf16[64,2048]{1,0:T(8,128)(2,1)S(1)} %collective-permute-done.3.second_ref), channel_id=1, source_target_pairs={{0,1},{1,0},{2,3},{3,2},{4,5},{5,4},{6,7},{7,6},{8,9},{9,8},{10,11... | collective-permute-start | bytes 786440 | tf_op jit(solution)/shard_map/ppermute | solution.py:25
  23.6 1.6 %collective-permute-start.7 = (bf16[512,256]{1,0:T(8,128)(2,1)S(1)}, bf16[512,256]{1,0:T(8,128)(2,1)S(1)}, u32[]{:S(2)}, u32[]{:S(2)}) collective-permute-start(bf16[512,256]{1,0:T(8,128)(2,1)S(1)} %pad_maximum_fusion.3.refs_1_), channel_id=1, source_target_pairs={{0,1},{1,0},{2,3},{3,2},{4,5},{5,4},{6,7},{7,6},{8,9},{9,8},{10,11... | collective-permute-start | bytes 786440 | tf_op jit(solution)/shard_map/ppermute | solution.py:25
  23.7 7.0 %copy-start.4 = (bf16[1,768,2048]{2,1,0:T(8,128)(2,1)S(1)}, bf16[1,768,2048]{2,1,0:T(8,128)(2,1)}, u32[]{:S(2)}) copy-start(bf16[1,768,2048]{2,1,0:T(8,128)(2,1)} %param.23) | copy-start | bytes 9437188
  23.8 17.6 %slice-start = ((s8[6291456]{0:T(1024)(128)(4,1)}), s8[4194304]{0:T(1024)(128)(4,1)S(1)}, s32[]{:S(2)}) async-start(s8[6291456]{0:T(1024)(128)(4,1)} %bitcast.29), calls=%async_computation | async-start | bytes 8388608
  24.6 16.7 %slice-start.1 = ((s8[6291456]{0:T(1024)(128)(4,1)}), s8[2097152]{0:T(1024)(128)(4,1)S(1)}, s32[]{:S(2)}) async-start(s8[6291456]{0:T(1024)(128)(4,1)} %bitcast.29), calls=%async_computation.1 | async-start | bytes 4194304
  28.0 13.4 %copy-start.8 = (bf16[1,64,2048]{2,1,0:T(8,128)(2,1)S(1)}, bf16[1,64,2048]{2,1,0:T(8,128)(2,1)}, u32[]{:S(2)}) copy-start(bf16[1,64,2048]{2,1,0:T(8,128)(2,1)} %param.12) | copy-start | bytes 786436
  28.0 13.7 %copy-start.9 = (f32[2048]{0:T(1024)S(1)}, f32[2048]{0:T(1024)}, u32[]{:S(2)}) copy-start(f32[2048]{0:T(1024)} %param.19) | copy-start | bytes 24580
  28.0 2.7 %collective-permute-start.8 = (f32[128,2048]{1,0:T(8,128)S(1)}, f32[128,2048]{1,0:T(8,128)S(1)}, u32[]{:S(2)}, u32[]{:S(2)}) collective-permute-start(f32[128,2048]{1,0:T(8,128)S(1)} %get-tuple-element.71), channel_id=1, source_target_pairs={{0,1},{1,0},{2,3},{3,2},{4,5},{5,4},{6,7},{7,6},{8,9},{9,8},{10,11... | collective-permute-start | bytes 3145736 | tf_op jit(solution)/shard_map/ppermute | solution.py:25
  30.7 9.0 %collective-permute-start.11 = (bf16[768,2048]{1,0:T(8,128)(2,1)S(1)}, bf16[768,2048]{1,0:T(8,128)(2,1)S(1)}, u32[]{:S(2)}, u32[]{:S(2)}) collective-permute-start(bf16[768,2048]{1,0:T(8,128)(2,1)S(1)} %bitcast.34), channel_id=1, source_target_pairs={{0,1},{1,0},{2,3},{3,2},{4,5},{5,4},{6,7},{7,6},{8,9},{9,8},{10,11... | collective-permute-start | bytes 9437192 | tf_op jit(solution)/shard_map/ppermute | solution.py:25
  31.0 31.7 %copy-start.6 = (f32[128,2048]{1,0:T(8,128)}, f32[128,2048]{1,0:T(8,128)S(1)}, u32[]{:S(2)}) copy-start(f32[128,2048]{1,0:T(8,128)S(1)} %add.104) | copy-start | bytes 3145732
  31.0 8.6 %collective-permute-start.9 = (bf16[64,2048]{1,0:T(8,128)(2,1)S(1)}, bf16[64,2048]{1,0:T(8,128)(2,1)S(1)}, u32[]{:S(2)}, u32[]{:S(2)}) collective-permute-start(bf16[64,2048]{1,0:T(8,128)(2,1)S(1)} %slice.137), channel_id=1, source_target_pairs={{0,2},{1,3},{2,0},{3,1},{4,6},{5,7},{6,4},{7,5},{8,10},{9,11},{10,... | collective-permute-start | bytes 786440 | tf_op jit(solution)/shard_map/ppermute | solution.py:25
  32.8 5.5 %collective-permute-start.10 = (bf16[2,256,128]{2,1,0:T(8,128)(2,1)S(1)}, bf16[2,256,128]{2,1,0:T(8,128)(2,1)S(1)}, u32[]{:S(2)}, u32[]{:S(2)}) collective-permute-start(bf16[2,256,128]{2,1,0:T(8,128)(2,1)S(1)} %pad_maximum_fusion.6), channel_id=1, source_target_pairs={{0,16},{16,0},{1,17},{17,1},{2,18},{18,2},{3,19},{19,3},{4,20},{20... | collective-permute-start | bytes 393224 | tf_op jit(solution)/shard_map/ppermute | solution.py:25
  39.7 1.7 %copy-start.5 = (bf16[768,2048]{1,0:T(8,128)(2,1)}, bf16[768,2048]{1,0:T(8,128)(2,1)S(1)}, u32[]{:S(2)}) copy-start(bf16[768,2048]{1,0:T(8,128)(2,1)S(1)} %collective-permute-done.11.refs_6_) | copy-start | bytes 9437188
  41.4 17.1 %collective-permute-start.15 = (bf16[2048,1536]{1,0:T(8,128)(2,1)S(1)}, bf16[2048,1536]{1,0:T(8,128)(2,1)S(1)}, u32[]{:S(2)}, u32[]{:S(2)}) collective-permute-start(bf16[2048,1536]{1,0:T(8,128)(2,1)S(1)} %bitcast.31), channel_id=1, source_target_pairs={{0,1},{1,0},{2,3},{3,2},{4,5},{5,4},{6,7},{7,6},{8,9},{9,8},{10,11... | collective-permute-start | bytes 18874376 | tf_op jit(solution)/shard_map/ppermute | solution.py:25
  41.8 15.5 %collective-permute-start.12 = (bf16[64,2048]{1,0:T(8,128)(2,1)S(1)}, bf16[64,2048]{1,0:T(8,128)(2,1)}, u32[]{:S(2)}, u32[]{:S(2)}) collective-permute-start(bf16[64,2048]{1,0:T(8,128)(2,1)S(1)} %multiply_convert_fusion.refs_9_), channel_id=1, source_target_pairs={{0,8},{4,12},{8,0},{12,4},{1,9},{5,13},{9,1},{13,5},{2,10},{6,14},... | collective-permute-start | bytes 786440 | tf_op jit(solution)/shard_map/ppermute | solution.py:25
  44.1 13.3 %collective-permute-start.14 = (bf16[64,2048]{1,0:T(8,128)(2,1)S(1)}, bf16[64,2048]{1,0:T(8,128)(2,1)S(1)}, u32[]{:S(2)}, u32[]{:S(2)}) collective-permute-start(bf16[64,2048]{1,0:T(8,128)(2,1)S(1)} %multiply_convert_fusion.refs_9_), channel_id=1, source_target_pairs={{0,4},{4,0},{8,12},{12,8},{1,5},{5,1},{9,13},{13,9},{2,6},{6,2},{1... | collective-permute-start | bytes 786440 | tf_op jit(solution)/shard_map/ppermute | solution.py:25
  46.1 12.3 %collective-permute-start.17 = (bf16[64,2048]{1,0:T(8,128)(2,1)S(1)}, bf16[64,2048]{1,0:T(8,128)(2,1)S(1)}, u32[]{:S(2)}, u32[]{:S(2)}) collective-permute-start(bf16[64,2048]{1,0:T(8,128)(2,1)S(1)} %multiply_convert_fusion.refs_9_), channel_id=1, source_target_pairs={{0,16},{16,0},{1,17},{17,1},{2,18},{18,2},{3,19},{19,3},{4,20},{20... | collective-permute-start | bytes 786440 | tf_op jit(solution)/shard_map/ppermute | solution.py:25
  47.6 10.9 %collective-permute-start.16 = (bf16[64,2048]{1,0:T(8,128)(2,1)S(1)}, bf16[64,2048]{1,0:T(8,128)(2,1)S(1)}, u32[]{:S(2)}, u32[]{:S(2)}) collective-permute-start(bf16[64,2048]{1,0:T(8,128)(2,1)S(1)} %multiply_convert_fusion.refs_9_), channel_id=1, source_target_pairs={{0,2},{1,3},{2,0},{3,1},{4,6},{5,7},{6,4},{7,5},{8,10},{9,11},{10,... | collective-permute-start | bytes 786440 | tf_op jit(solution)/shard_map/ppermute | solution.py:25
  57.3 8.5 %collective-permute-start.13 = (bf16[64,2048]{1,0:T(8,128)(2,1)}, bf16[64,2048]{1,0:T(8,128)(2,1)S(1)}, u32[]{:S(2)}, u32[]{:S(2)}) collective-permute-start(bf16[64,2048]{1,0:T(8,128)(2,1)} %collective-permute-done.12), channel_id=1, source_target_pairs={{0,4},{4,0},{8,12},{12,8},{1,5},{5,1},{9,13},{13,9},{2,6},{6,2},{1... | collective-permute-start | bytes 786440 | tf_op jit(solution)/shard_map/ppermute | solution.py:25
  58.5 2.7 %copy-start.3 = (bf16[2048,1536]{1,0:T(8,128)(2,1)}, bf16[2048,1536]{1,0:T(8,128)(2,1)S(1)}, u32[]{:S(2)}) copy-start(bf16[2048,1536]{1,0:T(8,128)(2,1)S(1)} %collective-permute-done.15.refs_4_) | copy-start | bytes 18874372
  61.2 20.4 %collective-permute-start.20 = (bf16[128,2048]{1,0:T(8,128)(2,1)S(1)}, bf16[128,2048]{1,0:T(8,128)(2,1)S(1)}, u32[]{:S(2)}, u32[]{:S(2)}) collective-permute-start(bf16[128,2048]{1,0:T(8,128)(2,1)S(1)} %pad_maximum_fusion.1.refs_10_), channel_id=1, source_target_pairs={{0,16},{16,0},{1,17},{17,1},{2,18},{18,2},{3,19},{19,3},{4,20},{20... | collective-permute-start | bytes 1572872 | tf_op jit(solution)/shard_map/ppermute | solution.py:25
  62.7 18.9 %collective-permute-start.18 = (bf16[128,2048]{1,0:T(8,128)(2,1)S(1)}, bf16[128,2048]{1,0:T(8,128)(2,1)S(1)}, u32[]{:S(2)}, u32[]{:S(2)}) collective-permute-start(bf16[128,2048]{1,0:T(8,128)(2,1)S(1)} %pad_maximum_fusion.1.refs_10_), channel_id=1, source_target_pairs={{0,2},{1,3},{2,0},{3,1},{4,6},{5,7},{6,4},{7,5},{8,10},{9,11},{10,... | collective-permute-start | bytes 1572872 | tf_op jit(solution)/shard_map/ppermute | solution.py:25
  65.8 14.6 %collective-permute-start.21 = (bf16[64,2048]{1,0:T(8,128)(2,1)S(1)}, bf16[64,2048]{1,0:T(8,128)(2,1)S(1)}, u32[]{:S(2)}, u32[]{:S(2)}) collective-permute-start(bf16[64,2048]{1,0:T(8,128)(2,1)S(1)} %collective-permute-done.13.refs_11_), channel_id=1, source_target_pairs={{0,16},{16,0},{1,17},{17,1},{2,18},{18,2},{3,19},{19,3},{4,20},{20... | collective-permute-start | bytes 786440 | tf_op jit(solution)/shard_map/ppermute | solution.py:25
  67.0 14.6 %collective-permute-start.19 = (bf16[64,2048]{1,0:T(8,128)(2,1)S(1)}, bf16[64,2048]{1,0:T(8,128)(2,1)S(1)}, u32[]{:S(2)}, u32[]{:S(2)}) collective-permute-start(bf16[64,2048]{1,0:T(8,128)(2,1)S(1)} %collective-permute-done.13.refs_11_), channel_id=1, source_target_pairs={{0,2},{1,3},{2,0},{3,1},{4,6},{5,7},{6,4},{7,5},{8,10},{9,11},{10,... | collective-permute-start | bytes 786440 | tf_op jit(solution)/shard_map/ppermute | solution.py:25
  81.7 12.5 %collective-permute-start.22 = (bf16[256,1024]{1,0:T(8,128)(2,1)S(1)}, bf16[256,1024]{1,0:T(8,128)(2,1)S(1)}, u32[]{:S(2)}, u32[]{:S(2)}) collective-permute-start(bf16[256,1024]{1,0:T(8,128)(2,1)S(1)} %get-tuple-element.94), channel_id=1, source_target_pairs={{0,16},{16,0},{1,17},{17,1},{2,18},{18,2},{3,19},{19,3},{4,20},{20... | collective-permute-start | bytes 1572872 | tf_op jit(solution)/shard_map/ppermute | solution.py:25
  82.3 12.2 %collective-permute-start.23 = (bf16[256,1024]{1,0:T(8,128)(2,1)S(1)}, bf16[256,1024]{1,0:T(8,128)(2,1)S(1)}, u32[]{:S(2)}, u32[]{:S(2)}) collective-permute-start(bf16[256,1024]{1,0:T(8,128)(2,1)S(1)} %get-tuple-element.95), channel_id=1, source_target_pairs={{0,2},{1,3},{2,0},{3,1},{4,6},{5,7},{6,4},{7,5},{8,10},{9,11},{10,... | collective-permute-start | bytes 1572872 | tf_op jit(solution)/shard_map/ppermute | solution.py:25
  94.5 12.7 %collective-permute-start.24 = (bf16[256,1024]{1,0:T(8,128)(2,1)S(1)}, bf16[256,1024]{1,0:T(8,128)(2,1)S(1)}, u32[]{:S(2)}, u32[]{:S(2)}) collective-permute-start(bf16[256,1024]{1,0:T(8,128)(2,1)S(1)} %get-tuple-element.96), channel_id=1, source_target_pairs={{0,16},{16,0},{1,17},{17,1},{2,18},{18,2},{3,19},{19,3},{4,20},{20... | collective-permute-start | bytes 1572872 | tf_op jit(solution)/shard_map/ppermute | solution.py:25
  95.9 11.2 %collective-permute-start.25 = (bf16[256,1024]{1,0:T(8,128)(2,1)S(1)}, bf16[256,1024]{1,0:T(8,128)(2,1)S(1)}, u32[]{:S(2)}, u32[]{:S(2)}) collective-permute-start(bf16[256,1024]{1,0:T(8,128)(2,1)S(1)} %get-tuple-element.97), channel_id=1, source_target_pairs={{0,2},{1,3},{2,0},{3,1},{4,6},{5,7},{6,4},{7,5},{8,10},{9,11},{10,... | collective-permute-start | bytes 1572872 | tf_op jit(solution)/shard_map/ppermute | solution.py:25
  107.2 9.3 %collective-permute-start.26 = (bf16[128,1024]{1,0:T(8,128)(2,1)S(1)}, bf16[128,1024]{1,0:T(8,128)(2,1)S(1)}, u32[]{:S(2)}, u32[]{:S(2)}) collective-permute-start(bf16[128,1024]{1,0:T(8,128)(2,1)S(1)} %get-tuple-element.109), channel_id=1, source_target_pairs={{0,16},{16,0},{1,17},{17,1},{2,18},{18,2},{3,19},{19,3},{4,20},{20... | collective-permute-start | bytes 786440 | tf_op jit(solution)/shard_map/ppermute | solution.py:25
  107.8 9.8 %collective-permute-start.28 = (bf16[128,1024]{1,0:T(8,128)(2,1)S(1)}, bf16[128,1024]{1,0:T(8,128)(2,1)S(1)}, u32[]{:S(2)}, u32[]{:S(2)}) collective-permute-start(bf16[128,1024]{1,0:T(8,128)(2,1)S(1)} %get-tuple-element.111), channel_id=1, source_target_pairs={{0,2},{1,3},{2,0},{3,1},{4,6},{5,7},{6,4},{7,5},{8,10},{9,11},{10,... | collective-permute-start | bytes 786440 | tf_op jit(solution)/shard_map/ppermute | solution.py:25
  109.3 11.3 %collective-permute-start.30 = (bf16[128,1024]{1,0:T(8,128)(2,1)S(1)}, bf16[128,1024]{1,0:T(8,128)(2,1)S(1)}, u32[]{:S(2)}, u32[]{:S(2)}) collective-permute-start(bf16[128,1024]{1,0:T(8,128)(2,1)S(1)} %get-tuple-element.112), channel_id=1, source_target_pairs={{0,16},{16,0},{1,17},{17,1},{2,18},{18,2},{3,19},{19,3},{4,20},{20... | collective-permute-start | bytes 786440 | tf_op jit(solution)/shard_map/ppermute | solution.py:25
  111.1 10.0 %collective-permute-start.31 = (bf16[128,1024]{1,0:T(8,128)(2,1)S(1)}, bf16[128,1024]{1,0:T(8,128)(2,1)S(1)}, u32[]{:S(2)}, u32[]{:S(2)}) collective-permute-start(bf16[128,1024]{1,0:T(8,128)(2,1)S(1)} %get-tuple-element.113), channel_id=1, source_target_pairs={{0,2},{1,3},{2,0},{3,1},{4,6},{5,7},{6,4},{7,5},{8,10},{9,11},{10,... | collective-permute-start | bytes 786440 | tf_op jit(solution)/shard_map/ppermute | solution.py:25
  116.5 8.3 %collective-permute-start.27 = (bf16[128,1024]{1,0:T(8,128)(2,1)S(1)}, bf16[128,1024]{1,0:T(8,128)(2,1)S(1)}, u32[]{:S(2)}, u32[]{:S(2)}) collective-permute-start(bf16[128,1024]{1,0:T(8,128)(2,1)S(1)} %add_convert_fusion.5), channel_id=1, source_target_pairs={{0,2},{1,3},{2,0},{3,1},{4,6},{5,7},{6,4},{7,5},{8,10},{9,11},{10,... | collective-permute-start | bytes 786440 | tf_op jit(solution)/shard_map/ppermute | solution.py:25
  117.7 7.1 %collective-permute-start.29 = (bf16[128,1024]{1,0:T(8,128)(2,1)S(1)}, bf16[128,1024]{1,0:T(8,128)(2,1)S(1)}, u32[]{:S(2)}, u32[]{:S(2)}) collective-permute-start(bf16[128,1024]{1,0:T(8,128)(2,1)S(1)} %add_convert_fusion.4), channel_id=1, source_target_pairs={{0,16},{16,0},{1,17},{17,1},{2,18},{18,2},{3,19},{19,3},{4,20},{20... | collective-permute-start | bytes 786440 | tf_op jit(solution)/shard_map/ppermute | solution.py:25
  125.3 20.1 %copy-start.7 = (f32[128,2048]{1,0:T(8,128)S(1)}, f32[128,2048]{1,0:T(8,128)}, u32[]{:S(2)}) copy-start(f32[128,2048]{1,0:T(8,128)} %copy-done.6) | copy-start | bytes 3145732
  125.4 6.4 %collective-permute-start.34 = (bf16[64,2048]{1,0:T(8,128)(2,1)S(1)}, bf16[64,2048]{1,0:T(8,128)(2,1)S(1)}, u32[]{:S(2)}, u32[]{:S(2)}) collective-permute-start(bf16[64,2048]{1,0:T(8,128)(2,1)S(1)} %get-tuple-element.126), channel_id=1, source_target_pairs={{0,4},{4,0},{8,12},{12,8},{1,5},{5,1},{9,13},{13,9},{2,6},{6,2},{1... | collective-permute-start | bytes 786440 | tf_op jit(solution)/shard_map/ppermute | solution.py:25
  125.7 6.4 %collective-permute-start.32 = (bf16[128,1024]{1,0:T(8,128)(2,1)S(1)}, bf16[128,1024]{1,0:T(8,128)(2,1)S(1)}, u32[]{:S(2)}, u32[]{:S(2)}) collective-permute-start(bf16[128,1024]{1,0:T(8,128)(2,1)S(1)} %get-tuple-element.120), channel_id=1, source_target_pairs={{0,2},{1,3},{2,0},{3,1},{4,6},{5,7},{6,4},{7,5},{8,10},{9,11},{10,... | collective-permute-start | bytes 786440 | tf_op jit(solution)/shard_map/ppermute | solution.py:25
  127.1 6.4 %collective-permute-start.33 = (bf16[128,1024]{1,0:T(8,128)(2,1)S(1)}, bf16[128,1024]{1,0:T(8,128)(2,1)S(1)}, u32[]{:S(2)}, u32[]{:S(2)}) collective-permute-start(bf16[128,1024]{1,0:T(8,128)(2,1)S(1)} %get-tuple-element.121), channel_id=1, source_target_pairs={{0,16},{16,0},{1,17},{17,1},{2,18},{18,2},{3,19},{19,3},{4,20},{20... | collective-permute-start | bytes 786440 | tf_op jit(solution)/shard_map/ppermute | solution.py:25
  133.6 10.9 %collective-permute-start.36 = (bf16[64,2048]{1,0:T(8,128)(2,1)S(1)}, bf16[64,2048]{1,0:T(8,128)(2,1)S(1)}, u32[]{:S(2)}, u32[]{:S(2)}) collective-permute-start(bf16[64,2048]{1,0:T(8,128)(2,1)S(1)} %fusion.6), channel_id=1, source_target_pairs={{0,8},{4,12},{8,0},{12,4},{1,9},{5,13},{9,1},{13,5},{2,10},{6,14},... | collective-permute-start | bytes 786440 | tf_op jit(solution)/shard_map/ppermute | solution.py:25
  137.3 8.1 %collective-permute-start.35 = (bf16[64,2048]{1,0:T(8,128)(2,1)S(1)}, bf16[64,2048]{1,0:T(8,128)(2,1)S(1)}, u32[]{:S(2)}, u32[]{:S(2)}) collective-permute-start(bf16[64,2048]{1,0:T(8,128)(2,1)S(1)} %get-tuple-element.123), channel_id=1, source_target_pairs={{0,4},{4,0},{8,12},{12,8},{1,5},{5,1},{9,13},{13,9},{2,6},{6,2},{1... | collective-permute-start | bytes 786440 | tf_op jit(solution)/shard_map/ppermute | solution.py:25

commit v11 on v10

--- a/solution.py
+++ b/solution.py
@@ -67,7 +67,7 @@
     )(*by_rep, *by_role)
 
 
-def spread_rows(own, weight, coded, tables_of):
+def spread_rows(own, coded, tables_of):
     rows, half = own.shape[0], own.shape[1] // 2
 
     def both_ways(part):
@@ -79,7 +79,7 @@
         blocks = blocks + [swap(block, "seq", bits) for block in blocks]
     beyond = [swap(block, "seq", bits_left[-1]) for block in blocks]
     middle = jnp.concatenate(blocks[1:] + beyond[:-1], axis=0)
-    middle, weight, coded, *outer = ready(middle, weight, coded, *both_ways(own))
+    middle, coded, *outer = ready(middle, coded, *both_ways(own))
     last, *tables = ready(beyond[-1], *tables_of(coded))
     by_rep, by_role = zip(outer, both_ways(middle), both_ways(last))
     low, high = pack_corners(by_rep, by_role)
@@ -90,7 +90,7 @@
         for parts in (by_rep, by_role, (own, middle, last))
     ]
     groups.insert(2, [(0, 0, corner_low), (0, half, corner_high)])
-    return groups, weight, tables
+    return groups, tables
 
 
 def added(first, second):
@@ -519,10 +519,10 @@
         hidden_in[0], attn_gain, w_keyval, k_gain, expert_ids[0], gate_fixed[0]
     )
     across_rows = swap(normed, "rep", ACROSS)
-    pair_rows = swap(normed, "rep", PAIR)
     line = jnp.concatenate(
         [own_payload] + [swap(own_payload, "seq", bits) for bits in seq_order()[1:]], axis=0
     )
+    pair_rows = swap(ready(normed, line)[0], "rep", PAIR)
     corner_rows = swap(across_rows, "rep", PAIR)
     line_routes = line[:, 2 * kv_width :]
 
@@ -534,7 +534,7 @@
         ]
 
     sent = jnp.concatenate(head_kv(rep_index ^ ACROSS) + [line_routes], axis=1)
-    sent, across_rows, pair_rows = ready(sent, across_rows, pair_rows)
+    sent, across_rows = ready(sent, across_rows)
     across = swap(sent, "rep", ACROSS)
     half_kv = jnp.concatenate(
         [jnp.concatenate(head_kv(rep_index), axis=1), across[:, : 2 * head_dim]], axis=0
@@ -547,12 +547,11 @@
     kept, leaving = attend(queries, half_kv, pair_kv, w_out, head_dim)
     leaving, own_dn = ready(swap(leaving, "rep", PAIR), w_down[0])
     halves = kept + leaving
-    far_dn = swap(own_dn, "rep", PAIR)
+    far_dn, far_gu = swap(own_dn, "rep", PAIR), swap(w_gateup[0], "rep", PAIR)
     far_sum = halves[row_count:].astype(jnp.bfloat16)
-    across_sum, coded, far_dn, own_gu = ready(
-        swap(far_sum, "rep", ACROSS), coded, far_dn, w_gateup[0]
-    )
-    far_gu = swap(own_gu, "rep", PAIR)
+    across_sum, coded, far_dn, far_gu = ready(
+        swap(far_sum, "rep", ACROSS), coded, far_dn, far_gu
+    )
     attended = halves[:row_count] + across_sum.astype(jnp.float32)
     mixed = tokens + attended
 
@@ -560,9 +559,8 @@
 
     capacity = max(2, 7 * row_count * top_count // (4 * expert_count))
     slots = -(-capacity * (coded.shape[1] // row_count) // 16) * 16
-    rows, far_gu, tables = spread_rows(
+    rows, tables = spread_rows(
         moe_in,
-        far_gu,
         coded,
         lambda codes: make_tables(codes, lax.axis_index(EVERY), slots, top_count),
     )

time: 146 us -> 140 us (0.959)
  local copies, waits for them, and re-layouts: 4.63 us -> 0.25 us
  waiting for transfers between devices: 65.7 us -> 63.5 us
    unnamed x27 -> x21, local copies, waits for them, and re-layouts: 4.46 us -> 0.08 us
    ppermute x37, waiting for transfers between devices: 65.7 us -> 63.5 us  [swap(): return lax.ppermute(block, axis, [(i, i ^ bits) for i in range(size)])]
  transfers between devices with their start and end apart: 37 -> 37, of which waited for: 22 -> 23; matrix products, arithmetic and copies ran while one was open for 1% -> 1% of each run, Pallas kernels for 15% -> 19%
where the time goes in v11:
time: 140 us
  waiting for transfers between devices  63.5 us (45%)
  starting transfers between devices  45 us (32%)
  Pallas kernels  27 us (19%)
  other arithmetic  3.34 us (2%)
    ppermute x37, waiting for transfers between devices, swap(): return lax.ppermute(block, axis, [(i, i ^ bits) for i in range(size)])  63.5 us
    ppermute x37, starting transfers between devices, swap(): return lax.ppermute(block, axis, [(i, i ^ bits) for i in range(size)])  45 us
    pallas_call x2, Pallas kernels, run_experts(): pl.pallas_call(lambda *refs: expert_kernel(first, spots, cuts, *refs), ou...  19.2 us
  transfers between devices with their start and end apart: 37, of which 23 were waited for; matrix products, arithmetic and copies ran while one was open for 1% of the time, Pallas kernels for 19%

profile of v11, /device:TPU:0, one launch (start us, length us, event | category | flops | bytes accessed | tf_op | source)
XLA Modules:
  0.0 139.5 jit_solution(7752861330759872873)
XLA Ops:
  0.0 0.5 collective-permute-start.12
  0.5 2.6 %prepare.1 = (bf16[64,2048]{1,0:T(8,128)(2,1)S(1)}, bf16[64,640]{1,0:T(8,128)(2,1)S(1)}) custom-call(bf16[64,2048]{1,0:T(8,128)(2,1)} %bitcast.33, f32[1,2048]{1,0:T(1,128)} %bitcast.34, bf16[2,2048,256]{2,1,0:T(8,128)(2,1)} %refs_2_.1, f32[1,128]{1,0:T(1,128)} %bitcast.37, s32[8,64]{1,0:T(8,128)} %bitcast.35, s32[8,64]{1,0:T(8,128)} %bitcast.36), custom_call_target="tpu_custom_call" | custom-call | flops 134217728 | bytes 2621440 | tf_op jit(solution)/shard_map/prepare/pallas_call | solution.py:189
  3.1 4.7 %collective-permute-start.2 = (bf16[64,640]{1,0:T(8,128)(2,1)S(1)}, bf16[64,640]{1,0:T(8,128)(2,1)S(1)}, u32[]{:S(2)}, u32[]{:S(2)}) collective-permute-start(bf16[64,640]{1,0:T(8,128)(2,1)S(1)} %get-tuple-element.65), channel_id=1, source_target_pairs={{0,12},{4,8},{8,4},{12,0},{1,13},{5,9},{9,5},{13,1},{2,14},{6,10},... | collective-permute-start | bytes 245768 | tf_op jit(solution)/shard_map/ppermute | solution.py:25
  7.7 0.6 collective-permute-start
  8.4 1.7 %collective-permute-start.3 = (bf16[64,2048]{1,0:T(8,128)(2,1)S(1)}, bf16[64,2048]{1,0:T(8,128)(2,1)S(1)}, u32[]{:S(2)}, u32[]{:S(2)}) collective-permute-start(bf16[64,2048]{1,0:T(8,128)(2,1)S(1)} %get-tuple-element.67.first_ref), channel_id=1, source_target_pairs={{0,2},{1,3},{2,0},{3,1},{4,6},{5,7},{6,4},{7,5},{8,10},{9,11},{10,... | collective-permute-start | bytes 786440 | tf_op jit(solution)/shard_map/ppermute | solution.py:25
  10.0 5.1 %collective-permute-done = bf16[64,640]{1,0:T(8,128)(2,1)S(1)} collective-permute-done((bf16[64,640]{1,0:T(8,128)(2,1)S(1)}, bf16[64,640]{1,0:T(8,128)(2,1)S(1)}, u32[]{:S(2)}, u32[]{:S(2)}) %collective-permute-start) | collective-permute-done | bytes 81952 | tf_op jit(solution)/shard_map/ppermute | solution.py:25
  15.3 1.1 collective-permute-done.3.second_ref
  16.4 1.5 %collective-permute-start.6 = (bf16[256,384]{1,0:T(8,128)(2,1)S(1)}, bf16[256,384]{1,0:T(8,128)(2,1)S(1)}, u32[]{:S(2)}, u32[]{:S(2)}) collective-permute-start(bf16[256,384]{1,0:T(8,128)(2,1)S(1)} %pad_maximum_fusion.5), channel_id=1, source_target_pairs={{0,2},{1,3},{2,0},{3,1},{4,6},{5,7},{6,4},{7,5},{8,10},{9,11},{10,... | collective-permute-start | bytes 589832 | tf_op jit(solution)/shard_map/ppermute | solution.py:25
  17.9 0.5 collective-permute-start.5
  18.4 3.7 %collective-permute-done.6 = bf16[256,384]{1,0:T(8,128)(2,1)S(1)} collective-permute-done((bf16[256,384]{1,0:T(8,128)(2,1)S(1)}, bf16[256,384]{1,0:T(8,128)(2,1)S(1)}, u32[]{:S(2)}, u32[]{:S(2)}) %collective-permute-start.6) | collective-permute-done | bytes 196640 | tf_op jit(solution)/shard_map/ppermute | solution.py:25
  22.3 0.9 queries.1.refs_0_
  23.1 0.6 collective-permute-done.7.refs_2_
  23.7 2.7 %attend.1 = (f32[128,2048]{1,0:T(8,128)S(1)}, f32[128,2048]{1,0:T(8,128)S(1)}) custom-call(bf16[256,512]{1,0:T(8,128)(2,1)S(1)} %queries.1.refs_0_, bf16[512,256]{1,0:T(8,128)(2,1)S(1)} %pad_maximum_fusion.3.refs_1_, bf16[512,256]{1,0:T(8,128)(2,1)S(1)} %collective-permute-done.7.refs_2_, bf16[512,2048]{1,0:T(8,128)(2,1)S(1)} %copy-done.2), custom_call_target="tpu_custom_call" | custom-call | flops 1073741824 | bytes 4194304 | tf_op jit(solution)/shard_map/attend/pallas_call | solution.py:268
  26.5 0.2 collective-permute-start.8
  26.7 2.5 %collective-permute-done.8 = f32[128,2048]{1,0:T(8,128)S(1)} collective-permute-done((f32[128,2048]{1,0:T(8,128)S(1)}, f32[128,2048]{1,0:T(8,128)S(1)}, u32[]{:S(2)}, u32[]{:S(2)}) %collective-permute-start.8) | collective-permute-done | bytes 1048608 | tf_op jit(solution)/shard_map/ppermute | solution.py:25
  29.5 1.5 %collective-permute-start.9 = (bf16[64,2048]{1,0:T(8,128)(2,1)S(1)}, bf16[64,2048]{1,0:T(8,128)(2,1)S(1)}, u32[]{:S(2)}, u32[]{:S(2)}) collective-permute-start(bf16[64,2048]{1,0:T(8,128)(2,1)S(1)} %slice.137), channel_id=1, source_target_pairs={{0,2},{1,3},{2,0},{3,1},{4,6},{5,7},{6,4},{7,5},{8,10},{9,11},{10,... | collective-permute-start | bytes 786440 | tf_op jit(solution)/shard_map/ppermute | solution.py:25
  31.1 1.6 %collective-permute-start.10 = (bf16[2,256,128]{2,1,0:T(8,128)(2,1)S(1)}, bf16[2,256,128]{2,1,0:T(8,128)(2,1)S(1)}, u32[]{:S(2)}, u32[]{:S(2)}) collective-permute-start(bf16[2,256,128]{2,1,0:T(8,128)(2,1)S(1)} %pad_maximum_fusion.6), channel_id=1, source_target_pairs={{0,16},{16,0},{1,17},{17,1},{2,18},{18,2},{3,19},{19,3},{4,20},{20... | collective-permute-start | bytes 393224 | tf_op jit(solution)/shard_map/ppermute | solution.py:25
  32.7 4.0 %collective-permute-done.10 = bf16[2,256,128]{2,1,0:T(8,128)(2,1)S(1)} collective-permute-done((bf16[2,256,128]{2,1,0:T(8,128)(2,1)S(1)}, bf16[2,256,128]{2,1,0:T(8,128)(2,1)S(1)}, u32[]{:S(2)}, u32[]{:S(2)}) %collective-permute-start.10) | collective-permute-done | bytes 131104 | tf_op jit(solution)/shard_map/ppermute | solution.py:25
  36.7 1.5 %collective-permute-done.9 = bf16[64,2048]{1,0:T(8,128)(2,1)S(1)} collective-permute-done((bf16[64,2048]{1,0:T(8,128)(2,1)S(1)}, bf16[64,2048]{1,0:T(8,128)(2,1)S(1)}, u32[]{:S(2)}, u32[]{:S(2)}) %collective-permute-start.9) | collective-permute-done | bytes 262176 | tf_op jit(solution)/shard_map/ppermute | solution.py:25
  38.2 0.2 multiply_reduce_fusion
  38.6 2.4 %collective-permute-start.13 = (bf16[64,2048]{1,0:T(8,128)(2,1)S(1)}, bf16[64,2048]{1,0:T(8,128)(2,1)}, u32[]{:S(2)}, u32[]{:S(2)}) collective-permute-start(bf16[64,2048]{1,0:T(8,128)(2,1)S(1)} %multiply_convert_fusion.refs_9_), channel_id=1, source_target_pairs={{0,8},{4,12},{8,0},{12,4},{1,9},{5,13},{9,1},{13,5},{2,10},{6,14},... | collective-permute-start | bytes 786440 | tf_op jit(solution)/shard_map/ppermute | solution.py:25
  40.9 1.7 %collective-permute-start.15 = (bf16[64,2048]{1,0:T(8,128)(2,1)S(1)}, bf16[64,2048]{1,0:T(8,128)(2,1)S(1)}, u32[]{:S(2)}, u32[]{:S(2)}) collective-permute-start(bf16[64,2048]{1,0:T(8,128)(2,1)S(1)} %multiply_convert_fusion.refs_9_), channel_id=1, source_target_pairs={{0,4},{4,0},{8,12},{12,8},{1,5},{5,1},{9,13},{13,9},{2,6},{6,2},{1... | collective-permute-start | bytes 786440 | tf_op jit(solution)/shard_map/ppermute | solution.py:25
  42.6 1.5 %collective-permute-start.17 = (bf16[64,2048]{1,0:T(8,128)(2,1)S(1)}, bf16[64,2048]{1,0:T(8,128)(2,1)S(1)}, u32[]{:S(2)}, u32[]{:S(2)}) collective-permute-start(bf16[64,2048]{1,0:T(8,128)(2,1)S(1)} %multiply_convert_fusion.refs_9_), channel_id=1, source_target_pairs={{0,16},{16,0},{1,17},{17,1},{2,18},{18,2},{3,19},{19,3},{4,20},{20... | collective-permute-start | bytes 786440 | tf_op jit(solution)/shard_map/ppermute | solution.py:25
  44.1 1.5 %collective-permute-start.16 = (bf16[64,2048]{1,0:T(8,128)(2,1)S(1)}, bf16[64,2048]{1,0:T(8,128)(2,1)S(1)}, u32[]{:S(2)}, u32[]{:S(2)}) collective-permute-start(bf16[64,2048]{1,0:T(8,128)(2,1)S(1)} %multiply_convert_fusion.refs_9_), channel_id=1, source_target_pairs={{0,2},{1,3},{2,0},{3,1},{4,6},{5,7},{6,4},{7,5},{8,10},{9,11},{10,... | collective-permute-start | bytes 786440 | tf_op jit(solution)/shard_map/ppermute | solution.py:25
  45.6 7.5 %collective-permute-done.13 = bf16[64,2048]{1,0:T(8,128)(2,1)} collective-permute-done((bf16[64,2048]{1,0:T(8,128)(2,1)S(1)}, bf16[64,2048]{1,0:T(8,128)(2,1)}, u32[]{:S(2)}, u32[]{:S(2)}) %collective-permute-start.13) | collective-permute-done | bytes 262176 | tf_op jit(solution)/shard_map/ppermute | solution.py:25
  53.3 1.0 pad_maximum_fusion.1.refs_10_
  54.3 1.6 %collective-permute-start.20 = (bf16[128,2048]{1,0:T(8,128)(2,1)S(1)}, bf16[128,2048]{1,0:T(8,128)(2,1)S(1)}, u32[]{:S(2)}, u32[]{:S(2)}) collective-permute-start(bf16[128,2048]{1,0:T(8,128)(2,1)S(1)} %pad_maximum_fusion.1.refs_10_), channel_id=1, source_target_pairs={{0,16},{16,0},{1,17},{17,1},{2,18},{18,2},{3,19},{19,3},{4,20},{20... | collective-permute-start | bytes 1572872 | tf_op jit(solution)/shard_map/ppermute | solution.py:25
  55.9 1.5 %collective-permute-start.18 = (bf16[128,2048]{1,0:T(8,128)(2,1)S(1)}, bf16[128,2048]{1,0:T(8,128)(2,1)S(1)}, u32[]{:S(2)}, u32[]{:S(2)}) collective-permute-start(bf16[128,2048]{1,0:T(8,128)(2,1)S(1)} %pad_maximum_fusion.1.refs_10_), channel_id=1, source_target_pairs={{0,2},{1,3},{2,0},{3,1},{4,6},{5,7},{6,4},{7,5},{8,10},{9,11},{10,... | collective-permute-start | bytes 1572872 | tf_op jit(solution)/shard_map/ppermute | solution.py:25
  57.4 1.6 %tables.1 = (bf16[4,224,256]{2,1,0:T(8,128)(2,1)S(1)}, bf16[2,4,256,112]{3,2,1,0:T(8,128)(2,1)S(1)}, f32[4,256,2]{2,1,0:T(8,128)S(1)}) custom-call(s32[1]{0:T(128)} %bitcast.12.refs_0_, bf16[4,256,128]{2,1,0:T(8,128)(2,1)S(1)} %pad_maximum_fusion.4.refs_1_), custom_call_target="tpu_custom_call" | custom-call | flops 134217728 | bytes 917504 | tf_op jit(solution)/shard_map/tables/pallas_call | solution.py:331
  59.0 1.6 %collective-permute-done.14.refs_11_ = bf16[64,2048]{1,0:T(8,128)(2,1)S(1)} collective-permute-done((bf16[64,2048]{1,0:T(8,128)(2,1)}, bf16[64,2048]{1,0:T(8,128)(2,1)S(1)}, u32[]{:S(2)}, u32[]{:S(2)}) %collective-permute-start.14) | collective-permute-done | bytes 262176 | tf_op jit(solution)/shard_map/ppermute | solution.py:25
  60.6 1.4 collective-permute-start.21
  62.0 1.5 %collective-permute-start.19 = (bf16[64,2048]{1,0:T(8,128)(2,1)S(1)}, bf16[64,2048]{1,0:T(8,128)(2,1)S(1)}, u32[]{:S(2)}, u32[]{:S(2)}) collective-permute-start(bf16[64,2048]{1,0:T(8,128)(2,1)S(1)} %collective-permute-done.14.refs_11_), channel_id=1, source_target_pairs={{0,2},{1,3},{2,0},{3,1},{4,6},{5,7},{6,4},{7,5},{8,10},{9,11},{10,... | collective-permute-start | bytes 786440 | tf_op jit(solution)/shard_map/ppermute | solution.py:25
  63.5 5.7 %collective-permute-done.20.refs_11_.refs_4_ = bf16[128,2048]{1,0:T(8,128)(2,1)S(1)} collective-permute-done((bf16[128,2048]{1,0:T(8,128)(2,1)S(1)}, bf16[128,2048]{1,0:T(8,128)(2,1)S(1)}, u32[]{:S(2)}, u32[]{:S(2)}) %collective-permute-start.20) | collective-permute-done | bytes 524320 | tf_op jit(solution)/shard_map/ppermute | solution.py:25
  69.2 1.5 %collective-permute-done.18.refs_8_.refs_1_ = bf16[128,2048]{1,0:T(8,128)(2,1)S(1)} collective-permute-done((bf16[128,2048]{1,0:T(8,128)(2,1)S(1)}, bf16[128,2048]{1,0:T(8,128)(2,1)S(1)}, u32[]{:S(2)}, u32[]{:S(2)}) %collective-permute-start.18) | collective-permute-done | bytes 524320 | tf_op jit(solution)/shard_map/ppermute | solution.py:25
  70.8 2.8 %collective-permute-done.21.refs_12_.refs_5_ = bf16[64,2048]{1,0:T(8,128)(2,1)S(1)} collective-permute-done((bf16[64,2048]{1,0:T(8,128)(2,1)S(1)}, bf16[64,2048]{1,0:T(8,128)(2,1)S(1)}, u32[]{:S(2)}, u32[]{:S(2)}) %collective-permute-start.21) | collective-permute-done | bytes 262176 | tf_op jit(solution)/shard_map/ppermute | solution.py:25
  73.6 1.2 collective-permute-done.19.refs_9_.refs_2_
  74.9 0.6 collective-permute-start.22
  75.5 1.5 %collective-permute-start.23 = (bf16[256,1024]{1,0:T(8,128)(2,1)S(1)}, bf16[256,1024]{1,0:T(8,128)(2,1)S(1)}, u32[]{:S(2)}, u32[]{:S(2)}) collective-permute-start(bf16[256,1024]{1,0:T(8,128)(2,1)S(1)} %get-tuple-element.93), channel_id=1, source_target_pairs={{0,2},{1,3},{2,0},{3,1},{4,6},{5,7},{6,4},{7,5},{8,10},{9,11},{10,... | collective-permute-start | bytes 1572872 | tf_op jit(solution)/shard_map/ppermute | solution.py:25
  77.0 9.5 %experts.2 = (bf16[256,1024]{1,0:T(8,128)(2,1)S(1)}, bf16[256,1024]{1,0:T(8,128)(2,1)S(1)}, bf16[256,1024]{1,0:T(8,128)(2,1)S(1)}, bf16[256,1024]{1,0:T(8,128)(2,1)S(1)}) custom-call(bf16[4,224,256]{2,1,0:T(8,128)(2,1)S(1)} %get-tuple-element.79.refs_0_, bf16[2,4,256,112]{3,2,1,0:T(8,128)(2,1)S(1)} %get-tuple-element.80.refs_1_, ...), custom_call_target="tpu_custom_call" | custom-call | flops 4227858432 | bytes 23068672 | tf_op jit(solution)/shard_map/experts/pallas_call | solution.py:461
  86.5 0.8 collective-permute-done.22.refs_7_
  87.3 0.3 collective-permute-done.23.refs_8_
  87.6 1.4 %collective-permute-start.24 = (bf16[256,1024]{1,0:T(8,128)(2,1)S(1)}, bf16[256,1024]{1,0:T(8,128)(2,1)S(1)}, u32[]{:S(2)}, u32[]{:S(2)}) collective-permute-start(bf16[256,1024]{1,0:T(8,128)(2,1)S(1)} %get-tuple-element.94), channel_id=1, source_target_pairs={{0,16},{16,0},{1,17},{17,1},{2,18},{18,2},{3,19},{19,3},{4,20},{20... | collective-permute-start | bytes 1572872 | tf_op jit(solution)/shard_map/ppermute | solution.py:25
  89.1 1.5 %collective-permute-start.25 = (bf16[256,1024]{1,0:T(8,128)(2,1)S(1)}, bf16[256,1024]{1,0:T(8,128)(2,1)S(1)}, u32[]{:S(2)}, u32[]{:S(2)}) collective-permute-start(bf16[256,1024]{1,0:T(8,128)(2,1)S(1)} %get-tuple-element.95), channel_id=1, source_target_pairs={{0,2},{1,3},{2,0},{3,1},{4,6},{5,7},{6,4},{7,5},{8,10},{9,11},{10,... | collective-permute-start | bytes 1572872 | tf_op jit(solution)/shard_map/ppermute | solution.py:25
  90.6 9.7 %experts.3 = (bf16[128,1024]{1,0:T(8,128)(2,1)S(1)}, bf16[128,1024]{1,0:T(8,128)(2,1)S(1)}, bf16[128,1024]{1,0:T(8,128)(2,1)S(1)}, bf16[128,1024]{1,0:T(8,128)(2...) custom-call(bf16[4,224,256]{2,1,0:T(8,128)(2,1)S(1)} %get-tuple-element.79.refs_0_, ...), custom_call_target="tpu_custom_call" | custom-call | flops 4227858432 | bytes 23068672 | tf_op jit(solution)/shard_map/experts/pallas_call | solution.py:461
  100.3 0.7 collective-permute-start.26
  100.9 1.5 %collective-permute-start.28 = (bf16[128,1024]{1,0:T(8,128)(2,1)S(1)}, bf16[128,1024]{1,0:T(8,128)(2,1)S(1)}, u32[]{:S(2)}, u32[]{:S(2)}) collective-permute-start(bf16[128,1024]{1,0:T(8,128)(2,1)S(1)} %get-tuple-element.109), channel_id=1, source_target_pairs={{0,2},{1,3},{2,0},{3,1},{4,6},{5,7},{6,4},{7,5},{8,10},{9,11},{10,... | collective-permute-start | bytes 786440 | tf_op jit(solution)/shard_map/ppermute | solution.py:25
  102.5 1.7 %collective-permute-start.30 = (bf16[128,1024]{1,0:T(8,128)(2,1)S(1)}, bf16[128,1024]{1,0:T(8,128)(2,1)S(1)}, u32[]{:S(2)}, u32[]{:S(2)}) collective-permute-start(bf16[128,1024]{1,0:T(8,128)(2,1)S(1)} %get-tuple-element.110), channel_id=1, source_target_pairs={{0,16},{16,0},{1,17},{17,1},{2,18},{18,2},{3,19},{19,3},{4,20},{20... | collective-permute-start | bytes 786440 | tf_op jit(solution)/shard_map/ppermute | solution.py:25
  104.4 5.2 %collective-permute-done.26 = bf16[128,1024]{1,0:T(8,128)(2,1)S(1)} collective-permute-done((bf16[128,1024]{1,0:T(8,128)(2,1)S(1)}, bf16[128,1024]{1,0:T(8,128)(2,1)S(1)}, u32[]{:S(2)}, u32[]{:S(2)}) %collective-permute-start.26) | collective-permute-done | bytes 262176 | tf_op jit(solution)/shard_map/ppermute | solution.py:25
  109.7 1.0 collective-permute-start.27
  110.7 1.3 collective-permute-start.29
  112.0 1.8 %collective-permute-done.30 = bf16[128,1024]{1,0:T(8,128)(2,1)S(1)} collective-permute-done((bf16[128,1024]{1,0:T(8,128)(2,1)S(1)}, bf16[128,1024]{1,0:T(8,128)(2,1)S(1)}, u32[]{:S(2)}, u32[]{:S(2)}) %collective-permute-start.30) | collective-permute-done | bytes 262176 | tf_op jit(solution)/shard_map/ppermute | solution.py:25
  113.8 0.4 collective-permute-done.31
  114.1 3.8 %collective-permute-done.27 = bf16[128,1024]{1,0:T(8,128)(2,1)S(1)} collective-permute-done((bf16[128,1024]{1,0:T(8,128)(2,1)S(1)}, bf16[128,1024]{1,0:T(8,128)(2,1)S(1)}, u32[]{:S(2)}, u32[]{:S(2)}) %collective-permute-start.27) | collective-permute-done | bytes 262176 | tf_op jit(solution)/shard_map/ppermute | solution.py:25
  117.9 0.2 add_convert_fusion.2
  118.1 0.3 add_convert_fusion
  118.6 1.6 %collective-permute-start.32 = (bf16[128,1024]{1,0:T(8,128)(2,1)S(1)}, bf16[128,1024]{1,0:T(8,128)(2,1)S(1)}, u32[]{:S(2)}, u32[]{:S(2)}) collective-permute-start(bf16[128,1024]{1,0:T(8,128)(2,1)S(1)} %get-tuple-element.118), channel_id=1, source_target_pairs={{0,2},{1,3},{2,0},{3,1},{4,6},{5,7},{6,4},{7,5},{8,10},{9,11},{10,... | collective-permute-start | bytes 786440 | tf_op jit(solution)/shard_map/ppermute | solution.py:25
  120.2 1.1 collective-permute-start.33
  121.3 4.0 %collective-permute-done.34 = bf16[64,2048]{1,0:T(8,128)(2,1)S(1)} collective-permute-done((bf16[64,2048]{1,0:T(8,128)(2,1)S(1)}, bf16[64,2048]{1,0:T(8,128)(2,1)S(1)}, u32[]{:S(2)}, u32[]{:S(2)}) %collective-permute-start.34) | collective-permute-done | bytes 262176 | tf_op jit(solution)/shard_map/ppermute | solution.py:25
  125.4 1.1 collective-permute-done.33
  126.7 3.6 %collective-permute-start.36 = (bf16[64,2048]{1,0:T(8,128)(2,1)S(1)}, bf16[64,2048]{1,0:T(8,128)(2,1)S(1)}, u32[]{:S(2)}, u32[]{:S(2)}) collective-permute-start(bf16[64,2048]{1,0:T(8,128)(2,1)S(1)} %fusion.6), channel_id=1, source_target_pairs={{0,8},{4,12},{8,0},{12,4},{1,9},{5,13},{9,1},{13,5},{2,10},{6,14},... | collective-permute-start | bytes 786440 | tf_op jit(solution)/shard_map/ppermute | solution.py:25
  130.4 1.0 collective-permute-start.35
  131.4 6.2 %collective-permute-done.36 = bf16[64,2048]{1,0:T(8,128)(2,1)S(1)} collective-permute-done((bf16[64,2048]{1,0:T(8,128)(2,1)S(1)}, bf16[64,2048]{1,0:T(8,128)(2,1)S(1)}, u32[]{:S(2)}, u32[]{:S(2)}) %collective-permute-start.36) | collective-permute-done | bytes 262176 | tf_op jit(solution)/shard_map/ppermute | solution.py:25
  137.6 1.0 collective-permute-done.35
  138.6 0.9 fusion.8
  (62 shorter events, 1.7 us)
Async XLA Ops:
  0.0 22.2 %copy-start.1 = (f32[128]{0:T(128)S(1)}, f32[128]{0:T(128)}, u32[]{:S(2)}) copy-start(f32[128]{0:T(128)} %param.16) | copy-start | bytes 1540
  0.0 22.2 %copy-start = (bf16[2048,512]{1,0:T(8,128)(2,1)S(1)}, bf16[2048,512]{1,0:T(8,128)(2,1)}, u32[]{:S(2)}) copy-start(bf16[2048,512]{1,0:T(8,128)(2,1)} %weight_ref.1) | copy-start | bytes 6291460
  0.0 38.2 %collective-permute-start.12 = (bf16[2048,1536]{1,0:T(8,128)(2,1)}, bf16[2048,1536]{1,0:T(8,128)(2,1)}, u32[]{:S(2)}, u32[]{:S(2)}) collective-permute-start(bf16[2048,1536]{1,0:T(8,128)(2,1)} %bitcast.27), channel_id=1, source_target_pairs={{0,1},{1,0},{2,3},{3,2},{4,5},{5,4},{6,7},{7,6},{8,9},{9,8},{10,11... | collective-permute-start | bytes 18874376 | tf_op jit(solution)/shard_map/ppermute | solution.py:25
  3.1 12.1 %collective-permute-start.2 = (bf16[64,640]{1,0:T(8,128)(2,1)S(1)}, bf16[64,640]{1,0:T(8,128)(2,1)S(1)}, u32[]{:S(2)}, u32[]{:S(2)}) collective-permute-start(bf16[64,640]{1,0:T(8,128)(2,1)S(1)} %get-tuple-element.65), channel_id=1, source_target_pairs={{0,12},{4,8},{8,4},{12,0},{1,13},{5,9},{9,5},{13,1},{2,14},{6,10},... | collective-permute-start | bytes 245768 | tf_op jit(solution)/shard_map/ppermute | solution.py:25
  7.7 7.4 %collective-permute-start.1 = (bf16[64,640]{1,0:T(8,128)(2,1)S(1)}, bf16[64,640]{1,0:T(8,128)(2,1)S(1)}, u32[]{:S(2)}, u32[]{:S(2)}) collective-permute-start(bf16[64,640]{1,0:T(8,128)(2,1)S(1)} %get-tuple-element.65), channel_id=1, source_target_pairs={{0,4},{4,0},{8,12},{12,8},{1,5},{5,1},{9,13},{13,9},{2,6},{6,2},{1... | collective-permute-start | bytes 245768 | tf_op jit(solution)/shard_map/ppermute | solution.py:25
  7.7 7.4 %collective-permute-start = (bf16[64,640]{1,0:T(8,128)(2,1)S(1)}, bf16[64,640]{1,0:T(8,128)(2,1)S(1)}, u32[]{:S(2)}, u32[]{:S(2)}) collective-permute-start(bf16[64,640]{1,0:T(8,128)(2,1)S(1)} %get-tuple-element.65), channel_id=1, source_target_pairs={{0,8},{4,12},{8,0},{12,4},{1,9},{5,13},{9,1},{13,5},{2,10},{6,14},... | collective-permute-start | bytes 245768 | tf_op jit(solution)/shard_map/ppermute | solution.py:25
  8.4 8.0 %collective-permute-start.3 = (bf16[64,2048]{1,0:T(8,128)(2,1)S(1)}, bf16[64,2048]{1,0:T(8,128)(2,1)S(1)}, u32[]{:S(2)}, u32[]{:S(2)}) collective-permute-start(bf16[64,2048]{1,0:T(8,128)(2,1)S(1)} %get-tuple-element.67.first_ref), channel_id=1, source_target_pairs={{0,2},{1,3},{2,0},{3,1},{4,6},{5,7},{6,4},{7,5},{8,10},{9,11},{10,... | collective-permute-start | bytes 786440 | tf_op jit(solution)/shard_map/ppermute | solution.py:25
  10.0 13.7 %copy-start.2 = (bf16[512,2048]{1,0:T(8,128)(2,1)S(1)}, bf16[512,2048]{1,0:T(8,128)(2,1)}, u32[]{:S(2)}) copy-start(bf16[512,2048]{1,0:T(8,128)(2,1)} %refs_3_.1) | copy-start | bytes 6291460
  16.4 5.7 %collective-permute-start.6 = (bf16[256,384]{1,0:T(8,128)(2,1)S(1)}, bf16[256,384]{1,0:T(8,128)(2,1)S(1)}, u32[]{:S(2)}, u32[]{:S(2)}) collective-permute-start(bf16[256,384]{1,0:T(8,128)(2,1)S(1)} %pad_maximum_fusion.5), channel_id=1, source_target_pairs={{0,2},{1,3},{2,0},{3,1},{4,6},{5,7},{6,4},{7,5},{8,10},{9,11},{10,... | collective-permute-start | bytes 589832 | tf_op jit(solution)/shard_map/ppermute | solution.py:25
  17.9 4.3 %collective-permute-start.4 = (bf16[64,2048]{1,0:T(8,128)(2,1)S(1)}, bf16[64,2048]{1,0:T(8,128)(2,1)S(1)}, u32[]{:S(2)}, u32[]{:S(2)}) collective-permute-start(bf16[64,2048]{1,0:T(8,128)(2,1)S(1)} %get-tuple-element.67.first_ref), channel_id=1, source_target_pairs={{0,1},{1,0},{2,3},{3,2},{4,5},{5,4},{6,7},{7,6},{8,9},{9,8},{10,11... | collective-permute-start | bytes 786440 | tf_op jit(solution)/shard_map/ppermute | solution.py:25
  17.9 4.3 %collective-permute-start.5 = (bf16[64,2048]{1,0:T(8,128)(2,1)S(1)}, bf16[64,2048]{1,0:T(8,128)(2,1)S(1)}, u32[]{:S(2)}, u32[]{:S(2)}) collective-permute-start(bf16[64,2048]{1,0:T(8,128)(2,1)S(1)} %collective-permute-done.3.second_ref), channel_id=1, source_target_pairs={{0,1},{1,0},{2,3},{3,2},{4,5},{5,4},{6,7},{7,6},{8,9},{9,8},{10,11... | collective-permute-start | bytes 786440 | tf_op jit(solution)/shard_map/ppermute | solution.py:25
  22.1 1.6 %collective-permute-start.7 = (bf16[512,256]{1,0:T(8,128)(2,1)S(1)}, bf16[512,256]{1,0:T(8,128)(2,1)S(1)}, u32[]{:S(2)}, u32[]{:S(2)}) collective-permute-start(bf16[512,256]{1,0:T(8,128)(2,1)S(1)} %pad_maximum_fusion.3.refs_1_), channel_id=1, source_target_pairs={{0,1},{1,0},{2,3},{3,2},{4,5},{5,4},{6,7},{7,6},{8,9},{9,8},{10,11... | collective-permute-start | bytes 786440 | tf_op jit(solution)/shard_map/ppermute | solution.py:25
  22.3 7.0 %copy-start.3 = (bf16[1,768,2048]{2,1,0:T(8,128)(2,1)S(1)}, bf16[1,768,2048]{2,1,0:T(8,128)(2,1)}, u32[]{:S(2)}) copy-start(bf16[1,768,2048]{2,1,0:T(8,128)(2,1)} %param.23) | copy-start | bytes 9437188
  26.5 11.7 %copy-start.7 = (bf16[1,64,2048]{2,1,0:T(8,128)(2,1)S(1)}, bf16[1,64,2048]{2,1,0:T(8,128)(2,1)}, u32[]{:S(2)}) copy-start(bf16[1,64,2048]{2,1,0:T(8,128)(2,1)} %param.12) | copy-start | bytes 786436
  26.5 11.9 %copy-start.8 = (f32[2048]{0:T(1024)S(1)}, f32[2048]{0:T(1024)}, u32[]{:S(2)}) copy-start(f32[2048]{0:T(1024)} %param.19) | copy-start | bytes 24580
  26.5 2.7 %collective-permute-start.8 = (f32[128,2048]{1,0:T(8,128)S(1)}, f32[128,2048]{1,0:T(8,128)S(1)}, u32[]{:S(2)}, u32[]{:S(2)}) collective-permute-start(f32[128,2048]{1,0:T(8,128)S(1)} %get-tuple-element.70), channel_id=1, source_target_pairs={{0,1},{1,0},{2,3},{3,2},{4,5},{5,4},{6,7},{7,6},{8,9},{9,8},{10,11... | collective-permute-start | bytes 3145736 | tf_op jit(solution)/shard_map/ppermute | solution.py:25
  29.2 9.0 %collective-permute-start.11 = (bf16[768,2048]{1,0:T(8,128)(2,1)S(1)}, bf16[768,2048]{1,0:T(8,128)(2,1)S(1)}, u32[]{:S(2)}, u32[]{:S(2)}) collective-permute-start(bf16[768,2048]{1,0:T(8,128)(2,1)S(1)} %bitcast.32), channel_id=1, source_target_pairs={{0,1},{1,0},{2,3},{3,2},{4,5},{5,4},{6,7},{7,6},{8,9},{9,8},{10,11... | collective-permute-start | bytes 9437192 | tf_op jit(solution)/shard_map/ppermute | solution.py:25
  29.5 26.4 %copy-start.5 = (f32[128,2048]{1,0:T(8,128)}, f32[128,2048]{1,0:T(8,128)S(1)}, u32[]{:S(2)}) copy-start(f32[128,2048]{1,0:T(8,128)S(1)} %add.104) | copy-start | bytes 3145732
  29.5 8.6 %collective-permute-start.9 = (bf16[64,2048]{1,0:T(8,128)(2,1)S(1)}, bf16[64,2048]{1,0:T(8,128)(2,1)S(1)}, u32[]{:S(2)}, u32[]{:S(2)}) collective-permute-start(bf16[64,2048]{1,0:T(8,128)(2,1)S(1)} %slice.137), channel_id=1, source_target_pairs={{0,2},{1,3},{2,0},{3,1},{4,6},{5,7},{6,4},{7,5},{8,10},{9,11},{10,... | collective-permute-start | bytes 786440 | tf_op jit(solution)/shard_map/ppermute | solution.py:25
  31.1 5.5 %collective-permute-start.10 = (bf16[2,256,128]{2,1,0:T(8,128)(2,1)S(1)}, bf16[2,256,128]{2,1,0:T(8,128)(2,1)S(1)}, u32[]{:S(2)}, u32[]{:S(2)}) collective-permute-start(bf16[2,256,128]{2,1,0:T(8,128)(2,1)S(1)} %pad_maximum_fusion.6), channel_id=1, source_target_pairs={{0,16},{16,0},{1,17},{17,1},{2,18},{18,2},{3,19},{19,3},{4,20},{20... | collective-permute-start | bytes 393224 | tf_op jit(solution)/shard_map/ppermute | solution.py:25
  38.2 16.1 %copy-start.4 = (bf16[768,2048]{1,0:T(8,128)(2,1)}, bf16[768,2048]{1,0:T(8,128)(2,1)S(1)}, u32[]{:S(2)}) copy-start(bf16[768,2048]{1,0:T(8,128)(2,1)S(1)} %collective-permute-done.11.refs_6_) | copy-start | bytes 9437188
  38.6 14.6 %collective-permute-start.13 = (bf16[64,2048]{1,0:T(8,128)(2,1)S(1)}, bf16[64,2048]{1,0:T(8,128)(2,1)}, u32[]{:S(2)}, u32[]{:S(2)}) collective-permute-start(bf16[64,2048]{1,0:T(8,128)(2,1)S(1)} %multiply_convert_fusion.refs_9_), channel_id=1, source_target_pairs={{0,8},{4,12},{8,0},{12,4},{1,9},{5,13},{9,1},{13,5},{2,10},{6,14},... | collective-permute-start | bytes 786440 | tf_op jit(solution)/shard_map/ppermute | solution.py:25
  40.9 12.4 %collective-permute-start.15 = (bf16[64,2048]{1,0:T(8,128)(2,1)S(1)}, bf16[64,2048]{1,0:T(8,128)(2,1)S(1)}, u32[]{:S(2)}, u32[]{:S(2)}) collective-permute-start(bf16[64,2048]{1,0:T(8,128)(2,1)S(1)} %multiply_convert_fusion.refs_9_), channel_id=1, source_target_pairs={{0,4},{4,0},{8,12},{12,8},{1,5},{5,1},{9,13},{13,9},{2,6},{6,2},{1... | collective-permute-start | bytes 786440 | tf_op jit(solution)/shard_map/ppermute | solution.py:25
  42.6 11.7 %collective-permute-start.17 = (bf16[64,2048]{1,0:T(8,128)(2,1)S(1)}, bf16[64,2048]{1,0:T(8,128)(2,1)S(1)}, u32[]{:S(2)}, u32[]{:S(2)}) collective-permute-start(bf16[64,2048]{1,0:T(8,128)(2,1)S(1)} %multiply_convert_fusion.refs_9_), channel_id=1, source_target_pairs={{0,16},{16,0},{1,17},{17,1},{2,18},{18,2},{3,19},{19,3},{4,20},{20... | collective-permute-start | bytes 786440 | tf_op jit(solution)/shard_map/ppermute | solution.py:25
  44.1 10.2 %collective-permute-start.16 = (bf16[64,2048]{1,0:T(8,128)(2,1)S(1)}, bf16[64,2048]{1,0:T(8,128)(2,1)S(1)}, u32[]{:S(2)}, u32[]{:S(2)}) collective-permute-start(bf16[64,2048]{1,0:T(8,128)(2,1)S(1)} %multiply_convert_fusion.refs_9_), channel_id=1, source_target_pairs={{0,2},{1,3},{2,0},{3,1},{4,6},{5,7},{6,4},{7,5},{8,10},{9,11},{10,... | collective-permute-start | bytes 786440 | tf_op jit(solution)/shard_map/ppermute | solution.py:25
  53.1 7.5 %collective-permute-start.14 = (bf16[64,2048]{1,0:T(8,128)(2,1)}, bf16[64,2048]{1,0:T(8,128)(2,1)S(1)}, u32[]{:S(2)}, u32[]{:S(2)}) collective-permute-start(bf16[64,2048]{1,0:T(8,128)(2,1)} %collective-permute-done.13), channel_id=1, source_target_pairs={{0,4},{4,0},{8,12},{12,8},{1,5},{5,1},{9,13},{13,9},{2,6},{6,2},{1... | collective-permute-start | bytes 786440 | tf_op jit(solution)/shard_map/ppermute | solution.py:25
  54.3 14.9 %collective-permute-start.20 = (bf16[128,2048]{1,0:T(8,128)(2,1)S(1)}, bf16[128,2048]{1,0:T(8,128)(2,1)S(1)}, u32[]{:S(2)}, u32[]{:S(2)}) collective-permute-start(bf16[128,2048]{1,0:T(8,128)(2,1)S(1)} %pad_maximum_fusion.1.refs_10_), channel_id=1, source_target_pairs={{0,16},{16,0},{1,17},{17,1},{2,18},{18,2},{3,19},{19,3},{4,20},{20... | collective-permute-start | bytes 1572872 | tf_op jit(solution)/shard_map/ppermute | solution.py:25
  55.9 14.9 %collective-permute-start.18 = (bf16[128,2048]{1,0:T(8,128)(2,1)S(1)}, bf16[128,2048]{1,0:T(8,128)(2,1)S(1)}, u32[]{:S(2)}, u32[]{:S(2)}) collective-permute-start(bf16[128,2048]{1,0:T(8,128)(2,1)S(1)} %pad_maximum_fusion.1.refs_10_), channel_id=1, source_target_pairs={{0,2},{1,3},{2,0},{3,1},{4,6},{5,7},{6,4},{7,5},{8,10},{9,11},{10,... | collective-permute-start | bytes 1572872 | tf_op jit(solution)/shard_map/ppermute | solution.py:25
  60.6 13.0 %collective-permute-start.21 = (bf16[64,2048]{1,0:T(8,128)(2,1)S(1)}, bf16[64,2048]{1,0:T(8,128)(2,1)S(1)}, u32[]{:S(2)}, u32[]{:S(2)}) collective-permute-start(bf16[64,2048]{1,0:T(8,128)(2,1)S(1)} %collective-permute-done.14.refs_11_), channel_id=1, source_target_pairs={{0,16},{16,0},{1,17},{17,1},{2,18},{18,2},{3,19},{19,3},{4,20},{20... | collective-permute-start | bytes 786440 | tf_op jit(solution)/shard_map/ppermute | solution.py:25
  62.0 12.8 %collective-permute-start.19 = (bf16[64,2048]{1,0:T(8,128)(2,1)S(1)}, bf16[64,2048]{1,0:T(8,128)(2,1)S(1)}, u32[]{:S(2)}, u32[]{:S(2)}) collective-permute-start(bf16[64,2048]{1,0:T(8,128)(2,1)S(1)} %collective-permute-done.14.refs_11_), channel_id=1, source_target_pairs={{0,2},{1,3},{2,0},{3,1},{4,6},{5,7},{6,4},{7,5},{8,10},{9,11},{10,... | collective-permute-start | bytes 786440 | tf_op jit(solution)/shard_map/ppermute | solution.py:25
  74.9 12.4 %collective-permute-start.22 = (bf16[256,1024]{1,0:T(8,128)(2,1)S(1)}, bf16[256,1024]{1,0:T(8,128)(2,1)S(1)}, u32[]{:S(2)}, u32[]{:S(2)}) collective-permute-start(bf16[256,1024]{1,0:T(8,128)(2,1)S(1)} %get-tuple-element.92), channel_id=1, source_target_pairs={{0,16},{16,0},{1,17},{17,1},{2,18},{18,2},{3,19},{19,3},{4,20},{20... | collective-permute-start | bytes 1572872 | tf_op jit(solution)/shard_map/ppermute | solution.py:25
  75.5 12.1 %collective-permute-start.23 = (bf16[256,1024]{1,0:T(8,128)(2,1)S(1)}, bf16[256,1024]{1,0:T(8,128)(2,1)S(1)}, u32[]{:S(2)}, u32[]{:S(2)}) collective-permute-start(bf16[256,1024]{1,0:T(8,128)(2,1)S(1)} %get-tuple-element.93), channel_id=1, source_target_pairs={{0,2},{1,3},{2,0},{3,1},{4,6},{5,7},{6,4},{7,5},{8,10},{9,11},{10,... | collective-permute-start | bytes 1572872 | tf_op jit(solution)/shard_map/ppermute | solution.py:25
  87.6 12.6 %collective-permute-start.24 = (bf16[256,1024]{1,0:T(8,128)(2,1)S(1)}, bf16[256,1024]{1,0:T(8,128)(2,1)S(1)}, u32[]{:S(2)}, u32[]{:S(2)}) collective-permute-start(bf16[256,1024]{1,0:T(8,128)(2,1)S(1)} %get-tuple-element.94), channel_id=1, source_target_pairs={{0,16},{16,0},{1,17},{17,1},{2,18},{18,2},{3,19},{19,3},{4,20},{20... | collective-permute-start | bytes 1572872 | tf_op jit(solution)/shard_map/ppermute | solution.py:25
  89.1 11.2 %collective-permute-start.25 = (bf16[256,1024]{1,0:T(8,128)(2,1)S(1)}, bf16[256,1024]{1,0:T(8,128)(2,1)S(1)}, u32[]{:S(2)}, u32[]{:S(2)}) collective-permute-start(bf16[256,1024]{1,0:T(8,128)(2,1)S(1)} %get-tuple-element.95), channel_id=1, source_target_pairs={{0,2},{1,3},{2,0},{3,1},{4,6},{5,7},{6,4},{7,5},{8,10},{9,11},{10,... | collective-permute-start | bytes 1572872 | tf_op jit(solution)/shard_map/ppermute | solution.py:25
  100.3 9.3 %collective-permute-start.26 = (bf16[128,1024]{1,0:T(8,128)(2,1)S(1)}, bf16[128,1024]{1,0:T(8,128)(2,1)S(1)}, u32[]{:S(2)}, u32[]{:S(2)}) collective-permute-start(bf16[128,1024]{1,0:T(8,128)(2,1)S(1)} %get-tuple-element.107), channel_id=1, source_target_pairs={{0,16},{16,0},{1,17},{17,1},{2,18},{18,2},{3,19},{19,3},{4,20},{20... | collective-permute-start | bytes 786440 | tf_op jit(solution)/shard_map/ppermute | solution.py:25
  100.9 9.7 %collective-permute-start.28 = (bf16[128,1024]{1,0:T(8,128)(2,1)S(1)}, bf16[128,1024]{1,0:T(8,128)(2,1)S(1)}, u32[]{:S(2)}, u32[]{:S(2)}) collective-permute-start(bf16[128,1024]{1,0:T(8,128)(2,1)S(1)} %get-tuple-element.109), channel_id=1, source_target_pairs={{0,2},{1,3},{2,0},{3,1},{4,6},{5,7},{6,4},{7,5},{8,10},{9,11},{10,... | collective-permute-start | bytes 786440 | tf_op jit(solution)/shard_map/ppermute | solution.py:25
  102.5 11.3 %collective-permute-start.30 = (bf16[128,1024]{1,0:T(8,128)(2,1)S(1)}, bf16[128,1024]{1,0:T(8,128)(2,1)S(1)}, u32[]{:S(2)}, u32[]{:S(2)}) collective-permute-start(bf16[128,1024]{1,0:T(8,128)(2,1)S(1)} %get-tuple-element.110), channel_id=1, source_target_pairs={{0,16},{16,0},{1,17},{17,1},{2,18},{18,2},{3,19},{19,3},{4,20},{20... | collective-permute-start | bytes 786440 | tf_op jit(solution)/shard_map/ppermute | solution.py:25
  104.2 9.9 %collective-permute-start.31 = (bf16[128,1024]{1,0:T(8,128)(2,1)S(1)}, bf16[128,1024]{1,0:T(8,128)(2,1)S(1)}, u32[]{:S(2)}, u32[]{:S(2)}) collective-permute-start(bf16[128,1024]{1,0:T(8,128)(2,1)S(1)} %get-tuple-element.111), channel_id=1, source_target_pairs={{0,2},{1,3},{2,0},{3,1},{4,6},{5,7},{6,4},{7,5},{8,10},{9,11},{10,... | collective-permute-start | bytes 786440 | tf_op jit(solution)/shard_map/ppermute | solution.py:25
  109.7 8.3 %collective-permute-start.27 = (bf16[128,1024]{1,0:T(8,128)(2,1)S(1)}, bf16[128,1024]{1,0:T(8,128)(2,1)S(1)}, u32[]{:S(2)}, u32[]{:S(2)}) collective-permute-start(bf16[128,1024]{1,0:T(8,128)(2,1)S(1)} %add_convert_fusion.5), channel_id=1, source_target_pairs={{0,2},{1,3},{2,0},{3,1},{4,6},{5,7},{6,4},{7,5},{8,10},{9,11},{10,... | collective-permute-start | bytes 786440 | tf_op jit(solution)/shard_map/ppermute | solution.py:25
  110.7 7.2 %collective-permute-start.29 = (bf16[128,1024]{1,0:T(8,128)(2,1)S(1)}, bf16[128,1024]{1,0:T(8,128)(2,1)S(1)}, u32[]{:S(2)}, u32[]{:S(2)}) collective-permute-start(bf16[128,1024]{1,0:T(8,128)(2,1)S(1)} %add_convert_fusion.4), channel_id=1, source_target_pairs={{0,16},{16,0},{1,17},{17,1},{2,18},{18,2},{3,19},{19,3},{4,20},{20... | collective-permute-start | bytes 786440 | tf_op jit(solution)/shard_map/ppermute | solution.py:25
  118.4 20.2 %copy-start.6 = (f32[128,2048]{1,0:T(8,128)S(1)}, f32[128,2048]{1,0:T(8,128)}, u32[]{:S(2)}) copy-start(f32[128,2048]{1,0:T(8,128)} %copy-done.5) | copy-start | bytes 3145732
  118.5 6.8 %collective-permute-start.34 = (bf16[64,2048]{1,0:T(8,128)(2,1)S(1)}, bf16[64,2048]{1,0:T(8,128)(2,1)S(1)}, u32[]{:S(2)}, u32[]{:S(2)}) collective-permute-start(bf16[64,2048]{1,0:T(8,128)(2,1)S(1)} %get-tuple-element.124), channel_id=1, source_target_pairs={{0,4},{4,0},{8,12},{12,8},{1,5},{5,1},{9,13},{13,9},{2,6},{6,2},{1... | collective-permute-start | bytes 786440 | tf_op jit(solution)/shard_map/ppermute | solution.py:25
  118.6 6.7 %collective-permute-start.32 = (bf16[128,1024]{1,0:T(8,128)(2,1)S(1)}, bf16[128,1024]{1,0:T(8,128)(2,1)S(1)}, u32[]{:S(2)}, u32[]{:S(2)}) collective-permute-start(bf16[128,1024]{1,0:T(8,128)(2,1)S(1)} %get-tuple-element.118), channel_id=1, source_target_pairs={{0,2},{1,3},{2,0},{3,1},{4,6},{5,7},{6,4},{7,5},{8,10},{9,11},{10,... | collective-permute-start | bytes 786440 | tf_op jit(solution)/shard_map/ppermute | solution.py:25
  120.2 6.4 %collective-permute-start.33 = (bf16[128,1024]{1,0:T(8,128)(2,1)S(1)}, bf16[128,1024]{1,0:T(8,128)(2,1)S(1)}, u32[]{:S(2)}, u32[]{:S(2)}) collective-permute-start(bf16[128,1024]{1,0:T(8,128)(2,1)S(1)} %get-tuple-element.119), channel_id=1, source_target_pairs={{0,16},{16,0},{1,17},{17,1},{2,18},{18,2},{3,19},{19,3},{4,20},{20... | collective-permute-start | bytes 786440 | tf_op jit(solution)/shard_map/ppermute | solution.py:25
  126.7 10.9 %collective-permute-start.36 = (bf16[64,2048]{1,0:T(8,128)(2,1)S(1)}, bf16[64,2048]{1,0:T(8,128)(2,1)S(1)}, u32[]{:S(2)}, u32[]{:S(2)}) collective-permute-start(bf16[64,2048]{1,0:T(8,128)(2,1)S(1)} %fusion.6), channel_id=1, source_target_pairs={{0,8},{4,12},{8,0},{12,4},{1,9},{5,13},{9,1},{13,5},{2,10},{6,14},... | collective-permute-start | bytes 786440 | tf_op jit(solution)/shard_map/ppermute | solution.py:25
  130.4 8.3 %collective-permute-start.35 = (bf16[64,2048]{1,0:T(8,128)(2,1)S(1)}, bf16[64,2048]{1,0:T(8,128)(2,1)S(1)}, u32[]{:S(2)}, u32[]{:S(2)}) collective-permute-start(bf16[64,2048]{1,0:T(8,128)(2,1)S(1)} %get-tuple-element.121), channel_id=1, source_target_pairs={{0,4},{4,0},{8,12},{12,8},{1,5},{5,1},{9,13},{13,9},{2,6},{6,2},{1... | collective-permute-start | bytes 786440 | tf_op jit(solution)/shard_map/ppermute | solution.py:25

commit v12 on v11

--- a/solution.py
+++ b/solution.py
@@ -28,13 +28,6 @@
 def seq_bits():
     size = lax.axis_size("seq")
     return [1 << place for place in reversed(range(size.bit_length() - 1))]
-
-
-def seq_order():
-    order = [0]
-    for bits in seq_bits():
-        order = order + [place ^ bits for place in order]
-    return order
 
 
 def ready(*arrays):
@@ -73,14 +66,12 @@
     def both_ways(part):
         return swap(part, "rep", ACROSS), swap(part, "role", 1)
 
-    first_bits, *bits_left = seq_bits()
-    blocks = [own, swap(own, "seq", first_bits)]
-    for bits in bits_left[:-1]:
-        blocks = blocks + [swap(block, "seq", bits) for block in blocks]
-    beyond = [swap(block, "seq", bits_left[-1]) for block in blocks]
-    middle = jnp.concatenate(blocks[1:] + beyond[:-1], axis=0)
+    blocks = {0: own}
+    for bits in seq_bits():
+        blocks |= {place ^ bits: swap(block, "seq", bits) for place, block in blocks.items()}
+    middle = jnp.concatenate([blocks[place] for place in range(1, len(blocks) - 1)], axis=0)
     middle, coded, *outer = ready(middle, coded, *both_ways(own))
-    last, *tables = ready(beyond[-1], *tables_of(coded))
+    last, *tables = ready(blocks[len(blocks) - 1], *tables_of(coded))
     by_rep, by_role = zip(outer, both_ways(middle), both_ways(last))
     low, high = pack_corners(by_rep, by_role)
     corner_low, corner_high = swap(low, "role", 1), swap(high, "rep", ACROSS)
@@ -97,7 +88,7 @@
     return (first.astype(jnp.float32) + second.astype(jnp.float32)).astype(jnp.bfloat16)
 
 
-def collect_rows(near, by_rep, by_role, corner):
+def collect_rows(row_count, near, by_rep, by_role, corner):
     straight_low = swap(by_role[0], "role", 1)
     straight_high = swap(by_rep[1], "rep", ACROSS)
     straight_low, straight_high, near_low, near_high, *corner = ready(
@@ -133,17 +124,21 @@
 
     far_corner, beside_corner = corners(1), corners(0)
     *far, corner_low, corner_high = ready(*turned(*sums(1, *far_corner)), *beside_corner)
-    leaving = merged(halves[1], *far).astype(jnp.bfloat16)
-    *near_sums, leaving = ready(*sums(0, corner_low, corner_high), leaving)
-    beside = turned(*near_sums)
-    total = merged(halves[0], *beside)
-    *later_bits, last_bits = reversed(seq_bits())
-    for bits in later_bits:
-        cut = total.shape[0] // 2
-        far, near = ready(swap(leaving[cut:], "seq", bits), leaving[:cut])
-        leaving = (total[cut:] + far.astype(jnp.float32)).astype(jnp.bfloat16)
-        total = total[:cut] + swap(near, "seq", bits).astype(jnp.float32)
-    return total + swap(leaving, "seq", last_bits).astype(jnp.float32)
+    upper = merged(halves[1], *far)
+    *near_sums, upper = ready(*sums(0, corner_low, corner_high), upper)
+    lower = merged(halves[0], *turned(*near_sums))
+    top_bits, *low_bits = seq_bits()
+
+    def folded(rows):
+        for bits in reversed(low_bits):
+            pairs = rows.reshape(-1, 2, row_count, rows.shape[1])
+            leaving = pairs[:, 1].astype(jnp.bfloat16).reshape(-1, rows.shape[1])
+            kept = pairs[:, 0].reshape(-1, rows.shape[1]).astype(jnp.float32)
+            rows = kept + swap(leaving, "seq", bits).astype(jnp.float32)
+        return rows
+
+    upper = folded(upper).astype(jnp.bfloat16)
+    return folded(lower) + swap(upper, "seq", top_bits).astype(jnp.float32)
 
 
 def prepare_kernel(*refs):
@@ -520,7 +515,7 @@
     )
     across_rows = swap(normed, "rep", ACROSS)
     line = jnp.concatenate(
-        [own_payload] + [swap(own_payload, "seq", bits) for bits in seq_order()[1:]], axis=0
+        [own_payload] + [swap(own_payload, "seq", bits) for bits in range(1, lax.axis_size("seq"))], axis=0
     )
     pair_rows = swap(ready(normed, line)[0], "rep", PAIR)
     corner_rows = swap(across_rows, "rep", PAIR)
@@ -577,7 +572,7 @@
     by_rep, by_role = (rep_low, rep_high), (role_low, role_high)
     pieces = [(row, column, array) for (row, column, _), array in zip(rows[2], held)]
     *corner, near = run_experts(2, [pieces, rows[3]], (2, 1), *tables)
-    routed = collect_rows(near, by_rep, by_role, corner)
+    routed = collect_rows(row_count, near, by_rep, by_role, corner)
     return (mixed + routed).astype(jnp.bfloat16)[None]
 
 

time: 140 us -> 141 us (level)
  no operation moved by 1% of the time
where the time goes in v12:
time: 141 us
  waiting for transfers between devices  64.5 us (46%)
  starting transfers between devices  45.2 us (32%)
  Pallas kernels  27 us (19%)
  other arithmetic  3.47 us (2%)
    ppermute x37, waiting for transfers between devices, swap(): return lax.ppermute(block, axis, [(i, i ^ bits) for i in range(size)])  64.5 us
    ppermute x37, starting transfers between devices, swap(): return lax.ppermute(block, axis, [(i, i ^ bits) for i in range(size)])  45.2 us
    pallas_call x2, Pallas kernels, run_experts(): pl.pallas_call(lambda *refs: expert_kernel(first, spots, cuts, *refs), ou...  19.2 us
  transfers between devices with their start and end apart: 37, of which 23 were waited for; matrix products, arithmetic and copies ran while one was open for 1% of the time, Pallas kernels for 19%

profile of v12, /device:TPU:0, one launch (start us, length us, event | category | flops | bytes accessed | tf_op | source)
XLA Modules:
  0.0 140.8 jit_solution(9374433963729335837)
XLA Ops:
  0.0 0.5 collective-permute-start.12
  0.5 2.6 %prepare.1 = (bf16[64,2048]{1,0:T(8,128)(2,1)S(1)}, bf16[64,640]{1,0:T(8,128)(2,1)S(1)}) custom-call(bf16[64,2048]{1,0:T(8,128)(2,1)} %bitcast.57, f32[1,2048]{1,0:T(1,128)} %bitcast.62, bf16[2,2048,256]{2,1,0:T(8,128)(2,1)} %refs_2_.1, f32[1,128]{1,0:T(1,128)} %bitcast.65, s32[8,64]{1,0:T(8,128)} %bitcast.63, s32[8,64]{1,0:T(8,128)} %bitcast.64), custom_call_target="tpu_custom_call" | custom-call | flops 134217728 | bytes 2621440 | tf_op jit(solution)/shard_map/prepare/pallas_call | solution.py:184
  3.1 4.7 %collective-permute-start.2 = (bf16[64,640]{1,0:T(8,128)(2,1)S(1)}, bf16[64,640]{1,0:T(8,128)(2,1)S(1)}, u32[]{:S(2)}, u32[]{:S(2)}) collective-permute-start(bf16[64,640]{1,0:T(8,128)(2,1)S(1)} %get-tuple-element.63), channel_id=1, source_target_pairs={{0,12},{4,8},{8,4},{12,0},{1,13},{5,9},{9,5},{13,1},{2,14},{6,10},... | collective-permute-start | bytes 245768 | tf_op jit(solution)/shard_map/ppermute | solution.py:25
  7.7 0.6 collective-permute-start
  8.4 1.7 %collective-permute-start.3 = (bf16[64,2048]{1,0:T(8,128)(2,1)S(1)}, bf16[64,2048]{1,0:T(8,128)(2,1)S(1)}, u32[]{:S(2)}, u32[]{:S(2)}) collective-permute-start(bf16[64,2048]{1,0:T(8,128)(2,1)S(1)} %get-tuple-element.65.first_ref), channel_id=1, source_target_pairs={{0,2},{1,3},{2,0},{3,1},{4,6},{5,7},{6,4},{7,5},{8,10},{9,11},{10,... | collective-permute-start | bytes 786440 | tf_op jit(solution)/shard_map/ppermute | solution.py:25
  10.0 3.5 %collective-permute-done = bf16[64,640]{1,0:T(8,128)(2,1)S(1)} collective-permute-done((bf16[64,640]{1,0:T(8,128)(2,1)S(1)}, bf16[64,640]{1,0:T(8,128)(2,1)S(1)}, u32[]{:S(2)}, u32[]{:S(2)}) %collective-permute-start) | collective-permute-done | bytes 81952 | tf_op jit(solution)/shard_map/ppermute | solution.py:25
  13.5 1.6 %collective-permute-done.1 = bf16[64,640]{1,0:T(8,128)(2,1)S(1)} collective-permute-done((bf16[64,640]{1,0:T(8,128)(2,1)S(1)}, bf16[64,640]{1,0:T(8,128)(2,1)S(1)}, u32[]{:S(2)}, u32[]{:S(2)}) %collective-permute-start.1) | collective-permute-done | bytes 81952 | tf_op jit(solution)/shard_map/ppermute | solution.py:25
  15.3 1.1 collective-permute-done.3.second_ref
  16.4 1.5 %collective-permute-start.6 = (bf16[256,384]{1,0:T(8,128)(2,1)S(1)}, bf16[256,384]{1,0:T(8,128)(2,1)S(1)}, u32[]{:S(2)}, u32[]{:S(2)}) collective-permute-start(bf16[256,384]{1,0:T(8,128)(2,1)S(1)} %pad_maximum_fusion.5), channel_id=1, source_target_pairs={{0,2},{1,3},{2,0},{3,1},{4,6},{5,7},{6,4},{7,5},{8,10},{9,11},{10,... | collective-permute-start | bytes 589832 | tf_op jit(solution)/shard_map/ppermute | solution.py:25
  17.9 0.5 collective-permute-start.5
  18.4 3.7 %collective-permute-done.6 = bf16[256,384]{1,0:T(8,128)(2,1)S(1)} collective-permute-done((bf16[256,384]{1,0:T(8,128)(2,1)S(1)}, bf16[256,384]{1,0:T(8,128)(2,1)S(1)}, u32[]{:S(2)}, u32[]{:S(2)}) %collective-permute-start.6) | collective-permute-done | bytes 196640 | tf_op jit(solution)/shard_map/ppermute | solution.py:25
  22.3 0.9 queries.1.refs_0_
  23.1 0.6 collective-permute-done.7.refs_2_
  23.7 2.7 %attend.1 = (f32[128,2048]{1,0:T(8,128)S(1)}, f32[128,2048]{1,0:T(8,128)S(1)}) custom-call(bf16[256,512]{1,0:T(8,128)(2,1)S(1)} %queries.1.refs_0_, bf16[512,256]{1,0:T(8,128)(2,1)S(1)} %pad_maximum_fusion.3.refs_1_, bf16[512,256]{1,0:T(8,128)(2,1)S(1)} %collective-permute-done.7.refs_2_, bf16[512,2048]{1,0:T(8,128)(2,1)S(1)} %copy-done.2), custom_call_target="tpu_custom_call" | custom-call | flops 1073741824 | bytes 4194304 | tf_op jit(solution)/shard_map/attend/pallas_call | solution.py:263
  26.5 0.2 collective-permute-start.8
  26.7 2.5 %collective-permute-done.8 = f32[128,2048]{1,0:T(8,128)S(1)} collective-permute-done((f32[128,2048]{1,0:T(8,128)S(1)}, f32[128,2048]{1,0:T(8,128)S(1)}, u32[]{:S(2)}, u32[]{:S(2)}) %collective-permute-start.8) | collective-permute-done | bytes 1048608 | tf_op jit(solution)/shard_map/ppermute | solution.py:25
  29.5 1.5 %collective-permute-start.9 = (bf16[64,2048]{1,0:T(8,128)(2,1)S(1)}, bf16[64,2048]{1,0:T(8,128)(2,1)S(1)}, u32[]{:S(2)}, u32[]{:S(2)}) collective-permute-start(bf16[64,2048]{1,0:T(8,128)(2,1)S(1)} %slice.145), channel_id=1, source_target_pairs={{0,2},{1,3},{2,0},{3,1},{4,6},{5,7},{6,4},{7,5},{8,10},{9,11},{10,... | collective-permute-start | bytes 786440 | tf_op jit(solution)/shard_map/ppermute | solution.py:25
  31.1 1.6 %collective-permute-start.10 = (bf16[2,256,128]{2,1,0:T(8,128)(2,1)S(1)}, bf16[2,256,128]{2,1,0:T(8,128)(2,1)S(1)}, u32[]{:S(2)}, u32[]{:S(2)}) collective-permute-start(bf16[2,256,128]{2,1,0:T(8,128)(2,1)S(1)} %pad_maximum_fusion.6), channel_id=1, source_target_pairs={{0,16},{16,0},{1,17},{17,1},{2,18},{18,2},{3,19},{19,3},{4,20},{20... | collective-permute-start | bytes 393224 | tf_op jit(solution)/shard_map/ppermute | solution.py:25
  32.7 4.0 %collective-permute-done.10 = bf16[2,256,128]{2,1,0:T(8,128)(2,1)S(1)} collective-permute-done((bf16[2,256,128]{2,1,0:T(8,128)(2,1)S(1)}, bf16[2,256,128]{2,1,0:T(8,128)(2,1)S(1)}, u32[]{:S(2)}, u32[]{:S(2)}) %collective-permute-start.10) | collective-permute-done | bytes 131104 | tf_op jit(solution)/shard_map/ppermute | solution.py:25
  36.7 1.5 %collective-permute-done.9 = bf16[64,2048]{1,0:T(8,128)(2,1)S(1)} collective-permute-done((bf16[64,2048]{1,0:T(8,128)(2,1)S(1)}, bf16[64,2048]{1,0:T(8,128)(2,1)S(1)}, u32[]{:S(2)}, u32[]{:S(2)}) %collective-permute-start.9) | collective-permute-done | bytes 262176 | tf_op jit(solution)/shard_map/ppermute | solution.py:25
  38.2 0.2 multiply_reduce_fusion
  38.6 2.4 %collective-permute-start.13 = (bf16[64,2048]{1,0:T(8,128)(2,1)S(1)}, bf16[64,2048]{1,0:T(8,128)(2,1)}, u32[]{:S(2)}, u32[]{:S(2)}) collective-permute-start(bf16[64,2048]{1,0:T(8,128)(2,1)S(1)} %multiply_convert_fusion.refs_9_), channel_id=1, source_target_pairs={{0,8},{4,12},{8,0},{12,4},{1,9},{5,13},{9,1},{13,5},{2,10},{6,14},... | collective-permute-start | bytes 786440 | tf_op jit(solution)/shard_map/ppermute | solution.py:25
  40.9 1.7 %collective-permute-start.15 = (bf16[64,2048]{1,0:T(8,128)(2,1)S(1)}, bf16[64,2048]{1,0:T(8,128)(2,1)S(1)}, u32[]{:S(2)}, u32[]{:S(2)}) collective-permute-start(bf16[64,2048]{1,0:T(8,128)(2,1)S(1)} %multiply_convert_fusion.refs_9_), channel_id=1, source_target_pairs={{0,4},{4,0},{8,12},{12,8},{1,5},{5,1},{9,13},{13,9},{2,6},{6,2},{1... | collective-permute-start | bytes 786440 | tf_op jit(solution)/shard_map/ppermute | solution.py:25
  42.6 1.5 %collective-permute-start.17 = (bf16[64,2048]{1,0:T(8,128)(2,1)S(1)}, bf16[64,2048]{1,0:T(8,128)(2,1)S(1)}, u32[]{:S(2)}, u32[]{:S(2)}) collective-permute-start(bf16[64,2048]{1,0:T(8,128)(2,1)S(1)} %multiply_convert_fusion.refs_9_), channel_id=1, source_target_pairs={{0,16},{16,0},{1,17},{17,1},{2,18},{18,2},{3,19},{19,3},{4,20},{20... | collective-permute-start | bytes 786440 | tf_op jit(solution)/shard_map/ppermute | solution.py:25
  44.1 1.5 %collective-permute-start.16 = (bf16[64,2048]{1,0:T(8,128)(2,1)S(1)}, bf16[64,2048]{1,0:T(8,128)(2,1)S(1)}, u32[]{:S(2)}, u32[]{:S(2)}) collective-permute-start(bf16[64,2048]{1,0:T(8,128)(2,1)S(1)} %multiply_convert_fusion.refs_9_), channel_id=1, source_target_pairs={{0,2},{1,3},{2,0},{3,1},{4,6},{5,7},{6,4},{7,5},{8,10},{9,11},{10,... | collective-permute-start | bytes 786440 | tf_op jit(solution)/shard_map/ppermute | solution.py:25
  45.6 7.5 %collective-permute-done.13 = bf16[64,2048]{1,0:T(8,128)(2,1)} collective-permute-done((bf16[64,2048]{1,0:T(8,128)(2,1)S(1)}, bf16[64,2048]{1,0:T(8,128)(2,1)}, u32[]{:S(2)}, u32[]{:S(2)}) %collective-permute-start.13) | collective-permute-done | bytes 262176 | tf_op jit(solution)/shard_map/ppermute | solution.py:25
  53.3 1.0 pad_maximum_fusion.2.refs_10_
  54.3 1.6 %collective-permute-start.20 = (bf16[128,2048]{1,0:T(8,128)(2,1)S(1)}, bf16[128,2048]{1,0:T(8,128)(2,1)S(1)}, u32[]{:S(2)}, u32[]{:S(2)}) collective-permute-start(bf16[128,2048]{1,0:T(8,128)(2,1)S(1)} %pad_maximum_fusion.2.refs_10_), channel_id=1, source_target_pairs={{0,16},{16,0},{1,17},{17,1},{2,18},{18,2},{3,19},{19,3},{4,20},{20... | collective-permute-start | bytes 1572872 | tf_op jit(solution)/shard_map/ppermute | solution.py:25
  55.9 1.5 %collective-permute-start.18 = (bf16[128,2048]{1,0:T(8,128)(2,1)S(1)}, bf16[128,2048]{1,0:T(8,128)(2,1)S(1)}, u32[]{:S(2)}, u32[]{:S(2)}) collective-permute-start(bf16[128,2048]{1,0:T(8,128)(2,1)S(1)} %pad_maximum_fusion.2.refs_10_), channel_id=1, source_target_pairs={{0,2},{1,3},{2,0},{3,1},{4,6},{5,7},{6,4},{7,5},{8,10},{9,11},{10,... | collective-permute-start | bytes 1572872 | tf_op jit(solution)/shard_map/ppermute | solution.py:25
  57.4 1.6 %tables.1 = (bf16[4,224,256]{2,1,0:T(8,128)(2,1)S(1)}, bf16[2,4,256,112]{3,2,1,0:T(8,128)(2,1)S(1)}, f32[4,256,2]{2,1,0:T(8,128)S(1)}) custom-call(s32[1]{0:T(128)} %bitcast.12.refs_0_, bf16[4,256,128]{2,1,0:T(8,128)(2,1)S(1)} %pad_maximum_fusion.4.refs_1_), custom_call_target="tpu_custom_call" | custom-call | flops 134217728 | bytes 917504 | tf_op jit(solution)/shard_map/tables/pallas_call | solution.py:326
  59.0 1.6 %collective-permute-done.14.refs_11_ = bf16[64,2048]{1,0:T(8,128)(2,1)S(1)} collective-permute-done((bf16[64,2048]{1,0:T(8,128)(2,1)}, bf16[64,2048]{1,0:T(8,128)(2,1)S(1)}, u32[]{:S(2)}, u32[]{:S(2)}) %collective-permute-start.14) | collective-permute-done | bytes 262176 | tf_op jit(solution)/shard_map/ppermute | solution.py:25
  60.6 1.4 collective-permute-start.21
  62.0 1.5 %collective-permute-start.19 = (bf16[64,2048]{1,0:T(8,128)(2,1)S(1)}, bf16[64,2048]{1,0:T(8,128)(2,1)S(1)}, u32[]{:S(2)}, u32[]{:S(2)}) collective-permute-start(bf16[64,2048]{1,0:T(8,128)(2,1)S(1)} %collective-permute-done.14.refs_11_), channel_id=1, source_target_pairs={{0,2},{1,3},{2,0},{3,1},{4,6},{5,7},{6,4},{7,5},{8,10},{9,11},{10,... | collective-permute-start | bytes 786440 | tf_op jit(solution)/shard_map/ppermute | solution.py:25
  63.5 5.7 %collective-permute-done.20.refs_11_.refs_4_ = bf16[128,2048]{1,0:T(8,128)(2,1)S(1)} collective-permute-done((bf16[128,2048]{1,0:T(8,128)(2,1)S(1)}, bf16[128,2048]{1,0:T(8,128)(2,1)S(1)}, u32[]{:S(2)}, u32[]{:S(2)}) %collective-permute-start.20) | collective-permute-done | bytes 524320 | tf_op jit(solution)/shard_map/ppermute | solution.py:25
  69.2 1.5 %collective-permute-done.18.refs_8_.refs_1_ = bf16[128,2048]{1,0:T(8,128)(2,1)S(1)} collective-permute-done((bf16[128,2048]{1,0:T(8,128)(2,1)S(1)}, bf16[128,2048]{1,0:T(8,128)(2,1)S(1)}, u32[]{:S(2)}, u32[]{:S(2)}) %collective-permute-start.18) | collective-permute-done | bytes 524320 | tf_op jit(solution)/shard_map/ppermute | solution.py:25
  70.8 2.8 %collective-permute-done.21.refs_12_.refs_5_ = bf16[64,2048]{1,0:T(8,128)(2,1)S(1)} collective-permute-done((bf16[64,2048]{1,0:T(8,128)(2,1)S(1)}, bf16[64,2048]{1,0:T(8,128)(2,1)S(1)}, u32[]{:S(2)}, u32[]{:S(2)}) %collective-permute-start.21) | collective-permute-done | bytes 262176 | tf_op jit(solution)/shard_map/ppermute | solution.py:25
  73.6 1.2 collective-permute-done.19.refs_9_.refs_2_
  74.9 0.6 collective-permute-start.22
  75.5 1.5 %collective-permute-start.23 = (bf16[256,1024]{1,0:T(8,128)(2,1)S(1)}, bf16[256,1024]{1,0:T(8,128)(2,1)S(1)}, u32[]{:S(2)}, u32[]{:S(2)}) collective-permute-start(bf16[256,1024]{1,0:T(8,128)(2,1)S(1)} %get-tuple-element.91), channel_id=1, source_target_pairs={{0,2},{1,3},{2,0},{3,1},{4,6},{5,7},{6,4},{7,5},{8,10},{9,11},{10,... | collective-permute-start | bytes 1572872 | tf_op jit(solution)/shard_map/ppermute | solution.py:25
  77.0 9.5 %experts.2 = (bf16[256,1024]{1,0:T(8,128)(2,1)S(1)}, bf16[256,1024]{1,0:T(8,128)(2,1)S(1)}, bf16[256,1024]{1,0:T(8,128)(2,1)S(1)}, bf16[256,1024]{1,0:T(8,128)(2,1)S(1)}) custom-call(bf16[4,224,256]{2,1,0:T(8,128)(2,1)S(1)} %get-tuple-element.77.refs_0_, bf16[2,4,256,112]{3,2,1,0:T(8,128)(2,1)S(1)} %get-tuple-element.78.refs_1_, ...), custom_call_target="tpu_custom_call" | custom-call | flops 4227858432 | bytes 23068672 | tf_op jit(solution)/shard_map/experts/pallas_call | solution.py:456
  86.5 0.8 collective-permute-done.22.refs_7_
  87.3 0.3 collective-permute-done.23.refs_8_
  87.6 1.4 %collective-permute-start.24 = (bf16[256,1024]{1,0:T(8,128)(2,1)S(1)}, bf16[256,1024]{1,0:T(8,128)(2,1)S(1)}, u32[]{:S(2)}, u32[]{:S(2)}) collective-permute-start(bf16[256,1024]{1,0:T(8,128)(2,1)S(1)} %get-tuple-element.92), channel_id=1, source_target_pairs={{0,16},{16,0},{1,17},{17,1},{2,18},{18,2},{3,19},{19,3},{4,20},{20... | collective-permute-start | bytes 1572872 | tf_op jit(solution)/shard_map/ppermute | solution.py:25
  89.0 1.5 %collective-permute-start.25 = (bf16[256,1024]{1,0:T(8,128)(2,1)S(1)}, bf16[256,1024]{1,0:T(8,128)(2,1)S(1)}, u32[]{:S(2)}, u32[]{:S(2)}) collective-permute-start(bf16[256,1024]{1,0:T(8,128)(2,1)S(1)} %get-tuple-element.93), channel_id=1, source_target_pairs={{0,2},{1,3},{2,0},{3,1},{4,6},{5,7},{6,4},{7,5},{8,10},{9,11},{10,... | collective-permute-start | bytes 1572872 | tf_op jit(solution)/shard_map/ppermute | solution.py:25
  90.5 9.7 %experts.3 = (bf16[128,1024]{1,0:T(8,128)(2,1)S(1)}, bf16[128,1024]{1,0:T(8,128)(2,1)S(1)}, bf16[128,1024]{1,0:T(8,128)(2,1)S(1)}, bf16[128,1024]{1,0:T(8,128)(2...) custom-call(bf16[4,224,256]{2,1,0:T(8,128)(2,1)S(1)} %get-tuple-element.77.refs_0_, ...), custom_call_target="tpu_custom_call" | custom-call | flops 4227858432 | bytes 23068672 | tf_op jit(solution)/shard_map/experts/pallas_call | solution.py:456
  100.3 0.7 collective-permute-start.26
  100.9 1.5 %collective-permute-start.28 = (bf16[128,1024]{1,0:T(8,128)(2,1)S(1)}, bf16[128,1024]{1,0:T(8,128)(2,1)S(1)}, u32[]{:S(2)}, u32[]{:S(2)}) collective-permute-start(bf16[128,1024]{1,0:T(8,128)(2,1)S(1)} %get-tuple-element.107), channel_id=1, source_target_pairs={{0,2},{1,3},{2,0},{3,1},{4,6},{5,7},{6,4},{7,5},{8,10},{9,11},{10,... | collective-permute-start | bytes 786440 | tf_op jit(solution)/shard_map/ppermute | solution.py:25
  102.5 1.7 %collective-permute-start.30 = (bf16[128,1024]{1,0:T(8,128)(2,1)S(1)}, bf16[128,1024]{1,0:T(8,128)(2,1)S(1)}, u32[]{:S(2)}, u32[]{:S(2)}) collective-permute-start(bf16[128,1024]{1,0:T(8,128)(2,1)S(1)} %get-tuple-element.108), channel_id=1, source_target_pairs={{0,16},{16,0},{1,17},{17,1},{2,18},{18,2},{3,19},{19,3},{4,20},{20... | collective-permute-start | bytes 786440 | tf_op jit(solution)/shard_map/ppermute | solution.py:25
  104.4 5.2 %collective-permute-done.26 = bf16[128,1024]{1,0:T(8,128)(2,1)S(1)} collective-permute-done((bf16[128,1024]{1,0:T(8,128)(2,1)S(1)}, bf16[128,1024]{1,0:T(8,128)(2,1)S(1)}, u32[]{:S(2)}, u32[]{:S(2)}) %collective-permute-start.26) | collective-permute-done | bytes 262176 | tf_op jit(solution)/shard_map/ppermute | solution.py:25
  109.7 1.0 collective-permute-start.27
  110.7 1.3 collective-permute-start.29
  112.0 1.8 %collective-permute-done.30 = bf16[128,1024]{1,0:T(8,128)(2,1)S(1)} collective-permute-done((bf16[128,1024]{1,0:T(8,128)(2,1)S(1)}, bf16[128,1024]{1,0:T(8,128)(2,1)S(1)}, u32[]{:S(2)}, u32[]{:S(2)}) %collective-permute-start.30) | collective-permute-done | bytes 262176 | tf_op jit(solution)/shard_map/ppermute | solution.py:25
  113.7 0.4 collective-permute-done.31
  114.1 3.8 %collective-permute-done.27 = bf16[128,1024]{1,0:T(8,128)(2,1)S(1)} collective-permute-done((bf16[128,1024]{1,0:T(8,128)(2,1)S(1)}, bf16[128,1024]{1,0:T(8,128)(2,1)S(1)}, u32[]{:S(2)}, u32[]{:S(2)}) %collective-permute-start.27) | collective-permute-done | bytes 262176 | tf_op jit(solution)/shard_map/ppermute | solution.py:25
  117.9 0.2 add_convert_fusion
  118.1 0.3 convert_add_fusion.2
  118.6 1.6 %collective-permute-start.32 = (bf16[128,1024]{1,0:T(8,128)(2,1)S(1)}, bf16[128,1024]{1,0:T(8,128)(2,1)S(1)}, u32[]{:S(2)}, u32[]{:S(2)}) collective-permute-start(bf16[128,1024]{1,0:T(8,128)(2,1)S(1)} %get-tuple-element.116), channel_id=1, source_target_pairs={{0,2},{1,3},{2,0},{3,1},{4,6},{5,7},{6,4},{7,5},{8,10},{9,11},{10,... | collective-permute-start | bytes 786440 | tf_op jit(solution)/shard_map/ppermute | solution.py:25
  120.2 1.1 collective-permute-start.33
  121.3 7.5 %collective-permute-done.35 = bf16[64,2048]{1,0:T(8,128)(2,1)S(1)} collective-permute-done((bf16[64,2048]{1,0:T(8,128)(2,1)S(1)}, bf16[64,2048]{1,0:T(8,128)(2,1)S(1)}, u32[]{:S(2)}, u32[]{:S(2)}) %collective-permute-start.35) | collective-permute-done | bytes 262176 | tf_op jit(solution)/shard_map/ppermute | solution.py:25
  128.9 2.2 %collective-permute-start.36 = (bf16[64,2048]{1,0:T(8,128)(2,1)S(1)}, bf16[64,2048]{1,0:T(8,128)(2,1)S(1)}, u32[]{:S(2)}, u32[]{:S(2)}) collective-permute-start(bf16[64,2048]{1,0:T(8,128)(2,1)S(1)} %fusion.1), channel_id=1, source_target_pairs={{0,8},{4,12},{8,0},{12,4},{1,9},{5,13},{9,1},{13,5},{2,10},{6,14},... | collective-permute-start | bytes 786440 | tf_op jit(solution)/shard_map/ppermute | solution.py:25
  131.5 2.5 %collective-permute-start.34 = (bf16[64,2048]{1,0:T(8,128)(2,1)S(1)}, bf16[64,2048]{1,0:T(8,128)(2,1)S(1)}, u32[]{:S(2)}, u32[]{:S(2)}) collective-permute-start(bf16[64,2048]{1,0:T(8,128)(2,1)S(1)} %fusion.8), channel_id=1, source_target_pairs={{0,4},{4,0},{8,12},{12,8},{1,5},{5,1},{9,13},{13,9},{2,6},{6,2},{1... | collective-permute-start | bytes 786440 | tf_op jit(solution)/shard_map/ppermute | solution.py:25
  134.0 5.1 %collective-permute-done.36 = bf16[64,2048]{1,0:T(8,128)(2,1)S(1)} collective-permute-done((bf16[64,2048]{1,0:T(8,128)(2,1)S(1)}, bf16[64,2048]{1,0:T(8,128)(2,1)S(1)}, u32[]{:S(2)}, u32[]{:S(2)}) %collective-permute-start.36) | collective-permute-done | bytes 262176 | tf_op jit(solution)/shard_map/ppermute | solution.py:25
  139.1 0.8 collective-permute-done.34
  139.9 0.9 fusion.7
  (64 shorter events, 1.9 us)
Async XLA Ops:
  0.0 22.2 %copy-start.1 = (f32[128]{0:T(128)S(1)}, f32[128]{0:T(128)}, u32[]{:S(2)}) copy-start(f32[128]{0:T(128)} %param.16) | copy-start | bytes 1540
  0.0 22.2 %copy-start = (bf16[2048,512]{1,0:T(8,128)(2,1)S(1)}, bf16[2048,512]{1,0:T(8,128)(2,1)}, u32[]{:S(2)}) copy-start(bf16[2048,512]{1,0:T(8,128)(2,1)} %weight_ref.1) | copy-start | bytes 6291460
  0.0 38.2 %collective-permute-start.12 = (bf16[2048,1536]{1,0:T(8,128)(2,1)}, bf16[2048,1536]{1,0:T(8,128)(2,1)}, u32[]{:S(2)}, u32[]{:S(2)}) collective-permute-start(bf16[2048,1536]{1,0:T(8,128)(2,1)} %bitcast.51), channel_id=1, source_target_pairs={{0,1},{1,0},{2,3},{3,2},{4,5},{5,4},{6,7},{7,6},{8,9},{9,8},{10,11... | collective-permute-start | bytes 18874376 | tf_op jit(solution)/shard_map/ppermute | solution.py:25
  3.1 12.0 %collective-permute-start.2 = (bf16[64,640]{1,0:T(8,128)(2,1)S(1)}, bf16[64,640]{1,0:T(8,128)(2,1)S(1)}, u32[]{:S(2)}, u32[]{:S(2)}) collective-permute-start(bf16[64,640]{1,0:T(8,128)(2,1)S(1)} %get-tuple-element.63), channel_id=1, source_target_pairs={{0,12},{4,8},{8,4},{12,0},{1,13},{5,9},{9,5},{13,1},{2,14},{6,10},... | collective-permute-start | bytes 245768 | tf_op jit(solution)/shard_map/ppermute | solution.py:25
  7.7 7.4 %collective-permute-start.1 = (bf16[64,640]{1,0:T(8,128)(2,1)S(1)}, bf16[64,640]{1,0:T(8,128)(2,1)S(1)}, u32[]{:S(2)}, u32[]{:S(2)}) collective-permute-start(bf16[64,640]{1,0:T(8,128)(2,1)S(1)} %get-tuple-element.63), channel_id=1, source_target_pairs={{0,8},{4,12},{8,0},{12,4},{1,9},{5,13},{9,1},{13,5},{2,10},{6,14},... | collective-permute-start | bytes 245768 | tf_op jit(solution)/shard_map/ppermute | solution.py:25
  7.7 5.8 %collective-permute-start = (bf16[64,640]{1,0:T(8,128)(2,1)S(1)}, bf16[64,640]{1,0:T(8,128)(2,1)S(1)}, u32[]{:S(2)}, u32[]{:S(2)}) collective-permute-start(bf16[64,640]{1,0:T(8,128)(2,1)S(1)} %get-tuple-element.63), channel_id=1, source_target_pairs={{0,4},{4,0},{8,12},{12,8},{1,5},{5,1},{9,13},{13,9},{2,6},{6,2},{1... | collective-permute-start | bytes 245768 | tf_op jit(solution)/shard_map/ppermute | solution.py:25
  8.4 8.0 %collective-permute-start.3 = (bf16[64,2048]{1,0:T(8,128)(2,1)S(1)}, bf16[64,2048]{1,0:T(8,128)(2,1)S(1)}, u32[]{:S(2)}, u32[]{:S(2)}) collective-permute-start(bf16[64,2048]{1,0:T(8,128)(2,1)S(1)} %get-tuple-element.65.first_ref), channel_id=1, source_target_pairs={{0,2},{1,3},{2,0},{3,1},{4,6},{5,7},{6,4},{7,5},{8,10},{9,11},{10,... | collective-permute-start | bytes 786440 | tf_op jit(solution)/shard_map/ppermute | solution.py:25
  10.0 13.7 %copy-start.2 = (bf16[512,2048]{1,0:T(8,128)(2,1)S(1)}, bf16[512,2048]{1,0:T(8,128)(2,1)}, u32[]{:S(2)}) copy-start(bf16[512,2048]{1,0:T(8,128)(2,1)} %refs_3_.1) | copy-start | bytes 6291460
  16.4 5.7 %collective-permute-start.6 = (bf16[256,384]{1,0:T(8,128)(2,1)S(1)}, bf16[256,384]{1,0:T(8,128)(2,1)S(1)}, u32[]{:S(2)}, u32[]{:S(2)}) collective-permute-start(bf16[256,384]{1,0:T(8,128)(2,1)S(1)} %pad_maximum_fusion.5), channel_id=1, source_target_pairs={{0,2},{1,3},{2,0},{3,1},{4,6},{5,7},{6,4},{7,5},{8,10},{9,11},{10,... | collective-permute-start | bytes 589832 | tf_op jit(solution)/shard_map/ppermute | solution.py:25
  17.9 4.3 %collective-permute-start.4 = (bf16[64,2048]{1,0:T(8,128)(2,1)S(1)}, bf16[64,2048]{1,0:T(8,128)(2,1)S(1)}, u32[]{:S(2)}, u32[]{:S(2)}) collective-permute-start(bf16[64,2048]{1,0:T(8,128)(2,1)S(1)} %get-tuple-element.65.first_ref), channel_id=1, source_target_pairs={{0,1},{1,0},{2,3},{3,2},{4,5},{5,4},{6,7},{7,6},{8,9},{9,8},{10,11... | collective-permute-start | bytes 786440 | tf_op jit(solution)/shard_map/ppermute | solution.py:25
  17.9 4.3 %collective-permute-start.5 = (bf16[64,2048]{1,0:T(8,128)(2,1)S(1)}, bf16[64,2048]{1,0:T(8,128)(2,1)S(1)}, u32[]{:S(2)}, u32[]{:S(2)}) collective-permute-start(bf16[64,2048]{1,0:T(8,128)(2,1)S(1)} %collective-permute-done.3.second_ref), channel_id=1, source_target_pairs={{0,1},{1,0},{2,3},{3,2},{4,5},{5,4},{6,7},{7,6},{8,9},{9,8},{10,11... | collective-permute-start | bytes 786440 | tf_op jit(solution)/shard_map/ppermute | solution.py:25
  22.1 1.6 %collective-permute-start.7 = (bf16[512,256]{1,0:T(8,128)(2,1)S(1)}, bf16[512,256]{1,0:T(8,128)(2,1)S(1)}, u32[]{:S(2)}, u32[]{:S(2)}) collective-permute-start(bf16[512,256]{1,0:T(8,128)(2,1)S(1)} %pad_maximum_fusion.3.refs_1_), channel_id=1, source_target_pairs={{0,1},{1,0},{2,3},{3,2},{4,5},{5,4},{6,7},{7,6},{8,9},{9,8},{10,11... | collective-permute-start | bytes 786440 | tf_op jit(solution)/shard_map/ppermute | solution.py:25
  22.3 7.0 %copy-start.3 = (bf16[1,768,2048]{2,1,0:T(8,128)(2,1)S(1)}, bf16[1,768,2048]{2,1,0:T(8,128)(2,1)}, u32[]{:S(2)}) copy-start(bf16[1,768,2048]{2,1,0:T(8,128)(2,1)} %param.23) | copy-start | bytes 9437188
  26.5 11.7 %copy-start.7 = (bf16[1,64,2048]{2,1,0:T(8,128)(2,1)S(1)}, bf16[1,64,2048]{2,1,0:T(8,128)(2,1)}, u32[]{:S(2)}) copy-start(bf16[1,64,2048]{2,1,0:T(8,128)(2,1)} %param.12) | copy-start | bytes 786436
  26.5 11.9 %copy-start.8 = (f32[2048]{0:T(1024)S(1)}, f32[2048]{0:T(1024)}, u32[]{:S(2)}) copy-start(f32[2048]{0:T(1024)} %param.19) | copy-start | bytes 24580
  26.5 2.7 %collective-permute-start.8 = (f32[128,2048]{1,0:T(8,128)S(1)}, f32[128,2048]{1,0:T(8,128)S(1)}, u32[]{:S(2)}, u32[]{:S(2)}) collective-permute-start(f32[128,2048]{1,0:T(8,128)S(1)} %get-tuple-element.68), channel_id=1, source_target_pairs={{0,1},{1,0},{2,3},{3,2},{4,5},{5,4},{6,7},{7,6},{8,9},{9,8},{10,11... | collective-permute-start | bytes 3145736 | tf_op jit(solution)/shard_map/ppermute | solution.py:25
  29.2 9.0 %collective-permute-start.11 = (bf16[768,2048]{1,0:T(8,128)(2,1)S(1)}, bf16[768,2048]{1,0:T(8,128)(2,1)S(1)}, u32[]{:S(2)}, u32[]{:S(2)}) collective-permute-start(bf16[768,2048]{1,0:T(8,128)(2,1)S(1)} %bitcast.56), channel_id=1, source_target_pairs={{0,1},{1,0},{2,3},{3,2},{4,5},{5,4},{6,7},{7,6},{8,9},{9,8},{10,11... | collective-permute-start | bytes 9437192 | tf_op jit(solution)/shard_map/ppermute | solution.py:25
  29.5 26.4 %copy-start.5 = (f32[128,2048]{1,0:T(8,128)}, f32[128,2048]{1,0:T(8,128)S(1)}, u32[]{:S(2)}) copy-start(f32[128,2048]{1,0:T(8,128)S(1)} %add.104) | copy-start | bytes 3145732
  29.5 8.6 %collective-permute-start.9 = (bf16[64,2048]{1,0:T(8,128)(2,1)S(1)}, bf16[64,2048]{1,0:T(8,128)(2,1)S(1)}, u32[]{:S(2)}, u32[]{:S(2)}) collective-permute-start(bf16[64,2048]{1,0:T(8,128)(2,1)S(1)} %slice.145), channel_id=1, source_target_pairs={{0,2},{1,3},{2,0},{3,1},{4,6},{5,7},{6,4},{7,5},{8,10},{9,11},{10,... | collective-permute-start | bytes 786440 | tf_op jit(solution)/shard_map/ppermute | solution.py:25
  31.1 5.5 %collective-permute-start.10 = (bf16[2,256,128]{2,1,0:T(8,128)(2,1)S(1)}, bf16[2,256,128]{2,1,0:T(8,128)(2,1)S(1)}, u32[]{:S(2)}, u32[]{:S(2)}) collective-permute-start(bf16[2,256,128]{2,1,0:T(8,128)(2,1)S(1)} %pad_maximum_fusion.6), channel_id=1, source_target_pairs={{0,16},{16,0},{1,17},{17,1},{2,18},{18,2},{3,19},{19,3},{4,20},{20... | collective-permute-start | bytes 393224 | tf_op jit(solution)/shard_map/ppermute | solution.py:25
  38.2 16.1 %copy-start.4 = (bf16[768,2048]{1,0:T(8,128)(2,1)}, bf16[768,2048]{1,0:T(8,128)(2,1)S(1)}, u32[]{:S(2)}) copy-start(bf16[768,2048]{1,0:T(8,128)(2,1)S(1)} %collective-permute-done.11.refs_6_) | copy-start | bytes 9437188
  38.6 14.6 %collective-permute-start.13 = (bf16[64,2048]{1,0:T(8,128)(2,1)S(1)}, bf16[64,2048]{1,0:T(8,128)(2,1)}, u32[]{:S(2)}, u32[]{:S(2)}) collective-permute-start(bf16[64,2048]{1,0:T(8,128)(2,1)S(1)} %multiply_convert_fusion.refs_9_), channel_id=1, source_target_pairs={{0,8},{4,12},{8,0},{12,4},{1,9},{5,13},{9,1},{13,5},{2,10},{6,14},... | collective-permute-start | bytes 786440 | tf_op jit(solution)/shard_map/ppermute | solution.py:25
  40.9 12.4 %collective-permute-start.15 = (bf16[64,2048]{1,0:T(8,128)(2,1)S(1)}, bf16[64,2048]{1,0:T(8,128)(2,1)S(1)}, u32[]{:S(2)}, u32[]{:S(2)}) collective-permute-start(bf16[64,2048]{1,0:T(8,128)(2,1)S(1)} %multiply_convert_fusion.refs_9_), channel_id=1, source_target_pairs={{0,4},{4,0},{8,12},{12,8},{1,5},{5,1},{9,13},{13,9},{2,6},{6,2},{1... | collective-permute-start | bytes 786440 | tf_op jit(solution)/shard_map/ppermute | solution.py:25
  42.6 11.7 %collective-permute-start.17 = (bf16[64,2048]{1,0:T(8,128)(2,1)S(1)}, bf16[64,2048]{1,0:T(8,128)(2,1)S(1)}, u32[]{:S(2)}, u32[]{:S(2)}) collective-permute-start(bf16[64,2048]{1,0:T(8,128)(2,1)S(1)} %multiply_convert_fusion.refs_9_), channel_id=1, source_target_pairs={{0,16},{16,0},{1,17},{17,1},{2,18},{18,2},{3,19},{19,3},{4,20},{20... | collective-permute-start | bytes 786440 | tf_op jit(solution)/shard_map/ppermute | solution.py:25
  44.1 10.2 %collective-permute-start.16 = (bf16[64,2048]{1,0:T(8,128)(2,1)S(1)}, bf16[64,2048]{1,0:T(8,128)(2,1)S(1)}, u32[]{:S(2)}, u32[]{:S(2)}) collective-permute-start(bf16[64,2048]{1,0:T(8,128)(2,1)S(1)} %multiply_convert_fusion.refs_9_), channel_id=1, source_target_pairs={{0,2},{1,3},{2,0},{3,1},{4,6},{5,7},{6,4},{7,5},{8,10},{9,11},{10,... | collective-permute-start | bytes 786440 | tf_op jit(solution)/shard_map/ppermute | solution.py:25
  53.1 7.5 %collective-permute-start.14 = (bf16[64,2048]{1,0:T(8,128)(2,1)}, bf16[64,2048]{1,0:T(8,128)(2,1)S(1)}, u32[]{:S(2)}, u32[]{:S(2)}) collective-permute-start(bf16[64,2048]{1,0:T(8,128)(2,1)} %collective-permute-done.13), channel_id=1, source_target_pairs={{0,4},{4,0},{8,12},{12,8},{1,5},{5,1},{9,13},{13,9},{2,6},{6,2},{1... | collective-permute-start | bytes 786440 | tf_op jit(solution)/shard_map/ppermute | solution.py:25
  54.3 14.9 %collective-permute-start.20 = (bf16[128,2048]{1,0:T(8,128)(2,1)S(1)}, bf16[128,2048]{1,0:T(8,128)(2,1)S(1)}, u32[]{:S(2)}, u32[]{:S(2)}) collective-permute-start(bf16[128,2048]{1,0:T(8,128)(2,1)S(1)} %pad_maximum_fusion.2.refs_10_), channel_id=1, source_target_pairs={{0,16},{16,0},{1,17},{17,1},{2,18},{18,2},{3,19},{19,3},{4,20},{20... | collective-permute-start | bytes 1572872 | tf_op jit(solution)/shard_map/ppermute | solution.py:25
  55.9 14.9 %collective-permute-start.18 = (bf16[128,2048]{1,0:T(8,128)(2,1)S(1)}, bf16[128,2048]{1,0:T(8,128)(2,1)S(1)}, u32[]{:S(2)}, u32[]{:S(2)}) collective-permute-start(bf16[128,2048]{1,0:T(8,128)(2,1)S(1)} %pad_maximum_fusion.2.refs_10_), channel_id=1, source_target_pairs={{0,2},{1,3},{2,0},{3,1},{4,6},{5,7},{6,4},{7,5},{8,10},{9,11},{10,... | collective-permute-start | bytes 1572872 | tf_op jit(solution)/shard_map/ppermute | solution.py:25
  60.6 13.0 %collective-permute-start.21 = (bf16[64,2048]{1,0:T(8,128)(2,1)S(1)}, bf16[64,2048]{1,0:T(8,128)(2,1)S(1)}, u32[]{:S(2)}, u32[]{:S(2)}) collective-permute-start(bf16[64,2048]{1,0:T(8,128)(2,1)S(1)} %collective-permute-done.14.refs_11_), channel_id=1, source_target_pairs={{0,16},{16,0},{1,17},{17,1},{2,18},{18,2},{3,19},{19,3},{4,20},{20... | collective-permute-start | bytes 786440 | tf_op jit(solution)/shard_map/ppermute | solution.py:25
  62.0 12.8 %collective-permute-start.19 = (bf16[64,2048]{1,0:T(8,128)(2,1)S(1)}, bf16[64,2048]{1,0:T(8,128)(2,1)S(1)}, u32[]{:S(2)}, u32[]{:S(2)}) collective-permute-start(bf16[64,2048]{1,0:T(8,128)(2,1)S(1)} %collective-permute-done.14.refs_11_), channel_id=1, source_target_pairs={{0,2},{1,3},{2,0},{3,1},{4,6},{5,7},{6,4},{7,5},{8,10},{9,11},{10,... | collective-permute-start | bytes 786440 | tf_op jit(solution)/shard_map/ppermute | solution.py:25
  74.9 12.4 %collective-permute-start.22 = (bf16[256,1024]{1,0:T(8,128)(2,1)S(1)}, bf16[256,1024]{1,0:T(8,128)(2,1)S(1)}, u32[]{:S(2)}, u32[]{:S(2)}) collective-permute-start(bf16[256,1024]{1,0:T(8,128)(2,1)S(1)} %get-tuple-element.90), channel_id=1, source_target_pairs={{0,16},{16,0},{1,17},{17,1},{2,18},{18,2},{3,19},{19,3},{4,20},{20... | collective-permute-start | bytes 1572872 | tf_op jit(solution)/shard_map/ppermute | solution.py:25
  75.5 12.1 %collective-permute-start.23 = (bf16[256,1024]{1,0:T(8,128)(2,1)S(1)}, bf16[256,1024]{1,0:T(8,128)(2,1)S(1)}, u32[]{:S(2)}, u32[]{:S(2)}) collective-permute-start(bf16[256,1024]{1,0:T(8,128)(2,1)S(1)} %get-tuple-element.91), channel_id=1, source_target_pairs={{0,2},{1,3},{2,0},{3,1},{4,6},{5,7},{6,4},{7,5},{8,10},{9,11},{10,... | collective-permute-start | bytes 1572872 | tf_op jit(solution)/shard_map/ppermute | solution.py:25
  87.6 12.6 %collective-permute-start.24 = (bf16[256,1024]{1,0:T(8,128)(2,1)S(1)}, bf16[256,1024]{1,0:T(8,128)(2,1)S(1)}, u32[]{:S(2)}, u32[]{:S(2)}) collective-permute-start(bf16[256,1024]{1,0:T(8,128)(2,1)S(1)} %get-tuple-element.92), channel_id=1, source_target_pairs={{0,16},{16,0},{1,17},{17,1},{2,18},{18,2},{3,19},{19,3},{4,20},{20... | collective-permute-start | bytes 1572872 | tf_op jit(solution)/shard_map/ppermute | solution.py:25
  89.0 11.2 %collective-permute-start.25 = (bf16[256,1024]{1,0:T(8,128)(2,1)S(1)}, bf16[256,1024]{1,0:T(8,128)(2,1)S(1)}, u32[]{:S(2)}, u32[]{:S(2)}) collective-permute-start(bf16[256,1024]{1,0:T(8,128)(2,1)S(1)} %get-tuple-element.93), channel_id=1, source_target_pairs={{0,2},{1,3},{2,0},{3,1},{4,6},{5,7},{6,4},{7,5},{8,10},{9,11},{10,... | collective-permute-start | bytes 1572872 | tf_op jit(solution)/shard_map/ppermute | solution.py:25
  100.3 9.3 %collective-permute-start.26 = (bf16[128,1024]{1,0:T(8,128)(2,1)S(1)}, bf16[128,1024]{1,0:T(8,128)(2,1)S(1)}, u32[]{:S(2)}, u32[]{:S(2)}) collective-permute-start(bf16[128,1024]{1,0:T(8,128)(2,1)S(1)} %get-tuple-element.105), channel_id=1, source_target_pairs={{0,16},{16,0},{1,17},{17,1},{2,18},{18,2},{3,19},{19,3},{4,20},{20... | collective-permute-start | bytes 786440 | tf_op jit(solution)/shard_map/ppermute | solution.py:25
  100.9 9.7 %collective-permute-start.28 = (bf16[128,1024]{1,0:T(8,128)(2,1)S(1)}, bf16[128,1024]{1,0:T(8,128)(2,1)S(1)}, u32[]{:S(2)}, u32[]{:S(2)}) collective-permute-start(bf16[128,1024]{1,0:T(8,128)(2,1)S(1)} %get-tuple-element.107), channel_id=1, source_target_pairs={{0,2},{1,3},{2,0},{3,1},{4,6},{5,7},{6,4},{7,5},{8,10},{9,11},{10,... | collective-permute-start | bytes 786440 | tf_op jit(solution)/shard_map/ppermute | solution.py:25
  102.5 11.3 %collective-permute-start.30 = (bf16[128,1024]{1,0:T(8,128)(2,1)S(1)}, bf16[128,1024]{1,0:T(8,128)(2,1)S(1)}, u32[]{:S(2)}, u32[]{:S(2)}) collective-permute-start(bf16[128,1024]{1,0:T(8,128)(2,1)S(1)} %get-tuple-element.108), channel_id=1, source_target_pairs={{0,16},{16,0},{1,17},{17,1},{2,18},{18,2},{3,19},{19,3},{4,20},{20... | collective-permute-start | bytes 786440 | tf_op jit(solution)/shard_map/ppermute | solution.py:25
  104.2 9.9 %collective-permute-start.31 = (bf16[128,1024]{1,0:T(8,128)(2,1)S(1)}, bf16[128,1024]{1,0:T(8,128)(2,1)S(1)}, u32[]{:S(2)}, u32[]{:S(2)}) collective-permute-start(bf16[128,1024]{1,0:T(8,128)(2,1)S(1)} %get-tuple-element.109), channel_id=1, source_target_pairs={{0,2},{1,3},{2,0},{3,1},{4,6},{5,7},{6,4},{7,5},{8,10},{9,11},{10,... | collective-permute-start | bytes 786440 | tf_op jit(solution)/shard_map/ppermute | solution.py:25
  109.7 8.2 %collective-permute-start.27 = (bf16[128,1024]{1,0:T(8,128)(2,1)S(1)}, bf16[128,1024]{1,0:T(8,128)(2,1)S(1)}, u32[]{:S(2)}, u32[]{:S(2)}) collective-permute-start(bf16[128,1024]{1,0:T(8,128)(2,1)S(1)} %add_convert_fusion.3), channel_id=1, source_target_pairs={{0,2},{1,3},{2,0},{3,1},{4,6},{5,7},{6,4},{7,5},{8,10},{9,11},{10,... | collective-permute-start | bytes 786440 | tf_op jit(solution)/shard_map/ppermute | solution.py:25
  110.7 7.2 %collective-permute-start.29 = (bf16[128,1024]{1,0:T(8,128)(2,1)S(1)}, bf16[128,1024]{1,0:T(8,128)(2,1)S(1)}, u32[]{:S(2)}, u32[]{:S(2)}) collective-permute-start(bf16[128,1024]{1,0:T(8,128)(2,1)S(1)} %add_convert_fusion.2), channel_id=1, source_target_pairs={{0,16},{16,0},{1,17},{17,1},{2,18},{18,2},{3,19},{19,3},{4,20},{20... | collective-permute-start | bytes 786440 | tf_op jit(solution)/shard_map/ppermute | solution.py:25
  118.5 21.4 %copy-start.6 = (f32[128,2048]{1,0:T(8,128)S(1)}, f32[128,2048]{1,0:T(8,128)}, u32[]{:S(2)}) copy-start(f32[128,2048]{1,0:T(8,128)} %copy-done.5) | copy-start | bytes 3145732
  118.5 10.3 %collective-permute-start.35 = (bf16[64,2048]{1,0:T(8,128)(2,1)S(1)}, bf16[64,2048]{1,0:T(8,128)(2,1)S(1)}, u32[]{:S(2)}, u32[]{:S(2)}) collective-permute-start(bf16[64,2048]{1,0:T(8,128)(2,1)S(1)} %fusion.9), channel_id=1, source_target_pairs={{0,4},{4,0},{8,12},{12,8},{1,5},{5,1},{9,13},{13,9},{2,6},{6,2},{1... | collective-permute-start | bytes 786440 | tf_op jit(solution)/shard_map/ppermute | solution.py:25
  118.6 12.5 %collective-permute-start.32 = (bf16[128,1024]{1,0:T(8,128)(2,1)S(1)}, bf16[128,1024]{1,0:T(8,128)(2,1)S(1)}, u32[]{:S(2)}, u32[]{:S(2)}) collective-permute-start(bf16[128,1024]{1,0:T(8,128)(2,1)S(1)} %get-tuple-element.116), channel_id=1, source_target_pairs={{0,2},{1,3},{2,0},{3,1},{4,6},{5,7},{6,4},{7,5},{8,10},{9,11},{10,... | collective-permute-start | bytes 786440 | tf_op jit(solution)/shard_map/ppermute | solution.py:25
  120.2 11.0 %collective-permute-start.33 = (bf16[128,1024]{1,0:T(8,128)(2,1)S(1)}, bf16[128,1024]{1,0:T(8,128)(2,1)S(1)}, u32[]{:S(2)}, u32[]{:S(2)}) collective-permute-start(bf16[128,1024]{1,0:T(8,128)(2,1)S(1)} %get-tuple-element.117), channel_id=1, source_target_pairs={{0,16},{16,0},{1,17},{17,1},{2,18},{18,2},{3,19},{19,3},{4,20},{20... | collective-permute-start | bytes 786440 | tf_op jit(solution)/shard_map/ppermute | solution.py:25
  128.9 10.3 %collective-permute-start.36 = (bf16[64,2048]{1,0:T(8,128)(2,1)S(1)}, bf16[64,2048]{1,0:T(8,128)(2,1)S(1)}, u32[]{:S(2)}, u32[]{:S(2)}) collective-permute-start(bf16[64,2048]{1,0:T(8,128)(2,1)S(1)} %fusion.1), channel_id=1, source_target_pairs={{0,8},{4,12},{8,0},{12,4},{1,9},{5,13},{9,1},{13,5},{2,10},{6,14},... | collective-permute-start | bytes 786440 | tf_op jit(solution)/shard_map/ppermute | solution.py:25
  131.5 8.5 %collective-permute-start.34 = (bf16[64,2048]{1,0:T(8,128)(2,1)S(1)}, bf16[64,2048]{1,0:T(8,128)(2,1)S(1)}, u32[]{:S(2)}, u32[]{:S(2)}) collective-permute-start(bf16[64,2048]{1,0:T(8,128)(2,1)S(1)} %fusion.8), channel_id=1, source_target_pairs={{0,4},{4,0},{8,12},{12,8},{1,5},{5,1},{9,13},{13,9},{2,6},{6,2},{1... | collective-permute-start | bytes 786440 | tf_op jit(solution)/shard_map/ppermute | solution.py:25

commit v13 on v12

--- a/solution.py
+++ b/solution.py
@@ -69,16 +69,18 @@
     blocks = {0: own}
     for bits in seq_bits():
         blocks |= {place ^ bits: swap(block, "seq", bits) for place, block in blocks.items()}
-    middle = jnp.concatenate([blocks[place] for place in range(1, len(blocks) - 1)], axis=0)
-    middle, coded, *outer = ready(middle, coded, *both_ways(own))
-    last, *tables = ready(blocks[len(blocks) - 1], *tables_of(coded))
-    by_rep, by_role = zip(outer, both_ways(middle), both_ways(last))
+    middle = [blocks[place] for place in range(2, len(blocks) - 1)]
+    middle = jnp.concatenate(middle, axis=0) if len(middle) > 1 else middle[0]
+    parts = [own, blocks[1], middle, blocks[len(blocks) - 1]]
+    parts[2], coded, *early = ready(parts[2], coded, *both_ways(own), *both_ways(parts[1]))
+    parts[3], *tables = ready(parts[3], *tables_of(coded))
+    by_rep, by_role = zip(early[:2], early[2:], both_ways(parts[2]), both_ways(parts[3]))
     low, high = pack_corners(by_rep, by_role)
     corner_low, corner_high = swap(low, "role", 1), swap(high, "rep", ACROSS)
-    starts = (0, rows, rows + middle.shape[0])
+    starts = (0, rows, 2 * rows, 2 * rows + middle.shape[0])
     groups = [
-        [(start, 0, part) for start, part in zip(starts, parts)]
-        for parts in (by_rep, by_role, (own, middle, last))
+        [(start, 0, part) for start, part in zip(starts, held)]
+        for held in (by_rep, by_role, parts)
     ]
     groups.insert(2, [(0, 0, corner_low), (0, half, corner_high)])
     return groups, tables

time: 141 us -> 138 us (0.979)
  starting transfers between devices: 45.2 us -> 43.4 us
    ppermute x37 -> x39, starting transfers between devices: 45.2 us -> 43.4 us  [swap(): return lax.ppermute(block, axis, [(i, i ^ bits) for i in range(size)])]
    ppermute x37 -> x39, waiting for transfers between devices: 64.5 us -> 64.8 us  [swap(): return lax.ppermute(block, axis, [(i, i ^ bits) for i in range(size)])]
  transfers between devices with their start and end apart: 37 -> 39, of which waited for: 23 -> 24; matrix products, arithmetic and copies ran while one was open for 1% -> 1% of each run, Pallas kernels for 19% -> 20%
where the time goes in v13:
time: 138 us
  waiting for transfers between devices  64.8 us (47%)
  starting transfers between devices  43.4 us (31%)
  Pallas kernels  27 us (20%)
  other arithmetic  2.46 us (2%)
    ppermute x39, waiting for transfers between devices, swap(): return lax.ppermute(block, axis, [(i, i ^ bits) for i in range(size)])  64.8 us
    ppermute x39, starting transfers between devices, swap(): return lax.ppermute(block, axis, [(i, i ^ bits) for i in range(size)])  43.4 us
    pallas_call x2, Pallas kernels, run_experts(): pl.pallas_call(lambda *refs: expert_kernel(first, spots, cuts, *refs), ou...  19.2 us
  transfers between devices with their start and end apart: 39, of which 24 were waited for; matrix products, arithmetic and copies ran while one was open for 1% of the time, Pallas kernels for 20%

profile of v13, /device:TPU:0, one launch (start us, length us, event | category | flops | bytes accessed | tf_op | source)
XLA Modules:
  0.0 138.3 jit_solution(8752307125144248738)
XLA Ops:
  0.0 0.5 collective-permute-start.12
  0.5 2.6 %prepare.1 = (bf16[64,2048]{1,0:T(8,128)(2,1)S(1)}, bf16[64,640]{1,0:T(8,128)(2,1)S(1)}) custom-call(bf16[64,2048]{1,0:T(8,128)(2,1)} %bitcast.57, f32[1,2048]{1,0:T(1,128)} %bitcast.62, bf16[2,2048,256]{2,1,0:T(8,128)(2,1)} %refs_2_.1, f32[1,128]{1,0:T(1,128)} %bitcast.65, s32[8,64]{1,0:T(8,128)} %bitcast.63, s32[8,64]{1,0:T(8,128)} %bitcast.64), custom_call_target="tpu_custom_call" | custom-call | flops 134217728 | bytes 2621440 | tf_op jit(solution)/shard_map/prepare/pallas_call | solution.py:186
  3.1 4.7 %collective-permute-start.2 = (bf16[64,640]{1,0:T(8,128)(2,1)S(1)}, bf16[64,640]{1,0:T(8,128)(2,1)S(1)}, u32[]{:S(2)}, u32[]{:S(2)}) collective-permute-start(bf16[64,640]{1,0:T(8,128)(2,1)S(1)} %get-tuple-element.65), channel_id=1, source_target_pairs={{0,12},{4,8},{8,4},{12,0},{1,13},{5,9},{9,5},{13,1},{2,14},{6,10},... | collective-permute-start | bytes 245768 | tf_op jit(solution)/shard_map/ppermute | solution.py:25
  7.7 0.6 collective-permute-start
  8.4 1.7 %collective-permute-start.3 = (bf16[64,2048]{1,0:T(8,128)(2,1)S(1)}, bf16[64,2048]{1,0:T(8,128)(2,1)S(1)}, u32[]{:S(2)}, u32[]{:S(2)}) collective-permute-start(bf16[64,2048]{1,0:T(8,128)(2,1)S(1)} %get-tuple-element.67.first_ref), channel_id=1, source_target_pairs={{0,2},{1,3},{2,0},{3,1},{4,6},{5,7},{6,4},{7,5},{8,10},{9,11},{10,... | collective-permute-start | bytes 786440 | tf_op jit(solution)/shard_map/ppermute | solution.py:25
  10.0 3.5 %collective-permute-done = bf16[64,640]{1,0:T(8,128)(2,1)S(1)} collective-permute-done((bf16[64,640]{1,0:T(8,128)(2,1)S(1)}, bf16[64,640]{1,0:T(8,128)(2,1)S(1)}, u32[]{:S(2)}, u32[]{:S(2)}) %collective-permute-start) | collective-permute-done | bytes 81952 | tf_op jit(solution)/shard_map/ppermute | solution.py:25
  13.5 1.6 %collective-permute-done.1 = bf16[64,640]{1,0:T(8,128)(2,1)S(1)} collective-permute-done((bf16[64,640]{1,0:T(8,128)(2,1)S(1)}, bf16[64,640]{1,0:T(8,128)(2,1)S(1)}, u32[]{:S(2)}, u32[]{:S(2)}) %collective-permute-start.1) | collective-permute-done | bytes 81952 | tf_op jit(solution)/shard_map/ppermute | solution.py:25
  15.3 1.1 collective-permute-done.3.second_ref
  16.4 1.5 %collective-permute-start.6 = (bf16[256,384]{1,0:T(8,128)(2,1)S(1)}, bf16[256,384]{1,0:T(8,128)(2,1)S(1)}, u32[]{:S(2)}, u32[]{:S(2)}) collective-permute-start(bf16[256,384]{1,0:T(8,128)(2,1)S(1)} %pad_maximum_fusion.4), channel_id=1, source_target_pairs={{0,2},{1,3},{2,0},{3,1},{4,6},{5,7},{6,4},{7,5},{8,10},{9,11},{10,... | collective-permute-start | bytes 589832 | tf_op jit(solution)/shard_map/ppermute | solution.py:25
  17.9 0.5 collective-permute-start.5
  18.4 3.7 %collective-permute-done.6 = bf16[256,384]{1,0:T(8,128)(2,1)S(1)} collective-permute-done((bf16[256,384]{1,0:T(8,128)(2,1)S(1)}, bf16[256,384]{1,0:T(8,128)(2,1)S(1)}, u32[]{:S(2)}, u32[]{:S(2)}) %collective-permute-start.6) | collective-permute-done | bytes 196640 | tf_op jit(solution)/shard_map/ppermute | solution.py:25
  22.3 0.9 queries.1.refs_0_
  23.1 0.6 collective-permute-done.7.refs_2_
  23.7 2.7 %attend.1 = (f32[128,2048]{1,0:T(8,128)S(1)}, f32[128,2048]{1,0:T(8,128)S(1)}) custom-call(bf16[256,512]{1,0:T(8,128)(2,1)S(1)} %queries.1.refs_0_, bf16[512,256]{1,0:T(8,128)(2,1)S(1)} %pad_maximum_fusion.2.refs_1_, bf16[512,256]{1,0:T(8,128)(2,1)S(1)} %collective-permute-done.7.refs_2_, bf16[512,2048]{1,0:T(8,128)(2,1)S(1)} %copy-done.2), custom_call_target="tpu_custom_call" | custom-call | flops 1073741824 | bytes 4194304 | tf_op jit(solution)/shard_map/attend/pallas_call | solution.py:265
  26.5 0.2 collective-permute-start.8
  26.7 2.5 %collective-permute-done.8 = f32[128,2048]{1,0:T(8,128)S(1)} collective-permute-done((f32[128,2048]{1,0:T(8,128)S(1)}, f32[128,2048]{1,0:T(8,128)S(1)}, u32[]{:S(2)}, u32[]{:S(2)}) %collective-permute-start.8) | collective-permute-done | bytes 1048608 | tf_op jit(solution)/shard_map/ppermute | solution.py:25
  29.5 1.5 %collective-permute-start.9 = (bf16[64,2048]{1,0:T(8,128)(2,1)S(1)}, bf16[64,2048]{1,0:T(8,128)(2,1)S(1)}, u32[]{:S(2)}, u32[]{:S(2)}) collective-permute-start(bf16[64,2048]{1,0:T(8,128)(2,1)S(1)} %slice.145), channel_id=1, source_target_pairs={{0,2},{1,3},{2,0},{3,1},{4,6},{5,7},{6,4},{7,5},{8,10},{9,11},{10,... | collective-permute-start | bytes 786440 | tf_op jit(solution)/shard_map/ppermute | solution.py:25
  31.1 1.6 %collective-permute-start.10 = (bf16[2,256,128]{2,1,0:T(8,128)(2,1)S(1)}, bf16[2,256,128]{2,1,0:T(8,128)(2,1)S(1)}, u32[]{:S(2)}, u32[]{:S(2)}) collective-permute-start(bf16[2,256,128]{2,1,0:T(8,128)(2,1)S(1)} %pad_maximum_fusion.5), channel_id=1, source_target_pairs={{0,16},{16,0},{1,17},{17,1},{2,18},{18,2},{3,19},{19,3},{4,20},{20... | collective-permute-start | bytes 393224 | tf_op jit(solution)/shard_map/ppermute | solution.py:25
  32.6 4.0 %collective-permute-done.10 = bf16[2,256,128]{2,1,0:T(8,128)(2,1)S(1)} collective-permute-done((bf16[2,256,128]{2,1,0:T(8,128)(2,1)S(1)}, bf16[2,256,128]{2,1,0:T(8,128)(2,1)S(1)}, u32[]{:S(2)}, u32[]{:S(2)}) %collective-permute-start.10) | collective-permute-done | bytes 131104 | tf_op jit(solution)/shard_map/ppermute | solution.py:25
  36.7 1.5 %collective-permute-done.9 = bf16[64,2048]{1,0:T(8,128)(2,1)S(1)} collective-permute-done((bf16[64,2048]{1,0:T(8,128)(2,1)S(1)}, bf16[64,2048]{1,0:T(8,128)(2,1)S(1)}, u32[]{:S(2)}, u32[]{:S(2)}) %collective-permute-start.9) | collective-permute-done | bytes 262176 | tf_op jit(solution)/shard_map/ppermute | solution.py:25
  38.2 0.2 multiply_reduce_fusion
  38.6 1.5 %collective-permute-start.17 = (bf16[64,2048]{1,0:T(8,128)(2,1)S(1)}, bf16[64,2048]{1,0:T(8,128)(2,1)S(1)}, u32[]{:S(2)}, u32[]{:S(2)}) collective-permute-start(bf16[64,2048]{1,0:T(8,128)(2,1)S(1)} %multiply_convert_fusion.refs_9_), channel_id=1, source_target_pairs={{0,4},{4,0},{8,12},{12,8},{1,5},{5,1},{9,13},{13,9},{2,6},{6,2},{1... | collective-permute-start | bytes 786440 | tf_op jit(solution)/shard_map/ppermute | solution.py:25
  40.0 2.6 %collective-permute-start.13 = (bf16[64,2048]{1,0:T(8,128)(2,1)S(1)}, bf16[64,2048]{1,0:T(8,128)(2,1)S(1)}, u32[]{:S(2)}, u32[]{:S(2)}) collective-permute-start(bf16[64,2048]{1,0:T(8,128)(2,1)S(1)} %multiply_convert_fusion.refs_9_), channel_id=1, source_target_pairs={{0,8},{4,12},{8,0},{12,4},{1,9},{5,13},{9,1},{13,5},{2,10},{6,14},... | collective-permute-start | bytes 786440 | tf_op jit(solution)/shard_map/ppermute | solution.py:25
  42.6 1.5 %collective-permute-start.16 = (bf16[64,2048]{1,0:T(8,128)(2,1)S(1)}, bf16[64,2048]{1,0:T(8,128)(2,1)S(1)}, u32[]{:S(2)}, u32[]{:S(2)}) collective-permute-start(bf16[64,2048]{1,0:T(8,128)(2,1)S(1)} %multiply_convert_fusion.refs_9_), channel_id=1, source_target_pairs={{0,16},{16,0},{1,17},{17,1},{2,18},{18,2},{3,19},{19,3},{4,20},{20... | collective-permute-start | bytes 786440 | tf_op jit(solution)/shard_map/ppermute | solution.py:25
  44.1 1.5 %collective-permute-start.15 = (bf16[64,2048]{1,0:T(8,128)(2,1)S(1)}, bf16[64,2048]{1,0:T(8,128)(2,1)S(1)}, u32[]{:S(2)}, u32[]{:S(2)}) collective-permute-start(bf16[64,2048]{1,0:T(8,128)(2,1)S(1)} %multiply_convert_fusion.refs_9_), channel_id=1, source_target_pairs={{0,2},{1,3},{2,0},{3,1},{4,6},{5,7},{6,4},{7,5},{8,10},{9,11},{10,... | collective-permute-start | bytes 786440 | tf_op jit(solution)/shard_map/ppermute | solution.py:25
  45.6 6.2 %collective-permute-done.17.refs_10_ = bf16[64,2048]{1,0:T(8,128)(2,1)S(1)} collective-permute-done((bf16[64,2048]{1,0:T(8,128)(2,1)S(1)}, bf16[64,2048]{1,0:T(8,128)(2,1)S(1)}, u32[]{:S(2)}, u32[]{:S(2)}) %collective-permute-start.17) | collective-permute-done | bytes 262176 | tf_op jit(solution)/shard_map/ppermute | solution.py:25
  51.8 1.4 %collective-permute-start.19 = (bf16[64,2048]{1,0:T(8,128)(2,1)S(1)}, bf16[64,2048]{1,0:T(8,128)(2,1)S(1)}, u32[]{:S(2)}, u32[]{:S(2)}) collective-permute-start(bf16[64,2048]{1,0:T(8,128)(2,1)S(1)} %collective-permute-done.17.refs_10_), channel_id=1, source_target_pairs={{0,16},{16,0},{1,17},{17,1},{2,18},{18,2},{3,19},{19,3},{4,20},{20... | collective-permute-start | bytes 786440 | tf_op jit(solution)/shard_map/ppermute | solution.py:25
  53.2 1.5 %collective-permute-start.18 = (bf16[64,2048]{1,0:T(8,128)(2,1)S(1)}, bf16[64,2048]{1,0:T(8,128)(2,1)S(1)}, u32[]{:S(2)}, u32[]{:S(2)}) collective-permute-start(bf16[64,2048]{1,0:T(8,128)(2,1)S(1)} %collective-permute-done.17.refs_10_), channel_id=1, source_target_pairs={{0,2},{1,3},{2,0},{3,1},{4,6},{5,7},{6,4},{7,5},{8,10},{9,11},{10,... | collective-permute-start | bytes 786440 | tf_op jit(solution)/shard_map/ppermute | solution.py:25
  54.8 3.8 %collective-permute-done.19.refs_12_.refs_5_ = bf16[64,2048]{1,0:T(8,128)(2,1)S(1)} collective-permute-done((bf16[64,2048]{1,0:T(8,128)(2,1)S(1)}, bf16[64,2048]{1,0:T(8,128)(2,1)S(1)}, u32[]{:S(2)}, u32[]{:S(2)}) %collective-permute-start.19) | collective-permute-done | bytes 262176 | tf_op jit(solution)/shard_map/ppermute | solution.py:25
  58.6 1.2 collective-permute-done.18.refs_8_.refs_1_
  59.8 0.6 collective-permute-start.22
  60.4 1.5 %collective-permute-start.20 = (bf16[64,2048]{1,0:T(8,128)(2,1)S(1)}, bf16[64,2048]{1,0:T(8,128)(2,1)S(1)}, u32[]{:S(2)}, u32[]{:S(2)}) collective-permute-start(bf16[64,2048]{1,0:T(8,128)(2,1)S(1)} %collective-permute-done.13.refs_11_), channel_id=1, source_target_pairs={{0,2},{1,3},{2,0},{3,1},{4,6},{5,7},{6,4},{7,5},{8,10},{9,11},{10,... | collective-permute-start | bytes 786440 | tf_op jit(solution)/shard_map/ppermute | solution.py:25
  61.8 1.6 %tables.1 = (bf16[4,224,256]{2,1,0:T(8,128)(2,1)S(1)}, bf16[2,4,256,112]{3,2,1,0:T(8,128)(2,1)S(1)}, f32[4,256,2]{2,1,0:T(8,128)S(1)}) custom-call(s32[1]{0:T(128)} %bitcast.12.refs_0_, bf16[4,256,128]{2,1,0:T(8,128)(2,1)S(1)} %pad_maximum_fusion.3.refs_1_), custom_call_target="tpu_custom_call" | custom-call | flops 134217728 | bytes 917504 | tf_op jit(solution)/shard_map/tables/pallas_call | solution.py:328
  63.4 1.5 %collective-permute-start.23 = (bf16[64,2048]{1,0:T(8,128)(2,1)S(1)}, bf16[64,2048]{1,0:T(8,128)(2,1)S(1)}, u32[]{:S(2)}, u32[]{:S(2)}) collective-permute-start(bf16[64,2048]{1,0:T(8,128)(2,1)S(1)} %collective-permute-done.14.refs_12_), channel_id=1, source_target_pairs={{0,16},{16,0},{1,17},{17,1},{2,18},{18,2},{3,19},{19,3},{4,20},{20... | collective-permute-start | bytes 786440 | tf_op jit(solution)/shard_map/ppermute | solution.py:25
  65.0 0.5 collective-permute-start.21
  65.5 3.1 %collective-permute-done.22.refs_13_.refs_6_ = bf16[64,2048]{1,0:T(8,128)(2,1)S(1)} collective-permute-done((bf16[64,2048]{1,0:T(8,128)(2,1)S(1)}, bf16[64,2048]{1,0:T(8,128)(2,1)S(1)}, u32[]{:S(2)}, u32[]{:S(2)}) %collective-permute-start.22) | collective-permute-done | bytes 262176 | tf_op jit(solution)/shard_map/ppermute | solution.py:25
  68.6 0.7 collective-permute-done.20.refs_9_.refs_2_
  69.3 2.1 %collective-permute-done.23.refs_14_.refs_7_ = bf16[64,2048]{1,0:T(8,128)(2,1)S(1)} collective-permute-done((bf16[64,2048]{1,0:T(8,128)(2,1)S(1)}, bf16[64,2048]{1,0:T(8,128)(2,1)S(1)}, u32[]{:S(2)}, u32[]{:S(2)}) %collective-permute-start.23) | collective-permute-done | bytes 262176 | tf_op jit(solution)/shard_map/ppermute | solution.py:25
  71.4 0.9 collective-permute-done.21.refs_10_.refs_3_
  72.4 0.9 collective-permute-start.24
  73.3 1.1 collective-permute-start.25
  74.5 9.5 %experts.2 = (bf16[256,1024]{1,0:T(8,128)(2,1)S(1)}, bf16[256,1024]{1,0:T(8,128)(2,1)S(1)}, bf16[256,1024]{1,0:T(8,128)(2,1)S(1)}, bf16[256,1024]{1,0:T(8,128)(2,1)S(1)}) custom-call(bf16[4,224,256]{2,1,0:T(8,128)(2,1)S(1)} %get-tuple-element.79.refs_0_, bf16[2,4,256,112]{3,2,1,0:T(8,128)(2,1)S(1)} %get-tuple-element.80.refs_1_, ...), custom_call_target="tpu_custom_call" | custom-call | flops 4227858432 | bytes 23068672 | tf_op jit(solution)/shard_map/experts/pallas_call | solution.py:458
  84.0 0.6 collective-permute-done.24.refs_7_
  84.6 1.7 %collective-permute-start.26 = (bf16[256,1024]{1,0:T(8,128)(2,1)S(1)}, bf16[256,1024]{1,0:T(8,128)(2,1)S(1)}, u32[]{:S(2)}, u32[]{:S(2)}) collective-permute-start(bf16[256,1024]{1,0:T(8,128)(2,1)S(1)} %get-tuple-element.96), channel_id=1, source_target_pairs={{0,16},{16,0},{1,17},{17,1},{2,18},{18,2},{3,19},{19,3},{4,20},{20... | collective-permute-start | bytes 1572872 | tf_op jit(solution)/shard_map/ppermute | solution.py:25
  86.3 9.7 %experts.3 = (bf16[128,1024]{1,0:T(8,128)(2,1)S(1)}, bf16[128,1024]{1,0:T(8,128)(2,1)S(1)}, bf16[128,1024]{1,0:T(8,128)(2,1)S(1)}, bf16[128,1024]{1,0:T(8,128)(2...) custom-call(bf16[4,224,256]{2,1,0:T(8,128)(2,1)S(1)} %get-tuple-element.79.refs_0_, ...), custom_call_target="tpu_custom_call" | custom-call | flops 4227858432 | bytes 23068672 | tf_op jit(solution)/shard_map/experts/pallas_call | solution.py:458
  96.1 0.9 collective-permute-start.28
  96.9 1.5 %collective-permute-start.30 = (bf16[128,1024]{1,0:T(8,128)(2,1)S(1)}, bf16[128,1024]{1,0:T(8,128)(2,1)S(1)}, u32[]{:S(2)}, u32[]{:S(2)}) collective-permute-start(bf16[128,1024]{1,0:T(8,128)(2,1)S(1)} %get-tuple-element.111), channel_id=1, source_target_pairs={{0,2},{1,3},{2,0},{3,1},{4,6},{5,7},{6,4},{7,5},{8,10},{9,11},{10,... | collective-permute-start | bytes 786440 | tf_op jit(solution)/shard_map/ppermute | solution.py:25
  98.4 1.7 %collective-permute-start.32 = (bf16[128,1024]{1,0:T(8,128)(2,1)S(1)}, bf16[128,1024]{1,0:T(8,128)(2,1)S(1)}, u32[]{:S(2)}, u32[]{:S(2)}) collective-permute-start(bf16[128,1024]{1,0:T(8,128)(2,1)S(1)} %get-tuple-element.112), channel_id=1, source_target_pairs={{0,16},{16,0},{1,17},{17,1},{2,18},{18,2},{3,19},{19,3},{4,20},{20... | collective-permute-start | bytes 786440 | tf_op jit(solution)/shard_map/ppermute | solution.py:25
  100.2 5.2 %collective-permute-done.28 = bf16[128,1024]{1,0:T(8,128)(2,1)S(1)} collective-permute-done((bf16[128,1024]{1,0:T(8,128)(2,1)S(1)}, bf16[128,1024]{1,0:T(8,128)(2,1)S(1)}, u32[]{:S(2)}, u32[]{:S(2)}) %collective-permute-start.28) | collective-permute-done | bytes 262176 | tf_op jit(solution)/shard_map/ppermute | solution.py:25
  105.5 1.4 %collective-permute-start.29 = (bf16[128,1024]{1,0:T(8,128)(2,1)S(1)}, bf16[128,1024]{1,0:T(8,128)(2,1)S(1)}, u32[]{:S(2)}, u32[]{:S(2)}) collective-permute-start(bf16[128,1024]{1,0:T(8,128)(2,1)S(1)} %add_convert_fusion.3), channel_id=1, source_target_pairs={{0,2},{1,3},{2,0},{3,1},{4,6},{5,7},{6,4},{7,5},{8,10},{9,11},{10,... | collective-permute-start | bytes 786440 | tf_op jit(solution)/shard_map/ppermute | solution.py:25
  107.0 1.0 collective-permute-start.31
  108.0 1.2 collective-permute-done.32
  109.2 0.4 collective-permute-done.33
  109.6 4.3 %collective-permute-done.29 = bf16[128,1024]{1,0:T(8,128)(2,1)S(1)} collective-permute-done((bf16[128,1024]{1,0:T(8,128)(2,1)S(1)}, bf16[128,1024]{1,0:T(8,128)(2,1)S(1)}, u32[]{:S(2)}, u32[]{:S(2)}) %collective-permute-start.29) | collective-permute-done | bytes 262176 | tf_op jit(solution)/shard_map/ppermute | solution.py:25
  113.9 1.6 %collective-permute-done.31 = bf16[128,1024]{1,0:T(8,128)(2,1)S(1)} collective-permute-done((bf16[128,1024]{1,0:T(8,128)(2,1)S(1)}, bf16[128,1024]{1,0:T(8,128)(2,1)S(1)}, u32[]{:S(2)}, u32[]{:S(2)}) %collective-permute-start.31) | collective-permute-done | bytes 262176 | tf_op jit(solution)/shard_map/ppermute | solution.py:25
  115.7 0.3 convert_add_fusion.2
  116.2 0.4 collective-permute-start.34
  116.6 0.8 collective-permute-start.35
  117.4 9.0 %collective-permute-done.37 = bf16[64,2048]{1,0:T(8,128)(2,1)S(1)} collective-permute-done((bf16[64,2048]{1,0:T(8,128)(2,1)S(1)}, bf16[64,2048]{1,0:T(8,128)(2,1)S(1)}, u32[]{:S(2)}, u32[]{:S(2)}) %collective-permute-start.37) | collective-permute-done | bytes 262176 | tf_op jit(solution)/shard_map/ppermute | solution.py:25
  126.4 2.1 %collective-permute-start.38 = (bf16[64,2048]{1,0:T(8,128)(2,1)S(1)}, bf16[64,2048]{1,0:T(8,128)(2,1)S(1)}, u32[]{:S(2)}, u32[]{:S(2)}) collective-permute-start(bf16[64,2048]{1,0:T(8,128)(2,1)S(1)} %fusion.1), channel_id=1, source_target_pairs={{0,8},{4,12},{8,0},{12,4},{1,9},{5,13},{9,1},{13,5},{2,10},{6,14},... | collective-permute-start | bytes 786440 | tf_op jit(solution)/shard_map/ppermute | solution.py:25
  128.9 2.5 %collective-permute-start.36 = (bf16[64,2048]{1,0:T(8,128)(2,1)S(1)}, bf16[64,2048]{1,0:T(8,128)(2,1)S(1)}, u32[]{:S(2)}, u32[]{:S(2)}) collective-permute-start(bf16[64,2048]{1,0:T(8,128)(2,1)S(1)} %fusion.8), channel_id=1, source_target_pairs={{0,4},{4,0},{8,12},{12,8},{1,5},{5,1},{9,13},{13,9},{2,6},{6,2},{1... | collective-permute-start | bytes 786440 | tf_op jit(solution)/shard_map/ppermute | solution.py:25
  131.4 5.2 %collective-permute-done.38 = bf16[64,2048]{1,0:T(8,128)(2,1)S(1)} collective-permute-done((bf16[64,2048]{1,0:T(8,128)(2,1)S(1)}, bf16[64,2048]{1,0:T(8,128)(2,1)S(1)}, u32[]{:S(2)}, u32[]{:S(2)}) %collective-permute-start.38) | collective-permute-done | bytes 262176 | tf_op jit(solution)/shard_map/ppermute | solution.py:25
  136.6 0.8 collective-permute-done.36
  137.4 0.9 fusion.7
  (69 shorter events, 1.9 us)
Async XLA Ops:
  0.0 22.2 %copy-start.1 = (f32[128]{0:T(128)S(1)}, f32[128]{0:T(128)}, u32[]{:S(2)}) copy-start(f32[128]{0:T(128)} %param.16) | copy-start | bytes 1540
  0.0 22.2 %copy-start = (bf16[2048,512]{1,0:T(8,128)(2,1)S(1)}, bf16[2048,512]{1,0:T(8,128)(2,1)}, u32[]{:S(2)}) copy-start(bf16[2048,512]{1,0:T(8,128)(2,1)} %weight_ref.1) | copy-start | bytes 6291460
  0.0 38.2 %collective-permute-start.12 = (bf16[2048,1536]{1,0:T(8,128)(2,1)}, bf16[2048,1536]{1,0:T(8,128)(2,1)}, u32[]{:S(2)}, u32[]{:S(2)}) collective-permute-start(bf16[2048,1536]{1,0:T(8,128)(2,1)} %bitcast.51), channel_id=1, source_target_pairs={{0,1},{1,0},{2,3},{3,2},{4,5},{5,4},{6,7},{7,6},{8,9},{9,8},{10,11... | collective-permute-start | bytes 18874376 | tf_op jit(solution)/shard_map/ppermute | solution.py:25
  3.1 12.0 %collective-permute-start.2 = (bf16[64,640]{1,0:T(8,128)(2,1)S(1)}, bf16[64,640]{1,0:T(8,128)(2,1)S(1)}, u32[]{:S(2)}, u32[]{:S(2)}) collective-permute-start(bf16[64,640]{1,0:T(8,128)(2,1)S(1)} %get-tuple-element.65), channel_id=1, source_target_pairs={{0,12},{4,8},{8,4},{12,0},{1,13},{5,9},{9,5},{13,1},{2,14},{6,10},... | collective-permute-start | bytes 245768 | tf_op jit(solution)/shard_map/ppermute | solution.py:25
  7.7 7.4 %collective-permute-start.1 = (bf16[64,640]{1,0:T(8,128)(2,1)S(1)}, bf16[64,640]{1,0:T(8,128)(2,1)S(1)}, u32[]{:S(2)}, u32[]{:S(2)}) collective-permute-start(bf16[64,640]{1,0:T(8,128)(2,1)S(1)} %get-tuple-element.65), channel_id=1, source_target_pairs={{0,8},{4,12},{8,0},{12,4},{1,9},{5,13},{9,1},{13,5},{2,10},{6,14},... | collective-permute-start | bytes 245768 | tf_op jit(solution)/shard_map/ppermute | solution.py:25
  7.7 5.8 %collective-permute-start = (bf16[64,640]{1,0:T(8,128)(2,1)S(1)}, bf16[64,640]{1,0:T(8,128)(2,1)S(1)}, u32[]{:S(2)}, u32[]{:S(2)}) collective-permute-start(bf16[64,640]{1,0:T(8,128)(2,1)S(1)} %get-tuple-element.65), channel_id=1, source_target_pairs={{0,4},{4,0},{8,12},{12,8},{1,5},{5,1},{9,13},{13,9},{2,6},{6,2},{1... | collective-permute-start | bytes 245768 | tf_op jit(solution)/shard_map/ppermute | solution.py:25
  8.4 8.0 %collective-permute-start.3 = (bf16[64,2048]{1,0:T(8,128)(2,1)S(1)}, bf16[64,2048]{1,0:T(8,128)(2,1)S(1)}, u32[]{:S(2)}, u32[]{:S(2)}) collective-permute-start(bf16[64,2048]{1,0:T(8,128)(2,1)S(1)} %get-tuple-element.67.first_ref), channel_id=1, source_target_pairs={{0,2},{1,3},{2,0},{3,1},{4,6},{5,7},{6,4},{7,5},{8,10},{9,11},{10,... | collective-permute-start | bytes 786440 | tf_op jit(solution)/shard_map/ppermute | solution.py:25
  10.0 13.7 %copy-start.2 = (bf16[512,2048]{1,0:T(8,128)(2,1)S(1)}, bf16[512,2048]{1,0:T(8,128)(2,1)}, u32[]{:S(2)}) copy-start(bf16[512,2048]{1,0:T(8,128)(2,1)} %refs_3_.1) | copy-start | bytes 6291460
  16.4 5.7 %collective-permute-start.6 = (bf16[256,384]{1,0:T(8,128)(2,1)S(1)}, bf16[256,384]{1,0:T(8,128)(2,1)S(1)}, u32[]{:S(2)}, u32[]{:S(2)}) collective-permute-start(bf16[256,384]{1,0:T(8,128)(2,1)S(1)} %pad_maximum_fusion.4), channel_id=1, source_target_pairs={{0,2},{1,3},{2,0},{3,1},{4,6},{5,7},{6,4},{7,5},{8,10},{9,11},{10,... | collective-permute-start | bytes 589832 | tf_op jit(solution)/shard_map/ppermute | solution.py:25
  17.9 4.3 %collective-permute-start.4 = (bf16[64,2048]{1,0:T(8,128)(2,1)S(1)}, bf16[64,2048]{1,0:T(8,128)(2,1)S(1)}, u32[]{:S(2)}, u32[]{:S(2)}) collective-permute-start(bf16[64,2048]{1,0:T(8,128)(2,1)S(1)} %get-tuple-element.67.first_ref), channel_id=1, source_target_pairs={{0,1},{1,0},{2,3},{3,2},{4,5},{5,4},{6,7},{7,6},{8,9},{9,8},{10,11... | collective-permute-start | bytes 786440 | tf_op jit(solution)/shard_map/ppermute | solution.py:25
  17.9 4.3 %collective-permute-start.5 = (bf16[64,2048]{1,0:T(8,128)(2,1)S(1)}, bf16[64,2048]{1,0:T(8,128)(2,1)S(1)}, u32[]{:S(2)}, u32[]{:S(2)}) collective-permute-start(bf16[64,2048]{1,0:T(8,128)(2,1)S(1)} %collective-permute-done.3.second_ref), channel_id=1, source_target_pairs={{0,1},{1,0},{2,3},{3,2},{4,5},{5,4},{6,7},{7,6},{8,9},{9,8},{10,11... | collective-permute-start | bytes 786440 | tf_op jit(solution)/shard_map/ppermute | solution.py:25
  22.1 1.6 %collective-permute-start.7 = (bf16[512,256]{1,0:T(8,128)(2,1)S(1)}, bf16[512,256]{1,0:T(8,128)(2,1)S(1)}, u32[]{:S(2)}, u32[]{:S(2)}) collective-permute-start(bf16[512,256]{1,0:T(8,128)(2,1)S(1)} %pad_maximum_fusion.2.refs_1_), channel_id=1, source_target_pairs={{0,1},{1,0},{2,3},{3,2},{4,5},{5,4},{6,7},{7,6},{8,9},{9,8},{10,11... | collective-permute-start | bytes 786440 | tf_op jit(solution)/shard_map/ppermute | solution.py:25
  22.3 7.0 %copy-start.3 = (bf16[1,768,2048]{2,1,0:T(8,128)(2,1)S(1)}, bf16[1,768,2048]{2,1,0:T(8,128)(2,1)}, u32[]{:S(2)}) copy-start(bf16[1,768,2048]{2,1,0:T(8,128)(2,1)} %param.23) | copy-start | bytes 9437188
  26.5 11.7 %copy-start.5 = (bf16[1,64,2048]{2,1,0:T(8,128)(2,1)S(1)}, bf16[1,64,2048]{2,1,0:T(8,128)(2,1)}, u32[]{:S(2)}) copy-start(bf16[1,64,2048]{2,1,0:T(8,128)(2,1)} %param.12) | copy-start | bytes 786436
  26.5 11.9 %copy-start.9 = (f32[2048]{0:T(1024)S(1)}, f32[2048]{0:T(1024)}, u32[]{:S(2)}) copy-start(f32[2048]{0:T(1024)} %param.19) | copy-start | bytes 24580
  26.5 2.7 %collective-permute-start.8 = (f32[128,2048]{1,0:T(8,128)S(1)}, f32[128,2048]{1,0:T(8,128)S(1)}, u32[]{:S(2)}, u32[]{:S(2)}) collective-permute-start(f32[128,2048]{1,0:T(8,128)S(1)} %get-tuple-element.70), channel_id=1, source_target_pairs={{0,1},{1,0},{2,3},{3,2},{4,5},{5,4},{6,7},{7,6},{8,9},{9,8},{10,11... | collective-permute-start | bytes 3145736 | tf_op jit(solution)/shard_map/ppermute | solution.py:25
  29.2 9.0 %collective-permute-start.11 = (bf16[768,2048]{1,0:T(8,128)(2,1)S(1)}, bf16[768,2048]{1,0:T(8,128)(2,1)S(1)}, u32[]{:S(2)}, u32[]{:S(2)}) collective-permute-start(bf16[768,2048]{1,0:T(8,128)(2,1)S(1)} %bitcast.56), channel_id=1, source_target_pairs={{0,1},{1,0},{2,3},{3,2},{4,5},{5,4},{6,7},{7,6},{8,9},{9,8},{10,11... | collective-permute-start | bytes 9437192 | tf_op jit(solution)/shard_map/ppermute | solution.py:25
  29.5 8.6 %collective-permute-start.9 = (bf16[64,2048]{1,0:T(8,128)(2,1)S(1)}, bf16[64,2048]{1,0:T(8,128)(2,1)S(1)}, u32[]{:S(2)}, u32[]{:S(2)}) collective-permute-start(bf16[64,2048]{1,0:T(8,128)(2,1)S(1)} %slice.145), channel_id=1, source_target_pairs={{0,2},{1,3},{2,0},{3,1},{4,6},{5,7},{6,4},{7,5},{8,10},{9,11},{10,... | collective-permute-start | bytes 786440 | tf_op jit(solution)/shard_map/ppermute | solution.py:25
  31.1 5.5 %collective-permute-start.10 = (bf16[2,256,128]{2,1,0:T(8,128)(2,1)S(1)}, bf16[2,256,128]{2,1,0:T(8,128)(2,1)S(1)}, u32[]{:S(2)}, u32[]{:S(2)}) collective-permute-start(bf16[2,256,128]{2,1,0:T(8,128)(2,1)S(1)} %pad_maximum_fusion.5), channel_id=1, source_target_pairs={{0,16},{16,0},{1,17},{17,1},{2,18},{18,2},{3,19},{19,3},{4,20},{20... | collective-permute-start | bytes 393224 | tf_op jit(solution)/shard_map/ppermute | solution.py:25
  38.2 16.6 %copy-start.7 = (bf16[64,2048]{1,0:T(8,128)(2,1)}, bf16[64,2048]{1,0:T(8,128)(2,1)S(1)}, u32[]{:S(2)}) copy-start(bf16[64,2048]{1,0:T(8,128)(2,1)S(1)} %collective-permute-done.9) | copy-start | bytes 786436
  38.2 16.6 %copy-start.4 = (bf16[768,2048]{1,0:T(8,128)(2,1)}, bf16[768,2048]{1,0:T(8,128)(2,1)S(1)}, u32[]{:S(2)}) copy-start(bf16[768,2048]{1,0:T(8,128)(2,1)S(1)} %collective-permute-done.11.refs_6_) | copy-start | bytes 9437188
  38.6 13.2 %collective-permute-start.17 = (bf16[64,2048]{1,0:T(8,128)(2,1)S(1)}, bf16[64,2048]{1,0:T(8,128)(2,1)S(1)}, u32[]{:S(2)}, u32[]{:S(2)}) collective-permute-start(bf16[64,2048]{1,0:T(8,128)(2,1)S(1)} %multiply_convert_fusion.refs_9_), channel_id=1, source_target_pairs={{0,4},{4,0},{8,12},{12,8},{1,5},{5,1},{9,13},{13,9},{2,6},{6,2},{1... | collective-permute-start | bytes 786440 | tf_op jit(solution)/shard_map/ppermute | solution.py:25
  40.0 14.7 %collective-permute-start.13 = (bf16[64,2048]{1,0:T(8,128)(2,1)S(1)}, bf16[64,2048]{1,0:T(8,128)(2,1)S(1)}, u32[]{:S(2)}, u32[]{:S(2)}) collective-permute-start(bf16[64,2048]{1,0:T(8,128)(2,1)S(1)} %multiply_convert_fusion.refs_9_), channel_id=1, source_target_pairs={{0,8},{4,12},{8,0},{12,4},{1,9},{5,13},{9,1},{13,5},{2,10},{6,14},... | collective-permute-start | bytes 786440 | tf_op jit(solution)/shard_map/ppermute | solution.py:25
  42.6 12.2 %collective-permute-start.16 = (bf16[64,2048]{1,0:T(8,128)(2,1)S(1)}, bf16[64,2048]{1,0:T(8,128)(2,1)S(1)}, u32[]{:S(2)}, u32[]{:S(2)}) collective-permute-start(bf16[64,2048]{1,0:T(8,128)(2,1)S(1)} %multiply_convert_fusion.refs_9_), channel_id=1, source_target_pairs={{0,16},{16,0},{1,17},{17,1},{2,18},{18,2},{3,19},{19,3},{4,20},{20... | collective-permute-start | bytes 786440 | tf_op jit(solution)/shard_map/ppermute | solution.py:25
  44.1 10.7 %collective-permute-start.15 = (bf16[64,2048]{1,0:T(8,128)(2,1)S(1)}, bf16[64,2048]{1,0:T(8,128)(2,1)S(1)}, u32[]{:S(2)}, u32[]{:S(2)}) collective-permute-start(bf16[64,2048]{1,0:T(8,128)(2,1)S(1)} %multiply_convert_fusion.refs_9_), channel_id=1, source_target_pairs={{0,2},{1,3},{2,0},{3,1},{4,6},{5,7},{6,4},{7,5},{8,10},{9,11},{10,... | collective-permute-start | bytes 786440 | tf_op jit(solution)/shard_map/ppermute | solution.py:25
  51.8 6.9 %collective-permute-start.19 = (bf16[64,2048]{1,0:T(8,128)(2,1)S(1)}, bf16[64,2048]{1,0:T(8,128)(2,1)S(1)}, u32[]{:S(2)}, u32[]{:S(2)}) collective-permute-start(bf16[64,2048]{1,0:T(8,128)(2,1)S(1)} %collective-permute-done.17.refs_10_), channel_id=1, source_target_pairs={{0,16},{16,0},{1,17},{17,1},{2,18},{18,2},{3,19},{19,3},{4,20},{20... | collective-permute-start | bytes 786440 | tf_op jit(solution)/shard_map/ppermute | solution.py:25
  53.2 6.6 %collective-permute-start.18 = (bf16[64,2048]{1,0:T(8,128)(2,1)S(1)}, bf16[64,2048]{1,0:T(8,128)(2,1)S(1)}, u32[]{:S(2)}, u32[]{:S(2)}) collective-permute-start(bf16[64,2048]{1,0:T(8,128)(2,1)S(1)} %collective-permute-done.17.refs_10_), channel_id=1, source_target_pairs={{0,2},{1,3},{2,0},{3,1},{4,6},{5,7},{6,4},{7,5},{8,10},{9,11},{10,... | collective-permute-start | bytes 786440 | tf_op jit(solution)/shard_map/ppermute | solution.py:25
  54.7 8.7 %collective-permute-start.14 = (bf16[64,2048]{1,0:T(8,128)(2,1)S(1)}, bf16[64,2048]{1,0:T(8,128)(2,1)S(1)}, u32[]{:S(2)}, u32[]{:S(2)}) collective-permute-start(bf16[64,2048]{1,0:T(8,128)(2,1)S(1)} %collective-permute-done.13.refs_11_), channel_id=1, source_target_pairs={{0,4},{4,0},{8,12},{12,8},{1,5},{5,1},{9,13},{13,9},{2,6},{6,2},{1... | collective-permute-start | bytes 786440 | tf_op jit(solution)/shard_map/ppermute | solution.py:25
  59.8 8.8 %collective-permute-start.22 = (bf16[64,2048]{1,0:T(8,128)(2,1)S(1)}, bf16[64,2048]{1,0:T(8,128)(2,1)S(1)}, u32[]{:S(2)}, u32[]{:S(2)}) collective-permute-start(bf16[64,2048]{1,0:T(8,128)(2,1)S(1)} %collective-permute-done.13.refs_11_), channel_id=1, source_target_pairs={{0,16},{16,0},{1,17},{17,1},{2,18},{18,2},{3,19},{19,3},{4,20},{20... | collective-permute-start | bytes 786440 | tf_op jit(solution)/shard_map/ppermute | solution.py:25
  60.4 8.9 %collective-permute-start.20 = (bf16[64,2048]{1,0:T(8,128)(2,1)S(1)}, bf16[64,2048]{1,0:T(8,128)(2,1)S(1)}, u32[]{:S(2)}, u32[]{:S(2)}) collective-permute-start(bf16[64,2048]{1,0:T(8,128)(2,1)S(1)} %collective-permute-done.13.refs_11_), channel_id=1, source_target_pairs={{0,2},{1,3},{2,0},{3,1},{4,6},{5,7},{6,4},{7,5},{8,10},{9,11},{10,... | collective-permute-start | bytes 786440 | tf_op jit(solution)/shard_map/ppermute | solution.py:25
  63.4 8.0 %collective-permute-start.23 = (bf16[64,2048]{1,0:T(8,128)(2,1)S(1)}, bf16[64,2048]{1,0:T(8,128)(2,1)S(1)}, u32[]{:S(2)}, u32[]{:S(2)}) collective-permute-start(bf16[64,2048]{1,0:T(8,128)(2,1)S(1)} %collective-permute-done.14.refs_12_), channel_id=1, source_target_pairs={{0,16},{16,0},{1,17},{17,1},{2,18},{18,2},{3,19},{19,3},{4,20},{20... | collective-permute-start | bytes 786440 | tf_op jit(solution)/shard_map/ppermute | solution.py:25
  65.0 7.4 %collective-permute-start.21 = (bf16[64,2048]{1,0:T(8,128)(2,1)S(1)}, bf16[64,2048]{1,0:T(8,128)(2,1)S(1)}, u32[]{:S(2)}, u32[]{:S(2)}) collective-permute-start(bf16[64,2048]{1,0:T(8,128)(2,1)S(1)} %collective-permute-done.14.refs_12_), channel_id=1, source_target_pairs={{0,2},{1,3},{2,0},{3,1},{4,6},{5,7},{6,4},{7,5},{8,10},{9,11},{10,... | collective-permute-start | bytes 786440 | tf_op jit(solution)/shard_map/ppermute | solution.py:25
  72.4 12.1 %collective-permute-start.24 = (bf16[256,1024]{1,0:T(8,128)(2,1)S(1)}, bf16[256,1024]{1,0:T(8,128)(2,1)S(1)}, u32[]{:S(2)}, u32[]{:S(2)}) collective-permute-start(bf16[256,1024]{1,0:T(8,128)(2,1)S(1)} %get-tuple-element.94), channel_id=1, source_target_pairs={{0,16},{16,0},{1,17},{17,1},{2,18},{18,2},{3,19},{19,3},{4,20},{20... | collective-permute-start | bytes 1572872 | tf_op jit(solution)/shard_map/ppermute | solution.py:25
  73.3 11.3 %collective-permute-start.25 = (bf16[256,1024]{1,0:T(8,128)(2,1)S(1)}, bf16[256,1024]{1,0:T(8,128)(2,1)S(1)}, u32[]{:S(2)}, u32[]{:S(2)}) collective-permute-start(bf16[256,1024]{1,0:T(8,128)(2,1)S(1)} %get-tuple-element.95), channel_id=1, source_target_pairs={{0,2},{1,3},{2,0},{3,1},{4,6},{5,7},{6,4},{7,5},{8,10},{9,11},{10,... | collective-permute-start | bytes 1572872 | tf_op jit(solution)/shard_map/ppermute | solution.py:25
  84.6 11.5 %collective-permute-start.26 = (bf16[256,1024]{1,0:T(8,128)(2,1)S(1)}, bf16[256,1024]{1,0:T(8,128)(2,1)S(1)}, u32[]{:S(2)}, u32[]{:S(2)}) collective-permute-start(bf16[256,1024]{1,0:T(8,128)(2,1)S(1)} %get-tuple-element.96), channel_id=1, source_target_pairs={{0,16},{16,0},{1,17},{17,1},{2,18},{18,2},{3,19},{19,3},{4,20},{20... | collective-permute-start | bytes 1572872 | tf_op jit(solution)/shard_map/ppermute | solution.py:25
  86.3 9.7 %collective-permute-start.27 = (bf16[256,1024]{1,0:T(8,128)(2,1)S(1)}, bf16[256,1024]{1,0:T(8,128)(2,1)S(1)}, u32[]{:S(2)}, u32[]{:S(2)}) collective-permute-start(bf16[256,1024]{1,0:T(8,128)(2,1)S(1)} %get-tuple-element.97), channel_id=1, source_target_pairs={{0,2},{1,3},{2,0},{3,1},{4,6},{5,7},{6,4},{7,5},{8,10},{9,11},{10,... | collective-permute-start | bytes 1572872 | tf_op jit(solution)/shard_map/ppermute | solution.py:25
  96.1 9.3 %collective-permute-start.28 = (bf16[128,1024]{1,0:T(8,128)(2,1)S(1)}, bf16[128,1024]{1,0:T(8,128)(2,1)S(1)}, u32[]{:S(2)}, u32[]{:S(2)}) collective-permute-start(bf16[128,1024]{1,0:T(8,128)(2,1)S(1)} %get-tuple-element.109), channel_id=1, source_target_pairs={{0,16},{16,0},{1,17},{17,1},{2,18},{18,2},{3,19},{19,3},{4,20},{20... | collective-permute-start | bytes 786440 | tf_op jit(solution)/shard_map/ppermute | solution.py:25
  96.9 10.0 %collective-permute-start.30 = (bf16[128,1024]{1,0:T(8,128)(2,1)S(1)}, bf16[128,1024]{1,0:T(8,128)(2,1)S(1)}, u32[]{:S(2)}, u32[]{:S(2)}) collective-permute-start(bf16[128,1024]{1,0:T(8,128)(2,1)S(1)} %get-tuple-element.111), channel_id=1, source_target_pairs={{0,2},{1,3},{2,0},{3,1},{4,6},{5,7},{6,4},{7,5},{8,10},{9,11},{10,... | collective-permute-start | bytes 786440 | tf_op jit(solution)/shard_map/ppermute | solution.py:25
  98.4 10.7 %collective-permute-start.32 = (bf16[128,1024]{1,0:T(8,128)(2,1)S(1)}, bf16[128,1024]{1,0:T(8,128)(2,1)S(1)}, u32[]{:S(2)}, u32[]{:S(2)}) collective-permute-start(bf16[128,1024]{1,0:T(8,128)(2,1)S(1)} %get-tuple-element.112), channel_id=1, source_target_pairs={{0,16},{16,0},{1,17},{17,1},{2,18},{18,2},{3,19},{19,3},{4,20},{20... | collective-permute-start | bytes 786440 | tf_op jit(solution)/shard_map/ppermute | solution.py:25
  100.2 9.4 %collective-permute-start.33 = (bf16[128,1024]{1,0:T(8,128)(2,1)S(1)}, bf16[128,1024]{1,0:T(8,128)(2,1)S(1)}, u32[]{:S(2)}, u32[]{:S(2)}) collective-permute-start(bf16[128,1024]{1,0:T(8,128)(2,1)S(1)} %get-tuple-element.113), channel_id=1, source_target_pairs={{0,2},{1,3},{2,0},{3,1},{4,6},{5,7},{6,4},{7,5},{8,10},{9,11},{10,... | collective-permute-start | bytes 786440 | tf_op jit(solution)/shard_map/ppermute | solution.py:25
  105.5 8.4 %collective-permute-start.29 = (bf16[128,1024]{1,0:T(8,128)(2,1)S(1)}, bf16[128,1024]{1,0:T(8,128)(2,1)S(1)}, u32[]{:S(2)}, u32[]{:S(2)}) collective-permute-start(bf16[128,1024]{1,0:T(8,128)(2,1)S(1)} %add_convert_fusion.3), channel_id=1, source_target_pairs={{0,2},{1,3},{2,0},{3,1},{4,6},{5,7},{6,4},{7,5},{8,10},{9,11},{10,... | collective-permute-start | bytes 786440 | tf_op jit(solution)/shard_map/ppermute | solution.py:25
  107.0 8.5 %collective-permute-start.31 = (bf16[128,1024]{1,0:T(8,128)(2,1)S(1)}, bf16[128,1024]{1,0:T(8,128)(2,1)S(1)}, u32[]{:S(2)}, u32[]{:S(2)}) collective-permute-start(bf16[128,1024]{1,0:T(8,128)(2,1)S(1)} %add_convert_fusion.2), channel_id=1, source_target_pairs={{0,16},{16,0},{1,17},{17,1},{2,18},{18,2},{3,19},{19,3},{4,20},{20... | collective-permute-start | bytes 786440 | tf_op jit(solution)/shard_map/ppermute | solution.py:25
  116.1 21.3 %copy-start.6 = (bf16[1,64,2048]{2,1,0:T(8,128)(2,1)S(1)}, bf16[1,64,2048]{2,1,0:T(8,128)(2,1)}, u32[]{:S(2)}) copy-start(bf16[1,64,2048]{2,1,0:T(8,128)(2,1)} %param.12) | copy-start | bytes 786436
  116.1 21.3 %copy-start.8 = (bf16[64,2048]{1,0:T(8,128)(2,1)S(1)}, bf16[64,2048]{1,0:T(8,128)(2,1)}, u32[]{:S(2)}) copy-start(bf16[64,2048]{1,0:T(8,128)(2,1)} %copy-done.7) | copy-start | bytes 786436
  116.1 10.2 %collective-permute-start.37 = (bf16[64,2048]{1,0:T(8,128)(2,1)S(1)}, bf16[64,2048]{1,0:T(8,128)(2,1)S(1)}, u32[]{:S(2)}, u32[]{:S(2)}) collective-permute-start(bf16[64,2048]{1,0:T(8,128)(2,1)S(1)} %fusion.9), channel_id=1, source_target_pairs={{0,4},{4,0},{8,12},{12,8},{1,5},{5,1},{9,13},{13,9},{2,6},{6,2},{1... | collective-permute-start | bytes 786440 | tf_op jit(solution)/shard_map/ppermute | solution.py:25
  116.2 12.3 %collective-permute-start.34 = (bf16[128,1024]{1,0:T(8,128)(2,1)S(1)}, bf16[128,1024]{1,0:T(8,128)(2,1)S(1)}, u32[]{:S(2)}, u32[]{:S(2)}) collective-permute-start(bf16[128,1024]{1,0:T(8,128)(2,1)S(1)} %get-tuple-element.120), channel_id=1, source_target_pairs={{0,2},{1,3},{2,0},{3,1},{4,6},{5,7},{6,4},{7,5},{8,10},{9,11},{10,... | collective-permute-start | bytes 786440 | tf_op jit(solution)/shard_map/ppermute | solution.py:25
  116.6 12.1 %collective-permute-start.35 = (bf16[128,1024]{1,0:T(8,128)(2,1)S(1)}, bf16[128,1024]{1,0:T(8,128)(2,1)S(1)}, u32[]{:S(2)}, u32[]{:S(2)}) collective-permute-start(bf16[128,1024]{1,0:T(8,128)(2,1)S(1)} %get-tuple-element.121), channel_id=1, source_target_pairs={{0,16},{16,0},{1,17},{17,1},{2,18},{18,2},{3,19},{19,3},{4,20},{20... | collective-permute-start | bytes 786440 | tf_op jit(solution)/shard_map/ppermute | solution.py:25
  126.4 10.3 %collective-permute-start.38 = (bf16[64,2048]{1,0:T(8,128)(2,1)S(1)}, bf16[64,2048]{1,0:T(8,128)(2,1)S(1)}, u32[]{:S(2)}, u32[]{:S(2)}) collective-permute-start(bf16[64,2048]{1,0:T(8,128)(2,1)S(1)} %fusion.1), channel_id=1, source_target_pairs={{0,8},{4,12},{8,0},{12,4},{1,9},{5,13},{9,1},{13,5},{2,10},{6,14},... | collective-permute-start | bytes 786440 | tf_op jit(solution)/shard_map/ppermute | solution.py:25
  128.9 8.5 %collective-permute-start.36 = (bf16[64,2048]{1,0:T(8,128)(2,1)S(1)}, bf16[64,2048]{1,0:T(8,128)(2,1)S(1)}, u32[]{:S(2)}, u32[]{:S(2)}) collective-permute-start(bf16[64,2048]{1,0:T(8,128)(2,1)S(1)} %fusion.8), channel_id=1, source_target_pairs={{0,4},{4,0},{8,12},{12,8},{1,5},{5,1},{9,13},{13,9},{2,6},{6,2},{1... | collective-permute-start | bytes 786440 | tf_op jit(solution)/shard_map/ppermute | solution.py:25

commit v14 on v13

--- a/solution.py
+++ b/solution.py
@@ -10,6 +10,7 @@
 ACROSS = 2
 TILE = 256
 LANES = 128
+WINDOW = 6
 
 
 def rms_rows(values_in, gain_vec):
@@ -379,11 +380,17 @@
                 )
         mine.append(pltpu.make_async_copy(dn_ref, dn_buf.at[expert], w_sem.at[expert, 2 * tiles]))
         weight_copies.append(mine)
+    waiting = [copy for mine in weight_copies for copy in mine]
+
+    def arrived(copy):
+        copy.wait()
+        if waiting:
+            waiting.pop(0).start()
+
     for _, copy in row_copies:
         copy.start()
-    for mine in weight_copies:
-        for copy in mine:
-            copy.start()
+    for _ in range(WINDOW):
+        waiting.pop(0).start()
 
     for group in range(groups):
         for where, copy in row_copies:
@@ -397,8 +404,8 @@
 
     for expert in range(2):
         for tile in range(tiles):
-            weight_copies[expert][2 * tile].wait()
-            weight_copies[expert][2 * tile + 1].wait()
+            arrived(weight_copies[expert][2 * tile])
+            arrived(weight_copies[expert][2 * tile + 1])
             gate = jnp.dot(
                 xs_buf[expert], gu_buf[expert, tile, 0], preferred_element_type=jnp.float32
             )
@@ -407,7 +414,7 @@
             )
             value = gate / (1.0 + jnp.exp(-gate)) * up
             hid_buf[:, tile * TILE : (tile + 1) * TILE] = value.astype(jnp.bfloat16)
-        weight_copies[expert][2 * tiles].wait()
+        arrived(weight_copies[expert][2 * tiles])
         for column in range(0, width, 2 * TILE):
             served_buf[expert, :, column : column + 2 * TILE] = jnp.dot(
                 hid_buf[...],

time: 138 us -> 139 us (level)
  no operation moved by 1% of the time
where the time goes in v14:
time: 139 us
  waiting for transfers between devices  64.9 us (47%)
  starting transfers between devices  43.1 us (31%)
  Pallas kernels  27.7 us (20%)
  other arithmetic  2.46 us (2%)
    ppermute x39, waiting for transfers between devices, swap(): return lax.ppermute(block, axis, [(i, i ^ bits) for i in range(size)])  64.9 us
    ppermute x39, starting transfers between devices, swap(): return lax.ppermute(block, axis, [(i, i ^ bits) for i in range(size)])  43.1 us
    pallas_call x2, Pallas kernels, run_experts(): pl.pallas_call(lambda *refs: expert_kernel(first, spots, cuts, *refs), ou...  19.8 us
  transfers between devices with their start and end apart: 39, of which 24 were waited for; matrix products, arithmetic and copies ran while one was open for 1% of the time, Pallas kernels for 20%

profile of v14, /device:TPU:0, one launch (start us, length us, event | category | flops | bytes accessed | tf_op | source)
XLA Modules:
  0.0 138.8 jit_solution(17427333818858750771)
XLA Ops:
  0.0 0.5 collective-permute-start.12
  0.5 2.6 %prepare.1 = (bf16[64,2048]{1,0:T(8,128)(2,1)S(1)}, bf16[64,640]{1,0:T(8,128)(2,1)S(1)}) custom-call(bf16[64,2048]{1,0:T(8,128)(2,1)} %bitcast.57, f32[1,2048]{1,0:T(1,128)} %bitcast.62, bf16[2,2048,256]{2,1,0:T(8,128)(2,1)} %refs_2_.1, f32[1,128]{1,0:T(1,128)} %bitcast.65, s32[8,64]{1,0:T(8,128)} %bitcast.63, s32[8,64]{1,0:T(8,128)} %bitcast.64), custom_call_target="tpu_custom_call" | custom-call | flops 134217728 | bytes 2621440 | tf_op jit(solution)/shard_map/prepare/pallas_call | solution.py:187
  3.1 4.7 %collective-permute-start.2 = (bf16[64,640]{1,0:T(8,128)(2,1)S(1)}, bf16[64,640]{1,0:T(8,128)(2,1)S(1)}, u32[]{:S(2)}, u32[]{:S(2)}) collective-permute-start(bf16[64,640]{1,0:T(8,128)(2,1)S(1)} %get-tuple-element.65), channel_id=1, source_target_pairs={{0,12},{4,8},{8,4},{12,0},{1,13},{5,9},{9,5},{13,1},{2,14},{6,10},... | collective-permute-start | bytes 245768 | tf_op jit(solution)/shard_map/ppermute | solution.py:26
  7.7 0.6 collective-permute-start
  8.4 1.7 %collective-permute-start.3 = (bf16[64,2048]{1,0:T(8,128)(2,1)S(1)}, bf16[64,2048]{1,0:T(8,128)(2,1)S(1)}, u32[]{:S(2)}, u32[]{:S(2)}) collective-permute-start(bf16[64,2048]{1,0:T(8,128)(2,1)S(1)} %get-tuple-element.67.first_ref), channel_id=1, source_target_pairs={{0,2},{1,3},{2,0},{3,1},{4,6},{5,7},{6,4},{7,5},{8,10},{9,11},{10,... | collective-permute-start | bytes 786440 | tf_op jit(solution)/shard_map/ppermute | solution.py:26
  10.0 3.5 %collective-permute-done = bf16[64,640]{1,0:T(8,128)(2,1)S(1)} collective-permute-done((bf16[64,640]{1,0:T(8,128)(2,1)S(1)}, bf16[64,640]{1,0:T(8,128)(2,1)S(1)}, u32[]{:S(2)}, u32[]{:S(2)}) %collective-permute-start) | collective-permute-done | bytes 81952 | tf_op jit(solution)/shard_map/ppermute | solution.py:26
  13.5 1.6 %collective-permute-done.1 = bf16[64,640]{1,0:T(8,128)(2,1)S(1)} collective-permute-done((bf16[64,640]{1,0:T(8,128)(2,1)S(1)}, bf16[64,640]{1,0:T(8,128)(2,1)S(1)}, u32[]{:S(2)}, u32[]{:S(2)}) %collective-permute-start.1) | collective-permute-done | bytes 81952 | tf_op jit(solution)/shard_map/ppermute | solution.py:26
  15.3 1.1 collective-permute-done.3.second_ref
  16.4 1.5 %collective-permute-start.6 = (bf16[256,384]{1,0:T(8,128)(2,1)S(1)}, bf16[256,384]{1,0:T(8,128)(2,1)S(1)}, u32[]{:S(2)}, u32[]{:S(2)}) collective-permute-start(bf16[256,384]{1,0:T(8,128)(2,1)S(1)} %pad_maximum_fusion.4), channel_id=1, source_target_pairs={{0,2},{1,3},{2,0},{3,1},{4,6},{5,7},{6,4},{7,5},{8,10},{9,11},{10,... | collective-permute-start | bytes 589832 | tf_op jit(solution)/shard_map/ppermute | solution.py:26
  17.9 0.5 collective-permute-start.5
  18.4 3.7 %collective-permute-done.6 = bf16[256,384]{1,0:T(8,128)(2,1)S(1)} collective-permute-done((bf16[256,384]{1,0:T(8,128)(2,1)S(1)}, bf16[256,384]{1,0:T(8,128)(2,1)S(1)}, u32[]{:S(2)}, u32[]{:S(2)}) %collective-permute-start.6) | collective-permute-done | bytes 196640 | tf_op jit(solution)/shard_map/ppermute | solution.py:26
  22.3 0.9 queries.1.refs_0_
  23.1 0.6 collective-permute-done.7.refs_2_
  23.7 2.7 %attend.1 = (f32[128,2048]{1,0:T(8,128)S(1)}, f32[128,2048]{1,0:T(8,128)S(1)}) custom-call(bf16[256,512]{1,0:T(8,128)(2,1)S(1)} %queries.1.refs_0_, bf16[512,256]{1,0:T(8,128)(2,1)S(1)} %pad_maximum_fusion.2.refs_1_, bf16[512,256]{1,0:T(8,128)(2,1)S(1)} %collective-permute-done.7.refs_2_, bf16[512,2048]{1,0:T(8,128)(2,1)S(1)} %copy-done.2), custom_call_target="tpu_custom_call" | custom-call | flops 1073741824 | bytes 4194304 | tf_op jit(solution)/shard_map/attend/pallas_call | solution.py:266
  26.5 0.2 collective-permute-start.8
  26.7 2.5 %collective-permute-done.8 = f32[128,2048]{1,0:T(8,128)S(1)} collective-permute-done((f32[128,2048]{1,0:T(8,128)S(1)}, f32[128,2048]{1,0:T(8,128)S(1)}, u32[]{:S(2)}, u32[]{:S(2)}) %collective-permute-start.8) | collective-permute-done | bytes 1048608 | tf_op jit(solution)/shard_map/ppermute | solution.py:26
  29.5 1.5 %collective-permute-start.9 = (bf16[64,2048]{1,0:T(8,128)(2,1)S(1)}, bf16[64,2048]{1,0:T(8,128)(2,1)S(1)}, u32[]{:S(2)}, u32[]{:S(2)}) collective-permute-start(bf16[64,2048]{1,0:T(8,128)(2,1)S(1)} %slice.145), channel_id=1, source_target_pairs={{0,2},{1,3},{2,0},{3,1},{4,6},{5,7},{6,4},{7,5},{8,10},{9,11},{10,... | collective-permute-start | bytes 786440 | tf_op jit(solution)/shard_map/ppermute | solution.py:26
  31.1 1.6 %collective-permute-start.10 = (bf16[2,256,128]{2,1,0:T(8,128)(2,1)S(1)}, bf16[2,256,128]{2,1,0:T(8,128)(2,1)S(1)}, u32[]{:S(2)}, u32[]{:S(2)}) collective-permute-start(bf16[2,256,128]{2,1,0:T(8,128)(2,1)S(1)} %pad_maximum_fusion.5), channel_id=1, source_target_pairs={{0,16},{16,0},{1,17},{17,1},{2,18},{18,2},{3,19},{19,3},{4,20},{20... | collective-permute-start | bytes 393224 | tf_op jit(solution)/shard_map/ppermute | solution.py:26
  32.6 4.0 %collective-permute-done.10 = bf16[2,256,128]{2,1,0:T(8,128)(2,1)S(1)} collective-permute-done((bf16[2,256,128]{2,1,0:T(8,128)(2,1)S(1)}, bf16[2,256,128]{2,1,0:T(8,128)(2,1)S(1)}, u32[]{:S(2)}, u32[]{:S(2)}) %collective-permute-start.10) | collective-permute-done | bytes 131104 | tf_op jit(solution)/shard_map/ppermute | solution.py:26
  36.7 1.5 %collective-permute-done.9 = bf16[64,2048]{1,0:T(8,128)(2,1)S(1)} collective-permute-done((bf16[64,2048]{1,0:T(8,128)(2,1)S(1)}, bf16[64,2048]{1,0:T(8,128)(2,1)S(1)}, u32[]{:S(2)}, u32[]{:S(2)}) %collective-permute-start.9) | collective-permute-done | bytes 262176 | tf_op jit(solution)/shard_map/ppermute | solution.py:26
  38.2 0.2 multiply_reduce_fusion
  38.6 1.5 %collective-permute-start.17 = (bf16[64,2048]{1,0:T(8,128)(2,1)S(1)}, bf16[64,2048]{1,0:T(8,128)(2,1)S(1)}, u32[]{:S(2)}, u32[]{:S(2)}) collective-permute-start(bf16[64,2048]{1,0:T(8,128)(2,1)S(1)} %multiply_convert_fusion.refs_9_), channel_id=1, source_target_pairs={{0,4},{4,0},{8,12},{12,8},{1,5},{5,1},{9,13},{13,9},{2,6},{6,2},{1... | collective-permute-start | bytes 786440 | tf_op jit(solution)/shard_map/ppermute | solution.py:26
  40.0 2.6 %collective-permute-start.13 = (bf16[64,2048]{1,0:T(8,128)(2,1)S(1)}, bf16[64,2048]{1,0:T(8,128)(2,1)S(1)}, u32[]{:S(2)}, u32[]{:S(2)}) collective-permute-start(bf16[64,2048]{1,0:T(8,128)(2,1)S(1)} %multiply_convert_fusion.refs_9_), channel_id=1, source_target_pairs={{0,8},{4,12},{8,0},{12,4},{1,9},{5,13},{9,1},{13,5},{2,10},{6,14},... | collective-permute-start | bytes 786440 | tf_op jit(solution)/shard_map/ppermute | solution.py:26
  42.6 1.5 %collective-permute-start.16 = (bf16[64,2048]{1,0:T(8,128)(2,1)S(1)}, bf16[64,2048]{1,0:T(8,128)(2,1)S(1)}, u32[]{:S(2)}, u32[]{:S(2)}) collective-permute-start(bf16[64,2048]{1,0:T(8,128)(2,1)S(1)} %multiply_convert_fusion.refs_9_), channel_id=1, source_target_pairs={{0,16},{16,0},{1,17},{17,1},{2,18},{18,2},{3,19},{19,3},{4,20},{20... | collective-permute-start | bytes 786440 | tf_op jit(solution)/shard_map/ppermute | solution.py:26
  44.1 1.5 %collective-permute-start.15 = (bf16[64,2048]{1,0:T(8,128)(2,1)S(1)}, bf16[64,2048]{1,0:T(8,128)(2,1)S(1)}, u32[]{:S(2)}, u32[]{:S(2)}) collective-permute-start(bf16[64,2048]{1,0:T(8,128)(2,1)S(1)} %multiply_convert_fusion.refs_9_), channel_id=1, source_target_pairs={{0,2},{1,3},{2,0},{3,1},{4,6},{5,7},{6,4},{7,5},{8,10},{9,11},{10,... | collective-permute-start | bytes 786440 | tf_op jit(solution)/shard_map/ppermute | solution.py:26
  45.6 6.2 %collective-permute-done.17.refs_10_ = bf16[64,2048]{1,0:T(8,128)(2,1)S(1)} collective-permute-done((bf16[64,2048]{1,0:T(8,128)(2,1)S(1)}, bf16[64,2048]{1,0:T(8,128)(2,1)S(1)}, u32[]{:S(2)}, u32[]{:S(2)}) %collective-permute-start.17) | collective-permute-done | bytes 262176 | tf_op jit(solution)/shard_map/ppermute | solution.py:26
  51.8 1.4 %collective-permute-start.19 = (bf16[64,2048]{1,0:T(8,128)(2,1)S(1)}, bf16[64,2048]{1,0:T(8,128)(2,1)S(1)}, u32[]{:S(2)}, u32[]{:S(2)}) collective-permute-start(bf16[64,2048]{1,0:T(8,128)(2,1)S(1)} %collective-permute-done.17.refs_10_), channel_id=1, source_target_pairs={{0,16},{16,0},{1,17},{17,1},{2,18},{18,2},{3,19},{19,3},{4,20},{20... | collective-permute-start | bytes 786440 | tf_op jit(solution)/shard_map/ppermute | solution.py:26
  53.2 1.5 %collective-permute-start.18 = (bf16[64,2048]{1,0:T(8,128)(2,1)S(1)}, bf16[64,2048]{1,0:T(8,128)(2,1)S(1)}, u32[]{:S(2)}, u32[]{:S(2)}) collective-permute-start(bf16[64,2048]{1,0:T(8,128)(2,1)S(1)} %collective-permute-done.17.refs_10_), channel_id=1, source_target_pairs={{0,2},{1,3},{2,0},{3,1},{4,6},{5,7},{6,4},{7,5},{8,10},{9,11},{10,... | collective-permute-start | bytes 786440 | tf_op jit(solution)/shard_map/ppermute | solution.py:26
  54.8 3.8 %collective-permute-done.19.refs_12_.refs_5_ = bf16[64,2048]{1,0:T(8,128)(2,1)S(1)} collective-permute-done((bf16[64,2048]{1,0:T(8,128)(2,1)S(1)}, bf16[64,2048]{1,0:T(8,128)(2,1)S(1)}, u32[]{:S(2)}, u32[]{:S(2)}) %collective-permute-start.19) | collective-permute-done | bytes 262176 | tf_op jit(solution)/shard_map/ppermute | solution.py:26
  58.6 1.2 collective-permute-done.18.refs_8_.refs_1_
  59.8 0.6 collective-permute-start.22
  60.4 1.5 %collective-permute-start.20 = (bf16[64,2048]{1,0:T(8,128)(2,1)S(1)}, bf16[64,2048]{1,0:T(8,128)(2,1)S(1)}, u32[]{:S(2)}, u32[]{:S(2)}) collective-permute-start(bf16[64,2048]{1,0:T(8,128)(2,1)S(1)} %collective-permute-done.13.refs_11_), channel_id=1, source_target_pairs={{0,2},{1,3},{2,0},{3,1},{4,6},{5,7},{6,4},{7,5},{8,10},{9,11},{10,... | collective-permute-start | bytes 786440 | tf_op jit(solution)/shard_map/ppermute | solution.py:26
  61.8 1.6 %tables.1 = (bf16[4,224,256]{2,1,0:T(8,128)(2,1)S(1)}, bf16[2,4,256,112]{3,2,1,0:T(8,128)(2,1)S(1)}, f32[4,256,2]{2,1,0:T(8,128)S(1)}) custom-call(s32[1]{0:T(128)} %bitcast.12.refs_0_, bf16[4,256,128]{2,1,0:T(8,128)(2,1)S(1)} %pad_maximum_fusion.3.refs_1_), custom_call_target="tpu_custom_call" | custom-call | flops 134217728 | bytes 917504 | tf_op jit(solution)/shard_map/tables/pallas_call | solution.py:329
  63.4 1.5 %collective-permute-start.23 = (bf16[64,2048]{1,0:T(8,128)(2,1)S(1)}, bf16[64,2048]{1,0:T(8,128)(2,1)S(1)}, u32[]{:S(2)}, u32[]{:S(2)}) collective-permute-start(bf16[64,2048]{1,0:T(8,128)(2,1)S(1)} %collective-permute-done.14.refs_12_), channel_id=1, source_target_pairs={{0,16},{16,0},{1,17},{17,1},{2,18},{18,2},{3,19},{19,3},{4,20},{20... | collective-permute-start | bytes 786440 | tf_op jit(solution)/shard_map/ppermute | solution.py:26
  65.0 0.5 collective-permute-start.21
  65.5 3.1 %collective-permute-done.22.refs_13_.refs_6_ = bf16[64,2048]{1,0:T(8,128)(2,1)S(1)} collective-permute-done((bf16[64,2048]{1,0:T(8,128)(2,1)S(1)}, bf16[64,2048]{1,0:T(8,128)(2,1)S(1)}, u32[]{:S(2)}, u32[]{:S(2)}) %collective-permute-start.22) | collective-permute-done | bytes 262176 | tf_op jit(solution)/shard_map/ppermute | solution.py:26
  68.6 0.7 collective-permute-done.20.refs_9_.refs_2_
  69.3 2.1 %collective-permute-done.23.refs_14_.refs_7_ = bf16[64,2048]{1,0:T(8,128)(2,1)S(1)} collective-permute-done((bf16[64,2048]{1,0:T(8,128)(2,1)S(1)}, bf16[64,2048]{1,0:T(8,128)(2,1)S(1)}, u32[]{:S(2)}, u32[]{:S(2)}) %collective-permute-start.23) | collective-permute-done | bytes 262176 | tf_op jit(solution)/shard_map/ppermute | solution.py:26
  71.4 0.9 collective-permute-done.21.refs_10_.refs_3_
  72.4 0.9 collective-permute-start.24
  73.3 1.1 collective-permute-start.25
  74.5 9.8 %experts.2 = (bf16[256,1024]{1,0:T(8,128)(2,1)S(1)}, bf16[256,1024]{1,0:T(8,128)(2,1)S(1)}, bf16[256,1024]{1,0:T(8,128)(2,1)S(1)}, bf16[256,1024]{1,0:T(8,128)(2,1)S(1)}) custom-call(bf16[4,224,256]{2,1,0:T(8,128)(2,1)S(1)} %get-tuple-element.79.refs_0_, bf16[2,4,256,112]{3,2,1,0:T(8,128)(2,1)S(1)} %get-tuple-element.80.refs_1_, ...), custom_call_target="tpu_custom_call" | custom-call | flops 4227858432 | bytes 23068672 | tf_op jit(solution)/shard_map/experts/pallas_call | solution.py:465
  84.3 0.3 collective-permute-done.24.refs_7_
  84.6 1.7 %collective-permute-start.26 = (bf16[256,1024]{1,0:T(8,128)(2,1)S(1)}, bf16[256,1024]{1,0:T(8,128)(2,1)S(1)}, u32[]{:S(2)}, u32[]{:S(2)}) collective-permute-start(bf16[256,1024]{1,0:T(8,128)(2,1)S(1)} %get-tuple-element.96), channel_id=1, source_target_pairs={{0,16},{16,0},{1,17},{17,1},{2,18},{18,2},{3,19},{19,3},{4,20},{20... | collective-permute-start | bytes 1572872 | tf_op jit(solution)/shard_map/ppermute | solution.py:26
  86.5 10.0 %experts.3 = (bf16[128,1024]{1,0:T(8,128)(2,1)S(1)}, bf16[128,1024]{1,0:T(8,128)(2,1)S(1)}, bf16[128,1024]{1,0:T(8,128)(2,1)S(1)}, bf16[128,1024]{1,0:T(8,128)(2...) custom-call(bf16[4,224,256]{2,1,0:T(8,128)(2,1)S(1)} %get-tuple-element.79.refs_0_, ...), custom_call_target="tpu_custom_call" | custom-call | flops 4227858432 | bytes 23068672 | tf_op jit(solution)/shard_map/experts/pallas_call | solution.py:465
  96.5 0.9 collective-permute-start.28
  97.4 1.4 collective-permute-start.30
  98.8 1.7 %collective-permute-start.32 = (bf16[128,1024]{1,0:T(8,128)(2,1)S(1)}, bf16[128,1024]{1,0:T(8,128)(2,1)S(1)}, u32[]{:S(2)}, u32[]{:S(2)}) collective-permute-start(bf16[128,1024]{1,0:T(8,128)(2,1)S(1)} %get-tuple-element.112), channel_id=1, source_target_pairs={{0,16},{16,0},{1,17},{17,1},{2,18},{18,2},{3,19},{19,3},{4,20},{20... | collective-permute-start | bytes 786440 | tf_op jit(solution)/shard_map/ppermute | solution.py:26
  100.6 5.2 %collective-permute-done.28 = bf16[128,1024]{1,0:T(8,128)(2,1)S(1)} collective-permute-done((bf16[128,1024]{1,0:T(8,128)(2,1)S(1)}, bf16[128,1024]{1,0:T(8,128)(2,1)S(1)}, u32[]{:S(2)}, u32[]{:S(2)}) %collective-permute-start.28) | collective-permute-done | bytes 262176 | tf_op jit(solution)/shard_map/ppermute | solution.py:26
  105.9 1.2 collective-permute-start.29
  107.1 1.2 collective-permute-start.31
  108.3 1.3 collective-permute-done.32
  109.7 4.0 %collective-permute-done.29 = bf16[128,1024]{1,0:T(8,128)(2,1)S(1)} collective-permute-done((bf16[128,1024]{1,0:T(8,128)(2,1)S(1)}, bf16[128,1024]{1,0:T(8,128)(2,1)S(1)}, u32[]{:S(2)}, u32[]{:S(2)}) %collective-permute-start.29) | collective-permute-done | bytes 262176 | tf_op jit(solution)/shard_map/ppermute | solution.py:26
  113.7 1.8 %collective-permute-done.31 = bf16[128,1024]{1,0:T(8,128)(2,1)S(1)} collective-permute-done((bf16[128,1024]{1,0:T(8,128)(2,1)S(1)}, bf16[128,1024]{1,0:T(8,128)(2,1)S(1)}, u32[]{:S(2)}, u32[]{:S(2)}) %collective-permute-start.31) | collective-permute-done | bytes 262176 | tf_op jit(solution)/shard_map/ppermute | solution.py:26
  115.5 0.2 add_convert_fusion
  115.7 0.3 convert_add_fusion.2
  116.2 0.5 collective-permute-start.34
  116.7 0.8 collective-permute-start.35
  117.5 9.3 %collective-permute-done.37 = bf16[64,2048]{1,0:T(8,128)(2,1)S(1)} collective-permute-done((bf16[64,2048]{1,0:T(8,128)(2,1)S(1)}, bf16[64,2048]{1,0:T(8,128)(2,1)S(1)}, u32[]{:S(2)}, u32[]{:S(2)}) %collective-permute-start.37) | collective-permute-done | bytes 262176 | tf_op jit(solution)/shard_map/ppermute | solution.py:26
  126.8 1.7 %collective-permute-start.38 = (bf16[64,2048]{1,0:T(8,128)(2,1)S(1)}, bf16[64,2048]{1,0:T(8,128)(2,1)S(1)}, u32[]{:S(2)}, u32[]{:S(2)}) collective-permute-start(bf16[64,2048]{1,0:T(8,128)(2,1)S(1)} %fusion.1), channel_id=1, source_target_pairs={{0,8},{4,12},{8,0},{12,4},{1,9},{5,13},{9,1},{13,5},{2,10},{6,14},... | collective-permute-start | bytes 786440 | tf_op jit(solution)/shard_map/ppermute | solution.py:26
  128.9 2.5 %collective-permute-start.36 = (bf16[64,2048]{1,0:T(8,128)(2,1)S(1)}, bf16[64,2048]{1,0:T(8,128)(2,1)S(1)}, u32[]{:S(2)}, u32[]{:S(2)}) collective-permute-start(bf16[64,2048]{1,0:T(8,128)(2,1)S(1)} %fusion.8), channel_id=1, source_target_pairs={{0,4},{4,0},{8,12},{12,8},{1,5},{5,1},{9,13},{13,9},{2,6},{6,2},{1... | collective-permute-start | bytes 786440 | tf_op jit(solution)/shard_map/ppermute | solution.py:26
  131.5 5.6 %collective-permute-done.38 = bf16[64,2048]{1,0:T(8,128)(2,1)S(1)} collective-permute-done((bf16[64,2048]{1,0:T(8,128)(2,1)S(1)}, bf16[64,2048]{1,0:T(8,128)(2,1)S(1)}, u32[]{:S(2)}, u32[]{:S(2)}) %collective-permute-start.38) | collective-permute-done | bytes 262176 | tf_op jit(solution)/shard_map/ppermute | solution.py:26
  137.1 0.8 collective-permute-done.36
  137.9 0.9 fusion.7
  (69 shorter events, 2.0 us)
Async XLA Ops:
  0.0 22.2 %copy-start.1 = (f32[128]{0:T(128)S(1)}, f32[128]{0:T(128)}, u32[]{:S(2)}) copy-start(f32[128]{0:T(128)} %param.16) | copy-start | bytes 1540
  0.0 22.2 %copy-start = (bf16[2048,512]{1,0:T(8,128)(2,1)S(1)}, bf16[2048,512]{1,0:T(8,128)(2,1)}, u32[]{:S(2)}) copy-start(bf16[2048,512]{1,0:T(8,128)(2,1)} %weight_ref.1) | copy-start | bytes 6291460
  0.0 38.2 %collective-permute-start.12 = (bf16[2048,1536]{1,0:T(8,128)(2,1)}, bf16[2048,1536]{1,0:T(8,128)(2,1)}, u32[]{:S(2)}, u32[]{:S(2)}) collective-permute-start(bf16[2048,1536]{1,0:T(8,128)(2,1)} %bitcast.51), channel_id=1, source_target_pairs={{0,1},{1,0},{2,3},{3,2},{4,5},{5,4},{6,7},{7,6},{8,9},{9,8},{10,11... | collective-permute-start | bytes 18874376 | tf_op jit(solution)/shard_map/ppermute | solution.py:26
  3.1 12.0 %collective-permute-start.2 = (bf16[64,640]{1,0:T(8,128)(2,1)S(1)}, bf16[64,640]{1,0:T(8,128)(2,1)S(1)}, u32[]{:S(2)}, u32[]{:S(2)}) collective-permute-start(bf16[64,640]{1,0:T(8,128)(2,1)S(1)} %get-tuple-element.65), channel_id=1, source_target_pairs={{0,12},{4,8},{8,4},{12,0},{1,13},{5,9},{9,5},{13,1},{2,14},{6,10},... | collective-permute-start | bytes 245768 | tf_op jit(solution)/shard_map/ppermute | solution.py:26
  7.7 7.4 %collective-permute-start.1 = (bf16[64,640]{1,0:T(8,128)(2,1)S(1)}, bf16[64,640]{1,0:T(8,128)(2,1)S(1)}, u32[]{:S(2)}, u32[]{:S(2)}) collective-permute-start(bf16[64,640]{1,0:T(8,128)(2,1)S(1)} %get-tuple-element.65), channel_id=1, source_target_pairs={{0,8},{4,12},{8,0},{12,4},{1,9},{5,13},{9,1},{13,5},{2,10},{6,14},... | collective-permute-start | bytes 245768 | tf_op jit(solution)/shard_map/ppermute | solution.py:26
  7.7 5.8 %collective-permute-start = (bf16[64,640]{1,0:T(8,128)(2,1)S(1)}, bf16[64,640]{1,0:T(8,128)(2,1)S(1)}, u32[]{:S(2)}, u32[]{:S(2)}) collective-permute-start(bf16[64,640]{1,0:T(8,128)(2,1)S(1)} %get-tuple-element.65), channel_id=1, source_target_pairs={{0,4},{4,0},{8,12},{12,8},{1,5},{5,1},{9,13},{13,9},{2,6},{6,2},{1... | collective-permute-start | bytes 245768 | tf_op jit(solution)/shard_map/ppermute | solution.py:26
  8.4 8.0 %collective-permute-start.3 = (bf16[64,2048]{1,0:T(8,128)(2,1)S(1)}, bf16[64,2048]{1,0:T(8,128)(2,1)S(1)}, u32[]{:S(2)}, u32[]{:S(2)}) collective-permute-start(bf16[64,2048]{1,0:T(8,128)(2,1)S(1)} %get-tuple-element.67.first_ref), channel_id=1, source_target_pairs={{0,2},{1,3},{2,0},{3,1},{4,6},{5,7},{6,4},{7,5},{8,10},{9,11},{10,... | collective-permute-start | bytes 786440 | tf_op jit(solution)/shard_map/ppermute | solution.py:26
  10.0 13.7 %copy-start.2 = (bf16[512,2048]{1,0:T(8,128)(2,1)S(1)}, bf16[512,2048]{1,0:T(8,128)(2,1)}, u32[]{:S(2)}) copy-start(bf16[512,2048]{1,0:T(8,128)(2,1)} %refs_3_.1) | copy-start | bytes 6291460
  16.4 5.7 %collective-permute-start.6 = (bf16[256,384]{1,0:T(8,128)(2,1)S(1)}, bf16[256,384]{1,0:T(8,128)(2,1)S(1)}, u32[]{:S(2)}, u32[]{:S(2)}) collective-permute-start(bf16[256,384]{1,0:T(8,128)(2,1)S(1)} %pad_maximum_fusion.4), channel_id=1, source_target_pairs={{0,2},{1,3},{2,0},{3,1},{4,6},{5,7},{6,4},{7,5},{8,10},{9,11},{10,... | collective-permute-start | bytes 589832 | tf_op jit(solution)/shard_map/ppermute | solution.py:26
  17.9 4.3 %collective-permute-start.4 = (bf16[64,2048]{1,0:T(8,128)(2,1)S(1)}, bf16[64,2048]{1,0:T(8,128)(2,1)S(1)}, u32[]{:S(2)}, u32[]{:S(2)}) collective-permute-start(bf16[64,2048]{1,0:T(8,128)(2,1)S(1)} %get-tuple-element.67.first_ref), channel_id=1, source_target_pairs={{0,1},{1,0},{2,3},{3,2},{4,5},{5,4},{6,7},{7,6},{8,9},{9,8},{10,11... | collective-permute-start | bytes 786440 | tf_op jit(solution)/shard_map/ppermute | solution.py:26
  17.9 4.3 %collective-permute-start.5 = (bf16[64,2048]{1,0:T(8,128)(2,1)S(1)}, bf16[64,2048]{1,0:T(8,128)(2,1)S(1)}, u32[]{:S(2)}, u32[]{:S(2)}) collective-permute-start(bf16[64,2048]{1,0:T(8,128)(2,1)S(1)} %collective-permute-done.3.second_ref), channel_id=1, source_target_pairs={{0,1},{1,0},{2,3},{3,2},{4,5},{5,4},{6,7},{7,6},{8,9},{9,8},{10,11... | collective-permute-start | bytes 786440 | tf_op jit(solution)/shard_map/ppermute | solution.py:26
  22.1 1.6 %collective-permute-start.7 = (bf16[512,256]{1,0:T(8,128)(2,1)S(1)}, bf16[512,256]{1,0:T(8,128)(2,1)S(1)}, u32[]{:S(2)}, u32[]{:S(2)}) collective-permute-start(bf16[512,256]{1,0:T(8,128)(2,1)S(1)} %pad_maximum_fusion.2.refs_1_), channel_id=1, source_target_pairs={{0,1},{1,0},{2,3},{3,2},{4,5},{5,4},{6,7},{7,6},{8,9},{9,8},{10,11... | collective-permute-start | bytes 786440 | tf_op jit(solution)/shard_map/ppermute | solution.py:26
  22.3 7.0 %copy-start.3 = (bf16[1,768,2048]{2,1,0:T(8,128)(2,1)S(1)}, bf16[1,768,2048]{2,1,0:T(8,128)(2,1)}, u32[]{:S(2)}) copy-start(bf16[1,768,2048]{2,1,0:T(8,128)(2,1)} %param.23) | copy-start | bytes 9437188
  26.5 11.7 %copy-start.5 = (bf16[1,64,2048]{2,1,0:T(8,128)(2,1)S(1)}, bf16[1,64,2048]{2,1,0:T(8,128)(2,1)}, u32[]{:S(2)}) copy-start(bf16[1,64,2048]{2,1,0:T(8,128)(2,1)} %param.12) | copy-start | bytes 786436
  26.5 11.9 %copy-start.9 = (f32[2048]{0:T(1024)S(1)}, f32[2048]{0:T(1024)}, u32[]{:S(2)}) copy-start(f32[2048]{0:T(1024)} %param.19) | copy-start | bytes 24580
  26.5 2.7 %collective-permute-start.8 = (f32[128,2048]{1,0:T(8,128)S(1)}, f32[128,2048]{1,0:T(8,128)S(1)}, u32[]{:S(2)}, u32[]{:S(2)}) collective-permute-start(f32[128,2048]{1,0:T(8,128)S(1)} %get-tuple-element.70), channel_id=1, source_target_pairs={{0,1},{1,0},{2,3},{3,2},{4,5},{5,4},{6,7},{7,6},{8,9},{9,8},{10,11... | collective-permute-start | bytes 3145736 | tf_op jit(solution)/shard_map/ppermute | solution.py:26
  29.2 9.0 %collective-permute-start.11 = (bf16[768,2048]{1,0:T(8,128)(2,1)S(1)}, bf16[768,2048]{1,0:T(8,128)(2,1)S(1)}, u32[]{:S(2)}, u32[]{:S(2)}) collective-permute-start(bf16[768,2048]{1,0:T(8,128)(2,1)S(1)} %bitcast.56), channel_id=1, source_target_pairs={{0,1},{1,0},{2,3},{3,2},{4,5},{5,4},{6,7},{7,6},{8,9},{9,8},{10,11... | collective-permute-start | bytes 9437192 | tf_op jit(solution)/shard_map/ppermute | solution.py:26
  29.5 8.6 %collective-permute-start.9 = (bf16[64,2048]{1,0:T(8,128)(2,1)S(1)}, bf16[64,2048]{1,0:T(8,128)(2,1)S(1)}, u32[]{:S(2)}, u32[]{:S(2)}) collective-permute-start(bf16[64,2048]{1,0:T(8,128)(2,1)S(1)} %slice.145), channel_id=1, source_target_pairs={{0,2},{1,3},{2,0},{3,1},{4,6},{5,7},{6,4},{7,5},{8,10},{9,11},{10,... | collective-permute-start | bytes 786440 | tf_op jit(solution)/shard_map/ppermute | solution.py:26
  31.1 5.5 %collective-permute-start.10 = (bf16[2,256,128]{2,1,0:T(8,128)(2,1)S(1)}, bf16[2,256,128]{2,1,0:T(8,128)(2,1)S(1)}, u32[]{:S(2)}, u32[]{:S(2)}) collective-permute-start(bf16[2,256,128]{2,1,0:T(8,128)(2,1)S(1)} %pad_maximum_fusion.5), channel_id=1, source_target_pairs={{0,16},{16,0},{1,17},{17,1},{2,18},{18,2},{3,19},{19,3},{4,20},{20... | collective-permute-start | bytes 393224 | tf_op jit(solution)/shard_map/ppermute | solution.py:26
  38.2 16.6 %copy-start.7 = (bf16[64,2048]{1,0:T(8,128)(2,1)}, bf16[64,2048]{1,0:T(8,128)(2,1)S(1)}, u32[]{:S(2)}) copy-start(bf16[64,2048]{1,0:T(8,128)(2,1)S(1)} %collective-permute-done.9) | copy-start | bytes 786436
  38.2 16.6 %copy-start.4 = (bf16[768,2048]{1,0:T(8,128)(2,1)}, bf16[768,2048]{1,0:T(8,128)(2,1)S(1)}, u32[]{:S(2)}) copy-start(bf16[768,2048]{1,0:T(8,128)(2,1)S(1)} %collective-permute-done.11.refs_6_) | copy-start | bytes 9437188
  38.6 13.2 %collective-permute-start.17 = (bf16[64,2048]{1,0:T(8,128)(2,1)S(1)}, bf16[64,2048]{1,0:T(8,128)(2,1)S(1)}, u32[]{:S(2)}, u32[]{:S(2)}) collective-permute-start(bf16[64,2048]{1,0:T(8,128)(2,1)S(1)} %multiply_convert_fusion.refs_9_), channel_id=1, source_target_pairs={{0,4},{4,0},{8,12},{12,8},{1,5},{5,1},{9,13},{13,9},{2,6},{6,2},{1... | collective-permute-start | bytes 786440 | tf_op jit(solution)/shard_map/ppermute | solution.py:26
  40.0 14.7 %collective-permute-start.13 = (bf16[64,2048]{1,0:T(8,128)(2,1)S(1)}, bf16[64,2048]{1,0:T(8,128)(2,1)S(1)}, u32[]{:S(2)}, u32[]{:S(2)}) collective-permute-start(bf16[64,2048]{1,0:T(8,128)(2,1)S(1)} %multiply_convert_fusion.refs_9_), channel_id=1, source_target_pairs={{0,8},{4,12},{8,0},{12,4},{1,9},{5,13},{9,1},{13,5},{2,10},{6,14},... | collective-permute-start | bytes 786440 | tf_op jit(solution)/shard_map/ppermute | solution.py:26
  42.6 12.2 %collective-permute-start.16 = (bf16[64,2048]{1,0:T(8,128)(2,1)S(1)}, bf16[64,2048]{1,0:T(8,128)(2,1)S(1)}, u32[]{:S(2)}, u32[]{:S(2)}) collective-permute-start(bf16[64,2048]{1,0:T(8,128)(2,1)S(1)} %multiply_convert_fusion.refs_9_), channel_id=1, source_target_pairs={{0,16},{16,0},{1,17},{17,1},{2,18},{18,2},{3,19},{19,3},{4,20},{20... | collective-permute-start | bytes 786440 | tf_op jit(solution)/shard_map/ppermute | solution.py:26
  44.1 10.7 %collective-permute-start.15 = (bf16[64,2048]{1,0:T(8,128)(2,1)S(1)}, bf16[64,2048]{1,0:T(8,128)(2,1)S(1)}, u32[]{:S(2)}, u32[]{:S(2)}) collective-permute-start(bf16[64,2048]{1,0:T(8,128)(2,1)S(1)} %multiply_convert_fusion.refs_9_), channel_id=1, source_target_pairs={{0,2},{1,3},{2,0},{3,1},{4,6},{5,7},{6,4},{7,5},{8,10},{9,11},{10,... | collective-permute-start | bytes 786440 | tf_op jit(solution)/shard_map/ppermute | solution.py:26
  51.8 6.9 %collective-permute-start.19 = (bf16[64,2048]{1,0:T(8,128)(2,1)S(1)}, bf16[64,2048]{1,0:T(8,128)(2,1)S(1)}, u32[]{:S(2)}, u32[]{:S(2)}) collective-permute-start(bf16[64,2048]{1,0:T(8,128)(2,1)S(1)} %collective-permute-done.17.refs_10_), channel_id=1, source_target_pairs={{0,16},{16,0},{1,17},{17,1},{2,18},{18,2},{3,19},{19,3},{4,20},{20... | collective-permute-start | bytes 786440 | tf_op jit(solution)/shard_map/ppermute | solution.py:26
  53.2 6.6 %collective-permute-start.18 = (bf16[64,2048]{1,0:T(8,128)(2,1)S(1)}, bf16[64,2048]{1,0:T(8,128)(2,1)S(1)}, u32[]{:S(2)}, u32[]{:S(2)}) collective-permute-start(bf16[64,2048]{1,0:T(8,128)(2,1)S(1)} %collective-permute-done.17.refs_10_), channel_id=1, source_target_pairs={{0,2},{1,3},{2,0},{3,1},{4,6},{5,7},{6,4},{7,5},{8,10},{9,11},{10,... | collective-permute-start | bytes 786440 | tf_op jit(solution)/shard_map/ppermute | solution.py:26
  54.7 8.7 %collective-permute-start.14 = (bf16[64,2048]{1,0:T(8,128)(2,1)S(1)}, bf16[64,2048]{1,0:T(8,128)(2,1)S(1)}, u32[]{:S(2)}, u32[]{:S(2)}) collective-permute-start(bf16[64,2048]{1,0:T(8,128)(2,1)S(1)} %collective-permute-done.13.refs_11_), channel_id=1, source_target_pairs={{0,4},{4,0},{8,12},{12,8},{1,5},{5,1},{9,13},{13,9},{2,6},{6,2},{1... | collective-permute-start | bytes 786440 | tf_op jit(solution)/shard_map/ppermute | solution.py:26
  59.8 8.8 %collective-permute-start.22 = (bf16[64,2048]{1,0:T(8,128)(2,1)S(1)}, bf16[64,2048]{1,0:T(8,128)(2,1)S(1)}, u32[]{:S(2)}, u32[]{:S(2)}) collective-permute-start(bf16[64,2048]{1,0:T(8,128)(2,1)S(1)} %collective-permute-done.13.refs_11_), channel_id=1, source_target_pairs={{0,16},{16,0},{1,17},{17,1},{2,18},{18,2},{3,19},{19,3},{4,20},{20... | collective-permute-start | bytes 786440 | tf_op jit(solution)/shard_map/ppermute | solution.py:26
  60.4 8.9 %collective-permute-start.20 = (bf16[64,2048]{1,0:T(8,128)(2,1)S(1)}, bf16[64,2048]{1,0:T(8,128)(2,1)S(1)}, u32[]{:S(2)}, u32[]{:S(2)}) collective-permute-start(bf16[64,2048]{1,0:T(8,128)(2,1)S(1)} %collective-permute-done.13.refs_11_), channel_id=1, source_target_pairs={{0,2},{1,3},{2,0},{3,1},{4,6},{5,7},{6,4},{7,5},{8,10},{9,11},{10,... | collective-permute-start | bytes 786440 | tf_op jit(solution)/shard_map/ppermute | solution.py:26
  63.4 8.0 %collective-permute-start.23 = (bf16[64,2048]{1,0:T(8,128)(2,1)S(1)}, bf16[64,2048]{1,0:T(8,128)(2,1)S(1)}, u32[]{:S(2)}, u32[]{:S(2)}) collective-permute-start(bf16[64,2048]{1,0:T(8,128)(2,1)S(1)} %collective-permute-done.14.refs_12_), channel_id=1, source_target_pairs={{0,16},{16,0},{1,17},{17,1},{2,18},{18,2},{3,19},{19,3},{4,20},{20... | collective-permute-start | bytes 786440 | tf_op jit(solution)/shard_map/ppermute | solution.py:26
  65.0 7.4 %collective-permute-start.21 = (bf16[64,2048]{1,0:T(8,128)(2,1)S(1)}, bf16[64,2048]{1,0:T(8,128)(2,1)S(1)}, u32[]{:S(2)}, u32[]{:S(2)}) collective-permute-start(bf16[64,2048]{1,0:T(8,128)(2,1)S(1)} %collective-permute-done.14.refs_12_), channel_id=1, source_target_pairs={{0,2},{1,3},{2,0},{3,1},{4,6},{5,7},{6,4},{7,5},{8,10},{9,11},{10,... | collective-permute-start | bytes 786440 | tf_op jit(solution)/shard_map/ppermute | solution.py:26
  72.4 12.1 %collective-permute-start.24 = (bf16[256,1024]{1,0:T(8,128)(2,1)S(1)}, bf16[256,1024]{1,0:T(8,128)(2,1)S(1)}, u32[]{:S(2)}, u32[]{:S(2)}) collective-permute-start(bf16[256,1024]{1,0:T(8,128)(2,1)S(1)} %get-tuple-element.94), channel_id=1, source_target_pairs={{0,16},{16,0},{1,17},{17,1},{2,18},{18,2},{3,19},{19,3},{4,20},{20... | collective-permute-start | bytes 1572872 | tf_op jit(solution)/shard_map/ppermute | solution.py:26
  73.3 11.3 %collective-permute-start.25 = (bf16[256,1024]{1,0:T(8,128)(2,1)S(1)}, bf16[256,1024]{1,0:T(8,128)(2,1)S(1)}, u32[]{:S(2)}, u32[]{:S(2)}) collective-permute-start(bf16[256,1024]{1,0:T(8,128)(2,1)S(1)} %get-tuple-element.95), channel_id=1, source_target_pairs={{0,2},{1,3},{2,0},{3,1},{4,6},{5,7},{6,4},{7,5},{8,10},{9,11},{10,... | collective-permute-start | bytes 1572872 | tf_op jit(solution)/shard_map/ppermute | solution.py:26
  84.6 11.9 %collective-permute-start.26 = (bf16[256,1024]{1,0:T(8,128)(2,1)S(1)}, bf16[256,1024]{1,0:T(8,128)(2,1)S(1)}, u32[]{:S(2)}, u32[]{:S(2)}) collective-permute-start(bf16[256,1024]{1,0:T(8,128)(2,1)S(1)} %get-tuple-element.96), channel_id=1, source_target_pairs={{0,16},{16,0},{1,17},{17,1},{2,18},{18,2},{3,19},{19,3},{4,20},{20... | collective-permute-start | bytes 1572872 | tf_op jit(solution)/shard_map/ppermute | solution.py:26
  86.3 10.2 %collective-permute-start.27 = (bf16[256,1024]{1,0:T(8,128)(2,1)S(1)}, bf16[256,1024]{1,0:T(8,128)(2,1)S(1)}, u32[]{:S(2)}, u32[]{:S(2)}) collective-permute-start(bf16[256,1024]{1,0:T(8,128)(2,1)S(1)} %get-tuple-element.97), channel_id=1, source_target_pairs={{0,2},{1,3},{2,0},{3,1},{4,6},{5,7},{6,4},{7,5},{8,10},{9,11},{10,... | collective-permute-start | bytes 1572872 | tf_op jit(solution)/shard_map/ppermute | solution.py:26
  96.5 9.3 %collective-permute-start.28 = (bf16[128,1024]{1,0:T(8,128)(2,1)S(1)}, bf16[128,1024]{1,0:T(8,128)(2,1)S(1)}, u32[]{:S(2)}, u32[]{:S(2)}) collective-permute-start(bf16[128,1024]{1,0:T(8,128)(2,1)S(1)} %get-tuple-element.109), channel_id=1, source_target_pairs={{0,16},{16,0},{1,17},{17,1},{2,18},{18,2},{3,19},{19,3},{4,20},{20... | collective-permute-start | bytes 786440 | tf_op jit(solution)/shard_map/ppermute | solution.py:26
  97.4 9.7 %collective-permute-start.30 = (bf16[128,1024]{1,0:T(8,128)(2,1)S(1)}, bf16[128,1024]{1,0:T(8,128)(2,1)S(1)}, u32[]{:S(2)}, u32[]{:S(2)}) collective-permute-start(bf16[128,1024]{1,0:T(8,128)(2,1)S(1)} %get-tuple-element.111), channel_id=1, source_target_pairs={{0,2},{1,3},{2,0},{3,1},{4,6},{5,7},{6,4},{7,5},{8,10},{9,11},{10,... | collective-permute-start | bytes 786440 | tf_op jit(solution)/shard_map/ppermute | solution.py:26
  98.8 10.9 %collective-permute-start.32 = (bf16[128,1024]{1,0:T(8,128)(2,1)S(1)}, bf16[128,1024]{1,0:T(8,128)(2,1)S(1)}, u32[]{:S(2)}, u32[]{:S(2)}) collective-permute-start(bf16[128,1024]{1,0:T(8,128)(2,1)S(1)} %get-tuple-element.112), channel_id=1, source_target_pairs={{0,16},{16,0},{1,17},{17,1},{2,18},{18,2},{3,19},{19,3},{4,20},{20... | collective-permute-start | bytes 786440 | tf_op jit(solution)/shard_map/ppermute | solution.py:26
  100.5 9.2 %collective-permute-start.33 = (bf16[128,1024]{1,0:T(8,128)(2,1)S(1)}, bf16[128,1024]{1,0:T(8,128)(2,1)S(1)}, u32[]{:S(2)}, u32[]{:S(2)}) collective-permute-start(bf16[128,1024]{1,0:T(8,128)(2,1)S(1)} %get-tuple-element.113), channel_id=1, source_target_pairs={{0,2},{1,3},{2,0},{3,1},{4,6},{5,7},{6,4},{7,5},{8,10},{9,11},{10,... | collective-permute-start | bytes 786440 | tf_op jit(solution)/shard_map/ppermute | solution.py:26
  105.9 7.8 %collective-permute-start.29 = (bf16[128,1024]{1,0:T(8,128)(2,1)S(1)}, bf16[128,1024]{1,0:T(8,128)(2,1)S(1)}, u32[]{:S(2)}, u32[]{:S(2)}) collective-permute-start(bf16[128,1024]{1,0:T(8,128)(2,1)S(1)} %add_convert_fusion.3), channel_id=1, source_target_pairs={{0,2},{1,3},{2,0},{3,1},{4,6},{5,7},{6,4},{7,5},{8,10},{9,11},{10,... | collective-permute-start | bytes 786440 | tf_op jit(solution)/shard_map/ppermute | solution.py:26
  107.1 8.4 %collective-permute-start.31 = (bf16[128,1024]{1,0:T(8,128)(2,1)S(1)}, bf16[128,1024]{1,0:T(8,128)(2,1)S(1)}, u32[]{:S(2)}, u32[]{:S(2)}) collective-permute-start(bf16[128,1024]{1,0:T(8,128)(2,1)S(1)} %add_convert_fusion.2), channel_id=1, source_target_pairs={{0,16},{16,0},{1,17},{17,1},{2,18},{18,2},{3,19},{19,3},{4,20},{20... | collective-permute-start | bytes 786440 | tf_op jit(solution)/shard_map/ppermute | solution.py:26
  116.1 21.8 %copy-start.6 = (bf16[1,64,2048]{2,1,0:T(8,128)(2,1)S(1)}, bf16[1,64,2048]{2,1,0:T(8,128)(2,1)}, u32[]{:S(2)}) copy-start(bf16[1,64,2048]{2,1,0:T(8,128)(2,1)} %param.12) | copy-start | bytes 786436
  116.1 21.8 %copy-start.8 = (bf16[64,2048]{1,0:T(8,128)(2,1)S(1)}, bf16[64,2048]{1,0:T(8,128)(2,1)}, u32[]{:S(2)}) copy-start(bf16[64,2048]{1,0:T(8,128)(2,1)} %copy-done.7) | copy-start | bytes 786436
  116.1 10.7 %collective-permute-start.37 = (bf16[64,2048]{1,0:T(8,128)(2,1)S(1)}, bf16[64,2048]{1,0:T(8,128)(2,1)S(1)}, u32[]{:S(2)}, u32[]{:S(2)}) collective-permute-start(bf16[64,2048]{1,0:T(8,128)(2,1)S(1)} %fusion.9), channel_id=1, source_target_pairs={{0,4},{4,0},{8,12},{12,8},{1,5},{5,1},{9,13},{13,9},{2,6},{6,2},{1... | collective-permute-start | bytes 786440 | tf_op jit(solution)/shard_map/ppermute | solution.py:26
  116.2 12.4 %collective-permute-start.34 = (bf16[128,1024]{1,0:T(8,128)(2,1)S(1)}, bf16[128,1024]{1,0:T(8,128)(2,1)S(1)}, u32[]{:S(2)}, u32[]{:S(2)}) collective-permute-start(bf16[128,1024]{1,0:T(8,128)(2,1)S(1)} %get-tuple-element.120), channel_id=1, source_target_pairs={{0,2},{1,3},{2,0},{3,1},{4,6},{5,7},{6,4},{7,5},{8,10},{9,11},{10,... | collective-permute-start | bytes 786440 | tf_op jit(solution)/shard_map/ppermute | solution.py:26
  116.7 12.0 %collective-permute-start.35 = (bf16[128,1024]{1,0:T(8,128)(2,1)S(1)}, bf16[128,1024]{1,0:T(8,128)(2,1)S(1)}, u32[]{:S(2)}, u32[]{:S(2)}) collective-permute-start(bf16[128,1024]{1,0:T(8,128)(2,1)S(1)} %get-tuple-element.121), channel_id=1, source_target_pairs={{0,16},{16,0},{1,17},{17,1},{2,18},{18,2},{3,19},{19,3},{4,20},{20... | collective-permute-start | bytes 786440 | tf_op jit(solution)/shard_map/ppermute | solution.py:26
  126.8 10.3 %collective-permute-start.38 = (bf16[64,2048]{1,0:T(8,128)(2,1)S(1)}, bf16[64,2048]{1,0:T(8,128)(2,1)S(1)}, u32[]{:S(2)}, u32[]{:S(2)}) collective-permute-start(bf16[64,2048]{1,0:T(8,128)(2,1)S(1)} %fusion.1), channel_id=1, source_target_pairs={{0,8},{4,12},{8,0},{12,4},{1,9},{5,13},{9,1},{13,5},{2,10},{6,14},... | collective-permute-start | bytes 786440 | tf_op jit(solution)/shard_map/ppermute | solution.py:26
  128.9 9.0 %collective-permute-start.36 = (bf16[64,2048]{1,0:T(8,128)(2,1)S(1)}, bf16[64,2048]{1,0:T(8,128)(2,1)S(1)}, u32[]{:S(2)}, u32[]{:S(2)}) collective-permute-start(bf16[64,2048]{1,0:T(8,128)(2,1)S(1)} %fusion.8), channel_id=1, source_target_pairs={{0,4},{4,0},{8,12},{12,8},{1,5},{5,1},{9,13},{13,9},{2,6},{6,2},{1... | collective-permute-start | bytes 786440 | tf_op jit(solution)/shard_map/ppermute | solution.py:26

commit v15 on v13

--- a/solution.py
+++ b/solution.py
@@ -72,9 +72,10 @@
     middle = [blocks[place] for place in range(2, len(blocks) - 1)]
     middle = jnp.concatenate(middle, axis=0) if len(middle) > 1 else middle[0]
     parts = [own, blocks[1], middle, blocks[len(blocks) - 1]]
-    parts[2], coded, *early = ready(parts[2], coded, *both_ways(own), *both_ways(parts[1]))
-    parts[3], *tables = ready(parts[3], *tables_of(coded))
-    by_rep, by_role = zip(early[:2], early[2:], both_ways(parts[2]), both_ways(parts[3]))
+    parts[2], coded, *outer = ready(parts[2], coded, *both_ways(own))
+    parts[3], *early = ready(parts[3], *both_ways(parts[1]), *tables_of(coded))
+    by_rep, by_role = zip(outer, early[:2], both_ways(parts[2]), both_ways(parts[3]))
+    tables = early[2:]
     low, high = pack_corners(by_rep, by_role)
     corner_low, corner_high = swap(low, "role", 1), swap(high, "rep", ACROSS)
     starts = (0, rows, 2 * rows, 2 * rows + middle.shape[0])
@@ -255,16 +256,19 @@
         columns = slice(column, column + 2 * TILE)
         partial = jnp.dot(held_ref[...], weight_ref[:, columns], preferred_element_type=jnp.float32)
         kept_ref[:, columns] = partial[:cut]
-        leaving_ref[:, columns] = partial[cut:]
+        leaving_ref[:, columns] = partial[cut:].astype(jnp.bfloat16)
 
 
 def attend(queries, near_kv, far_kv, w_out, head_dim):
     rows, width = queries.shape
     keys = 2 * near_kv.shape[0]
-    half = jax.ShapeDtypeStruct((rows // 2, w_out.shape[1]), jnp.float32)
+    half = (rows // 2, w_out.shape[1])
     return pl.pallas_call(
         lambda *refs: attend_kernel(head_dim, *refs),
-        out_shape=[half, half],
+        out_shape=[
+            jax.ShapeDtypeStruct(half, jnp.float32),
+            jax.ShapeDtypeStruct(half, jnp.bfloat16),
+        ],
         scratch_shapes=[pltpu.VMEM((rows, width), jnp.bfloat16)],
         compiler_params=pltpu.CompilerParams(vmem_limit_bytes=12 * 1024 * 1024),
         cost_estimate=pl.CostEstimate(
@@ -543,7 +547,7 @@
     queries = make_queries([normed, across_rows, pair_rows, corner_rows], w_query, q_gain)
     kept, leaving = attend(queries, half_kv, pair_kv, w_out, head_dim)
     leaving, own_dn = ready(swap(leaving, "rep", PAIR), w_down[0])
-    halves = kept + leaving
+    halves = kept + leaving.astype(jnp.float32)
     far_dn, far_gu = swap(own_dn, "rep", PAIR), swap(w_gateup[0], "rep", PAIR)
     far_sum = halves[row_count:].astype(jnp.bfloat16)
     across_sum, coded, far_dn, far_gu = ready(

time: 138 us -> 136 us (0.986)
  waiting for transfers between devices: 64.8 us -> 59.3 us
  starting transfers between devices: 43.4 us -> 46.6 us
    ppermute x39, waiting for transfers between devices: 64.8 us -> 59.3 us  [swap(): return lax.ppermute(block, axis, [(i, i ^ bits) for i in range(size)])]
    ppermute x39, starting transfers between devices: 43.4 us -> 46.6 us  [swap(): return lax.ppermute(block, axis, [(i, i ^ bits) for i in range(size)])]
  transfers between devices with their start and end apart: 39 -> 39, of which waited for: 24 -> 23; matrix products, arithmetic and copies ran while one was open for 1% -> 1% of each run, Pallas kernels for 20% -> 20%
where the time goes in v15:
time: 136 us
  waiting for transfers between devices  59.3 us (44%)
  starting transfers between devices  46.6 us (34%)
  Pallas kernels  27 us (20%)
  other arithmetic  2.45 us (2%)
    ppermute x39, waiting for transfers between devices, swap(): return lax.ppermute(block, axis, [(i, i ^ bits) for i in range(size)])  59.3 us
    ppermute x39, starting transfers between devices, swap(): return lax.ppermute(block, axis, [(i, i ^ bits) for i in range(size)])  46.6 us
    pallas_call x2, Pallas kernels, run_experts(): pl.pallas_call(lambda *refs: expert_kernel(first, spots, cuts, *refs), ou...  19.2 us
    pallas_call x1, Pallas kernels, attend(): pl.pallas_call(lambda *refs: attend_kernel(head_dim, *refs), out_shape=[j...  2.72 us
  transfers between devices with their start and end apart: 39, of which 23 were waited for; matrix products, arithmetic and copies ran while one was open for 1% of the time, Pallas kernels for 20%

profile of v15, /device:TPU:0, one launch (start us, length us, event | category | flops | bytes accessed | tf_op | source)
XLA Modules:
  0.0 136.1 jit_solution(5016621861814847919)
XLA Ops:
  0.0 0.5 collective-permute-start.12
  0.5 2.6 %prepare.1 = (bf16[64,2048]{1,0:T(8,128)(2,1)S(1)}, bf16[64,640]{1,0:T(8,128)(2,1)S(1)}) custom-call(bf16[64,2048]{1,0:T(8,128)(2,1)} %bitcast.57, f32[1,2048]{1,0:T(1,128)} %bitcast.62, bf16[2,2048,256]{2,1,0:T(8,128)(2,1)} %refs_2_.1, f32[1,128]{1,0:T(1,128)} %bitcast.65, s32[8,64]{1,0:T(8,128)} %bitcast.63, s32[8,64]{1,0:T(8,128)} %bitcast.64), custom_call_target="tpu_custom_call" | custom-call | flops 134217728 | bytes 2621440 | tf_op jit(solution)/shard_map/prepare/pallas_call | solution.py:187
  3.1 4.7 %collective-permute-start.2 = (bf16[64,640]{1,0:T(8,128)(2,1)S(1)}, bf16[64,640]{1,0:T(8,128)(2,1)S(1)}, u32[]{:S(2)}, u32[]{:S(2)}) collective-permute-start(bf16[64,640]{1,0:T(8,128)(2,1)S(1)} %get-tuple-element.65), channel_id=1, source_target_pairs={{0,12},{4,8},{8,4},{12,0},{1,13},{5,9},{9,5},{13,1},{2,14},{6,10},... | collective-permute-start | bytes 245768 | tf_op jit(solution)/shard_map/ppermute | solution.py:25
  7.7 0.6 collective-permute-start
  8.4 1.7 %collective-permute-start.3 = (bf16[64,2048]{1,0:T(8,128)(2,1)S(1)}, bf16[64,2048]{1,0:T(8,128)(2,1)S(1)}, u32[]{:S(2)}, u32[]{:S(2)}) collective-permute-start(bf16[64,2048]{1,0:T(8,128)(2,1)S(1)} %get-tuple-element.67.first_ref), channel_id=1, source_target_pairs={{0,2},{1,3},{2,0},{3,1},{4,6},{5,7},{6,4},{7,5},{8,10},{9,11},{10,... | collective-permute-start | bytes 786440 | tf_op jit(solution)/shard_map/ppermute | solution.py:25
  10.0 3.5 %collective-permute-done = bf16[64,640]{1,0:T(8,128)(2,1)S(1)} collective-permute-done((bf16[64,640]{1,0:T(8,128)(2,1)S(1)}, bf16[64,640]{1,0:T(8,128)(2,1)S(1)}, u32[]{:S(2)}, u32[]{:S(2)}) %collective-permute-start) | collective-permute-done | bytes 81952 | tf_op jit(solution)/shard_map/ppermute | solution.py:25
  13.5 1.6 %collective-permute-done.1 = bf16[64,640]{1,0:T(8,128)(2,1)S(1)} collective-permute-done((bf16[64,640]{1,0:T(8,128)(2,1)S(1)}, bf16[64,640]{1,0:T(8,128)(2,1)S(1)}, u32[]{:S(2)}, u32[]{:S(2)}) %collective-permute-start.1) | collective-permute-done | bytes 81952 | tf_op jit(solution)/shard_map/ppermute | solution.py:25
  15.3 1.1 collective-permute-done.3.second_ref
  16.4 1.5 %collective-permute-start.6 = (bf16[256,384]{1,0:T(8,128)(2,1)S(1)}, bf16[256,384]{1,0:T(8,128)(2,1)S(1)}, u32[]{:S(2)}, u32[]{:S(2)}) collective-permute-start(bf16[256,384]{1,0:T(8,128)(2,1)S(1)} %pad_maximum_fusion.4), channel_id=1, source_target_pairs={{0,2},{1,3},{2,0},{3,1},{4,6},{5,7},{6,4},{7,5},{8,10},{9,11},{10,... | collective-permute-start | bytes 589832 | tf_op jit(solution)/shard_map/ppermute | solution.py:25
  17.9 0.5 collective-permute-start.5
  18.4 3.7 %collective-permute-done.6 = bf16[256,384]{1,0:T(8,128)(2,1)S(1)} collective-permute-done((bf16[256,384]{1,0:T(8,128)(2,1)S(1)}, bf16[256,384]{1,0:T(8,128)(2,1)S(1)}, u32[]{:S(2)}, u32[]{:S(2)}) %collective-permute-start.6) | collective-permute-done | bytes 196640 | tf_op jit(solution)/shard_map/ppermute | solution.py:25
  22.3 0.9 queries.1.refs_0_
  23.2 0.6 collective-permute-done.7.refs_2_
  23.7 2.7 %attend.1 = (f32[128,2048]{1,0:T(8,128)S(1)}, bf16[128,2048]{1,0:T(8,128)(2,1)S(1)}) custom-call(bf16[256,512]{1,0:T(8,128)(2,1)S(1)} %queries.1.refs_0_, bf16[512,256]{1,0:T(8,128)(2,1)S(1)} %pad_maximum_fusion.2.refs_1_, bf16[512,256]{1,0:T(8,128)(2,1)S(1)} %collective-permute-done.7.refs_2_, bf16[512,2048]{1,0:T(8,128)(2,1)S(1)} %copy-done.2), custom_call_target="tpu_custom_call" | custom-call | flops 1073741824 | bytes 4194304 | tf_op jit(solution)/shard_map/attend/pallas_call | solution.py:266
  26.5 0.2 collective-permute-start.8
  26.7 1.8 %collective-permute-done.8 = bf16[128,2048]{1,0:T(8,128)(2,1)S(1)} collective-permute-done((bf16[128,2048]{1,0:T(8,128)(2,1)S(1)}, bf16[128,2048]{1,0:T(8,128)(2,1)S(1)}, u32[]{:S(2)}, u32[]{:S(2)}) %collective-permute-start.8) | collective-permute-done | bytes 524320 | tf_op jit(solution)/shard_map/ppermute | solution.py:25
  28.8 1.5 %collective-permute-start.9 = (bf16[64,2048]{1,0:T(8,128)(2,1)S(1)}, bf16[64,2048]{1,0:T(8,128)(2,1)S(1)}, u32[]{:S(2)}, u32[]{:S(2)}) collective-permute-start(bf16[64,2048]{1,0:T(8,128)(2,1)S(1)} %slice.145), channel_id=1, source_target_pairs={{0,2},{1,3},{2,0},{3,1},{4,6},{5,7},{6,4},{7,5},{8,10},{9,11},{10,... | collective-permute-start | bytes 786440 | tf_op jit(solution)/shard_map/ppermute | solution.py:25
  30.3 1.6 %collective-permute-start.10 = (bf16[2,256,128]{2,1,0:T(8,128)(2,1)S(1)}, bf16[2,256,128]{2,1,0:T(8,128)(2,1)S(1)}, u32[]{:S(2)}, u32[]{:S(2)}) collective-permute-start(bf16[2,256,128]{2,1,0:T(8,128)(2,1)S(1)} %pad_maximum_fusion.5), channel_id=1, source_target_pairs={{0,16},{16,0},{1,17},{17,1},{2,18},{18,2},{3,19},{19,3},{4,20},{20... | collective-permute-start | bytes 393224 | tf_op jit(solution)/shard_map/ppermute | solution.py:25
  31.9 4.0 %collective-permute-done.10 = bf16[2,256,128]{2,1,0:T(8,128)(2,1)S(1)} collective-permute-done((bf16[2,256,128]{2,1,0:T(8,128)(2,1)S(1)}, bf16[2,256,128]{2,1,0:T(8,128)(2,1)S(1)}, u32[]{:S(2)}, u32[]{:S(2)}) %collective-permute-start.10) | collective-permute-done | bytes 131104 | tf_op jit(solution)/shard_map/ppermute | solution.py:25
  35.9 1.5 %collective-permute-done.9 = bf16[64,2048]{1,0:T(8,128)(2,1)S(1)} collective-permute-done((bf16[64,2048]{1,0:T(8,128)(2,1)S(1)}, bf16[64,2048]{1,0:T(8,128)(2,1)S(1)}, u32[]{:S(2)}, u32[]{:S(2)}) %collective-permute-start.9) | collective-permute-done | bytes 262176 | tf_op jit(solution)/shard_map/ppermute | solution.py:25
  37.4 0.2 multiply_reduce_fusion
  37.8 1.5 %collective-permute-start.15 = (bf16[64,2048]{1,0:T(8,128)(2,1)S(1)}, bf16[64,2048]{1,0:T(8,128)(2,1)S(1)}, u32[]{:S(2)}, u32[]{:S(2)}) collective-permute-start(bf16[64,2048]{1,0:T(8,128)(2,1)S(1)} %multiply_convert_fusion.refs_9_), channel_id=1, source_target_pairs={{0,4},{4,0},{8,12},{12,8},{1,5},{5,1},{9,13},{13,9},{2,6},{6,2},{1... | collective-permute-start | bytes 786440 | tf_op jit(solution)/shard_map/ppermute | solution.py:25
  39.2 2.6 %collective-permute-start.13 = (bf16[64,2048]{1,0:T(8,128)(2,1)S(1)}, bf16[64,2048]{1,0:T(8,128)(2,1)S(1)}, u32[]{:S(2)}, u32[]{:S(2)}) collective-permute-start(bf16[64,2048]{1,0:T(8,128)(2,1)S(1)} %multiply_convert_fusion.refs_9_), channel_id=1, source_target_pairs={{0,8},{4,12},{8,0},{12,4},{1,9},{5,13},{9,1},{13,5},{2,10},{6,14},... | collective-permute-start | bytes 786440 | tf_op jit(solution)/shard_map/ppermute | solution.py:25
  41.8 1.5 %collective-permute-start.19 = (bf16[64,2048]{1,0:T(8,128)(2,1)S(1)}, bf16[64,2048]{1,0:T(8,128)(2,1)S(1)}, u32[]{:S(2)}, u32[]{:S(2)}) collective-permute-start(bf16[64,2048]{1,0:T(8,128)(2,1)S(1)} %multiply_convert_fusion.refs_9_), channel_id=1, source_target_pairs={{0,16},{16,0},{1,17},{17,1},{2,18},{18,2},{3,19},{19,3},{4,20},{20... | collective-permute-start | bytes 786440 | tf_op jit(solution)/shard_map/ppermute | solution.py:25
  43.3 1.5 %collective-permute-start.18 = (bf16[64,2048]{1,0:T(8,128)(2,1)S(1)}, bf16[64,2048]{1,0:T(8,128)(2,1)S(1)}, u32[]{:S(2)}, u32[]{:S(2)}) collective-permute-start(bf16[64,2048]{1,0:T(8,128)(2,1)S(1)} %multiply_convert_fusion.refs_9_), channel_id=1, source_target_pairs={{0,2},{1,3},{2,0},{3,1},{4,6},{5,7},{6,4},{7,5},{8,10},{9,11},{10,... | collective-permute-start | bytes 786440 | tf_op jit(solution)/shard_map/ppermute | solution.py:25
  44.8 6.2 %collective-permute-done.15.refs_10_ = bf16[64,2048]{1,0:T(8,128)(2,1)S(1)} collective-permute-done((bf16[64,2048]{1,0:T(8,128)(2,1)S(1)}, bf16[64,2048]{1,0:T(8,128)(2,1)S(1)}, u32[]{:S(2)}, u32[]{:S(2)}) %collective-permute-start.15) | collective-permute-done | bytes 262176 | tf_op jit(solution)/shard_map/ppermute | solution.py:25
  51.0 1.4 %collective-permute-start.17 = (bf16[64,2048]{1,0:T(8,128)(2,1)S(1)}, bf16[64,2048]{1,0:T(8,128)(2,1)S(1)}, u32[]{:S(2)}, u32[]{:S(2)}) collective-permute-start(bf16[64,2048]{1,0:T(8,128)(2,1)S(1)} %collective-permute-done.15.refs_10_), channel_id=1, source_target_pairs={{0,16},{16,0},{1,17},{17,1},{2,18},{18,2},{3,19},{19,3},{4,20},{20... | collective-permute-start | bytes 786440 | tf_op jit(solution)/shard_map/ppermute | solution.py:25
  52.4 1.5 %collective-permute-start.16 = (bf16[64,2048]{1,0:T(8,128)(2,1)S(1)}, bf16[64,2048]{1,0:T(8,128)(2,1)S(1)}, u32[]{:S(2)}, u32[]{:S(2)}) collective-permute-start(bf16[64,2048]{1,0:T(8,128)(2,1)S(1)} %collective-permute-done.15.refs_10_), channel_id=1, source_target_pairs={{0,2},{1,3},{2,0},{3,1},{4,6},{5,7},{6,4},{7,5},{8,10},{9,11},{10,... | collective-permute-start | bytes 786440 | tf_op jit(solution)/shard_map/ppermute | solution.py:25
  54.1 1.1 collective-permute-start.22
  55.1 1.5 %collective-permute-start.20 = (bf16[64,2048]{1,0:T(8,128)(2,1)S(1)}, bf16[64,2048]{1,0:T(8,128)(2,1)S(1)}, u32[]{:S(2)}, u32[]{:S(2)}) collective-permute-start(bf16[64,2048]{1,0:T(8,128)(2,1)S(1)} %collective-permute-done.13.refs_11_), channel_id=1, source_target_pairs={{0,2},{1,3},{2,0},{3,1},{4,6},{5,7},{6,4},{7,5},{8,10},{9,11},{10,... | collective-permute-start | bytes 786440 | tf_op jit(solution)/shard_map/ppermute | solution.py:25
  56.6 1.6 %tables.1 = (bf16[4,224,256]{2,1,0:T(8,128)(2,1)S(1)}, bf16[2,4,256,112]{3,2,1,0:T(8,128)(2,1)S(1)}, f32[4,256,2]{2,1,0:T(8,128)S(1)}) custom-call(s32[1]{0:T(128)} %bitcast.12.refs_0_, bf16[4,256,128]{2,1,0:T(8,128)(2,1)S(1)} %pad_maximum_fusion.3.refs_1_), custom_call_target="tpu_custom_call" | custom-call | flops 134217728 | bytes 917504 | tf_op jit(solution)/shard_map/tables/pallas_call | solution.py:332
  58.2 2.0 %collective-permute-done.17.refs_12_.refs_5_ = bf16[64,2048]{1,0:T(8,128)(2,1)S(1)} collective-permute-done((bf16[64,2048]{1,0:T(8,128)(2,1)S(1)}, bf16[64,2048]{1,0:T(8,128)(2,1)S(1)}, u32[]{:S(2)}, u32[]{:S(2)}) %collective-permute-start.17) | collective-permute-done | bytes 262176 | tf_op jit(solution)/shard_map/ppermute | solution.py:25
  60.2 1.4 %collective-permute-done.16.refs_8_.refs_1_ = bf16[64,2048]{1,0:T(8,128)(2,1)S(1)} collective-permute-done((bf16[64,2048]{1,0:T(8,128)(2,1)S(1)}, bf16[64,2048]{1,0:T(8,128)(2,1)S(1)}, u32[]{:S(2)}, u32[]{:S(2)}) %collective-permute-start.16) | collective-permute-done | bytes 262176 | tf_op jit(solution)/shard_map/ppermute | solution.py:25
  61.7 0.6 collective-permute-start.23
  62.3 1.5 %collective-permute-start.21 = (bf16[64,2048]{1,0:T(8,128)(2,1)S(1)}, bf16[64,2048]{1,0:T(8,128)(2,1)S(1)}, u32[]{:S(2)}, u32[]{:S(2)}) collective-permute-start(bf16[64,2048]{1,0:T(8,128)(2,1)S(1)} %collective-permute-done.14.refs_12_), channel_id=1, source_target_pairs={{0,2},{1,3},{2,0},{3,1},{4,6},{5,7},{6,4},{7,5},{8,10},{9,11},{10,... | collective-permute-start | bytes 786440 | tf_op jit(solution)/shard_map/ppermute | solution.py:25
  63.7 2.1 %collective-permute-done.22.refs_13_.refs_6_ = bf16[64,2048]{1,0:T(8,128)(2,1)S(1)} collective-permute-done((bf16[64,2048]{1,0:T(8,128)(2,1)S(1)}, bf16[64,2048]{1,0:T(8,128)(2,1)S(1)}, u32[]{:S(2)}, u32[]{:S(2)}) %collective-permute-start.22) | collective-permute-done | bytes 262176 | tf_op jit(solution)/shard_map/ppermute | solution.py:25
  65.9 1.4 %collective-permute-done.20.refs_9_.refs_2_ = bf16[64,2048]{1,0:T(8,128)(2,1)S(1)} collective-permute-done((bf16[64,2048]{1,0:T(8,128)(2,1)S(1)}, bf16[64,2048]{1,0:T(8,128)(2,1)S(1)}, u32[]{:S(2)}, u32[]{:S(2)}) %collective-permute-start.20) | collective-permute-done | bytes 262176 | tf_op jit(solution)/shard_map/ppermute | solution.py:25
  67.3 1.8 %collective-permute-done.23.refs_14_.refs_7_ = bf16[64,2048]{1,0:T(8,128)(2,1)S(1)} collective-permute-done((bf16[64,2048]{1,0:T(8,128)(2,1)S(1)}, bf16[64,2048]{1,0:T(8,128)(2,1)S(1)}, u32[]{:S(2)}, u32[]{:S(2)}) %collective-permute-start.23) | collective-permute-done | bytes 262176 | tf_op jit(solution)/shard_map/ppermute | solution.py:25
  69.1 1.2 collective-permute-done.21.refs_10_.refs_3_
  70.3 0.7 collective-permute-start.24
  71.0 1.5 %collective-permute-start.25 = (bf16[256,1024]{1,0:T(8,128)(2,1)S(1)}, bf16[256,1024]{1,0:T(8,128)(2,1)S(1)}, u32[]{:S(2)}, u32[]{:S(2)}) collective-permute-start(bf16[256,1024]{1,0:T(8,128)(2,1)S(1)} %get-tuple-element.95), channel_id=1, source_target_pairs={{0,2},{1,3},{2,0},{3,1},{4,6},{5,7},{6,4},{7,5},{8,10},{9,11},{10,... | collective-permute-start | bytes 1572872 | tf_op jit(solution)/shard_map/ppermute | solution.py:25
  72.4 9.5 %experts.2 = (bf16[256,1024]{1,0:T(8,128)(2,1)S(1)}, bf16[256,1024]{1,0:T(8,128)(2,1)S(1)}, bf16[256,1024]{1,0:T(8,128)(2,1)S(1)}, bf16[256,1024]{1,0:T(8,128)(2,1)S(1)}) custom-call(bf16[4,224,256]{2,1,0:T(8,128)(2,1)S(1)} %get-tuple-element.79.refs_0_, bf16[2,4,256,112]{3,2,1,0:T(8,128)(2,1)S(1)} %get-tuple-element.80.refs_1_, ...), custom_call_target="tpu_custom_call" | custom-call | flops 4227858432 | bytes 23068672 | tf_op jit(solution)/shard_map/experts/pallas_call | solution.py:462
  82.0 1.5 %collective-permute-start.26 = (bf16[256,1024]{1,0:T(8,128)(2,1)S(1)}, bf16[256,1024]{1,0:T(8,128)(2,1)S(1)}, u32[]{:S(2)}, u32[]{:S(2)}) collective-permute-start(bf16[256,1024]{1,0:T(8,128)(2,1)S(1)} %get-tuple-element.96), channel_id=1, source_target_pairs={{0,16},{16,0},{1,17},{17,1},{2,18},{18,2},{3,19},{19,3},{4,20},{20... | collective-permute-start | bytes 1572872 | tf_op jit(solution)/shard_map/ppermute | solution.py:25
  83.5 2.2 %collective-permute-start.27 = (bf16[256,1024]{1,0:T(8,128)(2,1)S(1)}, bf16[256,1024]{1,0:T(8,128)(2,1)S(1)}, u32[]{:S(2)}, u32[]{:S(2)}) collective-permute-start(bf16[256,1024]{1,0:T(8,128)(2,1)S(1)} %get-tuple-element.97), channel_id=1, source_target_pairs={{0,2},{1,3},{2,0},{3,1},{4,6},{5,7},{6,4},{7,5},{8,10},{9,11},{10,... | collective-permute-start | bytes 1572872 | tf_op jit(solution)/shard_map/ppermute | solution.py:25
  85.7 9.7 %experts.3 = (bf16[128,1024]{1,0:T(8,128)(2,1)S(1)}, bf16[128,1024]{1,0:T(8,128)(2,1)S(1)}, bf16[128,1024]{1,0:T(8,128)(2,1)S(1)}, bf16[128,1024]{1,0:T(8,128)(2...) custom-call(bf16[4,224,256]{2,1,0:T(8,128)(2,1)S(1)} %get-tuple-element.79.refs_0_, ...), custom_call_target="tpu_custom_call" | custom-call | flops 4227858432 | bytes 23068672 | tf_op jit(solution)/shard_map/experts/pallas_call | solution.py:462
  95.5 0.3 collective-permute-start.28
  95.8 0.4 collective-permute-start.30
  96.2 1.3 collective-permute-start.32
  97.5 2.0 %collective-permute-start.33 = (bf16[128,1024]{1,0:T(8,128)(2,1)S(1)}, bf16[128,1024]{1,0:T(8,128)(2,1)S(1)}, u32[]{:S(2)}, u32[]{:S(2)}) collective-permute-start(bf16[128,1024]{1,0:T(8,128)(2,1)S(1)} %get-tuple-element.113), channel_id=1, source_target_pairs={{0,2},{1,3},{2,0},{3,1},{4,6},{5,7},{6,4},{7,5},{8,10},{9,11},{10,... | collective-permute-start | bytes 786440 | tf_op jit(solution)/shard_map/ppermute | solution.py:25
  99.6 4.6 %collective-permute-done.28 = bf16[128,1024]{1,0:T(8,128)(2,1)S(1)} collective-permute-done((bf16[128,1024]{1,0:T(8,128)(2,1)S(1)}, bf16[128,1024]{1,0:T(8,128)(2,1)S(1)}, u32[]{:S(2)}, u32[]{:S(2)}) %collective-permute-start.28) | collective-permute-done | bytes 262176 | tf_op jit(solution)/shard_map/ppermute | solution.py:25
  104.3 0.6 collective-permute-start.29
  105.1 1.0 collective-permute-start.31
  106.1 1.4 %collective-permute-done.32 = bf16[128,1024]{1,0:T(8,128)(2,1)S(1)} collective-permute-done((bf16[128,1024]{1,0:T(8,128)(2,1)S(1)}, bf16[128,1024]{1,0:T(8,128)(2,1)S(1)}, u32[]{:S(2)}, u32[]{:S(2)}) %collective-permute-start.32) | collective-permute-done | bytes 262176 | tf_op jit(solution)/shard_map/ppermute | solution.py:25
  107.5 0.5 collective-permute-done.33
  108.0 4.6 %collective-permute-done.29 = bf16[128,1024]{1,0:T(8,128)(2,1)S(1)} collective-permute-done((bf16[128,1024]{1,0:T(8,128)(2,1)S(1)}, bf16[128,1024]{1,0:T(8,128)(2,1)S(1)}, u32[]{:S(2)}, u32[]{:S(2)}) %collective-permute-start.29) | collective-permute-done | bytes 262176 | tf_op jit(solution)/shard_map/ppermute | solution.py:25
  112.8 0.3 convert_add_fusion.3
  113.3 2.6 %collective-permute-start.34 = (bf16[128,1024]{1,0:T(8,128)(2,1)S(1)}, bf16[128,1024]{1,0:T(8,128)(2,1)S(1)}, u32[]{:S(2)}, u32[]{:S(2)}) collective-permute-start(bf16[128,1024]{1,0:T(8,128)(2,1)S(1)} %get-tuple-element.120), channel_id=1, source_target_pairs={{0,2},{1,3},{2,0},{3,1},{4,6},{5,7},{6,4},{7,5},{8,10},{9,11},{10,... | collective-permute-start | bytes 786440 | tf_op jit(solution)/shard_map/ppermute | solution.py:25
  115.9 0.5 collective-permute-start.35
  116.4 7.7 %collective-permute-done.37 = bf16[64,2048]{1,0:T(8,128)(2,1)S(1)} collective-permute-done((bf16[64,2048]{1,0:T(8,128)(2,1)S(1)}, bf16[64,2048]{1,0:T(8,128)(2,1)S(1)}, u32[]{:S(2)}, u32[]{:S(2)}) %collective-permute-start.37) | collective-permute-done | bytes 262176 | tf_op jit(solution)/shard_map/ppermute | solution.py:25
  124.1 1.7 %collective-permute-start.38 = (bf16[64,2048]{1,0:T(8,128)(2,1)S(1)}, bf16[64,2048]{1,0:T(8,128)(2,1)S(1)}, u32[]{:S(2)}, u32[]{:S(2)}) collective-permute-start(bf16[64,2048]{1,0:T(8,128)(2,1)S(1)} %fusion.1), channel_id=1, source_target_pairs={{0,8},{4,12},{8,0},{12,4},{1,9},{5,13},{9,1},{13,5},{2,10},{6,14},... | collective-permute-start | bytes 786440 | tf_op jit(solution)/shard_map/ppermute | solution.py:25
  126.2 2.5 %collective-permute-start.36 = (bf16[64,2048]{1,0:T(8,128)(2,1)S(1)}, bf16[64,2048]{1,0:T(8,128)(2,1)S(1)}, u32[]{:S(2)}, u32[]{:S(2)}) collective-permute-start(bf16[64,2048]{1,0:T(8,128)(2,1)S(1)} %fusion.8), channel_id=1, source_target_pairs={{0,4},{4,0},{8,12},{12,8},{1,5},{5,1},{9,13},{13,9},{2,6},{6,2},{1... | collective-permute-start | bytes 786440 | tf_op jit(solution)/shard_map/ppermute | solution.py:25
  128.7 5.6 %collective-permute-done.38 = bf16[64,2048]{1,0:T(8,128)(2,1)S(1)} collective-permute-done((bf16[64,2048]{1,0:T(8,128)(2,1)S(1)}, bf16[64,2048]{1,0:T(8,128)(2,1)S(1)}, u32[]{:S(2)}, u32[]{:S(2)}) %collective-permute-start.38) | collective-permute-done | bytes 262176 | tf_op jit(solution)/shard_map/ppermute | solution.py:25
  134.4 0.8 collective-permute-done.36
  135.2 0.9 fusion.7
  (69 shorter events, 2.0 us)
Async XLA Ops:
  0.0 22.2 %copy-start.1 = (f32[128]{0:T(128)S(1)}, f32[128]{0:T(128)}, u32[]{:S(2)}) copy-start(f32[128]{0:T(128)} %param.16) | copy-start | bytes 1540
  0.0 22.2 %copy-start = (bf16[2048,512]{1,0:T(8,128)(2,1)S(1)}, bf16[2048,512]{1,0:T(8,128)(2,1)}, u32[]{:S(2)}) copy-start(bf16[2048,512]{1,0:T(8,128)(2,1)} %weight_ref.1) | copy-start | bytes 6291460
  0.0 37.4 %collective-permute-start.12 = (bf16[2048,1536]{1,0:T(8,128)(2,1)}, bf16[2048,1536]{1,0:T(8,128)(2,1)}, u32[]{:S(2)}, u32[]{:S(2)}) collective-permute-start(bf16[2048,1536]{1,0:T(8,128)(2,1)} %bitcast.51), channel_id=1, source_target_pairs={{0,1},{1,0},{2,3},{3,2},{4,5},{5,4},{6,7},{7,6},{8,9},{9,8},{10,11... | collective-permute-start | bytes 18874376 | tf_op jit(solution)/shard_map/ppermute | solution.py:25
  3.1 12.0 %collective-permute-start.2 = (bf16[64,640]{1,0:T(8,128)(2,1)S(1)}, bf16[64,640]{1,0:T(8,128)(2,1)S(1)}, u32[]{:S(2)}, u32[]{:S(2)}) collective-permute-start(bf16[64,640]{1,0:T(8,128)(2,1)S(1)} %get-tuple-element.65), channel_id=1, source_target_pairs={{0,12},{4,8},{8,4},{12,0},{1,13},{5,9},{9,5},{13,1},{2,14},{6,10},... | collective-permute-start | bytes 245768 | tf_op jit(solution)/shard_map/ppermute | solution.py:25
  7.7 7.4 %collective-permute-start.1 = (bf16[64,640]{1,0:T(8,128)(2,1)S(1)}, bf16[64,640]{1,0:T(8,128)(2,1)S(1)}, u32[]{:S(2)}, u32[]{:S(2)}) collective-permute-start(bf16[64,640]{1,0:T(8,128)(2,1)S(1)} %get-tuple-element.65), channel_id=1, source_target_pairs={{0,8},{4,12},{8,0},{12,4},{1,9},{5,13},{9,1},{13,5},{2,10},{6,14},... | collective-permute-start | bytes 245768 | tf_op jit(solution)/shard_map/ppermute | solution.py:25
  7.7 5.8 %collective-permute-start = (bf16[64,640]{1,0:T(8,128)(2,1)S(1)}, bf16[64,640]{1,0:T(8,128)(2,1)S(1)}, u32[]{:S(2)}, u32[]{:S(2)}) collective-permute-start(bf16[64,640]{1,0:T(8,128)(2,1)S(1)} %get-tuple-element.65), channel_id=1, source_target_pairs={{0,4},{4,0},{8,12},{12,8},{1,5},{5,1},{9,13},{13,9},{2,6},{6,2},{1... | collective-permute-start | bytes 245768 | tf_op jit(solution)/shard_map/ppermute | solution.py:25
  8.4 8.0 %collective-permute-start.3 = (bf16[64,2048]{1,0:T(8,128)(2,1)S(1)}, bf16[64,2048]{1,0:T(8,128)(2,1)S(1)}, u32[]{:S(2)}, u32[]{:S(2)}) collective-permute-start(bf16[64,2048]{1,0:T(8,128)(2,1)S(1)} %get-tuple-element.67.first_ref), channel_id=1, source_target_pairs={{0,2},{1,3},{2,0},{3,1},{4,6},{5,7},{6,4},{7,5},{8,10},{9,11},{10,... | collective-permute-start | bytes 786440 | tf_op jit(solution)/shard_map/ppermute | solution.py:25
  10.0 13.7 %copy-start.2 = (bf16[512,2048]{1,0:T(8,128)(2,1)S(1)}, bf16[512,2048]{1,0:T(8,128)(2,1)}, u32[]{:S(2)}) copy-start(bf16[512,2048]{1,0:T(8,128)(2,1)} %refs_3_.1) | copy-start | bytes 6291460
  16.4 5.7 %collective-permute-start.6 = (bf16[256,384]{1,0:T(8,128)(2,1)S(1)}, bf16[256,384]{1,0:T(8,128)(2,1)S(1)}, u32[]{:S(2)}, u32[]{:S(2)}) collective-permute-start(bf16[256,384]{1,0:T(8,128)(2,1)S(1)} %pad_maximum_fusion.4), channel_id=1, source_target_pairs={{0,2},{1,3},{2,0},{3,1},{4,6},{5,7},{6,4},{7,5},{8,10},{9,11},{10,... | collective-permute-start | bytes 589832 | tf_op jit(solution)/shard_map/ppermute | solution.py:25
  17.9 4.3 %collective-permute-start.4 = (bf16[64,2048]{1,0:T(8,128)(2,1)S(1)}, bf16[64,2048]{1,0:T(8,128)(2,1)S(1)}, u32[]{:S(2)}, u32[]{:S(2)}) collective-permute-start(bf16[64,2048]{1,0:T(8,128)(2,1)S(1)} %get-tuple-element.67.first_ref), channel_id=1, source_target_pairs={{0,1},{1,0},{2,3},{3,2},{4,5},{5,4},{6,7},{7,6},{8,9},{9,8},{10,11... | collective-permute-start | bytes 786440 | tf_op jit(solution)/shard_map/ppermute | solution.py:25
  17.9 4.3 %collective-permute-start.5 = (bf16[64,2048]{1,0:T(8,128)(2,1)S(1)}, bf16[64,2048]{1,0:T(8,128)(2,1)S(1)}, u32[]{:S(2)}, u32[]{:S(2)}) collective-permute-start(bf16[64,2048]{1,0:T(8,128)(2,1)S(1)} %collective-permute-done.3.second_ref), channel_id=1, source_target_pairs={{0,1},{1,0},{2,3},{3,2},{4,5},{5,4},{6,7},{7,6},{8,9},{9,8},{10,11... | collective-permute-start | bytes 786440 | tf_op jit(solution)/shard_map/ppermute | solution.py:25
  22.1 1.6 %collective-permute-start.7 = (bf16[512,256]{1,0:T(8,128)(2,1)S(1)}, bf16[512,256]{1,0:T(8,128)(2,1)S(1)}, u32[]{:S(2)}, u32[]{:S(2)}) collective-permute-start(bf16[512,256]{1,0:T(8,128)(2,1)S(1)} %pad_maximum_fusion.2.refs_1_), channel_id=1, source_target_pairs={{0,1},{1,0},{2,3},{3,2},{4,5},{5,4},{6,7},{7,6},{8,9},{9,8},{10,11... | collective-permute-start | bytes 786440 | tf_op jit(solution)/shard_map/ppermute | solution.py:25
  22.3 6.2 %copy-start.3 = (bf16[1,768,2048]{2,1,0:T(8,128)(2,1)S(1)}, bf16[1,768,2048]{2,1,0:T(8,128)(2,1)}, u32[]{:S(2)}) copy-start(bf16[1,768,2048]{2,1,0:T(8,128)(2,1)} %param.23) | copy-start | bytes 9437188
  23.1 14.3 %copy-start.5 = (bf16[1,64,2048]{2,1,0:T(8,128)(2,1)S(1)}, bf16[1,64,2048]{2,1,0:T(8,128)(2,1)}, u32[]{:S(2)}) copy-start(bf16[1,64,2048]{2,1,0:T(8,128)(2,1)} %param.12) | copy-start | bytes 786436
  26.5 11.2 %copy-start.9 = (f32[2048]{0:T(1024)S(1)}, f32[2048]{0:T(1024)}, u32[]{:S(2)}) copy-start(f32[2048]{0:T(1024)} %param.19) | copy-start | bytes 24580
  26.5 2.0 %collective-permute-start.8 = (bf16[128,2048]{1,0:T(8,128)(2,1)S(1)}, bf16[128,2048]{1,0:T(8,128)(2,1)S(1)}, u32[]{:S(2)}, u32[]{:S(2)}) collective-permute-start(bf16[128,2048]{1,0:T(8,128)(2,1)S(1)} %get-tuple-element.70), channel_id=1, source_target_pairs={{0,1},{1,0},{2,3},{3,2},{4,5},{5,4},{6,7},{7,6},{8,9},{9,8},{10,11... | collective-permute-start | bytes 1572872 | tf_op jit(solution)/shard_map/ppermute | solution.py:25
  28.5 8.9 %collective-permute-start.11 = (bf16[768,2048]{1,0:T(8,128)(2,1)S(1)}, bf16[768,2048]{1,0:T(8,128)(2,1)S(1)}, u32[]{:S(2)}, u32[]{:S(2)}) collective-permute-start(bf16[768,2048]{1,0:T(8,128)(2,1)S(1)} %bitcast.56), channel_id=1, source_target_pairs={{0,1},{1,0},{2,3},{3,2},{4,5},{5,4},{6,7},{7,6},{8,9},{9,8},{10,11... | collective-permute-start | bytes 9437192 | tf_op jit(solution)/shard_map/ppermute | solution.py:25
  28.8 8.6 %collective-permute-start.9 = (bf16[64,2048]{1,0:T(8,128)(2,1)S(1)}, bf16[64,2048]{1,0:T(8,128)(2,1)S(1)}, u32[]{:S(2)}, u32[]{:S(2)}) collective-permute-start(bf16[64,2048]{1,0:T(8,128)(2,1)S(1)} %slice.145), channel_id=1, source_target_pairs={{0,2},{1,3},{2,0},{3,1},{4,6},{5,7},{6,4},{7,5},{8,10},{9,11},{10,... | collective-permute-start | bytes 786440 | tf_op jit(solution)/shard_map/ppermute | solution.py:25
  30.3 5.5 %collective-permute-start.10 = (bf16[2,256,128]{2,1,0:T(8,128)(2,1)S(1)}, bf16[2,256,128]{2,1,0:T(8,128)(2,1)S(1)}, u32[]{:S(2)}, u32[]{:S(2)}) collective-permute-start(bf16[2,256,128]{2,1,0:T(8,128)(2,1)S(1)} %pad_maximum_fusion.5), channel_id=1, source_target_pairs={{0,16},{16,0},{1,17},{17,1},{2,18},{18,2},{3,19},{19,3},{4,20},{20... | collective-permute-start | bytes 393224 | tf_op jit(solution)/shard_map/ppermute | solution.py:25
  37.4 16.6 %copy-start.7 = (bf16[64,2048]{1,0:T(8,128)(2,1)}, bf16[64,2048]{1,0:T(8,128)(2,1)S(1)}, u32[]{:S(2)}) copy-start(bf16[64,2048]{1,0:T(8,128)(2,1)S(1)} %collective-permute-done.9) | copy-start | bytes 786436
  37.4 16.6 %copy-start.4 = (bf16[768,2048]{1,0:T(8,128)(2,1)}, bf16[768,2048]{1,0:T(8,128)(2,1)S(1)}, u32[]{:S(2)}) copy-start(bf16[768,2048]{1,0:T(8,128)(2,1)S(1)} %collective-permute-done.11.refs_6_) | copy-start | bytes 9437188
  37.8 13.2 %collective-permute-start.15 = (bf16[64,2048]{1,0:T(8,128)(2,1)S(1)}, bf16[64,2048]{1,0:T(8,128)(2,1)S(1)}, u32[]{:S(2)}, u32[]{:S(2)}) collective-permute-start(bf16[64,2048]{1,0:T(8,128)(2,1)S(1)} %multiply_convert_fusion.refs_9_), channel_id=1, source_target_pairs={{0,4},{4,0},{8,12},{12,8},{1,5},{5,1},{9,13},{13,9},{2,6},{6,2},{1... | collective-permute-start | bytes 786440 | tf_op jit(solution)/shard_map/ppermute | solution.py:25
  39.2 14.7 %collective-permute-start.13 = (bf16[64,2048]{1,0:T(8,128)(2,1)S(1)}, bf16[64,2048]{1,0:T(8,128)(2,1)S(1)}, u32[]{:S(2)}, u32[]{:S(2)}) collective-permute-start(bf16[64,2048]{1,0:T(8,128)(2,1)S(1)} %multiply_convert_fusion.refs_9_), channel_id=1, source_target_pairs={{0,8},{4,12},{8,0},{12,4},{1,9},{5,13},{9,1},{13,5},{2,10},{6,14},... | collective-permute-start | bytes 786440 | tf_op jit(solution)/shard_map/ppermute | solution.py:25
  41.8 12.2 %collective-permute-start.19 = (bf16[64,2048]{1,0:T(8,128)(2,1)S(1)}, bf16[64,2048]{1,0:T(8,128)(2,1)S(1)}, u32[]{:S(2)}, u32[]{:S(2)}) collective-permute-start(bf16[64,2048]{1,0:T(8,128)(2,1)S(1)} %multiply_convert_fusion.refs_9_), channel_id=1, source_target_pairs={{0,16},{16,0},{1,17},{17,1},{2,18},{18,2},{3,19},{19,3},{4,20},{20... | collective-permute-start | bytes 786440 | tf_op jit(solution)/shard_map/ppermute | solution.py:25
  43.3 10.7 %collective-permute-start.18 = (bf16[64,2048]{1,0:T(8,128)(2,1)S(1)}, bf16[64,2048]{1,0:T(8,128)(2,1)S(1)}, u32[]{:S(2)}, u32[]{:S(2)}) collective-permute-start(bf16[64,2048]{1,0:T(8,128)(2,1)S(1)} %multiply_convert_fusion.refs_9_), channel_id=1, source_target_pairs={{0,2},{1,3},{2,0},{3,1},{4,6},{5,7},{6,4},{7,5},{8,10},{9,11},{10,... | collective-permute-start | bytes 786440 | tf_op jit(solution)/shard_map/ppermute | solution.py:25
  51.0 9.2 %collective-permute-start.17 = (bf16[64,2048]{1,0:T(8,128)(2,1)S(1)}, bf16[64,2048]{1,0:T(8,128)(2,1)S(1)}, u32[]{:S(2)}, u32[]{:S(2)}) collective-permute-start(bf16[64,2048]{1,0:T(8,128)(2,1)S(1)} %collective-permute-done.15.refs_10_), channel_id=1, source_target_pairs={{0,16},{16,0},{1,17},{17,1},{2,18},{18,2},{3,19},{19,3},{4,20},{20... | collective-permute-start | bytes 786440 | tf_op jit(solution)/shard_map/ppermute | solution.py:25
  52.4 9.2 %collective-permute-start.16 = (bf16[64,2048]{1,0:T(8,128)(2,1)S(1)}, bf16[64,2048]{1,0:T(8,128)(2,1)S(1)}, u32[]{:S(2)}, u32[]{:S(2)}) collective-permute-start(bf16[64,2048]{1,0:T(8,128)(2,1)S(1)} %collective-permute-done.15.refs_10_), channel_id=1, source_target_pairs={{0,2},{1,3},{2,0},{3,1},{4,6},{5,7},{6,4},{7,5},{8,10},{9,11},{10,... | collective-permute-start | bytes 786440 | tf_op jit(solution)/shard_map/ppermute | solution.py:25
  54.0 7.7 %collective-permute-start.14 = (bf16[64,2048]{1,0:T(8,128)(2,1)S(1)}, bf16[64,2048]{1,0:T(8,128)(2,1)S(1)}, u32[]{:S(2)}, u32[]{:S(2)}) collective-permute-start(bf16[64,2048]{1,0:T(8,128)(2,1)S(1)} %collective-permute-done.13.refs_11_), channel_id=1, source_target_pairs={{0,4},{4,0},{8,12},{12,8},{1,5},{5,1},{9,13},{13,9},{2,6},{6,2},{1... | collective-permute-start | bytes 786440 | tf_op jit(solution)/shard_map/ppermute | solution.py:25
  54.1 11.8 %collective-permute-start.22 = (bf16[64,2048]{1,0:T(8,128)(2,1)S(1)}, bf16[64,2048]{1,0:T(8,128)(2,1)S(1)}, u32[]{:S(2)}, u32[]{:S(2)}) collective-permute-start(bf16[64,2048]{1,0:T(8,128)(2,1)S(1)} %collective-permute-done.13.refs_11_), channel_id=1, source_target_pairs={{0,16},{16,0},{1,17},{17,1},{2,18},{18,2},{3,19},{19,3},{4,20},{20... | collective-permute-start | bytes 786440 | tf_op jit(solution)/shard_map/ppermute | solution.py:25
  55.1 12.2 %collective-permute-start.20 = (bf16[64,2048]{1,0:T(8,128)(2,1)S(1)}, bf16[64,2048]{1,0:T(8,128)(2,1)S(1)}, u32[]{:S(2)}, u32[]{:S(2)}) collective-permute-start(bf16[64,2048]{1,0:T(8,128)(2,1)S(1)} %collective-permute-done.13.refs_11_), channel_id=1, source_target_pairs={{0,2},{1,3},{2,0},{3,1},{4,6},{5,7},{6,4},{7,5},{8,10},{9,11},{10,... | collective-permute-start | bytes 786440 | tf_op jit(solution)/shard_map/ppermute | solution.py:25
  61.7 7.4 %collective-permute-start.23 = (bf16[64,2048]{1,0:T(8,128)(2,1)S(1)}, bf16[64,2048]{1,0:T(8,128)(2,1)S(1)}, u32[]{:S(2)}, u32[]{:S(2)}) collective-permute-start(bf16[64,2048]{1,0:T(8,128)(2,1)S(1)} %collective-permute-done.14.refs_12_), channel_id=1, source_target_pairs={{0,16},{16,0},{1,17},{17,1},{2,18},{18,2},{3,19},{19,3},{4,20},{20... | collective-permute-start | bytes 786440 | tf_op jit(solution)/shard_map/ppermute | solution.py:25
  62.3 8.0 %collective-permute-start.21 = (bf16[64,2048]{1,0:T(8,128)(2,1)S(1)}, bf16[64,2048]{1,0:T(8,128)(2,1)S(1)}, u32[]{:S(2)}, u32[]{:S(2)}) collective-permute-start(bf16[64,2048]{1,0:T(8,128)(2,1)S(1)} %collective-permute-done.14.refs_12_), channel_id=1, source_target_pairs={{0,2},{1,3},{2,0},{3,1},{4,6},{5,7},{6,4},{7,5},{8,10},{9,11},{10,... | collective-permute-start | bytes 786440 | tf_op jit(solution)/shard_map/ppermute | solution.py:25
  70.3 11.6 %collective-permute-start.24 = (bf16[256,1024]{1,0:T(8,128)(2,1)S(1)}, bf16[256,1024]{1,0:T(8,128)(2,1)S(1)}, u32[]{:S(2)}, u32[]{:S(2)}) collective-permute-start(bf16[256,1024]{1,0:T(8,128)(2,1)S(1)} %get-tuple-element.94), channel_id=1, source_target_pairs={{0,16},{16,0},{1,17},{17,1},{2,18},{18,2},{3,19},{19,3},{4,20},{20... | collective-permute-start | bytes 1572872 | tf_op jit(solution)/shard_map/ppermute | solution.py:25
  71.0 11.0 %collective-permute-start.25 = (bf16[256,1024]{1,0:T(8,128)(2,1)S(1)}, bf16[256,1024]{1,0:T(8,128)(2,1)S(1)}, u32[]{:S(2)}, u32[]{:S(2)}) collective-permute-start(bf16[256,1024]{1,0:T(8,128)(2,1)S(1)} %get-tuple-element.95), channel_id=1, source_target_pairs={{0,2},{1,3},{2,0},{3,1},{4,6},{5,7},{6,4},{7,5},{8,10},{9,11},{10,... | collective-permute-start | bytes 1572872 | tf_op jit(solution)/shard_map/ppermute | solution.py:25
  82.0 13.5 %collective-permute-start.26 = (bf16[256,1024]{1,0:T(8,128)(2,1)S(1)}, bf16[256,1024]{1,0:T(8,128)(2,1)S(1)}, u32[]{:S(2)}, u32[]{:S(2)}) collective-permute-start(bf16[256,1024]{1,0:T(8,128)(2,1)S(1)} %get-tuple-element.96), channel_id=1, source_target_pairs={{0,16},{16,0},{1,17},{17,1},{2,18},{18,2},{3,19},{19,3},{4,20},{20... | collective-permute-start | bytes 1572872 | tf_op jit(solution)/shard_map/ppermute | solution.py:25
  83.5 11.9 %collective-permute-start.27 = (bf16[256,1024]{1,0:T(8,128)(2,1)S(1)}, bf16[256,1024]{1,0:T(8,128)(2,1)S(1)}, u32[]{:S(2)}, u32[]{:S(2)}) collective-permute-start(bf16[256,1024]{1,0:T(8,128)(2,1)S(1)} %get-tuple-element.97), channel_id=1, source_target_pairs={{0,2},{1,3},{2,0},{3,1},{4,6},{5,7},{6,4},{7,5},{8,10},{9,11},{10,... | collective-permute-start | bytes 1572872 | tf_op jit(solution)/shard_map/ppermute | solution.py:25
  95.5 8.8 %collective-permute-start.28 = (bf16[128,1024]{1,0:T(8,128)(2,1)S(1)}, bf16[128,1024]{1,0:T(8,128)(2,1)S(1)}, u32[]{:S(2)}, u32[]{:S(2)}) collective-permute-start(bf16[128,1024]{1,0:T(8,128)(2,1)S(1)} %get-tuple-element.109), channel_id=1, source_target_pairs={{0,16},{16,0},{1,17},{17,1},{2,18},{18,2},{3,19},{19,3},{4,20},{20... | collective-permute-start | bytes 786440 | tf_op jit(solution)/shard_map/ppermute | solution.py:25
  95.8 9.2 %collective-permute-start.30 = (bf16[128,1024]{1,0:T(8,128)(2,1)S(1)}, bf16[128,1024]{1,0:T(8,128)(2,1)S(1)}, u32[]{:S(2)}, u32[]{:S(2)}) collective-permute-start(bf16[128,1024]{1,0:T(8,128)(2,1)S(1)} %get-tuple-element.111), channel_id=1, source_target_pairs={{0,2},{1,3},{2,0},{3,1},{4,6},{5,7},{6,4},{7,5},{8,10},{9,11},{10,... | collective-permute-start | bytes 786440 | tf_op jit(solution)/shard_map/ppermute | solution.py:25
  96.2 11.3 %collective-permute-start.32 = (bf16[128,1024]{1,0:T(8,128)(2,1)S(1)}, bf16[128,1024]{1,0:T(8,128)(2,1)S(1)}, u32[]{:S(2)}, u32[]{:S(2)}) collective-permute-start(bf16[128,1024]{1,0:T(8,128)(2,1)S(1)} %get-tuple-element.112), channel_id=1, source_target_pairs={{0,16},{16,0},{1,17},{17,1},{2,18},{18,2},{3,19},{19,3},{4,20},{20... | collective-permute-start | bytes 786440 | tf_op jit(solution)/shard_map/ppermute | solution.py:25
  97.5 10.4 %collective-permute-start.33 = (bf16[128,1024]{1,0:T(8,128)(2,1)S(1)}, bf16[128,1024]{1,0:T(8,128)(2,1)S(1)}, u32[]{:S(2)}, u32[]{:S(2)}) collective-permute-start(bf16[128,1024]{1,0:T(8,128)(2,1)S(1)} %get-tuple-element.113), channel_id=1, source_target_pairs={{0,2},{1,3},{2,0},{3,1},{4,6},{5,7},{6,4},{7,5},{8,10},{9,11},{10,... | collective-permute-start | bytes 786440 | tf_op jit(solution)/shard_map/ppermute | solution.py:25
  104.3 8.3 %collective-permute-start.29 = (bf16[128,1024]{1,0:T(8,128)(2,1)S(1)}, bf16[128,1024]{1,0:T(8,128)(2,1)S(1)}, u32[]{:S(2)}, u32[]{:S(2)}) collective-permute-start(bf16[128,1024]{1,0:T(8,128)(2,1)S(1)} %add_convert_fusion.3), channel_id=1, source_target_pairs={{0,2},{1,3},{2,0},{3,1},{4,6},{5,7},{6,4},{7,5},{8,10},{9,11},{10,... | collective-permute-start | bytes 786440 | tf_op jit(solution)/shard_map/ppermute | solution.py:25
  105.1 7.5 %collective-permute-start.31 = (bf16[128,1024]{1,0:T(8,128)(2,1)S(1)}, bf16[128,1024]{1,0:T(8,128)(2,1)S(1)}, u32[]{:S(2)}, u32[]{:S(2)}) collective-permute-start(bf16[128,1024]{1,0:T(8,128)(2,1)S(1)} %add_convert_fusion.2), channel_id=1, source_target_pairs={{0,16},{16,0},{1,17},{17,1},{2,18},{18,2},{3,19},{19,3},{4,20},{20... | collective-permute-start | bytes 786440 | tf_op jit(solution)/shard_map/ppermute | solution.py:25
  113.2 22.0 %copy-start.6 = (bf16[1,64,2048]{2,1,0:T(8,128)(2,1)S(1)}, bf16[1,64,2048]{2,1,0:T(8,128)(2,1)}, u32[]{:S(2)}) copy-start(bf16[1,64,2048]{2,1,0:T(8,128)(2,1)} %param.12) | copy-start | bytes 786436
  113.2 21.9 %copy-start.8 = (bf16[64,2048]{1,0:T(8,128)(2,1)S(1)}, bf16[64,2048]{1,0:T(8,128)(2,1)}, u32[]{:S(2)}) copy-start(bf16[64,2048]{1,0:T(8,128)(2,1)} %copy-done.7) | copy-start | bytes 786436
  113.3 10.8 %collective-permute-start.37 = (bf16[64,2048]{1,0:T(8,128)(2,1)S(1)}, bf16[64,2048]{1,0:T(8,128)(2,1)S(1)}, u32[]{:S(2)}, u32[]{:S(2)}) collective-permute-start(bf16[64,2048]{1,0:T(8,128)(2,1)S(1)} %fusion.9), channel_id=1, source_target_pairs={{0,4},{4,0},{8,12},{12,8},{1,5},{5,1},{9,13},{13,9},{2,6},{6,2},{1... | collective-permute-start | bytes 786440 | tf_op jit(solution)/shard_map/ppermute | solution.py:25
  113.3 12.5 %collective-permute-start.34 = (bf16[128,1024]{1,0:T(8,128)(2,1)S(1)}, bf16[128,1024]{1,0:T(8,128)(2,1)S(1)}, u32[]{:S(2)}, u32[]{:S(2)}) collective-permute-start(bf16[128,1024]{1,0:T(8,128)(2,1)S(1)} %get-tuple-element.120), channel_id=1, source_target_pairs={{0,2},{1,3},{2,0},{3,1},{4,6},{5,7},{6,4},{7,5},{8,10},{9,11},{10,... | collective-permute-start | bytes 786440 | tf_op jit(solution)/shard_map/ppermute | solution.py:25
  115.9 10.0 %collective-permute-start.35 = (bf16[128,1024]{1,0:T(8,128)(2,1)S(1)}, bf16[128,1024]{1,0:T(8,128)(2,1)S(1)}, u32[]{:S(2)}, u32[]{:S(2)}) collective-permute-start(bf16[128,1024]{1,0:T(8,128)(2,1)S(1)} %get-tuple-element.121), channel_id=1, source_target_pairs={{0,16},{16,0},{1,17},{17,1},{2,18},{18,2},{3,19},{19,3},{4,20},{20... | collective-permute-start | bytes 786440 | tf_op jit(solution)/shard_map/ppermute | solution.py:25
  124.1 10.3 %collective-permute-start.38 = (bf16[64,2048]{1,0:T(8,128)(2,1)S(1)}, bf16[64,2048]{1,0:T(8,128)(2,1)S(1)}, u32[]{:S(2)}, u32[]{:S(2)}) collective-permute-start(bf16[64,2048]{1,0:T(8,128)(2,1)S(1)} %fusion.1), channel_id=1, source_target_pairs={{0,8},{4,12},{8,0},{12,4},{1,9},{5,13},{9,1},{13,5},{2,10},{6,14},... | collective-permute-start | bytes 786440 | tf_op jit(solution)/shard_map/ppermute | solution.py:25
  126.2 9.0 %collective-permute-start.36 = (bf16[64,2048]{1,0:T(8,128)(2,1)S(1)}, bf16[64,2048]{1,0:T(8,128)(2,1)S(1)}, u32[]{:S(2)}, u32[]{:S(2)}) collective-permute-start(bf16[64,2048]{1,0:T(8,128)(2,1)S(1)} %fusion.8), channel_id=1, source_target_pairs={{0,4},{4,0},{8,12},{12,8},{1,5},{5,1},{9,13},{13,9},{2,6},{6,2},{1... | collective-permute-start | bytes 786440 | tf_op jit(solution)/shard_map/ppermute | solution.py:25

commit v16 on v15

--- a/solution.py
+++ b/solution.py
@@ -125,11 +125,11 @@
     def turned(low, high):
         return swap(low, "rep", ACROSS), swap(high, "role", 1)
 
-    far_corner, beside_corner = corners(1), corners(0)
-    *far, corner_low, corner_high = ready(*turned(*sums(1, *far_corner)), *beside_corner)
+    far_sums = sums(1, *corners(1))
+    corner[:2] = ready(*corner[:2], *far_sums)[:2]
+    far, beside = turned(*far_sums), turned(*sums(0, *corners(0)))
     upper = merged(halves[1], *far)
-    *near_sums, upper = ready(*sums(0, corner_low, corner_high), upper)
-    lower = merged(halves[0], *turned(*near_sums))
+    lower = merged(halves[0], *ready(*beside, upper)[:2])
     top_bits, *low_bits = seq_bits()
 
     def folded(rows):

time: 136 us -> 137 us (level)
  waiting for transfers between devices: 59.3 us -> 63 us
  starting transfers between devices: 46.6 us -> 43.8 us
    ppermute x39, waiting for transfers between devices: 59.3 us -> 63 us  [swap(): return lax.ppermute(block, axis, [(i, i ^ bits) for i in range(size)])]
    ppermute x39, starting transfers between devices: 46.6 us -> 43.8 us  [swap(): return lax.ppermute(block, axis, [(i, i ^ bits) for i in range(size)])]
  transfers between devices with their start and end apart: 39 -> 39, of which waited for: 23 -> 24; matrix products, arithmetic and copies ran while one was open for 1% -> 1% of each run, Pallas kernels for 20% -> 20%
where the time goes in v16:
time: 137 us
  waiting for transfers between devices  63 us (46%)
  starting transfers between devices  43.8 us (32%)
  Pallas kernels  27 us (20%)
  other arithmetic  2.39 us (2%)
    ppermute x39, waiting for transfers between devices, swap(): return lax.ppermute(block, axis, [(i, i ^ bits) for i in range(size)])  63 us
    ppermute x39, starting transfers between devices, swap(): return lax.ppermute(block, axis, [(i, i ^ bits) for i in range(size)])  43.8 us
    pallas_call x2, Pallas kernels, run_experts(): pl.pallas_call(lambda *refs: expert_kernel(first, spots, cuts, *refs), ou...  19.2 us
  transfers between devices with their start and end apart: 39, of which 24 were waited for; matrix products, arithmetic and copies ran while one was open for 1% of the time, Pallas kernels for 20%

profile of v16, /device:TPU:0, one launch (start us, length us, event | category | flops | bytes accessed | tf_op | source)
XLA Modules:
  0.0 136.9 jit_solution(17210879181718484118)
XLA Ops:
  0.0 0.5 collective-permute-start.12
  0.5 2.6 %prepare.1 = (bf16[64,2048]{1,0:T(8,128)(2,1)S(1)}, bf16[64,640]{1,0:T(8,128)(2,1)S(1)}) custom-call(bf16[64,2048]{1,0:T(8,128)(2,1)} %bitcast.57, f32[1,2048]{1,0:T(1,128)} %bitcast.62, bf16[2,2048,256]{2,1,0:T(8,128)(2,1)} %refs_2_.1, f32[1,128]{1,0:T(1,128)} %bitcast.65, s32[8,64]{1,0:T(8,128)} %bitcast.63, s32[8,64]{1,0:T(8,128)} %bitcast.64), custom_call_target="tpu_custom_call" | custom-call | flops 134217728 | bytes 2621440 | tf_op jit(solution)/shard_map/prepare/pallas_call | solution.py:187
  3.1 4.7 %collective-permute-start.2 = (bf16[64,640]{1,0:T(8,128)(2,1)S(1)}, bf16[64,640]{1,0:T(8,128)(2,1)S(1)}, u32[]{:S(2)}, u32[]{:S(2)}) collective-permute-start(bf16[64,640]{1,0:T(8,128)(2,1)S(1)} %get-tuple-element.62), channel_id=1, source_target_pairs={{0,12},{4,8},{8,4},{12,0},{1,13},{5,9},{9,5},{13,1},{2,14},{6,10},... | collective-permute-start | bytes 245768 | tf_op jit(solution)/shard_map/ppermute | solution.py:25
  7.7 0.6 collective-permute-start
  8.4 1.7 %collective-permute-start.3 = (bf16[64,2048]{1,0:T(8,128)(2,1)S(1)}, bf16[64,2048]{1,0:T(8,128)(2,1)S(1)}, u32[]{:S(2)}, u32[]{:S(2)}) collective-permute-start(bf16[64,2048]{1,0:T(8,128)(2,1)S(1)} %get-tuple-element.64.first_ref), channel_id=1, source_target_pairs={{0,2},{1,3},{2,0},{3,1},{4,6},{5,7},{6,4},{7,5},{8,10},{9,11},{10,... | collective-permute-start | bytes 786440 | tf_op jit(solution)/shard_map/ppermute | solution.py:25
  10.0 3.5 %collective-permute-done = bf16[64,640]{1,0:T(8,128)(2,1)S(1)} collective-permute-done((bf16[64,640]{1,0:T(8,128)(2,1)S(1)}, bf16[64,640]{1,0:T(8,128)(2,1)S(1)}, u32[]{:S(2)}, u32[]{:S(2)}) %collective-permute-start) | collective-permute-done | bytes 81952 | tf_op jit(solution)/shard_map/ppermute | solution.py:25
  13.5 1.6 %collective-permute-done.1 = bf16[64,640]{1,0:T(8,128)(2,1)S(1)} collective-permute-done((bf16[64,640]{1,0:T(8,128)(2,1)S(1)}, bf16[64,640]{1,0:T(8,128)(2,1)S(1)}, u32[]{:S(2)}, u32[]{:S(2)}) %collective-permute-start.1) | collective-permute-done | bytes 81952 | tf_op jit(solution)/shard_map/ppermute | solution.py:25
  15.3 1.1 collective-permute-done.3.second_ref
  16.4 1.5 %collective-permute-start.6 = (bf16[256,384]{1,0:T(8,128)(2,1)S(1)}, bf16[256,384]{1,0:T(8,128)(2,1)S(1)}, u32[]{:S(2)}, u32[]{:S(2)}) collective-permute-start(bf16[256,384]{1,0:T(8,128)(2,1)S(1)} %pad_maximum_fusion.4), channel_id=1, source_target_pairs={{0,2},{1,3},{2,0},{3,1},{4,6},{5,7},{6,4},{7,5},{8,10},{9,11},{10,... | collective-permute-start | bytes 589832 | tf_op jit(solution)/shard_map/ppermute | solution.py:25
  17.9 0.5 collective-permute-start.5
  18.4 3.7 %collective-permute-done.6 = bf16[256,384]{1,0:T(8,128)(2,1)S(1)} collective-permute-done((bf16[256,384]{1,0:T(8,128)(2,1)S(1)}, bf16[256,384]{1,0:T(8,128)(2,1)S(1)}, u32[]{:S(2)}, u32[]{:S(2)}) %collective-permute-start.6) | collective-permute-done | bytes 196640 | tf_op jit(solution)/shard_map/ppermute | solution.py:25
  22.3 0.9 queries.1.refs_0_
  23.2 0.6 collective-permute-done.7.refs_2_
  23.7 2.7 %attend.1 = (f32[128,2048]{1,0:T(8,128)S(1)}, bf16[128,2048]{1,0:T(8,128)(2,1)S(1)}) custom-call(bf16[256,512]{1,0:T(8,128)(2,1)S(1)} %queries.1.refs_0_, bf16[512,256]{1,0:T(8,128)(2,1)S(1)} %pad_maximum_fusion.2.refs_1_, bf16[512,256]{1,0:T(8,128)(2,1)S(1)} %collective-permute-done.7.refs_2_, bf16[512,2048]{1,0:T(8,128)(2,1)S(1)} %copy-done.2), custom_call_target="tpu_custom_call" | custom-call | flops 1073741824 | bytes 4194304 | tf_op jit(solution)/shard_map/attend/pallas_call | solution.py:266
  26.5 0.2 collective-permute-start.8
  26.7 1.8 %collective-permute-done.8 = bf16[128,2048]{1,0:T(8,128)(2,1)S(1)} collective-permute-done((bf16[128,2048]{1,0:T(8,128)(2,1)S(1)}, bf16[128,2048]{1,0:T(8,128)(2,1)S(1)}, u32[]{:S(2)}, u32[]{:S(2)}) %collective-permute-start.8) | collective-permute-done | bytes 524320 | tf_op jit(solution)/shard_map/ppermute | solution.py:25
  28.5 0.1 collective-permute-start.11
  28.8 1.5 %collective-permute-start.9 = (bf16[64,2048]{1,0:T(8,128)(2,1)S(1)}, bf16[64,2048]{1,0:T(8,128)(2,1)S(1)}, u32[]{:S(2)}, u32[]{:S(2)}) collective-permute-start(bf16[64,2048]{1,0:T(8,128)(2,1)S(1)} %slice.145), channel_id=1, source_target_pairs={{0,2},{1,3},{2,0},{3,1},{4,6},{5,7},{6,4},{7,5},{8,10},{9,11},{10,... | collective-permute-start | bytes 786440 | tf_op jit(solution)/shard_map/ppermute | solution.py:25
  30.3 1.6 %collective-permute-start.10 = (bf16[2,256,128]{2,1,0:T(8,128)(2,1)S(1)}, bf16[2,256,128]{2,1,0:T(8,128)(2,1)S(1)}, u32[]{:S(2)}, u32[]{:S(2)}) collective-permute-start(bf16[2,256,128]{2,1,0:T(8,128)(2,1)S(1)} %pad_maximum_fusion.5), channel_id=1, source_target_pairs={{0,16},{16,0},{1,17},{17,1},{2,18},{18,2},{3,19},{19,3},{4,20},{20... | collective-permute-start | bytes 393224 | tf_op jit(solution)/shard_map/ppermute | solution.py:25
  31.9 4.0 %collective-permute-done.10 = bf16[2,256,128]{2,1,0:T(8,128)(2,1)S(1)} collective-permute-done((bf16[2,256,128]{2,1,0:T(8,128)(2,1)S(1)}, bf16[2,256,128]{2,1,0:T(8,128)(2,1)S(1)}, u32[]{:S(2)}, u32[]{:S(2)}) %collective-permute-start.10) | collective-permute-done | bytes 131104 | tf_op jit(solution)/shard_map/ppermute | solution.py:25
  35.9 1.5 %collective-permute-done.9 = bf16[64,2048]{1,0:T(8,128)(2,1)S(1)} collective-permute-done((bf16[64,2048]{1,0:T(8,128)(2,1)S(1)}, bf16[64,2048]{1,0:T(8,128)(2,1)S(1)}, u32[]{:S(2)}, u32[]{:S(2)}) %collective-permute-start.9) | collective-permute-done | bytes 262176 | tf_op jit(solution)/shard_map/ppermute | solution.py:25
  37.4 0.2 multiply_reduce_fusion
  37.6 0.1 multiply_convert_fusion.refs_9_
  37.8 1.5 %collective-permute-start.15 = (bf16[64,2048]{1,0:T(8,128)(2,1)S(1)}, bf16[64,2048]{1,0:T(8,128)(2,1)S(1)}, u32[]{:S(2)}, u32[]{:S(2)}) collective-permute-start(bf16[64,2048]{1,0:T(8,128)(2,1)S(1)} %multiply_convert_fusion.refs_9_), channel_id=1, source_target_pairs={{0,4},{4,0},{8,12},{12,8},{1,5},{5,1},{9,13},{13,9},{2,6},{6,2},{1... | collective-permute-start | bytes 786440 | tf_op jit(solution)/shard_map/ppermute | solution.py:25
  39.2 2.6 %collective-permute-start.13 = (bf16[64,2048]{1,0:T(8,128)(2,1)S(1)}, bf16[64,2048]{1,0:T(8,128)(2,1)S(1)}, u32[]{:S(2)}, u32[]{:S(2)}) collective-permute-start(bf16[64,2048]{1,0:T(8,128)(2,1)S(1)} %multiply_convert_fusion.refs_9_), channel_id=1, source_target_pairs={{0,8},{4,12},{8,0},{12,4},{1,9},{5,13},{9,1},{13,5},{2,10},{6,14},... | collective-permute-start | bytes 786440 | tf_op jit(solution)/shard_map/ppermute | solution.py:25
  41.8 1.5 %collective-permute-start.19 = (bf16[64,2048]{1,0:T(8,128)(2,1)S(1)}, bf16[64,2048]{1,0:T(8,128)(2,1)S(1)}, u32[]{:S(2)}, u32[]{:S(2)}) collective-permute-start(bf16[64,2048]{1,0:T(8,128)(2,1)S(1)} %multiply_convert_fusion.refs_9_), channel_id=1, source_target_pairs={{0,16},{16,0},{1,17},{17,1},{2,18},{18,2},{3,19},{19,3},{4,20},{20... | collective-permute-start | bytes 786440 | tf_op jit(solution)/shard_map/ppermute | solution.py:25
  43.3 1.5 %collective-permute-start.18 = (bf16[64,2048]{1,0:T(8,128)(2,1)S(1)}, bf16[64,2048]{1,0:T(8,128)(2,1)S(1)}, u32[]{:S(2)}, u32[]{:S(2)}) collective-permute-start(bf16[64,2048]{1,0:T(8,128)(2,1)S(1)} %multiply_convert_fusion.refs_9_), channel_id=1, source_target_pairs={{0,2},{1,3},{2,0},{3,1},{4,6},{5,7},{6,4},{7,5},{8,10},{9,11},{10,... | collective-permute-start | bytes 786440 | tf_op jit(solution)/shard_map/ppermute | solution.py:25
  44.8 6.2 %collective-permute-done.15.refs_10_ = bf16[64,2048]{1,0:T(8,128)(2,1)S(1)} collective-permute-done((bf16[64,2048]{1,0:T(8,128)(2,1)S(1)}, bf16[64,2048]{1,0:T(8,128)(2,1)S(1)}, u32[]{:S(2)}, u32[]{:S(2)}) %collective-permute-start.15) | collective-permute-done | bytes 262176 | tf_op jit(solution)/shard_map/ppermute | solution.py:25
  51.0 1.4 %collective-permute-start.17 = (bf16[64,2048]{1,0:T(8,128)(2,1)S(1)}, bf16[64,2048]{1,0:T(8,128)(2,1)S(1)}, u32[]{:S(2)}, u32[]{:S(2)}) collective-permute-start(bf16[64,2048]{1,0:T(8,128)(2,1)S(1)} %collective-permute-done.15.refs_10_), channel_id=1, source_target_pairs={{0,16},{16,0},{1,17},{17,1},{2,18},{18,2},{3,19},{19,3},{4,20},{20... | collective-permute-start | bytes 786440 | tf_op jit(solution)/shard_map/ppermute | solution.py:25
  52.4 1.5 %collective-permute-start.16 = (bf16[64,2048]{1,0:T(8,128)(2,1)S(1)}, bf16[64,2048]{1,0:T(8,128)(2,1)S(1)}, u32[]{:S(2)}, u32[]{:S(2)}) collective-permute-start(bf16[64,2048]{1,0:T(8,128)(2,1)S(1)} %collective-permute-done.15.refs_10_), channel_id=1, source_target_pairs={{0,2},{1,3},{2,0},{3,1},{4,6},{5,7},{6,4},{7,5},{8,10},{9,11},{10,... | collective-permute-start | bytes 786440 | tf_op jit(solution)/shard_map/ppermute | solution.py:25
  54.1 1.1 collective-permute-start.22
  55.1 1.5 %collective-permute-start.20 = (bf16[64,2048]{1,0:T(8,128)(2,1)S(1)}, bf16[64,2048]{1,0:T(8,128)(2,1)S(1)}, u32[]{:S(2)}, u32[]{:S(2)}) collective-permute-start(bf16[64,2048]{1,0:T(8,128)(2,1)S(1)} %collective-permute-done.13.refs_11_), channel_id=1, source_target_pairs={{0,2},{1,3},{2,0},{3,1},{4,6},{5,7},{6,4},{7,5},{8,10},{9,11},{10,... | collective-permute-start | bytes 786440 | tf_op jit(solution)/shard_map/ppermute | solution.py:25
  56.6 1.6 %tables.1 = (bf16[4,224,256]{2,1,0:T(8,128)(2,1)S(1)}, bf16[2,4,256,112]{3,2,1,0:T(8,128)(2,1)S(1)}, f32[4,256,2]{2,1,0:T(8,128)S(1)}) custom-call(s32[1]{0:T(128)} %bitcast.12.refs_0_, bf16[4,256,128]{2,1,0:T(8,128)(2,1)S(1)} %pad_maximum_fusion.3.refs_1_), custom_call_target="tpu_custom_call" | custom-call | flops 134217728 | bytes 917504 | tf_op jit(solution)/shard_map/tables/pallas_call | solution.py:332
  58.2 2.0 %collective-permute-done.17.refs_12_.refs_5_ = bf16[64,2048]{1,0:T(8,128)(2,1)S(1)} collective-permute-done((bf16[64,2048]{1,0:T(8,128)(2,1)S(1)}, bf16[64,2048]{1,0:T(8,128)(2,1)S(1)}, u32[]{:S(2)}, u32[]{:S(2)}) %collective-permute-start.17) | collective-permute-done | bytes 262176 | tf_op jit(solution)/shard_map/ppermute | solution.py:25
  60.2 1.4 %collective-permute-done.16.refs_8_.refs_1_ = bf16[64,2048]{1,0:T(8,128)(2,1)S(1)} collective-permute-done((bf16[64,2048]{1,0:T(8,128)(2,1)S(1)}, bf16[64,2048]{1,0:T(8,128)(2,1)S(1)}, u32[]{:S(2)}, u32[]{:S(2)}) %collective-permute-start.16) | collective-permute-done | bytes 262176 | tf_op jit(solution)/shard_map/ppermute | solution.py:25
  61.7 0.6 collective-permute-start.23
  62.3 1.5 %collective-permute-start.21 = (bf16[64,2048]{1,0:T(8,128)(2,1)S(1)}, bf16[64,2048]{1,0:T(8,128)(2,1)S(1)}, u32[]{:S(2)}, u32[]{:S(2)}) collective-permute-start(bf16[64,2048]{1,0:T(8,128)(2,1)S(1)} %collective-permute-done.14.refs_12_), channel_id=1, source_target_pairs={{0,2},{1,3},{2,0},{3,1},{4,6},{5,7},{6,4},{7,5},{8,10},{9,11},{10,... | collective-permute-start | bytes 786440 | tf_op jit(solution)/shard_map/ppermute | solution.py:25
  63.7 2.1 %collective-permute-done.22.refs_13_.refs_6_ = bf16[64,2048]{1,0:T(8,128)(2,1)S(1)} collective-permute-done((bf16[64,2048]{1,0:T(8,128)(2,1)S(1)}, bf16[64,2048]{1,0:T(8,128)(2,1)S(1)}, u32[]{:S(2)}, u32[]{:S(2)}) %collective-permute-start.22) | collective-permute-done | bytes 262176 | tf_op jit(solution)/shard_map/ppermute | solution.py:25
  65.9 1.4 %collective-permute-done.20.refs_9_.refs_2_ = bf16[64,2048]{1,0:T(8,128)(2,1)S(1)} collective-permute-done((bf16[64,2048]{1,0:T(8,128)(2,1)S(1)}, bf16[64,2048]{1,0:T(8,128)(2,1)S(1)}, u32[]{:S(2)}, u32[]{:S(2)}) %collective-permute-start.20) | collective-permute-done | bytes 262176 | tf_op jit(solution)/shard_map/ppermute | solution.py:25
  67.3 1.8 %collective-permute-done.23.refs_14_.refs_7_ = bf16[64,2048]{1,0:T(8,128)(2,1)S(1)} collective-permute-done((bf16[64,2048]{1,0:T(8,128)(2,1)S(1)}, bf16[64,2048]{1,0:T(8,128)(2,1)S(1)}, u32[]{:S(2)}, u32[]{:S(2)}) %collective-permute-start.23) | collective-permute-done | bytes 262176 | tf_op jit(solution)/shard_map/ppermute | solution.py:25
  69.1 1.2 collective-permute-done.21.refs_10_.refs_3_
  70.3 0.7 collective-permute-start.24
  71.0 1.5 %collective-permute-start.25 = (bf16[256,1024]{1,0:T(8,128)(2,1)S(1)}, bf16[256,1024]{1,0:T(8,128)(2,1)S(1)}, u32[]{:S(2)}, u32[]{:S(2)}) collective-permute-start(bf16[256,1024]{1,0:T(8,128)(2,1)S(1)} %get-tuple-element.92), channel_id=1, source_target_pairs={{0,2},{1,3},{2,0},{3,1},{4,6},{5,7},{6,4},{7,5},{8,10},{9,11},{10,... | collective-permute-start | bytes 1572872 | tf_op jit(solution)/shard_map/ppermute | solution.py:25
  72.4 9.5 %experts.2 = (bf16[256,1024]{1,0:T(8,128)(2,1)S(1)}, bf16[256,1024]{1,0:T(8,128)(2,1)S(1)}, bf16[256,1024]{1,0:T(8,128)(2,1)S(1)}, bf16[256,1024]{1,0:T(8,128)(2,1)S(1)}) custom-call(bf16[4,224,256]{2,1,0:T(8,128)(2,1)S(1)} %get-tuple-element.76.refs_0_, bf16[2,4,256,112]{3,2,1,0:T(8,128)(2,1)S(1)} %get-tuple-element.77.refs_1_, ...), custom_call_target="tpu_custom_call" | custom-call | flops 4227858432 | bytes 23068672 | tf_op jit(solution)/shard_map/experts/pallas_call | solution.py:462
  82.0 1.5 %collective-permute-start.26 = (bf16[256,1024]{1,0:T(8,128)(2,1)S(1)}, bf16[256,1024]{1,0:T(8,128)(2,1)S(1)}, u32[]{:S(2)}, u32[]{:S(2)}) collective-permute-start(bf16[256,1024]{1,0:T(8,128)(2,1)S(1)} %get-tuple-element.93), channel_id=1, source_target_pairs={{0,16},{16,0},{1,17},{17,1},{2,18},{18,2},{3,19},{19,3},{4,20},{20... | collective-permute-start | bytes 1572872 | tf_op jit(solution)/shard_map/ppermute | solution.py:25
  83.5 2.2 %collective-permute-start.27 = (bf16[256,1024]{1,0:T(8,128)(2,1)S(1)}, bf16[256,1024]{1,0:T(8,128)(2,1)S(1)}, u32[]{:S(2)}, u32[]{:S(2)}) collective-permute-start(bf16[256,1024]{1,0:T(8,128)(2,1)S(1)} %get-tuple-element.94), channel_id=1, source_target_pairs={{0,2},{1,3},{2,0},{3,1},{4,6},{5,7},{6,4},{7,5},{8,10},{9,11},{10,... | collective-permute-start | bytes 1572872 | tf_op jit(solution)/shard_map/ppermute | solution.py:25
  85.7 9.7 %experts.3 = (bf16[128,1024]{1,0:T(8,128)(2,1)S(1)}, bf16[128,1024]{1,0:T(8,128)(2,1)S(1)}, bf16[128,1024]{1,0:T(8,128)(2,1)S(1)}, bf16[128,1024]{1,0:T(8,128)(2...) custom-call(bf16[4,224,256]{2,1,0:T(8,128)(2,1)S(1)} %get-tuple-element.76.refs_0_, ...), custom_call_target="tpu_custom_call" | custom-call | flops 4227858432 | bytes 23068672 | tf_op jit(solution)/shard_map/experts/pallas_call | solution.py:462
  95.5 0.3 collective-permute-start.28
  95.8 0.4 collective-permute-start.29
  96.2 8.2 %collective-permute-done.28 = bf16[128,1024]{1,0:T(8,128)(2,1)S(1)} collective-permute-done((bf16[128,1024]{1,0:T(8,128)(2,1)S(1)}, bf16[128,1024]{1,0:T(8,128)(2,1)S(1)}, u32[]{:S(2)}, u32[]{:S(2)}) %collective-permute-start.28) | collective-permute-done | bytes 262176 | tf_op jit(solution)/shard_map/ppermute | solution.py:25
  104.7 2.2 %collective-permute-start.30 = (bf16[128,1024]{1,0:T(8,128)(2,1)S(1)}, bf16[128,1024]{1,0:T(8,128)(2,1)S(1)}, u32[]{:S(2)}, u32[]{:S(2)}) collective-permute-start(bf16[128,1024]{1,0:T(8,128)(2,1)S(1)} %get-tuple-element.111), channel_id=1, source_target_pairs={{0,16},{16,0},{1,17},{17,1},{2,18},{18,2},{3,19},{19,3},{4,20},{20... | collective-permute-start | bytes 786440 | tf_op jit(solution)/shard_map/ppermute | solution.py:25
  106.9 2.0 %collective-permute-start.34 = (bf16[128,1024]{1,0:T(8,128)(2,1)S(1)}, bf16[128,1024]{1,0:T(8,128)(2,1)S(1)}, u32[]{:S(2)}, u32[]{:S(2)}) collective-permute-start(bf16[128,1024]{1,0:T(8,128)(2,1)S(1)} %add_convert_fusion.3), channel_id=1, source_target_pairs={{0,2},{1,3},{2,0},{3,1},{4,6},{5,7},{6,4},{7,5},{8,10},{9,11},{10,... | collective-permute-start | bytes 786440 | tf_op jit(solution)/shard_map/ppermute | solution.py:25
  109.0 4.4 %collective-permute-done.30 = bf16[128,1024]{1,0:T(8,128)(2,1)S(1)} collective-permute-done((bf16[128,1024]{1,0:T(8,128)(2,1)S(1)}, bf16[128,1024]{1,0:T(8,128)(2,1)S(1)}, u32[]{:S(2)}, u32[]{:S(2)}) %collective-permute-start.30) | collective-permute-done | bytes 262176 | tf_op jit(solution)/shard_map/ppermute | solution.py:25
  113.6 2.0 %collective-permute-start.33 = (bf16[128,1024]{1,0:T(8,128)(2,1)S(1)}, bf16[128,1024]{1,0:T(8,128)(2,1)S(1)}, u32[]{:S(2)}, u32[]{:S(2)}) collective-permute-start(bf16[128,1024]{1,0:T(8,128)(2,1)S(1)} %add_convert_fusion), channel_id=1, source_target_pairs={{0,16},{16,0},{1,17},{17,1},{2,18},{18,2},{3,19},{19,3},{4,20},{20... | collective-permute-start | bytes 786440 | tf_op jit(solution)/shard_map/ppermute | solution.py:25
  115.6 0.6 collective-permute-done.34
  116.7 3.2 %collective-permute-done.31 = bf16[128,1024]{1,0:T(8,128)(2,1)S(1)} collective-permute-done((bf16[128,1024]{1,0:T(8,128)(2,1)S(1)}, bf16[128,1024]{1,0:T(8,128)(2,1)S(1)}, u32[]{:S(2)}, u32[]{:S(2)}) %collective-permute-start.31) | collective-permute-done | bytes 262176 | tf_op jit(solution)/shard_map/ppermute | solution.py:25
  119.8 0.2 collective-permute-done.33
  120.0 0.3 convert_add_fusion.1
  120.4 5.4 %collective-permute-done.37 = bf16[64,2048]{1,0:T(8,128)(2,1)S(1)} collective-permute-done((bf16[64,2048]{1,0:T(8,128)(2,1)S(1)}, bf16[64,2048]{1,0:T(8,128)(2,1)S(1)}, u32[]{:S(2)}, u32[]{:S(2)}) %collective-permute-start.37) | collective-permute-done | bytes 262176 | tf_op jit(solution)/shard_map/ppermute | solution.py:25
  125.9 0.7 collective-permute-start.38
  126.6 2.3 %collective-permute-start.36 = (bf16[64,2048]{1,0:T(8,128)(2,1)S(1)}, bf16[64,2048]{1,0:T(8,128)(2,1)S(1)}, u32[]{:S(2)}, u32[]{:S(2)}) collective-permute-start(bf16[64,2048]{1,0:T(8,128)(2,1)S(1)} %fusion.8), channel_id=1, source_target_pairs={{0,4},{4,0},{8,12},{12,8},{1,5},{5,1},{9,13},{13,9},{2,6},{6,2},{1... | collective-permute-start | bytes 786440 | tf_op jit(solution)/shard_map/ppermute | solution.py:25
  128.9 6.8 %collective-permute-done.38 = bf16[64,2048]{1,0:T(8,128)(2,1)S(1)} collective-permute-done((bf16[64,2048]{1,0:T(8,128)(2,1)S(1)}, bf16[64,2048]{1,0:T(8,128)(2,1)S(1)}, u32[]{:S(2)}, u32[]{:S(2)}) %collective-permute-start.38) | collective-permute-done | bytes 262176 | tf_op jit(solution)/shard_map/ppermute | solution.py:25
  135.7 0.4 collective-permute-done.36
  136.0 0.9 fusion.7
  (70 shorter events, 1.7 us)
Async XLA Ops:
  0.0 22.2 %copy-start.1 = (f32[128]{0:T(128)S(1)}, f32[128]{0:T(128)}, u32[]{:S(2)}) copy-start(f32[128]{0:T(128)} %param.16) | copy-start | bytes 1540
  0.0 22.2 %copy-start = (bf16[2048,512]{1,0:T(8,128)(2,1)S(1)}, bf16[2048,512]{1,0:T(8,128)(2,1)}, u32[]{:S(2)}) copy-start(bf16[2048,512]{1,0:T(8,128)(2,1)} %weight_ref.1) | copy-start | bytes 6291460
  0.0 37.4 %collective-permute-start.12 = (bf16[2048,1536]{1,0:T(8,128)(2,1)}, bf16[2048,1536]{1,0:T(8,128)(2,1)}, u32[]{:S(2)}, u32[]{:S(2)}) collective-permute-start(bf16[2048,1536]{1,0:T(8,128)(2,1)} %bitcast.51), channel_id=1, source_target_pairs={{0,1},{1,0},{2,3},{3,2},{4,5},{5,4},{6,7},{7,6},{8,9},{9,8},{10,11... | collective-permute-start | bytes 18874376 | tf_op jit(solution)/shard_map/ppermute | solution.py:25
  3.1 12.0 %collective-permute-start.2 = (bf16[64,640]{1,0:T(8,128)(2,1)S(1)}, bf16[64,640]{1,0:T(8,128)(2,1)S(1)}, u32[]{:S(2)}, u32[]{:S(2)}) collective-permute-start(bf16[64,640]{1,0:T(8,128)(2,1)S(1)} %get-tuple-element.62), channel_id=1, source_target_pairs={{0,12},{4,8},{8,4},{12,0},{1,13},{5,9},{9,5},{13,1},{2,14},{6,10},... | collective-permute-start | bytes 245768 | tf_op jit(solution)/shard_map/ppermute | solution.py:25
  7.7 7.4 %collective-permute-start.1 = (bf16[64,640]{1,0:T(8,128)(2,1)S(1)}, bf16[64,640]{1,0:T(8,128)(2,1)S(1)}, u32[]{:S(2)}, u32[]{:S(2)}) collective-permute-start(bf16[64,640]{1,0:T(8,128)(2,1)S(1)} %get-tuple-element.62), channel_id=1, source_target_pairs={{0,8},{4,12},{8,0},{12,4},{1,9},{5,13},{9,1},{13,5},{2,10},{6,14},... | collective-permute-start | bytes 245768 | tf_op jit(solution)/shard_map/ppermute | solution.py:25
  7.7 5.8 %collective-permute-start = (bf16[64,640]{1,0:T(8,128)(2,1)S(1)}, bf16[64,640]{1,0:T(8,128)(2,1)S(1)}, u32[]{:S(2)}, u32[]{:S(2)}) collective-permute-start(bf16[64,640]{1,0:T(8,128)(2,1)S(1)} %get-tuple-element.62), channel_id=1, source_target_pairs={{0,4},{4,0},{8,12},{12,8},{1,5},{5,1},{9,13},{13,9},{2,6},{6,2},{1... | collective-permute-start | bytes 245768 | tf_op jit(solution)/shard_map/ppermute | solution.py:25
  8.4 8.0 %collective-permute-start.3 = (bf16[64,2048]{1,0:T(8,128)(2,1)S(1)}, bf16[64,2048]{1,0:T(8,128)(2,1)S(1)}, u32[]{:S(2)}, u32[]{:S(2)}) collective-permute-start(bf16[64,2048]{1,0:T(8,128)(2,1)S(1)} %get-tuple-element.64.first_ref), channel_id=1, source_target_pairs={{0,2},{1,3},{2,0},{3,1},{4,6},{5,7},{6,4},{7,5},{8,10},{9,11},{10,... | collective-permute-start | bytes 786440 | tf_op jit(solution)/shard_map/ppermute | solution.py:25
  10.0 13.7 %copy-start.2 = (bf16[512,2048]{1,0:T(8,128)(2,1)S(1)}, bf16[512,2048]{1,0:T(8,128)(2,1)}, u32[]{:S(2)}) copy-start(bf16[512,2048]{1,0:T(8,128)(2,1)} %refs_3_.1) | copy-start | bytes 6291460
  16.4 5.7 %collective-permute-start.6 = (bf16[256,384]{1,0:T(8,128)(2,1)S(1)}, bf16[256,384]{1,0:T(8,128)(2,1)S(1)}, u32[]{:S(2)}, u32[]{:S(2)}) collective-permute-start(bf16[256,384]{1,0:T(8,128)(2,1)S(1)} %pad_maximum_fusion.4), channel_id=1, source_target_pairs={{0,2},{1,3},{2,0},{3,1},{4,6},{5,7},{6,4},{7,5},{8,10},{9,11},{10,... | collective-permute-start | bytes 589832 | tf_op jit(solution)/shard_map/ppermute | solution.py:25
  17.9 4.3 %collective-permute-start.4 = (bf16[64,2048]{1,0:T(8,128)(2,1)S(1)}, bf16[64,2048]{1,0:T(8,128)(2,1)S(1)}, u32[]{:S(2)}, u32[]{:S(2)}) collective-permute-start(bf16[64,2048]{1,0:T(8,128)(2,1)S(1)} %get-tuple-element.64.first_ref), channel_id=1, source_target_pairs={{0,1},{1,0},{2,3},{3,2},{4,5},{5,4},{6,7},{7,6},{8,9},{9,8},{10,11... | collective-permute-start | bytes 786440 | tf_op jit(solution)/shard_map/ppermute | solution.py:25
  17.9 4.3 %collective-permute-start.5 = (bf16[64,2048]{1,0:T(8,128)(2,1)S(1)}, bf16[64,2048]{1,0:T(8,128)(2,1)S(1)}, u32[]{:S(2)}, u32[]{:S(2)}) collective-permute-start(bf16[64,2048]{1,0:T(8,128)(2,1)S(1)} %collective-permute-done.3.second_ref), channel_id=1, source_target_pairs={{0,1},{1,0},{2,3},{3,2},{4,5},{5,4},{6,7},{7,6},{8,9},{9,8},{10,11... | collective-permute-start | bytes 786440 | tf_op jit(solution)/shard_map/ppermute | solution.py:25
  22.1 1.6 %collective-permute-start.7 = (bf16[512,256]{1,0:T(8,128)(2,1)S(1)}, bf16[512,256]{1,0:T(8,128)(2,1)S(1)}, u32[]{:S(2)}, u32[]{:S(2)}) collective-permute-start(bf16[512,256]{1,0:T(8,128)(2,1)S(1)} %pad_maximum_fusion.2.refs_1_), channel_id=1, source_target_pairs={{0,1},{1,0},{2,3},{3,2},{4,5},{5,4},{6,7},{7,6},{8,9},{9,8},{10,11... | collective-permute-start | bytes 786440 | tf_op jit(solution)/shard_map/ppermute | solution.py:25
  22.3 6.2 %copy-start.3 = (bf16[1,768,2048]{2,1,0:T(8,128)(2,1)S(1)}, bf16[1,768,2048]{2,1,0:T(8,128)(2,1)}, u32[]{:S(2)}) copy-start(bf16[1,768,2048]{2,1,0:T(8,128)(2,1)} %param.23) | copy-start | bytes 9437188
  23.1 14.3 %copy-start.5 = (bf16[1,64,2048]{2,1,0:T(8,128)(2,1)S(1)}, bf16[1,64,2048]{2,1,0:T(8,128)(2,1)}, u32[]{:S(2)}) copy-start(bf16[1,64,2048]{2,1,0:T(8,128)(2,1)} %param.12) | copy-start | bytes 786436
  26.5 11.2 %copy-start.9 = (f32[2048]{0:T(1024)S(1)}, f32[2048]{0:T(1024)}, u32[]{:S(2)}) copy-start(f32[2048]{0:T(1024)} %param.19) | copy-start | bytes 24580
  26.5 2.0 %collective-permute-start.8 = (bf16[128,2048]{1,0:T(8,128)(2,1)S(1)}, bf16[128,2048]{1,0:T(8,128)(2,1)S(1)}, u32[]{:S(2)}, u32[]{:S(2)}) collective-permute-start(bf16[128,2048]{1,0:T(8,128)(2,1)S(1)} %get-tuple-element.67), channel_id=1, source_target_pairs={{0,1},{1,0},{2,3},{3,2},{4,5},{5,4},{6,7},{7,6},{8,9},{9,8},{10,11... | collective-permute-start | bytes 1572872 | tf_op jit(solution)/shard_map/ppermute | solution.py:25
  28.5 8.9 %collective-permute-start.11 = (bf16[768,2048]{1,0:T(8,128)(2,1)S(1)}, bf16[768,2048]{1,0:T(8,128)(2,1)S(1)}, u32[]{:S(2)}, u32[]{:S(2)}) collective-permute-start(bf16[768,2048]{1,0:T(8,128)(2,1)S(1)} %bitcast.56), channel_id=1, source_target_pairs={{0,1},{1,0},{2,3},{3,2},{4,5},{5,4},{6,7},{7,6},{8,9},{9,8},{10,11... | collective-permute-start | bytes 9437192 | tf_op jit(solution)/shard_map/ppermute | solution.py:25
  28.8 8.6 %collective-permute-start.9 = (bf16[64,2048]{1,0:T(8,128)(2,1)S(1)}, bf16[64,2048]{1,0:T(8,128)(2,1)S(1)}, u32[]{:S(2)}, u32[]{:S(2)}) collective-permute-start(bf16[64,2048]{1,0:T(8,128)(2,1)S(1)} %slice.145), channel_id=1, source_target_pairs={{0,2},{1,3},{2,0},{3,1},{4,6},{5,7},{6,4},{7,5},{8,10},{9,11},{10,... | collective-permute-start | bytes 786440 | tf_op jit(solution)/shard_map/ppermute | solution.py:25
  30.3 5.5 %collective-permute-start.10 = (bf16[2,256,128]{2,1,0:T(8,128)(2,1)S(1)}, bf16[2,256,128]{2,1,0:T(8,128)(2,1)S(1)}, u32[]{:S(2)}, u32[]{:S(2)}) collective-permute-start(bf16[2,256,128]{2,1,0:T(8,128)(2,1)S(1)} %pad_maximum_fusion.5), channel_id=1, source_target_pairs={{0,16},{16,0},{1,17},{17,1},{2,18},{18,2},{3,19},{19,3},{4,20},{20... | collective-permute-start | bytes 393224 | tf_op jit(solution)/shard_map/ppermute | solution.py:25
  37.4 16.6 %copy-start.7 = (bf16[64,2048]{1,0:T(8,128)(2,1)}, bf16[64,2048]{1,0:T(8,128)(2,1)S(1)}, u32[]{:S(2)}) copy-start(bf16[64,2048]{1,0:T(8,128)(2,1)S(1)} %collective-permute-done.9) | copy-start | bytes 786436
  37.4 16.6 %copy-start.4 = (bf16[768,2048]{1,0:T(8,128)(2,1)}, bf16[768,2048]{1,0:T(8,128)(2,1)S(1)}, u32[]{:S(2)}) copy-start(bf16[768,2048]{1,0:T(8,128)(2,1)S(1)} %collective-permute-done.11.refs_6_) | copy-start | bytes 9437188
  37.8 13.2 %collective-permute-start.15 = (bf16[64,2048]{1,0:T(8,128)(2,1)S(1)}, bf16[64,2048]{1,0:T(8,128)(2,1)S(1)}, u32[]{:S(2)}, u32[]{:S(2)}) collective-permute-start(bf16[64,2048]{1,0:T(8,128)(2,1)S(1)} %multiply_convert_fusion.refs_9_), channel_id=1, source_target_pairs={{0,4},{4,0},{8,12},{12,8},{1,5},{5,1},{9,13},{13,9},{2,6},{6,2},{1... | collective-permute-start | bytes 786440 | tf_op jit(solution)/shard_map/ppermute | solution.py:25
  39.2 14.7 %collective-permute-start.13 = (bf16[64,2048]{1,0:T(8,128)(2,1)S(1)}, bf16[64,2048]{1,0:T(8,128)(2,1)S(1)}, u32[]{:S(2)}, u32[]{:S(2)}) collective-permute-start(bf16[64,2048]{1,0:T(8,128)(2,1)S(1)} %multiply_convert_fusion.refs_9_), channel_id=1, source_target_pairs={{0,8},{4,12},{8,0},{12,4},{1,9},{5,13},{9,1},{13,5},{2,10},{6,14},... | collective-permute-start | bytes 786440 | tf_op jit(solution)/shard_map/ppermute | solution.py:25
  41.8 12.2 %collective-permute-start.19 = (bf16[64,2048]{1,0:T(8,128)(2,1)S(1)}, bf16[64,2048]{1,0:T(8,128)(2,1)S(1)}, u32[]{:S(2)}, u32[]{:S(2)}) collective-permute-start(bf16[64,2048]{1,0:T(8,128)(2,1)S(1)} %multiply_convert_fusion.refs_9_), channel_id=1, source_target_pairs={{0,16},{16,0},{1,17},{17,1},{2,18},{18,2},{3,19},{19,3},{4,20},{20... | collective-permute-start | bytes 786440 | tf_op jit(solution)/shard_map/ppermute | solution.py:25
  43.3 10.7 %collective-permute-start.18 = (bf16[64,2048]{1,0:T(8,128)(2,1)S(1)}, bf16[64,2048]{1,0:T(8,128)(2,1)S(1)}, u32[]{:S(2)}, u32[]{:S(2)}) collective-permute-start(bf16[64,2048]{1,0:T(8,128)(2,1)S(1)} %multiply_convert_fusion.refs_9_), channel_id=1, source_target_pairs={{0,2},{1,3},{2,0},{3,1},{4,6},{5,7},{6,4},{7,5},{8,10},{9,11},{10,... | collective-permute-start | bytes 786440 | tf_op jit(solution)/shard_map/ppermute | solution.py:25
  51.0 9.2 %collective-permute-start.17 = (bf16[64,2048]{1,0:T(8,128)(2,1)S(1)}, bf16[64,2048]{1,0:T(8,128)(2,1)S(1)}, u32[]{:S(2)}, u32[]{:S(2)}) collective-permute-start(bf16[64,2048]{1,0:T(8,128)(2,1)S(1)} %collective-permute-done.15.refs_10_), channel_id=1, source_target_pairs={{0,16},{16,0},{1,17},{17,1},{2,18},{18,2},{3,19},{19,3},{4,20},{20... | collective-permute-start | bytes 786440 | tf_op jit(solution)/shard_map/ppermute | solution.py:25
  52.4 9.2 %collective-permute-start.16 = (bf16[64,2048]{1,0:T(8,128)(2,1)S(1)}, bf16[64,2048]{1,0:T(8,128)(2,1)S(1)}, u32[]{:S(2)}, u32[]{:S(2)}) collective-permute-start(bf16[64,2048]{1,0:T(8,128)(2,1)S(1)} %collective-permute-done.15.refs_10_), channel_id=1, source_target_pairs={{0,2},{1,3},{2,0},{3,1},{4,6},{5,7},{6,4},{7,5},{8,10},{9,11},{10,... | collective-permute-start | bytes 786440 | tf_op jit(solution)/shard_map/ppermute | solution.py:25
  54.0 7.7 %collective-permute-start.14 = (bf16[64,2048]{1,0:T(8,128)(2,1)S(1)}, bf16[64,2048]{1,0:T(8,128)(2,1)S(1)}, u32[]{:S(2)}, u32[]{:S(2)}) collective-permute-start(bf16[64,2048]{1,0:T(8,128)(2,1)S(1)} %collective-permute-done.13.refs_11_), channel_id=1, source_target_pairs={{0,4},{4,0},{8,12},{12,8},{1,5},{5,1},{9,13},{13,9},{2,6},{6,2},{1... | collective-permute-start | bytes 786440 | tf_op jit(solution)/shard_map/ppermute | solution.py:25
  54.1 11.8 %collective-permute-start.22 = (bf16[64,2048]{1,0:T(8,128)(2,1)S(1)}, bf16[64,2048]{1,0:T(8,128)(2,1)S(1)}, u32[]{:S(2)}, u32[]{:S(2)}) collective-permute-start(bf16[64,2048]{1,0:T(8,128)(2,1)S(1)} %collective-permute-done.13.refs_11_), channel_id=1, source_target_pairs={{0,16},{16,0},{1,17},{17,1},{2,18},{18,2},{3,19},{19,3},{4,20},{20... | collective-permute-start | bytes 786440 | tf_op jit(solution)/shard_map/ppermute | solution.py:25
  55.1 12.2 %collective-permute-start.20 = (bf16[64,2048]{1,0:T(8,128)(2,1)S(1)}, bf16[64,2048]{1,0:T(8,128)(2,1)S(1)}, u32[]{:S(2)}, u32[]{:S(2)}) collective-permute-start(bf16[64,2048]{1,0:T(8,128)(2,1)S(1)} %collective-permute-done.13.refs_11_), channel_id=1, source_target_pairs={{0,2},{1,3},{2,0},{3,1},{4,6},{5,7},{6,4},{7,5},{8,10},{9,11},{10,... | collective-permute-start | bytes 786440 | tf_op jit(solution)/shard_map/ppermute | solution.py:25
  61.7 7.4 %collective-permute-start.23 = (bf16[64,2048]{1,0:T(8,128)(2,1)S(1)}, bf16[64,2048]{1,0:T(8,128)(2,1)S(1)}, u32[]{:S(2)}, u32[]{:S(2)}) collective-permute-start(bf16[64,2048]{1,0:T(8,128)(2,1)S(1)} %collective-permute-done.14.refs_12_), channel_id=1, source_target_pairs={{0,16},{16,0},{1,17},{17,1},{2,18},{18,2},{3,19},{19,3},{4,20},{20... | collective-permute-start | bytes 786440 | tf_op jit(solution)/shard_map/ppermute | solution.py:25
  62.3 8.0 %collective-permute-start.21 = (bf16[64,2048]{1,0:T(8,128)(2,1)S(1)}, bf16[64,2048]{1,0:T(8,128)(2,1)S(1)}, u32[]{:S(2)}, u32[]{:S(2)}) collective-permute-start(bf16[64,2048]{1,0:T(8,128)(2,1)S(1)} %collective-permute-done.14.refs_12_), channel_id=1, source_target_pairs={{0,2},{1,3},{2,0},{3,1},{4,6},{5,7},{6,4},{7,5},{8,10},{9,11},{10,... | collective-permute-start | bytes 786440 | tf_op jit(solution)/shard_map/ppermute | solution.py:25
  70.3 11.6 %collective-permute-start.24 = (bf16[256,1024]{1,0:T(8,128)(2,1)S(1)}, bf16[256,1024]{1,0:T(8,128)(2,1)S(1)}, u32[]{:S(2)}, u32[]{:S(2)}) collective-permute-start(bf16[256,1024]{1,0:T(8,128)(2,1)S(1)} %get-tuple-element.91), channel_id=1, source_target_pairs={{0,16},{16,0},{1,17},{17,1},{2,18},{18,2},{3,19},{19,3},{4,20},{20... | collective-permute-start | bytes 1572872 | tf_op jit(solution)/shard_map/ppermute | solution.py:25
  71.0 11.0 %collective-permute-start.25 = (bf16[256,1024]{1,0:T(8,128)(2,1)S(1)}, bf16[256,1024]{1,0:T(8,128)(2,1)S(1)}, u32[]{:S(2)}, u32[]{:S(2)}) collective-permute-start(bf16[256,1024]{1,0:T(8,128)(2,1)S(1)} %get-tuple-element.92), channel_id=1, source_target_pairs={{0,2},{1,3},{2,0},{3,1},{4,6},{5,7},{6,4},{7,5},{8,10},{9,11},{10,... | collective-permute-start | bytes 1572872 | tf_op jit(solution)/shard_map/ppermute | solution.py:25
  82.0 13.5 %collective-permute-start.26 = (bf16[256,1024]{1,0:T(8,128)(2,1)S(1)}, bf16[256,1024]{1,0:T(8,128)(2,1)S(1)}, u32[]{:S(2)}, u32[]{:S(2)}) collective-permute-start(bf16[256,1024]{1,0:T(8,128)(2,1)S(1)} %get-tuple-element.93), channel_id=1, source_target_pairs={{0,16},{16,0},{1,17},{17,1},{2,18},{18,2},{3,19},{19,3},{4,20},{20... | collective-permute-start | bytes 1572872 | tf_op jit(solution)/shard_map/ppermute | solution.py:25
  83.5 11.9 %collective-permute-start.27 = (bf16[256,1024]{1,0:T(8,128)(2,1)S(1)}, bf16[256,1024]{1,0:T(8,128)(2,1)S(1)}, u32[]{:S(2)}, u32[]{:S(2)}) collective-permute-start(bf16[256,1024]{1,0:T(8,128)(2,1)S(1)} %get-tuple-element.94), channel_id=1, source_target_pairs={{0,2},{1,3},{2,0},{3,1},{4,6},{5,7},{6,4},{7,5},{8,10},{9,11},{10,... | collective-permute-start | bytes 1572872 | tf_op jit(solution)/shard_map/ppermute | solution.py:25
  95.5 9.0 %collective-permute-start.28 = (bf16[128,1024]{1,0:T(8,128)(2,1)S(1)}, bf16[128,1024]{1,0:T(8,128)(2,1)S(1)}, u32[]{:S(2)}, u32[]{:S(2)}) collective-permute-start(bf16[128,1024]{1,0:T(8,128)(2,1)S(1)} %get-tuple-element.108), channel_id=1, source_target_pairs={{0,16},{16,0},{1,17},{17,1},{2,18},{18,2},{3,19},{19,3},{4,20},{20... | collective-permute-start | bytes 786440 | tf_op jit(solution)/shard_map/ppermute | solution.py:25
  95.8 8.8 %collective-permute-start.29 = (bf16[128,1024]{1,0:T(8,128)(2,1)S(1)}, bf16[128,1024]{1,0:T(8,128)(2,1)S(1)}, u32[]{:S(2)}, u32[]{:S(2)}) collective-permute-start(bf16[128,1024]{1,0:T(8,128)(2,1)S(1)} %get-tuple-element.110), channel_id=1, source_target_pairs={{0,2},{1,3},{2,0},{3,1},{4,6},{5,7},{6,4},{7,5},{8,10},{9,11},{10,... | collective-permute-start | bytes 786440 | tf_op jit(solution)/shard_map/ppermute | solution.py:25
  104.7 8.7 %collective-permute-start.30 = (bf16[128,1024]{1,0:T(8,128)(2,1)S(1)}, bf16[128,1024]{1,0:T(8,128)(2,1)S(1)}, u32[]{:S(2)}, u32[]{:S(2)}) collective-permute-start(bf16[128,1024]{1,0:T(8,128)(2,1)S(1)} %get-tuple-element.111), channel_id=1, source_target_pairs={{0,16},{16,0},{1,17},{17,1},{2,18},{18,2},{3,19},{19,3},{4,20},{20... | collective-permute-start | bytes 786440 | tf_op jit(solution)/shard_map/ppermute | solution.py:25
  106.9 6.6 %collective-permute-start.32 = (bf16[128,1024]{1,0:T(8,128)(2,1)S(1)}, bf16[128,1024]{1,0:T(8,128)(2,1)S(1)}, u32[]{:S(2)}, u32[]{:S(2)}) collective-permute-start(bf16[128,1024]{1,0:T(8,128)(2,1)S(1)} %get-tuple-element.112), channel_id=1, source_target_pairs={{0,2},{1,3},{2,0},{3,1},{4,6},{5,7},{6,4},{7,5},{8,10},{9,11},{10,... | collective-permute-start | bytes 786440 | tf_op jit(solution)/shard_map/ppermute | solution.py:25
  106.9 9.4 %collective-permute-start.34 = (bf16[128,1024]{1,0:T(8,128)(2,1)S(1)}, bf16[128,1024]{1,0:T(8,128)(2,1)S(1)}, u32[]{:S(2)}, u32[]{:S(2)}) collective-permute-start(bf16[128,1024]{1,0:T(8,128)(2,1)S(1)} %add_convert_fusion.3), channel_id=1, source_target_pairs={{0,2},{1,3},{2,0},{3,1},{4,6},{5,7},{6,4},{7,5},{8,10},{9,11},{10,... | collective-permute-start | bytes 786440 | tf_op jit(solution)/shard_map/ppermute | solution.py:25
  108.9 7.4 %collective-permute-start.35 = (bf16[128,1024]{1,0:T(8,128)(2,1)S(1)}, bf16[128,1024]{1,0:T(8,128)(2,1)S(1)}, u32[]{:S(2)}, u32[]{:S(2)}) collective-permute-start(bf16[128,1024]{1,0:T(8,128)(2,1)S(1)} %add_convert_fusion.2), channel_id=1, source_target_pairs={{0,16},{16,0},{1,17},{17,1},{2,18},{18,2},{3,19},{19,3},{4,20},{20... | collective-permute-start | bytes 786440 | tf_op jit(solution)/shard_map/ppermute | solution.py:25
  113.4 6.4 %collective-permute-start.31 = (bf16[128,1024]{1,0:T(8,128)(2,1)S(1)}, bf16[128,1024]{1,0:T(8,128)(2,1)S(1)}, u32[]{:S(2)}, u32[]{:S(2)}) collective-permute-start(bf16[128,1024]{1,0:T(8,128)(2,1)S(1)} %add_convert_fusion.1), channel_id=1, source_target_pairs={{0,2},{1,3},{2,0},{3,1},{4,6},{5,7},{6,4},{7,5},{8,10},{9,11},{10,... | collective-permute-start | bytes 786440 | tf_op jit(solution)/shard_map/ppermute | solution.py:25
  113.6 6.4 %collective-permute-start.33 = (bf16[128,1024]{1,0:T(8,128)(2,1)S(1)}, bf16[128,1024]{1,0:T(8,128)(2,1)S(1)}, u32[]{:S(2)}, u32[]{:S(2)}) collective-permute-start(bf16[128,1024]{1,0:T(8,128)(2,1)S(1)} %add_convert_fusion), channel_id=1, source_target_pairs={{0,16},{16,0},{1,17},{17,1},{2,18},{18,2},{3,19},{19,3},{4,20},{20... | collective-permute-start | bytes 786440 | tf_op jit(solution)/shard_map/ppermute | solution.py:25
  116.6 19.4 %copy-start.6 = (bf16[1,64,2048]{2,1,0:T(8,128)(2,1)S(1)}, bf16[1,64,2048]{2,1,0:T(8,128)(2,1)}, u32[]{:S(2)}) copy-start(bf16[1,64,2048]{2,1,0:T(8,128)(2,1)} %param.12) | copy-start | bytes 786436
  116.6 19.4 %copy-start.8 = (bf16[64,2048]{1,0:T(8,128)(2,1)S(1)}, bf16[64,2048]{1,0:T(8,128)(2,1)}, u32[]{:S(2)}) copy-start(bf16[64,2048]{1,0:T(8,128)(2,1)} %copy-done.7) | copy-start | bytes 786436
  116.6 9.2 %collective-permute-start.37 = (bf16[64,2048]{1,0:T(8,128)(2,1)S(1)}, bf16[64,2048]{1,0:T(8,128)(2,1)S(1)}, u32[]{:S(2)}, u32[]{:S(2)}) collective-permute-start(bf16[64,2048]{1,0:T(8,128)(2,1)S(1)} %fusion.9), channel_id=1, source_target_pairs={{0,4},{4,0},{8,12},{12,8},{1,5},{5,1},{9,13},{13,9},{2,6},{6,2},{1... | collective-permute-start | bytes 786440 | tf_op jit(solution)/shard_map/ppermute | solution.py:25
  125.9 9.8 %collective-permute-start.38 = (bf16[64,2048]{1,0:T(8,128)(2,1)S(1)}, bf16[64,2048]{1,0:T(8,128)(2,1)S(1)}, u32[]{:S(2)}, u32[]{:S(2)}) collective-permute-start(bf16[64,2048]{1,0:T(8,128)(2,1)S(1)} %fusion.1), channel_id=1, source_target_pairs={{0,8},{4,12},{8,0},{12,4},{1,9},{5,13},{9,1},{13,5},{2,10},{6,14},... | collective-permute-start | bytes 786440 | tf_op jit(solution)/shard_map/ppermute | solution.py:25
  126.6 9.4 %collective-permute-start.36 = (bf16[64,2048]{1,0:T(8,128)(2,1)S(1)}, bf16[64,2048]{1,0:T(8,128)(2,1)S(1)}, u32[]{:S(2)}, u32[]{:S(2)}) collective-permute-start(bf16[64,2048]{1,0:T(8,128)(2,1)S(1)} %fusion.8), channel_id=1, source_target_pairs={{0,4},{4,0},{8,12},{12,8},{1,5},{5,1},{9,13},{13,9},{2,6},{6,2},{1... | collective-permute-start | bytes 786440 | tf_op jit(solution)/shard_map/ppermute | solution.py:25

commit v17 on v16

--- a/solution.py
+++ b/solution.py
@@ -140,8 +140,8 @@
             rows = kept + swap(leaving, "seq", bits).astype(jnp.float32)
         return rows
 
-    upper = folded(upper).astype(jnp.bfloat16)
-    return folded(lower) + swap(upper, "seq", top_bits).astype(jnp.float32)
+    upper, lower = ready(folded(upper).astype(jnp.bfloat16), folded(lower))
+    return lower + swap(upper, "seq", top_bits).astype(jnp.float32)
 
 
 def prepare_kernel(*refs):

time: 137 us -> 140 us (1.022)
  waiting for transfers between devices: 63 us -> 67.4 us
  starting transfers between devices: 43.8 us -> 42.2 us
    ppermute x39, waiting for transfers between devices: 63 us -> 67.4 us  [swap(): return lax.ppermute(block, axis, [(i, i ^ bits) for i in range(size)])]
    ppermute x39, starting transfers between devices: 43.8 us -> 42.2 us  [swap(): return lax.ppermute(block, axis, [(i, i ^ bits) for i in range(size)])]
  transfers between devices with their start and end apart: 39 -> 39, of which waited for: 24 -> 24; matrix products, arithmetic and copies ran while one was open for 1% -> 1% of each run, Pallas kernels for 20% -> 19%
where the time goes in v17:
time: 140 us
  waiting for transfers between devices  67.4 us (48%)
  starting transfers between devices  42.2 us (30%)
  Pallas kernels  27 us (19%)
  other arithmetic  2.4 us (2%)
    ppermute x39, waiting for transfers between devices, swap(): return lax.ppermute(block, axis, [(i, i ^ bits) for i in range(size)])  67.4 us
    ppermute x39, starting transfers between devices, swap(): return lax.ppermute(block, axis, [(i, i ^ bits) for i in range(size)])  42.2 us
    pallas_call x2, Pallas kernels, run_experts(): pl.pallas_call(lambda *refs: expert_kernel(first, spots, cuts, *refs), ou...  19.2 us
  transfers between devices with their start and end apart: 39, of which 24 were waited for; matrix products, arithmetic and copies ran while one was open for 1% of the time, Pallas kernels for 19%

profile of v17, /device:TPU:0, one launch (start us, length us, event | category | flops | bytes accessed | tf_op | source)
XLA Modules:
  0.0 139.8 jit_solution(15579150414028939926)
XLA Ops:
  0.0 0.5 collective-permute-start.12
  0.5 2.6 %prepare.1 = (bf16[64,2048]{1,0:T(8,128)(2,1)S(1)}, bf16[64,640]{1,0:T(8,128)(2,1)S(1)}) custom-call(bf16[64,2048]{1,0:T(8,128)(2,1)} %bitcast.49, f32[1,2048]{1,0:T(1,128)} %bitcast.54, bf16[2,2048,256]{2,1,0:T(8,128)(2,1)} %refs_2_.1, f32[1,128]{1,0:T(1,128)} %bitcast.57, s32[8,64]{1,0:T(8,128)} %bitcast.55, s32[8,64]{1,0:T(8,128)} %bitcast.56), custom_call_target="tpu_custom_call" | custom-call | flops 134217728 | bytes 2621440 | tf_op jit(solution)/shard_map/prepare/pallas_call | solution.py:187
  3.1 4.7 %collective-permute-start.2 = (bf16[64,640]{1,0:T(8,128)(2,1)S(1)}, bf16[64,640]{1,0:T(8,128)(2,1)S(1)}, u32[]{:S(2)}, u32[]{:S(2)}) collective-permute-start(bf16[64,640]{1,0:T(8,128)(2,1)S(1)} %get-tuple-element.64), channel_id=1, source_target_pairs={{0,12},{4,8},{8,4},{12,0},{1,13},{5,9},{9,5},{13,1},{2,14},{6,10},... | collective-permute-start | bytes 245768 | tf_op jit(solution)/shard_map/ppermute | solution.py:25
  7.7 0.6 collective-permute-start
  8.4 1.7 %collective-permute-start.3 = (bf16[64,2048]{1,0:T(8,128)(2,1)S(1)}, bf16[64,2048]{1,0:T(8,128)(2,1)S(1)}, u32[]{:S(2)}, u32[]{:S(2)}) collective-permute-start(bf16[64,2048]{1,0:T(8,128)(2,1)S(1)} %get-tuple-element.66.first_ref), channel_id=1, source_target_pairs={{0,2},{1,3},{2,0},{3,1},{4,6},{5,7},{6,4},{7,5},{8,10},{9,11},{10,... | collective-permute-start | bytes 786440 | tf_op jit(solution)/shard_map/ppermute | solution.py:25
  10.0 3.5 %collective-permute-done = bf16[64,640]{1,0:T(8,128)(2,1)S(1)} collective-permute-done((bf16[64,640]{1,0:T(8,128)(2,1)S(1)}, bf16[64,640]{1,0:T(8,128)(2,1)S(1)}, u32[]{:S(2)}, u32[]{:S(2)}) %collective-permute-start) | collective-permute-done | bytes 81952 | tf_op jit(solution)/shard_map/ppermute | solution.py:25
  13.5 1.6 %collective-permute-done.1 = bf16[64,640]{1,0:T(8,128)(2,1)S(1)} collective-permute-done((bf16[64,640]{1,0:T(8,128)(2,1)S(1)}, bf16[64,640]{1,0:T(8,128)(2,1)S(1)}, u32[]{:S(2)}, u32[]{:S(2)}) %collective-permute-start.1) | collective-permute-done | bytes 81952 | tf_op jit(solution)/shard_map/ppermute | solution.py:25
  15.3 1.1 collective-permute-done.3.second_ref
  16.4 1.5 %collective-permute-start.6 = (bf16[256,384]{1,0:T(8,128)(2,1)S(1)}, bf16[256,384]{1,0:T(8,128)(2,1)S(1)}, u32[]{:S(2)}, u32[]{:S(2)}) collective-permute-start(bf16[256,384]{1,0:T(8,128)(2,1)S(1)} %pad_maximum_fusion.4), channel_id=1, source_target_pairs={{0,2},{1,3},{2,0},{3,1},{4,6},{5,7},{6,4},{7,5},{8,10},{9,11},{10,... | collective-permute-start | bytes 589832 | tf_op jit(solution)/shard_map/ppermute | solution.py:25
  17.9 0.5 collective-permute-start.5
  18.4 3.7 %collective-permute-done.6 = bf16[256,384]{1,0:T(8,128)(2,1)S(1)} collective-permute-done((bf16[256,384]{1,0:T(8,128)(2,1)S(1)}, bf16[256,384]{1,0:T(8,128)(2,1)S(1)}, u32[]{:S(2)}, u32[]{:S(2)}) %collective-permute-start.6) | collective-permute-done | bytes 196640 | tf_op jit(solution)/shard_map/ppermute | solution.py:25
  22.3 0.9 queries.1.refs_0_
  23.2 0.6 collective-permute-done.7.refs_2_
  23.7 2.7 %attend.1 = (f32[128,2048]{1,0:T(8,128)S(1)}, bf16[128,2048]{1,0:T(8,128)(2,1)S(1)}) custom-call(bf16[256,512]{1,0:T(8,128)(2,1)S(1)} %queries.1.refs_0_, bf16[512,256]{1,0:T(8,128)(2,1)S(1)} %pad_maximum_fusion.2.refs_1_, bf16[512,256]{1,0:T(8,128)(2,1)S(1)} %collective-permute-done.7.refs_2_, bf16[512,2048]{1,0:T(8,128)(2,1)S(1)} %copy-done.2), custom_call_target="tpu_custom_call" | custom-call | flops 1073741824 | bytes 4194304 | tf_op jit(solution)/shard_map/attend/pallas_call | solution.py:266
  26.5 0.2 collective-permute-start.8
  26.7 1.8 %collective-permute-done.8 = bf16[128,2048]{1,0:T(8,128)(2,1)S(1)} collective-permute-done((bf16[128,2048]{1,0:T(8,128)(2,1)S(1)}, bf16[128,2048]{1,0:T(8,128)(2,1)S(1)}, u32[]{:S(2)}, u32[]{:S(2)}) %collective-permute-start.8) | collective-permute-done | bytes 524320 | tf_op jit(solution)/shard_map/ppermute | solution.py:25
  28.5 0.1 collective-permute-start.11
  28.8 1.5 %collective-permute-start.9 = (bf16[64,2048]{1,0:T(8,128)(2,1)S(1)}, bf16[64,2048]{1,0:T(8,128)(2,1)S(1)}, u32[]{:S(2)}, u32[]{:S(2)}) collective-permute-start(bf16[64,2048]{1,0:T(8,128)(2,1)S(1)} %slice.137), channel_id=1, source_target_pairs={{0,2},{1,3},{2,0},{3,1},{4,6},{5,7},{6,4},{7,5},{8,10},{9,11},{10,... | collective-permute-start | bytes 786440 | tf_op jit(solution)/shard_map/ppermute | solution.py:25
  30.3 1.6 %collective-permute-start.10 = (bf16[2,256,128]{2,1,0:T(8,128)(2,1)S(1)}, bf16[2,256,128]{2,1,0:T(8,128)(2,1)S(1)}, u32[]{:S(2)}, u32[]{:S(2)}) collective-permute-start(bf16[2,256,128]{2,1,0:T(8,128)(2,1)S(1)} %pad_maximum_fusion.5), channel_id=1, source_target_pairs={{0,16},{16,0},{1,17},{17,1},{2,18},{18,2},{3,19},{19,3},{4,20},{20... | collective-permute-start | bytes 393224 | tf_op jit(solution)/shard_map/ppermute | solution.py:25
  31.9 4.0 %collective-permute-done.10 = bf16[2,256,128]{2,1,0:T(8,128)(2,1)S(1)} collective-permute-done((bf16[2,256,128]{2,1,0:T(8,128)(2,1)S(1)}, bf16[2,256,128]{2,1,0:T(8,128)(2,1)S(1)}, u32[]{:S(2)}, u32[]{:S(2)}) %collective-permute-start.10) | collective-permute-done | bytes 131104 | tf_op jit(solution)/shard_map/ppermute | solution.py:25
  35.9 1.5 %collective-permute-done.9 = bf16[64,2048]{1,0:T(8,128)(2,1)S(1)} collective-permute-done((bf16[64,2048]{1,0:T(8,128)(2,1)S(1)}, bf16[64,2048]{1,0:T(8,128)(2,1)S(1)}, u32[]{:S(2)}, u32[]{:S(2)}) %collective-permute-start.9) | collective-permute-done | bytes 262176 | tf_op jit(solution)/shard_map/ppermute | solution.py:25
  37.4 0.2 multiply_reduce_fusion
  37.6 0.1 multiply_convert_fusion.refs_9_
  37.8 1.5 %collective-permute-start.15 = (bf16[64,2048]{1,0:T(8,128)(2,1)S(1)}, bf16[64,2048]{1,0:T(8,128)(2,1)S(1)}, u32[]{:S(2)}, u32[]{:S(2)}) collective-permute-start(bf16[64,2048]{1,0:T(8,128)(2,1)S(1)} %multiply_convert_fusion.refs_9_), channel_id=1, source_target_pairs={{0,4},{4,0},{8,12},{12,8},{1,5},{5,1},{9,13},{13,9},{2,6},{6,2},{1... | collective-permute-start | bytes 786440 | tf_op jit(solution)/shard_map/ppermute | solution.py:25
  39.2 2.6 %collective-permute-start.13 = (bf16[64,2048]{1,0:T(8,128)(2,1)S(1)}, bf16[64,2048]{1,0:T(8,128)(2,1)S(1)}, u32[]{:S(2)}, u32[]{:S(2)}) collective-permute-start(bf16[64,2048]{1,0:T(8,128)(2,1)S(1)} %multiply_convert_fusion.refs_9_), channel_id=1, source_target_pairs={{0,8},{4,12},{8,0},{12,4},{1,9},{5,13},{9,1},{13,5},{2,10},{6,14},... | collective-permute-start | bytes 786440 | tf_op jit(solution)/shard_map/ppermute | solution.py:25
  41.8 1.5 %collective-permute-start.19 = (bf16[64,2048]{1,0:T(8,128)(2,1)S(1)}, bf16[64,2048]{1,0:T(8,128)(2,1)S(1)}, u32[]{:S(2)}, u32[]{:S(2)}) collective-permute-start(bf16[64,2048]{1,0:T(8,128)(2,1)S(1)} %multiply_convert_fusion.refs_9_), channel_id=1, source_target_pairs={{0,16},{16,0},{1,17},{17,1},{2,18},{18,2},{3,19},{19,3},{4,20},{20... | collective-permute-start | bytes 786440 | tf_op jit(solution)/shard_map/ppermute | solution.py:25
  43.3 1.5 %collective-permute-start.18 = (bf16[64,2048]{1,0:T(8,128)(2,1)S(1)}, bf16[64,2048]{1,0:T(8,128)(2,1)S(1)}, u32[]{:S(2)}, u32[]{:S(2)}) collective-permute-start(bf16[64,2048]{1,0:T(8,128)(2,1)S(1)} %multiply_convert_fusion.refs_9_), channel_id=1, source_target_pairs={{0,2},{1,3},{2,0},{3,1},{4,6},{5,7},{6,4},{7,5},{8,10},{9,11},{10,... | collective-permute-start | bytes 786440 | tf_op jit(solution)/shard_map/ppermute | solution.py:25
  44.8 6.2 %collective-permute-done.15.refs_10_ = bf16[64,2048]{1,0:T(8,128)(2,1)S(1)} collective-permute-done((bf16[64,2048]{1,0:T(8,128)(2,1)S(1)}, bf16[64,2048]{1,0:T(8,128)(2,1)S(1)}, u32[]{:S(2)}, u32[]{:S(2)}) %collective-permute-start.15) | collective-permute-done | bytes 262176 | tf_op jit(solution)/shard_map/ppermute | solution.py:25
  51.0 1.4 %collective-permute-start.17 = (bf16[64,2048]{1,0:T(8,128)(2,1)S(1)}, bf16[64,2048]{1,0:T(8,128)(2,1)S(1)}, u32[]{:S(2)}, u32[]{:S(2)}) collective-permute-start(bf16[64,2048]{1,0:T(8,128)(2,1)S(1)} %collective-permute-done.15.refs_10_), channel_id=1, source_target_pairs={{0,16},{16,0},{1,17},{17,1},{2,18},{18,2},{3,19},{19,3},{4,20},{20... | collective-permute-start | bytes 786440 | tf_op jit(solution)/shard_map/ppermute | solution.py:25
  52.4 1.5 %collective-permute-start.16 = (bf16[64,2048]{1,0:T(8,128)(2,1)S(1)}, bf16[64,2048]{1,0:T(8,128)(2,1)S(1)}, u32[]{:S(2)}, u32[]{:S(2)}) collective-permute-start(bf16[64,2048]{1,0:T(8,128)(2,1)S(1)} %collective-permute-done.15.refs_10_), channel_id=1, source_target_pairs={{0,2},{1,3},{2,0},{3,1},{4,6},{5,7},{6,4},{7,5},{8,10},{9,11},{10,... | collective-permute-start | bytes 786440 | tf_op jit(solution)/shard_map/ppermute | solution.py:25
  54.1 1.1 collective-permute-start.22
  55.1 1.5 %collective-permute-start.20 = (bf16[64,2048]{1,0:T(8,128)(2,1)S(1)}, bf16[64,2048]{1,0:T(8,128)(2,1)S(1)}, u32[]{:S(2)}, u32[]{:S(2)}) collective-permute-start(bf16[64,2048]{1,0:T(8,128)(2,1)S(1)} %collective-permute-done.13.refs_11_), channel_id=1, source_target_pairs={{0,2},{1,3},{2,0},{3,1},{4,6},{5,7},{6,4},{7,5},{8,10},{9,11},{10,... | collective-permute-start | bytes 786440 | tf_op jit(solution)/shard_map/ppermute | solution.py:25
  56.6 1.6 %tables.1 = (bf16[4,224,256]{2,1,0:T(8,128)(2,1)S(1)}, bf16[2,4,256,112]{3,2,1,0:T(8,128)(2,1)S(1)}, f32[4,256,2]{2,1,0:T(8,128)S(1)}) custom-call(s32[1]{0:T(128)} %bitcast.12.refs_0_, bf16[4,256,128]{2,1,0:T(8,128)(2,1)S(1)} %pad_maximum_fusion.3.refs_1_), custom_call_target="tpu_custom_call" | custom-call | flops 134217728 | bytes 917504 | tf_op jit(solution)/shard_map/tables/pallas_call | solution.py:332
  58.2 2.0 %collective-permute-done.17.refs_12_.refs_5_ = bf16[64,2048]{1,0:T(8,128)(2,1)S(1)} collective-permute-done((bf16[64,2048]{1,0:T(8,128)(2,1)S(1)}, bf16[64,2048]{1,0:T(8,128)(2,1)S(1)}, u32[]{:S(2)}, u32[]{:S(2)}) %collective-permute-start.17) | collective-permute-done | bytes 262176 | tf_op jit(solution)/shard_map/ppermute | solution.py:25
  60.2 1.4 %collective-permute-done.16.refs_8_.refs_1_ = bf16[64,2048]{1,0:T(8,128)(2,1)S(1)} collective-permute-done((bf16[64,2048]{1,0:T(8,128)(2,1)S(1)}, bf16[64,2048]{1,0:T(8,128)(2,1)S(1)}, u32[]{:S(2)}, u32[]{:S(2)}) %collective-permute-start.16) | collective-permute-done | bytes 262176 | tf_op jit(solution)/shard_map/ppermute | solution.py:25
  61.7 0.6 collective-permute-start.23
  62.3 1.5 %collective-permute-start.21 = (bf16[64,2048]{1,0:T(8,128)(2,1)S(1)}, bf16[64,2048]{1,0:T(8,128)(2,1)S(1)}, u32[]{:S(2)}, u32[]{:S(2)}) collective-permute-start(bf16[64,2048]{1,0:T(8,128)(2,1)S(1)} %collective-permute-done.14.refs_12_), channel_id=1, source_target_pairs={{0,2},{1,3},{2,0},{3,1},{4,6},{5,7},{6,4},{7,5},{8,10},{9,11},{10,... | collective-permute-start | bytes 786440 | tf_op jit(solution)/shard_map/ppermute | solution.py:25
  63.7 2.1 %collective-permute-done.22.refs_13_.refs_6_ = bf16[64,2048]{1,0:T(8,128)(2,1)S(1)} collective-permute-done((bf16[64,2048]{1,0:T(8,128)(2,1)S(1)}, bf16[64,2048]{1,0:T(8,128)(2,1)S(1)}, u32[]{:S(2)}, u32[]{:S(2)}) %collective-permute-start.22) | collective-permute-done | bytes 262176 | tf_op jit(solution)/shard_map/ppermute | solution.py:25
  65.9 1.4 %collective-permute-done.20.refs_9_.refs_2_ = bf16[64,2048]{1,0:T(8,128)(2,1)S(1)} collective-permute-done((bf16[64,2048]{1,0:T(8,128)(2,1)S(1)}, bf16[64,2048]{1,0:T(8,128)(2,1)S(1)}, u32[]{:S(2)}, u32[]{:S(2)}) %collective-permute-start.20) | collective-permute-done | bytes 262176 | tf_op jit(solution)/shard_map/ppermute | solution.py:25
  67.3 1.8 %collective-permute-done.23.refs_14_.refs_7_ = bf16[64,2048]{1,0:T(8,128)(2,1)S(1)} collective-permute-done((bf16[64,2048]{1,0:T(8,128)(2,1)S(1)}, bf16[64,2048]{1,0:T(8,128)(2,1)S(1)}, u32[]{:S(2)}, u32[]{:S(2)}) %collective-permute-start.23) | collective-permute-done | bytes 262176 | tf_op jit(solution)/shard_map/ppermute | solution.py:25
  69.1 1.2 collective-permute-done.21.refs_10_.refs_3_
  70.3 0.7 collective-permute-start.24
  71.0 1.5 %collective-permute-start.25 = (bf16[256,1024]{1,0:T(8,128)(2,1)S(1)}, bf16[256,1024]{1,0:T(8,128)(2,1)S(1)}, u32[]{:S(2)}, u32[]{:S(2)}) collective-permute-start(bf16[256,1024]{1,0:T(8,128)(2,1)S(1)} %get-tuple-element.94), channel_id=1, source_target_pairs={{0,2},{1,3},{2,0},{3,1},{4,6},{5,7},{6,4},{7,5},{8,10},{9,11},{10,... | collective-permute-start | bytes 1572872 | tf_op jit(solution)/shard_map/ppermute | solution.py:25
  72.4 9.5 %experts.2 = (bf16[256,1024]{1,0:T(8,128)(2,1)S(1)}, bf16[256,1024]{1,0:T(8,128)(2,1)S(1)}, bf16[256,1024]{1,0:T(8,128)(2,1)S(1)}, bf16[256,1024]{1,0:T(8,128)(2,1)S(1)}) custom-call(bf16[4,224,256]{2,1,0:T(8,128)(2,1)S(1)} %get-tuple-element.78.refs_0_, bf16[2,4,256,112]{3,2,1,0:T(8,128)(2,1)S(1)} %get-tuple-element.79.refs_1_, ...), custom_call_target="tpu_custom_call" | custom-call | flops 4227858432 | bytes 23068672 | tf_op jit(solution)/shard_map/experts/pallas_call | solution.py:462
  82.0 1.5 %collective-permute-start.26 = (bf16[256,1024]{1,0:T(8,128)(2,1)S(1)}, bf16[256,1024]{1,0:T(8,128)(2,1)S(1)}, u32[]{:S(2)}, u32[]{:S(2)}) collective-permute-start(bf16[256,1024]{1,0:T(8,128)(2,1)S(1)} %get-tuple-element.95), channel_id=1, source_target_pairs={{0,16},{16,0},{1,17},{17,1},{2,18},{18,2},{3,19},{19,3},{4,20},{20... | collective-permute-start | bytes 1572872 | tf_op jit(solution)/shard_map/ppermute | solution.py:25
  83.5 2.2 %collective-permute-start.27 = (bf16[256,1024]{1,0:T(8,128)(2,1)S(1)}, bf16[256,1024]{1,0:T(8,128)(2,1)S(1)}, u32[]{:S(2)}, u32[]{:S(2)}) collective-permute-start(bf16[256,1024]{1,0:T(8,128)(2,1)S(1)} %get-tuple-element.96), channel_id=1, source_target_pairs={{0,2},{1,3},{2,0},{3,1},{4,6},{5,7},{6,4},{7,5},{8,10},{9,11},{10,... | collective-permute-start | bytes 1572872 | tf_op jit(solution)/shard_map/ppermute | solution.py:25
  85.7 9.7 %experts.3 = (bf16[128,1024]{1,0:T(8,128)(2,1)S(1)}, bf16[128,1024]{1,0:T(8,128)(2,1)S(1)}, bf16[128,1024]{1,0:T(8,128)(2,1)S(1)}, bf16[128,1024]{1,0:T(8,128)(2...) custom-call(bf16[4,224,256]{2,1,0:T(8,128)(2,1)S(1)} %get-tuple-element.78.refs_0_, ...), custom_call_target="tpu_custom_call" | custom-call | flops 4227858432 | bytes 23068672 | tf_op jit(solution)/shard_map/experts/pallas_call | solution.py:462
  95.5 0.3 collective-permute-start.28
  95.8 0.4 collective-permute-start.30
  96.2 8.2 %collective-permute-done.28 = bf16[128,1024]{1,0:T(8,128)(2,1)S(1)} collective-permute-done((bf16[128,1024]{1,0:T(8,128)(2,1)S(1)}, bf16[128,1024]{1,0:T(8,128)(2,1)S(1)}, u32[]{:S(2)}, u32[]{:S(2)}) %collective-permute-start.28) | collective-permute-done | bytes 262176 | tf_op jit(solution)/shard_map/ppermute | solution.py:25
  104.7 2.2 %collective-permute-start.33 = (bf16[128,1024]{1,0:T(8,128)(2,1)S(1)}, bf16[128,1024]{1,0:T(8,128)(2,1)S(1)}, u32[]{:S(2)}, u32[]{:S(2)}) collective-permute-start(bf16[128,1024]{1,0:T(8,128)(2,1)S(1)} %get-tuple-element.115), channel_id=1, source_target_pairs={{0,16},{16,0},{1,17},{17,1},{2,18},{18,2},{3,19},{19,3},{4,20},{20... | collective-permute-start | bytes 786440 | tf_op jit(solution)/shard_map/ppermute | solution.py:25
  106.9 2.0 %collective-permute-start.29 = (bf16[128,1024]{1,0:T(8,128)(2,1)S(1)}, bf16[128,1024]{1,0:T(8,128)(2,1)S(1)}, u32[]{:S(2)}, u32[]{:S(2)}) collective-permute-start(bf16[128,1024]{1,0:T(8,128)(2,1)S(1)} %add_convert_fusion.4), channel_id=1, source_target_pairs={{0,2},{1,3},{2,0},{3,1},{4,6},{5,7},{6,4},{7,5},{8,10},{9,11},{10,... | collective-permute-start | bytes 786440 | tf_op jit(solution)/shard_map/ppermute | solution.py:25
  109.0 4.4 %collective-permute-done.33 = bf16[128,1024]{1,0:T(8,128)(2,1)S(1)} collective-permute-done((bf16[128,1024]{1,0:T(8,128)(2,1)S(1)}, bf16[128,1024]{1,0:T(8,128)(2,1)S(1)}, u32[]{:S(2)}, u32[]{:S(2)}) %collective-permute-start.33) | collective-permute-done | bytes 262176 | tf_op jit(solution)/shard_map/ppermute | solution.py:25
  113.6 2.0 %collective-permute-start.36 = (bf16[128,1024]{1,0:T(8,128)(2,1)S(1)}, bf16[128,1024]{1,0:T(8,128)(2,1)S(1)}, u32[]{:S(2)}, u32[]{:S(2)}) collective-permute-start(bf16[128,1024]{1,0:T(8,128)(2,1)S(1)} %add_convert_fusion.1), channel_id=1, source_target_pairs={{0,16},{16,0},{1,17},{17,1},{2,18},{18,2},{3,19},{19,3},{4,20},{20... | collective-permute-start | bytes 786440 | tf_op jit(solution)/shard_map/ppermute | solution.py:25
  115.6 0.6 collective-permute-done.29
  116.3 0.1 convert_add_fusion.3
  116.7 3.2 %collective-permute-done.34 = bf16[128,1024]{1,0:T(8,128)(2,1)S(1)} collective-permute-done((bf16[128,1024]{1,0:T(8,128)(2,1)S(1)}, bf16[128,1024]{1,0:T(8,128)(2,1)S(1)}, u32[]{:S(2)}, u32[]{:S(2)}) %collective-permute-start.34) | collective-permute-done | bytes 262176 | tf_op jit(solution)/shard_map/ppermute | solution.py:25
  119.8 0.2 collective-permute-done.36
  120.0 0.3 convert_add_fusion.1
  120.5 3.3 %collective-permute-done.32 = bf16[64,2048]{1,0:T(8,128)(2,1)S(1)} collective-permute-done((bf16[64,2048]{1,0:T(8,128)(2,1)S(1)}, bf16[64,2048]{1,0:T(8,128)(2,1)S(1)}, u32[]{:S(2)}, u32[]{:S(2)}) %collective-permute-start.32) | collective-permute-done | bytes 262176 | tf_op jit(solution)/shard_map/ppermute | solution.py:25
  123.9 4.8 %collective-permute-done.37 = bf16[64,2048]{1,0:T(8,128)(2,1)S(1)} collective-permute-done((bf16[64,2048]{1,0:T(8,128)(2,1)S(1)}, bf16[64,2048]{1,0:T(8,128)(2,1)S(1)}, u32[]{:S(2)}, u32[]{:S(2)}) %collective-permute-start.37) | collective-permute-done | bytes 262176 | tf_op jit(solution)/shard_map/ppermute | solution.py:25
  128.8 1.4 collective-permute-start.38
  130.2 8.8 %collective-permute-done.38 = bf16[64,2048]{1,0:T(8,128)(2,1)S(1)} collective-permute-done((bf16[64,2048]{1,0:T(8,128)(2,1)S(1)}, bf16[64,2048]{1,0:T(8,128)(2,1)S(1)}, u32[]{:S(2)}, u32[]{:S(2)}) %collective-permute-start.38) | collective-permute-done | bytes 262176 | tf_op jit(solution)/shard_map/ppermute | solution.py:25
  139.0 0.8 fusion.4
  (71 shorter events, 1.8 us)
Async XLA Ops:
  0.0 22.2 %copy-start.1 = (f32[128]{0:T(128)S(1)}, f32[128]{0:T(128)}, u32[]{:S(2)}) copy-start(f32[128]{0:T(128)} %param.16) | copy-start | bytes 1540
  0.0 22.2 %copy-start = (bf16[2048,512]{1,0:T(8,128)(2,1)S(1)}, bf16[2048,512]{1,0:T(8,128)(2,1)}, u32[]{:S(2)}) copy-start(bf16[2048,512]{1,0:T(8,128)(2,1)} %weight_ref.1) | copy-start | bytes 6291460
  0.0 37.4 %collective-permute-start.12 = (bf16[2048,1536]{1,0:T(8,128)(2,1)}, bf16[2048,1536]{1,0:T(8,128)(2,1)}, u32[]{:S(2)}, u32[]{:S(2)}) collective-permute-start(bf16[2048,1536]{1,0:T(8,128)(2,1)} %bitcast.43), channel_id=1, source_target_pairs={{0,1},{1,0},{2,3},{3,2},{4,5},{5,4},{6,7},{7,6},{8,9},{9,8},{10,11... | collective-permute-start | bytes 18874376 | tf_op jit(solution)/shard_map/ppermute | solution.py:25
  3.1 12.0 %collective-permute-start.2 = (bf16[64,640]{1,0:T(8,128)(2,1)S(1)}, bf16[64,640]{1,0:T(8,128)(2,1)S(1)}, u32[]{:S(2)}, u32[]{:S(2)}) collective-permute-start(bf16[64,640]{1,0:T(8,128)(2,1)S(1)} %get-tuple-element.64), channel_id=1, source_target_pairs={{0,12},{4,8},{8,4},{12,0},{1,13},{5,9},{9,5},{13,1},{2,14},{6,10},... | collective-permute-start | bytes 245768 | tf_op jit(solution)/shard_map/ppermute | solution.py:25
  7.7 7.4 %collective-permute-start.1 = (bf16[64,640]{1,0:T(8,128)(2,1)S(1)}, bf16[64,640]{1,0:T(8,128)(2,1)S(1)}, u32[]{:S(2)}, u32[]{:S(2)}) collective-permute-start(bf16[64,640]{1,0:T(8,128)(2,1)S(1)} %get-tuple-element.64), channel_id=1, source_target_pairs={{0,8},{4,12},{8,0},{12,4},{1,9},{5,13},{9,1},{13,5},{2,10},{6,14},... | collective-permute-start | bytes 245768 | tf_op jit(solution)/shard_map/ppermute | solution.py:25
  7.7 5.8 %collective-permute-start = (bf16[64,640]{1,0:T(8,128)(2,1)S(1)}, bf16[64,640]{1,0:T(8,128)(2,1)S(1)}, u32[]{:S(2)}, u32[]{:S(2)}) collective-permute-start(bf16[64,640]{1,0:T(8,128)(2,1)S(1)} %get-tuple-element.64), channel_id=1, source_target_pairs={{0,4},{4,0},{8,12},{12,8},{1,5},{5,1},{9,13},{13,9},{2,6},{6,2},{1... | collective-permute-start | bytes 245768 | tf_op jit(solution)/shard_map/ppermute | solution.py:25
  8.4 8.0 %collective-permute-start.3 = (bf16[64,2048]{1,0:T(8,128)(2,1)S(1)}, bf16[64,2048]{1,0:T(8,128)(2,1)S(1)}, u32[]{:S(2)}, u32[]{:S(2)}) collective-permute-start(bf16[64,2048]{1,0:T(8,128)(2,1)S(1)} %get-tuple-element.66.first_ref), channel_id=1, source_target_pairs={{0,2},{1,3},{2,0},{3,1},{4,6},{5,7},{6,4},{7,5},{8,10},{9,11},{10,... | collective-permute-start | bytes 786440 | tf_op jit(solution)/shard_map/ppermute | solution.py:25
  10.0 13.7 %copy-start.2 = (bf16[512,2048]{1,0:T(8,128)(2,1)S(1)}, bf16[512,2048]{1,0:T(8,128)(2,1)}, u32[]{:S(2)}) copy-start(bf16[512,2048]{1,0:T(8,128)(2,1)} %refs_3_.1) | copy-start | bytes 6291460
  16.4 5.7 %collective-permute-start.6 = (bf16[256,384]{1,0:T(8,128)(2,1)S(1)}, bf16[256,384]{1,0:T(8,128)(2,1)S(1)}, u32[]{:S(2)}, u32[]{:S(2)}) collective-permute-start(bf16[256,384]{1,0:T(8,128)(2,1)S(1)} %pad_maximum_fusion.4), channel_id=1, source_target_pairs={{0,2},{1,3},{2,0},{3,1},{4,6},{5,7},{6,4},{7,5},{8,10},{9,11},{10,... | collective-permute-start | bytes 589832 | tf_op jit(solution)/shard_map/ppermute | solution.py:25
  17.9 4.3 %collective-permute-start.4 = (bf16[64,2048]{1,0:T(8,128)(2,1)S(1)}, bf16[64,2048]{1,0:T(8,128)(2,1)S(1)}, u32[]{:S(2)}, u32[]{:S(2)}) collective-permute-start(bf16[64,2048]{1,0:T(8,128)(2,1)S(1)} %get-tuple-element.66.first_ref), channel_id=1, source_target_pairs={{0,1},{1,0},{2,3},{3,2},{4,5},{5,4},{6,7},{7,6},{8,9},{9,8},{10,11... | collective-permute-start | bytes 786440 | tf_op jit(solution)/shard_map/ppermute | solution.py:25
  17.9 4.3 %collective-permute-start.5 = (bf16[64,2048]{1,0:T(8,128)(2,1)S(1)}, bf16[64,2048]{1,0:T(8,128)(2,1)S(1)}, u32[]{:S(2)}, u32[]{:S(2)}) collective-permute-start(bf16[64,2048]{1,0:T(8,128)(2,1)S(1)} %collective-permute-done.3.second_ref), channel_id=1, source_target_pairs={{0,1},{1,0},{2,3},{3,2},{4,5},{5,4},{6,7},{7,6},{8,9},{9,8},{10,11... | collective-permute-start | bytes 786440 | tf_op jit(solution)/shard_map/ppermute | solution.py:25
  22.1 1.6 %collective-permute-start.7 = (bf16[512,256]{1,0:T(8,128)(2,1)S(1)}, bf16[512,256]{1,0:T(8,128)(2,1)S(1)}, u32[]{:S(2)}, u32[]{:S(2)}) collective-permute-start(bf16[512,256]{1,0:T(8,128)(2,1)S(1)} %pad_maximum_fusion.2.refs_1_), channel_id=1, source_target_pairs={{0,1},{1,0},{2,3},{3,2},{4,5},{5,4},{6,7},{7,6},{8,9},{9,8},{10,11... | collective-permute-start | bytes 786440 | tf_op jit(solution)/shard_map/ppermute | solution.py:25
  22.3 6.2 %copy-start.3 = (bf16[1,768,2048]{2,1,0:T(8,128)(2,1)S(1)}, bf16[1,768,2048]{2,1,0:T(8,128)(2,1)}, u32[]{:S(2)}) copy-start(bf16[1,768,2048]{2,1,0:T(8,128)(2,1)} %param.23) | copy-start | bytes 9437188
  23.1 14.3 %copy-start.5 = (bf16[1,64,2048]{2,1,0:T(8,128)(2,1)S(1)}, bf16[1,64,2048]{2,1,0:T(8,128)(2,1)}, u32[]{:S(2)}) copy-start(bf16[1,64,2048]{2,1,0:T(8,128)(2,1)} %param.12) | copy-start | bytes 786436
  26.5 11.2 %copy-start.9 = (f32[2048]{0:T(1024)S(1)}, f32[2048]{0:T(1024)}, u32[]{:S(2)}) copy-start(f32[2048]{0:T(1024)} %param.19) | copy-start | bytes 24580
  26.5 2.0 %collective-permute-start.8 = (bf16[128,2048]{1,0:T(8,128)(2,1)S(1)}, bf16[128,2048]{1,0:T(8,128)(2,1)S(1)}, u32[]{:S(2)}, u32[]{:S(2)}) collective-permute-start(bf16[128,2048]{1,0:T(8,128)(2,1)S(1)} %get-tuple-element.69), channel_id=1, source_target_pairs={{0,1},{1,0},{2,3},{3,2},{4,5},{5,4},{6,7},{7,6},{8,9},{9,8},{10,11... | collective-permute-start | bytes 1572872 | tf_op jit(solution)/shard_map/ppermute | solution.py:25
  28.5 8.9 %collective-permute-start.11 = (bf16[768,2048]{1,0:T(8,128)(2,1)S(1)}, bf16[768,2048]{1,0:T(8,128)(2,1)S(1)}, u32[]{:S(2)}, u32[]{:S(2)}) collective-permute-start(bf16[768,2048]{1,0:T(8,128)(2,1)S(1)} %bitcast.48), channel_id=1, source_target_pairs={{0,1},{1,0},{2,3},{3,2},{4,5},{5,4},{6,7},{7,6},{8,9},{9,8},{10,11... | collective-permute-start | bytes 9437192 | tf_op jit(solution)/shard_map/ppermute | solution.py:25
  28.8 8.6 %collective-permute-start.9 = (bf16[64,2048]{1,0:T(8,128)(2,1)S(1)}, bf16[64,2048]{1,0:T(8,128)(2,1)S(1)}, u32[]{:S(2)}, u32[]{:S(2)}) collective-permute-start(bf16[64,2048]{1,0:T(8,128)(2,1)S(1)} %slice.137), channel_id=1, source_target_pairs={{0,2},{1,3},{2,0},{3,1},{4,6},{5,7},{6,4},{7,5},{8,10},{9,11},{10,... | collective-permute-start | bytes 786440 | tf_op jit(solution)/shard_map/ppermute | solution.py:25
  30.3 5.5 %collective-permute-start.10 = (bf16[2,256,128]{2,1,0:T(8,128)(2,1)S(1)}, bf16[2,256,128]{2,1,0:T(8,128)(2,1)S(1)}, u32[]{:S(2)}, u32[]{:S(2)}) collective-permute-start(bf16[2,256,128]{2,1,0:T(8,128)(2,1)S(1)} %pad_maximum_fusion.5), channel_id=1, source_target_pairs={{0,16},{16,0},{1,17},{17,1},{2,18},{18,2},{3,19},{19,3},{4,20},{20... | collective-permute-start | bytes 393224 | tf_op jit(solution)/shard_map/ppermute | solution.py:25
  37.4 16.6 %copy-start.7 = (bf16[64,2048]{1,0:T(8,128)(2,1)}, bf16[64,2048]{1,0:T(8,128)(2,1)S(1)}, u32[]{:S(2)}) copy-start(bf16[64,2048]{1,0:T(8,128)(2,1)S(1)} %collective-permute-done.9) | copy-start | bytes 786436
  37.4 16.6 %copy-start.4 = (bf16[768,2048]{1,0:T(8,128)(2,1)}, bf16[768,2048]{1,0:T(8,128)(2,1)S(1)}, u32[]{:S(2)}) copy-start(bf16[768,2048]{1,0:T(8,128)(2,1)S(1)} %collective-permute-done.11.refs_6_) | copy-start | bytes 9437188
  37.8 13.2 %collective-permute-start.15 = (bf16[64,2048]{1,0:T(8,128)(2,1)S(1)}, bf16[64,2048]{1,0:T(8,128)(2,1)S(1)}, u32[]{:S(2)}, u32[]{:S(2)}) collective-permute-start(bf16[64,2048]{1,0:T(8,128)(2,1)S(1)} %multiply_convert_fusion.refs_9_), channel_id=1, source_target_pairs={{0,4},{4,0},{8,12},{12,8},{1,5},{5,1},{9,13},{13,9},{2,6},{6,2},{1... | collective-permute-start | bytes 786440 | tf_op jit(solution)/shard_map/ppermute | solution.py:25
  39.2 14.7 %collective-permute-start.13 = (bf16[64,2048]{1,0:T(8,128)(2,1)S(1)}, bf16[64,2048]{1,0:T(8,128)(2,1)S(1)}, u32[]{:S(2)}, u32[]{:S(2)}) collective-permute-start(bf16[64,2048]{1,0:T(8,128)(2,1)S(1)} %multiply_convert_fusion.refs_9_), channel_id=1, source_target_pairs={{0,8},{4,12},{8,0},{12,4},{1,9},{5,13},{9,1},{13,5},{2,10},{6,14},... | collective-permute-start | bytes 786440 | tf_op jit(solution)/shard_map/ppermute | solution.py:25
  41.8 12.2 %collective-permute-start.19 = (bf16[64,2048]{1,0:T(8,128)(2,1)S(1)}, bf16[64,2048]{1,0:T(8,128)(2,1)S(1)}, u32[]{:S(2)}, u32[]{:S(2)}) collective-permute-start(bf16[64,2048]{1,0:T(8,128)(2,1)S(1)} %multiply_convert_fusion.refs_9_), channel_id=1, source_target_pairs={{0,16},{16,0},{1,17},{17,1},{2,18},{18,2},{3,19},{19,3},{4,20},{20... | collective-permute-start | bytes 786440 | tf_op jit(solution)/shard_map/ppermute | solution.py:25
  43.3 10.7 %collective-permute-start.18 = (bf16[64,2048]{1,0:T(8,128)(2,1)S(1)}, bf16[64,2048]{1,0:T(8,128)(2,1)S(1)}, u32[]{:S(2)}, u32[]{:S(2)}) collective-permute-start(bf16[64,2048]{1,0:T(8,128)(2,1)S(1)} %multiply_convert_fusion.refs_9_), channel_id=1, source_target_pairs={{0,2},{1,3},{2,0},{3,1},{4,6},{5,7},{6,4},{7,5},{8,10},{9,11},{10,... | collective-permute-start | bytes 786440 | tf_op jit(solution)/shard_map/ppermute | solution.py:25
  51.0 9.2 %collective-permute-start.17 = (bf16[64,2048]{1,0:T(8,128)(2,1)S(1)}, bf16[64,2048]{1,0:T(8,128)(2,1)S(1)}, u32[]{:S(2)}, u32[]{:S(2)}) collective-permute-start(bf16[64,2048]{1,0:T(8,128)(2,1)S(1)} %collective-permute-done.15.refs_10_), channel_id=1, source_target_pairs={{0,16},{16,0},{1,17},{17,1},{2,18},{18,2},{3,19},{19,3},{4,20},{20... | collective-permute-start | bytes 786440 | tf_op jit(solution)/shard_map/ppermute | solution.py:25
  52.4 9.2 %collective-permute-start.16 = (bf16[64,2048]{1,0:T(8,128)(2,1)S(1)}, bf16[64,2048]{1,0:T(8,128)(2,1)S(1)}, u32[]{:S(2)}, u32[]{:S(2)}) collective-permute-start(bf16[64,2048]{1,0:T(8,128)(2,1)S(1)} %collective-permute-done.15.refs_10_), channel_id=1, source_target_pairs={{0,2},{1,3},{2,0},{3,1},{4,6},{5,7},{6,4},{7,5},{8,10},{9,11},{10,... | collective-permute-start | bytes 786440 | tf_op jit(solution)/shard_map/ppermute | solution.py:25
  54.0 7.7 %collective-permute-start.14 = (bf16[64,2048]{1,0:T(8,128)(2,1)S(1)}, bf16[64,2048]{1,0:T(8,128)(2,1)S(1)}, u32[]{:S(2)}, u32[]{:S(2)}) collective-permute-start(bf16[64,2048]{1,0:T(8,128)(2,1)S(1)} %collective-permute-done.13.refs_11_), channel_id=1, source_target_pairs={{0,4},{4,0},{8,12},{12,8},{1,5},{5,1},{9,13},{13,9},{2,6},{6,2},{1... | collective-permute-start | bytes 786440 | tf_op jit(solution)/shard_map/ppermute | solution.py:25
  54.1 11.8 %collective-permute-start.22 = (bf16[64,2048]{1,0:T(8,128)(2,1)S(1)}, bf16[64,2048]{1,0:T(8,128)(2,1)S(1)}, u32[]{:S(2)}, u32[]{:S(2)}) collective-permute-start(bf16[64,2048]{1,0:T(8,128)(2,1)S(1)} %collective-permute-done.13.refs_11_), channel_id=1, source_target_pairs={{0,16},{16,0},{1,17},{17,1},{2,18},{18,2},{3,19},{19,3},{4,20},{20... | collective-permute-start | bytes 786440 | tf_op jit(solution)/shard_map/ppermute | solution.py:25
  55.1 12.2 %collective-permute-start.20 = (bf16[64,2048]{1,0:T(8,128)(2,1)S(1)}, bf16[64,2048]{1,0:T(8,128)(2,1)S(1)}, u32[]{:S(2)}, u32[]{:S(2)}) collective-permute-start(bf16[64,2048]{1,0:T(8,128)(2,1)S(1)} %collective-permute-done.13.refs_11_), channel_id=1, source_target_pairs={{0,2},{1,3},{2,0},{3,1},{4,6},{5,7},{6,4},{7,5},{8,10},{9,11},{10,... | collective-permute-start | bytes 786440 | tf_op jit(solution)/shard_map/ppermute | solution.py:25
  61.7 7.4 %collective-permute-start.23 = (bf16[64,2048]{1,0:T(8,128)(2,1)S(1)}, bf16[64,2048]{1,0:T(8,128)(2,1)S(1)}, u32[]{:S(2)}, u32[]{:S(2)}) collective-permute-start(bf16[64,2048]{1,0:T(8,128)(2,1)S(1)} %collective-permute-done.14.refs_12_), channel_id=1, source_target_pairs={{0,16},{16,0},{1,17},{17,1},{2,18},{18,2},{3,19},{19,3},{4,20},{20... | collective-permute-start | bytes 786440 | tf_op jit(solution)/shard_map/ppermute | solution.py:25
  62.3 8.0 %collective-permute-start.21 = (bf16[64,2048]{1,0:T(8,128)(2,1)S(1)}, bf16[64,2048]{1,0:T(8,128)(2,1)S(1)}, u32[]{:S(2)}, u32[]{:S(2)}) collective-permute-start(bf16[64,2048]{1,0:T(8,128)(2,1)S(1)} %collective-permute-done.14.refs_12_), channel_id=1, source_target_pairs={{0,2},{1,3},{2,0},{3,1},{4,6},{5,7},{6,4},{7,5},{8,10},{9,11},{10,... | collective-permute-start | bytes 786440 | tf_op jit(solution)/shard_map/ppermute | solution.py:25
  70.3 11.6 %collective-permute-start.24 = (bf16[256,1024]{1,0:T(8,128)(2,1)S(1)}, bf16[256,1024]{1,0:T(8,128)(2,1)S(1)}, u32[]{:S(2)}, u32[]{:S(2)}) collective-permute-start(bf16[256,1024]{1,0:T(8,128)(2,1)S(1)} %get-tuple-element.93), channel_id=1, source_target_pairs={{0,16},{16,0},{1,17},{17,1},{2,18},{18,2},{3,19},{19,3},{4,20},{20... | collective-permute-start | bytes 1572872 | tf_op jit(solution)/shard_map/ppermute | solution.py:25
  71.0 11.0 %collective-permute-start.25 = (bf16[256,1024]{1,0:T(8,128)(2,1)S(1)}, bf16[256,1024]{1,0:T(8,128)(2,1)S(1)}, u32[]{:S(2)}, u32[]{:S(2)}) collective-permute-start(bf16[256,1024]{1,0:T(8,128)(2,1)S(1)} %get-tuple-element.94), channel_id=1, source_target_pairs={{0,2},{1,3},{2,0},{3,1},{4,6},{5,7},{6,4},{7,5},{8,10},{9,11},{10,... | collective-permute-start | bytes 1572872 | tf_op jit(solution)/shard_map/ppermute | solution.py:25
  82.0 13.5 %collective-permute-start.26 = (bf16[256,1024]{1,0:T(8,128)(2,1)S(1)}, bf16[256,1024]{1,0:T(8,128)(2,1)S(1)}, u32[]{:S(2)}, u32[]{:S(2)}) collective-permute-start(bf16[256,1024]{1,0:T(8,128)(2,1)S(1)} %get-tuple-element.95), channel_id=1, source_target_pairs={{0,16},{16,0},{1,17},{17,1},{2,18},{18,2},{3,19},{19,3},{4,20},{20... | collective-permute-start | bytes 1572872 | tf_op jit(solution)/shard_map/ppermute | solution.py:25
  83.5 11.9 %collective-permute-start.27 = (bf16[256,1024]{1,0:T(8,128)(2,1)S(1)}, bf16[256,1024]{1,0:T(8,128)(2,1)S(1)}, u32[]{:S(2)}, u32[]{:S(2)}) collective-permute-start(bf16[256,1024]{1,0:T(8,128)(2,1)S(1)} %get-tuple-element.96), channel_id=1, source_target_pairs={{0,2},{1,3},{2,0},{3,1},{4,6},{5,7},{6,4},{7,5},{8,10},{9,11},{10,... | collective-permute-start | bytes 1572872 | tf_op jit(solution)/shard_map/ppermute | solution.py:25
  95.5 9.0 %collective-permute-start.28 = (bf16[128,1024]{1,0:T(8,128)(2,1)S(1)}, bf16[128,1024]{1,0:T(8,128)(2,1)S(1)}, u32[]{:S(2)}, u32[]{:S(2)}) collective-permute-start(bf16[128,1024]{1,0:T(8,128)(2,1)S(1)} %get-tuple-element.108), channel_id=1, source_target_pairs={{0,16},{16,0},{1,17},{17,1},{2,18},{18,2},{3,19},{19,3},{4,20},{20... | collective-permute-start | bytes 786440 | tf_op jit(solution)/shard_map/ppermute | solution.py:25
  95.8 8.8 %collective-permute-start.30 = (bf16[128,1024]{1,0:T(8,128)(2,1)S(1)}, bf16[128,1024]{1,0:T(8,128)(2,1)S(1)}, u32[]{:S(2)}, u32[]{:S(2)}) collective-permute-start(bf16[128,1024]{1,0:T(8,128)(2,1)S(1)} %get-tuple-element.112), channel_id=1, source_target_pairs={{0,2},{1,3},{2,0},{3,1},{4,6},{5,7},{6,4},{7,5},{8,10},{9,11},{10,... | collective-permute-start | bytes 786440 | tf_op jit(solution)/shard_map/ppermute | solution.py:25
  104.7 8.7 %collective-permute-start.33 = (bf16[128,1024]{1,0:T(8,128)(2,1)S(1)}, bf16[128,1024]{1,0:T(8,128)(2,1)S(1)}, u32[]{:S(2)}, u32[]{:S(2)}) collective-permute-start(bf16[128,1024]{1,0:T(8,128)(2,1)S(1)} %get-tuple-element.115), channel_id=1, source_target_pairs={{0,16},{16,0},{1,17},{17,1},{2,18},{18,2},{3,19},{19,3},{4,20},{20... | collective-permute-start | bytes 786440 | tf_op jit(solution)/shard_map/ppermute | solution.py:25
  106.9 6.6 %collective-permute-start.35 = (bf16[128,1024]{1,0:T(8,128)(2,1)S(1)}, bf16[128,1024]{1,0:T(8,128)(2,1)S(1)}, u32[]{:S(2)}, u32[]{:S(2)}) collective-permute-start(bf16[128,1024]{1,0:T(8,128)(2,1)S(1)} %get-tuple-element.116), channel_id=1, source_target_pairs={{0,2},{1,3},{2,0},{3,1},{4,6},{5,7},{6,4},{7,5},{8,10},{9,11},{10,... | collective-permute-start | bytes 786440 | tf_op jit(solution)/shard_map/ppermute | solution.py:25
  106.9 9.4 %collective-permute-start.29 = (bf16[128,1024]{1,0:T(8,128)(2,1)S(1)}, bf16[128,1024]{1,0:T(8,128)(2,1)S(1)}, u32[]{:S(2)}, u32[]{:S(2)}) collective-permute-start(bf16[128,1024]{1,0:T(8,128)(2,1)S(1)} %add_convert_fusion.4), channel_id=1, source_target_pairs={{0,2},{1,3},{2,0},{3,1},{4,6},{5,7},{6,4},{7,5},{8,10},{9,11},{10,... | collective-permute-start | bytes 786440 | tf_op jit(solution)/shard_map/ppermute | solution.py:25
  108.9 7.4 %collective-permute-start.31 = (bf16[128,1024]{1,0:T(8,128)(2,1)S(1)}, bf16[128,1024]{1,0:T(8,128)(2,1)S(1)}, u32[]{:S(2)}, u32[]{:S(2)}) collective-permute-start(bf16[128,1024]{1,0:T(8,128)(2,1)S(1)} %add_convert_fusion.3), channel_id=1, source_target_pairs={{0,16},{16,0},{1,17},{17,1},{2,18},{18,2},{3,19},{19,3},{4,20},{20... | collective-permute-start | bytes 786440 | tf_op jit(solution)/shard_map/ppermute | solution.py:25
  113.4 6.4 %collective-permute-start.34 = (bf16[128,1024]{1,0:T(8,128)(2,1)S(1)}, bf16[128,1024]{1,0:T(8,128)(2,1)S(1)}, u32[]{:S(2)}, u32[]{:S(2)}) collective-permute-start(bf16[128,1024]{1,0:T(8,128)(2,1)S(1)} %add_convert_fusion.2), channel_id=1, source_target_pairs={{0,2},{1,3},{2,0},{3,1},{4,6},{5,7},{6,4},{7,5},{8,10},{9,11},{10,... | collective-permute-start | bytes 786440 | tf_op jit(solution)/shard_map/ppermute | solution.py:25
  113.6 6.4 %collective-permute-start.36 = (bf16[128,1024]{1,0:T(8,128)(2,1)S(1)}, bf16[128,1024]{1,0:T(8,128)(2,1)S(1)}, u32[]{:S(2)}, u32[]{:S(2)}) collective-permute-start(bf16[128,1024]{1,0:T(8,128)(2,1)S(1)} %add_convert_fusion.1), channel_id=1, source_target_pairs={{0,16},{16,0},{1,17},{17,1},{2,18},{18,2},{3,19},{19,3},{4,20},{20... | collective-permute-start | bytes 786440 | tf_op jit(solution)/shard_map/ppermute | solution.py:25
  116.6 7.3 %collective-permute-start.32 = (bf16[64,2048]{1,0:T(8,128)(2,1)S(1)}, bf16[64,2048]{1,0:T(8,128)(2,1)S(1)}, u32[]{:S(2)}, u32[]{:S(2)}) collective-permute-start(bf16[64,2048]{1,0:T(8,128)(2,1)S(1)} %fusion.5), channel_id=1, source_target_pairs={{0,4},{4,0},{8,12},{12,8},{1,5},{5,1},{9,13},{13,9},{2,6},{6,2},{1... | collective-permute-start | bytes 786440 | tf_op jit(solution)/shard_map/ppermute | solution.py:25
  120.3 18.7 %copy-start.6 = (bf16[1,64,2048]{2,1,0:T(8,128)(2,1)S(1)}, bf16[1,64,2048]{2,1,0:T(8,128)(2,1)}, u32[]{:S(2)}) copy-start(bf16[1,64,2048]{2,1,0:T(8,128)(2,1)} %param.12) | copy-start | bytes 786436
  120.3 18.7 %copy-start.8 = (bf16[64,2048]{1,0:T(8,128)(2,1)S(1)}, bf16[64,2048]{1,0:T(8,128)(2,1)}, u32[]{:S(2)}) copy-start(bf16[64,2048]{1,0:T(8,128)(2,1)} %copy-done.7) | copy-start | bytes 786436
  120.4 8.3 %collective-permute-start.37 = (bf16[64,2048]{1,0:T(8,128)(2,1)S(1)}, bf16[64,2048]{1,0:T(8,128)(2,1)S(1)}, u32[]{:S(2)}, u32[]{:S(2)}) collective-permute-start(bf16[64,2048]{1,0:T(8,128)(2,1)S(1)} %fusion.6), channel_id=1, source_target_pairs={{0,4},{4,0},{8,12},{12,8},{1,5},{5,1},{9,13},{13,9},{2,6},{6,2},{1... | collective-permute-start | bytes 786440 | tf_op jit(solution)/shard_map/ppermute | solution.py:25
  128.8 10.1 %collective-permute-start.38 = (bf16[64,2048]{1,0:T(8,128)(2,1)S(1)}, bf16[64,2048]{1,0:T(8,128)(2,1)S(1)}, u32[]{:S(2)}, u32[]{:S(2)}) collective-permute-start(bf16[64,2048]{1,0:T(8,128)(2,1)S(1)} %fusion.2), channel_id=1, source_target_pairs={{0,8},{4,12},{8,0},{12,4},{1,9},{5,13},{9,1},{13,5},{2,10},{6,14},... | collective-permute-start | bytes 786440 | tf_op jit(solution)/shard_map/ppermute | solution.py:25

commit v18 on v15

--- a/solution.py
+++ b/solution.py
@@ -356,19 +356,14 @@
     groups = len(cuts)
     piece_refs = refs[7 : 7 + len(spots)]
     out_refs = refs[7 + len(spots) : 7 + len(spots) + 2 * sum(cuts)]
-    x_buf, xs_buf, gu_buf, dn_buf, hid_buf, served_buf, y_buf, x_sem, w_sem, y_sem = refs[
+    xs_buf, gu_buf, dn_buf, hid_buf, served_buf, y_buf, w_sem, y_sem = refs[
         7 + len(spots) + len(out_refs) :
     ]
-    width = x_buf.shape[2]
+    width = xs_buf.shape[2]
     half = width // 2
     hidden = own_dn_ref.shape[0]
     tiles = hidden // TILE
 
-    row_copies = []
-    for number, ((group, row, column), piece) in enumerate(zip(spots, piece_refs)):
-        rows, columns = piece.shape
-        target = x_buf.at[group, pl.ds(row, rows), pl.ds(column, columns)]
-        row_copies.append((group, pltpu.make_async_copy(piece, target, x_sem.at[number])))
     weight_copies = []
     for expert, (gu_ref, dn_ref) in enumerate(((own_gu_ref, own_dn_ref), (far_gu_ref, far_dn_ref))):
         mine = []
@@ -383,21 +378,25 @@
                 )
         mine.append(pltpu.make_async_copy(dn_ref, dn_buf.at[expert], w_sem.at[expert, 2 * tiles]))
         weight_copies.append(mine)
-    for _, copy in row_copies:
-        copy.start()
     for mine in weight_copies:
         for copy in mine:
             copy.start()
 
     for group in range(groups):
-        for where, copy in row_copies:
-            if where == group:
-                copy.wait()
-        chosen = jnp.dot(
-            pick_ref[first + group], x_buf[group], preferred_element_type=jnp.float32
-        ).astype(jnp.bfloat16)
-        xs_buf[0, pl.ds(group * slots, slots)] = chosen[:slots]
-        xs_buf[1, pl.ds(group * slots, slots)] = chosen[slots:]
+        for column in range(0, width, half):
+            held = [
+                piece[:, column - start : column - start + half]
+                for (where, _, start), piece in zip(spots, piece_refs)
+                if where == group and start <= column < start + piece.shape[1]
+            ]
+            chosen = jnp.dot(
+                pick_ref[first + group],
+                jnp.concatenate(held, axis=0),
+                preferred_element_type=jnp.float32,
+            ).astype(jnp.bfloat16)
+            rows = pl.ds(group * slots, slots)
+            xs_buf[0, rows, column : column + half] = chosen[:slots]
+            xs_buf[1, rows, column : column + half] = chosen[slots:]
 
     for expert in range(2):
         for tile in range(tiles):
@@ -466,17 +465,15 @@
             for cut in cuts
             for _ in range(2 * cut)
         ],
-        in_specs=[inside] * 3 + [stored] * 4 + [anywhere] * len(arrays),
+        in_specs=[inside] * 3 + [stored] * 4 + [inside] * len(arrays),
         out_specs=[anywhere] * (2 * sum(cuts)),
         scratch_shapes=[
-            pltpu.VMEM((groups, group_rows, width), jnp.bfloat16),
             pltpu.VMEM((2, groups * slots, width), jnp.bfloat16),
             pltpu.VMEM((2, tiles, 2, width, TILE), jnp.bfloat16),
             pltpu.VMEM((2, hidden, width), jnp.bfloat16),
             pltpu.VMEM((groups * slots, hidden), jnp.bfloat16),
             pltpu.VMEM((2, groups * slots, width), jnp.bfloat16),
             pltpu.VMEM((groups, group_rows, width), jnp.bfloat16),
-            pltpu.SemaphoreType.DMA((len(arrays),)),
             pltpu.SemaphoreType.DMA((2, 2 * tiles + 1)),
             pltpu.SemaphoreType.DMA((2 * sum(cuts),)),
         ],

time: 136 us -> 137 us (level)
  no operation moved by 1% of the time
where the time goes in v18:
time: 137 us
  waiting for transfers between devices  60.1 us (44%)
  starting transfers between devices  45.9 us (34%)
  Pallas kernels  27.5 us (20%)
  other arithmetic  2.45 us (2%)
    ppermute x39, waiting for transfers between devices, swap(): return lax.ppermute(block, axis, [(i, i ^ bits) for i in range(size)])  60.1 us
    ppermute x39, starting transfers between devices, swap(): return lax.ppermute(block, axis, [(i, i ^ bits) for i in range(size)])  45.9 us
    pallas_call x2, Pallas kernels, run_experts(): pl.pallas_call(lambda *refs: expert_kernel(first, spots, cuts, *refs), ou...  19.7 us
  transfers between devices with their start and end apart: 39, of which 23 were waited for; matrix products, arithmetic and copies ran while one was open for 1% of the time, Pallas kernels for 20%

profile of v18, /device:TPU:0, one launch (start us, length us, event | category | flops | bytes accessed | tf_op | source)
XLA Modules:
  0.0 136.7 jit_solution(9547662711829725034)
XLA Ops:
  0.0 0.5 collective-permute-start.12
  0.5 2.6 %prepare.1 = (bf16[64,2048]{1,0:T(8,128)(2,1)S(1)}, bf16[64,640]{1,0:T(8,128)(2,1)S(1)}) custom-call(bf16[64,2048]{1,0:T(8,128)(2,1)} %bitcast.57, f32[1,2048]{1,0:T(1,128)} %bitcast.62, bf16[2,2048,256]{2,1,0:T(8,128)(2,1)} %refs_2_.1, f32[1,128]{1,0:T(1,128)} %bitcast.65, s32[8,64]{1,0:T(8,128)} %bitcast.63, s32[8,64]{1,0:T(8,128)} %bitcast.64), custom_call_target="tpu_custom_call" | custom-call | flops 134217728 | bytes 2621440 | tf_op jit(solution)/shard_map/prepare/pallas_call | solution.py:187
  3.1 4.7 %collective-permute-start.2 = (bf16[64,640]{1,0:T(8,128)(2,1)S(1)}, bf16[64,640]{1,0:T(8,128)(2,1)S(1)}, u32[]{:S(2)}, u32[]{:S(2)}) collective-permute-start(bf16[64,640]{1,0:T(8,128)(2,1)S(1)} %get-tuple-element.65), channel_id=1, source_target_pairs={{0,12},{4,8},{8,4},{12,0},{1,13},{5,9},{9,5},{13,1},{2,14},{6,10},... | collective-permute-start | bytes 245768 | tf_op jit(solution)/shard_map/ppermute | solution.py:25
  7.7 0.6 collective-permute-start
  8.4 1.7 %collective-permute-start.3 = (bf16[64,2048]{1,0:T(8,128)(2,1)S(1)}, bf16[64,2048]{1,0:T(8,128)(2,1)S(1)}, u32[]{:S(2)}, u32[]{:S(2)}) collective-permute-start(bf16[64,2048]{1,0:T(8,128)(2,1)S(1)} %get-tuple-element.67.first_ref), channel_id=1, source_target_pairs={{0,2},{1,3},{2,0},{3,1},{4,6},{5,7},{6,4},{7,5},{8,10},{9,11},{10,... | collective-permute-start | bytes 786440 | tf_op jit(solution)/shard_map/ppermute | solution.py:25
  10.0 3.5 %collective-permute-done = bf16[64,640]{1,0:T(8,128)(2,1)S(1)} collective-permute-done((bf16[64,640]{1,0:T(8,128)(2,1)S(1)}, bf16[64,640]{1,0:T(8,128)(2,1)S(1)}, u32[]{:S(2)}, u32[]{:S(2)}) %collective-permute-start) | collective-permute-done | bytes 81952 | tf_op jit(solution)/shard_map/ppermute | solution.py:25
  13.5 1.6 %collective-permute-done.1 = bf16[64,640]{1,0:T(8,128)(2,1)S(1)} collective-permute-done((bf16[64,640]{1,0:T(8,128)(2,1)S(1)}, bf16[64,640]{1,0:T(8,128)(2,1)S(1)}, u32[]{:S(2)}, u32[]{:S(2)}) %collective-permute-start.1) | collective-permute-done | bytes 81952 | tf_op jit(solution)/shard_map/ppermute | solution.py:25
  15.3 1.1 collective-permute-done.3.second_ref
  16.4 1.5 %collective-permute-start.6 = (bf16[256,384]{1,0:T(8,128)(2,1)S(1)}, bf16[256,384]{1,0:T(8,128)(2,1)S(1)}, u32[]{:S(2)}, u32[]{:S(2)}) collective-permute-start(bf16[256,384]{1,0:T(8,128)(2,1)S(1)} %pad_maximum_fusion.4), channel_id=1, source_target_pairs={{0,2},{1,3},{2,0},{3,1},{4,6},{5,7},{6,4},{7,5},{8,10},{9,11},{10,... | collective-permute-start | bytes 589832 | tf_op jit(solution)/shard_map/ppermute | solution.py:25
  17.9 0.5 collective-permute-start.5
  18.4 3.7 %collective-permute-done.6 = bf16[256,384]{1,0:T(8,128)(2,1)S(1)} collective-permute-done((bf16[256,384]{1,0:T(8,128)(2,1)S(1)}, bf16[256,384]{1,0:T(8,128)(2,1)S(1)}, u32[]{:S(2)}, u32[]{:S(2)}) %collective-permute-start.6) | collective-permute-done | bytes 196640 | tf_op jit(solution)/shard_map/ppermute | solution.py:25
  22.3 0.9 queries.1.refs_0_
  23.2 0.6 collective-permute-done.7.refs_2_
  23.7 2.7 %attend.1 = (f32[128,2048]{1,0:T(8,128)S(1)}, bf16[128,2048]{1,0:T(8,128)(2,1)S(1)}) custom-call(bf16[256,512]{1,0:T(8,128)(2,1)S(1)} %queries.1.refs_0_, bf16[512,256]{1,0:T(8,128)(2,1)S(1)} %pad_maximum_fusion.2.refs_1_, bf16[512,256]{1,0:T(8,128)(2,1)S(1)} %collective-permute-done.7.refs_2_, bf16[512,2048]{1,0:T(8,128)(2,1)S(1)} %copy-done.2), custom_call_target="tpu_custom_call" | custom-call | flops 1073741824 | bytes 4194304 | tf_op jit(solution)/shard_map/attend/pallas_call | solution.py:266
  26.5 0.2 collective-permute-start.8
  26.7 1.8 %collective-permute-done.8 = bf16[128,2048]{1,0:T(8,128)(2,1)S(1)} collective-permute-done((bf16[128,2048]{1,0:T(8,128)(2,1)S(1)}, bf16[128,2048]{1,0:T(8,128)(2,1)S(1)}, u32[]{:S(2)}, u32[]{:S(2)}) %collective-permute-start.8) | collective-permute-done | bytes 524320 | tf_op jit(solution)/shard_map/ppermute | solution.py:25
  28.8 1.5 %collective-permute-start.9 = (bf16[64,2048]{1,0:T(8,128)(2,1)S(1)}, bf16[64,2048]{1,0:T(8,128)(2,1)S(1)}, u32[]{:S(2)}, u32[]{:S(2)}) collective-permute-start(bf16[64,2048]{1,0:T(8,128)(2,1)S(1)} %slice.145), channel_id=1, source_target_pairs={{0,2},{1,3},{2,0},{3,1},{4,6},{5,7},{6,4},{7,5},{8,10},{9,11},{10,... | collective-permute-start | bytes 786440 | tf_op jit(solution)/shard_map/ppermute | solution.py:25
  30.3 1.6 %collective-permute-start.10 = (bf16[2,256,128]{2,1,0:T(8,128)(2,1)S(1)}, bf16[2,256,128]{2,1,0:T(8,128)(2,1)S(1)}, u32[]{:S(2)}, u32[]{:S(2)}) collective-permute-start(bf16[2,256,128]{2,1,0:T(8,128)(2,1)S(1)} %pad_maximum_fusion.5), channel_id=1, source_target_pairs={{0,16},{16,0},{1,17},{17,1},{2,18},{18,2},{3,19},{19,3},{4,20},{20... | collective-permute-start | bytes 393224 | tf_op jit(solution)/shard_map/ppermute | solution.py:25
  31.9 4.0 %collective-permute-done.10 = bf16[2,256,128]{2,1,0:T(8,128)(2,1)S(1)} collective-permute-done((bf16[2,256,128]{2,1,0:T(8,128)(2,1)S(1)}, bf16[2,256,128]{2,1,0:T(8,128)(2,1)S(1)}, u32[]{:S(2)}, u32[]{:S(2)}) %collective-permute-start.10) | collective-permute-done | bytes 131104 | tf_op jit(solution)/shard_map/ppermute | solution.py:25
  35.9 1.5 %collective-permute-done.9 = bf16[64,2048]{1,0:T(8,128)(2,1)S(1)} collective-permute-done((bf16[64,2048]{1,0:T(8,128)(2,1)S(1)}, bf16[64,2048]{1,0:T(8,128)(2,1)S(1)}, u32[]{:S(2)}, u32[]{:S(2)}) %collective-permute-start.9) | collective-permute-done | bytes 262176 | tf_op jit(solution)/shard_map/ppermute | solution.py:25
  37.4 0.2 multiply_reduce_fusion
  37.8 1.5 %collective-permute-start.15 = (bf16[64,2048]{1,0:T(8,128)(2,1)S(1)}, bf16[64,2048]{1,0:T(8,128)(2,1)S(1)}, u32[]{:S(2)}, u32[]{:S(2)}) collective-permute-start(bf16[64,2048]{1,0:T(8,128)(2,1)S(1)} %multiply_convert_fusion.refs_9_), channel_id=1, source_target_pairs={{0,4},{4,0},{8,12},{12,8},{1,5},{5,1},{9,13},{13,9},{2,6},{6,2},{1... | collective-permute-start | bytes 786440 | tf_op jit(solution)/shard_map/ppermute | solution.py:25
  39.2 2.6 %collective-permute-start.13 = (bf16[64,2048]{1,0:T(8,128)(2,1)S(1)}, bf16[64,2048]{1,0:T(8,128)(2,1)S(1)}, u32[]{:S(2)}, u32[]{:S(2)}) collective-permute-start(bf16[64,2048]{1,0:T(8,128)(2,1)S(1)} %multiply_convert_fusion.refs_9_), channel_id=1, source_target_pairs={{0,8},{4,12},{8,0},{12,4},{1,9},{5,13},{9,1},{13,5},{2,10},{6,14},... | collective-permute-start | bytes 786440 | tf_op jit(solution)/shard_map/ppermute | solution.py:25
  41.8 1.5 %collective-permute-start.19 = (bf16[64,2048]{1,0:T(8,128)(2,1)S(1)}, bf16[64,2048]{1,0:T(8,128)(2,1)S(1)}, u32[]{:S(2)}, u32[]{:S(2)}) collective-permute-start(bf16[64,2048]{1,0:T(8,128)(2,1)S(1)} %multiply_convert_fusion.refs_9_), channel_id=1, source_target_pairs={{0,16},{16,0},{1,17},{17,1},{2,18},{18,2},{3,19},{19,3},{4,20},{20... | collective-permute-start | bytes 786440 | tf_op jit(solution)/shard_map/ppermute | solution.py:25
  43.3 1.5 %collective-permute-start.18 = (bf16[64,2048]{1,0:T(8,128)(2,1)S(1)}, bf16[64,2048]{1,0:T(8,128)(2,1)S(1)}, u32[]{:S(2)}, u32[]{:S(2)}) collective-permute-start(bf16[64,2048]{1,0:T(8,128)(2,1)S(1)} %multiply_convert_fusion.refs_9_), channel_id=1, source_target_pairs={{0,2},{1,3},{2,0},{3,1},{4,6},{5,7},{6,4},{7,5},{8,10},{9,11},{10,... | collective-permute-start | bytes 786440 | tf_op jit(solution)/shard_map/ppermute | solution.py:25
  44.8 6.2 %collective-permute-done.15.refs_10_ = bf16[64,2048]{1,0:T(8,128)(2,1)S(1)} collective-permute-done((bf16[64,2048]{1,0:T(8,128)(2,1)S(1)}, bf16[64,2048]{1,0:T(8,128)(2,1)S(1)}, u32[]{:S(2)}, u32[]{:S(2)}) %collective-permute-start.15) | collective-permute-done | bytes 262176 | tf_op jit(solution)/shard_map/ppermute | solution.py:25
  51.0 1.4 %collective-permute-start.17 = (bf16[64,2048]{1,0:T(8,128)(2,1)S(1)}, bf16[64,2048]{1,0:T(8,128)(2,1)S(1)}, u32[]{:S(2)}, u32[]{:S(2)}) collective-permute-start(bf16[64,2048]{1,0:T(8,128)(2,1)S(1)} %collective-permute-done.15.refs_10_), channel_id=1, source_target_pairs={{0,16},{16,0},{1,17},{17,1},{2,18},{18,2},{3,19},{19,3},{4,20},{20... | collective-permute-start | bytes 786440 | tf_op jit(solution)/shard_map/ppermute | solution.py:25
  52.4 1.5 %collective-permute-start.16 = (bf16[64,2048]{1,0:T(8,128)(2,1)S(1)}, bf16[64,2048]{1,0:T(8,128)(2,1)S(1)}, u32[]{:S(2)}, u32[]{:S(2)}) collective-permute-start(bf16[64,2048]{1,0:T(8,128)(2,1)S(1)} %collective-permute-done.15.refs_10_), channel_id=1, source_target_pairs={{0,2},{1,3},{2,0},{3,1},{4,6},{5,7},{6,4},{7,5},{8,10},{9,11},{10,... | collective-permute-start | bytes 786440 | tf_op jit(solution)/shard_map/ppermute | solution.py:25
  54.1 1.1 collective-permute-start.22
  55.1 1.5 %collective-permute-start.20 = (bf16[64,2048]{1,0:T(8,128)(2,1)S(1)}, bf16[64,2048]{1,0:T(8,128)(2,1)S(1)}, u32[]{:S(2)}, u32[]{:S(2)}) collective-permute-start(bf16[64,2048]{1,0:T(8,128)(2,1)S(1)} %collective-permute-done.13.refs_11_), channel_id=1, source_target_pairs={{0,2},{1,3},{2,0},{3,1},{4,6},{5,7},{6,4},{7,5},{8,10},{9,11},{10,... | collective-permute-start | bytes 786440 | tf_op jit(solution)/shard_map/ppermute | solution.py:25
  56.6 1.6 %tables.1 = (bf16[4,224,256]{2,1,0:T(8,128)(2,1)S(1)}, bf16[2,4,256,112]{3,2,1,0:T(8,128)(2,1)S(1)}, f32[4,256,2]{2,1,0:T(8,128)S(1)}) custom-call(s32[1]{0:T(128)} %bitcast.12.refs_0_, bf16[4,256,128]{2,1,0:T(8,128)(2,1)S(1)} %pad_maximum_fusion.3.refs_1_), custom_call_target="tpu_custom_call" | custom-call | flops 134217728 | bytes 917504 | tf_op jit(solution)/shard_map/tables/pallas_call | solution.py:332
  58.2 2.0 %collective-permute-done.17.refs_12_.refs_5_ = bf16[64,2048]{1,0:T(8,128)(2,1)S(1)} collective-permute-done((bf16[64,2048]{1,0:T(8,128)(2,1)S(1)}, bf16[64,2048]{1,0:T(8,128)(2,1)S(1)}, u32[]{:S(2)}, u32[]{:S(2)}) %collective-permute-start.17) | collective-permute-done | bytes 262176 | tf_op jit(solution)/shard_map/ppermute | solution.py:25
  60.2 1.4 %collective-permute-done.16.refs_8_.refs_1_ = bf16[64,2048]{1,0:T(8,128)(2,1)S(1)} collective-permute-done((bf16[64,2048]{1,0:T(8,128)(2,1)S(1)}, bf16[64,2048]{1,0:T(8,128)(2,1)S(1)}, u32[]{:S(2)}, u32[]{:S(2)}) %collective-permute-start.16) | collective-permute-done | bytes 262176 | tf_op jit(solution)/shard_map/ppermute | solution.py:25
  61.7 0.6 collective-permute-start.23
  62.3 1.5 %collective-permute-start.21 = (bf16[64,2048]{1,0:T(8,128)(2,1)S(1)}, bf16[64,2048]{1,0:T(8,128)(2,1)S(1)}, u32[]{:S(2)}, u32[]{:S(2)}) collective-permute-start(bf16[64,2048]{1,0:T(8,128)(2,1)S(1)} %collective-permute-done.14.refs_12_), channel_id=1, source_target_pairs={{0,2},{1,3},{2,0},{3,1},{4,6},{5,7},{6,4},{7,5},{8,10},{9,11},{10,... | collective-permute-start | bytes 786440 | tf_op jit(solution)/shard_map/ppermute | solution.py:25
  63.7 2.1 %collective-permute-done.22.refs_13_.refs_6_ = bf16[64,2048]{1,0:T(8,128)(2,1)S(1)} collective-permute-done((bf16[64,2048]{1,0:T(8,128)(2,1)S(1)}, bf16[64,2048]{1,0:T(8,128)(2,1)S(1)}, u32[]{:S(2)}, u32[]{:S(2)}) %collective-permute-start.22) | collective-permute-done | bytes 262176 | tf_op jit(solution)/shard_map/ppermute | solution.py:25
  65.9 1.4 %collective-permute-done.20.refs_9_.refs_2_ = bf16[64,2048]{1,0:T(8,128)(2,1)S(1)} collective-permute-done((bf16[64,2048]{1,0:T(8,128)(2,1)S(1)}, bf16[64,2048]{1,0:T(8,128)(2,1)S(1)}, u32[]{:S(2)}, u32[]{:S(2)}) %collective-permute-start.20) | collective-permute-done | bytes 262176 | tf_op jit(solution)/shard_map/ppermute | solution.py:25
  67.3 1.8 %collective-permute-done.23.refs_14_.refs_7_ = bf16[64,2048]{1,0:T(8,128)(2,1)S(1)} collective-permute-done((bf16[64,2048]{1,0:T(8,128)(2,1)S(1)}, bf16[64,2048]{1,0:T(8,128)(2,1)S(1)}, u32[]{:S(2)}, u32[]{:S(2)}) %collective-permute-start.23) | collective-permute-done | bytes 262176 | tf_op jit(solution)/shard_map/ppermute | solution.py:25
  69.1 1.2 collective-permute-done.21.refs_10_.refs_3_
  70.3 0.7 collective-permute-start.24
  71.0 1.5 %collective-permute-start.25 = (bf16[256,1024]{1,0:T(8,128)(2,1)S(1)}, bf16[256,1024]{1,0:T(8,128)(2,1)S(1)}, u32[]{:S(2)}, u32[]{:S(2)}) collective-permute-start(bf16[256,1024]{1,0:T(8,128)(2,1)S(1)} %get-tuple-element.95), channel_id=1, source_target_pairs={{0,2},{1,3},{2,0},{3,1},{4,6},{5,7},{6,4},{7,5},{8,10},{9,11},{10,... | collective-permute-start | bytes 1572872 | tf_op jit(solution)/shard_map/ppermute | solution.py:25
  72.4 9.9 %experts.2 = (bf16[256,1024]{1,0:T(8,128)(2,1)S(1)}, bf16[256,1024]{1,0:T(8,128)(2,1)S(1)}, bf16[256,1024]{1,0:T(8,128)(2,1)S(1)}, bf16[256,1024]{1,0:T(8,128)(2,1)S(1)}) custom-call(bf16[4,224,256]{2,1,0:T(8,128)(2,1)S(1)} %get-tuple-element.79.refs_0_, bf16[2,4,256,112]{3,2,1,0:T(8,128)(2,1)S(1)} %get-tuple-element.80.refs_1_, ...), custom_call_target="tpu_custom_call" | custom-call | flops 4227858432 | bytes 23068672 | tf_op jit(solution)/shard_map/experts/pallas_call | solution.py:461
  82.4 1.5 %collective-permute-start.26 = (bf16[256,1024]{1,0:T(8,128)(2,1)S(1)}, bf16[256,1024]{1,0:T(8,128)(2,1)S(1)}, u32[]{:S(2)}, u32[]{:S(2)}) collective-permute-start(bf16[256,1024]{1,0:T(8,128)(2,1)S(1)} %get-tuple-element.96), channel_id=1, source_target_pairs={{0,16},{16,0},{1,17},{17,1},{2,18},{18,2},{3,19},{19,3},{4,20},{20... | collective-permute-start | bytes 1572872 | tf_op jit(solution)/shard_map/ppermute | solution.py:25
  84.0 1.6 %collective-permute-start.27 = (bf16[256,1024]{1,0:T(8,128)(2,1)S(1)}, bf16[256,1024]{1,0:T(8,128)(2,1)S(1)}, u32[]{:S(2)}, u32[]{:S(2)}) collective-permute-start(bf16[256,1024]{1,0:T(8,128)(2,1)S(1)} %get-tuple-element.97), channel_id=1, source_target_pairs={{0,2},{1,3},{2,0},{3,1},{4,6},{5,7},{6,4},{7,5},{8,10},{9,11},{10,... | collective-permute-start | bytes 1572872 | tf_op jit(solution)/shard_map/ppermute | solution.py:25
  85.5 9.7 %experts.3 = (bf16[128,1024]{1,0:T(8,128)(2,1)S(1)}, bf16[128,1024]{1,0:T(8,128)(2,1)S(1)}, bf16[128,1024]{1,0:T(8,128)(2,1)S(1)}, bf16[128,1024]{1,0:T(8,128)(2...) custom-call(bf16[4,224,256]{2,1,0:T(8,128)(2,1)S(1)} %get-tuple-element.79.refs_0_, ...), custom_call_target="tpu_custom_call" | custom-call | flops 4227858432 | bytes 23068672 | tf_op jit(solution)/shard_map/experts/pallas_call | solution.py:461
  95.3 0.3 collective-permute-start.28
  95.6 0.7 collective-permute-start.30
  96.4 1.5 %collective-permute-start.32 = (bf16[128,1024]{1,0:T(8,128)(2,1)S(1)}, bf16[128,1024]{1,0:T(8,128)(2,1)S(1)}, u32[]{:S(2)}, u32[]{:S(2)}) collective-permute-start(bf16[128,1024]{1,0:T(8,128)(2,1)S(1)} %get-tuple-element.112), channel_id=1, source_target_pairs={{0,16},{16,0},{1,17},{17,1},{2,18},{18,2},{3,19},{19,3},{4,20},{20... | collective-permute-start | bytes 786440 | tf_op jit(solution)/shard_map/ppermute | solution.py:25
  97.9 1.6 %collective-permute-start.33 = (bf16[128,1024]{1,0:T(8,128)(2,1)S(1)}, bf16[128,1024]{1,0:T(8,128)(2,1)S(1)}, u32[]{:S(2)}, u32[]{:S(2)}) collective-permute-start(bf16[128,1024]{1,0:T(8,128)(2,1)S(1)} %get-tuple-element.113), channel_id=1, source_target_pairs={{0,2},{1,3},{2,0},{3,1},{4,6},{5,7},{6,4},{7,5},{8,10},{9,11},{10,... | collective-permute-start | bytes 786440 | tf_op jit(solution)/shard_map/ppermute | solution.py:25
  99.4 4.1 %collective-permute-done.28 = bf16[128,1024]{1,0:T(8,128)(2,1)S(1)} collective-permute-done((bf16[128,1024]{1,0:T(8,128)(2,1)S(1)}, bf16[128,1024]{1,0:T(8,128)(2,1)S(1)}, u32[]{:S(2)}, u32[]{:S(2)}) %collective-permute-start.28) | collective-permute-done | bytes 262176 | tf_op jit(solution)/shard_map/ppermute | solution.py:25
  103.5 1.7 %collective-permute-start.29 = (bf16[128,1024]{1,0:T(8,128)(2,1)S(1)}, bf16[128,1024]{1,0:T(8,128)(2,1)S(1)}, u32[]{:S(2)}, u32[]{:S(2)}) collective-permute-start(bf16[128,1024]{1,0:T(8,128)(2,1)S(1)} %add_convert_fusion.3), channel_id=1, source_target_pairs={{0,2},{1,3},{2,0},{3,1},{4,6},{5,7},{6,4},{7,5},{8,10},{9,11},{10,... | collective-permute-start | bytes 786440 | tf_op jit(solution)/shard_map/ppermute | solution.py:25
  105.3 1.1 collective-permute-start.31
  106.3 1.0 collective-permute-done.32
  107.3 1.1 collective-permute-done.33
  108.4 4.2 %collective-permute-done.29 = bf16[128,1024]{1,0:T(8,128)(2,1)S(1)} collective-permute-done((bf16[128,1024]{1,0:T(8,128)(2,1)S(1)}, bf16[128,1024]{1,0:T(8,128)(2,1)S(1)}, u32[]{:S(2)}, u32[]{:S(2)}) %collective-permute-start.29) | collective-permute-done | bytes 262176 | tf_op jit(solution)/shard_map/ppermute | solution.py:25
  112.6 0.3 collective-permute-done.31
  113.1 0.3 convert_add_fusion.3
  113.7 2.1 %collective-permute-start.35 = (bf16[128,1024]{1,0:T(8,128)(2,1)S(1)}, bf16[128,1024]{1,0:T(8,128)(2,1)S(1)}, u32[]{:S(2)}, u32[]{:S(2)}) collective-permute-start(bf16[128,1024]{1,0:T(8,128)(2,1)S(1)} %get-tuple-element.121), channel_id=1, source_target_pairs={{0,16},{16,0},{1,17},{17,1},{2,18},{18,2},{3,19},{19,3},{4,20},{20... | collective-permute-start | bytes 786440 | tf_op jit(solution)/shard_map/ppermute | solution.py:25
  115.8 8.9 %collective-permute-done.37 = bf16[64,2048]{1,0:T(8,128)(2,1)S(1)} collective-permute-done((bf16[64,2048]{1,0:T(8,128)(2,1)S(1)}, bf16[64,2048]{1,0:T(8,128)(2,1)S(1)}, u32[]{:S(2)}, u32[]{:S(2)}) %collective-permute-start.37) | collective-permute-done | bytes 262176 | tf_op jit(solution)/shard_map/ppermute | solution.py:25
  124.7 1.4 %collective-permute-start.38 = (bf16[64,2048]{1,0:T(8,128)(2,1)S(1)}, bf16[64,2048]{1,0:T(8,128)(2,1)S(1)}, u32[]{:S(2)}, u32[]{:S(2)}) collective-permute-start(bf16[64,2048]{1,0:T(8,128)(2,1)S(1)} %fusion.1), channel_id=1, source_target_pairs={{0,8},{4,12},{8,0},{12,4},{1,9},{5,13},{9,1},{13,5},{2,10},{6,14},... | collective-permute-start | bytes 786440 | tf_op jit(solution)/shard_map/ppermute | solution.py:25
  126.5 2.5 %collective-permute-start.36 = (bf16[64,2048]{1,0:T(8,128)(2,1)S(1)}, bf16[64,2048]{1,0:T(8,128)(2,1)S(1)}, u32[]{:S(2)}, u32[]{:S(2)}) collective-permute-start(bf16[64,2048]{1,0:T(8,128)(2,1)S(1)} %fusion.8), channel_id=1, source_target_pairs={{0,4},{4,0},{8,12},{12,8},{1,5},{5,1},{9,13},{13,9},{2,6},{6,2},{1... | collective-permute-start | bytes 786440 | tf_op jit(solution)/shard_map/ppermute | solution.py:25
  129.1 5.9 %collective-permute-done.38 = bf16[64,2048]{1,0:T(8,128)(2,1)S(1)} collective-permute-done((bf16[64,2048]{1,0:T(8,128)(2,1)S(1)}, bf16[64,2048]{1,0:T(8,128)(2,1)S(1)}, u32[]{:S(2)}, u32[]{:S(2)}) %collective-permute-start.38) | collective-permute-done | bytes 262176 | tf_op jit(solution)/shard_map/ppermute | solution.py:25
  135.0 0.8 collective-permute-done.36
  135.8 0.9 fusion.7
  (69 shorter events, 2.0 us)
Async XLA Ops:
  0.0 22.2 %copy-start.1 = (f32[128]{0:T(128)S(1)}, f32[128]{0:T(128)}, u32[]{:S(2)}) copy-start(f32[128]{0:T(128)} %param.16) | copy-start | bytes 1540
  0.0 22.2 %copy-start = (bf16[2048,512]{1,0:T(8,128)(2,1)S(1)}, bf16[2048,512]{1,0:T(8,128)(2,1)}, u32[]{:S(2)}) copy-start(bf16[2048,512]{1,0:T(8,128)(2,1)} %weight_ref.1) | copy-start | bytes 6291460
  0.0 37.4 %collective-permute-start.12 = (bf16[2048,1536]{1,0:T(8,128)(2,1)}, bf16[2048,1536]{1,0:T(8,128)(2,1)}, u32[]{:S(2)}, u32[]{:S(2)}) collective-permute-start(bf16[2048,1536]{1,0:T(8,128)(2,1)} %bitcast.51), channel_id=1, source_target_pairs={{0,1},{1,0},{2,3},{3,2},{4,5},{5,4},{6,7},{7,6},{8,9},{9,8},{10,11... | collective-permute-start | bytes 18874376 | tf_op jit(solution)/shard_map/ppermute | solution.py:25
  3.1 12.0 %collective-permute-start.2 = (bf16[64,640]{1,0:T(8,128)(2,1)S(1)}, bf16[64,640]{1,0:T(8,128)(2,1)S(1)}, u32[]{:S(2)}, u32[]{:S(2)}) collective-permute-start(bf16[64,640]{1,0:T(8,128)(2,1)S(1)} %get-tuple-element.65), channel_id=1, source_target_pairs={{0,12},{4,8},{8,4},{12,0},{1,13},{5,9},{9,5},{13,1},{2,14},{6,10},... | collective-permute-start | bytes 245768 | tf_op jit(solution)/shard_map/ppermute | solution.py:25
  7.7 7.4 %collective-permute-start.1 = (bf16[64,640]{1,0:T(8,128)(2,1)S(1)}, bf16[64,640]{1,0:T(8,128)(2,1)S(1)}, u32[]{:S(2)}, u32[]{:S(2)}) collective-permute-start(bf16[64,640]{1,0:T(8,128)(2,1)S(1)} %get-tuple-element.65), channel_id=1, source_target_pairs={{0,8},{4,12},{8,0},{12,4},{1,9},{5,13},{9,1},{13,5},{2,10},{6,14},... | collective-permute-start | bytes 245768 | tf_op jit(solution)/shard_map/ppermute | solution.py:25
  7.7 5.8 %collective-permute-start = (bf16[64,640]{1,0:T(8,128)(2,1)S(1)}, bf16[64,640]{1,0:T(8,128)(2,1)S(1)}, u32[]{:S(2)}, u32[]{:S(2)}) collective-permute-start(bf16[64,640]{1,0:T(8,128)(2,1)S(1)} %get-tuple-element.65), channel_id=1, source_target_pairs={{0,4},{4,0},{8,12},{12,8},{1,5},{5,1},{9,13},{13,9},{2,6},{6,2},{1... | collective-permute-start | bytes 245768 | tf_op jit(solution)/shard_map/ppermute | solution.py:25
  8.4 8.0 %collective-permute-start.3 = (bf16[64,2048]{1,0:T(8,128)(2,1)S(1)}, bf16[64,2048]{1,0:T(8,128)(2,1)S(1)}, u32[]{:S(2)}, u32[]{:S(2)}) collective-permute-start(bf16[64,2048]{1,0:T(8,128)(2,1)S(1)} %get-tuple-element.67.first_ref), channel_id=1, source_target_pairs={{0,2},{1,3},{2,0},{3,1},{4,6},{5,7},{6,4},{7,5},{8,10},{9,11},{10,... | collective-permute-start | bytes 786440 | tf_op jit(solution)/shard_map/ppermute | solution.py:25
  10.0 13.7 %copy-start.2 = (bf16[512,2048]{1,0:T(8,128)(2,1)S(1)}, bf16[512,2048]{1,0:T(8,128)(2,1)}, u32[]{:S(2)}) copy-start(bf16[512,2048]{1,0:T(8,128)(2,1)} %refs_3_.1) | copy-start | bytes 6291460
  16.4 5.7 %collective-permute-start.6 = (bf16[256,384]{1,0:T(8,128)(2,1)S(1)}, bf16[256,384]{1,0:T(8,128)(2,1)S(1)}, u32[]{:S(2)}, u32[]{:S(2)}) collective-permute-start(bf16[256,384]{1,0:T(8,128)(2,1)S(1)} %pad_maximum_fusion.4), channel_id=1, source_target_pairs={{0,2},{1,3},{2,0},{3,1},{4,6},{5,7},{6,4},{7,5},{8,10},{9,11},{10,... | collective-permute-start | bytes 589832 | tf_op jit(solution)/shard_map/ppermute | solution.py:25
  17.9 4.3 %collective-permute-start.4 = (bf16[64,2048]{1,0:T(8,128)(2,1)S(1)}, bf16[64,2048]{1,0:T(8,128)(2,1)S(1)}, u32[]{:S(2)}, u32[]{:S(2)}) collective-permute-start(bf16[64,2048]{1,0:T(8,128)(2,1)S(1)} %get-tuple-element.67.first_ref), channel_id=1, source_target_pairs={{0,1},{1,0},{2,3},{3,2},{4,5},{5,4},{6,7},{7,6},{8,9},{9,8},{10,11... | collective-permute-start | bytes 786440 | tf_op jit(solution)/shard_map/ppermute | solution.py:25
  17.9 4.3 %collective-permute-start.5 = (bf16[64,2048]{1,0:T(8,128)(2,1)S(1)}, bf16[64,2048]{1,0:T(8,128)(2,1)S(1)}, u32[]{:S(2)}, u32[]{:S(2)}) collective-permute-start(bf16[64,2048]{1,0:T(8,128)(2,1)S(1)} %collective-permute-done.3.second_ref), channel_id=1, source_target_pairs={{0,1},{1,0},{2,3},{3,2},{4,5},{5,4},{6,7},{7,6},{8,9},{9,8},{10,11... | collective-permute-start | bytes 786440 | tf_op jit(solution)/shard_map/ppermute | solution.py:25
  22.1 1.6 %collective-permute-start.7 = (bf16[512,256]{1,0:T(8,128)(2,1)S(1)}, bf16[512,256]{1,0:T(8,128)(2,1)S(1)}, u32[]{:S(2)}, u32[]{:S(2)}) collective-permute-start(bf16[512,256]{1,0:T(8,128)(2,1)S(1)} %pad_maximum_fusion.2.refs_1_), channel_id=1, source_target_pairs={{0,1},{1,0},{2,3},{3,2},{4,5},{5,4},{6,7},{7,6},{8,9},{9,8},{10,11... | collective-permute-start | bytes 786440 | tf_op jit(solution)/shard_map/ppermute | solution.py:25
  22.3 6.2 %copy-start.3 = (bf16[1,768,2048]{2,1,0:T(8,128)(2,1)S(1)}, bf16[1,768,2048]{2,1,0:T(8,128)(2,1)}, u32[]{:S(2)}) copy-start(bf16[1,768,2048]{2,1,0:T(8,128)(2,1)} %param.23) | copy-start | bytes 9437188
  23.1 14.3 %copy-start.5 = (bf16[1,64,2048]{2,1,0:T(8,128)(2,1)S(1)}, bf16[1,64,2048]{2,1,0:T(8,128)(2,1)}, u32[]{:S(2)}) copy-start(bf16[1,64,2048]{2,1,0:T(8,128)(2,1)} %param.12) | copy-start | bytes 786436
  26.5 11.2 %copy-start.9 = (f32[2048]{0:T(1024)S(1)}, f32[2048]{0:T(1024)}, u32[]{:S(2)}) copy-start(f32[2048]{0:T(1024)} %param.19) | copy-start | bytes 24580
  26.5 2.0 %collective-permute-start.8 = (bf16[128,2048]{1,0:T(8,128)(2,1)S(1)}, bf16[128,2048]{1,0:T(8,128)(2,1)S(1)}, u32[]{:S(2)}, u32[]{:S(2)}) collective-permute-start(bf16[128,2048]{1,0:T(8,128)(2,1)S(1)} %get-tuple-element.70), channel_id=1, source_target_pairs={{0,1},{1,0},{2,3},{3,2},{4,5},{5,4},{6,7},{7,6},{8,9},{9,8},{10,11... | collective-permute-start | bytes 1572872 | tf_op jit(solution)/shard_map/ppermute | solution.py:25
  28.5 8.9 %collective-permute-start.11 = (bf16[768,2048]{1,0:T(8,128)(2,1)S(1)}, bf16[768,2048]{1,0:T(8,128)(2,1)S(1)}, u32[]{:S(2)}, u32[]{:S(2)}) collective-permute-start(bf16[768,2048]{1,0:T(8,128)(2,1)S(1)} %bitcast.56), channel_id=1, source_target_pairs={{0,1},{1,0},{2,3},{3,2},{4,5},{5,4},{6,7},{7,6},{8,9},{9,8},{10,11... | collective-permute-start | bytes 9437192 | tf_op jit(solution)/shard_map/ppermute | solution.py:25
  28.8 8.6 %collective-permute-start.9 = (bf16[64,2048]{1,0:T(8,128)(2,1)S(1)}, bf16[64,2048]{1,0:T(8,128)(2,1)S(1)}, u32[]{:S(2)}, u32[]{:S(2)}) collective-permute-start(bf16[64,2048]{1,0:T(8,128)(2,1)S(1)} %slice.145), channel_id=1, source_target_pairs={{0,2},{1,3},{2,0},{3,1},{4,6},{5,7},{6,4},{7,5},{8,10},{9,11},{10,... | collective-permute-start | bytes 786440 | tf_op jit(solution)/shard_map/ppermute | solution.py:25
  30.3 5.5 %collective-permute-start.10 = (bf16[2,256,128]{2,1,0:T(8,128)(2,1)S(1)}, bf16[2,256,128]{2,1,0:T(8,128)(2,1)S(1)}, u32[]{:S(2)}, u32[]{:S(2)}) collective-permute-start(bf16[2,256,128]{2,1,0:T(8,128)(2,1)S(1)} %pad_maximum_fusion.5), channel_id=1, source_target_pairs={{0,16},{16,0},{1,17},{17,1},{2,18},{18,2},{3,19},{19,3},{4,20},{20... | collective-permute-start | bytes 393224 | tf_op jit(solution)/shard_map/ppermute | solution.py:25
  37.4 16.6 %copy-start.7 = (bf16[64,2048]{1,0:T(8,128)(2,1)}, bf16[64,2048]{1,0:T(8,128)(2,1)S(1)}, u32[]{:S(2)}) copy-start(bf16[64,2048]{1,0:T(8,128)(2,1)S(1)} %collective-permute-done.9) | copy-start | bytes 786436
  37.4 16.6 %copy-start.4 = (bf16[768,2048]{1,0:T(8,128)(2,1)}, bf16[768,2048]{1,0:T(8,128)(2,1)S(1)}, u32[]{:S(2)}) copy-start(bf16[768,2048]{1,0:T(8,128)(2,1)S(1)} %collective-permute-done.11.refs_6_) | copy-start | bytes 9437188
  37.8 13.2 %collective-permute-start.15 = (bf16[64,2048]{1,0:T(8,128)(2,1)S(1)}, bf16[64,2048]{1,0:T(8,128)(2,1)S(1)}, u32[]{:S(2)}, u32[]{:S(2)}) collective-permute-start(bf16[64,2048]{1,0:T(8,128)(2,1)S(1)} %multiply_convert_fusion.refs_9_), channel_id=1, source_target_pairs={{0,4},{4,0},{8,12},{12,8},{1,5},{5,1},{9,13},{13,9},{2,6},{6,2},{1... | collective-permute-start | bytes 786440 | tf_op jit(solution)/shard_map/ppermute | solution.py:25
  39.2 14.7 %collective-permute-start.13 = (bf16[64,2048]{1,0:T(8,128)(2,1)S(1)}, bf16[64,2048]{1,0:T(8,128)(2,1)S(1)}, u32[]{:S(2)}, u32[]{:S(2)}) collective-permute-start(bf16[64,2048]{1,0:T(8,128)(2,1)S(1)} %multiply_convert_fusion.refs_9_), channel_id=1, source_target_pairs={{0,8},{4,12},{8,0},{12,4},{1,9},{5,13},{9,1},{13,5},{2,10},{6,14},... | collective-permute-start | bytes 786440 | tf_op jit(solution)/shard_map/ppermute | solution.py:25
  41.8 12.2 %collective-permute-start.19 = (bf16[64,2048]{1,0:T(8,128)(2,1)S(1)}, bf16[64,2048]{1,0:T(8,128)(2,1)S(1)}, u32[]{:S(2)}, u32[]{:S(2)}) collective-permute-start(bf16[64,2048]{1,0:T(8,128)(2,1)S(1)} %multiply_convert_fusion.refs_9_), channel_id=1, source_target_pairs={{0,16},{16,0},{1,17},{17,1},{2,18},{18,2},{3,19},{19,3},{4,20},{20... | collective-permute-start | bytes 786440 | tf_op jit(solution)/shard_map/ppermute | solution.py:25
  43.3 10.7 %collective-permute-start.18 = (bf16[64,2048]{1,0:T(8,128)(2,1)S(1)}, bf16[64,2048]{1,0:T(8,128)(2,1)S(1)}, u32[]{:S(2)}, u32[]{:S(2)}) collective-permute-start(bf16[64,2048]{1,0:T(8,128)(2,1)S(1)} %multiply_convert_fusion.refs_9_), channel_id=1, source_target_pairs={{0,2},{1,3},{2,0},{3,1},{4,6},{5,7},{6,4},{7,5},{8,10},{9,11},{10,... | collective-permute-start | bytes 786440 | tf_op jit(solution)/shard_map/ppermute | solution.py:25
  51.0 9.2 %collective-permute-start.17 = (bf16[64,2048]{1,0:T(8,128)(2,1)S(1)}, bf16[64,2048]{1,0:T(8,128)(2,1)S(1)}, u32[]{:S(2)}, u32[]{:S(2)}) collective-permute-start(bf16[64,2048]{1,0:T(8,128)(2,1)S(1)} %collective-permute-done.15.refs_10_), channel_id=1, source_target_pairs={{0,16},{16,0},{1,17},{17,1},{2,18},{18,2},{3,19},{19,3},{4,20},{20... | collective-permute-start | bytes 786440 | tf_op jit(solution)/shard_map/ppermute | solution.py:25
  52.4 9.2 %collective-permute-start.16 = (bf16[64,2048]{1,0:T(8,128)(2,1)S(1)}, bf16[64,2048]{1,0:T(8,128)(2,1)S(1)}, u32[]{:S(2)}, u32[]{:S(2)}) collective-permute-start(bf16[64,2048]{1,0:T(8,128)(2,1)S(1)} %collective-permute-done.15.refs_10_), channel_id=1, source_target_pairs={{0,2},{1,3},{2,0},{3,1},{4,6},{5,7},{6,4},{7,5},{8,10},{9,11},{10,... | collective-permute-start | bytes 786440 | tf_op jit(solution)/shard_map/ppermute | solution.py:25
  54.0 7.7 %collective-permute-start.14 = (bf16[64,2048]{1,0:T(8,128)(2,1)S(1)}, bf16[64,2048]{1,0:T(8,128)(2,1)S(1)}, u32[]{:S(2)}, u32[]{:S(2)}) collective-permute-start(bf16[64,2048]{1,0:T(8,128)(2,1)S(1)} %collective-permute-done.13.refs_11_), channel_id=1, source_target_pairs={{0,4},{4,0},{8,12},{12,8},{1,5},{5,1},{9,13},{13,9},{2,6},{6,2},{1... | collective-permute-start | bytes 786440 | tf_op jit(solution)/shard_map/ppermute | solution.py:25
  54.1 11.8 %collective-permute-start.22 = (bf16[64,2048]{1,0:T(8,128)(2,1)S(1)}, bf16[64,2048]{1,0:T(8,128)(2,1)S(1)}, u32[]{:S(2)}, u32[]{:S(2)}) collective-permute-start(bf16[64,2048]{1,0:T(8,128)(2,1)S(1)} %collective-permute-done.13.refs_11_), channel_id=1, source_target_pairs={{0,16},{16,0},{1,17},{17,1},{2,18},{18,2},{3,19},{19,3},{4,20},{20... | collective-permute-start | bytes 786440 | tf_op jit(solution)/shard_map/ppermute | solution.py:25
  55.1 12.2 %collective-permute-start.20 = (bf16[64,2048]{1,0:T(8,128)(2,1)S(1)}, bf16[64,2048]{1,0:T(8,128)(2,1)S(1)}, u32[]{:S(2)}, u32[]{:S(2)}) collective-permute-start(bf16[64,2048]{1,0:T(8,128)(2,1)S(1)} %collective-permute-done.13.refs_11_), channel_id=1, source_target_pairs={{0,2},{1,3},{2,0},{3,1},{4,6},{5,7},{6,4},{7,5},{8,10},{9,11},{10,... | collective-permute-start | bytes 786440 | tf_op jit(solution)/shard_map/ppermute | solution.py:25
  61.7 7.4 %collective-permute-start.23 = (bf16[64,2048]{1,0:T(8,128)(2,1)S(1)}, bf16[64,2048]{1,0:T(8,128)(2,1)S(1)}, u32[]{:S(2)}, u32[]{:S(2)}) collective-permute-start(bf16[64,2048]{1,0:T(8,128)(2,1)S(1)} %collective-permute-done.14.refs_12_), channel_id=1, source_target_pairs={{0,16},{16,0},{1,17},{17,1},{2,18},{18,2},{3,19},{19,3},{4,20},{20... | collective-permute-start | bytes 786440 | tf_op jit(solution)/shard_map/ppermute | solution.py:25
  62.3 8.0 %collective-permute-start.21 = (bf16[64,2048]{1,0:T(8,128)(2,1)S(1)}, bf16[64,2048]{1,0:T(8,128)(2,1)S(1)}, u32[]{:S(2)}, u32[]{:S(2)}) collective-permute-start(bf16[64,2048]{1,0:T(8,128)(2,1)S(1)} %collective-permute-done.14.refs_12_), channel_id=1, source_target_pairs={{0,2},{1,3},{2,0},{3,1},{4,6},{5,7},{6,4},{7,5},{8,10},{9,11},{10,... | collective-permute-start | bytes 786440 | tf_op jit(solution)/shard_map/ppermute | solution.py:25
  70.3 12.1 %collective-permute-start.24 = (bf16[256,1024]{1,0:T(8,128)(2,1)S(1)}, bf16[256,1024]{1,0:T(8,128)(2,1)S(1)}, u32[]{:S(2)}, u32[]{:S(2)}) collective-permute-start(bf16[256,1024]{1,0:T(8,128)(2,1)S(1)} %get-tuple-element.94), channel_id=1, source_target_pairs={{0,16},{16,0},{1,17},{17,1},{2,18},{18,2},{3,19},{19,3},{4,20},{20... | collective-permute-start | bytes 1572872 | tf_op jit(solution)/shard_map/ppermute | solution.py:25
  71.0 11.4 %collective-permute-start.25 = (bf16[256,1024]{1,0:T(8,128)(2,1)S(1)}, bf16[256,1024]{1,0:T(8,128)(2,1)S(1)}, u32[]{:S(2)}, u32[]{:S(2)}) collective-permute-start(bf16[256,1024]{1,0:T(8,128)(2,1)S(1)} %get-tuple-element.95), channel_id=1, source_target_pairs={{0,2},{1,3},{2,0},{3,1},{4,6},{5,7},{6,4},{7,5},{8,10},{9,11},{10,... | collective-permute-start | bytes 1572872 | tf_op jit(solution)/shard_map/ppermute | solution.py:25
  82.4 12.9 %collective-permute-start.26 = (bf16[256,1024]{1,0:T(8,128)(2,1)S(1)}, bf16[256,1024]{1,0:T(8,128)(2,1)S(1)}, u32[]{:S(2)}, u32[]{:S(2)}) collective-permute-start(bf16[256,1024]{1,0:T(8,128)(2,1)S(1)} %get-tuple-element.96), channel_id=1, source_target_pairs={{0,16},{16,0},{1,17},{17,1},{2,18},{18,2},{3,19},{19,3},{4,20},{20... | collective-permute-start | bytes 1572872 | tf_op jit(solution)/shard_map/ppermute | solution.py:25
  84.0 11.3 %collective-permute-start.27 = (bf16[256,1024]{1,0:T(8,128)(2,1)S(1)}, bf16[256,1024]{1,0:T(8,128)(2,1)S(1)}, u32[]{:S(2)}, u32[]{:S(2)}) collective-permute-start(bf16[256,1024]{1,0:T(8,128)(2,1)S(1)} %get-tuple-element.97), channel_id=1, source_target_pairs={{0,2},{1,3},{2,0},{3,1},{4,6},{5,7},{6,4},{7,5},{8,10},{9,11},{10,... | collective-permute-start | bytes 1572872 | tf_op jit(solution)/shard_map/ppermute | solution.py:25
  95.3 8.2 %collective-permute-start.28 = (bf16[128,1024]{1,0:T(8,128)(2,1)S(1)}, bf16[128,1024]{1,0:T(8,128)(2,1)S(1)}, u32[]{:S(2)}, u32[]{:S(2)}) collective-permute-start(bf16[128,1024]{1,0:T(8,128)(2,1)S(1)} %get-tuple-element.109), channel_id=1, source_target_pairs={{0,16},{16,0},{1,17},{17,1},{2,18},{18,2},{3,19},{19,3},{4,20},{20... | collective-permute-start | bytes 786440 | tf_op jit(solution)/shard_map/ppermute | solution.py:25
  95.6 9.6 %collective-permute-start.30 = (bf16[128,1024]{1,0:T(8,128)(2,1)S(1)}, bf16[128,1024]{1,0:T(8,128)(2,1)S(1)}, u32[]{:S(2)}, u32[]{:S(2)}) collective-permute-start(bf16[128,1024]{1,0:T(8,128)(2,1)S(1)} %get-tuple-element.111), channel_id=1, source_target_pairs={{0,2},{1,3},{2,0},{3,1},{4,6},{5,7},{6,4},{7,5},{8,10},{9,11},{10,... | collective-permute-start | bytes 786440 | tf_op jit(solution)/shard_map/ppermute | solution.py:25
  96.4 11.0 %collective-permute-start.32 = (bf16[128,1024]{1,0:T(8,128)(2,1)S(1)}, bf16[128,1024]{1,0:T(8,128)(2,1)S(1)}, u32[]{:S(2)}, u32[]{:S(2)}) collective-permute-start(bf16[128,1024]{1,0:T(8,128)(2,1)S(1)} %get-tuple-element.112), channel_id=1, source_target_pairs={{0,16},{16,0},{1,17},{17,1},{2,18},{18,2},{3,19},{19,3},{4,20},{20... | collective-permute-start | bytes 786440 | tf_op jit(solution)/shard_map/ppermute | solution.py:25
  97.9 10.6 %collective-permute-start.33 = (bf16[128,1024]{1,0:T(8,128)(2,1)S(1)}, bf16[128,1024]{1,0:T(8,128)(2,1)S(1)}, u32[]{:S(2)}, u32[]{:S(2)}) collective-permute-start(bf16[128,1024]{1,0:T(8,128)(2,1)S(1)} %get-tuple-element.113), channel_id=1, source_target_pairs={{0,2},{1,3},{2,0},{3,1},{4,6},{5,7},{6,4},{7,5},{8,10},{9,11},{10,... | collective-permute-start | bytes 786440 | tf_op jit(solution)/shard_map/ppermute | solution.py:25
  103.5 9.0 %collective-permute-start.29 = (bf16[128,1024]{1,0:T(8,128)(2,1)S(1)}, bf16[128,1024]{1,0:T(8,128)(2,1)S(1)}, u32[]{:S(2)}, u32[]{:S(2)}) collective-permute-start(bf16[128,1024]{1,0:T(8,128)(2,1)S(1)} %add_convert_fusion.3), channel_id=1, source_target_pairs={{0,2},{1,3},{2,0},{3,1},{4,6},{5,7},{6,4},{7,5},{8,10},{9,11},{10,... | collective-permute-start | bytes 786440 | tf_op jit(solution)/shard_map/ppermute | solution.py:25
  105.3 7.6 %collective-permute-start.31 = (bf16[128,1024]{1,0:T(8,128)(2,1)S(1)}, bf16[128,1024]{1,0:T(8,128)(2,1)S(1)}, u32[]{:S(2)}, u32[]{:S(2)}) collective-permute-start(bf16[128,1024]{1,0:T(8,128)(2,1)S(1)} %add_convert_fusion.2), channel_id=1, source_target_pairs={{0,16},{16,0},{1,17},{17,1},{2,18},{18,2},{3,19},{19,3},{4,20},{20... | collective-permute-start | bytes 786440 | tf_op jit(solution)/shard_map/ppermute | solution.py:25
  113.5 22.3 %copy-start.6 = (bf16[1,64,2048]{2,1,0:T(8,128)(2,1)S(1)}, bf16[1,64,2048]{2,1,0:T(8,128)(2,1)}, u32[]{:S(2)}) copy-start(bf16[1,64,2048]{2,1,0:T(8,128)(2,1)} %param.12) | copy-start | bytes 786436
  113.5 22.3 %copy-start.8 = (bf16[64,2048]{1,0:T(8,128)(2,1)S(1)}, bf16[64,2048]{1,0:T(8,128)(2,1)}, u32[]{:S(2)}) copy-start(bf16[64,2048]{1,0:T(8,128)(2,1)} %copy-done.7) | copy-start | bytes 786436
  113.5 11.2 %collective-permute-start.37 = (bf16[64,2048]{1,0:T(8,128)(2,1)S(1)}, bf16[64,2048]{1,0:T(8,128)(2,1)S(1)}, u32[]{:S(2)}, u32[]{:S(2)}) collective-permute-start(bf16[64,2048]{1,0:T(8,128)(2,1)S(1)} %fusion.9), channel_id=1, source_target_pairs={{0,4},{4,0},{8,12},{12,8},{1,5},{5,1},{9,13},{13,9},{2,6},{6,2},{1... | collective-permute-start | bytes 786440 | tf_op jit(solution)/shard_map/ppermute | solution.py:25
  113.6 12.6 %collective-permute-start.34 = (bf16[128,1024]{1,0:T(8,128)(2,1)S(1)}, bf16[128,1024]{1,0:T(8,128)(2,1)S(1)}, u32[]{:S(2)}, u32[]{:S(2)}) collective-permute-start(bf16[128,1024]{1,0:T(8,128)(2,1)S(1)} %get-tuple-element.120), channel_id=1, source_target_pairs={{0,2},{1,3},{2,0},{3,1},{4,6},{5,7},{6,4},{7,5},{8,10},{9,11},{10,... | collective-permute-start | bytes 786440 | tf_op jit(solution)/shard_map/ppermute | solution.py:25
  113.7 12.6 %collective-permute-start.35 = (bf16[128,1024]{1,0:T(8,128)(2,1)S(1)}, bf16[128,1024]{1,0:T(8,128)(2,1)S(1)}, u32[]{:S(2)}, u32[]{:S(2)}) collective-permute-start(bf16[128,1024]{1,0:T(8,128)(2,1)S(1)} %get-tuple-element.121), channel_id=1, source_target_pairs={{0,16},{16,0},{1,17},{17,1},{2,18},{18,2},{3,19},{19,3},{4,20},{20... | collective-permute-start | bytes 786440 | tf_op jit(solution)/shard_map/ppermute | solution.py:25
  124.7 10.3 %collective-permute-start.38 = (bf16[64,2048]{1,0:T(8,128)(2,1)S(1)}, bf16[64,2048]{1,0:T(8,128)(2,1)S(1)}, u32[]{:S(2)}, u32[]{:S(2)}) collective-permute-start(bf16[64,2048]{1,0:T(8,128)(2,1)S(1)} %fusion.1), channel_id=1, source_target_pairs={{0,8},{4,12},{8,0},{12,4},{1,9},{5,13},{9,1},{13,5},{2,10},{6,14},... | collective-permute-start | bytes 786440 | tf_op jit(solution)/shard_map/ppermute | solution.py:25
  126.5 9.2 %collective-permute-start.36 = (bf16[64,2048]{1,0:T(8,128)(2,1)S(1)}, bf16[64,2048]{1,0:T(8,128)(2,1)S(1)}, u32[]{:S(2)}, u32[]{:S(2)}) collective-permute-start(bf16[64,2048]{1,0:T(8,128)(2,1)S(1)} %fusion.8), channel_id=1, source_target_pairs={{0,4},{4,0},{8,12},{12,8},{1,5},{5,1},{9,13},{13,9},{2,6},{6,2},{1... | collective-permute-start | bytes 786440 | tf_op jit(solution)/shard_map/ppermute | solution.py:25
